TPU v7x, 32 devices: a whole 2x2x4 slice. The times are simulated.
32 devices in a mesh: expert: 16 (over z, y, core), tp: 2 (over x).
Axes of the slice: x: 2, y: 2, z: 4, core: 2. Of those that a mesh axis runs over, the one named last changes fastest.
Arguments:
- cotangent: bfloat16 [2048, 2048], P('expert'), may hold values from -6 to 6
- gates: float32 [2048, 8], P('expert'), may hold values from 0.05 to 0.6
- expert_ids: int32 [2048, 8], P('expert'), may hold values from 0 to 31, all different within a row; in each aligned block of 128 rows (0 to 127, 128 to 255, ...) at most 48 rows name the same one
- saved_gate: bfloat16 [32, 768, 768], P('expert', 'tp'), may hold values from -6 to 6
- saved_up: bfloat16 [32, 768, 768], P('expert', 'tp'), may hold values from -6 to 6
- w_gate: bfloat16 [32, 768, 2048], P('expert', 'tp'), may hold values from -0.125 to 0.125
- w_up: bfloat16 [32, 768, 2048], P('expert', 'tp'), may hold values from -0.125 to 0.125
- w_down: bfloat16 [32, 768, 2048], P('expert', 'tp'), may hold values from -0.21875 to 0.21875
Outputs:
- token_grad: float32 [2048, 2048], P(('expert', 'tp'))
Inputs may be any that keep to these rules, and one draw needn't show every extreme that they name: `expert_ids`: within the 128 tokens of one group, no expert is named by more than 48 route rows, a bound that some block reaches; a token names 8 different experts.
All inputs are finite; a program needn't handle non-finite values.
Results may differ from a plain program's by a relative error of at most 0.0049.
Values may be sent and summed in bfloat16 or wider, within the bound.
No kernel may reach another device: no remote copies, remote signals or barrier semaphores. Data moves between devices by JAX's collectives and lax.ppermute only.
A program may use at most 64 MiB of HBM per device.

v0:
```python
import jax
import jax.numpy as jnp
from jax import lax
from jax.sharding import PartitionSpec as P


def route_slots(expert_ids, expert_total):
    flat_ids = expert_ids.reshape(-1)
    one_hot = (flat_ids[:, None] == jnp.arange(expert_total, dtype=jnp.int32)[None, :]).astype(
        jnp.int32
    )
    before = jnp.cumsum(one_hot, axis=0) - one_hot
    return (flat_ids, jnp.sum(before * one_hot, axis=1))


def body(cotangent, gates, expert_ids, saved_gate, saved_up, w_gate, w_up, w_down):
    owners = lax.axis_size("expert")
    row_count, feature_dim = cotangent.shape
    top_count = expert_ids.shape[1]
    local_count, shard_width, slot_count = saved_gate.shape
    capacity = slot_count // owners
    flat_ids, slot_pos = route_slots(expert_ids, local_count * owners)
    target = flat_ids % local_count * slot_count + flat_ids // local_count * capacity + slot_pos
    scaled = (gates[:, :, None] * cotangent.astype(jnp.float32)[:, None, :]).astype(jnp.bfloat16)
    scaled = scaled.reshape(row_count * top_count, feature_dim)
    outgoing = (
        jnp.zeros((local_count * slot_count, feature_dim), jnp.bfloat16).at[target].set(scaled)
    )
    outgoing = outgoing.reshape(local_count, slot_count, feature_dim)
    arrived = lax.all_to_all(outgoing, "expert", split_axis=1, concat_axis=1, tiled=True)
    hidden_grad = jnp.einsum("efd,esd->efs", w_down, arrived, preferred_element_type=jnp.float32)
    gate_value = saved_gate.astype(jnp.float32)
    up_value = saved_up.astype(jnp.float32)
    sigmoid_gate = jax.nn.sigmoid(gate_value)
    up_grad = (hidden_grad * gate_value * sigmoid_gate).astype(jnp.bfloat16)
    gate_grad = (
        hidden_grad * up_value * sigmoid_gate * (1.0 + gate_value * (1.0 - sigmoid_gate))
    ).astype(jnp.bfloat16)
    partial_value = jnp.einsum(
        "efs,efd->esd", gate_grad, w_gate, preferred_element_type=jnp.float32
    )
    partial_value = partial_value + jnp.einsum(
        "efs,efd->esd", up_grad, w_up, preferred_element_type=jnp.float32
    )
    partial_value = partial_value.astype(jnp.bfloat16)
    returned = lax.all_to_all(partial_value, "expert", split_axis=1, concat_axis=1, tiled=True)
    picked = returned.reshape(local_count * slot_count, feature_dim)[target].astype(jnp.float32)
    combined = jnp.sum(picked.reshape(row_count, top_count, feature_dim), axis=1)
    return lax.psum_scatter(combined, "tp", scatter_dimension=0, tiled=True)


def solution(mesh):
    in_specs = (
        P("expert", None),
        P("expert", None),
        P("expert", None),
        P("expert", "tp", None),
        P("expert", "tp", None),
        P("expert", "tp", None),
        P("expert", "tp", None),
        P("expert", "tp", None),
    )
    out_specs = P(("expert", "tp"), None)
    return jax.shard_map(body, mesh=mesh, in_specs=in_specs, out_specs=out_specs, check_vma=False)
```

profile of v0, /device:TPU:0, one launch (start us, length us, event | category | flops | bytes accessed | tf_op | source)
XLA Modules:
  0.0 427.6 jit_solution(4638705611442049702)
XLA Ops:
  6.5 0.0 copy-start
  6.5 0.9 copy.30
  7.5 0.1 eq.31
  7.6 0.1 eq.27
  7.7 0.1 reshape.156
  7.8 0.8 copy.35
  8.5 0.1 mul.70
  8.7 9.0 %reduce-window.6 = s32[32,8,128]{2,1,0:T(8,128)S(1)} reduce-window(s32[32,8,128]{2,1,0:T(8,128)S(1)} %fusion.25, s32[]{:T(128)} %constant.35.clone.1), window={size=1x1x128 pad=0_0x0_0x127_0}, to_apply=%region_0.0 | reduce-window | flops 4161536 | bytes 262148 | tf_op jit(solution)/shard_map/reduce-window
  17.7 0.1 slice.10
  17.8 0.1 copy.33
  17.9 0.1 copy.34
  18.0 0.1 broadcast_add_fusion
  18.1 2.1 convert_element_type.38
  20.4 11.0 %scatter_custom_fusion = bf16[1536,2048]{1,0:T(8,128)(2,1)} fusion(s32[1024]{0:T(1024)S(1)} %bitcast.48, f32[128,2048]{1,0:T(8,128)} %convert_element_type.38, f32[1024]{0:T(1024)S(1)} %mul.70, bf16[]{:T(256)} %constant.34.clone.1), kind=kCustom, calls=%fused_computation.8 | custom fusion | flops 4194304 | bytes 7344130 | tf_op jit(solution)/shard_map/scatter | solution.py:27
  31.4 12.6 %copy.36 = bf16[2,768,2048]{2,0,1:T(2,128)(2,1)} copy(bf16[2,768,2048]{2,1,0:T(8,128)(2,1)} %bitcast.44) | data formatting | bytes 12582912 | tf_op jit(solution)/shard_map/reshape | solution.py:29
  44.0 7.4 %all-to-all-start = ((bf16[2,768,2048]{2,0,1:T(2,128)(2,1)}), bf16[2,768,2048]{2,0,1:T(2,128)(2,1)}, u32[]{:S(2)}, u32[]{:S(2)}) async-start(bf16[2,768,2048]{2,0,1:T(2,128)(2,1)} %copy.36), calls=%async_computation | async-start | bytes 12582912 | tf_op jit(solution)/shard_map/all_to_all | solution.py:30
  51.5 2.4 copy.39
  53.9 2.4 copy.38
  56.3 109.4 %all-to-all-done = bf16[2,768,2048]{2,0,1:T(2,128)(2,1)} async-done(((bf16[2,768,2048]{2,0,1:T(2,128)(2,1)}), bf16[2,768,2048]{2,0,1:T(2,128)(2,1)}, u32[]{:S(2)}, u32[]{:S(2)}) %all-to-all-start) | async-done | bytes 6291488 | tf_op jit(solution)/shard_map/all_to_all | solution.py:30
  165.7 0.0 copy-start.2
  165.7 0.0 copy-start.3
  165.7 9.2 %fusion.1 = f32[2,768,384]{2,1,0:T(8,128)S(1)} fusion(bf16[2,384,2048]{2,1,0:T(8,128)(2,1)} %param.15, bf16[2,768,2048]{2,0,1:T(2,128)(2,1)} %all-to-all-done), kind=kOutput, calls=%fused_computation.6 | convolution fusion | flops 2415919104 | bytes 11796480 | tf_op jit(solution)/shard_map/efd,esd->efs/dot_general | solution.py:31
  174.9 0.0 copy-done
  174.9 0.0 copy-done.2
  174.9 0.0 copy-done.3
  174.9 6.6 %fusion.18 = f32[2,768,2048]{2,1,0:T(8,128)} fusion(bf16[2,384,2048]{2,1,0:T(8,128)(2,1)S(1)} %copy-done, bf16[2,384,768]{1,2,0:T(8,128)(2,1)S(1)} %copy-done.2, f32[2,768,384]{2,1,0:T(8,128)S(1)} %fusion.1, bf16[2,384,768]{1,2,0:T(8,128)(2,1)S(1)} %copy-done.3), kind=kOutput, calls=%fused_computation.25 | convolution fusion | flops 2422996992 | bytes 20447232 | tf_op jit(solution)/shard_map/efs,efd->esd/dot_general | solution.py:39
  181.5 7.4 %add_convert_fusion = bf16[2,768,2048]{2,1,0:T(8,128)(2,1)S(1)} fusion(f32[2,768,2048]{2,1,0:T(8,128)} %fusion.18, bf16[2,384,2048]{2,1,0:T(8,128)(2,1)} %param.14, bf16[2,384,768]{1,2,0:T(8,128)(2,1)S(1)} %copy-done.2, f32[2,768,384]{2,1,0:T(8,128)S(1)} %fusion.1), kind=kOutput, calls=%fused_computation.2 | convolution fusion | flops 2426339328 | bytes 25559040 | tf_op jit(solution)/shard_map/efs,efd->esd/dot_general | solution.py:42
  188.9 18.8 %copy.40 = bf16[2,768,2048]{2,0,1:T(2,128)(2,1)} copy(bf16[2,768,2048]{2,1,0:T(8,128)(2,1)S(1)} %add_convert_fusion) | data formatting | bytes 12582912 | tf_op jit(solution)/shard_map/convert_element_type | solution.py:45
  207.7 28.1 %all-to-all-start.1 = ((bf16[2,768,2048]{2,0,1:T(2,128)(2,1)}), bf16[2,768,2048]{2,0,1:T(2,128)(2,1)}, u32[]{:S(2)}, u32[]{:S(2)}) async-start(bf16[2,768,2048]{2,0,1:T(2,128)(2,1)} %copy.40), calls=%async_computation.1 | async-start | bytes 12582912 | tf_op jit(solution)/shard_map/all_to_all | solution.py:46
  235.8 0.3 reduce-scatter.2.cloned.1.call-start
  236.1 113.9 %all-to-all-done.1 = bf16[2,768,2048]{2,0,1:T(2,128)(2,1)} async-done(((bf16[2,768,2048]{2,0,1:T(2,128)(2,1)}), bf16[2,768,2048]{2,0,1:T(2,128)(2,1)}, u32[]{:S(2)}, u32[]{:S(2)}) %all-to-all-start.1) | async-done | bytes 6291488 | tf_op jit(solution)/shard_map/all_to_all | solution.py:46
  350.0 8.3 %copy.41 = bf16[2,768,2048]{2,1,0:T(8,128)(2,1)} copy(bf16[2,768,2048]{2,0,1:T(2,128)(2,1)} %all-to-all-done.1) | data formatting | bytes 12582912 | tf_op jit(solution)/shard_map/all_to_all | solution.py:46
  358.4 0.0 copy-start.1
  358.4 12.6 %gather_fusion = bf16[1024,2048]{1,0:T(8,128)(2,1)} fusion(bf16[1536,2048]{1,0:T(8,128)(2,1)} %bitcast.43, s32[1024]{0:T(1024)S(1)} %broadcast_clamp_fusion), kind=kCustom, calls=%fused_computation | custom fusion | bytes 8392704 | tf_op jit(solution)/shard_map/gather | solution.py:47
  370.9 6.0 %convert_reduce_fusion = f32[128,2048]{1,0:T(8,128)} fusion(bf16[1024,2048]{1,0:T(8,128)(2,1)} %gather_fusion), kind=kLoop, calls=%fused_computation.3 | loop fusion | flops 3932160 | bytes 5242880 | tf_op jit(solution)/shard_map/reduce_sum | solution.py:48
  376.9 0.0 reduce-scatter.2.cloned.1.call-update
  377.0 43.8 %reduce-scatter.2.cloned.1.call-done = f32[64,2048]{1,0:T(8,128)} async-done(((f32[128,2048]{1,0:T(8,128)}), f32[64,2048]{1,0:T(8,128)}) %reduce-scatter.2.cloned.1.call-update) | async-done | bytes 524304 | tf_op jit(solution)/shard_map/reduce_scatter | solution.py:49
  420.8 0.0 copy-done.1
  (6 shorter events, 0.1 us)
Async XLA Ops:
  6.5 168.3 %copy-start = (bf16[2,384,2048]{2,1,0:T(8,128)(2,1)S(1)}, bf16[2,384,2048]{2,1,0:T(8,128)(2,1)}, u32[]{:S(2)}) copy-start(bf16[2,384,2048]{2,1,0:T(8,128)(2,1)} %param.13) | copy-start | bytes 9437188
  44.0 121.6 %all-to-all-start = ((bf16[2,768,2048]{2,0,1:T(2,128)(2,1)}), bf16[2,768,2048]{2,0,1:T(2,128)(2,1)}, u32[]{:S(2)}, u32[]{:S(2)}) async-start(bf16[2,768,2048]{2,0,1:T(2,128)(2,1)} %copy.36), calls=%async_computation | async-start | bytes 12582912 | tf_op jit(solution)/shard_map/all_to_all | solution.py:30
  165.7 9.2 %copy-start.2 = (bf16[2,384,768]{1,2,0:T(8,128)(2,1)S(1)}, bf16[2,384,768]{1,2,0:T(8,128)(2,1)}, u32[]{:S(2)}) copy-start(bf16[2,384,768]{1,2,0:T(8,128)(2,1)} %copy.39) | copy-start | bytes 3538948
  165.7 9.2 %copy-start.3 = (bf16[2,384,768]{1,2,0:T(8,128)(2,1)S(1)}, bf16[2,384,768]{1,2,0:T(8,128)(2,1)}, u32[]{:S(2)}) copy-start(bf16[2,384,768]{1,2,0:T(8,128)(2,1)} %copy.38) | copy-start | bytes 3538948
  207.7 142.3 %all-to-all-start.1 = ((bf16[2,768,2048]{2,0,1:T(2,128)(2,1)}), bf16[2,768,2048]{2,0,1:T(2,128)(2,1)}, u32[]{:S(2)}, u32[]{:S(2)}) async-start(bf16[2,768,2048]{2,0,1:T(2,128)(2,1)} %copy.40), calls=%async_computation.1 | async-start | bytes 12582912 | tf_op jit(solution)/shard_map/all_to_all | solution.py:46
  235.8 185.0 %reduce-scatter.2.cloned.1.call-start = ((), (), s32[]{:S(2)}) async-start(), calls=%async_computation.3 | async-start | bytes 1572864 | tf_op jit(solution)/shard_map/reduce_scatter | solution.py:49
  358.4 62.4 %copy-start.1 = (bf16[2,384,2048]{2,1,0:T(8,128)(2,1)S(1)}, bf16[2,384,2048]{2,1,0:T(8,128)(2,1)}, u32[]{:S(2)}) copy-start(bf16[2,384,2048]{2,1,0:T(8,128)(2,1)} %param.13) | copy-start | bytes 9437188
Sparse Core Ops, SparseCore 0:
  377.1 43.6 reduce-scatter.1
where the time goes:
time: 428 us
  waiting for transfers between devices  267 us (62%)
  local copies, waits for them, and re-layouts  59.5 us (14%)
  starting transfers between devices  35.8 us (8%)
  other arithmetic  28.4 us (7%)
  matrix products  23.2 us (5%)
  between operations  13.5 us (3%)
    all_to_all x1, waiting for transfers between devices, body(): lax.all_to_all(partial_value, 'expert', split_axis=1, concat_axis=1, tile...  114 us
    all_to_all x1, waiting for transfers between devices, body(): lax.all_to_all(outgoing, 'expert', split_axis=1, concat_axis=1, tiled=True)  109 us
    reduce_scatter x1, waiting for transfers between devices, body(): return lax.psum_scatter(combined, 'tp', scatter_dimension=0, tiled=True)  43.8 us
    all_to_all x1, starting transfers between devices, body(): lax.all_to_all(partial_value, 'expert', split_axis=1, concat_axis=1, tile...  28.1 us
    convert_element_type x1, local copies, waits for them, and re-layouts, body(): partial_value = partial_value.astype(jnp.bfloat16)  18.8 us
    reshape x1, local copies, waits for them, and re-layouts, body(): outgoing = outgoing.reshape(local_count, slot_count, feature_dim)  12.6 us
    gather x1, local copies, waits for them, and re-layouts, body(): returned.reshape(local_count * slot_count, feature_dim)[target]  12.6 us
    scatter x1, other arithmetic, body(): jnp.zeros((local_count * slot_count, feature_dim), jnp.bfloat16).at[target]  11 us
  transfers between devices with their start and end apart: 3, of which 3 were waited for; matrix products, arithmetic and copies ran while one was open for 1% of the time, Pallas kernels for 0%

commit v1 on v0

v1 whole, which is shorter than its diff:
```python
import jax
import jax.numpy as jnp
from jax import lax
from jax.sharding import PartitionSpec as P


def route_slots(expert_ids, expert_total):
    flat_ids = expert_ids.reshape(-1)
    one_hot = (flat_ids[:, None] == jnp.arange(expert_total, dtype=jnp.int32)[None, :]).astype(
        jnp.int32
    )
    before = jnp.cumsum(one_hot, axis=0) - one_hot
    return (flat_ids, jnp.sum(before * one_hot, axis=1))


def expert_step(arrived, saved_gate, saved_up, w_gate, w_up, w_down):
    hidden_grad = jnp.einsum("efd,esd->efs", w_down, arrived, preferred_element_type=jnp.float32)
    gate_value = saved_gate.astype(jnp.float32)
    up_value = saved_up.astype(jnp.float32)
    sigmoid_gate = jax.nn.sigmoid(gate_value)
    up_grad = (hidden_grad * gate_value * sigmoid_gate).astype(jnp.bfloat16)
    gate_grad = (
        hidden_grad * up_value * sigmoid_gate * (1.0 + gate_value * (1.0 - sigmoid_gate))
    ).astype(jnp.bfloat16)
    partial_value = jnp.einsum(
        "efs,efd->esd", gate_grad, w_gate, preferred_element_type=jnp.float32
    )
    partial_value = partial_value + jnp.einsum(
        "efs,efd->esd", up_grad, w_up, preferred_element_type=jnp.float32
    )
    return partial_value.astype(jnp.bfloat16)


def slots_body(cotangent, gates, expert_ids, saved_gate, saved_up, w_gate, w_up, w_down):
    owners = lax.axis_size("expert")
    row_count, feature_dim = cotangent.shape
    top_count = expert_ids.shape[1]
    local_count, _, slot_count = saved_gate.shape
    capacity = slot_count // owners
    flat_ids, slot_pos = route_slots(expert_ids, local_count * owners)
    target = flat_ids % local_count * slot_count + flat_ids // local_count * capacity + slot_pos
    scaled = (gates[:, :, None] * cotangent.astype(jnp.float32)[:, None, :]).astype(jnp.bfloat16)
    scaled = scaled.reshape(row_count * top_count, feature_dim)
    outgoing = (
        jnp.zeros((local_count * slot_count, feature_dim), jnp.bfloat16).at[target].set(scaled)
    )
    outgoing = outgoing.reshape(local_count, slot_count, feature_dim)
    arrived = lax.all_to_all(outgoing, "expert", split_axis=1, concat_axis=1, tiled=True)
    partial_value = expert_step(arrived, saved_gate, saved_up, w_gate, w_up, w_down)
    returned = lax.all_to_all(partial_value, "expert", split_axis=1, concat_axis=1, tiled=True)
    picked = returned.reshape(local_count * slot_count, feature_dim)[target].astype(jnp.float32)
    combined = jnp.sum(picked.reshape(row_count, top_count, feature_dim), axis=1)
    return lax.psum_scatter(combined, "tp", scatter_dimension=0, tiled=True)


def swap(value, axis, step):
    count = lax.axis_size(axis)
    return lax.ppermute(value, axis, [(i, i ^ step) for i in range(count)])


def half(value, axis, index):
    return lax.index_in_dim(value, 0, axis, keepdims=False) if value.shape[axis] == 1 else (
        lax.dynamic_index_in_dim(value, index, axis, keepdims=False)
    )


def add(kept, came):
    return (kept.astype(jnp.float32) + came.astype(jnp.float32)).astype(jnp.bfloat16)


def scatter_sums(total):
    owners = lax.axis_size("expert")
    shards = lax.axis_size("tp")
    outer = owners // 4
    row_count, feature_dim = total.shape
    piece = row_count // owners // shards
    me = lax.axis_index("expert")
    core, row, line = me % 2, me // 2 % 2, me // 4
    side = lax.axis_index("tp")
    total = total.reshape(outer, 2, 2, shards, piece, feature_dim)
    came = swap(half(total, 2, 1 - core), "expert", 1)
    total = add(half(total, 2, core), came)
    left, right = total[..., :feature_dim // 2], total[..., feature_dim // 2:]
    left_came = swap(half(left, 2, 1 - side), "tp", 1)
    right_came = swap(half(right, 1, 1 - row), "expert", 2)
    left = add(half(left, 2, side), left_came)
    right = add(half(right, 1, row), right_came)
    left_came = swap(half(left, 1, 1 - row), "expert", 2)
    right_came = swap(half(right, 1, 1 - side), "tp", 1)
    left = add(half(left, 1, row), left_came)
    right = add(half(right, 1, side), right_came)
    total = jnp.concatenate([left, right], axis=-1)
    result = half(total, 0, line).astype(jnp.float32)
    for shift in range(1, outer):
        perm = [(i, (i + 4 * shift) % owners) for i in range(owners)]
        came = lax.ppermute(half(total, 0, (line + shift) % outer), "expert", perm)
        result = result + came.astype(jnp.float32)
    return result


def tokens_body(cotangent, gates, expert_ids, saved_gate, saved_up, w_gate, w_up, w_down):
    owners = lax.axis_size("expert")
    shards = lax.axis_size("tp")
    row_count, feature_dim = cotangent.shape
    local_count, _, slot_count = saved_gate.shape
    capacity = slot_count // owners
    piece = row_count // shards
    start = lax.axis_index("tp") * piece
    high = lax.reduce_precision(gates, 8, 7)
    middle = lax.reduce_precision(gates - high, 8, 7)
    low = gates - high - middle
    side = jnp.concatenate(
        [high, middle, low, expert_ids.astype(jnp.float32)], axis=1
    ).astype(jnp.bfloat16)
    side = jnp.pad(side, ((0, 0), (0, 128 - side.shape[1])))
    own = lax.dynamic_slice_in_dim(jnp.concatenate([cotangent, side], axis=1), start, piece, 0)
    every = lax.all_gather(own, ("expert", "tp"), axis=0, tiled=True)
    every = every.reshape(owners, row_count, feature_dim + 128)
    tokens = every[:, :, :feature_dim]
    top = gates.shape[1]
    sides = every[:, :, feature_dim:].astype(jnp.float32)
    every_gate = sides[:, :, :top] + sides[:, :, top:2 * top] + sides[:, :, 2 * top:3 * top]
    every_id = sides[:, :, 3 * top:4 * top].astype(jnp.int32)
    mine = lax.axis_index("expert") * local_count + jnp.arange(local_count, dtype=jnp.int32)
    named = every_id[None] == mine[:, None, None, None]
    gate_of = jnp.sum(jnp.where(named, every_gate[None], 0.0), axis=-1)
    hit = jnp.any(named, axis=-1)
    ones = hit.astype(jnp.int32)
    slot = jnp.cumsum(ones, axis=2) - ones
    pick = (
        (slot[:, :, None, :] == jnp.arange(capacity, dtype=jnp.int32)[None, None, :, None])
        & hit[:, :, None, :]
    )
    slot_gate = jnp.sum(jnp.where(pick, gate_of[:, :, None, :], 0.0), axis=-1)
    pick = pick.astype(jnp.bfloat16)
    rows = jnp.einsum("egst,gtd->egsd", pick, tokens, preferred_element_type=jnp.float32)
    arrived = (rows * slot_gate[..., None]).astype(jnp.bfloat16)
    arrived = arrived.reshape(local_count, slot_count, feature_dim)
    partial_value = expert_step(arrived, saved_gate, saved_up, w_gate, w_up, w_down)
    partial_value = partial_value.reshape(local_count, owners, capacity, feature_dim)
    total = jnp.einsum("egst,egsd->gtd", pick, partial_value, preferred_element_type=jnp.float32)
    total = total.astype(jnp.bfloat16).reshape(owners * row_count, feature_dim)
    return scatter_sums(total)


def solution(mesh):
    in_specs = (
        P("expert", None),
        P("expert", None),
        P("expert", None),
        P("expert", "tp", None),
        P("expert", "tp", None),
        P("expert", "tp", None),
        P("expert", "tp", None),
        P("expert", "tp", None),
    )
    out_specs = P(("expert", "tp"), None)
    fits = mesh.shape["expert"] in (4, 8, 16) and mesh.shape["tp"] == 2
    body = tokens_body if fits else slots_body
    return jax.shard_map(body, mesh=mesh, in_specs=in_specs, out_specs=out_specs, check_vma=False)
```

time: 428 us -> 239 us (0.56)
  waiting for transfers between devices: 267 us -> 134 us
  local copies, waits for them, and re-layouts: 59.5 us -> 27.2 us
  starting transfers between devices: 35.8 us -> 9.25 us
  matrix products: 23.2 us -> 31.2 us
  other arithmetic: 28.4 us -> 20.6 us
    all_to_all x2 -> x0, waiting for transfers between devices: 223 us -> none  [the longest x1 114 us: body(): lax.all_to_all(partial_value, 'expert', split_axis=1, concat_axis=1, tile...]
    all_gather x0 -> x1, waiting for transfers between devices: none -> 77.9 us  [tokens_body(): every = lax.all_gather(own, ('expert', 'tp'), axis=0, tiled=True)]
    ppermute x0 -> x8, waiting for transfers between devices: none -> 55.6 us  [the longest x5 40.6 us: swap(): return lax.ppermute(value, axis, [(i, i ^ step) for i in range(count)])]
    reduce_scatter x1 -> x0, waiting for transfers between devices: 43.8 us -> none  [body(): return lax.psum_scatter(combined, 'tp', scatter_dimension=0, tiled=True)]
    all_to_all x2 -> x0, starting transfers between devices: 35.6 us -> none  [the longest x1 28.1 us: body(): lax.all_to_all(partial_value, 'expert', split_axis=1, concat_axis=1, tile...]
    convert_element_type x1, local copies, waits for them, and re-layouts: 18.8 us -> 3.51 us  [tokens_body(): arrived = (rows * slot_gate[..., None]).astype(jnp.bfloat16)]
    reshape x2 -> x0, local copies, waits for them, and re-layouts: 12.7 us -> none  [the longest x1 12.6 us: body(): outgoing = outgoing.reshape(local_count, slot_count, feature_dim)]
    gather x1 -> x0, local copies, waits for them, and re-layouts: 12.6 us -> none  [body(): returned.reshape(local_count * slot_count, feature_dim)[target]]
  transfers between devices with their start and end apart: 3 -> 9, of which waited for: 3 -> 7; matrix products, arithmetic and copies ran while one was open for 1% -> 5% of each run, Pallas kernels for 0% -> 0%
where the time goes in v1:
time: 239 us; the launch traced here: 235 us
  waiting for transfers between devices  134 us (56%)
  matrix products  31.2 us (13%)
  local copies, waits for them, and re-layouts  27.2 us (11%)
  other arithmetic  20.6 us (9%)
  between operations  13.6 us (6%)
  starting transfers between devices  9.25 us (4%)
    all_gather x1, waiting for transfers between devices, tokens_body(): every = lax.all_gather(own, ('expert', 'tp'), axis=0, tiled=True)  77.9 us
    ppermute x5, waiting for transfers between devices, swap(): return lax.ppermute(value, axis, [(i, i ^ step) for i in range(count)])  40.6 us
    ppermute x3, waiting for transfers between devices, scatter_sums(): came = lax.ppermute(half(total, 0, (line + shift) % outer), 'expert', perm)  15.1 us
    convert_element_type x5, other arithmetic, add(): (kept.astype(jnp.float32) + came.astype(jnp.float32)).astype(jnp.bfloat16)  11.9 us
    unnamed x25, local copies, waits for them, and re-layouts  9.47 us
    dynamic_slice x2, local copies, waits for them, and re-layouts, half(): lax.dynamic_index_in_dim(value, index, axis, keepdims=False)  8.81 us
    dot_general x1, matrix products, expert_step(): jnp.einsum('efs,efd->esd', up_grad, w_up, preferred_element_type=jnp.floa...  8.11 us
    dot_general x1, matrix products, tokens_body(): jnp.einsum('egst,gtd->egsd', pick, tokens, preferred_element_type=jnp.flo...  7.86 us
  transfers between devices with their start and end apart: 9, of which 7 were waited for; matrix products, arithmetic and copies ran while one was open for 5% of the time, Pallas kernels for 0%

profile of v1, /device:TPU:0, one launch (start us, length us, event | category | flops | bytes accessed | tf_op | source)
XLA Modules:
  0.0 235.4 jit_solution(4923419343652007203)
XLA Ops:
  6.5 0.0 copy-start
  6.5 0.0 all-gather.2.cloned.1.call-start
  6.5 0.8 reduce-precision_convert_fusion.1
  7.4 0.8 convert_convert_fusion
  8.2 0.1 copy.62
  8.3 1.7 fusion.32
  10.0 0.0 all-gather.2.cloned.1.call-update
  10.0 2.4 %copy.69 = bf16[2,384,768]{1,2,0:T(8,128)(2,1)} copy(bf16[2,384,768]{2,1,0:T(8,128)(2,1)} %param.11) | data formatting | bytes 2359296 | tf_op args[3]
  12.4 2.4 %copy.68 = bf16[2,384,768]{1,2,0:T(8,128)(2,1)} copy(bf16[2,384,768]{2,1,0:T(8,128)(2,1)} %param.12) | data formatting | bytes 2359296 | tf_op args[4]
  14.8 77.9 %all-gather.2.cloned.1.call-done = bf16[2048,2176]{1,0:T(8,128)(2,1)} async-done(((bf16[64,2176]{1,0:T(8,128)(2,1)}), bf16[2048,2176]{1,0:T(8,128)(2,1)}) %all-gather.2.cloned.1.call-update) | async-done | bytes 8912912 | tf_op jit(solution)/shard_map/all_gather | solution.py:117
  92.7 1.9 slice.32
  94.6 2.1 copy.75
  96.7 1.1 convert_element_type.121
  97.9 0.1 compare_reduce_fusion
  98.0 0.6 reduce_window_sum.11
  98.6 0.1 fusion.41
  98.7 0.3 select_reduce_fusion
  99.1 7.9 %fusion = bf16[2,16,48,2048]{3,2,0,1:T(8,128)(2,1)} fusion(f32[2,16,48]{2,0,1:T(2,128)S(1)} %select_reduce_fusion, bf16[16,128,2176]{2,1,0:T(8,128)(2,1)} %bitcast.74, s32[2,16,128]{2,0,1:T(2,128)S(1)} %copy.64, pred[2,16,128]{2,0,1:T(4,128)(4,1)S(1)} %copy.65), kind=kOutput, calls=%fused_computation.2 | convolution fusion | flops 811991040 | bytes 14706688 | tf_op jit(solution)/shard_map/egst,gtd->egsd/dot_general | solution.py:136
  107.0 3.5 %copy.67 = bf16[2,16,48,2048]{3,2,1,0:T(8,128)(2,1)S(1)} copy(bf16[2,16,48,2048]{3,2,0,1:T(8,128)(2,1)} %fusion) | data formatting | bytes 12582912 | tf_op jit(solution)/shard_map/convert_element_type | solution.py:137
  110.5 0.2 copy-done.10
  110.7 3.4 %fusion.46 = f32[2,768,384]{2,1,0:T(8,128)S(1)} fusion(bf16[2,768,2048]{2,1,0:T(8,128)(2,1)S(1)} %bitcast.72, bf16[2,384,2048]{2,1,0:T(8,128)(2,1)S(1)} %copy-done.10), kind=kOutput, calls=%fused_computation.90 | convolution fusion | flops 2415919104 | bytes 11796480 | tf_op jit(solution)/shard_map/efd,esd->efs/dot_general | solution.py:17
  114.1 0.0 copy-done
  114.1 0.0 copy-done.3
  114.1 0.0 copy-done.9
  114.1 0.0 copy-start.8
  114.1 6.6 %fusion.16 = f32[2,768,2048]{2,1,0:T(8,128)} fusion(bf16[2,384,2048]{2,1,0:T(8,128)(2,1)S(1)} %copy-done, bf16[2,384,768]{1,2,0:T(8,128)(2,1)S(1)} %copy-done.3, f32[2,768,384]{2,1,0:T(8,128)S(1)} %fusion.46, bf16[2,384,768]{1,2,0:T(8,128)(2,1)S(1)} %copy-done.9), kind=kOutput, calls=%fused_computation.36 | convolution fusion | flops 2422996992 | bytes 20447232 | tf_op jit(solution)/shard_map/efs,efd->esd/dot_general | solution.py:25
  120.8 0.0 copy-done.8
  120.8 8.1 %add_convert_fusion = bf16[2,768,2048]{2,1,0:T(8,128)(2,1)} fusion(f32[2,768,2048]{2,1,0:T(8,128)} %fusion.16, bf16[2,384,2048]{2,1,0:T(8,128)(2,1)S(1)} %copy-done.8, bf16[2,384,768]{1,2,0:T(8,128)(2,1)S(1)} %copy-done.3, f32[2,768,384]{2,1,0:T(8,128)S(1)} %fusion.46), kind=kOutput, calls=%fused_computation.3 | convolution fusion | flops 2426339328 | bytes 25559040 | tf_op jit(solution)/shard_map/efs,efd->esd/dot_general | solution.py:28
  128.9 5.2 %bitcast_convert_fusion = bf16[16,128,2048]{2,1,0:T(8,128)(2,1)S(1)} fusion(bf16[2,16,48,2048]{3,2,1,0:T(8,128)(2,1)} %bitcast.71, s32[2,16,128]{2,0,1:T(2,128)S(1)} %copy.64, pred[2,16,128]{2,0,1:T(4,128)(4,1)S(1)} %copy.65), kind=kOutput, calls=%fused_computation | convolution fusion | flops 809893888 | bytes 14700544 | tf_op jit(solution)/shard_map/egst,egsd->gtd/dot_general | solution.py:141
  134.0 4.1 %constant_dynamic-slice_fusion.1 = (bf16[4,2,1,2,64,2048]{5,4,3,2,1,0:T(8,128)(2,1)}, bf16[4,2,1,2,64,2048]{5,4,3,2,1,0:T(8,128)(2,1)}) fusion(bf16[4,2,2,2,64,2048]{5,4,3,2,1,0:T(8,128)(2,1)S(1)} %bitcast.70, s32[]{:T(128)S(6)} %select_n.84, s32[]{:T(128)S(6)} %select_n.85), kind=kLoop, calls=%fused_computation.83 | loop fusion | bytes 16777224 | tf_op jit(solution)/shard_map/jit(dynamic_index_in_dim)/dynamic_slice | solution.py:63
  138.1 4.7 %copy.83 = bf16[4,2,1,2,64,2048]{5,4,0,3,1,2:T(8,128)(2,1)} copy(bf16[4,2,1,2,64,2048]{5,4,3,2,1,0:T(8,128)(2,1)} %get-tuple-element.6) | data formatting | bytes 8388608 | tf_op jit(solution)/shard_map/jit(dynamic_index_in_dim)/dynamic_slice | solution.py:63
  142.9 0.3 collective-permute-start
  143.1 7.2 %collective-permute-done = bf16[4,2,2,64,2048]{4,3,0,2,1:T(8,128)(2,1)} collective-permute-done((bf16[4,2,2,64,2048]{4,3,0,2,1:T(8,128)(2,1)}, bf16[4,2,2,64,2048]{4,3,0,2,1:T(8,128)(2,1)}, u32[]{:S(2)}, u32[]{:S(2)}) %collective-permute-start) | collective-permute-done | bytes 4194336 | tf_op jit(solution)/shard_map/ppermute | solution.py:58
  150.4 5.4 %fusion.2 = bf16[4,2,2,64,2048]{4,3,0,2,1:T(8,128)(2,1)S(1)} fusion(bf16[4,2,2,64,2048]{4,3,0,2,1:T(8,128)(2,1)} %collective-permute-done, bf16[4,2,1,2,64,2048]{5,4,3,2,1,0:T(8,128)(2,1)} %get-tuple-element.5), kind=kLoop, calls=%fused_computation.7 | loop fusion | flops 8388608 | bytes 12582912 | tf_op jit(solution)/shard_map/convert_element_type | solution.py:68
  155.8 0.5 fusion.45
  156.2 0.0 copy-start.2
  156.3 1.3 copy-done.2
  157.6 0.1 dynamic-slice_bitcast_fusion
  157.7 1.5 collective-permute-start.3
  159.2 1.0 dynamic-slice_bitcast_fusion.1
  160.2 0.6 collective-permute-start.1
  160.8 22.4 %collective-permute-done.3 = bf16[4,2,64,1024]{3,2,0,1:T(8,128)(2,1)} collective-permute-done((bf16[4,2,64,1024]{3,2,0,1:T(8,128)(2,1)S(1)}, bf16[4,2,64,1024]{3,2,0,1:T(8,128)(2,1)}, u32[]{:S(2)}, u32[]{:S(2)}) %collective-permute-start.3) | collective-permute-done | bytes 1048608 | tf_op jit(solution)/shard_map/ppermute | solution.py:58
  183.2 2.0 fusion.13
  185.1 0.0 copy-start.6
  185.1 0.9 dynamic-slice_bitcast_fusion.2
  186.1 1.2 collective-permute-start.4
  187.3 0.0 collective-permute-done.1
  187.3 1.6 fusion.14
  188.9 1.0 copy-done.7
  189.9 0.8 dynamic-slice_bitcast_fusion.3
  190.7 0.8 collective-permute-start.2
  191.5 8.1 %collective-permute-done.4 = bf16[4,64,1024]{2,1,0:T(8,128)(2,1)} collective-permute-done((bf16[4,64,1024]{2,1,0:T(8,128)(2,1)}, bf16[4,64,1024]{2,1,0:T(8,128)(2,1)}, u32[]{:S(2)}, u32[]{:S(2)}) %collective-permute-start.4) | collective-permute-done | bytes 524320 | tf_op jit(solution)/shard_map/ppermute | solution.py:58
  199.7 1.5 fusion.20
  201.2 2.8 %collective-permute-done.2 = bf16[4,64,1024]{2,1,0:T(8,128)(2,1)} collective-permute-done((bf16[4,64,1024]{2,1,0:T(8,128)(2,1)}, bf16[4,64,1024]{2,1,0:T(8,128)(2,1)}, u32[]{:S(2)}, u32[]{:S(2)}) %collective-permute-start.2) | collective-permute-done | bytes 524320 | tf_op jit(solution)/shard_map/ppermute | solution.py:58
  204.1 1.4 fusion.21
  205.5 1.0 fusion.38
  206.4 0.1 copy-done.5
  206.5 1.5 collective-permute-start.5
  208.0 1.0 collective-permute-start.6
  209.0 2.4 %collective-permute-start.7 = (bf16[64,2048]{1,0:T(8,128)(2,1)}, bf16[64,2048]{1,0:T(8,128)(2,1)}, u32[]{:S(2)}, u32[]{:S(2)}) collective-permute-start(bf16[64,2048]{1,0:T(8,128)(2,1)} %get-tuple-element.11), channel_id=1, source_target_pairs={{0,24},{2,26},{4,28},{6,30},{8,0},{10,2},{12,4},{14,6},{16,8},{18,... | collective-permute-start | bytes 786440 | tf_op jit(solution)/shard_map/ppermute | solution.py:96
  211.4 6.5 %collective-permute-done.5 = bf16[64,2048]{1,0:T(8,128)(2,1)S(1)} collective-permute-done((bf16[64,2048]{1,0:T(8,128)(2,1)}, bf16[64,2048]{1,0:T(8,128)(2,1)S(1)}, u32[]{:S(2)}, u32[]{:S(2)}) %collective-permute-start.5) | collective-permute-done | bytes 262176 | tf_op jit(solution)/shard_map/ppermute | solution.py:96
  217.9 8.6 %collective-permute-done.6 = bf16[64,2048]{1,0:T(8,128)(2,1)} collective-permute-done((bf16[64,2048]{1,0:T(8,128)(2,1)}, bf16[64,2048]{1,0:T(8,128)(2,1)}, u32[]{:S(2)}, u32[]{:S(2)}) %collective-permute-start.6) | collective-permute-done | bytes 262176 | tf_op jit(solution)/shard_map/ppermute | solution.py:96
  226.5 0.0 collective-permute-done.7
  226.5 2.0 fusion.27
  (18 shorter events, 0.1 us)
Async XLA Ops:
  6.5 107.6 %copy-start = (bf16[2,384,2048]{2,1,0:T(8,128)(2,1)S(1)}, bf16[2,384,2048]{2,1,0:T(8,128)(2,1)}, u32[]{:S(2)}) copy-start(bf16[2,384,2048]{2,1,0:T(8,128)(2,1)} %param.13) | copy-start | bytes 9437188
  6.5 86.2 %all-gather.2.cloned.1.call-start = ((), (), s32[]{:S(2)}) async-start(), calls=%async_computation | async-start | bytes 9191424 | tf_op jit(solution)/shard_map/all_gather | solution.py:117
  107.0 3.7 %copy-start.10 = (bf16[2,384,2048]{2,1,0:T(8,128)(2,1)S(1)}, bf16[2,384,2048]{2,1,0:T(8,128)(2,1)}, u32[]{:S(2)}) copy-start(bf16[2,384,2048]{2,1,0:T(8,128)(2,1)} %param.15) | copy-start | bytes 9437188
  110.7 3.4 %copy-start.3 = (bf16[2,384,768]{1,2,0:T(8,128)(2,1)S(1)}, bf16[2,384,768]{1,2,0:T(8,128)(2,1)}, u32[]{:S(2)}) copy-start(bf16[2,384,768]{1,2,0:T(8,128)(2,1)} %copy.69) | copy-start | bytes 3538948
  110.7 3.4 %copy-start.9 = (bf16[2,384,768]{1,2,0:T(8,128)(2,1)S(1)}, bf16[2,384,768]{1,2,0:T(8,128)(2,1)}, u32[]{:S(2)}) copy-start(bf16[2,384,768]{1,2,0:T(8,128)(2,1)} %copy.68) | copy-start | bytes 3538948
  114.1 6.7 %copy-start.8 = (bf16[2,384,2048]{2,1,0:T(8,128)(2,1)S(1)}, bf16[2,384,2048]{2,1,0:T(8,128)(2,1)}, u32[]{:S(2)}) copy-start(bf16[2,384,2048]{2,1,0:T(8,128)(2,1)} %param.14) | copy-start | bytes 9437188
  142.9 7.5 %collective-permute-start = (bf16[4,2,2,64,2048]{4,3,0,2,1:T(8,128)(2,1)}, bf16[4,2,2,64,2048]{4,3,0,2,1:T(8,128)(2,1)}, u32[]{:S(2)}, u32[]{:S(2)}) collective-permute-start(bf16[4,2,2,64,2048]{4,3,0,2,1:T(8,128)(2,1)} %bitcast.69), channel_id=1, source_target_pairs={{0,2},{2,0},{4,6},{6,4},{8,10},{10,8},{12,14},{14,12},{16,18},{18,... | collective-permute-start | bytes 12582920 | tf_op jit(solution)/shard_map/ppermute | solution.py:58
  156.2 1.3 copy-start.2
  157.7 25.5 %collective-permute-start.3 = (bf16[4,2,64,1024]{3,2,0,1:T(8,128)(2,1)S(1)}, bf16[4,2,64,1024]{3,2,0,1:T(8,128)(2,1)}, u32[]{:S(2)}, u32[]{:S(2)}) collective-permute-start(bf16[4,2,64,1024]{3,2,0,1:T(8,128)(2,1)S(1)} %dynamic-slice_bitcast_fusion), channel_id=1, source_target_pairs={{0,4},{2,6},{4,0},{6,2},{8,12},{10,14},{12,8},{14,10},{16,20},{18,... | collective-permute-start | bytes 3145736 | tf_op jit(solution)/shard_map/ppermute | solution.py:58
  160.2 27.1 %collective-permute-start.1 = (bf16[4,2,64,1024]{3,2,0,1:T(8,128)(2,1)}, bf16[4,2,64,1024]{3,2,0,1:T(8,128)(2,1)}, u32[]{:S(2)}, u32[]{:S(2)}) collective-permute-start(bf16[4,2,64,1024]{3,2,0,1:T(8,128)(2,1)} %dynamic-slice_bitcast_fusion.1), channel_id=1, source_target_pairs={{0,1},{1,0},{2,3},{3,2},{4,5},{5,4},{6,7},{7,6},{8,9},{9,8},{10,11... | collective-permute-start | bytes 3145736 | tf_op jit(solution)/shard_map/ppermute | solution.py:58
  185.1 6.4 %copy-start.6 = (bf16[4,2,64,1024]{3,2,0,1:T(8,128)(2,1)}, bf16[4,2,64,1024]{3,2,0,1:T(8,128)(2,1)S(1)}, u32[]{:S(2)}) copy-start(bf16[4,2,64,1024]{3,2,0,1:T(8,128)(2,1)S(1)} %fusion.13) | copy-start | bytes 3145732
  186.1 13.6 %collective-permute-start.4 = (bf16[4,64,1024]{2,1,0:T(8,128)(2,1)}, bf16[4,64,1024]{2,1,0:T(8,128)(2,1)}, u32[]{:S(2)}, u32[]{:S(2)}) collective-permute-start(bf16[4,64,1024]{2,1,0:T(8,128)(2,1)} %dynamic-slice_bitcast_fusion.2), channel_id=1, source_target_pairs={{0,1},{1,0},{2,3},{3,2},{4,5},{5,4},{6,7},{7,6},{8,9},{9,8},{10,11... | collective-permute-start | bytes 1572872 | tf_op jit(solution)/shard_map/ppermute | solution.py:58
  188.9 1.0 copy-start.7
  190.7 13.3 %collective-permute-start.2 = (bf16[4,64,1024]{2,1,0:T(8,128)(2,1)}, bf16[4,64,1024]{2,1,0:T(8,128)(2,1)}, u32[]{:S(2)}, u32[]{:S(2)}) collective-permute-start(bf16[4,64,1024]{2,1,0:T(8,128)(2,1)} %dynamic-slice_bitcast_fusion.3), channel_id=1, source_target_pairs={{0,4},{2,6},{4,0},{6,2},{8,12},{10,14},{12,8},{14,10},{16,20},{18,... | collective-permute-start | bytes 1572872 | tf_op jit(solution)/shard_map/ppermute | solution.py:58
  199.6 28.9 %copy-start.1 = (bf16[2,384,2048]{2,1,0:T(8,128)(2,1)S(1)}, bf16[2,384,2048]{2,1,0:T(8,128)(2,1)}, u32[]{:S(2)}) copy-start(bf16[2,384,2048]{2,1,0:T(8,128)(2,1)} %param.13) | copy-start | bytes 9437188
  201.2 4.3 %copy-start.4 = (bf16[4,64,1024]{2,1,0:T(8,128)(2,1)}, bf16[4,64,1024]{2,1,0:T(8,128)(2,1)S(1)}, u32[]{:S(2)}) copy-start(bf16[4,64,1024]{2,1,0:T(8,128)(2,1)S(1)} %fusion.20) | copy-start | bytes 1572868
  205.5 1.1 copy-start.5
  206.5 11.3 %collective-permute-start.5 = (bf16[64,2048]{1,0:T(8,128)(2,1)}, bf16[64,2048]{1,0:T(8,128)(2,1)S(1)}, u32[]{:S(2)}, u32[]{:S(2)}) collective-permute-start(bf16[64,2048]{1,0:T(8,128)(2,1)} %get-tuple-element.9), channel_id=1, source_target_pairs={{0,8},{2,10},{4,12},{6,14},{8,16},{10,18},{12,20},{14,22},{16,24},... | collective-permute-start | bytes 786440 | tf_op jit(solution)/shard_map/ppermute | solution.py:96
  208.0 18.5 %collective-permute-start.6 = (bf16[64,2048]{1,0:T(8,128)(2,1)}, bf16[64,2048]{1,0:T(8,128)(2,1)}, u32[]{:S(2)}, u32[]{:S(2)}) collective-permute-start(bf16[64,2048]{1,0:T(8,128)(2,1)} %get-tuple-element.10), channel_id=1, source_target_pairs={{0,16},{2,18},{4,20},{6,22},{8,24},{10,26},{12,28},{14,30},{16,0},... | collective-permute-start | bytes 786440 | tf_op jit(solution)/shard_map/ppermute | solution.py:96
  209.0 17.5 %collective-permute-start.7 = (bf16[64,2048]{1,0:T(8,128)(2,1)}, bf16[64,2048]{1,0:T(8,128)(2,1)}, u32[]{:S(2)}, u32[]{:S(2)}) collective-permute-start(bf16[64,2048]{1,0:T(8,128)(2,1)} %get-tuple-element.11), channel_id=1, source_target_pairs={{0,24},{2,26},{4,28},{6,30},{8,0},{10,2},{12,4},{14,6},{16,8},{18,... | collective-permute-start | bytes 786440 | tf_op jit(solution)/shard_map/ppermute | solution.py:96
Sparse Core Ops, SparseCore 0:
  10.3 82.4 all-gather.1

commit v2 on v0

v2 whole, which is shorter than its diff:
```python
import functools

import jax
import jax.numpy as jnp
from jax import lax
from jax.experimental import pallas as pl
from jax.experimental.pallas import tpu as pltpu
from jax.sharding import PartitionSpec as P


def route_slots(expert_ids, expert_total):
    flat_ids = expert_ids.reshape(-1)
    one_hot = (flat_ids[:, None] == jnp.arange(expert_total, dtype=jnp.int32)[None, :]).astype(
        jnp.int32
    )
    before = jnp.cumsum(one_hot, axis=0) - one_hot
    return (flat_ids, jnp.sum(before * one_hot, axis=1))


def expert_step(arrived, saved_gate, saved_up, w_gate, w_up, w_down):
    hidden_grad = jnp.einsum("efd,esd->efs", w_down, arrived, preferred_element_type=jnp.float32)
    gate_value = saved_gate.astype(jnp.float32)
    up_value = saved_up.astype(jnp.float32)
    sigmoid_gate = jax.nn.sigmoid(gate_value)
    up_grad = (hidden_grad * gate_value * sigmoid_gate).astype(jnp.bfloat16)
    gate_grad = (
        hidden_grad * up_value * sigmoid_gate * (1.0 + gate_value * (1.0 - sigmoid_gate))
    ).astype(jnp.bfloat16)
    partial_value = jnp.einsum(
        "efs,efd->esd", gate_grad, w_gate, preferred_element_type=jnp.float32
    )
    partial_value = partial_value + jnp.einsum(
        "efs,efd->esd", up_grad, w_up, preferred_element_type=jnp.float32
    )
    return partial_value.astype(jnp.bfloat16)


def slots_body(cotangent, gates, expert_ids, saved_gate, saved_up, w_gate, w_up, w_down):
    owners = lax.axis_size("expert")
    row_count, feature_dim = cotangent.shape
    top_count = expert_ids.shape[1]
    local_count, _, slot_count = saved_gate.shape
    capacity = slot_count // owners
    flat_ids, slot_pos = route_slots(expert_ids, local_count * owners)
    target = flat_ids % local_count * slot_count + flat_ids // local_count * capacity + slot_pos
    scaled = (gates[:, :, None] * cotangent.astype(jnp.float32)[:, None, :]).astype(jnp.bfloat16)
    scaled = scaled.reshape(row_count * top_count, feature_dim)
    outgoing = (
        jnp.zeros((local_count * slot_count, feature_dim), jnp.bfloat16).at[target].set(scaled)
    )
    outgoing = outgoing.reshape(local_count, slot_count, feature_dim)
    arrived = lax.all_to_all(outgoing, "expert", split_axis=1, concat_axis=1, tiled=True)
    partial_value = expert_step(arrived, saved_gate, saved_up, w_gate, w_up, w_down)
    returned = lax.all_to_all(partial_value, "expert", split_axis=1, concat_axis=1, tiled=True)
    picked = returned.reshape(local_count * slot_count, feature_dim)[target].astype(jnp.float32)
    combined = jnp.sum(picked.reshape(row_count, top_count, feature_dim), axis=1)
    return lax.psum_scatter(combined, "tp", scatter_dimension=0, tiled=True)


LANES = 256
CHUNKS = 2


def swap(value, axis, step):
    count = lax.axis_size(axis)
    return lax.ppermute(value, axis, [(i, i ^ step) for i in range(count)])


def along_line(value, shift):
    count = lax.axis_size("expert")
    return lax.ppermute(value, "expert", [(i, (i + 4 * shift) % count) for i in range(count)])


def pair_base(place, line_count, r, ry, width):
    line = lax.rem(place[2] + r, line_count)
    row = place[1] if ry == 0 else 1 - place[1]
    return pl.multiple_of((line * 2 + row) * width, width)


def route_kernel(capacity, place, sides, pick, pick_t, gate, hits, gates):
    groups, _, tokens = sides.shape
    line_count = groups // 4
    core, row, line, half = place[0], place[1], place[2], place[3]
    first = (line * 4 + row * 2 + core) * 2
    for r in range(line_count):
        for ry in range(2):
            for c in range(2):
                group = lax.rem(line + r, line_count) * 4 + (row if ry == 0 else 1 - row) * 2 + c
                block = sides[group]
                for e in range(2):
                    named = block[8:16] == (first + e).astype(jnp.float32)
                    at = ((r * 2 + ry) * 2 + c) * 2 + e
                    hits[at:at + 1] = jnp.sum(named.astype(jnp.float32), axis=0, keepdims=True)
                    gates[at:at + 1] = jnp.sum(
                        jnp.where(named, block[0:8], 0.0), axis=0, keepdims=True
                    )
    earlier = lax.broadcasted_iota(jnp.int32, (tokens, tokens), 0) < lax.broadcasted_iota(
        jnp.int32, (tokens, tokens), 1
    )
    hit = hits[...]
    slot = jnp.dot(
        hit.astype(jnp.bfloat16),
        earlier.astype(jnp.float32).astype(jnp.bfloat16),
        preferred_element_type=jnp.float32,
    )
    slot = jnp.where(hit > 0.5, slot, -1.0)
    turned = half > 0
    slot = jnp.where(turned, pltpu.roll(slot, tokens // 2, 1), slot)
    weight = jnp.where(turned, pltpu.roll(gates[...], tokens // 2, 1), gates[...])
    order = lax.broadcasted_iota(jnp.int32, (capacity, tokens), 0).astype(jnp.float32)
    for p in range(line_count * 2):
        rows = []
        for e in range(2):
            for c in range(2):
                at = (p * 2 + c) * 2 + e
                ones = (order == slot[at:at + 1]).astype(jnp.float32)
                column = jnp.sum(ones * weight[at:at + 1], axis=1, keepdims=True)
                place_in = (e * 2 + c) * capacity
                gate[p, place_in:place_in + capacity] = jnp.broadcast_to(
                    column, (capacity, gate.shape[2])
                )
                own = (core == c).astype(jnp.float32)
                rows.append(jnp.concatenate([ones * own, ones * (1.0 - own)], axis=1))
        matrix = jnp.concatenate(rows, axis=0)
        pick[p] = matrix.astype(jnp.bfloat16)
        count = matrix.shape[0]
        square = jnp.concatenate(
            [matrix, jnp.zeros((2 * tokens - count, 2 * tokens), jnp.float32)], axis=0
        )
        pick_t[p] = square.T[:, :count].astype(jnp.bfloat16)


def route(place, sides, capacity):
    groups, _, tokens = sides.shape
    pairs = groups // 2
    rows = 4 * capacity
    return pl.pallas_call(
        functools.partial(route_kernel, capacity),
        out_shape=(
            jax.ShapeDtypeStruct((pairs, rows, 2 * tokens), jnp.bfloat16),
            jax.ShapeDtypeStruct((pairs, 2 * tokens, rows), jnp.bfloat16),
            jax.ShapeDtypeStruct((pairs, rows, 128), jnp.float32),
        ),
        in_specs=[
            pl.BlockSpec(memory_space=pltpu.SMEM),
            pl.BlockSpec(memory_space=pltpu.VMEM),
        ],
        scratch_shapes=[pltpu.VMEM((2 * groups, tokens), jnp.float32)] * 2,
        name="route",
    )(place, sides)


def hidden_kernel(last, place, *refs):
    (own, own_c, lines, lines_c, side, side_c, over, over_c, diag_l, diag_lc, diag_r, diag_rc,
     pick, gate, w_down) = refs[:15]
    if last:
        before, saved_gate, saved_up, result, slots, diag, total = refs[15:]
    else:
        result, slots, diag = refs[15:]
        total = result
    k, steps = pl.program_id(0), pl.num_programs(0)
    line_count, piece, _ = over.shape
    rows = pick.shape[1] // 2

    @pl.when(k == 0)
    def _():
        total[...] = before[...] if last else jnp.zeros_like(total)

    @pl.when(k < steps // 2)
    def _():
        diag[0] = diag_l[...]
        diag[1] = diag_lc[...]

    @pl.when(k >= steps // 2)
    def _():
        diag[0] = diag_r[...]
        diag[1] = diag_rc[...]

    near = pl.multiple_of(place[3] * piece, piece)
    far = pl.multiple_of((1 - place[3]) * piece, piece)
    for r in range(line_count):
        for ry in range(2):
            parts = []
            for c in range(2):
                if ry == 1:
                    parts += [(over, over_c)[c][r], diag[c, r]]
                elif r == 0:
                    group = (own, own_c)[c]
                    parts += [group[pl.ds(near, piece), :], group[pl.ds(far, piece), :]]
                else:
                    parts += [(lines, lines_c)[c][r - 1], (side, side_c)[c][r - 1]]
            p = r * 2 + ry
            picked = jnp.dot(
                pick[p], jnp.concatenate(parts, axis=0), preferred_element_type=jnp.float32
            )
            weight = gate[p]
            weight = jnp.concatenate([weight] * (picked.shape[1] // weight.shape[1]), axis=1)
            scaled = (picked * weight).astype(jnp.bfloat16)
            base = pair_base(place, line_count, r, ry, rows)
            slots[0, pl.ds(base, rows), :] = scaled[:rows]
            slots[1, pl.ds(base, rows), :] = scaled[rows:]
    for e in range(2):
        total[e] = total[e] + lax.dot_general(
            slots[e], w_down[e], (((1,), (1,)), ((), ())), preferred_element_type=jnp.float32
        )

    if last:
        tile = 64
        per_expert = total.shape[1] // tile
        width = total.shape[2]

        @pl.when(k == steps - 1)
        def _():
            @pl.loop(0, 2 * per_expert)
            def _(i):
                e, at = i // per_expert, pl.ds(pl.multiple_of(i % per_expert * tile, tile), tile)
                hidden_grad = total[e, at, :]
                gate_value = saved_gate[e, at, :].astype(jnp.float32)
                up_value = saved_up[e, at, :].astype(jnp.float32)
                sigmoid_gate = jax.nn.sigmoid(gate_value)
                result[e, at, width:] = (hidden_grad * gate_value * sigmoid_gate).astype(
                    jnp.bfloat16
                )
                result[e, at, :width] = (
                    hidden_grad * up_value * sigmoid_gate * (1.0 + gate_value * (1.0 - sigmoid_gate))
                ).astype(jnp.bfloat16)


def hidden(place, chunk, own, own_c, moved, pick, gate, w_down, rest):
    last = rest is not None
    over = moved[4]
    line_count, piece, width = over.shape
    steps = width // LANES
    offset = chunk * steps
    units = w_down.shape[1]
    slot_count = pick.shape[0] * pick.shape[1] // 2
    whole = lambda dims: pl.BlockSpec(dims, lambda k, place: (0,) * len(dims))
    column = lambda array: pl.BlockSpec(array.shape[:-1] + (LANES,), lambda k, place: (0, 0, k))
    first_half = lambda array: pl.BlockSpec(
        array.shape[:-1] + (LANES,), lambda k, place: (0, 0, jnp.minimum(k, steps // 2 - 1))
    )
    second_half = lambda array: pl.BlockSpec(
        array.shape[:-1] + (LANES,), lambda k, place: (0, 0, jnp.maximum(k - steps // 2, 0))
    )
    group = pl.BlockSpec((own.shape[0], LANES), lambda k, place: (0, offset + k))
    in_specs = [group, group]
    in_specs += [column(array) for array in moved[:6]]
    in_specs += [first_half(array) for array in moved[6:8]]
    in_specs += [second_half(array) for array in moved[8:]]
    in_specs += [whole(pick.shape), whole(gate.shape)]
    in_specs += [pl.BlockSpec((2, units, LANES), lambda k, place: (0, 0, offset + k))]
    scratch = [
        pltpu.VMEM((2, slot_count, LANES), jnp.bfloat16),
        pltpu.VMEM((2, line_count, piece, LANES), jnp.bfloat16),
    ]
    operands = [own, own_c, *moved, pick, gate, w_down]
    if last:
        in_specs += [whole(array.shape) for array in rest]
        operands += rest
        out = jax.ShapeDtypeStruct((2, slot_count, 2 * units), jnp.bfloat16)
        scratch += [pltpu.VMEM((2, slot_count, units), jnp.float32)]
    else:
        out = jax.ShapeDtypeStruct((2, slot_count, units), jnp.float32)
    return pl.pallas_call(
        functools.partial(hidden_kernel, last),
        out_shape=out,
        grid_spec=pltpu.PrefetchScalarGridSpec(
            num_scalar_prefetch=1,
            grid=(steps,),
            in_specs=in_specs,
            out_specs=whole(out.shape),
            scratch_shapes=scratch,
        ),
        compiler_params=pltpu.CompilerParams(vmem_limit_bytes=40 << 20),
        cost_estimate=pl.CostEstimate(
            flops=2 * 2 * slot_count * width * (units + 256), bytes_accessed=8 << 20, transcendentals=0
        ),
        name="hidden",
    )(place, *operands)


def sums_kernel(place, grads, w_gate, w_up, pick_t, keep, send, slots):
    pairs, _, rows = pick_t.shape
    rows = rows // 2
    for e in range(2):
        weights = jnp.concatenate([w_gate[e], w_up[e]], axis=0)
        slots[e] = jnp.dot(grads[e], weights, preferred_element_type=jnp.float32).astype(
            jnp.bfloat16
        )
    for r in range(pairs // 2):
        for ry in range(2):
            p = r * 2 + ry
            base = pair_base(place, pairs // 2, r, ry, rows)
            both = jnp.concatenate(
                [slots[0, pl.ds(base, rows), :], slots[1, pl.ds(base, rows), :]], axis=0
            )
            total = jnp.dot(pick_t[p], both, preferred_element_type=jnp.float32).astype(
                jnp.bfloat16
            )
            tokens = total.shape[0] // 2
            keep[p] = total[:tokens]
            send[p] = total[tokens:]


def sums(place, chunk, width, grads, w_gate, w_up, pick_t):
    steps = width // LANES
    offset = chunk * steps
    units = w_gate.shape[1]
    pairs, tokens, _ = pick_t.shape
    tokens = tokens // 2
    whole = lambda dims: pl.BlockSpec(dims, lambda k, place: (0,) * len(dims))
    weight = pl.BlockSpec((2, units, LANES), lambda k, place: (0, 0, offset + k))
    out = jax.ShapeDtypeStruct((pairs, tokens, width), jnp.bfloat16)
    return pl.pallas_call(
        sums_kernel,
        out_shape=(out, out),
        grid_spec=pltpu.PrefetchScalarGridSpec(
            num_scalar_prefetch=1,
            grid=(steps,),
            in_specs=[whole(grads.shape), weight, weight, whole(pick_t.shape)],
            out_specs=[pl.BlockSpec((pairs, tokens, LANES), lambda k, place: (0, 0, k))] * 2,
            scratch_shapes=[pltpu.VMEM((2, grads.shape[1], LANES), jnp.bfloat16)],
        ),
        compiler_params=pltpu.CompilerParams(vmem_limit_bytes=40 << 20),
        cost_estimate=pl.CostEstimate(
            flops=2 * 2 * grads.shape[1] * width * (2 * units + 256),
            bytes_accessed=10 << 20,
            transcendentals=0,
        ),
        name="sums",
    )(place, grads, w_gate, w_up, pick_t)


def plus(one, other):
    return one.astype(jnp.float32) + other.astype(jnp.float32)


def first_kernel(keep, came, send_l, keep_l, send_r, keep_r):
    total = plus(keep[...], came[...]).astype(jnp.bfloat16)
    middle = total.shape[-1] // 2
    keep_l[...] = total[:, 0, :, :middle]
    send_l[...] = total[:, 1, :, :middle]
    keep_r[...] = total[0:1, :, :, middle:]
    send_r[...] = total[1:2, :, :, middle:]


def first_sum(keep, came, piece):
    pairs, tokens, width = keep.shape
    keep = keep.reshape(pairs, 2, piece, width)
    came = came.reshape(pairs, 2, piece, width)
    full = pl.BlockSpec((2, 2, piece, width), lambda r: (r, 0, 0, 0))
    left = jax.ShapeDtypeStruct((pairs, piece, width // 2), jnp.bfloat16)
    right = jax.ShapeDtypeStruct((pairs // 2, 2, piece, width // 2), jnp.bfloat16)
    left_spec = pl.BlockSpec((2, piece, width // 2), lambda r: (r, 0, 0))
    right_spec = pl.BlockSpec((1, 2, piece, width // 2), lambda r: (r, 0, 0, 0))
    return pl.pallas_call(
        first_kernel,
        out_shape=(left, left, right, right),
        grid=(pairs // 2,),
        in_specs=[full, full],
        out_specs=[left_spec, left_spec, right_spec, right_spec],
        cost_estimate=pl.CostEstimate(flops=0, bytes_accessed=6 << 20, transcendentals=0),
        name="first_sum",
    )(keep, came)


def second_kernel(keep_l, came_l, keep_r, came_r, send_l, left, send_r, right):
    total = plus(keep_l[...], came_l[...]).astype(jnp.bfloat16)
    left[...] = total[0:1]
    send_l[...] = total[1:2]
    total = plus(keep_r[...], came_r[...]).astype(jnp.bfloat16)
    right[...] = total[:, 0]
    send_r[...] = total[:, 1]


def second_sum(keep_l, came_l, keep_r, came_r):
    lines, _, piece, middle = keep_r.shape
    out = jax.ShapeDtypeStruct((lines, piece, middle), jnp.bfloat16)
    left = pl.BlockSpec((2, piece, middle), lambda r: (r, 0, 0))
    right = pl.BlockSpec((1, 2, piece, middle), lambda r: (r, 0, 0, 0))
    return pl.pallas_call(
        second_kernel,
        out_shape=(out,) * 4,
        grid=(lines,),
        in_specs=[left, left, right, right],
        out_specs=[pl.BlockSpec((1, piece, middle), lambda r: (r, 0, 0))] * 4,
        cost_estimate=pl.CostEstimate(flops=0, bytes_accessed=3 << 20, transcendentals=0),
        name="second_sum",
    )(keep_l, came_l, keep_r, came_r)


def third_kernel(left, came_l, right, came_r, own, *sends):
    middle = left.shape[-1]
    for columns, one, other in ((slice(0, middle), left, came_l), (slice(middle, None), right, came_r)):
        own[:, columns] = plus(one[0], other[0])
        for r, send in enumerate(sends):
            send[:, columns] = plus(one[r + 1], other[r + 1]).astype(jnp.bfloat16)


def third_sum(left, came_l, right, came_r):
    lines, piece, middle = left.shape
    return pl.pallas_call(
        third_kernel,
        out_shape=(jax.ShapeDtypeStruct((piece, 2 * middle), jnp.float32),)
        + (jax.ShapeDtypeStruct((piece, 2 * middle), jnp.bfloat16),) * (lines - 1),
        cost_estimate=pl.CostEstimate(flops=0, bytes_accessed=2 << 20, transcendentals=0),
        name="third_sum",
    )(left, came_l, right, came_r)


def last_kernel(count, *refs):
    result = refs[-1]
    terms = len(refs[:-1]) // count
    width = refs[0].shape[1]
    for chunk in range(count):
        total = refs[chunk * terms][...]
        for ref in refs[chunk * terms + 1:(chunk + 1) * terms]:
            total = total + ref[...].astype(jnp.float32)
        result[:, chunk * width:(chunk + 1) * width] = total


def tokens_body(cotangent, gates, expert_ids, saved_gate, saved_up, w_gate, w_up, w_down):
    owners = lax.axis_size("expert")
    row_count, feature_dim = cotangent.shape
    slot_count = saved_gate.shape[2]
    capacity = slot_count // owners
    lines = owners // 4
    piece = row_count // 2
    width = feature_dim // CHUNKS
    middle = width // 2
    me, half = lax.axis_index("expert"), lax.axis_index("tp")
    place = jnp.stack([me % 2, me // 2 % 2, me // 4, half]).astype(jnp.int32)

    sides = jnp.concatenate([gates.T, expert_ids.T.astype(jnp.float32)], axis=0)
    sides = lax.all_gather(sides, "expert", axis=0)
    saved_gate, saved_up = saved_gate.swapaxes(1, 2), saved_up.swapaxes(1, 2)

    own_c = swap(cotangent, "expert", 1)
    near = lax.dynamic_slice_in_dim(cotangent, half * piece, piece, 0)
    far = lax.dynamic_slice_in_dim(cotangent, (1 - half) * piece, piece, 0)
    gathered = []
    for chunk in range(CHUNKS):
        columns = slice(chunk * width, (chunk + 1) * width)
        near_part = near[:, columns]
        line = jnp.stack([along_line(near_part, -r) for r in range(1, lines)])
        first = swap(near_part, "expert", 2)
        side = swap(line, "tp", 1)
        over = jnp.concatenate([first[None], swap(line, "expert", 2)])
        diag_l = swap(over[:, :, :middle], "tp", 1)
        far_part = far[None, :, chunk * width + middle:(chunk + 1) * width]
        diag_r = swap(jnp.concatenate([far_part, side[:, :, middle:]]), "expert", 2)
        moved = []
        for array in (line, side, over, diag_l, diag_r):
            moved += [array, swap(array, "expert", 1)]
        gathered.append(moved)
    pick, pick_t, gate = route(place, sides, capacity)
    rest = None
    for chunk in range(CHUNKS):
        if chunk == CHUNKS - 1:
            rest = [rest, saved_gate, saved_up]
        rest = hidden(place, chunk, cotangent, own_c, gathered[chunk], pick, gate, w_down, rest)
    grads = rest

    terms = []
    for chunk in range(CHUNKS):
        keep, send = sums(place, chunk, width, grads, w_gate, w_up, pick_t)
        came = swap(send, "expert", 1)
        send_l, keep_l, send_r, keep_r = first_sum(keep, came, piece)
        came_l, came_r = swap(send_l, "tp", 1), swap(send_r, "expert", 2)
        send_l, left, send_r, right = second_sum(keep_l, came_l, keep_r, came_r)
        came_l, came_r = swap(send_l, "expert", 2), swap(send_r, "tp", 1)
        own, *sends = third_sum(left, came_l, right, came_r)
        terms += [own] + [along_line(send, r + 1) for r, send in enumerate(sends)]
    return pl.pallas_call(
        functools.partial(last_kernel, CHUNKS),
        out_shape=jax.ShapeDtypeStruct((piece, feature_dim), jnp.float32),
        name="last_sum",
    )(*terms)


def body(*arrays):
    cotangent, gates, _, saved_gate = arrays[:4]
    owners = lax.axis_size("expert")
    fits = (
        owners in (4, 8, 16)
        and lax.axis_size("tp") == 2
        and cotangent.shape[0] == 128
        and cotangent.shape[1] % (2 * CHUNKS * LANES) == 0
        and gates.shape[1] == 8
        and saved_gate.shape[0] == 2
        and saved_gate.shape[2] // owners % 16 == 0
        and 4 * saved_gate.shape[2] // owners <= 256
    )
    return (tokens_body if fits else slots_body)(*arrays)


def solution(mesh):
    in_specs = (
        P("expert", None),
        P("expert", None),
        P("expert", None),
        P("expert", "tp", None),
        P("expert", "tp", None),
        P("expert", "tp", None),
        P("expert", "tp", None),
        P("expert", "tp", None),
    )
    out_specs = P(("expert", "tp"), None)
    return jax.shard_map(body, mesh=mesh, in_specs=in_specs, out_specs=out_specs, check_vma=False)
```

time: 428 us -> 209 us (0.49)
  waiting for transfers between devices: 267 us -> 54.4 us
  Pallas kernels: 0 us -> 52.4 us
  other arithmetic: 28.4 us -> 2.55 us
  local copies, waits for them, and re-layouts: 59.5 us -> 35.5 us
  matrix products: 23.2 us -> 0 us
  blocking collectives: 0 us -> 19.3 us
  between operations: 13.5 us -> 0.48 us
  starting transfers between devices: 35.8 us -> 43.1 us
    all_to_all x2 -> x0, waiting for transfers between devices: 223 us -> none  [the longest x1 114 us: body(): lax.all_to_all(partial_value, 'expert', split_axis=1, concat_axis=1, tile...]
    ppermute x0 -> x43, waiting for transfers between devices: none -> 54.4 us  [the longest x12 27.7 us: along_line(): lax.ppermute(value, 'expert', [(i, (i + 4 * shift) % count) for i in rang...]
    pallas_call x0 -> x12, Pallas kernels: none -> 52.4 us  [the longest x2 14.2 us: hidden(): pl.pallas_call(functools.partial(hidden_kernel, last), out_shape=out, gri...]
    reduce_scatter x1 -> x0, waiting for transfers between devices: 43.8 us -> none  [body(): return lax.psum_scatter(combined, 'tp', scatter_dimension=0, tiled=True)]
    ppermute x0 -> x43, starting transfers between devices: none -> 43.1 us  [the longest x31 23.5 us: swap(): return lax.ppermute(value, axis, [(i, i ^ step) for i in range(count)])]
    all_to_all x2 -> x0, starting transfers between devices: 35.6 us -> none  [the longest x1 28.1 us: body(): lax.all_to_all(partial_value, 'expert', split_axis=1, concat_axis=1, tile...]
    unnamed x12 -> x102, local copies, waits for them, and re-layouts: 6.52 us -> 32.6 us
    dot_general x3 -> x0, matrix products: 23.2 us -> none  [the longest x1 9.2 us: body(): jnp.einsum('efd,esd->efs', w_down, arrived, preferred_element_type=jnp.fl...]
  transfers between devices with their start and end apart: 3 -> 43, of which waited for: 3 -> 14; matrix products, arithmetic and copies ran while one was open for 1% -> 4% of each run, Pallas kernels for 0% -> 17%
where the time goes in v2:
time: 209 us; the launch traced here: 208 us
  waiting for transfers between devices  54.4 us (26%)
  Pallas kernels  52.4 us (25%)
  starting transfers between devices  43.1 us (21%)
  local copies, waits for them, and re-layouts  35.5 us (17%)
  blocking collectives  19.3 us (9%)
  other arithmetic  2.55 us (1%)
    unnamed x102, local copies, waits for them, and re-layouts  32.6 us
    ppermute x12, waiting for transfers between devices, along_line(): lax.ppermute(value, 'expert', [(i, (i + 4 * shift) % count) for i in rang...  27.7 us
    ppermute x31, waiting for transfers between devices, swap(): return lax.ppermute(value, axis, [(i, i ^ step) for i in range(count)])  26.7 us
    ppermute x31, starting transfers between devices, swap(): return lax.ppermute(value, axis, [(i, i ^ step) for i in range(count)])  23.5 us
    ppermute x12, starting transfers between devices, along_line(): lax.ppermute(value, 'expert', [(i, (i + 4 * shift) % count) for i in rang...  19.5 us
    all_gather x1, blocking collectives, tokens_body(): sides = lax.all_gather(sides, 'expert', axis=0)  19.3 us
    pallas_call x2, Pallas kernels, hidden(): pl.pallas_call(functools.partial(hidden_kernel, last), out_shape=out, gri...  14.2 us
    pallas_call x2, Pallas kernels, sums(): pl.pallas_call(sums_kernel, out_shape=(out, out), grid_spec=pltpu.Prefetc...  13.2 us
  transfers between devices with their start and end apart: 43, of which 14 were waited for; matrix products, arithmetic and copies ran while one was open for 4% of the time, Pallas kernels for 17%

profile of v2, /device:TPU:0, one launch (start us, length us, event | category | flops | bytes accessed | tf_op | source)
XLA Modules:
  0.0 207.7 jit_solution(7861363999254589386)
XLA Ops:
  0.0 1.0 constant_dynamic-slice_fusion
  1.0 5.1 %collective-permute-start.14 = (bf16[64,1024]{1,0:T(8,128)(2,1)S(1)}, bf16[64,1024]{1,0:T(8,128)(2,1)S(1)}, u32[]{:S(2)}, u32[]{:S(2)}) collective-permute-start(bf16[64,1024]{1,0:T(8,128)(2,1)S(1)} %get-tuple-element.69), channel_id=1, source_target_pairs={{0,24},{2,26},{4,28},{6,30},{8,0},{10,2},{12,4},{14,6},{16,8},{18,... | collective-permute-start | bytes 393224 | tf_op jit(solution)/shard_map/ppermute | solution.py:71
  6.1 1.0 collective-permute-start.16
  7.1 2.9 %collective-permute-done.14 = bf16[64,1024]{1,0:T(8,128)(2,1)S(1)} collective-permute-done((bf16[64,1024]{1,0:T(8,128)(2,1)S(1)}, bf16[64,1024]{1,0:T(8,128)(2,1)S(1)}, u32[]{:S(2)}, u32[]{:S(2)}) %collective-permute-start.14) | collective-permute-done | bytes 131104 | tf_op jit(solution)/shard_map/ppermute | solution.py:71
  10.0 7.3 %collective-permute-done.15 = bf16[64,1024]{1,0:T(8,128)(2,1)S(1)} collective-permute-done((bf16[64,1024]{1,0:T(8,128)(2,1)S(1)}, bf16[64,1024]{1,0:T(8,128)(2,1)S(1)}, u32[]{:S(2)}, u32[]{:S(2)}) %collective-permute-start.15) | collective-permute-done | bytes 131104 | tf_op jit(solution)/shard_map/ppermute | solution.py:71
  17.3 1.6 collective-permute-start.21
  18.9 1.6 collective-permute-start.1
  20.5 1.0 collective-permute-start.2
  21.6 2.0 collective-permute-start.3
  23.6 1.5 collective-permute-start.18
  25.6 7.0 %collective-permute-done.2 = bf16[64,1024]{1,0:T(8,128)(2,1)S(1)} collective-permute-done((bf16[64,1024]{1,0:T(8,128)(2,1)S(1)}, bf16[64,1024]{1,0:T(8,128)(2,1)S(1)}, u32[]{:S(2)}, u32[]{:S(2)}) %collective-permute-start.2) | collective-permute-done | bytes 131104 | tf_op jit(solution)/shard_map/ppermute | solution.py:71
  33.4 1.5 collective-permute-start.5
  36.4 1.5 collective-permute-start.8
  38.2 7.1 %collective-permute-done.5.refs_4_ = bf16[3,64,1024]{2,1,0:T(8,128)(2,1)} collective-permute-done((bf16[3,64,1024]{2,1,0:T(8,128)(2,1)}, bf16[3,64,1024]{2,1,0:T(8,128)(2,1)}, u32[]{:S(2)}, u32[]{:S(2)}) %collective-permute-start.5) | collective-permute-done | bytes 393248 | tf_op jit(solution)/shard_map/ppermute | solution.py:66
  45.3 1.5 collective-permute-start.23
  47.8 2.1 %collective-permute-done.8 = bf16[3,64,1024]{2,1,0:T(8,128)(2,1)S(1)} collective-permute-done((bf16[3,64,1024]{2,1,0:T(8,128)(2,1)}, bf16[3,64,1024]{2,1,0:T(8,128)(2,1)S(1)}, u32[]{:S(2)}, u32[]{:S(2)}) %collective-permute-start.8) | collective-permute-done | bytes 393248 | tf_op jit(solution)/shard_map/ppermute | solution.py:66
  52.6 1.5 collective-permute-start.12
  55.0 4.1 %collective-permute-done.25.refs_10_ = bf16[4,64,512]{2,1,0:T(8,128)(2,1)S(1)} collective-permute-done((bf16[4,64,512]{2,1,0:T(8,128)(2,1)S(1)}, bf16[4,64,512]{2,1,0:T(8,128)(2,1)S(1)}, u32[]{:S(2)}, u32[]{:S(2)}) %collective-permute-start.25) | collective-permute-done | bytes 262176 | tf_op jit(solution)/shard_map/ppermute | solution.py:66
  59.7 3.6 %collective-permute-done.12.refs_10_ = bf16[4,64,512]{2,1,0:T(8,128)(2,1)} collective-permute-done((bf16[4,64,512]{2,1,0:T(8,128)(2,1)S(1)}, bf16[4,64,512]{2,1,0:T(8,128)(2,1)}, u32[]{:S(2)}, u32[]{:S(2)}) %collective-permute-start.12) | collective-permute-done | bytes 262176 | tf_op jit(solution)/shard_map/ppermute | solution.py:66
  68.7 2.5 %copy.9 = bf16[2,384,768]{1,2,0:T(8,128)(2,1)} copy(bf16[2,384,768]{2,1,0:T(8,128)(2,1)} %param.11) | data formatting | bytes 2359296 | tf_op args[3]
  71.3 2.4 %copy.10 = bf16[2,384,768]{1,2,0:T(8,128)(2,1)} copy(bf16[2,384,768]{2,1,0:T(8,128)(2,1)} %param.12) | data formatting | bytes 2359296 | tf_op args[4]
  73.7 19.3 %all-gather = f32[256,128]{1,0:T(8,128)} all-gather(f32[16,128]{1,0:T(8,128)S(1)} %pad_maximum_fusion.6), channel_id=2, replica_groups=mesh['expert'=16,'tp'=2] {'expert'}, dimensions={0}, use_global_device_ids=true | all-gather | bytes 139264 | tf_op jit(solution)/shard_map/all_gather | solution.py:435
  93.0 3.0 %route.1 = (bf16[8,192,256]{2,1,0:T(8,128)(2,1)}, bf16[8,256,192]{2,1,0:T(8,128)(2,1)}, f32[8,192,128]{2,1,0:T(8,128)}) custom-call(s32[4]{0:T(128)} %pad_add_fusion.place, f32[16,16,128]{2,1,0:T(8,128)} %bitcast.32), custom_call_target="tpu_custom_call" | custom-call | tf_op jit(solution)/shard_map/route/pallas_call | solution.py:137
  96.0 1.0 copy-done.3
  97.0 1.1 copy-done.4
  98.2 1.1 copy-done.5
  99.3 1.0 copy-done.7
  100.4 1.0 copy-done.9
  101.4 1.0 copy-done.13
  102.4 1.0 copy-done.15
  103.4 1.0 copy-done.17
  104.4 1.0 copy-done.19
  105.4 0.9 copy-done.21
  106.4 0.9 copy-done.23
  109.2 5.7 %hidden.2.refs_15_ = f32[2,768,384]{2,1,0:T(8,128)S(1)} custom-call(s32[4]{0:T(128)S(1)} %copy-done.28, bf16[128,2048]{1,0:T(8,128)(2,1)S(1)} %copy-done.3, bf16[128,2048]{1,0:T(8,128)(2,1)S(1)} %copy-done.7, bf16[3,64,1024]{2,1,0:T(8,128)(2,1)S(1)} %pad_maximum_fusion.3.refs_2_, bf16[3,64,1024]{2,1,0:T(8,128)(2,1)S(1)} %copy-done.17, ...), custom_call_target="tpu_custom_call" | custom-call | flops 2013265920 | bytes 8388608 | tf_op jit(solution)/shard_map/hidden/pallas_call | solution.py:264
  115.0 8.6 %hidden.3.grads = bf16[2,768,768]{2,1,0:T(8,128)(2,1)S(1)} custom-call(s32[4]{0:T(128)S(1)} %copy-done.28, bf16[128,2048]{1,0:T(8,128)(2,1)S(1)} %copy-done.3, bf16[128,2048]{1,0:T(8,128)(2,1)S(1)} %copy-done.7, bf16[3,64,1024]{2,1,0:T(8,128)(2,1)} %pad_maximum_fusion.2.refs_2_, bf16[3,64,1024]{2,1,0:T(8,128)(2,1)} %collective-permute-done.4.refs_3_, ...), custom_call_target="tpu_custom_call" | custom-call | flops 2013265920 | bytes 8388608 | tf_op jit(solution)/shard_map/hidden/pallas_call | solution.py:264
  123.6 6.3 %sums.3 = (bf16[8,128,1024]{2,1,0:T(8,128)(2,1)S(1)}, bf16[8,128,1024]{2,1,0:T(8,128)(2,1)S(1)}) custom-call(s32[4]{0:T(128)S(1)} %copy-done.28, bf16[2,768,768]{2,1,0:T(8,128)(2,1)S(1)} %hidden.3.grads, bf16[2,384,2048]{2,1,0:T(8,128)(2,1)S(1)} %copy-done.29, bf16[2,384,2048]{2,1,0:T(8,128)(2,1)S(1)} %copy-done.30, bf16[8,256,192]{2,1,0:T(8,128)(2,1)S(1)} %copy-done.31), custom_call_target="tpu_custom_call" | custom-call | flops 3221225472 | bytes 10485760 | tf_op jit(solution)/shard_map/sums/pallas_call | solution.py:314
  130.0 1.3 copy-done.11
  131.6 6.9 %sums.2 = (bf16[8,128,1024]{2,1,0:T(8,128)(2,1)S(1)}, bf16[8,128,1024]{2,1,0:T(8,128)(2,1)}) custom-call(s32[4]{0:T(128)S(1)} %copy-done.28, bf16[2,768,768]{2,1,0:T(8,128)(2,1)S(1)} %hidden.3.grads, bf16[2,384,2048]{2,1,0:T(8,128)(2,1)S(1)} %copy-done.29, bf16[2,384,2048]{2,1,0:T(8,128)(2,1)S(1)} %copy-done.30, bf16[8,256,192]{2,1,0:T(8,128)(2,1)S(1)} %copy-done.31), custom_call_target="tpu_custom_call" | custom-call | flops 3221225472 | bytes 10485760 | tf_op jit(solution)/shard_map/sums/pallas_call | solution.py:314
  138.5 1.3 copy-done.10
  140.0 1.4 copy-done.33
  141.4 4.2 %first_sum.3 = (bf16[8,64,512]{2,1,0:T(8,128)(2,1)}, bf16[8,64,512]{2,1,0:T(8,128)(2,1)}, bf16[4,2,64,512]{3,2,1,0:T(8,128)(2,1)}, bf16[4,2,64,512]{3,2,1,0:T(8,128)(2,1)}) custom-call(bf16[8,2,64,1024]{3,2,1,0:T(8,128)(2,1)} %bitcast.29, bf16[8,2,64,1024]{3,2,1,0:T(8,128)(2,1)} %bitcast.31), custom_call_target="tpu_custom_call" | custom-call | bytes 6291456 | tf_op jit(solution)/shard_map/first_sum/pallas_call | solution.py:356
  146.1 1.5 collective-permute-start.37
  147.6 1.3 copy-done.32
  148.9 4.1 %first_sum.2 = (bf16[8,64,512]{2,1,0:T(8,128)(2,1)}, bf16[8,64,512]{2,1,0:T(8,128)(2,1)}, bf16[4,2,64,512]{3,2,1,0:T(8,128)(2,1)}, bf16[4,2,64,512]{3,2,1,0:T(8,128)(2,1)}) custom-call(bf16[8,2,64,1024]{3,2,1,0:T(8,128)(2,1)} %bitcast.28, bf16[8,2,64,1024]{3,2,1,0:T(8,128)(2,1)} %bitcast.30), custom_call_target="tpu_custom_call" | custom-call | bytes 6291456 | tf_op jit(solution)/shard_map/first_sum/pallas_call | solution.py:356
  153.1 1.5 collective-permute-start.28
  155.1 5.4 %collective-permute-done.36.came_l = bf16[8,64,512]{2,1,0:T(8,128)(2,1)S(1)} collective-permute-done((bf16[8,64,512]{2,1,0:T(8,128)(2,1)}, bf16[8,64,512]{2,1,0:T(8,128)(2,1)S(1)}, u32[]{:S(2)}, u32[]{:S(2)}) %collective-permute-start.36) | collective-permute-done | bytes 524320 | tf_op jit(solution)/shard_map/ppermute | solution.py:66
  161.9 3.6 %second_sum.3 = (bf16[4,64,512]{2,1,0:T(8,128)(2,1)}, bf16[4,64,512]{2,1,0:T(8,128)(2,1)}, bf16[4,64,512]{2,1,0:T(8,128)(2,1)}, bf16[4,64,512]{2,1,0:T(8,128)(2,1)}) custom-call(bf16[8,64,512]{2,1,0:T(8,128)(2,1)} %get-tuple-element.55.keep_l, bf16[8,64,512]{2,1,0:T(8,128)(2,1)} %copy-done.36, bf16[4,2,64,512]{3,2,1,0:T(8,128)(2,1)} %get-tuple-element.57.keep_r, ...), custom_call_target="tpu_custom_call" | custom-call | bytes 3145728 | tf_op jit(solution)/shard_map/second_sum/pallas_call | solution.py:381
  165.5 1.6 collective-permute-start.38
  167.1 1.5 collective-permute-start.39
  168.6 3.2 %collective-permute-done.28.came_l = bf16[8,64,512]{2,1,0:T(8,128)(2,1)S(1)} collective-permute-done((bf16[8,64,512]{2,1,0:T(8,128)(2,1)}, bf16[8,64,512]{2,1,0:T(8,128)(2,1)S(1)}, u32[]{:S(2)}, u32[]{:S(2)}) %collective-permute-start.28) | collective-permute-done | bytes 524320 | tf_op jit(solution)/shard_map/ppermute | solution.py:66
  173.1 3.6 %second_sum.2 = (bf16[4,64,512]{2,1,0:T(8,128)(2,1)}, bf16[4,64,512]{2,1,0:T(8,128)(2,1)}, bf16[4,64,512]{2,1,0:T(8,128)(2,1)}, bf16[4,64,512]{2,1,0:T(8,128)(2,1)}) custom-call(bf16[8,64,512]{2,1,0:T(8,128)(2,1)} %get-tuple-element.41.keep_l, bf16[8,64,512]{2,1,0:T(8,128)(2,1)} %copy-done.34, bf16[4,2,64,512]{3,2,1,0:T(8,128)(2,1)} %get-tuple-element.43.keep_r, ...), custom_call_target="tpu_custom_call" | custom-call | bytes 3145728 | tf_op jit(solution)/shard_map/second_sum/pallas_call | solution.py:381
  176.7 1.6 collective-permute-start.30
  178.3 1.5 collective-permute-start.31
  180.5 2.1 third_sum.3
  182.6 1.1 collective-permute-start.41
  183.7 2.7 %collective-permute-start.42 = (bf16[64,1024]{1,0:T(8,128)(2,1)}, bf16[64,1024]{1,0:T(8,128)(2,1)S(1)}, u32[]{:S(2)}, u32[]{:S(2)}) collective-permute-start(bf16[64,1024]{1,0:T(8,128)(2,1)} %get-tuple-element.66), channel_id=1, source_target_pairs={{0,24},{2,26},{4,28},{6,30},{8,0},{10,2},{12,4},{14,6},{16,8},{18,... | collective-permute-start | bytes 393224 | tf_op jit(solution)/shard_map/ppermute | solution.py:71
  187.2 2.1 third_sum.2
  189.9 1.5 collective-permute-start.33
  191.3 2.9 %collective-permute-start.34 = (bf16[64,1024]{1,0:T(8,128)(2,1)}, bf16[64,1024]{1,0:T(8,128)(2,1)S(1)}, u32[]{:S(2)}, u32[]{:S(2)}) collective-permute-start(bf16[64,1024]{1,0:T(8,128)(2,1)} %get-tuple-element.52), channel_id=1, source_target_pairs={{0,24},{2,26},{4,28},{6,30},{8,0},{10,2},{12,4},{14,6},{16,8},{18,... | collective-permute-start | bytes 393224 | tf_op jit(solution)/shard_map/ppermute | solution.py:71
  194.2 2.8 %collective-permute-done.41.refs_6_ = bf16[64,1024]{1,0:T(8,128)(2,1)S(1)} collective-permute-done((bf16[64,1024]{1,0:T(8,128)(2,1)}, bf16[64,1024]{1,0:T(8,128)(2,1)S(1)}, u32[]{:S(2)}, u32[]{:S(2)}) %collective-permute-start.41) | collective-permute-done | bytes 131104 | tf_op jit(solution)/shard_map/ppermute | solution.py:71
  197.0 1.5 collective-permute-done.32.refs_1_
  198.5 6.3 %collective-permute-done.33.refs_2_ = bf16[64,1024]{1,0:T(8,128)(2,1)S(1)} collective-permute-done((bf16[64,1024]{1,0:T(8,128)(2,1)}, bf16[64,1024]{1,0:T(8,128)(2,1)S(1)}, u32[]{:S(2)}, u32[]{:S(2)}) %collective-permute-start.33) | collective-permute-done | bytes 131104 | tf_op jit(solution)/shard_map/ppermute | solution.py:71
  205.5 2.2 %last_sum.1 = f32[64,2048]{1,0:T(8,128)} custom-call(f32[64,1024]{1,0:T(8,128)} %get-tuple-element.49.refs_0_, bf16[64,1024]{1,0:T(8,128)(2,1)} %copy-done.45, bf16[64,1024]{1,0:T(8,128)(2,1)} %copy-done.46, bf16[64,1024]{1,0:T(8,128)(2,1)} %copy-done.47, f32[64,1024]{1,0:T(8,128)} %get-tuple-element.63.refs_4_, bf16[64,1024]{1,0:T(8,128)(2,1)} %copy-done.42, ...), custom_call_target="tpu_custom_call" | custom-call | tf_op jit(solution)/shard_map/last_sum/pallas_call | solution.py:474
  (152 shorter events, 22.6 us)
Async XLA Ops:
  1.0 9.0 %collective-permute-start.14 = (bf16[64,1024]{1,0:T(8,128)(2,1)S(1)}, bf16[64,1024]{1,0:T(8,128)(2,1)S(1)}, u32[]{:S(2)}, u32[]{:S(2)}) collective-permute-start(bf16[64,1024]{1,0:T(8,128)(2,1)S(1)} %get-tuple-element.69), channel_id=1, source_target_pairs={{0,24},{2,26},{4,28},{6,30},{8,0},{10,2},{12,4},{14,6},{16,8},{18,... | collective-permute-start | bytes 393224 | tf_op jit(solution)/shard_map/ppermute | solution.py:71
  6.1 11.2 %collective-permute-start.15 = (bf16[64,1024]{1,0:T(8,128)(2,1)S(1)}, bf16[64,1024]{1,0:T(8,128)(2,1)S(1)}, u32[]{:S(2)}, u32[]{:S(2)}) collective-permute-start(bf16[64,1024]{1,0:T(8,128)(2,1)S(1)} %get-tuple-element.69), channel_id=1, source_target_pairs={{0,16},{2,18},{4,20},{6,22},{8,24},{10,26},{12,28},{14,30},{16,0},... | collective-permute-start | bytes 393224 | tf_op jit(solution)/shard_map/ppermute | solution.py:71
  6.1 11.2 %collective-permute-start.16 = (bf16[64,1024]{1,0:T(8,128)(2,1)S(1)}, bf16[64,1024]{1,0:T(8,128)(2,1)S(1)}, u32[]{:S(2)}, u32[]{:S(2)}) collective-permute-start(bf16[64,1024]{1,0:T(8,128)(2,1)S(1)} %get-tuple-element.69), channel_id=1, source_target_pairs={{0,8},{2,10},{4,12},{6,14},{8,16},{10,18},{12,20},{14,22},{16,24},... | collective-permute-start | bytes 393224 | tf_op jit(solution)/shard_map/ppermute | solution.py:71
  17.3 19.0 %collective-permute-start.21 = (bf16[3,64,1024]{2,1,0:T(8,128)(2,1)S(1)}, bf16[3,64,1024]{2,1,0:T(8,128)(2,1)S(1)}, u32[]{:S(2)}, u32[]{:S(2)}) collective-permute-start(bf16[3,64,1024]{2,1,0:T(8,128)(2,1)S(1)} %pad_maximum_fusion.3.refs_2_), channel_id=1, source_target_pairs={{0,4},{2,6},{4,0},{6,2},{8,12},{10,14},{12,8},{14,10},{16,20},{18,... | collective-permute-start | bytes 1179656 | tf_op jit(solution)/shard_map/ppermute | solution.py:66
  18.9 6.2 %collective-permute-start.1 = (bf16[64,1024]{1,0:T(8,128)(2,1)S(1)}, bf16[64,1024]{1,0:T(8,128)(2,1)S(1)}, u32[]{:S(2)}, u32[]{:S(2)}) collective-permute-start(bf16[64,1024]{1,0:T(8,128)(2,1)S(1)} %get-tuple-element.70), channel_id=1, source_target_pairs={{0,24},{2,26},{4,28},{6,30},{8,0},{10,2},{12,4},{14,6},{16,8},{18,... | collective-permute-start | bytes 393224 | tf_op jit(solution)/shard_map/ppermute | solution.py:71
  20.5 12.1 %collective-permute-start.2 = (bf16[64,1024]{1,0:T(8,128)(2,1)S(1)}, bf16[64,1024]{1,0:T(8,128)(2,1)S(1)}, u32[]{:S(2)}, u32[]{:S(2)}) collective-permute-start(bf16[64,1024]{1,0:T(8,128)(2,1)S(1)} %get-tuple-element.70), channel_id=1, source_target_pairs={{0,16},{2,18},{4,20},{6,22},{8,24},{10,26},{12,28},{14,30},{16,0},... | collective-permute-start | bytes 393224 | tf_op jit(solution)/shard_map/ppermute | solution.py:71
  21.6 11.0 %collective-permute-start.3 = (bf16[64,1024]{1,0:T(8,128)(2,1)S(1)}, bf16[64,1024]{1,0:T(8,128)(2,1)S(1)}, u32[]{:S(2)}, u32[]{:S(2)}) collective-permute-start(bf16[64,1024]{1,0:T(8,128)(2,1)S(1)} %get-tuple-element.70), channel_id=1, source_target_pairs={{0,8},{2,10},{4,12},{6,14},{8,16},{10,18},{12,20},{14,22},{16,24},... | collective-permute-start | bytes 393224 | tf_op jit(solution)/shard_map/ppermute | solution.py:71
  23.6 14.4 %collective-permute-start.18 = (bf16[3,64,1024]{2,1,0:T(8,128)(2,1)S(1)}, bf16[3,64,1024]{2,1,0:T(8,128)(2,1)S(1)}, u32[]{:S(2)}, u32[]{:S(2)}) collective-permute-start(bf16[3,64,1024]{2,1,0:T(8,128)(2,1)S(1)} %pad_maximum_fusion.3.refs_2_), channel_id=1, source_target_pairs={{0,1},{1,0},{2,3},{3,2},{4,5},{5,4},{6,7},{7,6},{8,9},{9,8},{10,11... | collective-permute-start | bytes 1179656 | tf_op jit(solution)/shard_map/ppermute | solution.py:66
  25.1 10.7 %collective-permute-start.20 = (bf16[64,1024]{1,0:T(8,128)(2,1)S(1)}, bf16[64,1024]{1,0:T(8,128)(2,1)S(1)}, u32[]{:S(2)}, u32[]{:S(2)}) collective-permute-start(bf16[64,1024]{1,0:T(8,128)(2,1)S(1)} %get-tuple-element.69), channel_id=1, source_target_pairs={{0,4},{2,6},{4,0},{6,2},{8,12},{10,14},{12,8},{14,10},{16,20},{18,... | collective-permute-start | bytes 393224 | tf_op jit(solution)/shard_map/ppermute | solution.py:66
  32.6 19.2 %collective-permute-start = (bf16[128,2048]{1,0:T(8,128)(2,1)}, bf16[128,2048]{1,0:T(8,128)(2,1)S(1)}, u32[]{:S(2)}, u32[]{:S(2)}) collective-permute-start(bf16[128,2048]{1,0:T(8,128)(2,1)} %refs_0_.3), channel_id=1, source_target_pairs={{0,2},{2,0},{4,6},{6,4},{8,10},{10,8},{12,14},{14,12},{16,18},{18,... | collective-permute-start | bytes 1572872 | tf_op jit(solution)/shard_map/ppermute | solution.py:66
  33.4 11.8 %collective-permute-start.5 = (bf16[3,64,1024]{2,1,0:T(8,128)(2,1)}, bf16[3,64,1024]{2,1,0:T(8,128)(2,1)}, u32[]{:S(2)}, u32[]{:S(2)}) collective-permute-start(bf16[3,64,1024]{2,1,0:T(8,128)(2,1)} %pad_maximum_fusion.2.refs_2_), channel_id=1, source_target_pairs={{0,1},{1,0},{2,3},{3,2},{4,5},{5,4},{6,7},{7,6},{8,9},{9,8},{10,11... | collective-permute-start | bytes 1179656 | tf_op jit(solution)/shard_map/ppermute | solution.py:66
  35.8 11.9 %collective-permute-start.7 = (bf16[64,1024]{1,0:T(8,128)(2,1)S(1)}, bf16[64,1024]{1,0:T(8,128)(2,1)S(1)}, u32[]{:S(2)}, u32[]{:S(2)}) collective-permute-start(bf16[64,1024]{1,0:T(8,128)(2,1)S(1)} %get-tuple-element.70), channel_id=1, source_target_pairs={{0,4},{2,6},{4,0},{6,2},{8,12},{10,14},{12,8},{14,10},{16,20},{18,... | collective-permute-start | bytes 393224 | tf_op jit(solution)/shard_map/ppermute | solution.py:66
  36.4 13.5 %collective-permute-start.8 = (bf16[3,64,1024]{2,1,0:T(8,128)(2,1)}, bf16[3,64,1024]{2,1,0:T(8,128)(2,1)S(1)}, u32[]{:S(2)}, u32[]{:S(2)}) collective-permute-start(bf16[3,64,1024]{2,1,0:T(8,128)(2,1)} %pad_maximum_fusion.2.refs_2_), channel_id=1, source_target_pairs={{0,4},{2,6},{4,0},{6,2},{8,12},{10,14},{12,8},{14,10},{16,20},{18,... | collective-permute-start | bytes 1179656 | tf_op jit(solution)/shard_map/ppermute | solution.py:66
  38.0 17.1 %copy-start.8 = (bf16[4,64,1024]{2,1,0:T(8,128)(2,1)}, bf16[4,64,1024]{2,1,0:T(8,128)(2,1)S(1)}, u32[]{:S(2)}) copy-start(bf16[4,64,1024]{2,1,0:T(8,128)(2,1)S(1)} %pad_maximum_fusion.1.refs_6_) | copy-start | bytes 1572868
  38.0 17.1 %copy-start.12 = (bf16[3,64,1024]{2,1,0:T(8,128)(2,1)}, bf16[3,64,1024]{2,1,0:T(8,128)(2,1)S(1)}, u32[]{:S(2)}) copy-start(bf16[3,64,1024]{2,1,0:T(8,128)(2,1)S(1)} %collective-permute-done.18.refs_4_) | copy-start | bytes 1179652
  38.0 12.5 %collective-permute-start.17 = (bf16[3,64,1024]{2,1,0:T(8,128)(2,1)S(1)}, bf16[3,64,1024]{2,1,0:T(8,128)(2,1)S(1)}, u32[]{:S(2)}, u32[]{:S(2)}) collective-permute-start(bf16[3,64,1024]{2,1,0:T(8,128)(2,1)S(1)} %pad_maximum_fusion.3.refs_2_), channel_id=1, source_target_pairs={{0,2},{2,0},{4,6},{6,4},{8,10},{10,8},{12,14},{14,12},{16,18},{18,... | collective-permute-start | bytes 1179656 | tf_op jit(solution)/shard_map/ppermute | solution.py:66
  38.1 25.9 %copy-start.48 = (s32[128,8]{0,1:T(8,128)S(1)}, s32[128,8]{0,1:T(8,128)}, u32[]{:S(2)}) copy-start(s32[128,8]{0,1:T(8,128)} %param.10) | copy-start | bytes 12292
  38.1 28.0 %copy-start.49 = (f32[128,8]{0,1:T(8,128)S(1)}, f32[128,8]{0,1:T(8,128)}, u32[]{:S(2)}) copy-start(f32[128,8]{0,1:T(8,128)} %param.9) | copy-start | bytes 12292
  45.3 8.8 %collective-permute-start.23 = (bf16[4,64,512]{2,1,0:T(8,128)(2,1)S(1)}, bf16[4,64,512]{2,1,0:T(8,128)(2,1)S(1)}, u32[]{:S(2)}, u32[]{:S(2)}) collective-permute-start(bf16[4,64,512]{2,1,0:T(8,128)(2,1)S(1)} %fusion), channel_id=1, source_target_pairs={{0,1},{1,0},{2,3},{3,2},{4,5},{5,4},{6,7},{7,6},{8,9},{9,8},{10,11... | collective-permute-start | bytes 786440 | tf_op jit(solution)/shard_map/ppermute | solution.py:66
  47.8 17.5 %collective-permute-start.22 = (bf16[4,64,1024]{2,1,0:T(8,128)(2,1)S(1)}, bf16[4,64,1024]{2,1,0:T(8,128)(2,1)S(1)}, u32[]{:S(2)}, u32[]{:S(2)}) collective-permute-start(bf16[4,64,1024]{2,1,0:T(8,128)(2,1)S(1)} %pad_maximum_fusion.1.refs_6_), channel_id=1, source_target_pairs={{0,2},{2,0},{4,6},{6,4},{8,10},{10,8},{12,14},{14,12},{16,18},{18,... | collective-permute-start | bytes 1572872 | tf_op jit(solution)/shard_map/ppermute | solution.py:66
  49.9 9.2 %collective-permute-start.25 = (bf16[4,64,512]{2,1,0:T(8,128)(2,1)S(1)}, bf16[4,64,512]{2,1,0:T(8,128)(2,1)S(1)}, u32[]{:S(2)}, u32[]{:S(2)}) collective-permute-start(bf16[4,64,512]{2,1,0:T(8,128)(2,1)S(1)} %pad_maximum_fusion.5), channel_id=1, source_target_pairs={{0,4},{2,6},{4,0},{6,2},{8,12},{10,14},{12,8},{14,10},{16,20},{18,... | collective-permute-start | bytes 786440 | tf_op jit(solution)/shard_map/ppermute | solution.py:66
  51.3 7.9 %collective-permute-start.10 = (bf16[4,64,512]{2,1,0:T(8,128)(2,1)S(1)}, bf16[4,64,512]{2,1,0:T(8,128)(2,1)}, u32[]{:S(2)}, u32[]{:S(2)}) collective-permute-start(bf16[4,64,512]{2,1,0:T(8,128)(2,1)S(1)} %fusion.1), channel_id=1, source_target_pairs={{0,1},{1,0},{2,3},{3,2},{4,5},{5,4},{6,7},{7,6},{8,9},{9,8},{10,11... | collective-permute-start | bytes 786440 | tf_op jit(solution)/shard_map/ppermute | solution.py:66
  52.6 10.7 %collective-permute-start.12 = (bf16[4,64,512]{2,1,0:T(8,128)(2,1)S(1)}, bf16[4,64,512]{2,1,0:T(8,128)(2,1)}, u32[]{:S(2)}, u32[]{:S(2)}) collective-permute-start(bf16[4,64,512]{2,1,0:T(8,128)(2,1)S(1)} %pad_maximum_fusion.4), channel_id=1, source_target_pairs={{0,4},{2,6},{4,0},{6,2},{8,12},{10,14},{12,8},{14,10},{16,20},{18,... | collective-permute-start | bytes 786440 | tf_op jit(solution)/shard_map/ppermute | solution.py:66
  54.1 14.0 %copy-start.20 = (bf16[4,64,512]{2,1,0:T(8,128)(2,1)}, bf16[4,64,512]{2,1,0:T(8,128)(2,1)S(1)}, u32[]{:S(2)}) copy-start(bf16[4,64,512]{2,1,0:T(8,128)(2,1)S(1)} %collective-permute-done.23.refs_8_) | copy-start | bytes 786436
  54.1 9.9 %collective-permute-start.19 = (bf16[3,64,1024]{2,1,0:T(8,128)(2,1)S(1)}, bf16[3,64,1024]{2,1,0:T(8,128)(2,1)S(1)}, u32[]{:S(2)}, u32[]{:S(2)}) collective-permute-start(bf16[3,64,1024]{2,1,0:T(8,128)(2,1)S(1)} %collective-permute-done.18.refs_4_), channel_id=1, source_target_pairs={{0,2},{2,0},{4,6},{6,4},{8,10},{10,8},{12,14},{14,12},{16,18},{18,... | collective-permute-start | bytes 1179656 | tf_op jit(solution)/shard_map/ppermute | solution.py:66
  59.2 55.7 %collective-permute-start.9 = (bf16[4,64,1024]{2,1,0:T(8,128)(2,1)}, bf16[4,64,1024]{2,1,0:T(8,128)(2,1)}, u32[]{:S(2)}, u32[]{:S(2)}) collective-permute-start(bf16[4,64,1024]{2,1,0:T(8,128)(2,1)} %pad_maximum_fusion.refs_6_), channel_id=1, source_target_pairs={{0,2},{2,0},{4,6},{6,4},{8,10},{10,8},{12,14},{14,12},{16,18},{18,... | collective-permute-start | bytes 1572872 | tf_op jit(solution)/shard_map/ppermute | solution.py:66
  59.2 7.0 %collective-permute-start.24 = (bf16[4,64,512]{2,1,0:T(8,128)(2,1)S(1)}, bf16[4,64,512]{2,1,0:T(8,128)(2,1)S(1)}, u32[]{:S(2)}, u32[]{:S(2)}) collective-permute-start(bf16[4,64,512]{2,1,0:T(8,128)(2,1)S(1)} %collective-permute-done.23.refs_8_), channel_id=1, source_target_pairs={{0,2},{2,0},{4,6},{6,4},{8,10},{10,8},{12,14},{14,12},{16,18},{18,... | collective-permute-start | bytes 786440 | tf_op jit(solution)/shard_map/ppermute | solution.py:66
  63.3 4.1 %collective-permute-start.26 = (bf16[4,64,512]{2,1,0:T(8,128)(2,1)S(1)}, bf16[4,64,512]{2,1,0:T(8,128)(2,1)S(1)}, u32[]{:S(2)}, u32[]{:S(2)}) collective-permute-start(bf16[4,64,512]{2,1,0:T(8,128)(2,1)S(1)} %collective-permute-done.25.refs_10_), channel_id=1, source_target_pairs={{0,2},{2,0},{4,6},{6,4},{8,10},{10,8},{12,14},{14,12},{16,18},{18,... | collective-permute-start | bytes 786440 | tf_op jit(solution)/shard_map/ppermute | solution.py:66
  64.8 50.1 %collective-permute-start.4 = (bf16[3,64,1024]{2,1,0:T(8,128)(2,1)}, bf16[3,64,1024]{2,1,0:T(8,128)(2,1)}, u32[]{:S(2)}, u32[]{:S(2)}) collective-permute-start(bf16[3,64,1024]{2,1,0:T(8,128)(2,1)} %pad_maximum_fusion.2.refs_2_), channel_id=1, source_target_pairs={{0,2},{2,0},{4,6},{6,4},{8,10},{10,8},{12,14},{14,12},{16,18},{18,... | collective-permute-start | bytes 1179656 | tf_op jit(solution)/shard_map/ppermute | solution.py:66
  66.1 48.8 %collective-permute-start.6 = (bf16[3,64,1024]{2,1,0:T(8,128)(2,1)}, bf16[3,64,1024]{2,1,0:T(8,128)(2,1)}, u32[]{:S(2)}, u32[]{:S(2)}) collective-permute-start(bf16[3,64,1024]{2,1,0:T(8,128)(2,1)} %collective-permute-done.5.refs_4_), channel_id=1, source_target_pairs={{0,2},{2,0},{4,6},{6,4},{8,10},{10,8},{12,14},{14,12},{16,18},{18,... | collective-permute-start | bytes 1179656 | tf_op jit(solution)/shard_map/ppermute | solution.py:66
  66.9 48.0 %collective-permute-start.11 = (bf16[4,64,512]{2,1,0:T(8,128)(2,1)}, bf16[4,64,512]{2,1,0:T(8,128)(2,1)}, u32[]{:S(2)}, u32[]{:S(2)}) collective-permute-start(bf16[4,64,512]{2,1,0:T(8,128)(2,1)} %collective-permute-done.10.refs_8_), channel_id=1, source_target_pairs={{0,2},{2,0},{4,6},{6,4},{8,10},{10,8},{12,14},{14,12},{16,18},{18,... | collective-permute-start | bytes 786440 | tf_op jit(solution)/shard_map/ppermute | solution.py:66
  68.1 46.9 %collective-permute-start.13 = (bf16[4,64,512]{2,1,0:T(8,128)(2,1)}, bf16[4,64,512]{2,1,0:T(8,128)(2,1)}, u32[]{:S(2)}, u32[]{:S(2)}) collective-permute-start(bf16[4,64,512]{2,1,0:T(8,128)(2,1)} %collective-permute-done.12.refs_10_), channel_id=1, source_target_pairs={{0,2},{2,0},{4,6},{6,4},{8,10},{10,8},{12,14},{14,12},{16,18},{18,... | collective-permute-start | bytes 786440 | tf_op jit(solution)/shard_map/ppermute | solution.py:66
  68.7 27.3 %copy-start = (bf16[2,384,2048]{2,1,0:T(8,128)(2,1)S(1)}, bf16[2,384,2048]{2,1,0:T(8,128)(2,1)}, u32[]{:S(2)}) copy-start(bf16[2,384,2048]{2,1,0:T(8,128)(2,1)} %refs_14_.3) | copy-start | bytes 9437188
  68.7 27.3 %copy-start.28 = (s32[4]{0:T(128)S(1)}, s32[4]{0:T(128)}, u32[]{:S(2)}) copy-start(s32[4]{0:T(128)} %pad_add_fusion.place) | copy-start | bytes 52
  97.0 1.1 copy-start.4
  109.2 5.7 %copy-start.1 = (bf16[2,384,768]{1,2,0:T(8,128)(2,1)S(1)}, bf16[2,384,768]{1,2,0:T(8,128)(2,1)}, u32[]{:S(2)}) copy-start(bf16[2,384,768]{1,2,0:T(8,128)(2,1)} %copy.9) | copy-start | bytes 3538948
  109.2 5.7 %copy-start.2 = (bf16[2,384,768]{1,2,0:T(8,128)(2,1)S(1)}, bf16[2,384,768]{1,2,0:T(8,128)(2,1)}, u32[]{:S(2)}) copy-start(bf16[2,384,768]{1,2,0:T(8,128)(2,1)} %copy.10) | copy-start | bytes 3538948
  115.0 8.6 %copy-start.29 = (bf16[2,384,2048]{2,1,0:T(8,128)(2,1)S(1)}, bf16[2,384,2048]{2,1,0:T(8,128)(2,1)}, u32[]{:S(2)}) copy-start(bf16[2,384,2048]{2,1,0:T(8,128)(2,1)} %w_gate.3) | copy-start | bytes 9437188
  115.0 8.6 %copy-start.30 = (bf16[2,384,2048]{2,1,0:T(8,128)(2,1)S(1)}, bf16[2,384,2048]{2,1,0:T(8,128)(2,1)}, u32[]{:S(2)}) copy-start(bf16[2,384,2048]{2,1,0:T(8,128)(2,1)} %w_up.3) | copy-start | bytes 9437188
  115.0 8.6 %copy-start.31 = (bf16[8,256,192]{2,1,0:T(8,128)(2,1)S(1)}, bf16[8,256,192]{2,1,0:T(8,128)(2,1)}, u32[]{:S(2)}) copy-start(bf16[8,256,192]{2,1,0:T(8,128)(2,1)} %get-tuple-element.38.pick_t) | copy-start | bytes 2359300
  130.0 1.3 copy-start.11
  131.3 8.7 %collective-permute-start.35 = (bf16[8,128,1024]{2,1,0:T(8,128)(2,1)S(1)}, bf16[8,128,1024]{2,1,0:T(8,128)(2,1)S(1)}, u32[]{:S(2)}, u32[]{:S(2)}) collective-permute-start(bf16[8,128,1024]{2,1,0:T(8,128)(2,1)S(1)} %get-tuple-element.54), channel_id=1, source_target_pairs={{0,2},{2,0},{4,6},{6,4},{8,10},{10,8},{12,14},{14,12},{16,18},{18,... | collective-permute-start | bytes 6291464 | tf_op jit(solution)/shard_map/ppermute | solution.py:66
  138.5 1.3 copy-start.10
  139.8 7.8 %collective-permute-start.27 = (bf16[8,128,1024]{2,1,0:T(8,128)(2,1)}, bf16[8,128,1024]{2,1,0:T(8,128)(2,1)S(1)}, u32[]{:S(2)}, u32[]{:S(2)}) collective-permute-start(bf16[8,128,1024]{2,1,0:T(8,128)(2,1)} %get-tuple-element.40), channel_id=1, source_target_pairs={{0,2},{2,0},{4,6},{6,4},{8,10},{10,8},{12,14},{14,12},{16,18},{18,... | collective-permute-start | bytes 6291464 | tf_op jit(solution)/shard_map/ppermute | solution.py:66
  140.0 1.4 copy-start.33
  145.5 15.0 %collective-permute-start.36 = (bf16[8,64,512]{2,1,0:T(8,128)(2,1)}, bf16[8,64,512]{2,1,0:T(8,128)(2,1)S(1)}, u32[]{:S(2)}, u32[]{:S(2)}) collective-permute-start(bf16[8,64,512]{2,1,0:T(8,128)(2,1)} %get-tuple-element.56), channel_id=1, source_target_pairs={{0,1},{1,0},{2,3},{3,2},{4,5},{5,4},{6,7},{7,6},{8,9},{9,8},{10,11... | collective-permute-start | bytes 1572872 | tf_op jit(solution)/shard_map/ppermute | solution.py:66
  146.1 15.0 %collective-permute-start.37 = (bf16[4,2,64,512]{3,2,1,0:T(8,128)(2,1)}, bf16[4,2,64,512]{3,2,1,0:T(8,128)(2,1)S(1)}, u32[]{:S(2)}, u32[]{:S(2)}) collective-permute-start(bf16[4,2,64,512]{3,2,1,0:T(8,128)(2,1)} %get-tuple-element.58), channel_id=1, source_target_pairs={{0,4},{2,6},{4,0},{6,2},{8,12},{10,14},{12,8},{14,10},{16,20},{18,... | collective-permute-start | bytes 1572872 | tf_op jit(solution)/shard_map/ppermute | solution.py:66
  147.6 1.3 copy-start.32
  153.1 18.7 %collective-permute-start.28 = (bf16[8,64,512]{2,1,0:T(8,128)(2,1)}, bf16[8,64,512]{2,1,0:T(8,128)(2,1)S(1)}, u32[]{:S(2)}, u32[]{:S(2)}) collective-permute-start(bf16[8,64,512]{2,1,0:T(8,128)(2,1)} %get-tuple-element.42), channel_id=1, source_target_pairs={{0,1},{1,0},{2,3},{3,2},{4,5},{5,4},{6,7},{7,6},{8,9},{9,8},{10,11... | collective-permute-start | bytes 1572872 | tf_op jit(solution)/shard_map/ppermute | solution.py:66
  154.5 17.7 %collective-permute-start.29 = (bf16[4,2,64,512]{3,2,1,0:T(8,128)(2,1)}, bf16[4,2,64,512]{3,2,1,0:T(8,128)(2,1)S(1)}, u32[]{:S(2)}, u32[]{:S(2)}) collective-permute-start(bf16[4,2,64,512]{3,2,1,0:T(8,128)(2,1)} %get-tuple-element.44), channel_id=1, source_target_pairs={{0,4},{2,6},{4,0},{6,2},{8,12},{10,14},{12,8},{14,10},{16,20},{18,... | collective-permute-start | bytes 1572872 | tf_op jit(solution)/shard_map/ppermute | solution.py:66
  165.5 14.2 %collective-permute-start.38 = (bf16[4,64,512]{2,1,0:T(8,128)(2,1)}, bf16[4,64,512]{2,1,0:T(8,128)(2,1)S(1)}, u32[]{:S(2)}, u32[]{:S(2)}) collective-permute-start(bf16[4,64,512]{2,1,0:T(8,128)(2,1)} %get-tuple-element.60), channel_id=1, source_target_pairs={{0,4},{2,6},{4,0},{6,2},{8,12},{10,14},{12,8},{14,10},{16,20},{18,... | collective-permute-start | bytes 786440 | tf_op jit(solution)/shard_map/ppermute | solution.py:66
  167.1 12.7 %collective-permute-start.39 = (bf16[4,64,512]{2,1,0:T(8,128)(2,1)}, bf16[4,64,512]{2,1,0:T(8,128)(2,1)S(1)}, u32[]{:S(2)}, u32[]{:S(2)}) collective-permute-start(bf16[4,64,512]{2,1,0:T(8,128)(2,1)} %get-tuple-element.62), channel_id=1, source_target_pairs={{0,1},{1,0},{2,3},{3,2},{4,5},{5,4},{6,7},{7,6},{8,9},{9,8},{10,11... | collective-permute-start | bytes 786440 | tf_op jit(solution)/shard_map/ppermute | solution.py:66
  176.7 9.7 %collective-permute-start.30 = (bf16[4,64,512]{2,1,0:T(8,128)(2,1)}, bf16[4,64,512]{2,1,0:T(8,128)(2,1)S(1)}, u32[]{:S(2)}, u32[]{:S(2)}) collective-permute-start(bf16[4,64,512]{2,1,0:T(8,128)(2,1)} %get-tuple-element.46), channel_id=1, source_target_pairs={{0,4},{2,6},{4,0},{6,2},{8,12},{10,14},{12,8},{14,10},{16,20},{18,... | collective-permute-start | bytes 786440 | tf_op jit(solution)/shard_map/ppermute | solution.py:66
  178.3 8.2 %collective-permute-start.31 = (bf16[4,64,512]{2,1,0:T(8,128)(2,1)}, bf16[4,64,512]{2,1,0:T(8,128)(2,1)S(1)}, u32[]{:S(2)}, u32[]{:S(2)}) collective-permute-start(bf16[4,64,512]{2,1,0:T(8,128)(2,1)} %get-tuple-element.48), channel_id=1, source_target_pairs={{0,1},{1,0},{2,3},{3,2},{4,5},{5,4},{6,7},{7,6},{8,9},{9,8},{10,11... | collective-permute-start | bytes 786440 | tf_op jit(solution)/shard_map/ppermute | solution.py:66
  182.6 8.7 %collective-permute-start.40 = (bf16[64,1024]{1,0:T(8,128)(2,1)}, bf16[64,1024]{1,0:T(8,128)(2,1)S(1)}, u32[]{:S(2)}, u32[]{:S(2)}) collective-permute-start(bf16[64,1024]{1,0:T(8,128)(2,1)} %get-tuple-element.64), channel_id=1, source_target_pairs={{0,8},{2,10},{4,12},{6,14},{8,16},{10,18},{12,20},{14,22},{16,24},... | collective-permute-start | bytes 393224 | tf_op jit(solution)/shard_map/ppermute | solution.py:71
  182.6 14.4 %collective-permute-start.41 = (bf16[64,1024]{1,0:T(8,128)(2,1)}, bf16[64,1024]{1,0:T(8,128)(2,1)S(1)}, u32[]{:S(2)}, u32[]{:S(2)}) collective-permute-start(bf16[64,1024]{1,0:T(8,128)(2,1)} %get-tuple-element.65), channel_id=1, source_target_pairs={{0,16},{2,18},{4,20},{6,22},{8,24},{10,26},{12,28},{14,30},{16,0},... | collective-permute-start | bytes 393224 | tf_op jit(solution)/shard_map/ppermute | solution.py:71
  183.7 13.3 %collective-permute-start.42 = (bf16[64,1024]{1,0:T(8,128)(2,1)}, bf16[64,1024]{1,0:T(8,128)(2,1)S(1)}, u32[]{:S(2)}, u32[]{:S(2)}) collective-permute-start(bf16[64,1024]{1,0:T(8,128)(2,1)} %get-tuple-element.66), channel_id=1, source_target_pairs={{0,24},{2,26},{4,28},{6,30},{8,0},{10,2},{12,4},{14,6},{16,8},{18,... | collective-permute-start | bytes 393224 | tf_op jit(solution)/shard_map/ppermute | solution.py:71
  189.3 9.2 %collective-permute-start.32 = (bf16[64,1024]{1,0:T(8,128)(2,1)}, bf16[64,1024]{1,0:T(8,128)(2,1)S(1)}, u32[]{:S(2)}, u32[]{:S(2)}) collective-permute-start(bf16[64,1024]{1,0:T(8,128)(2,1)} %get-tuple-element.50), channel_id=1, source_target_pairs={{0,8},{2,10},{4,12},{6,14},{8,16},{10,18},{12,20},{14,22},{16,24},... | collective-permute-start | bytes 393224 | tf_op jit(solution)/shard_map/ppermute | solution.py:71
  189.9 14.9 %collective-permute-start.33 = (bf16[64,1024]{1,0:T(8,128)(2,1)}, bf16[64,1024]{1,0:T(8,128)(2,1)S(1)}, u32[]{:S(2)}, u32[]{:S(2)}) collective-permute-start(bf16[64,1024]{1,0:T(8,128)(2,1)} %get-tuple-element.51), channel_id=1, source_target_pairs={{0,16},{2,18},{4,20},{6,22},{8,24},{10,26},{12,28},{14,30},{16,0},... | collective-permute-start | bytes 393224 | tf_op jit(solution)/shard_map/ppermute | solution.py:71
  191.3 13.5 %copy-start.42 = (bf16[64,1024]{1,0:T(8,128)(2,1)}, bf16[64,1024]{1,0:T(8,128)(2,1)S(1)}, u32[]{:S(2)}) copy-start(bf16[64,1024]{1,0:T(8,128)(2,1)S(1)} %collective-permute-done.40.refs_5_) | copy-start | bytes 393220
  191.3 13.5 %collective-permute-start.34 = (bf16[64,1024]{1,0:T(8,128)(2,1)}, bf16[64,1024]{1,0:T(8,128)(2,1)S(1)}, u32[]{:S(2)}, u32[]{:S(2)}) collective-permute-start(bf16[64,1024]{1,0:T(8,128)(2,1)} %get-tuple-element.52), channel_id=1, source_target_pairs={{0,24},{2,26},{4,28},{6,30},{8,0},{10,2},{12,4},{14,6},{16,8},{18,... | collective-permute-start | bytes 393224 | tf_op jit(solution)/shard_map/ppermute | solution.py:71
  197.0 7.8 %copy-start.43 = (bf16[64,1024]{1,0:T(8,128)(2,1)}, bf16[64,1024]{1,0:T(8,128)(2,1)S(1)}, u32[]{:S(2)}) copy-start(bf16[64,1024]{1,0:T(8,128)(2,1)S(1)} %collective-permute-done.41.refs_6_) | copy-start | bytes 393220
  197.0 7.8 %copy-start.44 = (bf16[64,1024]{1,0:T(8,128)(2,1)}, bf16[64,1024]{1,0:T(8,128)(2,1)S(1)}, u32[]{:S(2)}) copy-start(bf16[64,1024]{1,0:T(8,128)(2,1)S(1)} %collective-permute-done.42.refs_7_) | copy-start | bytes 393220
  198.5 6.3 %copy-start.45 = (bf16[64,1024]{1,0:T(8,128)(2,1)}, bf16[64,1024]{1,0:T(8,128)(2,1)S(1)}, u32[]{:S(2)}) copy-start(bf16[64,1024]{1,0:T(8,128)(2,1)S(1)} %collective-permute-done.32.refs_1_) | copy-start | bytes 393220
  (29 other events, 24.9 us)

commit v3 on v2

--- a/solution.py
+++ b/solution.py
@@ -77,22 +77,66 @@
     return pl.multiple_of((line * 2 + row) * width, width)
 
 
-def route_kernel(capacity, place, sides, pick, pick_t, gate, hits, gates):
-    groups, _, tokens = sides.shape
-    line_count = groups // 4
+def prepare_kernel(width, place, tokens, gates, ids, first, *others):
+    piece = first.shape[0]
+    near = pl.multiple_of(place[3] * piece, piece)
+    first[:, :width] = tokens[pl.ds(near, piece), :width]
+    for i, other in enumerate(others[:-1]):
+        other[...] = tokens[pl.ds(near, piece), (i + 1) * width:(i + 2) * width]
+    rest = gates[...]
+    terms = []
+    for _ in range(3):
+        term = rest.astype(jnp.bfloat16).astype(jnp.float32)
+        terms.append(term)
+        rest = rest - term
+    terms.append(ids[...].astype(jnp.float32))
+    unused = piece - 4 * gates.shape[0]
+    terms.append(jnp.zeros((unused, gates.shape[1]), jnp.float32))
+    table = jnp.concatenate(terms, axis=0).astype(jnp.bfloat16)
+    first[:, width:] = table
+    others[-1][...] = table
+
+
+def prepare(place, cotangent, gates, ids, piece, width):
+    feature_dim = cotangent.shape[1]
+    shapes = [(piece, width + 128)] + [(piece, width)] * (feature_dim // width - 1) + [(piece, 128)]
+    return pl.pallas_call(
+        functools.partial(prepare_kernel, width),
+        out_shape=[jax.ShapeDtypeStruct(dims, jnp.bfloat16) for dims in shapes],
+        in_specs=[pl.BlockSpec(memory_space=pltpu.SMEM)] + [pl.BlockSpec(memory_space=pltpu.VMEM)] * 3,
+        compiler_params=pltpu.CompilerParams(vmem_limit_bytes=4 << 20),
+        name="prepare",
+    )(place, cotangent, gates, ids)
+
+
+def route_kernel(capacity, place, own, own_c, lines, lines_c, over, over_c, pick, pick_t, gate, hits, gates):
+    line_count, _, tokens = over.shape
     core, row, line, half = place[0], place[1], place[2], place[3]
     first = (line * 4 + row * 2 + core) * 2
     for r in range(line_count):
         for ry in range(2):
+            tables = []
             for c in range(2):
-                group = lax.rem(line + r, line_count) * 4 + (row if ry == 0 else 1 - row) * 2 + c
-                block = sides[group]
+                if ry == 1:
+                    table = (over, over_c)[c][r]
+                elif r == 0:
+                    table = (own, own_c)[c][...]
+                else:
+                    table = (lines, lines_c)[c][r - 1]
+                tables.append(table[:32].astype(jnp.float32))
+            swapped = core > 0
+            ordered = [
+                jnp.where(swapped, tables[1], tables[0]), jnp.where(swapped, tables[0], tables[1])
+            ]
+            for c in range(2):
+                block = ordered[c]
+                value = block[0:8] + block[8:16] + block[16:24]
                 for e in range(2):
-                    named = block[8:16] == (first + e).astype(jnp.float32)
+                    named = block[24:32] == (first + e).astype(jnp.float32)
                     at = ((r * 2 + ry) * 2 + c) * 2 + e
                     hits[at:at + 1] = jnp.sum(named.astype(jnp.float32), axis=0, keepdims=True)
                     gates[at:at + 1] = jnp.sum(
-                        jnp.where(named, block[0:8], 0.0), axis=0, keepdims=True
+                        jnp.where(named, value, 0.0), axis=0, keepdims=True
                     )
     earlier = lax.broadcasted_iota(jnp.int32, (tokens, tokens), 0) < lax.broadcasted_iota(
         jnp.int32, (tokens, tokens), 1
@@ -119,8 +163,8 @@
                 gate[p, place_in:place_in + capacity] = jnp.broadcast_to(
                     column, (capacity, gate.shape[2])
                 )
-                own = (core == c).astype(jnp.float32)
-                rows.append(jnp.concatenate([ones * own, ones * (1.0 - own)], axis=1))
+                own_core = (core == c).astype(jnp.float32)
+                rows.append(jnp.concatenate([ones * own_core, ones * (1.0 - own_core)], axis=1))
         matrix = jnp.concatenate(rows, axis=0)
         pick[p] = matrix.astype(jnp.bfloat16)
         count = matrix.shape[0]
@@ -130,24 +174,31 @@
         pick_t[p] = square.T[:, :count].astype(jnp.bfloat16)
 
 
-def route(place, sides, capacity):
-    groups, _, tokens = sides.shape
-    pairs = groups // 2
+def route(place, own, own_c, lines, lines_c, over, over_c, capacity):
+    line_count, piece, whole_width = over.shape
+    tokens = 2 * piece
+    pairs = 2 * line_count
     rows = 4 * capacity
+    last = whole_width // 128 - 1
+    table = lambda array: pl.BlockSpec(array.shape[:-1] + (128,), lambda i, place: (0, 0, last))
+    alone = pl.BlockSpec((piece, 128), lambda i, place: (0, 0))
+    shapes = ((pairs, rows, 2 * tokens), (pairs, 2 * tokens, rows), (pairs, rows, 128))
     return pl.pallas_call(
         functools.partial(route_kernel, capacity),
-        out_shape=(
-            jax.ShapeDtypeStruct((pairs, rows, 2 * tokens), jnp.bfloat16),
-            jax.ShapeDtypeStruct((pairs, 2 * tokens, rows), jnp.bfloat16),
-            jax.ShapeDtypeStruct((pairs, rows, 128), jnp.float32),
+        out_shape=[
+            jax.ShapeDtypeStruct(dims, kind)
+            for dims, kind in zip(shapes, (jnp.bfloat16, jnp.bfloat16, jnp.float32))
+        ],
+        grid_spec=pltpu.PrefetchScalarGridSpec(
+            num_scalar_prefetch=1,
+            grid=(1,),
+            in_specs=[alone, alone] + [table(array) for array in (lines, lines_c, over, over_c)],
+            out_specs=[pl.BlockSpec(dims, lambda i, place: (0, 0, 0)) for dims in shapes],
+            scratch_shapes=[pltpu.VMEM((4 * pairs, tokens), jnp.float32)] * 2,
         ),
-        in_specs=[
-            pl.BlockSpec(memory_space=pltpu.SMEM),
-            pl.BlockSpec(memory_space=pltpu.VMEM),
-        ],
-        scratch_shapes=[pltpu.VMEM((2 * groups, tokens), jnp.float32)] * 2,
+        compiler_params=pltpu.CompilerParams(vmem_limit_bytes=8 << 20),
         name="route",
-    )(place, sides)
+    )(place, own, own_c, lines, lines_c, over, over_c)
 
 
 def hidden_kernel(last, place, *refs):
@@ -228,13 +279,15 @@
 
 def hidden(place, chunk, own, own_c, moved, pick, gate, w_down, rest):
     last = rest is not None
-    over = moved[4]
-    line_count, piece, width = over.shape
+    line_count, piece, _ = moved[4].shape
+    width = 2 * moved[6].shape[-1]
     steps = width // LANES
     offset = chunk * steps
     units = w_down.shape[1]
     slot_count = pick.shape[0] * pick.shape[1] // 2
-    whole = lambda dims: pl.BlockSpec(dims, lambda k, place: (0,) * len(dims))
+    whole = lambda dims: pl.BlockSpec(
+        dims, lambda k, place: (0,) * len(dims), pipeline_mode=pl.Buffered(1)
+    )
     column = lambda array: pl.BlockSpec(array.shape[:-1] + (LANES,), lambda k, place: (0, 0, k))
     first_half = lambda array: pl.BlockSpec(
         array.shape[:-1] + (LANES,), lambda k, place: (0, 0, jnp.minimum(k, steps // 2 - 1))
@@ -271,7 +324,7 @@
             out_specs=whole(out.shape),
             scratch_shapes=scratch,
         ),
-        compiler_params=pltpu.CompilerParams(vmem_limit_bytes=40 << 20),
+        compiler_params=pltpu.CompilerParams(vmem_limit_bytes=24 << 20),
         cost_estimate=pl.CostEstimate(
             flops=2 * 2 * slot_count * width * (units + 256), bytes_accessed=8 << 20, transcendentals=0
         ),
@@ -308,7 +361,9 @@
     units = w_gate.shape[1]
     pairs, tokens, _ = pick_t.shape
     tokens = tokens // 2
-    whole = lambda dims: pl.BlockSpec(dims, lambda k, place: (0,) * len(dims))
+    whole = lambda dims: pl.BlockSpec(
+        dims, lambda k, place: (0,) * len(dims), pipeline_mode=pl.Buffered(1)
+    )
     weight = pl.BlockSpec((2, units, LANES), lambda k, place: (0, 0, offset + k))
     out = jax.ShapeDtypeStruct((pairs, tokens, width), jnp.bfloat16)
     return pl.pallas_call(
@@ -321,7 +376,7 @@
             out_specs=[pl.BlockSpec((pairs, tokens, LANES), lambda k, place: (0, 0, k))] * 2,
             scratch_shapes=[pltpu.VMEM((2, grads.shape[1], LANES), jnp.bfloat16)],
         ),
-        compiler_params=pltpu.CompilerParams(vmem_limit_bytes=40 << 20),
+        compiler_params=pltpu.CompilerParams(vmem_limit_bytes=16 << 20),
         cost_estimate=pl.CostEstimate(
             flops=2 * 2 * grads.shape[1] * width * (2 * units + 256),
             bytes_accessed=10 << 20,
@@ -331,12 +386,8 @@
     )(place, grads, w_gate, w_up, pick_t)
 
 
-def plus(one, other):
-    return one.astype(jnp.float32) + other.astype(jnp.float32)
-
-
 def first_kernel(keep, came, send_l, keep_l, send_r, keep_r):
-    total = plus(keep[...], came[...]).astype(jnp.bfloat16)
+    total = keep[...] + came[...]
     middle = total.shape[-1] // 2
     keep_l[...] = total[:, 0, :, :middle]
     send_l[...] = total[:, 1, :, :middle]
@@ -360,15 +411,16 @@
         in_specs=[full, full],
         out_specs=[left_spec, left_spec, right_spec, right_spec],
         cost_estimate=pl.CostEstimate(flops=0, bytes_accessed=6 << 20, transcendentals=0),
+        compiler_params=pltpu.CompilerParams(vmem_limit_bytes=8 << 20),
         name="first_sum",
     )(keep, came)
 
 
 def second_kernel(keep_l, came_l, keep_r, came_r, send_l, left, send_r, right):
-    total = plus(keep_l[...], came_l[...]).astype(jnp.bfloat16)
+    total = keep_l[...] + came_l[...]
     left[...] = total[0:1]
     send_l[...] = total[1:2]
-    total = plus(keep_r[...], came_r[...]).astype(jnp.bfloat16)
+    total = keep_r[...] + came_r[...]
     right[...] = total[:, 0]
     send_r[...] = total[:, 1]
 
@@ -385,6 +437,7 @@
         in_specs=[left, left, right, right],
         out_specs=[pl.BlockSpec((1, piece, middle), lambda r: (r, 0, 0))] * 4,
         cost_estimate=pl.CostEstimate(flops=0, bytes_accessed=3 << 20, transcendentals=0),
+        compiler_params=pltpu.CompilerParams(vmem_limit_bytes=8 << 20),
         name="second_sum",
     )(keep_l, came_l, keep_r, came_r)
 
@@ -392,9 +445,9 @@
 def third_kernel(left, came_l, right, came_r, own, *sends):
     middle = left.shape[-1]
     for columns, one, other in ((slice(0, middle), left, came_l), (slice(middle, None), right, came_r)):
-        own[:, columns] = plus(one[0], other[0])
+        own[:, columns] = one[0].astype(jnp.float32) + other[0].astype(jnp.float32)
         for r, send in enumerate(sends):
-            send[:, columns] = plus(one[r + 1], other[r + 1]).astype(jnp.bfloat16)
+            send[:, columns] = one[r + 1] + other[r + 1]
 
 
 def third_sum(left, came_l, right, came_r):
@@ -404,6 +457,7 @@
         out_shape=(jax.ShapeDtypeStruct((piece, 2 * middle), jnp.float32),)
         + (jax.ShapeDtypeStruct((piece, 2 * middle), jnp.bfloat16),) * (lines - 1),
         cost_estimate=pl.CostEstimate(flops=0, bytes_accessed=2 << 20, transcendentals=0),
+        compiler_params=pltpu.CompilerParams(vmem_limit_bytes=8 << 20),
         name="third_sum",
     )(left, came_l, right, came_r)
 
@@ -431,29 +485,25 @@
     me, half = lax.axis_index("expert"), lax.axis_index("tp")
     place = jnp.stack([me % 2, me // 2 % 2, me // 4, half]).astype(jnp.int32)
 
-    sides = jnp.concatenate([gates.T, expert_ids.T.astype(jnp.float32)], axis=0)
-    sides = lax.all_gather(sides, "expert", axis=0)
+    *parts, table = prepare(place, cotangent, gates.T, expert_ids.T, piece, width)
     saved_gate, saved_up = saved_gate.swapaxes(1, 2), saved_up.swapaxes(1, 2)
-
-    own_c = swap(cotangent, "expert", 1)
-    near = lax.dynamic_slice_in_dim(cotangent, half * piece, piece, 0)
+    own_c, table_c = swap(cotangent, "expert", 1), swap(table, "expert", 1)
     far = lax.dynamic_slice_in_dim(cotangent, (1 - half) * piece, piece, 0)
     gathered = []
-    for chunk in range(CHUNKS):
-        columns = slice(chunk * width, (chunk + 1) * width)
-        near_part = near[:, columns]
-        line = jnp.stack([along_line(near_part, -r) for r in range(1, lines)])
-        first = swap(near_part, "expert", 2)
+    for chunk, part in enumerate(parts):
+        line = jnp.stack([along_line(part, -r) for r in range(1, lines)])
+        first = swap(part, "expert", 2)
         side = swap(line, "tp", 1)
         over = jnp.concatenate([first[None], swap(line, "expert", 2)])
         diag_l = swap(over[:, :, :middle], "tp", 1)
         far_part = far[None, :, chunk * width + middle:(chunk + 1) * width]
-        diag_r = swap(jnp.concatenate([far_part, side[:, :, middle:]]), "expert", 2)
+        diag_r = swap(jnp.concatenate([far_part, side[:, :, middle:width]]), "expert", 2)
         moved = []
         for array in (line, side, over, diag_l, diag_r):
             moved += [array, swap(array, "expert", 1)]
         gathered.append(moved)
-    pick, pick_t, gate = route(place, sides, capacity)
+    lines_n, lines_c, _, _, over_n, over_c = gathered[0][:6]
+    pick, pick_t, gate = route(place, table, table_c, lines_n, lines_c, over_n, over_c, capacity)
     rest = None
     for chunk in range(CHUNKS):
         if chunk == CHUNKS - 1:
@@ -474,6 +524,7 @@
     return pl.pallas_call(
         functools.partial(last_kernel, CHUNKS),
         out_shape=jax.ShapeDtypeStruct((piece, feature_dim), jnp.float32),
+        compiler_params=pltpu.CompilerParams(vmem_limit_bytes=8 << 20),
         name="last_sum",
     )(*terms)
 

time: 209 us -> 180 us (0.86)
  Pallas kernels: 52.4 us -> 31.3 us
  blocking collectives: 19.3 us -> 0 us
  waiting for transfers between devices: 54.4 us -> 68.8 us
  local copies, waits for them, and re-layouts: 35.5 us -> 27.8 us
  starting transfers between devices: 43.1 us -> 49.5 us
    all_gather x1 -> x0, blocking collectives: 19.3 us -> none  [tokens_body(): sides = lax.all_gather(sides, 'expert', axis=0)]
    ppermute x31 -> x32, waiting for transfers between devices: 26.7 us -> 41.7 us  [swap(): return lax.ppermute(value, axis, [(i, i ^ step) for i in range(count)])]
    pallas_call x2, Pallas kernels: 8.31 us -> 0.63 us  [first_sum(): pl.pallas_call(first_kernel, out_shape=(left, left, right, right), grid=(...]
    pallas_call x2, Pallas kernels: 7.22 us -> 0.31 us  [second_sum(): pl.pallas_call(second_kernel, out_shape=(out,) * 4, grid=(lines,), in_spe...]
    unnamed x102 -> x82, local copies, waits for them, and re-layouts: 32.6 us -> 26.9 us
    pallas_call x2, Pallas kernels: 4.13 us -> 0.12 us  [third_sum(): pl.pallas_call(third_kernel, out_shape=(jax.ShapeDtypeStruct((piece, 2 *...]
    ppermute x31 -> x32, starting transfers between devices: 23.5 us -> 27.1 us  [swap(): return lax.ppermute(value, axis, [(i, i ^ step) for i in range(count)])]
    ppermute x12, starting transfers between devices: 19.5 us -> 22.4 us  [along_line(): lax.ppermute(value, 'expert', [(i, (i + 4 * shift) % count) for i in rang...]
  transfers between devices with their start and end apart: 43 -> 44, of which waited for: 14 -> 16; matrix products, arithmetic and copies ran while one was open for 4% -> 4% of each run, Pallas kernels for 17% -> 8%
where the time goes in v3:
time: 180 us; the launch traced here: 179 us
  waiting for transfers between devices  68.8 us (38%)
  starting transfers between devices  49.5 us (28%)
  Pallas kernels  31.3 us (17%)
  local copies, waits for them, and re-layouts  27.8 us (15%)
    ppermute x32, waiting for transfers between devices, swap(): return lax.ppermute(value, axis, [(i, i ^ step) for i in range(count)])  41.7 us
    ppermute x12, waiting for transfers between devices, along_line(): lax.ppermute(value, 'expert', [(i, (i + 4 * shift) % count) for i in rang...  27.1 us
    ppermute x32, starting transfers between devices, swap(): return lax.ppermute(value, axis, [(i, i ^ step) for i in range(count)])  27.1 us
    unnamed x82, local copies, waits for them, and re-layouts  26.9 us
    ppermute x12, starting transfers between devices, along_line(): lax.ppermute(value, 'expert', [(i, (i + 4 * shift) % count) for i in rang...  22.4 us
    pallas_call x2, Pallas kernels, hidden(): pl.pallas_call(functools.partial(hidden_kernel, last), out_shape=out, gri...  14.7 us
    pallas_call x2, Pallas kernels, sums(): pl.pallas_call(sums_kernel, out_shape=(out, out), grid_spec=pltpu.Prefetc...  12.7 us
  transfers between devices with their start and end apart: 44, of which 16 were waited for; matrix products, arithmetic and copies ran while one was open for 4% of the time, Pallas kernels for 8%

profile of v3, /device:TPU:0, one launch (start us, length us, event | category | flops | bytes accessed | tf_op | source)
XLA Modules:
  0.0 179.1 jit_solution(14250766310260752014)
XLA Ops:
  0.1 1.0 copy-done.1
  3.1 5.1 %collective-permute-start.1 = (bf16[64,1024]{1,0:T(8,128)(2,1)S(1)}, bf16[64,1024]{1,0:T(8,128)(2,1)S(1)}, u32[]{:S(2)}, u32[]{:S(2)}) collective-permute-start(bf16[64,1024]{1,0:T(8,128)(2,1)S(1)} %get-tuple-element.39), channel_id=1, source_target_pairs={{0,24},{2,26},{4,28},{6,30},{8,0},{10,2},{12,4},{14,6},{16,8},{18,... | collective-permute-start | bytes 393224 | tf_op jit(solution)/shard_map/ppermute | solution.py:71
  8.2 1.0 collective-permute-start.3
  9.2 2.8 %collective-permute-start.15 = (bf16[64,1152]{1,0:T(8,128)(2,1)S(1)}, bf16[64,1152]{1,0:T(8,128)(2,1)S(1)}, u32[]{:S(2)}, u32[]{:S(2)}) collective-permute-start(bf16[64,1152]{1,0:T(8,128)(2,1)S(1)} %get-tuple-element.41), channel_id=1, source_target_pairs={{0,24},{2,26},{4,28},{6,30},{8,0},{10,2},{12,4},{14,6},{16,8},{18,... | collective-permute-start | bytes 442376 | tf_op jit(solution)/shard_map/ppermute | solution.py:71
  12.0 1.1 collective-permute-start.16
  13.1 7.6 %collective-permute-done.2 = bf16[64,1024]{1,0:T(8,128)(2,1)S(1)} collective-permute-done((bf16[64,1024]{1,0:T(8,128)(2,1)S(1)}, bf16[64,1024]{1,0:T(8,128)(2,1)S(1)}, u32[]{:S(2)}, u32[]{:S(2)}) %collective-permute-start.2) | collective-permute-done | bytes 131104 | tf_op jit(solution)/shard_map/ppermute | solution.py:71
  20.8 1.6 collective-permute-start.8
  22.4 1.5 collective-permute-start.5
  23.9 8.1 %collective-permute-done.16 = bf16[64,1152]{1,0:T(8,128)(2,1)S(1)} collective-permute-done((bf16[64,1152]{1,0:T(8,128)(2,1)S(1)}, bf16[64,1152]{1,0:T(8,128)(2,1)S(1)}, u32[]{:S(2)}, u32[]{:S(2)}) %collective-permute-start.16) | collective-permute-done | bytes 147488 | tf_op jit(solution)/shard_map/ppermute | solution.py:71
  32.1 1.6 collective-permute-start.20
  34.2 1.5 collective-permute-start.22
  35.7 1.6 collective-permute-start.19
  37.3 0.9 slice.26
  38.2 9.7 %collective-permute-done.7 = bf16[64,1024]{1,0:T(8,128)(2,1)S(1)} collective-permute-done((bf16[64,1024]{1,0:T(8,128)(2,1)S(1)}, bf16[64,1024]{1,0:T(8,128)(2,1)S(1)}, u32[]{:S(2)}, u32[]{:S(2)}) %collective-permute-start.7) | collective-permute-done | bytes 131104 | tf_op jit(solution)/shard_map/ppermute | solution.py:66
  48.6 0.9 collective-permute-done.19
  49.6 1.5 collective-permute-start.10
  52.4 0.8 copy-done.4
  53.8 1.6 collective-permute-start.26
  55.4 3.4 %collective-permute-done.10.refs_8_ = bf16[4,64,512]{2,1,0:T(8,128)(2,1)} collective-permute-done((bf16[4,64,512]{2,1,0:T(8,128)(2,1)S(1)}, bf16[4,64,512]{2,1,0:T(8,128)(2,1)}, u32[]{:S(2)}, u32[]{:S(2)}) %collective-permute-start.10) | collective-permute-done | bytes 262176 | tf_op jit(solution)/shard_map/ppermute | solution.py:66
  58.8 1.5 collective-permute-start.12
  60.3 3.6 %collective-permute-done.24.refs_8_ = bf16[4,64,512]{2,1,0:T(8,128)(2,1)S(1)} collective-permute-done((bf16[4,64,512]{2,1,0:T(8,128)(2,1)S(1)}, bf16[4,64,512]{2,1,0:T(8,128)(2,1)S(1)}, u32[]{:S(2)}, u32[]{:S(2)}) %collective-permute-start.24) | collective-permute-done | bytes 262176 | tf_op jit(solution)/shard_map/ppermute | solution.py:66
  63.9 0.9 pad_maximum_fusion.1.refs_6_
  66.0 1.8 %collective-permute-done.12.refs_10_ = bf16[4,64,512]{2,1,0:T(8,128)(2,1)} collective-permute-done((bf16[4,64,512]{2,1,0:T(8,128)(2,1)S(1)}, bf16[4,64,512]{2,1,0:T(8,128)(2,1)}, u32[]{:S(2)}, u32[]{:S(2)}) %collective-permute-start.12) | collective-permute-done | bytes 262176 | tf_op jit(solution)/shard_map/ppermute | solution.py:66
  71.0 0.8 copy-done.12
  71.9 2.4 %copy.9 = bf16[2,384,768]{1,2,0:T(8,128)(2,1)} copy(bf16[2,384,768]{2,1,0:T(8,128)(2,1)} %param.11) | data formatting | bytes 2359296 | tf_op args[3]
  74.3 2.5 %copy.10 = bf16[2,384,768]{1,2,0:T(8,128)(2,1)} copy(bf16[2,384,768]{2,1,0:T(8,128)(2,1)} %param.12) | data formatting | bytes 2359296 | tf_op args[4]
  76.8 1.1 copy-done.5
  77.9 1.0 copy-done.10
  78.9 1.1 copy-done.13
  79.9 1.0 copy-done.17
  82.3 1.4 route.1
  83.8 1.0 copy-done.11
  84.8 1.0 copy-done.15
  85.8 1.0 copy-done.18
  86.8 1.0 copy-done.20
  87.8 1.0 copy-done.22
  88.8 0.9 copy-done.24
  89.8 0.9 copy-done.26
  90.7 0.9 copy-done.28
  91.7 0.9 copy-done.30
  92.6 6.2 %hidden.2.refs_15_ = f32[2,768,384]{2,1,0:T(8,128)S(1)} custom-call(s32[4]{0:T(128)S(1)} %copy-done.35, bf16[128,2048]{1,0:T(8,128)(2,1)S(1)} %copy-done.3, bf16[128,2048]{1,0:T(8,128)(2,1)S(1)} %copy-done.15, bf16[3,64,1152]{2,1,0:T(8,128)(2,1)S(1)} %copy-done.11, bf16[3,64,1152]{2,1,0:T(8,128)(2,1)S(1)} %copy-done.18, bf16[3,64,1152]{2,1,0:T(8,128)(2,1)S(1)} %copy-done.20, ...), custom_call_target="tpu_custom_call" | custom-call | flops 2013265920 | bytes 8388608 | tf_op jit(solution)/shard_map/hidden/pallas_call | solution.py:317
  99.0 8.4 %hidden.3.grads = bf16[2,768,768]{2,1,0:T(8,128)(2,1)S(1)} custom-call(s32[4]{0:T(128)S(1)} %copy-done.35, bf16[128,2048]{1,0:T(8,128)(2,1)S(1)} %copy-done.3, bf16[128,2048]{1,0:T(8,128)(2,1)S(1)} %copy-done.15, bf16[3,64,1024]{2,1,0:T(8,128)(2,1)S(1)} %pad_maximum_fusion.3.refs_2_, bf16[3,64,1024]{2,1,0:T(8,128)(2,1)} %collective-permute-done.4.refs_3_, ...), custom_call_target="tpu_custom_call" | custom-call | flops 2013265920 | bytes 8388608 | tf_op jit(solution)/shard_map/hidden/pallas_call | solution.py:317
  107.4 6.4 %sums.3 = (bf16[8,128,1024]{2,1,0:T(8,128)(2,1)S(1)}, bf16[8,128,1024]{2,1,0:T(8,128)(2,1)S(1)}) custom-call(s32[4]{0:T(128)S(1)} %copy-done.35, bf16[2,768,768]{2,1,0:T(8,128)(2,1)S(1)} %hidden.3.grads, bf16[2,384,2048]{2,1,0:T(8,128)(2,1)S(1)} %copy-done.38, bf16[2,384,2048]{2,1,0:T(8,128)(2,1)S(1)} %copy-done.39, ...), custom_call_target="tpu_custom_call" | custom-call | flops 3221225472 | bytes 10485760 | tf_op jit(solution)/shard_map/sums/pallas_call | solution.py:369
  114.4 6.3 %sums.2 = (bf16[8,128,1024]{2,1,0:T(8,128)(2,1)S(1)}, bf16[8,128,1024]{2,1,0:T(8,128)(2,1)S(1)}) custom-call(s32[4]{0:T(128)S(1)} %copy-done.35, bf16[2,768,768]{2,1,0:T(8,128)(2,1)S(1)} %hidden.3.grads, bf16[2,384,2048]{2,1,0:T(8,128)(2,1)S(1)} %copy-done.38, bf16[2,384,2048]{2,1,0:T(8,128)(2,1)S(1)} %copy-done.39, ...), custom_call_target="tpu_custom_call" | custom-call | flops 3221225472 | bytes 10485760 | tf_op jit(solution)/shard_map/sums/pallas_call | solution.py:369
  121.2 1.5 collective-permute-start.37
  122.7 1.5 collective-permute-start.38
  125.3 1.5 collective-permute-start.29
  126.8 1.5 collective-permute-start.30
  128.3 7.6 %collective-permute-done.37.came_l = bf16[8,64,512]{2,1,0:T(8,128)(2,1)S(1)} collective-permute-done((bf16[8,64,512]{2,1,0:T(8,128)(2,1)S(1)}, bf16[8,64,512]{2,1,0:T(8,128)(2,1)S(1)}, u32[]{:S(2)}, u32[]{:S(2)}) %collective-permute-start.37) | collective-permute-done | bytes 524320 | tf_op jit(solution)/shard_map/ppermute | solution.py:66
  135.9 1.5 collective-permute-done.38.came_r
  137.6 1.6 collective-permute-start.39
  139.7 7.4 %collective-permute-done.29.came_l = bf16[8,64,512]{2,1,0:T(8,128)(2,1)S(1)} collective-permute-done((bf16[8,64,512]{2,1,0:T(8,128)(2,1)S(1)}, bf16[8,64,512]{2,1,0:T(8,128)(2,1)S(1)}, u32[]{:S(2)}, u32[]{:S(2)}) %collective-permute-start.29) | collective-permute-done | bytes 524320 | tf_op jit(solution)/shard_map/ppermute | solution.py:66
  147.2 1.5 collective-permute-done.30.came_r
  148.9 1.6 collective-permute-start.31
  151.0 3.3 %collective-permute-done.39.came_l = bf16[4,64,512]{2,1,0:T(8,128)(2,1)S(1)} collective-permute-done((bf16[4,64,512]{2,1,0:T(8,128)(2,1)S(1)}, bf16[4,64,512]{2,1,0:T(8,128)(2,1)S(1)}, u32[]{:S(2)}, u32[]{:S(2)}) %collective-permute-start.39) | collective-permute-done | bytes 262176 | tf_op jit(solution)/shard_map/ppermute | solution.py:66
  154.4 2.2 %collective-permute-start.41 = (bf16[64,1024]{1,0:T(8,128)(2,1)S(1)}, bf16[64,1024]{1,0:T(8,128)(2,1)S(1)}, u32[]{:S(2)}, u32[]{:S(2)}) collective-permute-start(bf16[64,1024]{1,0:T(8,128)(2,1)S(1)} %get-tuple-element.70), channel_id=1, source_target_pairs={{0,8},{2,10},{4,12},{6,14},{8,16},{10,18},{12,20},{14,22},{16,24},... | collective-permute-start | bytes 393224 | tf_op jit(solution)/shard_map/ppermute | solution.py:71
  156.6 2.5 %collective-permute-start.42 = (bf16[64,1024]{1,0:T(8,128)(2,1)S(1)}, bf16[64,1024]{1,0:T(8,128)(2,1)S(1)}, u32[]{:S(2)}, u32[]{:S(2)}) collective-permute-start(bf16[64,1024]{1,0:T(8,128)(2,1)S(1)} %get-tuple-element.71), channel_id=1, source_target_pairs={{0,16},{2,18},{4,20},{6,22},{8,24},{10,26},{12,28},{14,30},{16,0},... | collective-permute-start | bytes 393224 | tf_op jit(solution)/shard_map/ppermute | solution.py:71
  159.1 2.8 %collective-permute-start.43 = (bf16[64,1024]{1,0:T(8,128)(2,1)S(1)}, bf16[64,1024]{1,0:T(8,128)(2,1)S(1)}, u32[]{:S(2)}, u32[]{:S(2)}) collective-permute-start(bf16[64,1024]{1,0:T(8,128)(2,1)S(1)} %get-tuple-element.72), channel_id=1, source_target_pairs={{0,24},{2,26},{4,28},{6,30},{8,0},{10,2},{12,4},{14,6},{16,8},{18,... | collective-permute-start | bytes 393224 | tf_op jit(solution)/shard_map/ppermute | solution.py:71
  162.1 1.9 %collective-permute-start.34 = (bf16[64,1024]{1,0:T(8,128)(2,1)S(1)}, bf16[64,1024]{1,0:T(8,128)(2,1)S(1)}, u32[]{:S(2)}, u32[]{:S(2)}) collective-permute-start(bf16[64,1024]{1,0:T(8,128)(2,1)S(1)} %get-tuple-element.57), channel_id=1, source_target_pairs={{0,16},{2,18},{4,20},{6,22},{8,24},{10,26},{12,28},{14,30},{16,0},... | collective-permute-start | bytes 393224 | tf_op jit(solution)/shard_map/ppermute | solution.py:71
  164.0 2.8 %collective-permute-start.35 = (bf16[64,1024]{1,0:T(8,128)(2,1)S(1)}, bf16[64,1024]{1,0:T(8,128)(2,1)S(1)}, u32[]{:S(2)}, u32[]{:S(2)}) collective-permute-start(bf16[64,1024]{1,0:T(8,128)(2,1)S(1)} %get-tuple-element.58), channel_id=1, source_target_pairs={{0,24},{2,26},{4,28},{6,30},{8,0},{10,2},{12,4},{14,6},{16,8},{18,... | collective-permute-start | bytes 393224 | tf_op jit(solution)/shard_map/ppermute | solution.py:71
  166.8 3.5 %collective-permute-done.42.refs_6_ = bf16[64,1024]{1,0:T(8,128)(2,1)S(1)} collective-permute-done((bf16[64,1024]{1,0:T(8,128)(2,1)S(1)}, bf16[64,1024]{1,0:T(8,128)(2,1)S(1)}, u32[]{:S(2)}, u32[]{:S(2)}) %collective-permute-start.42) | collective-permute-done | bytes 131104 | tf_op jit(solution)/shard_map/ppermute | solution.py:71
  170.3 1.7 collective-permute-done.33.refs_1_
  172.0 6.2 %collective-permute-done.34.refs_2_ = bf16[64,1024]{1,0:T(8,128)(2,1)S(1)} collective-permute-done((bf16[64,1024]{1,0:T(8,128)(2,1)S(1)}, bf16[64,1024]{1,0:T(8,128)(2,1)S(1)}, u32[]{:S(2)}, u32[]{:S(2)}) %collective-permute-start.34) | collective-permute-done | bytes 131104 | tf_op jit(solution)/shard_map/ppermute | solution.py:71
  178.2 0.9 last_sum.1
  (131 shorter events, 14.6 us)
Async XLA Ops:
  0.1 31.9 %copy-start.33 = (s32[4]{0:T(128)}, s32[4]{0:T(128)S(1)}, u32[]{:S(2)}) copy-start(s32[4]{0:T(128)S(1)} %pad_add_fusion.place) | copy-start | bytes 52
  0.1 1.0 copy-start.1
  2.5 33.2 %copy-start.2 = (bf16[128,2048]{1,0:T(8,128)(2,1)S(1)}, bf16[128,2048]{1,0:T(8,128)(2,1)}, u32[]{:S(2)}) copy-start(bf16[128,2048]{1,0:T(8,128)(2,1)} %refs_0_.3) | copy-start | bytes 1572868
  3.1 10.1 %collective-permute-start.1 = (bf16[64,1024]{1,0:T(8,128)(2,1)S(1)}, bf16[64,1024]{1,0:T(8,128)(2,1)S(1)}, u32[]{:S(2)}, u32[]{:S(2)}) collective-permute-start(bf16[64,1024]{1,0:T(8,128)(2,1)S(1)} %get-tuple-element.39), channel_id=1, source_target_pairs={{0,24},{2,26},{4,28},{6,30},{8,0},{10,2},{12,4},{14,6},{16,8},{18,... | collective-permute-start | bytes 393224 | tf_op jit(solution)/shard_map/ppermute | solution.py:71
  8.2 12.6 %collective-permute-start.2 = (bf16[64,1024]{1,0:T(8,128)(2,1)S(1)}, bf16[64,1024]{1,0:T(8,128)(2,1)S(1)}, u32[]{:S(2)}, u32[]{:S(2)}) collective-permute-start(bf16[64,1024]{1,0:T(8,128)(2,1)S(1)} %get-tuple-element.39), channel_id=1, source_target_pairs={{0,16},{2,18},{4,20},{6,22},{8,24},{10,26},{12,28},{14,30},{16,0},... | collective-permute-start | bytes 393224 | tf_op jit(solution)/shard_map/ppermute | solution.py:71
  8.2 12.6 %collective-permute-start.3 = (bf16[64,1024]{1,0:T(8,128)(2,1)S(1)}, bf16[64,1024]{1,0:T(8,128)(2,1)S(1)}, u32[]{:S(2)}, u32[]{:S(2)}) collective-permute-start(bf16[64,1024]{1,0:T(8,128)(2,1)S(1)} %get-tuple-element.39), channel_id=1, source_target_pairs={{0,8},{2,10},{4,12},{6,14},{8,16},{10,18},{12,20},{14,22},{16,24},... | collective-permute-start | bytes 393224 | tf_op jit(solution)/shard_map/ppermute | solution.py:71
  9.2 14.7 %collective-permute-start.15 = (bf16[64,1152]{1,0:T(8,128)(2,1)S(1)}, bf16[64,1152]{1,0:T(8,128)(2,1)S(1)}, u32[]{:S(2)}, u32[]{:S(2)}) collective-permute-start(bf16[64,1152]{1,0:T(8,128)(2,1)S(1)} %get-tuple-element.41), channel_id=1, source_target_pairs={{0,24},{2,26},{4,28},{6,30},{8,0},{10,2},{12,4},{14,6},{16,8},{18,... | collective-permute-start | bytes 442376 | tf_op jit(solution)/shard_map/ppermute | solution.py:71
  12.0 20.0 %collective-permute-start.16 = (bf16[64,1152]{1,0:T(8,128)(2,1)S(1)}, bf16[64,1152]{1,0:T(8,128)(2,1)S(1)}, u32[]{:S(2)}, u32[]{:S(2)}) collective-permute-start(bf16[64,1152]{1,0:T(8,128)(2,1)S(1)} %get-tuple-element.41), channel_id=1, source_target_pairs={{0,16},{2,18},{4,20},{6,22},{8,24},{10,26},{12,28},{14,30},{16,0},... | collective-permute-start | bytes 442376 | tf_op jit(solution)/shard_map/ppermute | solution.py:71
  13.1 18.9 %collective-permute-start.17 = (bf16[64,1152]{1,0:T(8,128)(2,1)S(1)}, bf16[64,1152]{1,0:T(8,128)(2,1)S(1)}, u32[]{:S(2)}, u32[]{:S(2)}) collective-permute-start(bf16[64,1152]{1,0:T(8,128)(2,1)S(1)} %get-tuple-element.41), channel_id=1, source_target_pairs={{0,8},{2,10},{4,12},{6,14},{8,16},{10,18},{12,20},{14,22},{16,24},... | collective-permute-start | bytes 442376 | tf_op jit(solution)/shard_map/ppermute | solution.py:71
  20.8 27.2 %collective-permute-start.8 = (bf16[3,64,1024]{2,1,0:T(8,128)(2,1)S(1)}, bf16[3,64,1024]{2,1,0:T(8,128)(2,1)S(1)}, u32[]{:S(2)}, u32[]{:S(2)}) collective-permute-start(bf16[3,64,1024]{2,1,0:T(8,128)(2,1)S(1)} %pad_maximum_fusion.3.refs_2_), channel_id=1, source_target_pairs={{0,4},{2,6},{4,0},{6,2},{8,12},{10,14},{12,8},{14,10},{16,20},{18,... | collective-permute-start | bytes 1179656 | tf_op jit(solution)/shard_map/ppermute | solution.py:66
  22.4 13.3 %collective-permute-start.5 = (bf16[3,64,1024]{2,1,0:T(8,128)(2,1)S(1)}, bf16[3,64,1024]{2,1,0:T(8,128)(2,1)}, u32[]{:S(2)}, u32[]{:S(2)}) collective-permute-start(bf16[3,64,1024]{2,1,0:T(8,128)(2,1)S(1)} %pad_maximum_fusion.3.refs_2_), channel_id=1, source_target_pairs={{0,1},{1,0},{2,3},{3,2},{4,5},{5,4},{6,7},{7,6},{8,9},{9,8},{10,11... | collective-permute-start | bytes 1179656 | tf_op jit(solution)/shard_map/ppermute | solution.py:66
  32.1 19.7 %copy-start.9 = (bf16[3,64,1152]{2,1,0:T(8,128)(2,1)}, bf16[3,64,1152]{2,1,0:T(8,128)(2,1)S(1)}, u32[]{:S(2)}) copy-start(bf16[3,64,1152]{2,1,0:T(8,128)(2,1)S(1)} %pad_maximum_fusion.2.lines.refs_2_) | copy-start | bytes 1327108
  32.1 17.5 %collective-permute-start.20 = (bf16[3,64,1152]{2,1,0:T(8,128)(2,1)S(1)}, bf16[3,64,1152]{2,1,0:T(8,128)(2,1)S(1)}, u32[]{:S(2)}, u32[]{:S(2)}) collective-permute-start(bf16[3,64,1152]{2,1,0:T(8,128)(2,1)S(1)} %pad_maximum_fusion.2.lines.refs_2_), channel_id=1, source_target_pairs={{0,4},{2,6},{4,0},{6,2},{8,12},{10,14},{12,8},{14,10},{16,20},{18,... | collective-permute-start | bytes 1327112 | tf_op jit(solution)/shard_map/ppermute | solution.py:66
  33.7 14.3 %collective-permute-start.7 = (bf16[64,1024]{1,0:T(8,128)(2,1)S(1)}, bf16[64,1024]{1,0:T(8,128)(2,1)S(1)}, u32[]{:S(2)}, u32[]{:S(2)}) collective-permute-start(bf16[64,1024]{1,0:T(8,128)(2,1)S(1)} %get-tuple-element.39), channel_id=1, source_target_pairs={{0,4},{2,6},{4,0},{6,2},{8,12},{10,14},{12,8},{14,10},{16,20},{18,... | collective-permute-start | bytes 393224 | tf_op jit(solution)/shard_map/ppermute | solution.py:66
  34.2 16.9 %collective-permute-start.22 = (bf16[3,64,1152]{2,1,0:T(8,128)(2,1)S(1)}, bf16[3,64,1152]{2,1,0:T(8,128)(2,1)S(1)}, u32[]{:S(2)}, u32[]{:S(2)}) collective-permute-start(bf16[3,64,1152]{2,1,0:T(8,128)(2,1)S(1)} %pad_maximum_fusion.2.lines.refs_2_), channel_id=1, source_target_pairs={{0,1},{1,0},{2,3},{3,2},{4,5},{5,4},{6,7},{7,6},{8,9},{9,8},{10,11... | collective-permute-start | bytes 1327112 | tf_op jit(solution)/shard_map/ppermute | solution.py:66
  35.7 13.8 %collective-permute-start.19 = (bf16[64,1152]{1,0:T(8,128)(2,1)S(1)}, bf16[64,1152]{1,0:T(8,128)(2,1)S(1)}, u32[]{:S(2)}, u32[]{:S(2)}) collective-permute-start(bf16[64,1152]{1,0:T(8,128)(2,1)S(1)} %get-tuple-element.41), channel_id=1, source_target_pairs={{0,4},{2,6},{4,0},{6,2},{8,12},{10,14},{12,8},{14,10},{16,20},{18,... | collective-permute-start | bytes 442376 | tf_op jit(solution)/shard_map/ppermute | solution.py:66
  48.0 5.3 %collective-permute-start = (bf16[128,2048]{1,0:T(8,128)(2,1)S(1)}, bf16[128,2048]{1,0:T(8,128)(2,1)S(1)}, u32[]{:S(2)}, u32[]{:S(2)}) collective-permute-start(bf16[128,2048]{1,0:T(8,128)(2,1)S(1)} %copy-done.2), channel_id=1, source_target_pairs={{0,2},{2,0},{4,6},{6,4},{8,10},{10,8},{12,14},{14,12},{16,18},{18,... | collective-permute-start | bytes 1572872 | tf_op jit(solution)/shard_map/ppermute | solution.py:66
  48.0 3.8 %collective-permute-start.14 = (bf16[64,128]{1,0:T(8,128)(2,1)S(1)}, bf16[64,128]{1,0:T(8,128)(2,1)S(1)}, u32[]{:S(2)}, u32[]{:S(2)}) collective-permute-start(bf16[64,128]{1,0:T(8,128)(2,1)S(1)} %get-tuple-element.40.own), channel_id=1, source_target_pairs={{0,2},{2,0},{4,6},{6,4},{8,10},{10,8},{12,14},{14,12},{16,18},{18,... | collective-permute-start | bytes 49160 | tf_op jit(solution)/shard_map/ppermute | solution.py:66
  49.6 4.2 %collective-permute-start.18 = (bf16[3,64,1152]{2,1,0:T(8,128)(2,1)S(1)}, bf16[3,64,1152]{2,1,0:T(8,128)(2,1)S(1)}, u32[]{:S(2)}, u32[]{:S(2)}) collective-permute-start(bf16[3,64,1152]{2,1,0:T(8,128)(2,1)S(1)} %pad_maximum_fusion.2.lines.refs_2_), channel_id=1, source_target_pairs={{0,2},{2,0},{4,6},{6,4},{8,10},{10,8},{12,14},{14,12},{16,18},{18,... | collective-permute-start | bytes 1327112 | tf_op jit(solution)/shard_map/ppermute | solution.py:66
  49.6 9.2 %collective-permute-start.10 = (bf16[4,64,512]{2,1,0:T(8,128)(2,1)S(1)}, bf16[4,64,512]{2,1,0:T(8,128)(2,1)}, u32[]{:S(2)}, u32[]{:S(2)}) collective-permute-start(bf16[4,64,512]{2,1,0:T(8,128)(2,1)S(1)} %fusion), channel_id=1, source_target_pairs={{0,1},{1,0},{2,3},{3,2},{4,5},{5,4},{6,7},{7,6},{8,9},{9,8},{10,11... | collective-permute-start | bytes 786440 | tf_op jit(solution)/shard_map/ppermute | solution.py:66
  51.1 20.8 %copy-start.19 = (bf16[3,64,1152]{2,1,0:T(8,128)(2,1)}, bf16[3,64,1152]{2,1,0:T(8,128)(2,1)S(1)}, u32[]{:S(2)}) copy-start(bf16[3,64,1152]{2,1,0:T(8,128)(2,1)S(1)} %collective-permute-done.22.refs_4_) | copy-start | bytes 1327108
  51.1 12.8 %collective-permute-start.24 = (bf16[4,64,512]{2,1,0:T(8,128)(2,1)S(1)}, bf16[4,64,512]{2,1,0:T(8,128)(2,1)S(1)}, u32[]{:S(2)}, u32[]{:S(2)}) collective-permute-start(bf16[4,64,512]{2,1,0:T(8,128)(2,1)S(1)} %fusion.1), channel_id=1, source_target_pairs={{0,1},{1,0},{2,3},{3,2},{4,5},{5,4},{6,7},{7,6},{8,9},{9,8},{10,11... | collective-permute-start | bytes 786440 | tf_op jit(solution)/shard_map/ppermute | solution.py:66
  52.4 18.6 %collective-permute-start.21 = (bf16[4,64,1152]{2,1,0:T(8,128)(2,1)S(1)}, bf16[4,64,1152]{2,1,0:T(8,128)(2,1)S(1)}, u32[]{:S(2)}, u32[]{:S(2)}) collective-permute-start(bf16[4,64,1152]{2,1,0:T(8,128)(2,1)S(1)} %pad_maximum_fusion.over.refs_6_), channel_id=1, source_target_pairs={{0,2},{2,0},{4,6},{6,4},{8,10},{10,8},{12,14},{14,12},{16,18},{18,... | collective-permute-start | bytes 1769480 | tf_op jit(solution)/shard_map/ppermute | solution.py:66
  53.2 17.8 %copy-start.14 = (bf16[128,2048]{1,0:T(8,128)(2,1)}, bf16[128,2048]{1,0:T(8,128)(2,1)S(1)}, u32[]{:S(2)}) copy-start(bf16[128,2048]{1,0:T(8,128)(2,1)S(1)} %collective-permute-done.refs_1_) | copy-start | bytes 1572868
  53.2 14.6 %collective-permute-start.23 = (bf16[3,64,1152]{2,1,0:T(8,128)(2,1)S(1)}, bf16[3,64,1152]{2,1,0:T(8,128)(2,1)S(1)}, u32[]{:S(2)}, u32[]{:S(2)}) collective-permute-start(bf16[3,64,1152]{2,1,0:T(8,128)(2,1)S(1)} %collective-permute-done.22.refs_4_), channel_id=1, source_target_pairs={{0,2},{2,0},{4,6},{6,4},{8,10},{10,8},{12,14},{14,12},{16,18},{18,... | collective-permute-start | bytes 1327112 | tf_op jit(solution)/shard_map/ppermute | solution.py:66
  53.8 17.2 %copy-start.16 = (bf16[3,64,1152]{2,1,0:T(8,128)(2,1)}, bf16[3,64,1152]{2,1,0:T(8,128)(2,1)S(1)}, u32[]{:S(2)}) copy-start(bf16[3,64,1152]{2,1,0:T(8,128)(2,1)S(1)} %collective-permute-done.18.lines_c.refs_3_) | copy-start | bytes 1327108
  53.8 11.0 %collective-permute-start.26 = (bf16[4,64,512]{2,1,0:T(8,128)(2,1)S(1)}, bf16[4,64,512]{2,1,0:T(8,128)(2,1)S(1)}, u32[]{:S(2)}, u32[]{:S(2)}) collective-permute-start(bf16[4,64,512]{2,1,0:T(8,128)(2,1)S(1)} %pad_maximum_fusion.5), channel_id=1, source_target_pairs={{0,4},{2,6},{4,0},{6,2},{8,12},{10,14},{12,8},{14,10},{16,20},{18,... | collective-permute-start | bytes 786440 | tf_op jit(solution)/shard_map/ppermute | solution.py:66
  58.8 9.0 %collective-permute-start.12 = (bf16[4,64,512]{2,1,0:T(8,128)(2,1)S(1)}, bf16[4,64,512]{2,1,0:T(8,128)(2,1)}, u32[]{:S(2)}, u32[]{:S(2)}) collective-permute-start(bf16[4,64,512]{2,1,0:T(8,128)(2,1)S(1)} %pad_maximum_fusion.4), channel_id=1, source_target_pairs={{0,4},{2,6},{4,0},{6,2},{8,12},{10,14},{12,8},{14,10},{16,20},{18,... | collective-permute-start | bytes 786440 | tf_op jit(solution)/shard_map/ppermute | solution.py:66
  63.9 8.0 %copy-start.23 = (bf16[4,64,512]{2,1,0:T(8,128)(2,1)}, bf16[4,64,512]{2,1,0:T(8,128)(2,1)S(1)}, u32[]{:S(2)}) copy-start(bf16[4,64,512]{2,1,0:T(8,128)(2,1)S(1)} %collective-permute-done.24.refs_8_) | copy-start | bytes 786436
  63.9 5.2 %collective-permute-start.25 = (bf16[4,64,512]{2,1,0:T(8,128)(2,1)S(1)}, bf16[4,64,512]{2,1,0:T(8,128)(2,1)S(1)}, u32[]{:S(2)}, u32[]{:S(2)}) collective-permute-start(bf16[4,64,512]{2,1,0:T(8,128)(2,1)S(1)} %collective-permute-done.24.refs_8_), channel_id=1, source_target_pairs={{0,2},{2,0},{4,6},{6,4},{8,10},{10,8},{12,14},{14,12},{16,18},{18,... | collective-permute-start | bytes 786440 | tf_op jit(solution)/shard_map/ppermute | solution.py:66
  64.8 5.0 %collective-permute-start.27 = (bf16[4,64,512]{2,1,0:T(8,128)(2,1)S(1)}, bf16[4,64,512]{2,1,0:T(8,128)(2,1)S(1)}, u32[]{:S(2)}, u32[]{:S(2)}) collective-permute-start(bf16[4,64,512]{2,1,0:T(8,128)(2,1)S(1)} %collective-permute-done.26.refs_10_), channel_id=1, source_target_pairs={{0,2},{2,0},{4,6},{6,4},{8,10},{10,8},{12,14},{14,12},{16,18},{18,... | collective-permute-start | bytes 786440 | tf_op jit(solution)/shard_map/ppermute | solution.py:66
  67.8 31.1 %collective-permute-start.9 = (bf16[4,64,1024]{2,1,0:T(8,128)(2,1)}, bf16[4,64,1024]{2,1,0:T(8,128)(2,1)}, u32[]{:S(2)}, u32[]{:S(2)}) collective-permute-start(bf16[4,64,1024]{2,1,0:T(8,128)(2,1)} %pad_maximum_fusion.1.refs_6_), channel_id=1, source_target_pairs={{0,2},{2,0},{4,6},{6,4},{8,10},{10,8},{12,14},{14,12},{16,18},{18,... | collective-permute-start | bytes 1572872 | tf_op jit(solution)/shard_map/ppermute | solution.py:66
  68.6 30.3 %collective-permute-start.4 = (bf16[3,64,1024]{2,1,0:T(8,128)(2,1)S(1)}, bf16[3,64,1024]{2,1,0:T(8,128)(2,1)}, u32[]{:S(2)}, u32[]{:S(2)}) collective-permute-start(bf16[3,64,1024]{2,1,0:T(8,128)(2,1)S(1)} %pad_maximum_fusion.3.refs_2_), channel_id=1, source_target_pairs={{0,2},{2,0},{4,6},{6,4},{8,10},{10,8},{12,14},{14,12},{16,18},{18,... | collective-permute-start | bytes 1179656 | tf_op jit(solution)/shard_map/ppermute | solution.py:66
  69.8 29.1 %collective-permute-start.6 = (bf16[3,64,1024]{2,1,0:T(8,128)(2,1)}, bf16[3,64,1024]{2,1,0:T(8,128)(2,1)}, u32[]{:S(2)}, u32[]{:S(2)}) collective-permute-start(bf16[3,64,1024]{2,1,0:T(8,128)(2,1)} %collective-permute-done.5.refs_4_), channel_id=1, source_target_pairs={{0,2},{2,0},{4,6},{6,4},{8,10},{10,8},{12,14},{14,12},{16,18},{18,... | collective-permute-start | bytes 1179656 | tf_op jit(solution)/shard_map/ppermute | solution.py:66
  70.5 28.4 %collective-permute-start.11 = (bf16[4,64,512]{2,1,0:T(8,128)(2,1)}, bf16[4,64,512]{2,1,0:T(8,128)(2,1)}, u32[]{:S(2)}, u32[]{:S(2)}) collective-permute-start(bf16[4,64,512]{2,1,0:T(8,128)(2,1)} %collective-permute-done.10.refs_8_), channel_id=1, source_target_pairs={{0,2},{2,0},{4,6},{6,4},{8,10},{10,8},{12,14},{14,12},{16,18},{18,... | collective-permute-start | bytes 786440 | tf_op jit(solution)/shard_map/ppermute | solution.py:66
  71.9 27.1 %collective-permute-start.13 = (bf16[4,64,512]{2,1,0:T(8,128)(2,1)}, bf16[4,64,512]{2,1,0:T(8,128)(2,1)}, u32[]{:S(2)}, u32[]{:S(2)}) collective-permute-start(bf16[4,64,512]{2,1,0:T(8,128)(2,1)} %collective-permute-done.12.refs_10_), channel_id=1, source_target_pairs={{0,2},{2,0},{4,6},{6,4},{8,10},{10,8},{12,14},{14,12},{16,18},{18,... | collective-permute-start | bytes 786440 | tf_op jit(solution)/shard_map/ppermute | solution.py:66
  74.3 9.4 %copy-start = (bf16[2,384,2048]{2,1,0:T(8,128)(2,1)S(1)}, bf16[2,384,2048]{2,1,0:T(8,128)(2,1)}, u32[]{:S(2)}) copy-start(bf16[2,384,2048]{2,1,0:T(8,128)(2,1)} %refs_14_.3) | copy-start | bytes 9437188
  76.8 1.1 copy-start.5
  78.9 1.1 copy-start.13
  82.3 1.4 copy-start.3
  82.3 1.5 copy-start.6
  82.3 1.5 copy-start.35
  83.7 1.0 copy-start.11
  84.8 1.0 copy-start.15
  92.6 6.3 %copy-start.7 = (bf16[2,384,768]{1,2,0:T(8,128)(2,1)S(1)}, bf16[2,384,768]{1,2,0:T(8,128)(2,1)}, u32[]{:S(2)}) copy-start(bf16[2,384,768]{1,2,0:T(8,128)(2,1)} %copy.9) | copy-start | bytes 3538948
  92.6 6.3 %copy-start.8 = (bf16[2,384,768]{1,2,0:T(8,128)(2,1)S(1)}, bf16[2,384,768]{1,2,0:T(8,128)(2,1)}, u32[]{:S(2)}) copy-start(bf16[2,384,768]{1,2,0:T(8,128)(2,1)} %copy.10) | copy-start | bytes 3538948
  99.0 8.5 %copy-start.38 = (bf16[2,384,2048]{2,1,0:T(8,128)(2,1)S(1)}, bf16[2,384,2048]{2,1,0:T(8,128)(2,1)}, u32[]{:S(2)}) copy-start(bf16[2,384,2048]{2,1,0:T(8,128)(2,1)} %w_gate.3) | copy-start | bytes 9437188
  99.0 8.4 %copy-start.39 = (bf16[2,384,2048]{2,1,0:T(8,128)(2,1)S(1)}, bf16[2,384,2048]{2,1,0:T(8,128)(2,1)}, u32[]{:S(2)}) copy-start(bf16[2,384,2048]{2,1,0:T(8,128)(2,1)} %w_up.3) | copy-start | bytes 9437188
  113.8 7.0 %collective-permute-start.36 = (bf16[8,128,1024]{2,1,0:T(8,128)(2,1)S(1)}, bf16[8,128,1024]{2,1,0:T(8,128)(2,1)S(1)}, u32[]{:S(2)}, u32[]{:S(2)}) collective-permute-start(bf16[8,128,1024]{2,1,0:T(8,128)(2,1)S(1)} %get-tuple-element.60), channel_id=1, source_target_pairs={{0,2},{2,0},{4,6},{6,4},{8,10},{10,8},{12,14},{14,12},{16,18},{18,... | collective-permute-start | bytes 6291464 | tf_op jit(solution)/shard_map/ppermute | solution.py:66
  120.7 4.2 %collective-permute-start.28 = (bf16[8,128,1024]{2,1,0:T(8,128)(2,1)S(1)}, bf16[8,128,1024]{2,1,0:T(8,128)(2,1)S(1)}, u32[]{:S(2)}, u32[]{:S(2)}) collective-permute-start(bf16[8,128,1024]{2,1,0:T(8,128)(2,1)S(1)} %get-tuple-element.46), channel_id=1, source_target_pairs={{0,2},{2,0},{4,6},{6,4},{8,10},{10,8},{12,14},{14,12},{16,18},{18,... | collective-permute-start | bytes 6291464 | tf_op jit(solution)/shard_map/ppermute | solution.py:66
  121.2 14.8 %collective-permute-start.37 = (bf16[8,64,512]{2,1,0:T(8,128)(2,1)S(1)}, bf16[8,64,512]{2,1,0:T(8,128)(2,1)S(1)}, u32[]{:S(2)}, u32[]{:S(2)}) collective-permute-start(bf16[8,64,512]{2,1,0:T(8,128)(2,1)S(1)} %get-tuple-element.62), channel_id=1, source_target_pairs={{0,1},{1,0},{2,3},{3,2},{4,5},{5,4},{6,7},{7,6},{8,9},{9,8},{10,11... | collective-permute-start | bytes 1572872 | tf_op jit(solution)/shard_map/ppermute | solution.py:66
  122.7 14.8 %collective-permute-start.38 = (bf16[4,2,64,512]{3,2,1,0:T(8,128)(2,1)S(1)}, bf16[4,2,64,512]{3,2,1,0:T(8,128)(2,1)S(1)}, u32[]{:S(2)}, u32[]{:S(2)}) collective-permute-start(bf16[4,2,64,512]{3,2,1,0:T(8,128)(2,1)S(1)} %get-tuple-element.64), channel_id=1, source_target_pairs={{0,4},{2,6},{4,0},{6,2},{8,12},{10,14},{12,8},{14,10},{16,20},{18,... | collective-permute-start | bytes 1572872 | tf_op jit(solution)/shard_map/ppermute | solution.py:66
  125.3 21.9 %collective-permute-start.29 = (bf16[8,64,512]{2,1,0:T(8,128)(2,1)S(1)}, bf16[8,64,512]{2,1,0:T(8,128)(2,1)S(1)}, u32[]{:S(2)}, u32[]{:S(2)}) collective-permute-start(bf16[8,64,512]{2,1,0:T(8,128)(2,1)S(1)} %get-tuple-element.48), channel_id=1, source_target_pairs={{0,1},{1,0},{2,3},{3,2},{4,5},{5,4},{6,7},{7,6},{8,9},{9,8},{10,11... | collective-permute-start | bytes 1572872 | tf_op jit(solution)/shard_map/ppermute | solution.py:66
  126.8 21.9 %collective-permute-start.30 = (bf16[4,2,64,512]{3,2,1,0:T(8,128)(2,1)S(1)}, bf16[4,2,64,512]{3,2,1,0:T(8,128)(2,1)S(1)}, u32[]{:S(2)}, u32[]{:S(2)}) collective-permute-start(bf16[4,2,64,512]{3,2,1,0:T(8,128)(2,1)S(1)} %get-tuple-element.50), channel_id=1, source_target_pairs={{0,4},{2,6},{4,0},{6,2},{8,12},{10,14},{12,8},{14,10},{16,20},{18,... | collective-permute-start | bytes 1572872 | tf_op jit(solution)/shard_map/ppermute | solution.py:66
  137.6 16.7 %collective-permute-start.39 = (bf16[4,64,512]{2,1,0:T(8,128)(2,1)S(1)}, bf16[4,64,512]{2,1,0:T(8,128)(2,1)S(1)}, u32[]{:S(2)}, u32[]{:S(2)}) collective-permute-start(bf16[4,64,512]{2,1,0:T(8,128)(2,1)S(1)} %get-tuple-element.66), channel_id=1, source_target_pairs={{0,4},{2,6},{4,0},{6,2},{8,12},{10,14},{12,8},{14,10},{16,20},{18,... | collective-permute-start | bytes 786440 | tf_op jit(solution)/shard_map/ppermute | solution.py:66
  139.2 15.1 %collective-permute-start.40 = (bf16[4,64,512]{2,1,0:T(8,128)(2,1)S(1)}, bf16[4,64,512]{2,1,0:T(8,128)(2,1)S(1)}, u32[]{:S(2)}, u32[]{:S(2)}) collective-permute-start(bf16[4,64,512]{2,1,0:T(8,128)(2,1)S(1)} %get-tuple-element.68), channel_id=1, source_target_pairs={{0,1},{1,0},{2,3},{3,2},{4,5},{5,4},{6,7},{7,6},{8,9},{9,8},{10,11... | collective-permute-start | bytes 786440 | tf_op jit(solution)/shard_map/ppermute | solution.py:66
  148.9 13.1 %collective-permute-start.31 = (bf16[4,64,512]{2,1,0:T(8,128)(2,1)S(1)}, bf16[4,64,512]{2,1,0:T(8,128)(2,1)S(1)}, u32[]{:S(2)}, u32[]{:S(2)}) collective-permute-start(bf16[4,64,512]{2,1,0:T(8,128)(2,1)S(1)} %get-tuple-element.52), channel_id=1, source_target_pairs={{0,4},{2,6},{4,0},{6,2},{8,12},{10,14},{12,8},{14,10},{16,20},{18,... | collective-permute-start | bytes 786440 | tf_op jit(solution)/shard_map/ppermute | solution.py:66
  150.4 11.5 %collective-permute-start.32 = (bf16[4,64,512]{2,1,0:T(8,128)(2,1)S(1)}, bf16[4,64,512]{2,1,0:T(8,128)(2,1)S(1)}, u32[]{:S(2)}, u32[]{:S(2)}) collective-permute-start(bf16[4,64,512]{2,1,0:T(8,128)(2,1)S(1)} %get-tuple-element.54), channel_id=1, source_target_pairs={{0,1},{1,0},{2,3},{3,2},{4,5},{5,4},{6,7},{7,6},{8,9},{9,8},{10,11... | collective-permute-start | bytes 786440 | tf_op jit(solution)/shard_map/ppermute | solution.py:66
  154.4 9.6 %collective-permute-start.41 = (bf16[64,1024]{1,0:T(8,128)(2,1)S(1)}, bf16[64,1024]{1,0:T(8,128)(2,1)S(1)}, u32[]{:S(2)}, u32[]{:S(2)}) collective-permute-start(bf16[64,1024]{1,0:T(8,128)(2,1)S(1)} %get-tuple-element.70), channel_id=1, source_target_pairs={{0,8},{2,10},{4,12},{6,14},{8,16},{10,18},{12,20},{14,22},{16,24},... | collective-permute-start | bytes 393224 | tf_op jit(solution)/shard_map/ppermute | solution.py:71
  156.6 13.7 %collective-permute-start.42 = (bf16[64,1024]{1,0:T(8,128)(2,1)S(1)}, bf16[64,1024]{1,0:T(8,128)(2,1)S(1)}, u32[]{:S(2)}, u32[]{:S(2)}) collective-permute-start(bf16[64,1024]{1,0:T(8,128)(2,1)S(1)} %get-tuple-element.71), channel_id=1, source_target_pairs={{0,16},{2,18},{4,20},{6,22},{8,24},{10,26},{12,28},{14,30},{16,0},... | collective-permute-start | bytes 393224 | tf_op jit(solution)/shard_map/ppermute | solution.py:71
  159.1 11.2 %collective-permute-start.43 = (bf16[64,1024]{1,0:T(8,128)(2,1)S(1)}, bf16[64,1024]{1,0:T(8,128)(2,1)S(1)}, u32[]{:S(2)}, u32[]{:S(2)}) collective-permute-start(bf16[64,1024]{1,0:T(8,128)(2,1)S(1)} %get-tuple-element.72), channel_id=1, source_target_pairs={{0,24},{2,26},{4,28},{6,30},{8,0},{10,2},{12,4},{14,6},{16,8},{18,... | collective-permute-start | bytes 393224 | tf_op jit(solution)/shard_map/ppermute | solution.py:71
  162.0 10.0 %collective-permute-start.33 = (bf16[64,1024]{1,0:T(8,128)(2,1)S(1)}, bf16[64,1024]{1,0:T(8,128)(2,1)S(1)}, u32[]{:S(2)}, u32[]{:S(2)}) collective-permute-start(bf16[64,1024]{1,0:T(8,128)(2,1)S(1)} %get-tuple-element.56), channel_id=1, source_target_pairs={{0,8},{2,10},{4,12},{6,14},{8,16},{10,18},{12,20},{14,22},{16,24},... | collective-permute-start | bytes 393224 | tf_op jit(solution)/shard_map/ppermute | solution.py:71
  162.1 16.1 %collective-permute-start.34 = (bf16[64,1024]{1,0:T(8,128)(2,1)S(1)}, bf16[64,1024]{1,0:T(8,128)(2,1)S(1)}, u32[]{:S(2)}, u32[]{:S(2)}) collective-permute-start(bf16[64,1024]{1,0:T(8,128)(2,1)S(1)} %get-tuple-element.57), channel_id=1, source_target_pairs={{0,16},{2,18},{4,20},{6,22},{8,24},{10,26},{12,28},{14,30},{16,0},... | collective-permute-start | bytes 393224 | tf_op jit(solution)/shard_map/ppermute | solution.py:71
  164.0 14.2 %collective-permute-start.35 = (bf16[64,1024]{1,0:T(8,128)(2,1)S(1)}, bf16[64,1024]{1,0:T(8,128)(2,1)S(1)}, u32[]{:S(2)}, u32[]{:S(2)}) collective-permute-start(bf16[64,1024]{1,0:T(8,128)(2,1)S(1)} %get-tuple-element.58), channel_id=1, source_target_pairs={{0,24},{2,26},{4,28},{6,30},{8,0},{10,2},{12,4},{14,6},{16,8},{18,... | collective-permute-start | bytes 393224 | tf_op jit(solution)/shard_map/ppermute | solution.py:71
  (20 other events, 16.7 us)

commit v4 on v3

--- a/solution.py
+++ b/solution.py
@@ -77,12 +77,34 @@
     return pl.multiple_of((line * 2 + row) * width, width)
 
 
-def prepare_kernel(width, place, tokens, gates, ids, first, *others):
+def small(kernel, name, shapes, kinds, operands, scratch=(), limit=8, moved=0):
+    spaces = {"s": pltpu.SMEM, "v": pltpu.VMEM, "a": pl.ANY, "o": pl.ANY}
+    return pl.pallas_call(
+        kernel,
+        out_shape=[jax.ShapeDtypeStruct(dims, jnp.bfloat16) for dims in shapes],
+        in_specs=[pl.BlockSpec(memory_space=spaces[kind]) for kind in kinds],
+        scratch_shapes=list(scratch),
+        compiler_params=pltpu.CompilerParams(vmem_limit_bytes=limit << 20),
+        cost_estimate=pl.CostEstimate(flops=0, bytes_accessed=moved, transcendentals=0),
+        name=name,
+    )(*operands)
+
+
+def prepare_kernel(place, tokens, gates_any, ids_any, first, table, gates, ids, sems):
     piece = first.shape[0]
+    width = first.shape[1] - table.shape[1]
     near = pl.multiple_of(place[3] * piece, piece)
-    first[:, :width] = tokens[pl.ds(near, piece), :width]
-    for i, other in enumerate(others[:-1]):
-        other[...] = tokens[pl.ds(near, piece), (i + 1) * width:(i + 2) * width]
+    copies = [
+        pltpu.make_async_copy(gates_any, gates, sems.at[0]),
+        pltpu.make_async_copy(ids_any, ids, sems.at[1]),
+        pltpu.make_async_copy(
+            tokens.at[pl.ds(near, piece), pl.ds(0, width)], first.at[:, pl.ds(0, width)], sems.at[2]
+        ),
+    ]
+    for copy in copies:
+        copy.start()
+    copies[0].wait()
+    copies[1].wait()
     rest = gates[...]
     terms = []
     for _ in range(3):
@@ -92,21 +114,132 @@
     terms.append(ids[...].astype(jnp.float32))
     unused = piece - 4 * gates.shape[0]
     terms.append(jnp.zeros((unused, gates.shape[1]), jnp.float32))
-    table = jnp.concatenate(terms, axis=0).astype(jnp.bfloat16)
-    first[:, width:] = table
-    others[-1][...] = table
+    packed = jnp.concatenate(terms, axis=0).astype(jnp.bfloat16)
+    first[:, width:] = packed
+    table[...] = packed
+    copies[2].wait()
 
 
 def prepare(place, cotangent, gates, ids, piece, width):
-    feature_dim = cotangent.shape[1]
-    shapes = [(piece, width + 128)] + [(piece, width)] * (feature_dim // width - 1) + [(piece, 128)]
-    return pl.pallas_call(
-        functools.partial(prepare_kernel, width),
-        out_shape=[jax.ShapeDtypeStruct(dims, jnp.bfloat16) for dims in shapes],
-        in_specs=[pl.BlockSpec(memory_space=pltpu.SMEM)] + [pl.BlockSpec(memory_space=pltpu.VMEM)] * 3,
-        compiler_params=pltpu.CompilerParams(vmem_limit_bytes=4 << 20),
-        name="prepare",
-    )(place, cotangent, gates, ids)
+    return small(
+        prepare_kernel,
+        "prepare",
+        [(piece, width + 128), (piece, 128)],
+        "saaa",
+        (place, cotangent, gates, ids),
+        [
+            pltpu.VMEM(gates.shape, jnp.float32),
+            pltpu.VMEM(ids.shape, jnp.int32),
+            pltpu.SemaphoreType.DMA((3,)),
+        ],
+        limit=4,
+        moved=1 << 18,
+    )
+
+
+def stack_kernel(offset, place, tokens, *refs):
+    if offset is None:
+        *pieces, _, lines = refs
+    else:
+        *pieces, lines, following, sem = refs
+        piece, width = following.shape
+        near = pl.multiple_of(place[3] * piece, piece)
+        copy = pltpu.make_async_copy(
+            tokens.at[pl.ds(near, piece), pl.ds(offset, width)], following, sem.at[0]
+        )
+        copy.start()
+    for r, ref in enumerate(pieces):
+        lines[r] = ref[...]
+    if offset is not None:
+        copy.wait()
+
+
+def stack(place, cotangent, pieces, offset, width, after):
+    dims = pieces[0].shape
+    count = len(pieces)
+    shapes = [(count,) + dims]
+    operands = [place, cotangent, *pieces]
+    kinds = "sa" + "v" * count
+    scratch = ()
+    if offset is None:
+        operands.append(after)
+        kinds += "o"
+    else:
+        shapes.append((dims[0], width))
+        scratch = (pltpu.SemaphoreType.DMA((1,)),)
+    return small(
+        functools.partial(stack_kernel, offset), "stack", shapes, kinds, operands, scratch, moved=1 << 20
+    )
+
+
+def turn_kernel(gate, up, _, gate_t, up_t):
+    tile = 128
+    for source, target in ((gate, gate_t), (up, up_t)):
+        for e in range(source.shape[0]):
+            for at in range(0, source.shape[2], tile):
+                target[e, at:at + tile] = source[e, :, at:at + tile].astype(jnp.float32).T.astype(
+                    jnp.bfloat16
+                )
+
+
+def turn(saved_gate, saved_up, after):
+    count, units, slots = saved_gate.shape
+    return small(
+        turn_kernel,
+        "turn",
+        [(count, slots, units)] * 2,
+        "vvo",
+        (saved_gate, saved_up, after),
+        limit=12,
+        moved=8 << 20,
+    )
+
+
+def corner_kernel(offset, place, tokens, first, over, side, whole_over, left, right, sem):
+    _, piece, middle = left.shape
+    far = pl.multiple_of((1 - place[3]) * piece, piece)
+    copy = pltpu.make_async_copy(
+        tokens.at[pl.ds(far, piece), pl.ds(offset, middle)], right.at[0], sem.at[0]
+    )
+    copy.start()
+    whole_over[0] = first[...]
+    whole_over[1:] = over[...]
+    left[0] = first[:, :middle]
+    left[1:] = over[:, :, :middle]
+    right[1:] = side[:, :, middle:2 * middle]
+    copy.wait()
+
+
+def corner(place, cotangent, first, over, side, offset, middle):
+    count, piece, width = over.shape
+    return small(
+        functools.partial(corner_kernel, offset + middle),
+        "corner",
+        [(count + 1, piece, width)] + [(count + 1, piece, middle)] * 2,
+        "savvv",
+        (place, cotangent, first, over, side),
+        (pltpu.SemaphoreType.DMA((1,)),),
+        moved=3 << 20,
+    )
+
+
+def join_kernel(left, right, *refs):
+    result = refs[-1]
+    middle = left.shape[-1]
+    result[:, :, :middle] = left[...]
+    result[:, :, middle:] = right[...]
+
+
+def join(left, right, *after):
+    dims = left.shape
+    return small(
+        join_kernel,
+        "join",
+        [dims[:-1] + (2 * dims[-1],)],
+        "vv" + "o" * len(after),
+        (left, right, *after),
+        moved=1 << 20,
+    )[0]
 
 
 def route_kernel(capacity, place, own, own_c, lines, lines_c, over, over_c, pick, pick_t, gate, hits, gates):
@@ -202,12 +335,12 @@
 
 
 def hidden_kernel(last, place, *refs):
-    (own, own_c, lines, lines_c, side, side_c, over, over_c, diag_l, diag_lc, diag_r, diag_rc,
-     pick, gate, w_down) = refs[:15]
+    own, own_c, lines, lines_c, side, side_c, over, over_c, diag, diag_c = refs[:10]
+    pick, gate, w_down, _ = refs[10:14]
     if last:
-        before, saved_gate, saved_up, result, slots, diag, total = refs[15:]
+        before, saved_gate, saved_up, result, slots, total = refs[14:]
     else:
-        result, slots, diag = refs[15:]
+        result, slots = refs[14:]
         total = result
     k, steps = pl.program_id(0), pl.num_programs(0)
     line_count, piece, _ = over.shape
@@ -216,16 +349,6 @@
     @pl.when(k == 0)
     def _():
         total[...] = before[...] if last else jnp.zeros_like(total)
-
-    @pl.when(k < steps // 2)
-    def _():
-        diag[0] = diag_l[...]
-        diag[1] = diag_lc[...]
-
-    @pl.when(k >= steps // 2)
-    def _():
-        diag[0] = diag_r[...]
-        diag[1] = diag_rc[...]
 
     near = pl.multiple_of(place[3] * piece, piece)
     far = pl.multiple_of((1 - place[3]) * piece, piece)
@@ -234,7 +357,7 @@
             parts = []
             for c in range(2):
                 if ry == 1:
-                    parts += [(over, over_c)[c][r], diag[c, r]]
+                    parts += [(over, over_c)[c][r], (diag, diag_c)[c][r]]
                 elif r == 0:
                     group = (own, own_c)[c]
                     parts += [group[pl.ds(near, piece), :], group[pl.ds(far, piece), :]]
@@ -277,10 +400,10 @@
                 ).astype(jnp.bfloat16)
 
 
-def hidden(place, chunk, own, own_c, moved, pick, gate, w_down, rest):
+def hidden(place, chunk, own, own_c, moved, pick, gate, w_down, after, rest):
     last = rest is not None
     line_count, piece, _ = moved[4].shape
-    width = 2 * moved[6].shape[-1]
+    width = moved[6].shape[-1]
     steps = width // LANES
     offset = chunk * steps
     units = w_down.shape[1]
@@ -289,24 +412,14 @@
         dims, lambda k, place: (0,) * len(dims), pipeline_mode=pl.Buffered(1)
     )
     column = lambda array: pl.BlockSpec(array.shape[:-1] + (LANES,), lambda k, place: (0, 0, k))
-    first_half = lambda array: pl.BlockSpec(
-        array.shape[:-1] + (LANES,), lambda k, place: (0, 0, jnp.minimum(k, steps // 2 - 1))
-    )
-    second_half = lambda array: pl.BlockSpec(
-        array.shape[:-1] + (LANES,), lambda k, place: (0, 0, jnp.maximum(k - steps // 2, 0))
-    )
     group = pl.BlockSpec((own.shape[0], LANES), lambda k, place: (0, offset + k))
     in_specs = [group, group]
-    in_specs += [column(array) for array in moved[:6]]
-    in_specs += [first_half(array) for array in moved[6:8]]
-    in_specs += [second_half(array) for array in moved[8:]]
+    in_specs += [column(array) for array in moved]
     in_specs += [whole(pick.shape), whole(gate.shape)]
     in_specs += [pl.BlockSpec((2, units, LANES), lambda k, place: (0, 0, offset + k))]
-    scratch = [
-        pltpu.VMEM((2, slot_count, LANES), jnp.bfloat16),
-        pltpu.VMEM((2, line_count, piece, LANES), jnp.bfloat16),
-    ]
-    operands = [own, own_c, *moved, pick, gate, w_down]
+    in_specs += [pl.BlockSpec(memory_space=pl.ANY)]
+    scratch = [pltpu.VMEM((2, slot_count, LANES), jnp.bfloat16)]
+    operands = [own, own_c, *moved, pick, gate, w_down, after]
     if last:
         in_specs += [whole(array.shape) for array in rest]
         operands += rest
@@ -386,7 +499,7 @@
     )(place, grads, w_gate, w_up, pick_t)
 
 
-def first_kernel(keep, came, send_l, keep_l, send_r, keep_r):
+def first_kernel(keep, came, _, send_l, keep_l, send_r, keep_r):
     total = keep[...] + came[...]
     middle = total.shape[-1] // 2
     keep_l[...] = total[:, 0, :, :middle]
@@ -395,7 +508,7 @@
     send_r[...] = total[1:2, :, :, middle:]
 
 
-def first_sum(keep, came, piece):
+def first_sum(keep, came, piece, after):
     pairs, tokens, width = keep.shape
     keep = keep.reshape(pairs, 2, piece, width)
     came = came.reshape(pairs, 2, piece, width)
@@ -408,12 +521,12 @@
         first_kernel,
         out_shape=(left, left, right, right),
         grid=(pairs // 2,),
-        in_specs=[full, full],
+        in_specs=[full, full, pl.BlockSpec(memory_space=pl.ANY)],
         out_specs=[left_spec, left_spec, right_spec, right_spec],
         cost_estimate=pl.CostEstimate(flops=0, bytes_accessed=6 << 20, transcendentals=0),
         compiler_params=pltpu.CompilerParams(vmem_limit_bytes=8 << 20),
         name="first_sum",
-    )(keep, came)
+    )(keep, came, after)
 
 
 def second_kernel(keep_l, came_l, keep_r, came_r, send_l, left, send_r, right):
@@ -485,39 +598,46 @@
     me, half = lax.axis_index("expert"), lax.axis_index("tp")
     place = jnp.stack([me % 2, me // 2 % 2, me // 4, half]).astype(jnp.int32)
 
-    *parts, table = prepare(place, cotangent, gates.T, expert_ids.T, piece, width)
-    saved_gate, saved_up = saved_gate.swapaxes(1, 2), saved_up.swapaxes(1, 2)
+    part, table = prepare(place, cotangent, gates.T, expert_ids.T, piece, width)
     own_c, table_c = swap(cotangent, "expert", 1), swap(table, "expert", 1)
-    far = lax.dynamic_slice_in_dim(cotangent, (1 - half) * piece, piece, 0)
-    gathered = []
-    for chunk, part in enumerate(parts):
-        line = jnp.stack([along_line(part, -r) for r in range(1, lines)])
+    gathered, saved, rest = [], None, None
+    for chunk in range(CHUNKS):
+        last = chunk == CHUNKS - 1
         first = swap(part, "expert", 2)
-        side = swap(line, "tp", 1)
-        over = jnp.concatenate([first[None], swap(line, "expert", 2)])
-        diag_l = swap(over[:, :, :middle], "tp", 1)
-        far_part = far[None, :, chunk * width + middle:(chunk + 1) * width]
-        diag_r = swap(jnp.concatenate([far_part, side[:, :, middle:width]]), "expert", 2)
+        pieces = [along_line(part, -r) for r in range(1, lines)]
+        if last:
+            line, = stack(place, cotangent, pieces, None, width, saved[0])
+        else:
+            line, part = stack(place, cotangent, pieces, (chunk + 1) * width, width, None)
+            saved = turn(saved_gate, saved_up, line)
+        side, over = swap(line, "tp", 1), swap(line, "expert", 2)
+        over, left, right = corner(place, cotangent, first, over, side, chunk * width, middle)
+        left_came, right_came = swap(left, "tp", 1), swap(right, "expert", 2)
+        if last:
+            for index, moved in enumerate(gathered):
+                rest = hidden(place, index, cotangent, own_c, moved, pick, gate, w_down, left, rest)
+            diag = join(left_came, right_came, rest)
+        else:
+            diag = join(left_came, right_came)
         moved = []
-        for array in (line, side, over, diag_l, diag_r):
+        for array in (line, side, over, diag):
             moved += [array, swap(array, "expert", 1)]
         gathered.append(moved)
-    lines_n, lines_c, _, _, over_n, over_c = gathered[0][:6]
-    pick, pick_t, gate = route(place, table, table_c, lines_n, lines_c, over_n, over_c, capacity)
-    rest = None
-    for chunk in range(CHUNKS):
-        if chunk == CHUNKS - 1:
-            rest = [rest, saved_gate, saved_up]
-        rest = hidden(place, chunk, cotangent, own_c, gathered[chunk], pick, gate, w_down, rest)
-    grads = rest
+        if chunk == 0:
+            lines_c, over_c = moved[1], moved[5]
+            pick, pick_t, gate = route(place, table, table_c, line, lines_c, over, over_c, capacity)
+    rest = [rest, *saved]
+    grads = hidden(place, chunk, cotangent, own_c, moved, pick, gate, w_down, left, rest)
 
     terms = []
+    after = grads
     for chunk in range(CHUNKS):
         keep, send = sums(place, chunk, width, grads, w_gate, w_up, pick_t)
         came = swap(send, "expert", 1)
-        send_l, keep_l, send_r, keep_r = first_sum(keep, came, piece)
+        send_l, keep_l, send_r, keep_r = first_sum(keep, came, piece, after)
         came_l, came_r = swap(send_l, "tp", 1), swap(send_r, "expert", 2)
         send_l, left, send_r, right = second_sum(keep_l, came_l, keep_r, came_r)
+        after = send_l
         came_l, came_r = swap(send_l, "expert", 2), swap(send_r, "tp", 1)
         own, *sends = third_sum(left, came_l, right, came_r)
         terms += [own] + [along_line(send, r + 1) for r, send in enumerate(sends)]

time: 180 us -> 158 us (0.88)
  local copies, waits for them, and re-layouts: 27.8 us -> 3.48 us
  waiting for transfers between devices: 68.8 us -> 82 us
  starting transfers between devices: 49.5 us -> 38.6 us
  Pallas kernels: 31.3 us -> 33.1 us
    unnamed x82 -> x20, local copies, waits for them, and re-layouts: 26.9 us -> 3.48 us
    ppermute x32 -> x30, waiting for transfers between devices: 41.7 us -> 53.3 us  [swap(): return lax.ppermute(value, axis, [(i, i ^ step) for i in range(count)])]
    ppermute x32 -> x30, starting transfers between devices: 27.1 us -> 21.3 us  [swap(): return lax.ppermute(value, axis, [(i, i ^ step) for i in range(count)])]
    ppermute x12, starting transfers between devices: 22.4 us -> 17.4 us  [along_line(): lax.ppermute(value, 'expert', [(i, (i + 4 * shift) % count) for i in rang...]
    pallas_call x1 -> x8, Pallas kernels: 0.56 us -> 3.81 us  [small(): pl.pallas_call(kernel, out_shape=[jax.ShapeDtypeStruct(dims, jnp.bfloat16...]
  transfers between devices with their start and end apart: 44 -> 42, of which waited for: 16 -> 19; matrix products, arithmetic and copies ran while one was open for 4% -> 0% of each run, Pallas kernels for 8% -> 11%
where the time goes in v4:
time: 158 us; the launch traced here: 157 us
  waiting for transfers between devices  82 us (52%)
  starting transfers between devices  38.6 us (24%)
  Pallas kernels  33.1 us (21%)
  local copies, waits for them, and re-layouts  3.48 us (2%)
    ppermute x30, waiting for transfers between devices, swap(): return lax.ppermute(value, axis, [(i, i ^ step) for i in range(count)])  53.3 us
    ppermute x12, waiting for transfers between devices, along_line(): lax.ppermute(value, 'expert', [(i, (i + 4 * shift) % count) for i in rang...  28.7 us
    ppermute x30, starting transfers between devices, swap(): return lax.ppermute(value, axis, [(i, i ^ step) for i in range(count)])  21.3 us
    ppermute x12, starting transfers between devices, along_line(): lax.ppermute(value, 'expert', [(i, (i + 4 * shift) % count) for i in rang...  17.4 us
    pallas_call x2, Pallas kernels, hidden(): pl.pallas_call(functools.partial(hidden_kernel, last), out_shape=out, gri...  13.2 us
    pallas_call x2, Pallas kernels, sums(): pl.pallas_call(sums_kernel, out_shape=(out, out), grid_spec=pltpu.Prefetc...  12.7 us
    pallas_call x8, Pallas kernels, small(): pl.pallas_call(kernel, out_shape=[jax.ShapeDtypeStruct(dims, jnp.bfloat16...  3.81 us
    unnamed x20, local copies, waits for them, and re-layouts  3.48 us
  transfers between devices with their start and end apart: 42, of which 19 were waited for; matrix products, arithmetic and copies ran while one was open for 0% of the time, Pallas kernels for 11%

profile of v4, /device:TPU:0, one launch (start us, length us, event | category | flops | bytes accessed | tf_op | source)
XLA Modules:
  0.0 157.5 jit_solution(8443449990590696963)
XLA Ops:
  0.1 1.0 copy-done
  1.1 0.7 copy-done.6
  1.8 0.7 copy-done.7
  2.5 0.6 prepare.1
  3.1 5.1 %collective-permute-start.1 = (bf16[64,1152]{1,0:T(8,128)(2,1)S(1)}, bf16[64,1152]{1,0:T(8,128)(2,1)S(1)}, u32[]{:S(2)}, u32[]{:S(2)}) collective-permute-start(bf16[64,1152]{1,0:T(8,128)(2,1)S(1)} %get-tuple-element.48), channel_id=1, source_target_pairs={{0,24},{2,26},{4,28},{6,30},{8,0},{10,2},{12,4},{14,6},{16,8},{18,... | collective-permute-start | bytes 442376 | tf_op jit(solution)/shard_map/ppermute | solution.py:71
  8.2 1.0 collective-permute-start.3
  9.2 3.3 %collective-permute-done.1.refs_0_ = bf16[64,1152]{1,0:T(8,128)(2,1)S(1)} collective-permute-done((bf16[64,1152]{1,0:T(8,128)(2,1)S(1)}, bf16[64,1152]{1,0:T(8,128)(2,1)S(1)}, u32[]{:S(2)}, u32[]{:S(2)}) %collective-permute-start.1) | collective-permute-done | bytes 147488 | tf_op jit(solution)/shard_map/ppermute | solution.py:71
  12.5 8.2 %collective-permute-done.2.refs_1_ = bf16[64,1152]{1,0:T(8,128)(2,1)S(1)} collective-permute-done((bf16[64,1152]{1,0:T(8,128)(2,1)S(1)}, bf16[64,1152]{1,0:T(8,128)(2,1)S(1)}, u32[]{:S(2)}, u32[]{:S(2)}) %collective-permute-start.2) | collective-permute-done | bytes 147488 | tf_op jit(solution)/shard_map/ppermute | solution.py:71
  20.7 1.0 copy-done.1
  21.8 0.6 stack.22
  22.4 1.6 collective-permute-start.16
  23.9 1.5 collective-permute-start.19
  25.4 0.5 collective-permute-start.18
  26.0 1.4 collective-permute-start.4
  27.4 1.4 collective-permute-start.5
  28.8 9.5 %collective-permute-done.18.first = bf16[64,1152]{1,0:T(8,128)(2,1)S(1)} collective-permute-done((bf16[64,1152]{1,0:T(8,128)(2,1)S(1)}, bf16[64,1152]{1,0:T(8,128)(2,1)S(1)}, u32[]{:S(2)}, u32[]{:S(2)}) %collective-permute-start.18) | collective-permute-done | bytes 147488 | tf_op jit(solution)/shard_map/ppermute | solution.py:66
  38.3 0.7 collective-permute-start.6
  39.0 0.6 corner.3
  39.6 0.6 collective-permute-start.21
  40.3 0.7 turn.1
  41.0 4.1 %collective-permute-done.6.refs_2_ = bf16[64,1024]{1,0:T(8,128)(2,1)S(1)} collective-permute-done((bf16[64,1024]{1,0:T(8,128)(2,1)S(1)}, bf16[64,1024]{1,0:T(8,128)(2,1)S(1)}, u32[]{:S(2)}, u32[]{:S(2)}) %collective-permute-start.6) | collective-permute-done | bytes 131104 | tf_op jit(solution)/shard_map/ppermute | solution.py:71
  45.0 0.6 stack.23.refs_2_
  45.6 1.6 %collective-permute-start.11 = (bf16[3,64,1024]{2,1,0:T(8,128)(2,1)S(1)}, bf16[3,64,1024]{2,1,0:T(8,128)(2,1)S(1)}, u32[]{:S(2)}, u32[]{:S(2)}) collective-permute-start(bf16[3,64,1024]{2,1,0:T(8,128)(2,1)S(1)} %stack.23.refs_2_), channel_id=1, source_target_pairs={{0,4},{2,6},{4,0},{6,2},{8,12},{10,14},{12,8},{14,10},{16,20},{18,... | collective-permute-start | bytes 1179656 | tf_op jit(solution)/shard_map/ppermute | solution.py:66
  47.2 0.5 collective-permute-start.8
  47.7 0.5 collective-permute-start.22
  48.2 1.2 collective-permute-done.24.own_c
  49.6 1.5 collective-permute-start.10
  51.1 9.6 %collective-permute-done.22.right = bf16[4,64,512]{2,1,0:T(8,128)(2,1)S(1)} collective-permute-done((bf16[4,64,512]{2,1,0:T(8,128)(2,1)S(1)}, bf16[4,64,512]{2,1,0:T(8,128)(2,1)S(1)}, u32[]{:S(2)}, u32[]{:S(2)}) %collective-permute-start.22) | collective-permute-done | bytes 262176 | tf_op jit(solution)/shard_map/ppermute | solution.py:66
  60.8 1.4 collective-permute-done.10.first
  62.2 0.5 collective-permute-start.15
  62.7 0.6 corner.2
  63.4 1.3 collective-permute-done.15.lines_c.refs_3_
  64.7 0.5 collective-permute-start.13
  65.2 1.5 collective-permute-start.14
  66.8 1.4 route.1
  68.3 6.0 %hidden.2.refs_0_.refs_14_ = f32[2,768,384]{2,1,0:T(8,128)S(1)} custom-call(s32[4]{0:T(128)S(1)} %pad_add_fusion.place, bf16[128,2048]{1,0:T(8,128)(2,1)S(1)} %copy-done.2, bf16[128,2048]{1,0:T(8,128)(2,1)S(1)} %collective-permute-done.refs_1_, bf16[3,64,1152]{2,1,0:T(8,128)(2,1)S(1)} %get-tuple-element.50._.lines.refs_2_, ...), custom_call_target="tpu_custom_call" | custom-call | flops 2013265920 | bytes 8388608 | tf_op jit(solution)/shard_map/hidden/pallas_call | solution.py:430
  74.4 0.5 collective-permute-start.25
  75.5 1.6 %collective-permute-done.7.refs_3_ = bf16[3,64,1024]{2,1,0:T(8,128)(2,1)S(1)} collective-permute-done((bf16[3,64,1024]{2,1,0:T(8,128)(2,1)S(1)}, bf16[3,64,1024]{2,1,0:T(8,128)(2,1)S(1)}, u32[]{:S(2)}, u32[]{:S(2)}) %collective-permute-start.7) | collective-permute-done | bytes 393248 | tf_op jit(solution)/shard_map/ppermute | solution.py:66
  77.1 0.6 collective-permute-done.9.refs_5_
  77.7 7.1 %hidden.3.grads._ = bf16[2,768,768]{2,1,0:T(8,128)(2,1)S(1)} custom-call(s32[4]{0:T(128)S(1)} %pad_add_fusion.place, bf16[128,2048]{1,0:T(8,128)(2,1)S(1)} %copy-done.2, bf16[128,2048]{1,0:T(8,128)(2,1)S(1)} %collective-permute-done.refs_1_, bf16[3,64,1024]{2,1,0:T(8,128)(2,1)S(1)} %stack.23.refs_2_, ...), custom_call_target="tpu_custom_call" | custom-call | flops 2013265920 | bytes 8388608 | tf_op jit(solution)/shard_map/hidden/pallas_call | solution.py:430
  84.8 6.3 %sums.2 = (bf16[8,128,1024]{2,1,0:T(8,128)(2,1)S(1)}, bf16[8,128,1024]{2,1,0:T(8,128)(2,1)S(1)}) custom-call(s32[4]{0:T(128)S(1)} %pad_add_fusion.place, bf16[2,768,768]{2,1,0:T(8,128)(2,1)S(1)} %hidden.3.grads._, bf16[2,384,2048]{2,1,0:T(8,128)(2,1)S(1)} %copy-done.8, bf16[2,384,2048]{2,1,0:T(8,128)(2,1)S(1)} %copy-done.9, ...), custom_call_target="tpu_custom_call" | custom-call | flops 3221225472 | bytes 10485760 | tf_op jit(solution)/shard_map/sums/pallas_call | solution.py:482
  91.6 6.4 %sums.3 = (bf16[8,128,1024]{2,1,0:T(8,128)(2,1)S(1)}, bf16[8,128,1024]{2,1,0:T(8,128)(2,1)S(1)}) custom-call(s32[4]{0:T(128)S(1)} %pad_add_fusion.place, bf16[2,768,768]{2,1,0:T(8,128)(2,1)S(1)} %hidden.3.grads._, bf16[2,384,2048]{2,1,0:T(8,128)(2,1)S(1)} %copy-done.8, bf16[2,384,2048]{2,1,0:T(8,128)(2,1)S(1)} %copy-done.9, ...), custom_call_target="tpu_custom_call" | custom-call | flops 3221225472 | bytes 10485760 | tf_op jit(solution)/shard_map/sums/pallas_call | solution.py:482
  98.5 1.6 %collective-permute-start.27 = (bf16[8,64,512]{2,1,0:T(8,128)(2,1)S(1)}, bf16[8,64,512]{2,1,0:T(8,128)(2,1)S(1)}, u32[]{:S(2)}, u32[]{:S(2)}) collective-permute-start(bf16[8,64,512]{2,1,0:T(8,128)(2,1)S(1)} %get-tuple-element.66), channel_id=1, source_target_pairs={{0,1},{1,0},{2,3},{3,2},{4,5},{5,4},{6,7},{7,6},{8,9},{9,8},{10,11... | collective-permute-start | bytes 1572872 | tf_op jit(solution)/shard_map/ppermute | solution.py:66
  100.1 0.5 collective-permute-start.28
  100.6 12.2 %collective-permute-done.27.came_l = bf16[8,64,512]{2,1,0:T(8,128)(2,1)S(1)} collective-permute-done((bf16[8,64,512]{2,1,0:T(8,128)(2,1)S(1)}, bf16[8,64,512]{2,1,0:T(8,128)(2,1)S(1)}, u32[]{:S(2)}, u32[]{:S(2)}) %collective-permute-start.27) | collective-permute-done | bytes 524320 | tf_op jit(solution)/shard_map/ppermute | solution.py:66
  112.8 1.3 collective-permute-done.28.came_r
  114.5 0.6 collective-permute-start.35
  115.1 0.5 collective-permute-start.36
  115.6 1.5 collective-permute-start.29
  117.1 1.5 collective-permute-start.30
  118.7 10.8 %collective-permute-done.35.came_l = bf16[8,64,512]{2,1,0:T(8,128)(2,1)S(1)} collective-permute-done((bf16[8,64,512]{2,1,0:T(8,128)(2,1)S(1)}, bf16[8,64,512]{2,1,0:T(8,128)(2,1)S(1)}, u32[]{:S(2)}, u32[]{:S(2)}) %collective-permute-start.35) | collective-permute-done | bytes 524320 | tf_op jit(solution)/shard_map/ppermute | solution.py:66
  130.1 0.6 collective-permute-start.37
  130.7 1.5 collective-permute-start.38
  132.2 3.4 %collective-permute-done.29.came_l = bf16[4,64,512]{2,1,0:T(8,128)(2,1)S(1)} collective-permute-done((bf16[4,64,512]{2,1,0:T(8,128)(2,1)S(1)}, bf16[4,64,512]{2,1,0:T(8,128)(2,1)S(1)}, u32[]{:S(2)}, u32[]{:S(2)}) %collective-permute-start.29) | collective-permute-done | bytes 262176 | tf_op jit(solution)/shard_map/ppermute | solution.py:66
  135.7 1.2 collective-permute-start.32
  136.9 2.6 %collective-permute-start.33 = (bf16[64,1024]{1,0:T(8,128)(2,1)S(1)}, bf16[64,1024]{1,0:T(8,128)(2,1)S(1)}, u32[]{:S(2)}, u32[]{:S(2)}) collective-permute-start(bf16[64,1024]{1,0:T(8,128)(2,1)S(1)} %get-tuple-element.76), channel_id=1, source_target_pairs={{0,24},{2,26},{4,28},{6,30},{8,0},{10,2},{12,4},{14,6},{16,8},{18,... | collective-permute-start | bytes 393224 | tf_op jit(solution)/shard_map/ppermute | solution.py:71
  139.6 0.6 collective-permute-start.39
  140.2 1.5 collective-permute-start.40
  141.8 1.5 collective-permute-done.31.refs_1_
  143.2 1.7 %collective-permute-start.41 = (bf16[64,1024]{1,0:T(8,128)(2,1)S(1)}, bf16[64,1024]{1,0:T(8,128)(2,1)S(1)}, u32[]{:S(2)}, u32[]{:S(2)}) collective-permute-start(bf16[64,1024]{1,0:T(8,128)(2,1)S(1)} %get-tuple-element.90), channel_id=1, source_target_pairs={{0,24},{2,26},{4,28},{6,30},{8,0},{10,2},{12,4},{14,6},{16,8},{18,... | collective-permute-start | bytes 393224 | tf_op jit(solution)/shard_map/ppermute | solution.py:71
  144.9 4.0 %collective-permute-done.32.refs_2_ = bf16[64,1024]{1,0:T(8,128)(2,1)S(1)} collective-permute-done((bf16[64,1024]{1,0:T(8,128)(2,1)S(1)}, bf16[64,1024]{1,0:T(8,128)(2,1)S(1)}, u32[]{:S(2)}, u32[]{:S(2)}) %collective-permute-start.32) | collective-permute-done | bytes 131104 | tf_op jit(solution)/shard_map/ppermute | solution.py:71
  148.9 2.2 %collective-permute-done.39.refs_5_ = bf16[64,1024]{1,0:T(8,128)(2,1)S(1)} collective-permute-done((bf16[64,1024]{1,0:T(8,128)(2,1)S(1)}, bf16[64,1024]{1,0:T(8,128)(2,1)S(1)}, u32[]{:S(2)}, u32[]{:S(2)}) %collective-permute-start.39) | collective-permute-done | bytes 131104 | tf_op jit(solution)/shard_map/ppermute | solution.py:71
  151.1 5.5 %collective-permute-done.40.refs_6_ = bf16[64,1024]{1,0:T(8,128)(2,1)S(1)} collective-permute-done((bf16[64,1024]{1,0:T(8,128)(2,1)S(1)}, bf16[64,1024]{1,0:T(8,128)(2,1)S(1)}, u32[]{:S(2)}, u32[]{:S(2)}) %collective-permute-start.40) | collective-permute-done | bytes 131104 | tf_op jit(solution)/shard_map/ppermute | solution.py:71
  156.6 0.9 last_sum.1
  (61 shorter events, 3.3 us)
Async XLA Ops:
  0.1 1.0 copy-start
  1.1 0.7 copy-start.6
  1.8 0.7 copy-start.7
  3.1 9.4 %collective-permute-start.1 = (bf16[64,1152]{1,0:T(8,128)(2,1)S(1)}, bf16[64,1152]{1,0:T(8,128)(2,1)S(1)}, u32[]{:S(2)}, u32[]{:S(2)}) collective-permute-start(bf16[64,1152]{1,0:T(8,128)(2,1)S(1)} %get-tuple-element.48), channel_id=1, source_target_pairs={{0,24},{2,26},{4,28},{6,30},{8,0},{10,2},{12,4},{14,6},{16,8},{18,... | collective-permute-start | bytes 442376 | tf_op jit(solution)/shard_map/ppermute | solution.py:71
  8.2 12.5 %collective-permute-start.2 = (bf16[64,1152]{1,0:T(8,128)(2,1)S(1)}, bf16[64,1152]{1,0:T(8,128)(2,1)S(1)}, u32[]{:S(2)}, u32[]{:S(2)}) collective-permute-start(bf16[64,1152]{1,0:T(8,128)(2,1)S(1)} %get-tuple-element.48), channel_id=1, source_target_pairs={{0,16},{2,18},{4,20},{6,22},{8,24},{10,26},{12,28},{14,30},{16,0},... | collective-permute-start | bytes 442376 | tf_op jit(solution)/shard_map/ppermute | solution.py:71
  8.2 12.5 %collective-permute-start.3 = (bf16[64,1152]{1,0:T(8,128)(2,1)S(1)}, bf16[64,1152]{1,0:T(8,128)(2,1)S(1)}, u32[]{:S(2)}, u32[]{:S(2)}) collective-permute-start(bf16[64,1152]{1,0:T(8,128)(2,1)S(1)} %get-tuple-element.48), channel_id=1, source_target_pairs={{0,8},{2,10},{4,12},{6,14},{8,16},{10,18},{12,20},{14,22},{16,24},... | collective-permute-start | bytes 442376 | tf_op jit(solution)/shard_map/ppermute | solution.py:71
  20.7 1.0 copy-start.1
  21.7 18.5 %copy-start.4 = (bf16[2,384,768]{2,1,0:T(8,128)(2,1)S(1)}, bf16[2,384,768]{2,1,0:T(8,128)(2,1)}, u32[]{:S(2)}) copy-start(bf16[2,384,768]{2,1,0:T(8,128)(2,1)} %gate.1) | copy-start | bytes 3538948
  21.7 18.5 %copy-start.5 = (bf16[2,384,768]{2,1,0:T(8,128)(2,1)S(1)}, bf16[2,384,768]{2,1,0:T(8,128)(2,1)}, u32[]{:S(2)}) copy-start(bf16[2,384,768]{2,1,0:T(8,128)(2,1)} %up.1) | copy-start | bytes 3538948
  22.4 16.6 %collective-permute-start.16 = (bf16[3,64,1152]{2,1,0:T(8,128)(2,1)S(1)}, bf16[3,64,1152]{2,1,0:T(8,128)(2,1)S(1)}, u32[]{:S(2)}, u32[]{:S(2)}) collective-permute-start(bf16[3,64,1152]{2,1,0:T(8,128)(2,1)S(1)} %get-tuple-element.50._.lines.refs_2_), channel_id=1, source_target_pairs={{0,1},{1,0},{2,3},{3,2},{4,5},{5,4},{6,7},{7,6},{8,9},{9,8},{10,11... | collective-permute-start | bytes 1327112 | tf_op jit(solution)/shard_map/ppermute | solution.py:66
  23.9 15.1 %collective-permute-start.19 = (bf16[3,64,1152]{2,1,0:T(8,128)(2,1)S(1)}, bf16[3,64,1152]{2,1,0:T(8,128)(2,1)S(1)}, u32[]{:S(2)}, u32[]{:S(2)}) collective-permute-start(bf16[3,64,1152]{2,1,0:T(8,128)(2,1)S(1)} %get-tuple-element.50._.lines.refs_2_), channel_id=1, source_target_pairs={{0,4},{2,6},{4,0},{6,2},{8,12},{10,14},{12,8},{14,10},{16,20},{18,... | collective-permute-start | bytes 1327112 | tf_op jit(solution)/shard_map/ppermute | solution.py:66
  25.4 12.8 %collective-permute-start.18 = (bf16[64,1152]{1,0:T(8,128)(2,1)S(1)}, bf16[64,1152]{1,0:T(8,128)(2,1)S(1)}, u32[]{:S(2)}, u32[]{:S(2)}) collective-permute-start(bf16[64,1152]{1,0:T(8,128)(2,1)S(1)} %get-tuple-element.48), channel_id=1, source_target_pairs={{0,4},{2,6},{4,0},{6,2},{8,12},{10,14},{12,8},{14,10},{16,20},{18,... | collective-permute-start | bytes 442376 | tf_op jit(solution)/shard_map/ppermute | solution.py:66
  26.0 19.1 %copy-start.2 = (bf16[128,2048]{1,0:T(8,128)(2,1)S(1)}, bf16[128,2048]{1,0:T(8,128)(2,1)}, u32[]{:S(2)}) copy-start(bf16[128,2048]{1,0:T(8,128)(2,1)} %refs_0_.3) | copy-start | bytes 1572868
  26.0 15.0 %collective-permute-start.4 = (bf16[64,1024]{1,0:T(8,128)(2,1)S(1)}, bf16[64,1024]{1,0:T(8,128)(2,1)S(1)}, u32[]{:S(2)}, u32[]{:S(2)}) collective-permute-start(bf16[64,1024]{1,0:T(8,128)(2,1)S(1)} %get-tuple-element.49), channel_id=1, source_target_pairs={{0,24},{2,26},{4,28},{6,30},{8,0},{10,2},{12,4},{14,6},{16,8},{18,... | collective-permute-start | bytes 393224 | tf_op jit(solution)/shard_map/ppermute | solution.py:71
  27.4 13.6 %collective-permute-start.5 = (bf16[64,1024]{1,0:T(8,128)(2,1)S(1)}, bf16[64,1024]{1,0:T(8,128)(2,1)S(1)}, u32[]{:S(2)}, u32[]{:S(2)}) collective-permute-start(bf16[64,1024]{1,0:T(8,128)(2,1)S(1)} %get-tuple-element.49), channel_id=1, source_target_pairs={{0,16},{2,18},{4,20},{6,22},{8,24},{10,26},{12,28},{14,30},{16,0},... | collective-permute-start | bytes 393224 | tf_op jit(solution)/shard_map/ppermute | solution.py:71
  38.3 6.8 %collective-permute-start.6 = (bf16[64,1024]{1,0:T(8,128)(2,1)S(1)}, bf16[64,1024]{1,0:T(8,128)(2,1)S(1)}, u32[]{:S(2)}, u32[]{:S(2)}) collective-permute-start(bf16[64,1024]{1,0:T(8,128)(2,1)S(1)} %get-tuple-element.49), channel_id=1, source_target_pairs={{0,8},{2,10},{4,12},{6,14},{8,16},{10,18},{12,20},{14,22},{16,24},... | collective-permute-start | bytes 393224 | tf_op jit(solution)/shard_map/ppermute | solution.py:71
  39.6 10.0 %collective-permute-start.21 = (bf16[4,64,512]{2,1,0:T(8,128)(2,1)S(1)}, bf16[4,64,512]{2,1,0:T(8,128)(2,1)S(1)}, u32[]{:S(2)}, u32[]{:S(2)}) collective-permute-start(bf16[4,64,512]{2,1,0:T(8,128)(2,1)S(1)} %get-tuple-element.56), channel_id=1, source_target_pairs={{0,1},{1,0},{2,3},{3,2},{4,5},{5,4},{6,7},{7,6},{8,9},{9,8},{10,11... | collective-permute-start | bytes 786440 | tf_op jit(solution)/shard_map/ppermute | solution.py:66
  45.6 16.5 %collective-permute-start.11 = (bf16[3,64,1024]{2,1,0:T(8,128)(2,1)S(1)}, bf16[3,64,1024]{2,1,0:T(8,128)(2,1)S(1)}, u32[]{:S(2)}, u32[]{:S(2)}) collective-permute-start(bf16[3,64,1024]{2,1,0:T(8,128)(2,1)S(1)} %stack.23.refs_2_), channel_id=1, source_target_pairs={{0,4},{2,6},{4,0},{6,2},{8,12},{10,14},{12,8},{14,10},{16,20},{18,... | collective-permute-start | bytes 1179656 | tf_op jit(solution)/shard_map/ppermute | solution.py:66
  47.2 15.5 %collective-permute-start.8 = (bf16[3,64,1024]{2,1,0:T(8,128)(2,1)S(1)}, bf16[3,64,1024]{2,1,0:T(8,128)(2,1)S(1)}, u32[]{:S(2)}, u32[]{:S(2)}) collective-permute-start(bf16[3,64,1024]{2,1,0:T(8,128)(2,1)S(1)} %stack.23.refs_2_), channel_id=1, source_target_pairs={{0,1},{1,0},{2,3},{3,2},{4,5},{5,4},{6,7},{7,6},{8,9},{9,8},{10,11... | collective-permute-start | bytes 1179656 | tf_op jit(solution)/shard_map/ppermute | solution.py:66
  47.7 13.0 %collective-permute-start.22 = (bf16[4,64,512]{2,1,0:T(8,128)(2,1)S(1)}, bf16[4,64,512]{2,1,0:T(8,128)(2,1)S(1)}, u32[]{:S(2)}, u32[]{:S(2)}) collective-permute-start(bf16[4,64,512]{2,1,0:T(8,128)(2,1)S(1)} %get-tuple-element.57), channel_id=1, source_target_pairs={{0,4},{2,6},{4,0},{6,2},{8,12},{10,14},{12,8},{14,10},{16,20},{18,... | collective-permute-start | bytes 786440 | tf_op jit(solution)/shard_map/ppermute | solution.py:66
  48.2 1.2 collective-permute-start.24
  49.4 18.9 %copy-start.3 = (bf16[2,384,2048]{2,1,0:T(8,128)(2,1)S(1)}, bf16[2,384,2048]{2,1,0:T(8,128)(2,1)}, u32[]{:S(2)}) copy-start(bf16[2,384,2048]{2,1,0:T(8,128)(2,1)} %refs_12_.3) | copy-start | bytes 9437188
  49.4 15.8 %collective-permute-start.20 = (bf16[4,64,1152]{2,1,0:T(8,128)(2,1)S(1)}, bf16[4,64,1152]{2,1,0:T(8,128)(2,1)S(1)}, u32[]{:S(2)}, u32[]{:S(2)}) collective-permute-start(bf16[4,64,1152]{2,1,0:T(8,128)(2,1)S(1)} %get-tuple-element.55.over.refs_6_), channel_id=1, source_target_pairs={{0,2},{2,0},{4,6},{6,4},{8,10},{10,8},{12,14},{14,12},{16,18},{18,... | collective-permute-start | bytes 1769480 | tf_op jit(solution)/shard_map/ppermute | solution.py:66
  49.6 12.6 %collective-permute-start.10 = (bf16[64,1024]{1,0:T(8,128)(2,1)S(1)}, bf16[64,1024]{1,0:T(8,128)(2,1)S(1)}, u32[]{:S(2)}, u32[]{:S(2)}) collective-permute-start(bf16[64,1024]{1,0:T(8,128)(2,1)S(1)} %get-tuple-element.49), channel_id=1, source_target_pairs={{0,4},{2,6},{4,0},{6,2},{8,12},{10,14},{12,8},{14,10},{16,20},{18,... | collective-permute-start | bytes 393224 | tf_op jit(solution)/shard_map/ppermute | solution.py:66
  60.8 7.5 %collective-permute-start = (bf16[128,2048]{1,0:T(8,128)(2,1)S(1)}, bf16[128,2048]{1,0:T(8,128)(2,1)S(1)}, u32[]{:S(2)}, u32[]{:S(2)}) collective-permute-start(bf16[128,2048]{1,0:T(8,128)(2,1)S(1)} %copy-done.2), channel_id=1, source_target_pairs={{0,2},{2,0},{4,6},{6,4},{8,10},{10,8},{12,14},{14,12},{16,18},{18,... | collective-permute-start | bytes 1572872 | tf_op jit(solution)/shard_map/ppermute | solution.py:66
  62.2 6.2 %collective-permute-start.23 = (bf16[4,64,1024]{2,1,0:T(8,128)(2,1)S(1)}, bf16[4,64,1024]{2,1,0:T(8,128)(2,1)S(1)}, u32[]{:S(2)}, u32[]{:S(2)}) collective-permute-start(bf16[4,64,1024]{2,1,0:T(8,128)(2,1)S(1)} %join.2.refs_8_), channel_id=1, source_target_pairs={{0,2},{2,0},{4,6},{6,4},{8,10},{10,8},{12,14},{14,12},{16,18},{18,... | collective-permute-start | bytes 1572872 | tf_op jit(solution)/shard_map/ppermute | solution.py:66
  62.2 2.5 %collective-permute-start.15 = (bf16[3,64,1152]{2,1,0:T(8,128)(2,1)S(1)}, bf16[3,64,1152]{2,1,0:T(8,128)(2,1)S(1)}, u32[]{:S(2)}, u32[]{:S(2)}) collective-permute-start(bf16[3,64,1152]{2,1,0:T(8,128)(2,1)S(1)} %get-tuple-element.50._.lines.refs_2_), channel_id=1, source_target_pairs={{0,2},{2,0},{4,6},{6,4},{8,10},{10,8},{12,14},{14,12},{16,18},{18,... | collective-permute-start | bytes 1327112 | tf_op jit(solution)/shard_map/ppermute | solution.py:66
  62.7 5.6 %collective-permute-start.17 = (bf16[3,64,1152]{2,1,0:T(8,128)(2,1)S(1)}, bf16[3,64,1152]{2,1,0:T(8,128)(2,1)S(1)}, u32[]{:S(2)}, u32[]{:S(2)}) collective-permute-start(bf16[3,64,1152]{2,1,0:T(8,128)(2,1)S(1)} %collective-permute-done.16.side.refs_4_), channel_id=1, source_target_pairs={{0,2},{2,0},{4,6},{6,4},{8,10},{10,8},{12,14},{14,12},{16,18},{18,... | collective-permute-start | bytes 1327112 | tf_op jit(solution)/shard_map/ppermute | solution.py:66
  64.7 9.7 %collective-permute-start.13 = (bf16[4,64,512]{2,1,0:T(8,128)(2,1)S(1)}, bf16[4,64,512]{2,1,0:T(8,128)(2,1)S(1)}, u32[]{:S(2)}, u32[]{:S(2)}) collective-permute-start(bf16[4,64,512]{2,1,0:T(8,128)(2,1)S(1)} %get-tuple-element.53.refs_13_), channel_id=1, source_target_pairs={{0,1},{1,0},{2,3},{3,2},{4,5},{5,4},{6,7},{7,6},{8,9},{9,8},{10,11... | collective-permute-start | bytes 786440 | tf_op jit(solution)/shard_map/ppermute | solution.py:66
  65.2 9.1 %collective-permute-start.14 = (bf16[4,64,512]{2,1,0:T(8,128)(2,1)S(1)}, bf16[4,64,512]{2,1,0:T(8,128)(2,1)S(1)}, u32[]{:S(2)}, u32[]{:S(2)}) collective-permute-start(bf16[4,64,512]{2,1,0:T(8,128)(2,1)S(1)} %get-tuple-element.54), channel_id=1, source_target_pairs={{0,4},{2,6},{4,0},{6,2},{8,12},{10,14},{12,8},{14,10},{16,20},{18,... | collective-permute-start | bytes 786440 | tf_op jit(solution)/shard_map/ppermute | solution.py:66
  68.2 9.4 %collective-permute-start.12 = (bf16[4,64,1024]{2,1,0:T(8,128)(2,1)S(1)}, bf16[4,64,1024]{2,1,0:T(8,128)(2,1)S(1)}, u32[]{:S(2)}, u32[]{:S(2)}) collective-permute-start(bf16[4,64,1024]{2,1,0:T(8,128)(2,1)S(1)} %get-tuple-element.52.refs_6_), channel_id=1, source_target_pairs={{0,2},{2,0},{4,6},{6,4},{8,10},{10,8},{12,14},{14,12},{16,18},{18,... | collective-permute-start | bytes 1572872 | tf_op jit(solution)/shard_map/ppermute | solution.py:66
  74.4 3.2 %collective-permute-start.25 = (bf16[4,64,1024]{2,1,0:T(8,128)(2,1)S(1)}, bf16[4,64,1024]{2,1,0:T(8,128)(2,1)S(1)}, u32[]{:S(2)}, u32[]{:S(2)}) collective-permute-start(bf16[4,64,1024]{2,1,0:T(8,128)(2,1)S(1)} %join.3.refs_8_), channel_id=1, source_target_pairs={{0,2},{2,0},{4,6},{6,4},{8,10},{10,8},{12,14},{14,12},{16,18},{18,... | collective-permute-start | bytes 1572872 | tf_op jit(solution)/shard_map/ppermute | solution.py:66
  75.0 2.1 %collective-permute-start.7 = (bf16[3,64,1024]{2,1,0:T(8,128)(2,1)S(1)}, bf16[3,64,1024]{2,1,0:T(8,128)(2,1)S(1)}, u32[]{:S(2)}, u32[]{:S(2)}) collective-permute-start(bf16[3,64,1024]{2,1,0:T(8,128)(2,1)S(1)} %stack.23.refs_2_), channel_id=1, source_target_pairs={{0,2},{2,0},{4,6},{6,4},{8,10},{10,8},{12,14},{14,12},{16,18},{18,... | collective-permute-start | bytes 1179656 | tf_op jit(solution)/shard_map/ppermute | solution.py:66
  75.1 2.6 %collective-permute-start.9 = (bf16[3,64,1024]{2,1,0:T(8,128)(2,1)S(1)}, bf16[3,64,1024]{2,1,0:T(8,128)(2,1)S(1)}, u32[]{:S(2)}, u32[]{:S(2)}) collective-permute-start(bf16[3,64,1024]{2,1,0:T(8,128)(2,1)S(1)} %collective-permute-done.8.side.refs_4_), channel_id=1, source_target_pairs={{0,2},{2,0},{4,6},{6,4},{8,10},{10,8},{12,14},{14,12},{16,18},{18,... | collective-permute-start | bytes 1179656 | tf_op jit(solution)/shard_map/ppermute | solution.py:66
  77.6 7.2 %copy-start.8 = (bf16[2,384,2048]{2,1,0:T(8,128)(2,1)S(1)}, bf16[2,384,2048]{2,1,0:T(8,128)(2,1)}, u32[]{:S(2)}) copy-start(bf16[2,384,2048]{2,1,0:T(8,128)(2,1)} %w_gate.3) | copy-start | bytes 9437188
  77.6 7.2 %copy-start.9 = (bf16[2,384,2048]{2,1,0:T(8,128)(2,1)S(1)}, bf16[2,384,2048]{2,1,0:T(8,128)(2,1)}, u32[]{:S(2)}) copy-start(bf16[2,384,2048]{2,1,0:T(8,128)(2,1)} %w_up.3) | copy-start | bytes 9437188
  91.2 7.0 %collective-permute-start.26 = (bf16[8,128,1024]{2,1,0:T(8,128)(2,1)S(1)}, bf16[8,128,1024]{2,1,0:T(8,128)(2,1)S(1)}, u32[]{:S(2)}, u32[]{:S(2)}) collective-permute-start(bf16[8,128,1024]{2,1,0:T(8,128)(2,1)S(1)} %get-tuple-element.64), channel_id=1, source_target_pairs={{0,2},{2,0},{4,6},{6,4},{8,10},{10,8},{12,14},{14,12},{16,18},{18,... | collective-permute-start | bytes 6291464 | tf_op jit(solution)/shard_map/ppermute | solution.py:66
  98.0 16.2 %collective-permute-start.34 = (bf16[8,128,1024]{2,1,0:T(8,128)(2,1)S(1)}, bf16[8,128,1024]{2,1,0:T(8,128)(2,1)S(1)}, u32[]{:S(2)}, u32[]{:S(2)}) collective-permute-start(bf16[8,128,1024]{2,1,0:T(8,128)(2,1)S(1)} %get-tuple-element.78), channel_id=1, source_target_pairs={{0,2},{2,0},{4,6},{6,4},{8,10},{10,8},{12,14},{14,12},{16,18},{18,... | collective-permute-start | bytes 6291464 | tf_op jit(solution)/shard_map/ppermute | solution.py:66
  98.5 14.3 %collective-permute-start.27 = (bf16[8,64,512]{2,1,0:T(8,128)(2,1)S(1)}, bf16[8,64,512]{2,1,0:T(8,128)(2,1)S(1)}, u32[]{:S(2)}, u32[]{:S(2)}) collective-permute-start(bf16[8,64,512]{2,1,0:T(8,128)(2,1)S(1)} %get-tuple-element.66), channel_id=1, source_target_pairs={{0,1},{1,0},{2,3},{3,2},{4,5},{5,4},{6,7},{7,6},{8,9},{9,8},{10,11... | collective-permute-start | bytes 1572872 | tf_op jit(solution)/shard_map/ppermute | solution.py:66
  100.1 13.9 %collective-permute-start.28 = (bf16[4,2,64,512]{3,2,1,0:T(8,128)(2,1)S(1)}, bf16[4,2,64,512]{3,2,1,0:T(8,128)(2,1)S(1)}, u32[]{:S(2)}, u32[]{:S(2)}) collective-permute-start(bf16[4,2,64,512]{3,2,1,0:T(8,128)(2,1)S(1)} %get-tuple-element.68), channel_id=1, source_target_pairs={{0,4},{2,6},{4,0},{6,2},{8,12},{10,14},{12,8},{14,10},{16,20},{18,... | collective-permute-start | bytes 1572872 | tf_op jit(solution)/shard_map/ppermute | solution.py:66
  114.5 14.9 %collective-permute-start.35 = (bf16[8,64,512]{2,1,0:T(8,128)(2,1)S(1)}, bf16[8,64,512]{2,1,0:T(8,128)(2,1)S(1)}, u32[]{:S(2)}, u32[]{:S(2)}) collective-permute-start(bf16[8,64,512]{2,1,0:T(8,128)(2,1)S(1)} %get-tuple-element.80), channel_id=1, source_target_pairs={{0,1},{1,0},{2,3},{3,2},{4,5},{5,4},{6,7},{7,6},{8,9},{9,8},{10,11... | collective-permute-start | bytes 1572872 | tf_op jit(solution)/shard_map/ppermute | solution.py:66
  115.1 14.9 %collective-permute-start.36 = (bf16[4,2,64,512]{3,2,1,0:T(8,128)(2,1)S(1)}, bf16[4,2,64,512]{3,2,1,0:T(8,128)(2,1)S(1)}, u32[]{:S(2)}, u32[]{:S(2)}) collective-permute-start(bf16[4,2,64,512]{3,2,1,0:T(8,128)(2,1)S(1)} %get-tuple-element.82), channel_id=1, source_target_pairs={{0,4},{2,6},{4,0},{6,2},{8,12},{10,14},{12,8},{14,10},{16,20},{18,... | collective-permute-start | bytes 1572872 | tf_op jit(solution)/shard_map/ppermute | solution.py:66
  115.6 20.0 %collective-permute-start.29 = (bf16[4,64,512]{2,1,0:T(8,128)(2,1)S(1)}, bf16[4,64,512]{2,1,0:T(8,128)(2,1)S(1)}, u32[]{:S(2)}, u32[]{:S(2)}) collective-permute-start(bf16[4,64,512]{2,1,0:T(8,128)(2,1)S(1)} %get-tuple-element.70._), channel_id=1, source_target_pairs={{0,4},{2,6},{4,0},{6,2},{8,12},{10,14},{12,8},{14,10},{16,20},{18,... | collective-permute-start | bytes 786440 | tf_op jit(solution)/shard_map/ppermute | solution.py:66
  117.1 18.5 %collective-permute-start.30 = (bf16[4,64,512]{2,1,0:T(8,128)(2,1)S(1)}, bf16[4,64,512]{2,1,0:T(8,128)(2,1)S(1)}, u32[]{:S(2)}, u32[]{:S(2)}) collective-permute-start(bf16[4,64,512]{2,1,0:T(8,128)(2,1)S(1)} %get-tuple-element.72), channel_id=1, source_target_pairs={{0,1},{1,0},{2,3},{3,2},{4,5},{5,4},{6,7},{7,6},{8,9},{9,8},{10,11... | collective-permute-start | bytes 786440 | tf_op jit(solution)/shard_map/ppermute | solution.py:66
  130.1 9.4 %collective-permute-start.37 = (bf16[4,64,512]{2,1,0:T(8,128)(2,1)S(1)}, bf16[4,64,512]{2,1,0:T(8,128)(2,1)S(1)}, u32[]{:S(2)}, u32[]{:S(2)}) collective-permute-start(bf16[4,64,512]{2,1,0:T(8,128)(2,1)S(1)} %get-tuple-element.84), channel_id=1, source_target_pairs={{0,4},{2,6},{4,0},{6,2},{8,12},{10,14},{12,8},{14,10},{16,20},{18,... | collective-permute-start | bytes 786440 | tf_op jit(solution)/shard_map/ppermute | solution.py:66
  130.7 8.8 %collective-permute-start.38 = (bf16[4,64,512]{2,1,0:T(8,128)(2,1)S(1)}, bf16[4,64,512]{2,1,0:T(8,128)(2,1)S(1)}, u32[]{:S(2)}, u32[]{:S(2)}) collective-permute-start(bf16[4,64,512]{2,1,0:T(8,128)(2,1)S(1)} %get-tuple-element.86), channel_id=1, source_target_pairs={{0,1},{1,0},{2,3},{3,2},{4,5},{5,4},{6,7},{7,6},{8,9},{9,8},{10,11... | collective-permute-start | bytes 786440 | tf_op jit(solution)/shard_map/ppermute | solution.py:66
  135.6 7.6 %collective-permute-start.31 = (bf16[64,1024]{1,0:T(8,128)(2,1)S(1)}, bf16[64,1024]{1,0:T(8,128)(2,1)S(1)}, u32[]{:S(2)}, u32[]{:S(2)}) collective-permute-start(bf16[64,1024]{1,0:T(8,128)(2,1)S(1)} %get-tuple-element.74), channel_id=1, source_target_pairs={{0,8},{2,10},{4,12},{6,14},{8,16},{10,18},{12,20},{14,22},{16,24},... | collective-permute-start | bytes 393224 | tf_op jit(solution)/shard_map/ppermute | solution.py:71
  135.7 13.2 %collective-permute-start.32 = (bf16[64,1024]{1,0:T(8,128)(2,1)S(1)}, bf16[64,1024]{1,0:T(8,128)(2,1)S(1)}, u32[]{:S(2)}, u32[]{:S(2)}) collective-permute-start(bf16[64,1024]{1,0:T(8,128)(2,1)S(1)} %get-tuple-element.75), channel_id=1, source_target_pairs={{0,16},{2,18},{4,20},{6,22},{8,24},{10,26},{12,28},{14,30},{16,0},... | collective-permute-start | bytes 393224 | tf_op jit(solution)/shard_map/ppermute | solution.py:71
  136.9 12.0 %collective-permute-start.33 = (bf16[64,1024]{1,0:T(8,128)(2,1)S(1)}, bf16[64,1024]{1,0:T(8,128)(2,1)S(1)}, u32[]{:S(2)}, u32[]{:S(2)}) collective-permute-start(bf16[64,1024]{1,0:T(8,128)(2,1)S(1)} %get-tuple-element.76), channel_id=1, source_target_pairs={{0,24},{2,26},{4,28},{6,30},{8,0},{10,2},{12,4},{14,6},{16,8},{18,... | collective-permute-start | bytes 393224 | tf_op jit(solution)/shard_map/ppermute | solution.py:71
  139.6 11.5 %collective-permute-start.39 = (bf16[64,1024]{1,0:T(8,128)(2,1)S(1)}, bf16[64,1024]{1,0:T(8,128)(2,1)S(1)}, u32[]{:S(2)}, u32[]{:S(2)}) collective-permute-start(bf16[64,1024]{1,0:T(8,128)(2,1)S(1)} %get-tuple-element.88), channel_id=1, source_target_pairs={{0,8},{2,10},{4,12},{6,14},{8,16},{10,18},{12,20},{14,22},{16,24},... | collective-permute-start | bytes 393224 | tf_op jit(solution)/shard_map/ppermute | solution.py:71
  140.2 16.4 %collective-permute-start.40 = (bf16[64,1024]{1,0:T(8,128)(2,1)S(1)}, bf16[64,1024]{1,0:T(8,128)(2,1)S(1)}, u32[]{:S(2)}, u32[]{:S(2)}) collective-permute-start(bf16[64,1024]{1,0:T(8,128)(2,1)S(1)} %get-tuple-element.89), channel_id=1, source_target_pairs={{0,16},{2,18},{4,20},{6,22},{8,24},{10,26},{12,28},{14,30},{16,0},... | collective-permute-start | bytes 393224 | tf_op jit(solution)/shard_map/ppermute | solution.py:71
  143.2 13.4 %collective-permute-start.41 = (bf16[64,1024]{1,0:T(8,128)(2,1)S(1)}, bf16[64,1024]{1,0:T(8,128)(2,1)S(1)}, u32[]{:S(2)}, u32[]{:S(2)}) collective-permute-start(bf16[64,1024]{1,0:T(8,128)(2,1)S(1)} %get-tuple-element.90), channel_id=1, source_target_pairs={{0,24},{2,26},{4,28},{6,30},{8,0},{10,2},{12,4},{14,6},{16,8},{18,... | collective-permute-start | bytes 393224 | tf_op jit(solution)/shard_map/ppermute | solution.py:71

commit v5 on v0

v5 whole, which is shorter than its diff:
```python
import functools

import jax
import jax.numpy as jnp
from jax import lax
from jax.experimental import pallas as pl
from jax.experimental.pallas import tpu as pltpu
from jax.sharding import PartitionSpec as P


def route_slots(expert_ids, expert_total):
    flat_ids = expert_ids.reshape(-1)
    one_hot = (flat_ids[:, None] == jnp.arange(expert_total, dtype=jnp.int32)[None, :]).astype(
        jnp.int32
    )
    before = jnp.cumsum(one_hot, axis=0) - one_hot
    return (flat_ids, jnp.sum(before * one_hot, axis=1))


def expert_step(arrived, saved_gate, saved_up, w_gate, w_up, w_down):
    hidden_grad = jnp.einsum("efd,esd->efs", w_down, arrived, preferred_element_type=jnp.float32)
    gate_value = saved_gate.astype(jnp.float32)
    up_value = saved_up.astype(jnp.float32)
    sigmoid_gate = jax.nn.sigmoid(gate_value)
    up_grad = (hidden_grad * gate_value * sigmoid_gate).astype(jnp.bfloat16)
    gate_grad = (
        hidden_grad * up_value * sigmoid_gate * (1.0 + gate_value * (1.0 - sigmoid_gate))
    ).astype(jnp.bfloat16)
    partial_value = jnp.einsum(
        "efs,efd->esd", gate_grad, w_gate, preferred_element_type=jnp.float32
    )
    partial_value = partial_value + jnp.einsum(
        "efs,efd->esd", up_grad, w_up, preferred_element_type=jnp.float32
    )
    return partial_value.astype(jnp.bfloat16)


def slots_body(cotangent, gates, expert_ids, saved_gate, saved_up, w_gate, w_up, w_down):
    owners = lax.axis_size("expert")
    row_count, feature_dim = cotangent.shape
    top_count = expert_ids.shape[1]
    local_count, _, slot_count = saved_gate.shape
    capacity = slot_count // owners
    flat_ids, slot_pos = route_slots(expert_ids, local_count * owners)
    target = flat_ids % local_count * slot_count + flat_ids // local_count * capacity + slot_pos
    scaled = (gates[:, :, None] * cotangent.astype(jnp.float32)[:, None, :]).astype(jnp.bfloat16)
    scaled = scaled.reshape(row_count * top_count, feature_dim)
    outgoing = (
        jnp.zeros((local_count * slot_count, feature_dim), jnp.bfloat16).at[target].set(scaled)
    )
    outgoing = outgoing.reshape(local_count, slot_count, feature_dim)
    arrived = lax.all_to_all(outgoing, "expert", split_axis=1, concat_axis=1, tiled=True)
    partial_value = expert_step(arrived, saved_gate, saved_up, w_gate, w_up, w_down)
    returned = lax.all_to_all(partial_value, "expert", split_axis=1, concat_axis=1, tiled=True)
    picked = returned.reshape(local_count * slot_count, feature_dim)[target].astype(jnp.float32)
    combined = jnp.sum(picked.reshape(row_count, top_count, feature_dim), axis=1)
    return lax.psum_scatter(combined, "tp", scatter_dimension=0, tiled=True)


CHUNKS = ((0, 2), (1, 3))
TILE = 512


def swap(value, axis, step):
    count = lax.axis_size(axis)
    return lax.ppermute(value, axis, [(i, i ^ step) for i in range(count)])


def along_line(value, shift):
    count = lax.axis_size("expert")
    return lax.ppermute(value, "expert", [(i, (i + 4 * shift) % count) for i in range(count)])


def small(kernel, name, outs, kinds, operands, scratch=(), limit=8, work=0):
    spaces = {"s": pltpu.SMEM, "v": pltpu.VMEM, "h": pltpu.HBM, "o": pl.ANY}
    return pl.pallas_call(
        kernel,
        out_shape=[
            out if hasattr(out, "dtype") else jax.ShapeDtypeStruct(out, jnp.bfloat16) for out in outs
        ],
        in_specs=[pl.BlockSpec(memory_space=spaces[kind]) for kind in kinds],
        scratch_shapes=list(scratch),
        compiler_params=pltpu.CompilerParams(vmem_limit_bytes=limit << 20),
        cost_estimate=pl.CostEstimate(flops=work, bytes_accessed=work >> 8, transcendentals=0),
        name=name,
    )(*operands)


def prepare_kernel(place, tokens, gates_any, ids_any, first, table, gates, ids, sems):
    piece = first.shape[0]
    width = first.shape[1] - table.shape[1]
    near = pl.multiple_of(place[3] * piece, piece)
    copies = [
        pltpu.make_async_copy(gates_any, gates, sems.at[0]),
        pltpu.make_async_copy(ids_any, ids, sems.at[1]),
        pltpu.make_async_copy(
            tokens.at[pl.ds(near, piece), :], first.at[:, pl.ds(0, width)], sems.at[2]
        ),
    ]
    for copy in copies:
        copy.start()
    copies[0].wait()
    copies[1].wait()
    rest = gates[...]
    terms = []
    for _ in range(3):
        term = rest.astype(jnp.bfloat16).astype(jnp.float32)
        terms.append(term)
        rest = rest - term
    terms.append(ids[...].astype(jnp.float32))
    unused = piece - 4 * gates.shape[0]
    terms.append(jnp.zeros((unused, gates.shape[1]), jnp.float32))
    packed = jnp.concatenate(terms, axis=0).astype(jnp.bfloat16)
    first[:, width:] = packed
    table[...] = packed
    copies[2].wait()


def prepare(place, cotangent, gates, ids, piece):
    return small(
        prepare_kernel,
        "prepare",
        [(piece, cotangent.shape[1] + 128), (piece, 128)],
        "shhh",
        (place, cotangent, gates, ids),
        [
            pltpu.VMEM(gates.shape, jnp.float32),
            pltpu.VMEM(ids.shape, jnp.int32),
            pltpu.SemaphoreType.DMA((3,)),
        ],
        limit=4,
    )


def stack_kernel(*refs):
    lines = refs[-1]
    for r in range(lines.shape[0]):
        lines[r] = refs[r][...]


def stack(pieces, *after):
    return small(
        stack_kernel,
        "stack",
        [(len(pieces),) + pieces[0].shape],
        "v" * len(pieces) + "o" * len(after),
        (*pieces, *after),
    )[0]


def relay_kernel(came, part, line, following):
    line[0] = came[...]
    following[...] = part[...]


def relay(came, part):
    return small(
        relay_kernel, "relay", [(1,) + came.shape, part.shape], "vv", (came, part)
    )


def turn_kernel(gate, up, _, gate_t, up_t):
    tile = 128
    for source, target in ((gate, gate_t), (up, up_t)):
        for e in range(source.shape[0]):
            for at in range(0, source.shape[2], tile):
                target[e, at:at + tile] = source[e, :, at:at + tile].astype(jnp.float32).T.astype(
                    jnp.bfloat16
                )


def turn(saved_gate, saved_up, after):
    count, units, slots = saved_gate.shape
    return small(
        turn_kernel,
        "turn",
        [(count, slots, units)] * 2,
        "vvo",
        (saved_gate, saved_up, after),
        limit=12,
    )


def corner_kernel(place, tokens, first, over, side, whole_over, left, right, sem):
    _, piece, middle = left.shape
    far = pl.multiple_of((1 - place[3]) * piece, piece)
    copy = pltpu.make_async_copy(
        tokens.at[pl.ds(far, piece), pl.ds(middle, middle)], right.at[0], sem.at[0]
    )
    copy.start()
    whole_over[0] = first[...]
    whole_over[1:] = over[...]
    left[0] = first[:, :middle]
    left[1:] = over[:, :, :middle]
    right[1:] = side[:, :, middle:2 * middle]
    copy.wait()


def own_corner(place, cotangent, first, over, side):
    count, piece, width = over.shape
    middle = cotangent.shape[1] // 2
    return small(
        corner_kernel,
        "own_corner",
        [(count + 1, piece, width)] + [(count + 1, piece, middle)] * 2,
        "shvvv",
        (place, cotangent, first, over, side),
        (pltpu.SemaphoreType.DMA((1,)),),
    )


def plain_corner_kernel(over, side, _, left, right):
    middle = left.shape[-1]
    left[...] = over[:, :, :middle]
    right[...] = side[:, :, middle:2 * middle]


def corner(over, side, middle, after):
    return small(
        plain_corner_kernel,
        "corner",
        [over.shape[:2] + (middle,)] * 2,
        "vvo",
        (over, side, after),
    )


def join_kernel(left, right, *refs):
    result = refs[-1]
    middle = left.shape[-1]
    result[:, :, :middle] = left[...]
    result[:, :, middle:] = right[...]


def join(left, right, *after):
    dims = left.shape
    return small(
        join_kernel,
        "join",
        [dims[:-1] + (2 * dims[-1],)],
        "vv" + "o" * len(after),
        (left, right, *after),
        work=1 << 36,
    )[0]


def tokens_of(own, lines, r, offsets):
    if r == 0:
        return own[...]
    return lines[r_place(r, offsets)]


def r_place(r, offsets):
    return [offset for offset in offsets if offset != 0].index(r)


def pair_base(place, line_count, r, ry, width):
    line = lax.rem(place[2] + r, line_count)
    row = place[1] if ry == 0 else 1 - place[1]
    return pl.multiple_of((line * 2 + row) * width, width)


def route_kernel(offsets, capacity, place, own, own_c, lines, lines_c, over, over_c, pick, pick_t, gate,
                 hits, gates):
    tokens = pick.shape[2] // 2
    width = over.shape[2] - 128
    core, row, line, half = place[0], place[1], place[2], place[3]
    first = (line * 4 + row * 2 + core) * 2
    for i, r in enumerate(offsets):
        for ry in range(2):
            tables = []
            for c in range(2):
                if ry == 1:
                    table = (over, over_c)[c][i, :32, width:]
                elif r == 0:
                    table = (own, own_c)[c][:32]
                else:
                    table = (lines, lines_c)[c][r_place(r, offsets), :32, width:]
                tables.append(table.astype(jnp.float32))
            swapped = core > 0
            ordered = [
                jnp.where(swapped, tables[1], tables[0]), jnp.where(swapped, tables[0], tables[1])
            ]
            for c in range(2):
                block = ordered[c]
                value = block[0:8] + block[8:16] + block[16:24]
                for e in range(2):
                    named = block[24:32] == (first + e).astype(jnp.float32)
                    at = ((i * 2 + ry) * 2 + c) * 2 + e
                    hits[at:at + 1] = jnp.sum(named.astype(jnp.float32), axis=0, keepdims=True)
                    gates[at:at + 1] = jnp.sum(
                        jnp.where(named, value, 0.0), axis=0, keepdims=True
                    )
    earlier = lax.broadcasted_iota(jnp.int32, (tokens, tokens), 0) < lax.broadcasted_iota(
        jnp.int32, (tokens, tokens), 1
    )
    hit = hits[...]
    slot = jnp.dot(
        hit.astype(jnp.bfloat16),
        earlier.astype(jnp.float32).astype(jnp.bfloat16),
        preferred_element_type=jnp.float32,
    )
    slot = jnp.where(hit > 0.5, slot, -1.0)
    turned = half > 0
    slot = jnp.where(turned, pltpu.roll(slot, tokens // 2, 1), slot)
    weight = jnp.where(turned, pltpu.roll(gates[...], tokens // 2, 1), gates[...])
    order = lax.broadcasted_iota(jnp.int32, (capacity, tokens), 0).astype(jnp.float32)
    for p in range(pick.shape[0]):
        rows = []
        for e in range(2):
            for c in range(2):
                at = (p * 2 + c) * 2 + e
                ones = (order == slot[at:at + 1]).astype(jnp.float32)
                column = jnp.sum(ones * weight[at:at + 1], axis=1, keepdims=True)
                place_in = (e * 2 + c) * capacity
                gate[p, place_in:place_in + capacity] = jnp.broadcast_to(
                    column, (capacity, gate.shape[2])
                )
                own_core = (core == c).astype(jnp.float32)
                rows.append(jnp.concatenate([ones * own_core, ones * (1.0 - own_core)], axis=1))
        matrix = jnp.concatenate(rows, axis=0)
        pick[p] = matrix.astype(jnp.bfloat16)
        count = matrix.shape[0]
        square = jnp.concatenate(
            [matrix, jnp.zeros((2 * tokens - count, 2 * tokens), jnp.float32)], axis=0
        )
        pick_t[p] = square.T[:, :count].astype(jnp.bfloat16)


def route(offsets, place, table, table_c, lines, lines_c, over, over_c, capacity):
    tokens = 2 * over.shape[1]
    pairs = 2 * len(offsets)
    rows = 4 * capacity
    return small(
        functools.partial(route_kernel, offsets, capacity),
        "route",
        [
            (pairs, rows, 2 * tokens),
            (pairs, 2 * tokens, rows),
            jax.ShapeDtypeStruct((pairs, rows, 128), jnp.float32),
        ],
        "s" + "v" * 6,
        (place, table, table_c, lines, lines_c, over, over_c),
        [pltpu.VMEM((4 * pairs, tokens), jnp.float32)] * 2,
    )


def hidden_kernel(offsets, line_count, place, own, own_c, lines, lines_c, side, side_c, over, over_c,
                  diag, diag_c, pick, gate, w_down, saved_gate, saved_up, _, grads, slots):
    piece = over.shape[1]
    width = diag.shape[2]
    rows = pick.shape[1] // 2
    units = w_down.shape[1]
    near = pl.multiple_of(place[3] * piece, piece)
    far = pl.multiple_of((1 - place[3]) * piece, piece)

    @pl.loop(0, width // TILE)
    def _(k):
        at = pl.ds(pl.multiple_of(k * TILE, TILE), TILE)
        for i, r in enumerate(offsets):
            for ry in range(2):
                parts = []
                for c in range(2):
                    if ry == 1:
                        parts += [(over, over_c)[c][i, :, at], (diag, diag_c)[c][i, :, at]]
                    elif r == 0:
                        group = (own, own_c)[c]
                        parts += [group[pl.ds(near, piece), at], group[pl.ds(far, piece), at]]
                    else:
                        j = r_place(r, offsets)
                        parts += [(lines, lines_c)[c][j, :, at], (side, side_c)[c][j, :, at]]
                p = i * 2 + ry
                picked = jnp.dot(
                    pick[p], jnp.concatenate(parts, axis=0), preferred_element_type=jnp.float32
                )
                weight = gate[p]
                weight = jnp.concatenate([weight] * (TILE // weight.shape[1]), axis=1)
                scaled = (picked * weight).astype(jnp.bfloat16)
                slots[0, p * rows:(p + 1) * rows, at] = scaled[:rows]
                slots[1, p * rows:(p + 1) * rows, at] = scaled[rows:]

    for e in range(2):
        total = lax.dot_general(
            slots[e], w_down[e], (((1,), (1,)), ((), ())), preferred_element_type=jnp.float32
        )
        for i, r in enumerate(offsets):
            for ry in range(2):
                p = i * 2 + ry
                mine = slice(p * rows, (p + 1) * rows)
                saved = pl.ds(pair_base(place, line_count, r, ry, rows), rows)
                hidden_grad = total[mine]
                gate_value = saved_gate[e, saved, :].astype(jnp.float32)
                up_value = saved_up[e, saved, :].astype(jnp.float32)
                sigmoid_gate = jax.nn.sigmoid(gate_value)
                grads[e, mine, units:] = (hidden_grad * gate_value * sigmoid_gate).astype(
                    jnp.bfloat16
                )
                grads[e, mine, :units] = (
                    hidden_grad * up_value * sigmoid_gate * (1.0 + gate_value * (1.0 - sigmoid_gate))
                ).astype(jnp.bfloat16)


def hidden(offsets, line_count, place, own, own_c, moved, pick, gate, w_down, saved, after):
    width = own.shape[1]
    units = w_down.shape[1]
    count = pick.shape[0] * pick.shape[1] // 2
    return small(
        functools.partial(hidden_kernel, offsets, line_count),
        "hidden",
        [(2, count, 2 * units)],
        "s" + "v" * 15 + "o",
        (place, own, own_c, *moved, pick, gate, w_down, *saved, after),
        [pltpu.VMEM((2, count, width), jnp.bfloat16)],
        limit=12,
    )[0]


def sums_kernel(offset, grads, w_gate, w_up, pick_t, _, keep, send, slots):
    rows = pick_t.shape[2] // 2
    tokens = pick_t.shape[1] // 2

    @pl.loop(0, keep.shape[2] // TILE)
    def _(k):
        at = pl.ds(pl.multiple_of(k * TILE, TILE), TILE)
        source = pl.ds(pl.multiple_of(offset + k * TILE, TILE), TILE)
        for e in range(2):
            weights = jnp.concatenate([w_gate[e, :, source], w_up[e, :, source]], axis=0)
            slots[e] = jnp.dot(grads[e], weights, preferred_element_type=jnp.float32).astype(
                jnp.bfloat16
            )
        for p in range(pick_t.shape[0]):
            mine = slice(p * rows, (p + 1) * rows)
            both = jnp.concatenate([slots[0, mine], slots[1, mine]], axis=0)
            total = jnp.dot(pick_t[p], both, preferred_element_type=jnp.float32).astype(
                jnp.bfloat16
            )
            keep[p, :, at] = total[:tokens]
            send[p, :, at] = total[tokens:]


def sums(offset, width, grads, w_gate, w_up, pick_t, after):
    pairs, tokens, _ = pick_t.shape
    _, count, units = grads.shape
    return small(
        functools.partial(sums_kernel, offset),
        "sums",
        [(pairs, tokens // 2, width)] * 2,
        "vvvvo",
        (grads, w_gate, w_up, pick_t, after),
        [pltpu.VMEM((2, count, TILE), jnp.bfloat16)],
        limit=8,
    )


def first_left_kernel(keep, came, _, send, kept):
    piece = kept.shape[1]
    kept[...] = keep[:, :piece] + came[:, :piece]
    send[...] = keep[:, piece:] + came[:, piece:]


def first_left(keep, came, after):
    pairs, tokens, width = keep.shape
    return small(
        first_left_kernel,
        "first_left",
        [(pairs, tokens // 2, width)] * 2,
        "vvo",
        (keep, came, after),
    )


def first_right_kernel(keep, came, _, send, kept):
    for i in range(kept.shape[0]):
        kept[i] = keep[2 * i] + came[2 * i]
        send[i] = keep[2 * i + 1] + came[2 * i + 1]


def first_right(keep, came, after):
    pairs, tokens, width = keep.shape
    return small(
        first_right_kernel,
        "first_right",
        [(pairs // 2, tokens, width)] * 2,
        "vvo",
        (keep, came, after),
    )


def second_kernel(keep_l, came_l, keep_r, came_r, _, send_l, left, send_r, right):
    piece = left.shape[1]
    for i in range(left.shape[0]):
        left[i] = keep_l[2 * i] + came_l[2 * i]
        send_l[i] = keep_l[2 * i + 1] + came_l[2 * i + 1]
        right[i] = keep_r[i, :piece] + came_r[i, :piece]
        send_r[i] = keep_r[i, piece:] + came_r[i, piece:]


def second_sum(keep_l, came_l, keep_r, came_r, after):
    lines = keep_r.shape[0]
    _, piece, middle = keep_l.shape
    return small(
        second_kernel,
        "second_sum",
        [(lines, piece, middle)] * 4,
        "vvvvo",
        (keep_l, came_l, keep_r, came_r, after),
        work=1 << 36,
    )


def third_kernel(left, came_l, right, came_r, _, *outs):
    middle = left.shape[-1]
    for columns, one, other in ((slice(0, middle), left, came_l), (slice(middle, None), right, came_r)):
        for i, out in enumerate(outs):
            out[:, columns] = (one[i].astype(jnp.float32) + other[i].astype(jnp.float32)).astype(
                out.dtype
            )


def third_sum(offsets, left, came_l, right, came_r, after):
    _, piece, middle = left.shape
    return small(
        third_kernel,
        "third_sum",
        [
            jax.ShapeDtypeStruct((piece, 2 * middle), jnp.float32 if r == 0 else jnp.bfloat16)
            for r in offsets
        ],
        "vvvvo",
        (left, came_l, right, came_r, after),
        work=1 << 36,
    )


def last_kernel(*refs):
    total = refs[0][...]
    for ref in refs[1:-1]:
        total = total + ref[...].astype(jnp.float32)
    refs[-1][...] = total


def tokens_body(cotangent, gates, expert_ids, saved_gate, saved_up, w_gate, w_up, w_down):
    owners = lax.axis_size("expert")
    row_count, feature_dim = cotangent.shape
    capacity = saved_gate.shape[2] // owners
    lines = owners // 4
    piece = row_count // 2
    middle = feature_dim // 2
    me, half = lax.axis_index("expert"), lax.axis_index("tp")
    place = jnp.stack([me % 2, me // 2 % 2, me // 4, half]).astype(jnp.int32)

    part, table = prepare(place, cotangent, gates.T, expert_ids.T, piece)
    first = swap(part, "expert", 2)
    own_c, table_c = swap(cotangent, "expert", 1), swap(table, "expert", 1)
    gathered, saved = [], None

    def compute(index, after):
        offsets, moved = CHUNKS[index], gathered[index]
        line, line_c, _, _, over, over_c = moved[:6]
        pick, pick_t, gate = route(
            offsets, place, table, table_c, line, line_c, over, over_c, capacity
        )
        grads = hidden(
            offsets, lines, place, cotangent, own_c, moved, pick, gate, w_down, saved, after
        )
        return grads, pick_t

    def spread(grads, pick_t, after):
        keep_l, send_l = sums(0, middle, grads, w_gate, w_up, pick_t, after)
        keep_r, send_r = sums(middle, middle, grads, w_gate, w_up, pick_t, send_l)
        return keep_l, swap(send_l, "expert", 1), keep_r, swap(send_r, "expert", 1), send_r

    for offsets in CHUNKS:
        pieces = [along_line(part, -r) for r in offsets if r != 0]
        if saved is None:
            line, part = relay(pieces[0], part)
            saved = turn(saved_gate, saved_up, line)
        else:
            line = stack(pieces, saved[0])
        side, over = swap(line, "tp", 1), swap(line, "expert", 2)
        if offsets[0] == 0:
            over, left, right = own_corner(place, cotangent, first, over, side)
            after = (left,)
        else:
            early = compute(0, line)
            left, right = corner(over, side, middle, early[0])
            early = spread(*early, left)
            after = (early[-1],)
        diag = join(swap(left, "tp", 1), swap(right, "expert", 2), *after)
        moved = []
        for array in (line, side, over, diag):
            moved += [array, swap(array, "expert", 1)]
        gathered.append(moved)

    def first_step(keep_l, came_l, keep_r, came_r, after):
        send_l, keep_l = first_left(keep_l, came_l, after)
        send_r, keep_r = first_right(keep_r, came_r, send_l)
        return keep_l, swap(send_l, "tp", 1), keep_r, swap(send_r, "expert", 2), send_r

    def second_step(offsets, sums_of_two, after, came):
        send_l, left, send_r, right = second_sum(*sums_of_two, after)
        came_l, came_r = swap(send_l, "expert", 2), swap(send_r, "tp", 1)
        rows = third_sum(offsets, left, came_l, right, came_r, send_l if came is None else came)
        return rows[0], [row if r == 0 else along_line(row, r) for r, row in zip(offsets, rows)], send_l

    early = first_step(*early[:4], gathered[1][6])
    late = spread(*compute(1, early[4]), early[4])
    done, early, after = second_step(CHUNKS[0], early[:4], early[4], None)
    late = first_step(*late[:4], after)
    _, late, _ = second_step(CHUNKS[1], late[:4], done, early[-1])
    terms = early + late
    return pl.pallas_call(
        last_kernel,
        out_shape=jax.ShapeDtypeStruct((piece, feature_dim), jnp.float32),
        compiler_params=pltpu.CompilerParams(vmem_limit_bytes=8 << 20),
        name="last_sum",
    )(*terms)


def body(*arrays):
    cotangent, gates, _, saved_gate = arrays[:4]
    owners = lax.axis_size("expert")
    fits = (
        owners == 16
        and lax.axis_size("tp") == 2
        and cotangent.shape[0] == 128
        and cotangent.shape[1] % (2 * TILE) == 0
        and gates.shape[1] == 8
        and saved_gate.shape[0] == 2
        and saved_gate.shape[2] // owners % 16 == 0
        and 4 * saved_gate.shape[2] // owners <= 256
    )
    return (tokens_body if fits else slots_body)(*arrays)


def solution(mesh):
    in_specs = (
        P("expert", None),
        P("expert", None),
        P("expert", None),
        P("expert", "tp", None),
        P("expert", "tp", None),
        P("expert", "tp", None),
        P("expert", "tp", None),
        P("expert", "tp", None),
    )
    out_specs = P(("expert", "tp"), None)
    return jax.shard_map(body, mesh=mesh, in_specs=in_specs, out_specs=out_specs, check_vma=False)
```

time: 428 us -> 120 us (0.28)
  waiting for transfers between devices: 267 us -> 59 us
  local copies, waits for them, and re-layouts: 59.5 us -> 3.71 us
  other arithmetic: 28.4 us -> 0.08 us
  Pallas kernels: 0 us -> 23.4 us
  matrix products: 23.2 us -> 0 us
  between operations: 13.5 us -> 0.25 us
    all_to_all x2 -> x0, waiting for transfers between devices: 223 us -> none  [the longest x1 114 us: body(): lax.all_to_all(partial_value, 'expert', split_axis=1, concat_axis=1, tile...]
    ppermute x0 -> x37, waiting for transfers between devices: none -> 59 us  [the longest x31 35 us: swap(): return lax.ppermute(value, axis, [(i, i ^ step) for i in range(count)])]
    reduce_scatter x1 -> x0, waiting for transfers between devices: 43.8 us -> none  [body(): return lax.psum_scatter(combined, 'tp', scatter_dimension=0, tiled=True)]
    all_to_all x2 -> x0, starting transfers between devices: 35.6 us -> none  [the longest x1 28.1 us: body(): lax.all_to_all(partial_value, 'expert', split_axis=1, concat_axis=1, tile...]
    ppermute x0 -> x37, starting transfers between devices: none -> 33.4 us  [the longest x31 21.8 us: swap(): return lax.ppermute(value, axis, [(i, i ^ step) for i in range(count)])]
    pallas_call x0 -> x25, Pallas kernels: none -> 23.4 us  [the longest x24 22.5 us: small(): pl.pallas_call(kernel, out_shape=[out if hasattr(out, 'dtype') else jax.S...]
    dot_general x3 -> x0, matrix products: 23.2 us -> none  [the longest x1 9.2 us: body(): jnp.einsum('efd,esd->efs', w_down, arrived, preferred_element_type=jnp.fl...]
    convert_element_type x1 -> x0, local copies, waits for them, and re-layouts: 18.8 us -> none  [body(): partial_value = partial_value.astype(jnp.bfloat16)]
  transfers between devices with their start and end apart: 3 -> 37, of which waited for: 3 -> 20; matrix products, arithmetic and copies ran while one was open for 1% -> 0% of each run, Pallas kernels for 0% -> 18%
where the time goes in v5:
time: 120 us
  waiting for transfers between devices  59 us (49%)
  starting transfers between devices  33.4 us (28%)
  Pallas kernels  23.4 us (20%)
  local copies, waits for them, and re-layouts  3.71 us (3%)
    ppermute x31, waiting for transfers between devices, swap(): return lax.ppermute(value, axis, [(i, i ^ step) for i in range(count)])  35 us
    ppermute x6, waiting for transfers between devices, along_line(): lax.ppermute(value, 'expert', [(i, (i + 4 * shift) % count) for i in rang...  24 us
    pallas_call x24, Pallas kernels, small(): pl.pallas_call(kernel, out_shape=[out if hasattr(out, 'dtype') else jax.S...  22.5 us
    ppermute x31, starting transfers between devices, swap(): return lax.ppermute(value, axis, [(i, i ^ step) for i in range(count)])  21.8 us
    ppermute x6, starting transfers between devices, along_line(): lax.ppermute(value, 'expert', [(i, (i + 4 * shift) % count) for i in rang...  11.5 us
    unnamed x18, local copies, waits for them, and re-layouts  3.71 us
  transfers between devices with their start and end apart: 37, of which 20 were waited for; matrix products, arithmetic and copies ran while one was open for 0% of the time, Pallas kernels for 18%

profile of v5, /device:TPU:0, one launch (start us, length us, event | category | flops | bytes accessed | tf_op | source)
XLA Modules:
  0.0 119.8 jit_solution(7915756534346885362)
XLA Ops:
  0.1 1.0 copy-done.3
  1.1 0.7 copy-done.7
  1.8 0.7 copy-done.8
  2.5 0.6 prepare.1
  3.1 4.1 %collective-permute-start.1 = (bf16[64,2176]{1,0:T(8,128)(2,1)S(1)}, bf16[64,2176]{1,0:T(8,128)(2,1)S(1)}, u32[]{:S(2)}, u32[]{:S(2)}) collective-permute-start(bf16[64,2176]{1,0:T(8,128)(2,1)S(1)} %get-tuple-element.50.part), channel_id=1, source_target_pairs={{0,16},{2,18},{4,20},{6,22},{8,24},{10,26},{12,28},{14,30},{16,0},... | collective-permute-start | bytes 835592 | tf_op jit(solution)/shard_map/ppermute | solution.py:71
  7.2 1.5 %collective-permute-start.5 = (bf16[64,2176]{1,0:T(8,128)(2,1)S(1)}, bf16[64,2176]{1,0:T(8,128)(2,1)S(1)}, u32[]{:S(2)}, u32[]{:S(2)}) collective-permute-start(bf16[64,2176]{1,0:T(8,128)(2,1)S(1)} %get-tuple-element.50.part), channel_id=1, source_target_pairs={{0,4},{2,6},{4,0},{6,2},{8,12},{10,14},{12,8},{14,10},{16,20},{18,... | collective-permute-start | bytes 835592 | tf_op jit(solution)/shard_map/ppermute | solution.py:66
  8.7 11.1 %collective-permute-done.1.came = bf16[64,2176]{1,0:T(8,128)(2,1)S(1)} collective-permute-done((bf16[64,2176]{1,0:T(8,128)(2,1)S(1)}, bf16[64,2176]{1,0:T(8,128)(2,1)S(1)}, u32[]{:S(2)}, u32[]{:S(2)}) %collective-permute-start.1) | collective-permute-done | bytes 278560 | tf_op jit(solution)/shard_map/ppermute | solution.py:71
  19.9 1.6 %collective-permute-start.3 = (bf16[1,64,2176]{2,1,0:T(8,128)(2,1)S(1)}, bf16[1,64,2176]{2,1,0:T(8,128)(2,1)S(1)}, u32[]{:S(2)}, u32[]{:S(2)}) collective-permute-start(bf16[1,64,2176]{2,1,0:T(8,128)(2,1)S(1)} %get-tuple-element.51.lines._), channel_id=1, source_target_pairs={{0,1},{1,0},{2,3},{3,2},{4,5},{5,4},{6,7},{7,6},{8,9},{9,8},{10,11... | collective-permute-start | bytes 835592 | tf_op jit(solution)/shard_map/ppermute | solution.py:66
  21.5 1.5 %collective-permute-start.6 = (bf16[1,64,2176]{2,1,0:T(8,128)(2,1)S(1)}, bf16[1,64,2176]{2,1,0:T(8,128)(2,1)S(1)}, u32[]{:S(2)}, u32[]{:S(2)}) collective-permute-start(bf16[1,64,2176]{2,1,0:T(8,128)(2,1)S(1)} %get-tuple-element.51.lines._), channel_id=1, source_target_pairs={{0,4},{2,6},{4,0},{6,2},{8,12},{10,14},{12,8},{14,10},{16,20},{18,... | collective-permute-start | bytes 835592 | tf_op jit(solution)/shard_map/ppermute | solution.py:66
  23.0 3.5 %collective-permute-start.12 = (bf16[64,2176]{1,0:T(8,128)(2,1)S(1)}, bf16[64,2176]{1,0:T(8,128)(2,1)S(1)}, u32[]{:S(2)}, u32[]{:S(2)}) collective-permute-start(bf16[64,2176]{1,0:T(8,128)(2,1)S(1)} %get-tuple-element.60), channel_id=1, source_target_pairs={{0,24},{2,26},{4,28},{6,30},{8,0},{10,2},{12,4},{14,6},{16,8},{18,... | collective-permute-start | bytes 835592 | tf_op jit(solution)/shard_map/ppermute | solution.py:71
  26.5 1.3 %collective-permute-done.3.side = bf16[1,64,2176]{2,1,0:T(8,128)(2,1)S(1)} collective-permute-done((bf16[1,64,2176]{2,1,0:T(8,128)(2,1)S(1)}, bf16[1,64,2176]{2,1,0:T(8,128)(2,1)S(1)}, u32[]{:S(2)}, u32[]{:S(2)}) %collective-permute-start.3) | collective-permute-done | bytes 278560 | tf_op jit(solution)/shard_map/ppermute | solution.py:66
  27.8 1.0 collective-permute-done.6.over
  28.8 0.6 own_corner.1
  29.4 0.8 collective-permute-start.8
  30.3 1.3 %collective-permute-start.9 = (bf16[2,64,1024]{2,1,0:T(8,128)(2,1)S(1)}, bf16[2,64,1024]{2,1,0:T(8,128)(2,1)S(1)}, u32[]{:S(2)}, u32[]{:S(2)}) collective-permute-start(bf16[2,64,1024]{2,1,0:T(8,128)(2,1)S(1)} %get-tuple-element.54), channel_id=1, source_target_pairs={{0,4},{2,6},{4,0},{6,2},{8,12},{10,14},{12,8},{14,10},{16,20},{18,... | collective-permute-start | bytes 786440 | tf_op jit(solution)/shard_map/ppermute | solution.py:66
  31.5 1.3 %copy-done.6 = bf16[2,384,768]{2,1,0:T(8,128)(2,1)S(1)} copy-done((bf16[2,384,768]{2,1,0:T(8,128)(2,1)S(1)}, bf16[2,384,768]{2,1,0:T(8,128)(2,1)}, u32[]{:S(2)}) %copy-start.6) | copy-done | bytes 1179672
  32.8 0.7 turn.1
  33.6 0.5 collective-permute-start.2
  34.1 4.7 %collective-permute-done.13.refs_1_ = bf16[64,2176]{1,0:T(8,128)(2,1)S(1)} collective-permute-done((bf16[64,2176]{1,0:T(8,128)(2,1)S(1)}, bf16[64,2176]{1,0:T(8,128)(2,1)S(1)}, u32[]{:S(2)}, u32[]{:S(2)}) %collective-permute-start.13) | collective-permute-done | bytes 278560 | tf_op jit(solution)/shard_map/ppermute | solution.py:71
  38.8 0.6 collective-permute-start.14
  39.4 0.5 collective-permute-start.15
  40.0 0.6 collective-permute-start
  40.6 1.2 %collective-permute-done.7.over_c = bf16[2,64,2176]{2,1,0:T(8,128)(2,1)S(1)} collective-permute-done((bf16[2,64,2176]{2,1,0:T(8,128)(2,1)S(1)}, bf16[2,64,2176]{2,1,0:T(8,128)(2,1)S(1)}, u32[]{:S(2)}, u32[]{:S(2)}) %collective-permute-start.7) | collective-permute-done | bytes 557088 | tf_op jit(solution)/shard_map/ppermute | solution.py:66
  41.9 0.1 collective-permute-start.4
  42.0 1.1 route.2
  43.1 0.6 collective-permute-done.4.side_c
  43.8 4.2 %hidden.2._.grads = bf16[2,384,768]{2,1,0:T(8,128)(2,1)S(1)} custom-call(s32[4]{0:T(128)S(1)} %pad_add_fusion.place, bf16[128,2048]{1,0:T(8,128)(2,1)S(1)} %copy-done.4, bf16[128,2048]{1,0:T(8,128)(2,1)S(1)} %collective-permute-done.own_c, bf16[1,64,2176]{2,1,0:T(8,128)(2,1)S(1)} %get-tuple-element.51.lines._, ...), custom_call_target="tpu_custom_call" | custom-call | tf_op jit(solution)/shard_map/hidden/pallas_call | solution.py:76
  47.9 4.3 %collective-permute-done.14.over = bf16[2,64,2176]{2,1,0:T(8,128)(2,1)S(1)} collective-permute-done((bf16[2,64,2176]{2,1,0:T(8,128)(2,1)S(1)}, bf16[2,64,2176]{2,1,0:T(8,128)(2,1)S(1)}, u32[]{:S(2)}, u32[]{:S(2)}) %collective-permute-start.14) | collective-permute-done | bytes 557088 | tf_op jit(solution)/shard_map/ppermute | solution.py:66
  52.2 0.2 collective-permute-done.15.side
  52.5 0.6 collective-permute-start.17
  53.1 1.5 %collective-permute-start.18 = (bf16[2,64,1024]{2,1,0:T(8,128)(2,1)S(1)}, bf16[2,64,1024]{2,1,0:T(8,128)(2,1)S(1)}, u32[]{:S(2)}, u32[]{:S(2)}) collective-permute-start(bf16[2,64,1024]{2,1,0:T(8,128)(2,1)S(1)} %get-tuple-element.65), channel_id=1, source_target_pairs={{0,4},{2,6},{4,0},{6,2},{8,12},{10,14},{12,8},{14,10},{16,20},{18,... | collective-permute-start | bytes 786440 | tf_op jit(solution)/shard_map/ppermute | solution.py:66
  54.6 0.5 collective-permute-start.26
  55.1 2.2 %sums.4 = (bf16[4,128,1024]{2,1,0:T(8,128)(2,1)S(1)}, bf16[4,128,1024]{2,1,0:T(8,128)(2,1)S(1)}) custom-call(bf16[2,384,768]{2,1,0:T(8,128)(2,1)S(1)} %hidden.2._.grads, bf16[2,384,2048]{2,1,0:T(8,128)(2,1)S(1)} %copy-done, bf16[2,384,2048]{2,1,0:T(8,128)(2,1)S(1)} %copy-done.1, bf16[4,256,192]{2,1,0:T(8,128)(2,1)S(1)} %get-tuple-element.61.pick_t, ...), custom_call_target="tpu_custom_call" | custom-call | tf_op jit(solution)/shard_map/sums/pallas_call | solution.py:76
  57.4 2.2 %sums.5 = (bf16[4,128,1024]{2,1,0:T(8,128)(2,1)S(1)}, bf16[4,128,1024]{2,1,0:T(8,128)(2,1)S(1)}) custom-call(bf16[2,384,768]{2,1,0:T(8,128)(2,1)S(1)} %hidden.2._.grads, bf16[2,384,2048]{2,1,0:T(8,128)(2,1)S(1)} %copy-done, bf16[2,384,2048]{2,1,0:T(8,128)(2,1)S(1)} %copy-done.1, bf16[4,256,192]{2,1,0:T(8,128)(2,1)S(1)} %get-tuple-element.61.pick_t, ...), custom_call_target="tpu_custom_call" | custom-call | tf_op jit(solution)/shard_map/sums/pallas_call | solution.py:76
  59.7 0.6 collective-permute-start.16
  60.4 2.2 %collective-permute-done.16.came = bf16[4,128,1024]{2,1,0:T(8,128)(2,1)S(1)} collective-permute-done((bf16[4,128,1024]{2,1,0:T(8,128)(2,1)S(1)}, bf16[4,128,1024]{2,1,0:T(8,128)(2,1)S(1)}, u32[]{:S(2)}, u32[]{:S(2)}) %collective-permute-start.16) | collective-permute-done | bytes 1048608 | tf_op jit(solution)/shard_map/ppermute | solution.py:66
  62.5 0.4 collective-permute-start.28
  62.9 0.2 first_left.2
  63.0 1.0 collective-permute-done.20.came
  64.0 1.5 %collective-permute-start.19 = (bf16[4,64,1024]{2,1,0:T(8,128)(2,1)S(1)}, bf16[4,64,1024]{2,1,0:T(8,128)(2,1)S(1)}, u32[]{:S(2)}, u32[]{:S(2)}) collective-permute-start(bf16[4,64,1024]{2,1,0:T(8,128)(2,1)S(1)} %get-tuple-element.68._), channel_id=1, source_target_pairs={{0,1},{1,0},{2,3},{3,2},{4,5},{5,4},{6,7},{7,6},{8,9},{9,8},{10,11... | collective-permute-start | bytes 1572872 | tf_op jit(solution)/shard_map/ppermute | solution.py:66
  65.6 0.6 collective-permute-start.21
  66.2 1.1 route.3
  67.3 4.1 %hidden.3.grads = bf16[2,384,768]{2,1,0:T(8,128)(2,1)S(1)} custom-call(s32[4]{0:T(128)S(1)} %pad_add_fusion.place, bf16[128,2048]{1,0:T(8,128)(2,1)S(1)} %copy-done.4, bf16[128,2048]{1,0:T(8,128)(2,1)S(1)} %collective-permute-done.own_c, bf16[2,64,2176]{2,1,0:T(8,128)(2,1)S(1)} %stack.21._.lines, bf16[2,64,2176]{2,1,0:T(8,128)(2,1)S(1)} %collective-permute-done.25.lines_c, ...), custom_call_target="tpu_custom_call" | custom-call | tf_op jit(solution)/shard_map/hidden/pallas_call | solution.py:76
  71.5 2.2 %sums.6 = (bf16[4,128,1024]{2,1,0:T(8,128)(2,1)S(1)}, bf16[4,128,1024]{2,1,0:T(8,128)(2,1)S(1)}) custom-call(bf16[2,384,768]{2,1,0:T(8,128)(2,1)S(1)} %hidden.3.grads, bf16[2,384,2048]{2,1,0:T(8,128)(2,1)S(1)} %copy-done, bf16[2,384,2048]{2,1,0:T(8,128)(2,1)S(1)} %copy-done.1, bf16[4,256,192]{2,1,0:T(8,128)(2,1)S(1)} %get-tuple-element.80.pick_t, ...), custom_call_target="tpu_custom_call" | custom-call | tf_op jit(solution)/shard_map/sums/pallas_call | solution.py:76
  73.8 2.2 %sums.7 = (bf16[4,128,1024]{2,1,0:T(8,128)(2,1)S(1)}, bf16[4,128,1024]{2,1,0:T(8,128)(2,1)S(1)}) custom-call(bf16[2,384,768]{2,1,0:T(8,128)(2,1)S(1)} %hidden.3.grads, bf16[2,384,2048]{2,1,0:T(8,128)(2,1)S(1)} %copy-done, bf16[2,384,2048]{2,1,0:T(8,128)(2,1)S(1)} %copy-done.1, bf16[4,256,192]{2,1,0:T(8,128)(2,1)S(1)} %get-tuple-element.80.pick_t, ...), custom_call_target="tpu_custom_call" | custom-call | tf_op jit(solution)/shard_map/sums/pallas_call | solution.py:76
  76.1 0.6 collective-permute-start.31
  76.6 1.6 %collective-permute-done.19.came_l = bf16[4,64,1024]{2,1,0:T(8,128)(2,1)S(1)} collective-permute-done((bf16[4,64,1024]{2,1,0:T(8,128)(2,1)S(1)}, bf16[4,64,1024]{2,1,0:T(8,128)(2,1)S(1)}, u32[]{:S(2)}, u32[]{:S(2)}) %collective-permute-start.19) | collective-permute-done | bytes 524320 | tf_op jit(solution)/shard_map/ppermute | solution.py:66
  78.2 1.4 %collective-permute-done.21.came_r = bf16[2,128,1024]{2,1,0:T(8,128)(2,1)S(1)} collective-permute-done((bf16[2,128,1024]{2,1,0:T(8,128)(2,1)S(1)}, bf16[2,128,1024]{2,1,0:T(8,128)(2,1)S(1)}, u32[]{:S(2)}, u32[]{:S(2)}) %collective-permute-start.21) | collective-permute-done | bytes 524320 | tf_op jit(solution)/shard_map/ppermute | solution.py:66
  79.7 0.6 collective-permute-start.22
  80.3 0.6 collective-permute-start.23
  81.0 1.5 %collective-permute-start.30 = (bf16[4,64,1024]{2,1,0:T(8,128)(2,1)S(1)}, bf16[4,64,1024]{2,1,0:T(8,128)(2,1)S(1)}, u32[]{:S(2)}, u32[]{:S(2)}) collective-permute-start(bf16[4,64,1024]{2,1,0:T(8,128)(2,1)S(1)} %get-tuple-element.84._), channel_id=1, source_target_pairs={{0,1},{1,0},{2,3},{3,2},{4,5},{5,4},{6,7},{7,6},{8,9},{9,8},{10,11... | collective-permute-start | bytes 1572872 | tf_op jit(solution)/shard_map/ppermute | solution.py:66
  82.6 1.6 %collective-permute-start.32 = (bf16[2,128,1024]{2,1,0:T(8,128)(2,1)S(1)}, bf16[2,128,1024]{2,1,0:T(8,128)(2,1)S(1)}, u32[]{:S(2)}, u32[]{:S(2)}) collective-permute-start(bf16[2,128,1024]{2,1,0:T(8,128)(2,1)S(1)} %get-tuple-element.88), channel_id=1, source_target_pairs={{0,4},{2,6},{4,0},{6,2},{8,12},{10,14},{12,8},{14,10},{16,20},{18,... | collective-permute-start | bytes 1572872 | tf_op jit(solution)/shard_map/ppermute | solution.py:66
  84.2 4.8 %collective-permute-done.22.came_l = bf16[2,64,1024]{2,1,0:T(8,128)(2,1)S(1)} collective-permute-done((bf16[2,64,1024]{2,1,0:T(8,128)(2,1)S(1)}, bf16[2,64,1024]{2,1,0:T(8,128)(2,1)S(1)}, u32[]{:S(2)}, u32[]{:S(2)}) %collective-permute-start.22) | collective-permute-done | bytes 262176 | tf_op jit(solution)/shard_map/ppermute | solution.py:66
  89.0 0.5 collective-permute-done.23.came_r
  89.7 9.0 %collective-permute-done.30.came_l = bf16[4,64,1024]{2,1,0:T(8,128)(2,1)S(1)} collective-permute-done((bf16[4,64,1024]{2,1,0:T(8,128)(2,1)S(1)}, bf16[4,64,1024]{2,1,0:T(8,128)(2,1)S(1)}, u32[]{:S(2)}, u32[]{:S(2)}) %collective-permute-start.30) | collective-permute-done | bytes 524320 | tf_op jit(solution)/shard_map/ppermute | solution.py:66
  98.8 1.6 %collective-permute-start.33 = (bf16[2,64,1024]{2,1,0:T(8,128)(2,1)S(1)}, bf16[2,64,1024]{2,1,0:T(8,128)(2,1)S(1)}, u32[]{:S(2)}, u32[]{:S(2)}) collective-permute-start(bf16[2,64,1024]{2,1,0:T(8,128)(2,1)S(1)} %get-tuple-element.90), channel_id=1, source_target_pairs={{0,4},{2,6},{4,0},{6,2},{8,12},{10,14},{12,8},{14,10},{16,20},{18,... | collective-permute-start | bytes 786440 | tf_op jit(solution)/shard_map/ppermute | solution.py:66
  100.4 0.5 collective-permute-start.34
  101.0 4.3 %collective-permute-done.33.came_l = bf16[2,64,1024]{2,1,0:T(8,128)(2,1)S(1)} collective-permute-done((bf16[2,64,1024]{2,1,0:T(8,128)(2,1)S(1)}, bf16[2,64,1024]{2,1,0:T(8,128)(2,1)S(1)}, u32[]{:S(2)}, u32[]{:S(2)}) %collective-permute-start.33) | collective-permute-done | bytes 262176 | tf_op jit(solution)/shard_map/ppermute | solution.py:66
  105.3 1.5 %collective-permute-done.34.came_r = bf16[2,64,1024]{2,1,0:T(8,128)(2,1)S(1)} collective-permute-done((bf16[2,64,1024]{2,1,0:T(8,128)(2,1)S(1)}, bf16[2,64,1024]{2,1,0:T(8,128)(2,1)S(1)}, u32[]{:S(2)}, u32[]{:S(2)}) %collective-permute-start.34) | collective-permute-done | bytes 262176 | tf_op jit(solution)/shard_map/ppermute | solution.py:66
  106.9 1.6 %collective-permute-start.35 = (bf16[64,2048]{1,0:T(8,128)(2,1)S(1)}, bf16[64,2048]{1,0:T(8,128)(2,1)S(1)}, u32[]{:S(2)}, u32[]{:S(2)}) collective-permute-start(bf16[64,2048]{1,0:T(8,128)(2,1)S(1)} %get-tuple-element.93), channel_id=1, source_target_pairs={{0,8},{2,10},{4,12},{6,14},{8,16},{10,18},{12,20},{14,22},{16,24},... | collective-permute-start | bytes 786440 | tf_op jit(solution)/shard_map/ppermute | solution.py:71
  108.5 2.3 %collective-permute-start.36 = (bf16[64,2048]{1,0:T(8,128)(2,1)S(1)}, bf16[64,2048]{1,0:T(8,128)(2,1)S(1)}, u32[]{:S(2)}, u32[]{:S(2)}) collective-permute-start(bf16[64,2048]{1,0:T(8,128)(2,1)S(1)} %get-tuple-element.94), channel_id=1, source_target_pairs={{0,24},{2,26},{4,28},{6,30},{8,0},{10,2},{12,4},{14,6},{16,8},{18,... | collective-permute-start | bytes 786440 | tf_op jit(solution)/shard_map/ppermute | solution.py:71
  110.8 6.1 %collective-permute-done.35.refs_2_ = bf16[64,2048]{1,0:T(8,128)(2,1)S(1)} collective-permute-done((bf16[64,2048]{1,0:T(8,128)(2,1)S(1)}, bf16[64,2048]{1,0:T(8,128)(2,1)S(1)}, u32[]{:S(2)}, u32[]{:S(2)}) %collective-permute-start.35) | collective-permute-done | bytes 262176 | tf_op jit(solution)/shard_map/ppermute | solution.py:71
  116.9 2.0 %collective-permute-done.36.refs_3_ = bf16[64,2048]{1,0:T(8,128)(2,1)S(1)} collective-permute-done((bf16[64,2048]{1,0:T(8,128)(2,1)S(1)}, bf16[64,2048]{1,0:T(8,128)(2,1)S(1)}, u32[]{:S(2)}, u32[]{:S(2)}) %collective-permute-start.36) | collective-permute-done | bytes 262176 | tf_op jit(solution)/shard_map/ppermute | solution.py:71
  118.9 0.9 last_sum.1
  (54 shorter events, 1.6 us)
Async XLA Ops:
  0.1 1.0 copy-start.3
  1.1 0.7 copy-start.7
  1.8 0.7 copy-start.8
  2.5 26.3 %copy-start.4 = (bf16[128,2048]{1,0:T(8,128)(2,1)S(1)}, bf16[128,2048]{1,0:T(8,128)(2,1)}, u32[]{:S(2)}) copy-start(bf16[128,2048]{1,0:T(8,128)(2,1)} %own.3) | copy-start | bytes 1572868
  2.5 29.0 %copy-start.5 = (bf16[2,384,768]{2,1,0:T(8,128)(2,1)S(1)}, bf16[2,384,768]{2,1,0:T(8,128)(2,1)}, u32[]{:S(2)}) copy-start(bf16[2,384,768]{2,1,0:T(8,128)(2,1)} %gate.1) | copy-start | bytes 3538948
  3.1 16.7 %collective-permute-start.1 = (bf16[64,2176]{1,0:T(8,128)(2,1)S(1)}, bf16[64,2176]{1,0:T(8,128)(2,1)S(1)}, u32[]{:S(2)}, u32[]{:S(2)}) collective-permute-start(bf16[64,2176]{1,0:T(8,128)(2,1)S(1)} %get-tuple-element.50.part), channel_id=1, source_target_pairs={{0,16},{2,18},{4,20},{6,22},{8,24},{10,26},{12,28},{14,30},{16,0},... | collective-permute-start | bytes 835592 | tf_op jit(solution)/shard_map/ppermute | solution.py:71
  7.2 19.3 %collective-permute-start.5 = (bf16[64,2176]{1,0:T(8,128)(2,1)S(1)}, bf16[64,2176]{1,0:T(8,128)(2,1)S(1)}, u32[]{:S(2)}, u32[]{:S(2)}) collective-permute-start(bf16[64,2176]{1,0:T(8,128)(2,1)S(1)} %get-tuple-element.50.part), channel_id=1, source_target_pairs={{0,4},{2,6},{4,0},{6,2},{8,12},{10,14},{12,8},{14,10},{16,20},{18,... | collective-permute-start | bytes 835592 | tf_op jit(solution)/shard_map/ppermute | solution.py:66
  19.9 7.9 %collective-permute-start.3 = (bf16[1,64,2176]{2,1,0:T(8,128)(2,1)S(1)}, bf16[1,64,2176]{2,1,0:T(8,128)(2,1)S(1)}, u32[]{:S(2)}, u32[]{:S(2)}) collective-permute-start(bf16[1,64,2176]{2,1,0:T(8,128)(2,1)S(1)} %get-tuple-element.51.lines._), channel_id=1, source_target_pairs={{0,1},{1,0},{2,3},{3,2},{4,5},{5,4},{6,7},{7,6},{8,9},{9,8},{10,11... | collective-permute-start | bytes 835592 | tf_op jit(solution)/shard_map/ppermute | solution.py:66
  21.5 7.3 %collective-permute-start.6 = (bf16[1,64,2176]{2,1,0:T(8,128)(2,1)S(1)}, bf16[1,64,2176]{2,1,0:T(8,128)(2,1)S(1)}, u32[]{:S(2)}, u32[]{:S(2)}) collective-permute-start(bf16[1,64,2176]{2,1,0:T(8,128)(2,1)S(1)} %get-tuple-element.51.lines._), channel_id=1, source_target_pairs={{0,4},{2,6},{4,0},{6,2},{8,12},{10,14},{12,8},{14,10},{16,20},{18,... | collective-permute-start | bytes 835592 | tf_op jit(solution)/shard_map/ppermute | solution.py:66
  23.0 10.6 %collective-permute-start.12 = (bf16[64,2176]{1,0:T(8,128)(2,1)S(1)}, bf16[64,2176]{1,0:T(8,128)(2,1)S(1)}, u32[]{:S(2)}, u32[]{:S(2)}) collective-permute-start(bf16[64,2176]{1,0:T(8,128)(2,1)S(1)} %get-tuple-element.60), channel_id=1, source_target_pairs={{0,24},{2,26},{4,28},{6,30},{8,0},{10,2},{12,4},{14,6},{16,8},{18,... | collective-permute-start | bytes 835592 | tf_op jit(solution)/shard_map/ppermute | solution.py:71
  26.5 12.2 %collective-permute-start.13 = (bf16[64,2176]{1,0:T(8,128)(2,1)S(1)}, bf16[64,2176]{1,0:T(8,128)(2,1)S(1)}, u32[]{:S(2)}, u32[]{:S(2)}) collective-permute-start(bf16[64,2176]{1,0:T(8,128)(2,1)S(1)} %get-tuple-element.60), channel_id=1, source_target_pairs={{0,8},{2,10},{4,12},{6,14},{8,16},{10,18},{12,20},{14,22},{16,24},... | collective-permute-start | bytes 835592 | tf_op jit(solution)/shard_map/ppermute | solution.py:71
  29.4 9.9 %collective-permute-start.8 = (bf16[2,64,1024]{2,1,0:T(8,128)(2,1)S(1)}, bf16[2,64,1024]{2,1,0:T(8,128)(2,1)S(1)}, u32[]{:S(2)}, u32[]{:S(2)}) collective-permute-start(bf16[2,64,1024]{2,1,0:T(8,128)(2,1)S(1)} %get-tuple-element.53.refs_0_), channel_id=1, source_target_pairs={{0,1},{1,0},{2,3},{3,2},{4,5},{5,4},{6,7},{7,6},{8,9},{9,8},{10,11... | collective-permute-start | bytes 786440 | tf_op jit(solution)/shard_map/ppermute | solution.py:66
  30.3 9.6 %collective-permute-start.9 = (bf16[2,64,1024]{2,1,0:T(8,128)(2,1)S(1)}, bf16[2,64,1024]{2,1,0:T(8,128)(2,1)S(1)}, u32[]{:S(2)}, u32[]{:S(2)}) collective-permute-start(bf16[2,64,1024]{2,1,0:T(8,128)(2,1)S(1)} %get-tuple-element.54), channel_id=1, source_target_pairs={{0,4},{2,6},{4,0},{6,2},{8,12},{10,14},{12,8},{14,10},{16,20},{18,... | collective-permute-start | bytes 786440 | tf_op jit(solution)/shard_map/ppermute | solution.py:66
  31.5 8.4 %collective-permute-start.11 = (bf16[64,128]{1,0:T(8,128)(2,1)S(1)}, bf16[64,128]{1,0:T(8,128)(2,1)S(1)}, u32[]{:S(2)}, u32[]{:S(2)}) collective-permute-start(bf16[64,128]{1,0:T(8,128)(2,1)S(1)} %get-tuple-element.55.own), channel_id=1, source_target_pairs={{0,2},{2,0},{4,6},{6,4},{8,10},{10,8},{12,14},{14,12},{16,18},{18,... | collective-permute-start | bytes 49160 | tf_op jit(solution)/shard_map/ppermute | solution.py:66
  31.5 1.3 %copy-start.6 = (bf16[2,384,768]{2,1,0:T(8,128)(2,1)S(1)}, bf16[2,384,768]{2,1,0:T(8,128)(2,1)}, u32[]{:S(2)}) copy-start(bf16[2,384,768]{2,1,0:T(8,128)(2,1)} %up.1) | copy-start | bytes 3538948
  33.6 6.9 %collective-permute-start.2 = (bf16[1,64,2176]{2,1,0:T(8,128)(2,1)S(1)}, bf16[1,64,2176]{2,1,0:T(8,128)(2,1)S(1)}, u32[]{:S(2)}, u32[]{:S(2)}) collective-permute-start(bf16[1,64,2176]{2,1,0:T(8,128)(2,1)S(1)} %get-tuple-element.51.lines._), channel_id=1, source_target_pairs={{0,2},{2,0},{4,6},{6,4},{8,10},{10,8},{12,14},{14,12},{16,18},{18,... | collective-permute-start | bytes 835592 | tf_op jit(solution)/shard_map/ppermute | solution.py:66
  38.8 13.4 %collective-permute-start.14 = (bf16[2,64,2176]{2,1,0:T(8,128)(2,1)S(1)}, bf16[2,64,2176]{2,1,0:T(8,128)(2,1)S(1)}, u32[]{:S(2)}, u32[]{:S(2)}) collective-permute-start(bf16[2,64,2176]{2,1,0:T(8,128)(2,1)S(1)} %stack.21._.lines), channel_id=1, source_target_pairs={{0,4},{2,6},{4,0},{6,2},{8,12},{10,14},{12,8},{14,10},{16,20},{18,... | collective-permute-start | bytes 1671176 | tf_op jit(solution)/shard_map/ppermute | solution.py:66
  39.4 13.1 %collective-permute-start.15 = (bf16[2,64,2176]{2,1,0:T(8,128)(2,1)S(1)}, bf16[2,64,2176]{2,1,0:T(8,128)(2,1)S(1)}, u32[]{:S(2)}, u32[]{:S(2)}) collective-permute-start(bf16[2,64,2176]{2,1,0:T(8,128)(2,1)S(1)} %stack.21._.lines), channel_id=1, source_target_pairs={{0,1},{1,0},{2,3},{3,2},{4,5},{5,4},{6,7},{7,6},{8,9},{9,8},{10,11... | collective-permute-start | bytes 1671176 | tf_op jit(solution)/shard_map/ppermute | solution.py:66
  39.9 2.0 %collective-permute-start.7 = (bf16[2,64,2176]{2,1,0:T(8,128)(2,1)S(1)}, bf16[2,64,2176]{2,1,0:T(8,128)(2,1)S(1)}, u32[]{:S(2)}, u32[]{:S(2)}) collective-permute-start(bf16[2,64,2176]{2,1,0:T(8,128)(2,1)S(1)} %get-tuple-element.52.over), channel_id=1, source_target_pairs={{0,2},{2,0},{4,6},{6,4},{8,10},{10,8},{12,14},{14,12},{16,18},{18,... | collective-permute-start | bytes 1671176 | tf_op jit(solution)/shard_map/ppermute | solution.py:66
  39.9 3.9 %copy-start.2 = (bf16[2,384,2048]{2,1,0:T(8,128)(2,1)S(1)}, bf16[2,384,2048]{2,1,0:T(8,128)(2,1)}, u32[]{:S(2)}) copy-start(bf16[2,384,2048]{2,1,0:T(8,128)(2,1)} %w_down.3) | copy-start | bytes 9437188
  40.0 3.1 %collective-permute-start = (bf16[128,2048]{1,0:T(8,128)(2,1)S(1)}, bf16[128,2048]{1,0:T(8,128)(2,1)S(1)}, u32[]{:S(2)}, u32[]{:S(2)}) collective-permute-start(bf16[128,2048]{1,0:T(8,128)(2,1)S(1)} %copy-done.4), channel_id=1, source_target_pairs={{0,2},{2,0},{4,6},{6,4},{8,10},{10,8},{12,14},{14,12},{16,18},{18,... | collective-permute-start | bytes 1572872 | tf_op jit(solution)/shard_map/ppermute | solution.py:66
  40.5 3.2 %collective-permute-start.10 = (bf16[2,64,2048]{2,1,0:T(8,128)(2,1)S(1)}, bf16[2,64,2048]{2,1,0:T(8,128)(2,1)S(1)}, u32[]{:S(2)}, u32[]{:S(2)}) collective-permute-start(bf16[2,64,2048]{2,1,0:T(8,128)(2,1)S(1)} %join.2.diag), channel_id=1, source_target_pairs={{0,2},{2,0},{4,6},{6,4},{8,10},{10,8},{12,14},{14,12},{16,18},{18,... | collective-permute-start | bytes 1572872 | tf_op jit(solution)/shard_map/ppermute | solution.py:66
  41.9 1.9 %collective-permute-start.4 = (bf16[1,64,2176]{2,1,0:T(8,128)(2,1)S(1)}, bf16[1,64,2176]{2,1,0:T(8,128)(2,1)S(1)}, u32[]{:S(2)}, u32[]{:S(2)}) collective-permute-start(bf16[1,64,2176]{2,1,0:T(8,128)(2,1)S(1)} %collective-permute-done.3.side), channel_id=1, source_target_pairs={{0,2},{2,0},{4,6},{6,4},{8,10},{10,8},{12,14},{14,12},{16,18},{18,... | collective-permute-start | bytes 835592 | tf_op jit(solution)/shard_map/ppermute | solution.py:66
  43.8 11.4 %copy-start = (bf16[2,384,2048]{2,1,0:T(8,128)(2,1)S(1)}, bf16[2,384,2048]{2,1,0:T(8,128)(2,1)}, u32[]{:S(2)}) copy-start(bf16[2,384,2048]{2,1,0:T(8,128)(2,1)} %w_gate.7) | copy-start | bytes 9437188
  43.8 11.4 %copy-start.1 = (bf16[2,384,2048]{2,1,0:T(8,128)(2,1)S(1)}, bf16[2,384,2048]{2,1,0:T(8,128)(2,1)}, u32[]{:S(2)}) copy-start(bf16[2,384,2048]{2,1,0:T(8,128)(2,1)} %w_up.7) | copy-start | bytes 9437188
  52.5 7.2 %collective-permute-start.17 = (bf16[2,64,1024]{2,1,0:T(8,128)(2,1)S(1)}, bf16[2,64,1024]{2,1,0:T(8,128)(2,1)S(1)}, u32[]{:S(2)}, u32[]{:S(2)}) collective-permute-start(bf16[2,64,1024]{2,1,0:T(8,128)(2,1)S(1)} %get-tuple-element.62._), channel_id=1, source_target_pairs={{0,1},{1,0},{2,3},{3,2},{4,5},{5,4},{6,7},{7,6},{8,9},{9,8},{10,11... | collective-permute-start | bytes 786440 | tf_op jit(solution)/shard_map/ppermute | solution.py:66
  53.1 7.1 %collective-permute-start.18 = (bf16[2,64,1024]{2,1,0:T(8,128)(2,1)S(1)}, bf16[2,64,1024]{2,1,0:T(8,128)(2,1)S(1)}, u32[]{:S(2)}, u32[]{:S(2)}) collective-permute-start(bf16[2,64,1024]{2,1,0:T(8,128)(2,1)S(1)} %get-tuple-element.65), channel_id=1, source_target_pairs={{0,4},{2,6},{4,0},{6,2},{8,12},{10,14},{12,8},{14,10},{16,20},{18,... | collective-permute-start | bytes 786440 | tf_op jit(solution)/shard_map/ppermute | solution.py:66
  54.6 11.0 %collective-permute-start.25 = (bf16[2,64,2176]{2,1,0:T(8,128)(2,1)S(1)}, bf16[2,64,2176]{2,1,0:T(8,128)(2,1)S(1)}, u32[]{:S(2)}, u32[]{:S(2)}) collective-permute-start(bf16[2,64,2176]{2,1,0:T(8,128)(2,1)S(1)} %stack.21._.lines), channel_id=1, source_target_pairs={{0,2},{2,0},{4,6},{6,4},{8,10},{10,8},{12,14},{14,12},{16,18},{18,... | collective-permute-start | bytes 1671176 | tf_op jit(solution)/shard_map/ppermute | solution.py:66
  54.6 12.7 %collective-permute-start.26 = (bf16[2,64,2176]{2,1,0:T(8,128)(2,1)S(1)}, bf16[2,64,2176]{2,1,0:T(8,128)(2,1)S(1)}, u32[]{:S(2)}, u32[]{:S(2)}) collective-permute-start(bf16[2,64,2176]{2,1,0:T(8,128)(2,1)S(1)} %collective-permute-done.15.side), channel_id=1, source_target_pairs={{0,2},{2,0},{4,6},{6,4},{8,10},{10,8},{12,14},{14,12},{16,18},{18,... | collective-permute-start | bytes 1671176 | tf_op jit(solution)/shard_map/ppermute | solution.py:66
  55.1 11.1 %collective-permute-start.27 = (bf16[2,64,2176]{2,1,0:T(8,128)(2,1)S(1)}, bf16[2,64,2176]{2,1,0:T(8,128)(2,1)S(1)}, u32[]{:S(2)}, u32[]{:S(2)}) collective-permute-start(bf16[2,64,2176]{2,1,0:T(8,128)(2,1)S(1)} %collective-permute-done.14.over), channel_id=1, source_target_pairs={{0,2},{2,0},{4,6},{6,4},{8,10},{10,8},{12,14},{14,12},{16,18},{18,... | collective-permute-start | bytes 1671176 | tf_op jit(solution)/shard_map/ppermute | solution.py:66
  59.7 2.9 %collective-permute-start.16 = (bf16[4,128,1024]{2,1,0:T(8,128)(2,1)S(1)}, bf16[4,128,1024]{2,1,0:T(8,128)(2,1)S(1)}, u32[]{:S(2)}, u32[]{:S(2)}) collective-permute-start(bf16[4,128,1024]{2,1,0:T(8,128)(2,1)S(1)} %get-tuple-element.64._), channel_id=1, source_target_pairs={{0,2},{2,0},{4,6},{6,4},{8,10},{10,8},{12,14},{14,12},{16,18},{18,... | collective-permute-start | bytes 3145736 | tf_op jit(solution)/shard_map/ppermute | solution.py:66
  60.2 3.8 %collective-permute-start.20 = (bf16[4,128,1024]{2,1,0:T(8,128)(2,1)S(1)}, bf16[4,128,1024]{2,1,0:T(8,128)(2,1)S(1)}, u32[]{:S(2)}, u32[]{:S(2)}) collective-permute-start(bf16[4,128,1024]{2,1,0:T(8,128)(2,1)S(1)} %get-tuple-element.66.refs_0_), channel_id=1, source_target_pairs={{0,2},{2,0},{4,6},{6,4},{8,10},{10,8},{12,14},{14,12},{16,18},{18,... | collective-permute-start | bytes 3145736 | tf_op jit(solution)/shard_map/ppermute | solution.py:66
  62.5 4.8 %collective-permute-start.28 = (bf16[2,64,2048]{2,1,0:T(8,128)(2,1)S(1)}, bf16[2,64,2048]{2,1,0:T(8,128)(2,1)S(1)}, u32[]{:S(2)}, u32[]{:S(2)}) collective-permute-start(bf16[2,64,2048]{2,1,0:T(8,128)(2,1)S(1)} %join.3._.diag), channel_id=1, source_target_pairs={{0,2},{2,0},{4,6},{6,4},{8,10},{10,8},{12,14},{14,12},{16,18},{18,... | collective-permute-start | bytes 1572872 | tf_op jit(solution)/shard_map/ppermute | solution.py:66
  64.0 14.2 %collective-permute-start.19 = (bf16[4,64,1024]{2,1,0:T(8,128)(2,1)S(1)}, bf16[4,64,1024]{2,1,0:T(8,128)(2,1)S(1)}, u32[]{:S(2)}, u32[]{:S(2)}) collective-permute-start(bf16[4,64,1024]{2,1,0:T(8,128)(2,1)S(1)} %get-tuple-element.68._), channel_id=1, source_target_pairs={{0,1},{1,0},{2,3},{3,2},{4,5},{5,4},{6,7},{7,6},{8,9},{9,8},{10,11... | collective-permute-start | bytes 1572872 | tf_op jit(solution)/shard_map/ppermute | solution.py:66
  65.6 14.0 %collective-permute-start.21 = (bf16[2,128,1024]{2,1,0:T(8,128)(2,1)S(1)}, bf16[2,128,1024]{2,1,0:T(8,128)(2,1)S(1)}, u32[]{:S(2)}, u32[]{:S(2)}) collective-permute-start(bf16[2,128,1024]{2,1,0:T(8,128)(2,1)S(1)} %get-tuple-element.71._), channel_id=1, source_target_pairs={{0,4},{2,6},{4,0},{6,2},{8,12},{10,14},{12,8},{14,10},{16,20},{18,... | collective-permute-start | bytes 1572872 | tf_op jit(solution)/shard_map/ppermute | solution.py:66
  73.7 7.1 %collective-permute-start.29 = (bf16[4,128,1024]{2,1,0:T(8,128)(2,1)S(1)}, bf16[4,128,1024]{2,1,0:T(8,128)(2,1)S(1)}, u32[]{:S(2)}, u32[]{:S(2)}) collective-permute-start(bf16[4,128,1024]{2,1,0:T(8,128)(2,1)S(1)} %get-tuple-element.82._), channel_id=1, source_target_pairs={{0,2},{2,0},{4,6},{6,4},{8,10},{10,8},{12,14},{14,12},{16,18},{18,... | collective-permute-start | bytes 3145736 | tf_op jit(solution)/shard_map/ppermute | solution.py:66
  76.1 6.4 %collective-permute-start.31 = (bf16[4,128,1024]{2,1,0:T(8,128)(2,1)S(1)}, bf16[4,128,1024]{2,1,0:T(8,128)(2,1)S(1)}, u32[]{:S(2)}, u32[]{:S(2)}) collective-permute-start(bf16[4,128,1024]{2,1,0:T(8,128)(2,1)S(1)} %get-tuple-element.86), channel_id=1, source_target_pairs={{0,2},{2,0},{4,6},{6,4},{8,10},{10,8},{12,14},{14,12},{16,18},{18,... | collective-permute-start | bytes 3145736 | tf_op jit(solution)/shard_map/ppermute | solution.py:66
  79.7 9.3 %collective-permute-start.22 = (bf16[2,64,1024]{2,1,0:T(8,128)(2,1)S(1)}, bf16[2,64,1024]{2,1,0:T(8,128)(2,1)S(1)}, u32[]{:S(2)}, u32[]{:S(2)}) collective-permute-start(bf16[2,64,1024]{2,1,0:T(8,128)(2,1)S(1)} %get-tuple-element.73._), channel_id=1, source_target_pairs={{0,4},{2,6},{4,0},{6,2},{8,12},{10,14},{12,8},{14,10},{16,20},{18,... | collective-permute-start | bytes 786440 | tf_op jit(solution)/shard_map/ppermute | solution.py:66
  80.3 9.2 %collective-permute-start.23 = (bf16[2,64,1024]{2,1,0:T(8,128)(2,1)S(1)}, bf16[2,64,1024]{2,1,0:T(8,128)(2,1)S(1)}, u32[]{:S(2)}, u32[]{:S(2)}) collective-permute-start(bf16[2,64,1024]{2,1,0:T(8,128)(2,1)S(1)} %get-tuple-element.75), channel_id=1, source_target_pairs={{0,1},{1,0},{2,3},{3,2},{4,5},{5,4},{6,7},{7,6},{8,9},{9,8},{10,11... | collective-permute-start | bytes 786440 | tf_op jit(solution)/shard_map/ppermute | solution.py:66
  81.0 17.7 %collective-permute-start.30 = (bf16[4,64,1024]{2,1,0:T(8,128)(2,1)S(1)}, bf16[4,64,1024]{2,1,0:T(8,128)(2,1)S(1)}, u32[]{:S(2)}, u32[]{:S(2)}) collective-permute-start(bf16[4,64,1024]{2,1,0:T(8,128)(2,1)S(1)} %get-tuple-element.84._), channel_id=1, source_target_pairs={{0,1},{1,0},{2,3},{3,2},{4,5},{5,4},{6,7},{7,6},{8,9},{9,8},{10,11... | collective-permute-start | bytes 1572872 | tf_op jit(solution)/shard_map/ppermute | solution.py:66
  82.6 16.1 %collective-permute-start.32 = (bf16[2,128,1024]{2,1,0:T(8,128)(2,1)S(1)}, bf16[2,128,1024]{2,1,0:T(8,128)(2,1)S(1)}, u32[]{:S(2)}, u32[]{:S(2)}) collective-permute-start(bf16[2,128,1024]{2,1,0:T(8,128)(2,1)S(1)} %get-tuple-element.88), channel_id=1, source_target_pairs={{0,4},{2,6},{4,0},{6,2},{8,12},{10,14},{12,8},{14,10},{16,20},{18,... | collective-permute-start | bytes 1572872 | tf_op jit(solution)/shard_map/ppermute | solution.py:66
  89.6 11.3 %collective-permute-start.24 = (bf16[64,2048]{1,0:T(8,128)(2,1)S(1)}, bf16[64,2048]{1,0:T(8,128)(2,1)S(1)}, u32[]{:S(2)}, u32[]{:S(2)}) collective-permute-start(bf16[64,2048]{1,0:T(8,128)(2,1)S(1)} %get-tuple-element.77), channel_id=1, source_target_pairs={{0,16},{2,18},{4,20},{6,22},{8,24},{10,26},{12,28},{14,30},{16,0},... | collective-permute-start | bytes 786440 | tf_op jit(solution)/shard_map/ppermute | solution.py:71
  98.8 6.4 %collective-permute-start.33 = (bf16[2,64,1024]{2,1,0:T(8,128)(2,1)S(1)}, bf16[2,64,1024]{2,1,0:T(8,128)(2,1)S(1)}, u32[]{:S(2)}, u32[]{:S(2)}) collective-permute-start(bf16[2,64,1024]{2,1,0:T(8,128)(2,1)S(1)} %get-tuple-element.90), channel_id=1, source_target_pairs={{0,4},{2,6},{4,0},{6,2},{8,12},{10,14},{12,8},{14,10},{16,20},{18,... | collective-permute-start | bytes 786440 | tf_op jit(solution)/shard_map/ppermute | solution.py:66
  100.4 6.4 %collective-permute-start.34 = (bf16[2,64,1024]{2,1,0:T(8,128)(2,1)S(1)}, bf16[2,64,1024]{2,1,0:T(8,128)(2,1)S(1)}, u32[]{:S(2)}, u32[]{:S(2)}) collective-permute-start(bf16[2,64,1024]{2,1,0:T(8,128)(2,1)S(1)} %get-tuple-element.92), channel_id=1, source_target_pairs={{0,1},{1,0},{2,3},{3,2},{4,5},{5,4},{6,7},{7,6},{8,9},{9,8},{10,11... | collective-permute-start | bytes 786440 | tf_op jit(solution)/shard_map/ppermute | solution.py:66
  106.9 10.0 %collective-permute-start.35 = (bf16[64,2048]{1,0:T(8,128)(2,1)S(1)}, bf16[64,2048]{1,0:T(8,128)(2,1)S(1)}, u32[]{:S(2)}, u32[]{:S(2)}) collective-permute-start(bf16[64,2048]{1,0:T(8,128)(2,1)S(1)} %get-tuple-element.93), channel_id=1, source_target_pairs={{0,8},{2,10},{4,12},{6,14},{8,16},{10,18},{12,20},{14,22},{16,24},... | collective-permute-start | bytes 786440 | tf_op jit(solution)/shard_map/ppermute | solution.py:71
  108.5 10.5 %collective-permute-start.36 = (bf16[64,2048]{1,0:T(8,128)(2,1)S(1)}, bf16[64,2048]{1,0:T(8,128)(2,1)S(1)}, u32[]{:S(2)}, u32[]{:S(2)}) collective-permute-start(bf16[64,2048]{1,0:T(8,128)(2,1)S(1)} %get-tuple-element.94), channel_id=1, source_target_pairs={{0,24},{2,26},{4,28},{6,30},{8,0},{10,2},{12,4},{14,6},{16,8},{18,... | collective-permute-start | bytes 786440 | tf_op jit(solution)/shard_map/ppermute | solution.py:71

commit v6 on v5

--- a/solution.py
+++ b/solution.py
@@ -57,7 +57,7 @@
     return lax.psum_scatter(combined, "tp", scatter_dimension=0, tiled=True)
 
 
-CHUNKS = ((0, 2), (1, 3))
+CHUNKS = ((0, 2), (3, 1))
 TILE = 512
 
 
@@ -128,34 +128,24 @@
             pltpu.VMEM(ids.shape, jnp.int32),
             pltpu.SemaphoreType.DMA((3,)),
         ],
-        limit=4,
-    )
-
-
-def stack_kernel(*refs):
-    lines = refs[-1]
-    for r in range(lines.shape[0]):
-        lines[r] = refs[r][...]
-
-
-def stack(pieces, *after):
-    return small(
-        stack_kernel,
-        "stack",
-        [(len(pieces),) + pieces[0].shape],
+        limit=60,
+    )
+
+
+def relay_kernel(*refs):
+    count = len(refs) // 2
+    for source, target in zip(refs[:count], refs[len(refs) - count:]):
+        target[...] = source[...]
+
+
+def relay(pieces, *after, work=0):
+    return small(
+        relay_kernel,
+        "relay",
+        [piece.shape for piece in pieces],
         "v" * len(pieces) + "o" * len(after),
         (*pieces, *after),
-    )[0]
-
-
-def relay_kernel(came, part, line, following):
-    line[0] = came[...]
-    following[...] = part[...]
-
-
-def relay(came, part):
-    return small(
-        relay_kernel, "relay", [(1,) + came.shape, part.shape], "vv", (came, part)
+        work=work,
     )
 
 
@@ -181,47 +171,27 @@
     )
 
 
-def corner_kernel(place, tokens, first, over, side, whole_over, left, right, sem):
-    _, piece, middle = left.shape
-    far = pl.multiple_of((1 - place[3]) * piece, piece)
-    copy = pltpu.make_async_copy(
-        tokens.at[pl.ds(far, piece), pl.ds(middle, middle)], right.at[0], sem.at[0]
-    )
-    copy.start()
-    whole_over[0] = first[...]
-    whole_over[1:] = over[...]
-    left[0] = first[:, :middle]
-    left[1:] = over[:, :, :middle]
-    right[1:] = side[:, :, middle:2 * middle]
-    copy.wait()
-
-
-def own_corner(place, cotangent, first, over, side):
-    count, piece, width = over.shape
-    middle = cotangent.shape[1] // 2
+def corner_kernel(place, tokens, *refs):
+    *sources, _, left, right = refs
+    count, piece, middle = left.shape
+    overs, sides = sources[:count], sources[count:]
+    for i, over in enumerate(overs):
+        left[i] = over[:, :middle]
+    if len(sides) < count:
+        far = pl.multiple_of((1 - place[3]) * piece, piece)
+        right[0] = tokens[pl.ds(far, piece), middle:]
+    for i, side in enumerate(sides):
+        right[count - len(sides) + i] = side[:, middle:2 * middle]
+
+
+def corner(place, cotangent, overs, sides, after):
+    dims = (len(overs), overs[0].shape[0], cotangent.shape[1] // 2)
     return small(
         corner_kernel,
-        "own_corner",
-        [(count + 1, piece, width)] + [(count + 1, piece, middle)] * 2,
-        "shvvv",
-        (place, cotangent, first, over, side),
-        (pltpu.SemaphoreType.DMA((1,)),),
-    )
-
-
-def plain_corner_kernel(over, side, _, left, right):
-    middle = left.shape[-1]
-    left[...] = over[:, :, :middle]
-    right[...] = side[:, :, middle:2 * middle]
-
-
-def corner(over, side, middle, after):
-    return small(
-        plain_corner_kernel,
         "corner",
-        [over.shape[:2] + (middle,)] * 2,
-        "vvo",
-        (over, side, after),
+        [dims] * 2,
+        "sv" + "v" * (len(overs) + len(sides)) + "o",
+        (place, cotangent, *overs, *sides, after),
     )
 
 
@@ -232,7 +202,7 @@
     result[:, :, middle:] = right[...]
 
 
-def join(left, right, *after):
+def join(left, right, *after, work=0):
     dims = left.shape
     return small(
         join_kernel,
@@ -240,18 +210,8 @@
         [dims[:-1] + (2 * dims[-1],)],
         "vv" + "o" * len(after),
         (left, right, *after),
-        work=1 << 36,
+        work=work,
     )[0]
-
-
-def tokens_of(own, lines, r, offsets):
-    if r == 0:
-        return own[...]
-    return lines[r_place(r, offsets)]
-
-
-def r_place(r, offsets):
-    return [offset for offset in offsets if offset != 0].index(r)
 
 
 def pair_base(place, line_count, r, ry, width):
@@ -260,22 +220,18 @@
     return pl.multiple_of((line * 2 + row) * width, width)
 
 
-def route_kernel(offsets, capacity, place, own, own_c, lines, lines_c, over, over_c, pick, pick_t, gate,
-                 hits, gates):
+def route_kernel(offsets, capacity, place, *refs):
+    nears, overs = refs[:2 * len(offsets)], refs[2 * len(offsets):4 * len(offsets)]
+    pick, pick_t, gate, hits, gates = refs[-5:]
     tokens = pick.shape[2] // 2
-    width = over.shape[2] - 128
     core, row, line, half = place[0], place[1], place[2], place[3]
     first = (line * 4 + row * 2 + core) * 2
     for i, r in enumerate(offsets):
         for ry in range(2):
             tables = []
             for c in range(2):
-                if ry == 1:
-                    table = (over, over_c)[c][i, :32, width:]
-                elif r == 0:
-                    table = (own, own_c)[c][:32]
-                else:
-                    table = (lines, lines_c)[c][r_place(r, offsets), :32, width:]
+                source = (nears, overs)[ry][2 * i + c]
+                table = source[:32, source.shape[1] - 128:]
                 tables.append(table.astype(jnp.float32))
             swapped = core > 0
             ordered = [
@@ -327,8 +283,8 @@
         pick_t[p] = square.T[:, :count].astype(jnp.bfloat16)
 
 
-def route(offsets, place, table, table_c, lines, lines_c, over, over_c, capacity):
-    tokens = 2 * over.shape[1]
+def route(offsets, place, nears, overs, capacity, *after):
+    tokens = 2 * overs[0].shape[0]
     pairs = 2 * len(offsets)
     rows = 4 * capacity
     return small(
@@ -339,16 +295,18 @@
             (pairs, 2 * tokens, rows),
             jax.ShapeDtypeStruct((pairs, rows, 128), jnp.float32),
         ],
-        "s" + "v" * 6,
-        (place, table, table_c, lines, lines_c, over, over_c),
+        "s" + "v" * (len(nears) + len(overs)) + "o" * len(after),
+        (place, *nears, *overs, *after),
         [pltpu.VMEM((4 * pairs, tokens), jnp.float32)] * 2,
     )
 
 
-def hidden_kernel(offsets, line_count, place, own, own_c, lines, lines_c, side, side_c, over, over_c,
-                  diag, diag_c, pick, gate, w_down, saved_gate, saved_up, _, grads, slots):
-    piece = over.shape[1]
-    width = diag.shape[2]
+def hidden_kernel(offsets, line_count, place, *refs):
+    *sources, pick, gate, w_down, saved_gate, saved_up, _, grads, slots = refs
+    nears, sides, overs, diag = (
+        sources[2 * at * len(offsets):2 * (at + 1) * len(offsets)] for at in range(4)
+    )
+    _, piece, width = diag[0].shape
     rows = pick.shape[1] // 2
     units = w_down.shape[1]
     near = pl.multiple_of(place[3] * piece, piece)
@@ -362,13 +320,12 @@
                 parts = []
                 for c in range(2):
                     if ry == 1:
-                        parts += [(over, over_c)[c][i, :, at], (diag, diag_c)[c][i, :, at]]
+                        parts += [overs[2 * i + c][:, at], diag[c][i, :, at]]
                     elif r == 0:
-                        group = (own, own_c)[c]
+                        group = nears[2 * i + c]
                         parts += [group[pl.ds(near, piece), at], group[pl.ds(far, piece), at]]
                     else:
-                        j = r_place(r, offsets)
-                        parts += [(lines, lines_c)[c][j, :, at], (side, side_c)[c][j, :, at]]
+                        parts += [nears[2 * i + c][:, at], sides[2 * i + c][:, at]]
                 p = i * 2 + ry
                 picked = jnp.dot(
                     pick[p], jnp.concatenate(parts, axis=0), preferred_element_type=jnp.float32
@@ -400,16 +357,15 @@
                 ).astype(jnp.bfloat16)
 
 
-def hidden(offsets, line_count, place, own, own_c, moved, pick, gate, w_down, saved, after):
-    width = own.shape[1]
-    units = w_down.shape[1]
+def hidden(offsets, line_count, place, sources, pick, gate, w_down, saved, after):
+    _, units, width = w_down.shape
     count = pick.shape[0] * pick.shape[1] // 2
     return small(
         functools.partial(hidden_kernel, offsets, line_count),
         "hidden",
         [(2, count, 2 * units)],
-        "s" + "v" * 15 + "o",
-        (place, own, own_c, *moved, pick, gate, w_down, *saved, after),
+        "s" + "v" * (len(sources) + 5) + "o",
+        (place, *sources, pick, gate, w_down, *saved, after),
         [pltpu.VMEM((2, count, width), jnp.bfloat16)],
         limit=12,
     )[0]
@@ -438,7 +394,7 @@
             send[p, :, at] = total[tokens:]
 
 
-def sums(offset, width, grads, w_gate, w_up, pick_t, after):
+def sums(offset, width, grads, w_gate, w_up, pick_t, after, work=0):
     pairs, tokens, _ = pick_t.shape
     _, count, units = grads.shape
     return small(
@@ -449,6 +405,7 @@
         (grads, w_gate, w_up, pick_t, after),
         [pltpu.VMEM((2, count, TILE), jnp.bfloat16)],
         limit=8,
+        work=work,
     )
 
 
@@ -549,48 +506,49 @@
     me, half = lax.axis_index("expert"), lax.axis_index("tp")
     place = jnp.stack([me % 2, me // 2 % 2, me // 4, half]).astype(jnp.int32)
 
+    def both_cores(arrays):
+        return [each for array in arrays for each in (array, swap(array, "expert", 1))]
+
+    def sums_by_token(offset, grads, pick_t, after, work=0):
+        keep, send = sums(offset, middle, grads, w_gate, w_up, pick_t, after, work)
+        return [keep, swap(send, "expert", 1)], send
+
     part, table = prepare(place, cotangent, gates.T, expert_ids.T, piece)
     first = swap(part, "expert", 2)
-    own_c, table_c = swap(cotangent, "expert", 1), swap(table, "expert", 1)
-    gathered, saved = [], None
-
-    def compute(index, after):
-        offsets, moved = CHUNKS[index], gathered[index]
-        line, line_c, _, _, over, over_c = moved[:6]
-        pick, pick_t, gate = route(
-            offsets, place, table, table_c, line, line_c, over, over_c, capacity
-        )
-        grads = hidden(
-            offsets, lines, place, cotangent, own_c, moved, pick, gate, w_down, saved, after
-        )
-        return grads, pick_t
-
-    def spread(grads, pick_t, after):
-        keep_l, send_l = sums(0, middle, grads, w_gate, w_up, pick_t, after)
-        keep_r, send_r = sums(middle, middle, grads, w_gate, w_up, pick_t, send_l)
-        return keep_l, swap(send_l, "expert", 1), keep_r, swap(send_r, "expert", 1), send_r
-
-    for offsets in CHUNKS:
-        pieces = [along_line(part, -r) for r in offsets if r != 0]
-        if saved is None:
-            line, part = relay(pieces[0], part)
-            saved = turn(saved_gate, saved_up, line)
-        else:
-            line = stack(pieces, saved[0])
+    near, third, second = CHUNKS[0][1], *CHUNKS[1]
+    own, tables = both_cores([cotangent]), both_cores([table])
+
+    line, part = relay([along_line(part, -near), part])
+    side, over = swap(line, "tp", 1), swap(line, "expert", 2)
+    later = [along_line(part, -third), along_line(part, -second)]
+    saved = turn(saved_gate, saved_up, line)
+    left, right = corner(place, cotangent, [first, over], [side], line)
+    lines_0, sides_0, overs_0 = both_cores([line]), both_cores([side]), both_cores([first, over])
+    pick, pick_t, gate = route(
+        CHUNKS[0], place, tables + lines_0, overs_0, capacity, own[1], sides_0[1], saved[0]
+    )
+    left_came, right_came = swap(left, "tp", 1), swap(right, "expert", 2)
+    lines_1, sides_1, overs_1 = [], [], []
+    after = saved[0]
+    for piece_of in later:
+        line, = relay([piece_of], after)
+        after = line
+        lines_1.append(line)
         side, over = swap(line, "tp", 1), swap(line, "expert", 2)
-        if offsets[0] == 0:
-            over, left, right = own_corner(place, cotangent, first, over, side)
-            after = (left,)
-        else:
-            early = compute(0, line)
-            left, right = corner(over, side, middle, early[0])
-            early = spread(*early, left)
-            after = (early[-1],)
-        diag = join(swap(left, "tp", 1), swap(right, "expert", 2), *after)
-        moved = []
-        for array in (line, side, over, diag):
-            moved += [array, swap(array, "expert", 1)]
-        gathered.append(moved)
+        if not sides_1:
+            side, over = relay([side, over], work=1 << 30)
+        sides_1.append(side)
+        overs_1.append(over)
+    diag = both_cores([join(left_came, right_came, line)])
+    grads = hidden(
+        CHUNKS[0], lines, place, own + lines_0 + own + sides_0 + overs_0 + diag, pick, gate, w_down,
+        saved, overs_1[0],
+    )
+    early_l, after = sums_by_token(0, grads, pick_t, grads)
+    left, right = corner(place, cotangent, overs_1, sides_1, after)
+    early_r, after = sums_by_token(middle, grads, pick_t, left, 1 << 36)
+    lines_1, sides_1, overs_1 = both_cores(lines_1), both_cores(sides_1), both_cores(overs_1)
+    pick, pick_t, gate = route(CHUNKS[1], place, lines_1, overs_1, capacity)
 
     def first_step(keep_l, came_l, keep_r, came_r, after):
         send_l, keep_l = first_left(keep_l, came_l, after)
@@ -603,10 +561,16 @@
         rows = third_sum(offsets, left, came_l, right, came_r, send_l if came is None else came)
         return rows[0], [row if r == 0 else along_line(row, r) for r, row in zip(offsets, rows)], send_l
 
-    early = first_step(*early[:4], gathered[1][6])
-    late = spread(*compute(1, early[4]), early[4])
+    diag = join(swap(left, "tp", 1), swap(right, "expert", 2), after, work=8589934592)
+    diag = both_cores([diag])
+    early = first_step(*early_l, *early_r, diag[0])
+    grads = hidden(
+        CHUNKS[1], lines, place, lines_1 + sides_1 + overs_1 + diag, pick, gate, w_down, saved, early[4]
+    )
+    late_l, after = sums_by_token(0, grads, pick_t, grads)
+    late_r, _ = sums_by_token(middle, grads, pick_t, after)
     done, early, after = second_step(CHUNKS[0], early[:4], early[4], None)
-    late = first_step(*late[:4], after)
+    late = first_step(*late_l, *late_r, after)
     _, late, _ = second_step(CHUNKS[1], late[:4], done, early[-1])
     terms = early + late
     return pl.pallas_call(

time: 120 us -> 129 us (1.075)
  waiting for transfers between devices: 59 us -> 62.7 us
  Pallas kernels: 23.4 us -> 25.9 us
  starting transfers between devices: 33.4 us -> 35.9 us
    ppermute x6, waiting for transfers between devices: 24 us -> 28.8 us  [along_line(): lax.ppermute(value, 'expert', [(i, (i + 4 * shift) % count) for i in rang...]
    ppermute x31 -> x37, starting transfers between devices: 21.8 us -> 25 us  [swap(): return lax.ppermute(value, axis, [(i, i ^ step) for i in range(count)])]
    pallas_call x24 -> x26, Pallas kernels: 22.5 us -> 25 us  [small(): pl.pallas_call(kernel, out_shape=[out if hasattr(out, 'dtype') else jax.S...]
    ppermute x31 -> x37, waiting for transfers between devices: 35 us -> 33.9 us  [swap(): return lax.ppermute(value, axis, [(i, i ^ step) for i in range(count)])]
    unnamed x18 -> x20, local copies, waits for them, and re-layouts: 3.71 us -> 2.89 us
  transfers between devices with their start and end apart: 37 -> 43, of which waited for: 20 -> 19; matrix products, arithmetic and copies ran while one was open for 0% -> 0% of each run, Pallas kernels for 18% -> 18%
where the time goes in v6:
time: 129 us; the launch traced here: 128 us
  waiting for transfers between devices  62.7 us (49%)
  starting transfers between devices  35.9 us (28%)
  Pallas kernels  25.9 us (20%)
  local copies, waits for them, and re-layouts  2.89 us (2%)
    ppermute x37, waiting for transfers between devices, swap(): return lax.ppermute(value, axis, [(i, i ^ step) for i in range(count)])  33.9 us
    ppermute x6, waiting for transfers between devices, along_line(): lax.ppermute(value, 'expert', [(i, (i + 4 * shift) % count) for i in rang...  28.8 us
    pallas_call x26, Pallas kernels, small(): pl.pallas_call(kernel, out_shape=[out if hasattr(out, 'dtype') else jax.S...  25 us
    ppermute x37, starting transfers between devices, swap(): return lax.ppermute(value, axis, [(i, i ^ step) for i in range(count)])  25 us
    ppermute x6, starting transfers between devices, along_line(): lax.ppermute(value, 'expert', [(i, (i + 4 * shift) % count) for i in rang...  10.9 us
    unnamed x20, local copies, waits for them, and re-layouts  2.89 us
  transfers between devices with their start and end apart: 43, of which 19 were waited for; matrix products, arithmetic and copies ran while one was open for 0% of the time, Pallas kernels for 18%

profile of v6, /device:TPU:0, one launch (start us, length us, event | category | flops | bytes accessed | tf_op | source)
XLA Modules:
  0.0 128.4 jit_solution(1942868904197877323)
XLA Ops:
  0.0 0.6 pad_add_fusion.place
  0.6 2.4 %prepare.1 = (bf16[64,2176]{1,0:T(8,128)(2,1)}, bf16[64,128]{1,0:T(8,128)(2,1)}) custom-call(s32[4]{0:T(128)} %pad_add_fusion.place, bf16[128,2048]{1,0:T(8,128)(2,1)} %tokens.5, f32[8,128]{1,0:T(8,128)} %bitcast.6, s32[8,128]{1,0:T(8,128)} %bitcast.7), custom_call_target="tpu_custom_call" | custom-call | tf_op jit(solution)/shard_map/prepare/pallas_call | solution.py:76
  3.0 4.1 %collective-permute-start.1 = (bf16[64,2176]{1,0:T(8,128)(2,1)}, bf16[64,2176]{1,0:T(8,128)(2,1)S(1)}, u32[]{:S(2)}, u32[]{:S(2)}) collective-permute-start(bf16[64,2176]{1,0:T(8,128)(2,1)} %get-tuple-element.51.refs_1_), channel_id=1, source_target_pairs={{0,16},{2,18},{4,20},{6,22},{8,24},{10,26},{12,28},{14,30},{16,0},... | collective-permute-start | bytes 835592 | tf_op jit(solution)/shard_map/ppermute | solution.py:71
  7.1 1.5 %collective-permute-start.5 = (bf16[64,2176]{1,0:T(8,128)(2,1)}, bf16[64,2176]{1,0:T(8,128)(2,1)S(1)}, u32[]{:S(2)}, u32[]{:S(2)}) collective-permute-start(bf16[64,2176]{1,0:T(8,128)(2,1)} %get-tuple-element.51.refs_1_), channel_id=1, source_target_pairs={{0,4},{2,6},{4,0},{6,2},{8,12},{10,14},{12,8},{14,10},{16,20},{18,... | collective-permute-start | bytes 835592 | tf_op jit(solution)/shard_map/ppermute | solution.py:66
  8.6 11.3 %collective-permute-done.1.refs_0_ = bf16[64,2176]{1,0:T(8,128)(2,1)S(1)} collective-permute-done((bf16[64,2176]{1,0:T(8,128)(2,1)}, bf16[64,2176]{1,0:T(8,128)(2,1)S(1)}, u32[]{:S(2)}, u32[]{:S(2)}) %collective-permute-start.1) | collective-permute-done | bytes 278560 | tf_op jit(solution)/shard_map/ppermute | solution.py:71
  20.0 1.0 copy-done.6
  21.0 1.6 %collective-permute-start.3 = (bf16[64,2176]{1,0:T(8,128)(2,1)S(1)}, bf16[64,2176]{1,0:T(8,128)(2,1)S(1)}, u32[]{:S(2)}, u32[]{:S(2)}) collective-permute-start(bf16[64,2176]{1,0:T(8,128)(2,1)S(1)} %get-tuple-element.52.refs_3_._.refs_2_), channel_id=1, source_target_pairs={{0,1},{1,0},{2,3},{3,2},{4,5},{5,4},{6,7},{7,6},{8,9},{9,8},{10,11... | collective-permute-start | bytes 835592 | tf_op jit(solution)/shard_map/ppermute | solution.py:66
  22.6 1.5 %collective-permute-start.7 = (bf16[64,2176]{1,0:T(8,128)(2,1)S(1)}, bf16[64,2176]{1,0:T(8,128)(2,1)S(1)}, u32[]{:S(2)}, u32[]{:S(2)}) collective-permute-start(bf16[64,2176]{1,0:T(8,128)(2,1)S(1)} %get-tuple-element.52.refs_3_._.refs_2_), channel_id=1, source_target_pairs={{0,4},{2,6},{4,0},{6,2},{8,12},{10,14},{12,8},{14,10},{16,20},{18,... | collective-permute-start | bytes 835592 | tf_op jit(solution)/shard_map/ppermute | solution.py:66
  24.1 3.5 %collective-permute-start.11 = (bf16[64,2176]{1,0:T(8,128)(2,1)S(1)}, bf16[64,2176]{1,0:T(8,128)(2,1)S(1)}, u32[]{:S(2)}, u32[]{:S(2)}) collective-permute-start(bf16[64,2176]{1,0:T(8,128)(2,1)S(1)} %get-tuple-element.55), channel_id=1, source_target_pairs={{0,24},{2,26},{4,28},{6,30},{8,0},{10,2},{12,4},{14,6},{16,8},{18,... | collective-permute-start | bytes 835592 | tf_op jit(solution)/shard_map/ppermute | solution.py:71
  27.6 1.3 collective-permute-done.3.refs_2_.refs_6_
  28.9 1.0 collective-permute-done.7.refs_1_.refs_6_.refs_10_
  29.8 0.6 copy-done.7
  30.5 0.6 corner.2
  31.0 0.8 collective-permute-start.9
  31.9 1.3 collective-permute-start.10
  33.2 1.4 %collective-permute-done.11.refs_0_ = bf16[64,2176]{1,0:T(8,128)(2,1)S(1)} collective-permute-done((bf16[64,2176]{1,0:T(8,128)(2,1)S(1)}, bf16[64,2176]{1,0:T(8,128)(2,1)S(1)}, u32[]{:S(2)}, u32[]{:S(2)}) %collective-permute-start.11) | collective-permute-done | bytes 278560 | tf_op jit(solution)/shard_map/ppermute | solution.py:71
  34.6 6.3 %collective-permute-done.12.refs_0_ = bf16[64,2176]{1,0:T(8,128)(2,1)S(1)} collective-permute-done((bf16[64,2176]{1,0:T(8,128)(2,1)S(1)}, bf16[64,2176]{1,0:T(8,128)(2,1)S(1)}, u32[]{:S(2)}, u32[]{:S(2)}) %collective-permute-start.12) | collective-permute-done | bytes 278560 | tf_op jit(solution)/shard_map/ppermute | solution.py:71
  40.9 0.5 collective-permute-start.4
  41.5 1.3 copy-done.5
  42.7 0.7 turn.1
  43.6 0.5 collective-permute-start.13
  44.1 0.5 collective-permute-start.15
  44.6 0.5 collective-permute-start.16
  45.1 1.5 %collective-permute-start.18 = (bf16[64,2176]{1,0:T(8,128)(2,1)S(1)}, bf16[64,2176]{1,0:T(8,128)(2,1)S(1)}, u32[]{:S(2)}, u32[]{:S(2)}) collective-permute-start(bf16[64,2176]{1,0:T(8,128)(2,1)S(1)} %relay.6.refs_0_.refs_2_), channel_id=1, source_target_pairs={{0,4},{2,6},{4,0},{6,2},{8,12},{10,14},{12,8},{14,10},{16,20},{18,... | collective-permute-start | bytes 835592 | tf_op jit(solution)/shard_map/ppermute | solution.py:66
  46.6 1.5 %collective-permute-start.19 = (bf16[64,2176]{1,0:T(8,128)(2,1)S(1)}, bf16[64,2176]{1,0:T(8,128)(2,1)S(1)}, u32[]{:S(2)}, u32[]{:S(2)}) collective-permute-start(bf16[64,2176]{1,0:T(8,128)(2,1)S(1)} %relay.6.refs_0_.refs_2_), channel_id=1, source_target_pairs={{0,1},{1,0},{2,3},{3,2},{4,5},{5,4},{6,7},{7,6},{8,9},{9,8},{10,11... | collective-permute-start | bytes 835592 | tf_op jit(solution)/shard_map/ppermute | solution.py:66
  48.1 1.1 route.2
  49.3 4.3 %collective-permute-done.15.refs_0_ = bf16[64,2176]{1,0:T(8,128)(2,1)S(1)} collective-permute-done((bf16[64,2176]{1,0:T(8,128)(2,1)S(1)}, bf16[64,2176]{1,0:T(8,128)(2,1)S(1)}, u32[]{:S(2)}, u32[]{:S(2)}) %collective-permute-start.15) | collective-permute-done | bytes 278560 | tf_op jit(solution)/shard_map/ppermute | solution.py:66
  53.6 0.6 collective-permute-done.16.refs_1_
  54.2 4.4 %hidden.2.grads._ = bf16[2,384,768]{2,1,0:T(8,128)(2,1)S(1)} custom-call(s32[4]{0:T(128)S(1)} %copy-done.8, bf16[128,2048]{1,0:T(8,128)(2,1)S(1)} %copy-done.2, bf16[128,2048]{1,0:T(8,128)(2,1)S(1)} %collective-permute-done.refs_8_.refs_1_.refs_5_, bf16[64,2176]{1,0:T(8,128)(2,1)S(1)} %get-tuple-element.52.refs_3_._.refs_2_, ...), custom_call_target="tpu_custom_call" | custom-call | tf_op jit(solution)/shard_map/hidden/pallas_call | solution.py:76
  58.6 2.3 %sums.4 = (bf16[4,128,1024]{2,1,0:T(8,128)(2,1)S(1)}, bf16[4,128,1024]{2,1,0:T(8,128)(2,1)S(1)}) custom-call(bf16[2,384,768]{2,1,0:T(8,128)(2,1)S(1)} %hidden.2.grads._, bf16[2,384,2048]{2,1,0:T(8,128)(2,1)S(1)} %copy-done, bf16[2,384,2048]{2,1,0:T(8,128)(2,1)S(1)} %copy-done.1, bf16[4,256,192]{2,1,0:T(8,128)(2,1)S(1)} %get-tuple-element.62.pick_t, ...), custom_call_target="tpu_custom_call" | custom-call | tf_op jit(solution)/shard_map/sums/pallas_call | solution.py:76
  61.0 0.6 corner.3
  61.6 1.5 %collective-permute-start.20 = (bf16[2,64,1024]{2,1,0:T(8,128)(2,1)S(1)}, bf16[2,64,1024]{2,1,0:T(8,128)(2,1)S(1)}, u32[]{:S(2)}, u32[]{:S(2)}) collective-permute-start(bf16[2,64,1024]{2,1,0:T(8,128)(2,1)S(1)} %get-tuple-element.66._), channel_id=1, source_target_pairs={{0,1},{1,0},{2,3},{3,2},{4,5},{5,4},{6,7},{7,6},{8,9},{9,8},{10,11... | collective-permute-start | bytes 786440 | tf_op jit(solution)/shard_map/ppermute | solution.py:66
  63.1 0.5 collective-permute-start.21
  63.6 2.2 %sums.5 = (bf16[4,128,1024]{2,1,0:T(8,128)(2,1)S(1)}, bf16[4,128,1024]{2,1,0:T(8,128)(2,1)S(1)}) custom-call(bf16[2,384,768]{2,1,0:T(8,128)(2,1)S(1)} %hidden.2.grads._, bf16[2,384,2048]{2,1,0:T(8,128)(2,1)S(1)} %copy-done, bf16[2,384,2048]{2,1,0:T(8,128)(2,1)S(1)} %copy-done.1, bf16[4,256,192]{2,1,0:T(8,128)(2,1)S(1)} %get-tuple-element.62.pick_t, ...), custom_call_target="tpu_custom_call" | custom-call | flops 68719476736 | bytes 268435456 | tf_op jit(solution)/shard_map/sums/pallas_call | solution.py:76
  66.0 0.5 collective-permute-start.28
  66.5 3.9 %collective-permute-done.20.left = bf16[2,64,1024]{2,1,0:T(8,128)(2,1)S(1)} collective-permute-done((bf16[2,64,1024]{2,1,0:T(8,128)(2,1)S(1)}, bf16[2,64,1024]{2,1,0:T(8,128)(2,1)S(1)}, u32[]{:S(2)}, u32[]{:S(2)}) %collective-permute-start.20) | collective-permute-done | bytes 262176 | tf_op jit(solution)/shard_map/ppermute | solution.py:66
  70.3 1.2 collective-permute-done.21.right
  71.5 0.5 collective-permute-start.33
  72.4 0.8 collective-permute-start.22
  73.3 0.5 collective-permute-start.24
  73.8 0.5 collective-permute-start.31
  74.3 1.1 route.3
  75.5 0.3 collective-permute-done.31.refs_7_
  75.8 4.1 %hidden.3.grads._ = bf16[2,384,768]{2,1,0:T(8,128)(2,1)S(1)} custom-call(s32[4]{0:T(128)S(1)} %copy-done.8, bf16[64,2176]{1,0:T(8,128)(2,1)S(1)} %relay.5.refs_1_.refs_0_, bf16[64,2176]{1,0:T(8,128)(2,1)S(1)} %collective-permute-done.28.refs_1_, bf16[64,2176]{1,0:T(8,128)(2,1)S(1)} %relay.6.refs_0_.refs_2_, ...), custom_call_target="tpu_custom_call" | custom-call | tf_op jit(solution)/shard_map/hidden/pallas_call | solution.py:76
  79.9 2.2 %sums.6 = (bf16[4,128,1024]{2,1,0:T(8,128)(2,1)S(1)}, bf16[4,128,1024]{2,1,0:T(8,128)(2,1)S(1)}) custom-call(bf16[2,384,768]{2,1,0:T(8,128)(2,1)S(1)} %hidden.3.grads._, bf16[2,384,2048]{2,1,0:T(8,128)(2,1)S(1)} %copy-done, bf16[2,384,2048]{2,1,0:T(8,128)(2,1)S(1)} %copy-done.1, bf16[4,256,192]{2,1,0:T(8,128)(2,1)S(1)} %get-tuple-element.82.pick_t, ...), custom_call_target="tpu_custom_call" | custom-call | tf_op jit(solution)/shard_map/sums/pallas_call | solution.py:76
  82.4 2.2 %sums.7 = (bf16[4,128,1024]{2,1,0:T(8,128)(2,1)S(1)}, bf16[4,128,1024]{2,1,0:T(8,128)(2,1)S(1)}) custom-call(bf16[2,384,768]{2,1,0:T(8,128)(2,1)S(1)} %hidden.3.grads._, bf16[2,384,2048]{2,1,0:T(8,128)(2,1)S(1)} %copy-done, bf16[2,384,2048]{2,1,0:T(8,128)(2,1)S(1)} %copy-done.1, bf16[4,256,192]{2,1,0:T(8,128)(2,1)S(1)} %get-tuple-element.82.pick_t, ...), custom_call_target="tpu_custom_call" | custom-call | tf_op jit(solution)/shard_map/sums/pallas_call | solution.py:76
  84.6 0.4 collective-permute-start.37
  85.0 1.8 %collective-permute-done.22.came_l = bf16[4,64,1024]{2,1,0:T(8,128)(2,1)S(1)} collective-permute-done((bf16[4,64,1024]{2,1,0:T(8,128)(2,1)S(1)}, bf16[4,64,1024]{2,1,0:T(8,128)(2,1)S(1)}, u32[]{:S(2)}, u32[]{:S(2)}) %collective-permute-start.22) | collective-permute-done | bytes 524320 | tf_op jit(solution)/shard_map/ppermute | solution.py:66
  87.3 0.5 collective-permute-start.25
  87.8 1.5 %collective-permute-start.26 = (bf16[2,64,1024]{2,1,0:T(8,128)(2,1)S(1)}, bf16[2,64,1024]{2,1,0:T(8,128)(2,1)S(1)}, u32[]{:S(2)}, u32[]{:S(2)}) collective-permute-start(bf16[2,64,1024]{2,1,0:T(8,128)(2,1)S(1)} %get-tuple-element.77), channel_id=1, source_target_pairs={{0,1},{1,0},{2,3},{3,2},{4,5},{5,4},{6,7},{7,6},{8,9},{9,8},{10,11... | collective-permute-start | bytes 786440 | tf_op jit(solution)/shard_map/ppermute | solution.py:66
  89.4 0.6 collective-permute-start.36
  90.1 1.6 %collective-permute-start.38 = (bf16[2,128,1024]{2,1,0:T(8,128)(2,1)S(1)}, bf16[2,128,1024]{2,1,0:T(8,128)(2,1)S(1)}, u32[]{:S(2)}, u32[]{:S(2)}) collective-permute-start(bf16[2,128,1024]{2,1,0:T(8,128)(2,1)S(1)} %get-tuple-element.90), channel_id=1, source_target_pairs={{0,4},{2,6},{4,0},{6,2},{8,12},{10,14},{12,8},{14,10},{16,20},{18,... | collective-permute-start | bytes 1572872 | tf_op jit(solution)/shard_map/ppermute | solution.py:66
  91.7 4.8 %collective-permute-done.25.came_l = bf16[2,64,1024]{2,1,0:T(8,128)(2,1)S(1)} collective-permute-done((bf16[2,64,1024]{2,1,0:T(8,128)(2,1)S(1)}, bf16[2,64,1024]{2,1,0:T(8,128)(2,1)S(1)}, u32[]{:S(2)}, u32[]{:S(2)}) %collective-permute-start.25) | collective-permute-done | bytes 262176 | tf_op jit(solution)/shard_map/ppermute | solution.py:66
  96.6 0.5 collective-permute-done.26.came_r
  97.2 0.3 collective-permute-start.27
  97.5 9.0 %collective-permute-done.36.came_l = bf16[4,64,1024]{2,1,0:T(8,128)(2,1)S(1)} collective-permute-done((bf16[4,64,1024]{2,1,0:T(8,128)(2,1)S(1)}, bf16[4,64,1024]{2,1,0:T(8,128)(2,1)S(1)}, u32[]{:S(2)}, u32[]{:S(2)}) %collective-permute-start.36) | collective-permute-done | bytes 524320 | tf_op jit(solution)/shard_map/ppermute | solution.py:66
  106.6 1.6 %collective-permute-start.39 = (bf16[2,64,1024]{2,1,0:T(8,128)(2,1)S(1)}, bf16[2,64,1024]{2,1,0:T(8,128)(2,1)S(1)}, u32[]{:S(2)}, u32[]{:S(2)}) collective-permute-start(bf16[2,64,1024]{2,1,0:T(8,128)(2,1)S(1)} %get-tuple-element.92), channel_id=1, source_target_pairs={{0,4},{2,6},{4,0},{6,2},{8,12},{10,14},{12,8},{14,10},{16,20},{18,... | collective-permute-start | bytes 786440 | tf_op jit(solution)/shard_map/ppermute | solution.py:66
  108.1 1.4 %collective-permute-start.40 = (bf16[2,64,1024]{2,1,0:T(8,128)(2,1)S(1)}, bf16[2,64,1024]{2,1,0:T(8,128)(2,1)S(1)}, u32[]{:S(2)}, u32[]{:S(2)}) collective-permute-start(bf16[2,64,1024]{2,1,0:T(8,128)(2,1)S(1)} %get-tuple-element.94), channel_id=1, source_target_pairs={{0,1},{1,0},{2,3},{3,2},{4,5},{5,4},{6,7},{7,6},{8,9},{9,8},{10,11... | collective-permute-start | bytes 786440 | tf_op jit(solution)/shard_map/ppermute | solution.py:66
  109.6 3.6 %collective-permute-done.39.came_l = bf16[2,64,1024]{2,1,0:T(8,128)(2,1)S(1)} collective-permute-done((bf16[2,64,1024]{2,1,0:T(8,128)(2,1)S(1)}, bf16[2,64,1024]{2,1,0:T(8,128)(2,1)S(1)}, u32[]{:S(2)}, u32[]{:S(2)}) %collective-permute-start.39) | collective-permute-done | bytes 262176 | tf_op jit(solution)/shard_map/ppermute | solution.py:66
  113.1 1.4 %collective-permute-done.40.came_r = bf16[2,64,1024]{2,1,0:T(8,128)(2,1)S(1)} collective-permute-done((bf16[2,64,1024]{2,1,0:T(8,128)(2,1)S(1)}, bf16[2,64,1024]{2,1,0:T(8,128)(2,1)S(1)}, u32[]{:S(2)}, u32[]{:S(2)}) %collective-permute-start.40) | collective-permute-done | bytes 262176 | tf_op jit(solution)/shard_map/ppermute | solution.py:66
  114.6 3.0 %collective-permute-start.41 = (bf16[64,2048]{1,0:T(8,128)(2,1)S(1)}, bf16[64,2048]{1,0:T(8,128)(2,1)S(1)}, u32[]{:S(2)}, u32[]{:S(2)}) collective-permute-start(bf16[64,2048]{1,0:T(8,128)(2,1)S(1)} %get-tuple-element.95), channel_id=1, source_target_pairs={{0,24},{2,26},{4,28},{6,30},{8,0},{10,2},{12,4},{14,6},{16,8},{18,... | collective-permute-start | bytes 786440 | tf_op jit(solution)/shard_map/ppermute | solution.py:71
  117.7 5.8 %collective-permute-done.41.refs_2_ = bf16[64,2048]{1,0:T(8,128)(2,1)S(1)} collective-permute-done((bf16[64,2048]{1,0:T(8,128)(2,1)S(1)}, bf16[64,2048]{1,0:T(8,128)(2,1)S(1)}, u32[]{:S(2)}, u32[]{:S(2)}) %collective-permute-start.41) | collective-permute-done | bytes 262176 | tf_op jit(solution)/shard_map/ppermute | solution.py:71
  123.4 4.1 %collective-permute-done.42.refs_3_ = bf16[64,2048]{1,0:T(8,128)(2,1)S(1)} collective-permute-done((bf16[64,2048]{1,0:T(8,128)(2,1)S(1)}, bf16[64,2048]{1,0:T(8,128)(2,1)S(1)}, u32[]{:S(2)}, u32[]{:S(2)}) %collective-permute-start.42) | collective-permute-done | bytes 262176 | tf_op jit(solution)/shard_map/ppermute | solution.py:71
  127.5 0.9 last_sum.1
  (70 shorter events, 2.1 us)
Async XLA Ops:
  0.0 24.1 %copy-start.2 = (bf16[128,2048]{1,0:T(8,128)(2,1)S(1)}, bf16[128,2048]{1,0:T(8,128)(2,1)}, u32[]{:S(2)}) copy-start(bf16[128,2048]{1,0:T(8,128)(2,1)} %tokens.5) | copy-start | bytes 1572868
  3.0 38.5 %copy-start.4 = (bf16[2,384,768]{2,1,0:T(8,128)(2,1)S(1)}, bf16[2,384,768]{2,1,0:T(8,128)(2,1)}, u32[]{:S(2)}) copy-start(bf16[2,384,768]{2,1,0:T(8,128)(2,1)} %gate.1) | copy-start | bytes 3538948
  3.0 16.9 %collective-permute-start.1 = (bf16[64,2176]{1,0:T(8,128)(2,1)}, bf16[64,2176]{1,0:T(8,128)(2,1)S(1)}, u32[]{:S(2)}, u32[]{:S(2)}) collective-permute-start(bf16[64,2176]{1,0:T(8,128)(2,1)} %get-tuple-element.51.refs_1_), channel_id=1, source_target_pairs={{0,16},{2,18},{4,20},{6,22},{8,24},{10,26},{12,28},{14,30},{16,0},... | collective-permute-start | bytes 835592 | tf_op jit(solution)/shard_map/ppermute | solution.py:71
  7.1 20.5 %collective-permute-start.5 = (bf16[64,2176]{1,0:T(8,128)(2,1)}, bf16[64,2176]{1,0:T(8,128)(2,1)S(1)}, u32[]{:S(2)}, u32[]{:S(2)}) collective-permute-start(bf16[64,2176]{1,0:T(8,128)(2,1)} %get-tuple-element.51.refs_1_), channel_id=1, source_target_pairs={{0,4},{2,6},{4,0},{6,2},{8,12},{10,14},{12,8},{14,10},{16,20},{18,... | collective-permute-start | bytes 835592 | tf_op jit(solution)/shard_map/ppermute | solution.py:66
  20.0 1.0 copy-start.6
  21.0 7.9 %collective-permute-start.3 = (bf16[64,2176]{1,0:T(8,128)(2,1)S(1)}, bf16[64,2176]{1,0:T(8,128)(2,1)S(1)}, u32[]{:S(2)}, u32[]{:S(2)}) collective-permute-start(bf16[64,2176]{1,0:T(8,128)(2,1)S(1)} %get-tuple-element.52.refs_3_._.refs_2_), channel_id=1, source_target_pairs={{0,1},{1,0},{2,3},{3,2},{4,5},{5,4},{6,7},{7,6},{8,9},{9,8},{10,11... | collective-permute-start | bytes 835592 | tf_op jit(solution)/shard_map/ppermute | solution.py:66
  22.6 7.3 %collective-permute-start.7 = (bf16[64,2176]{1,0:T(8,128)(2,1)S(1)}, bf16[64,2176]{1,0:T(8,128)(2,1)S(1)}, u32[]{:S(2)}, u32[]{:S(2)}) collective-permute-start(bf16[64,2176]{1,0:T(8,128)(2,1)S(1)} %get-tuple-element.52.refs_3_._.refs_2_), channel_id=1, source_target_pairs={{0,4},{2,6},{4,0},{6,2},{8,12},{10,14},{12,8},{14,10},{16,20},{18,... | collective-permute-start | bytes 835592 | tf_op jit(solution)/shard_map/ppermute | solution.py:66
  24.1 19.5 %collective-permute-start = (bf16[128,2048]{1,0:T(8,128)(2,1)S(1)}, bf16[128,2048]{1,0:T(8,128)(2,1)S(1)}, u32[]{:S(2)}, u32[]{:S(2)}) collective-permute-start(bf16[128,2048]{1,0:T(8,128)(2,1)S(1)} %copy-done.2), channel_id=1, source_target_pairs={{0,2},{2,0},{4,6},{6,4},{8,10},{10,8},{12,14},{14,12},{16,18},{18,... | collective-permute-start | bytes 1572872 | tf_op jit(solution)/shard_map/ppermute | solution.py:66
  24.1 10.5 %collective-permute-start.11 = (bf16[64,2176]{1,0:T(8,128)(2,1)S(1)}, bf16[64,2176]{1,0:T(8,128)(2,1)S(1)}, u32[]{:S(2)}, u32[]{:S(2)}) collective-permute-start(bf16[64,2176]{1,0:T(8,128)(2,1)S(1)} %get-tuple-element.55), channel_id=1, source_target_pairs={{0,24},{2,26},{4,28},{6,30},{8,0},{10,2},{12,4},{14,6},{16,8},{18,... | collective-permute-start | bytes 835592 | tf_op jit(solution)/shard_map/ppermute | solution.py:71
  27.6 13.3 %collective-permute-start.12 = (bf16[64,2176]{1,0:T(8,128)(2,1)S(1)}, bf16[64,2176]{1,0:T(8,128)(2,1)S(1)}, u32[]{:S(2)}, u32[]{:S(2)}) collective-permute-start(bf16[64,2176]{1,0:T(8,128)(2,1)S(1)} %get-tuple-element.55), channel_id=1, source_target_pairs={{0,8},{2,10},{4,12},{6,14},{8,16},{10,18},{12,20},{14,22},{16,24},... | collective-permute-start | bytes 835592 | tf_op jit(solution)/shard_map/ppermute | solution.py:71
  28.9 3.0 %collective-permute-start.14 = (bf16[64,128]{1,0:T(8,128)(2,1)}, bf16[64,128]{1,0:T(8,128)(2,1)S(1)}, u32[]{:S(2)}, u32[]{:S(2)}) collective-permute-start(bf16[64,128]{1,0:T(8,128)(2,1)} %get-tuple-element.57.refs_0_), channel_id=1, source_target_pairs={{0,2},{2,0},{4,6},{6,4},{8,10},{10,8},{12,14},{14,12},{16,18},{18,... | collective-permute-start | bytes 49160 | tf_op jit(solution)/shard_map/ppermute | solution.py:66
  29.8 0.6 copy-start.7
  31.0 9.8 %collective-permute-start.9 = (bf16[2,64,1024]{2,1,0:T(8,128)(2,1)S(1)}, bf16[2,64,1024]{2,1,0:T(8,128)(2,1)S(1)}, u32[]{:S(2)}, u32[]{:S(2)}) collective-permute-start(bf16[2,64,1024]{2,1,0:T(8,128)(2,1)S(1)} %get-tuple-element.53), channel_id=1, source_target_pairs={{0,1},{1,0},{2,3},{3,2},{4,5},{5,4},{6,7},{7,6},{8,9},{9,8},{10,11... | collective-permute-start | bytes 786440 | tf_op jit(solution)/shard_map/ppermute | solution.py:66
  31.9 9.5 %collective-permute-start.10 = (bf16[2,64,1024]{2,1,0:T(8,128)(2,1)S(1)}, bf16[2,64,1024]{2,1,0:T(8,128)(2,1)S(1)}, u32[]{:S(2)}, u32[]{:S(2)}) collective-permute-start(bf16[2,64,1024]{2,1,0:T(8,128)(2,1)S(1)} %get-tuple-element.54), channel_id=1, source_target_pairs={{0,4},{2,6},{4,0},{6,2},{8,12},{10,14},{12,8},{14,10},{16,20},{18,... | collective-permute-start | bytes 786440 | tf_op jit(solution)/shard_map/ppermute | solution.py:66
  34.6 9.5 %collective-permute-start.2 = (bf16[64,2176]{1,0:T(8,128)(2,1)S(1)}, bf16[64,2176]{1,0:T(8,128)(2,1)S(1)}, u32[]{:S(2)}, u32[]{:S(2)}) collective-permute-start(bf16[64,2176]{1,0:T(8,128)(2,1)S(1)} %get-tuple-element.52.refs_3_._.refs_2_), channel_id=1, source_target_pairs={{0,2},{2,0},{4,6},{6,4},{8,10},{10,8},{12,14},{14,12},{16,18},{18,... | collective-permute-start | bytes 835592 | tf_op jit(solution)/shard_map/ppermute | solution.py:66
  40.9 3.7 %collective-permute-start.6 = (bf16[64,2176]{1,0:T(8,128)(2,1)S(1)}, bf16[64,2176]{1,0:T(8,128)(2,1)S(1)}, u32[]{:S(2)}, u32[]{:S(2)}) collective-permute-start(bf16[64,2176]{1,0:T(8,128)(2,1)S(1)} %collective-permute-done.5.refs_0_.refs_4_.refs_8_), channel_id=1, source_target_pairs={{0,2},{2,0},{4,6},{6,4},{8,10},{10,8},{12,14},{14,12},{16,18},{18,... | collective-permute-start | bytes 835592 | tf_op jit(solution)/shard_map/ppermute | solution.py:66
  40.9 4.2 %collective-permute-start.4 = (bf16[64,2176]{1,0:T(8,128)(2,1)S(1)}, bf16[64,2176]{1,0:T(8,128)(2,1)S(1)}, u32[]{:S(2)}, u32[]{:S(2)}) collective-permute-start(bf16[64,2176]{1,0:T(8,128)(2,1)S(1)} %collective-permute-done.3.refs_2_.refs_6_), channel_id=1, source_target_pairs={{0,2},{2,0},{4,6},{6,4},{8,10},{10,8},{12,14},{14,12},{16,18},{18,... | collective-permute-start | bytes 835592 | tf_op jit(solution)/shard_map/ppermute | solution.py:66
  41.4 5.2 %collective-permute-start.8 = (bf16[64,2176]{1,0:T(8,128)(2,1)S(1)}, bf16[64,2176]{1,0:T(8,128)(2,1)S(1)}, u32[]{:S(2)}, u32[]{:S(2)}) collective-permute-start(bf16[64,2176]{1,0:T(8,128)(2,1)S(1)} %collective-permute-done.7.refs_1_.refs_6_.refs_10_), channel_id=1, source_target_pairs={{0,2},{2,0},{4,6},{6,4},{8,10},{10,8},{12,14},{14,12},{16,18},{18,... | collective-permute-start | bytes 835592 | tf_op jit(solution)/shard_map/ppermute | solution.py:66
  41.5 1.3 copy-start.5
  43.4 4.7 %copy-start.8 = (s32[4]{0:T(128)S(1)}, s32[4]{0:T(128)}, u32[]{:S(2)}) copy-start(s32[4]{0:T(128)} %pad_add_fusion.place) | copy-start | bytes 52
  43.5 4.7 %copy-start.9 = (bf16[64,128]{1,0:T(8,128)(2,1)S(1)}, bf16[64,128]{1,0:T(8,128)(2,1)}, u32[]{:S(2)}) copy-start(bf16[64,128]{1,0:T(8,128)(2,1)} %get-tuple-element.57.refs_0_) | copy-start | bytes 49156
  43.6 10.6 %collective-permute-start.13 = (bf16[2,64,2048]{2,1,0:T(8,128)(2,1)S(1)}, bf16[2,64,2048]{2,1,0:T(8,128)(2,1)S(1)}, u32[]{:S(2)}, u32[]{:S(2)}) collective-permute-start(bf16[2,64,2048]{2,1,0:T(8,128)(2,1)S(1)} %join.2.refs_12_), channel_id=1, source_target_pairs={{0,2},{2,0},{4,6},{6,4},{8,10},{10,8},{12,14},{14,12},{16,18},{18,... | collective-permute-start | bytes 1572872 | tf_op jit(solution)/shard_map/ppermute | solution.py:66
  44.1 9.5 %collective-permute-start.15 = (bf16[64,2176]{1,0:T(8,128)(2,1)S(1)}, bf16[64,2176]{1,0:T(8,128)(2,1)S(1)}, u32[]{:S(2)}, u32[]{:S(2)}) collective-permute-start(bf16[64,2176]{1,0:T(8,128)(2,1)S(1)} %relay.5.refs_1_.refs_0_), channel_id=1, source_target_pairs={{0,1},{1,0},{2,3},{3,2},{4,5},{5,4},{6,7},{7,6},{8,9},{9,8},{10,11... | collective-permute-start | bytes 835592 | tf_op jit(solution)/shard_map/ppermute | solution.py:66
  44.6 9.6 %collective-permute-start.16 = (bf16[64,2176]{1,0:T(8,128)(2,1)S(1)}, bf16[64,2176]{1,0:T(8,128)(2,1)S(1)}, u32[]{:S(2)}, u32[]{:S(2)}) collective-permute-start(bf16[64,2176]{1,0:T(8,128)(2,1)S(1)} %relay.5.refs_1_.refs_0_), channel_id=1, source_target_pairs={{0,4},{2,6},{4,0},{6,2},{8,12},{10,14},{12,8},{14,10},{16,20},{18,... | collective-permute-start | bytes 835592 | tf_op jit(solution)/shard_map/ppermute | solution.py:66
  45.1 15.9 %collective-permute-start.18 = (bf16[64,2176]{1,0:T(8,128)(2,1)S(1)}, bf16[64,2176]{1,0:T(8,128)(2,1)S(1)}, u32[]{:S(2)}, u32[]{:S(2)}) collective-permute-start(bf16[64,2176]{1,0:T(8,128)(2,1)S(1)} %relay.6.refs_0_.refs_2_), channel_id=1, source_target_pairs={{0,4},{2,6},{4,0},{6,2},{8,12},{10,14},{12,8},{14,10},{16,20},{18,... | collective-permute-start | bytes 835592 | tf_op jit(solution)/shard_map/ppermute | solution.py:66
  46.6 14.4 %collective-permute-start.19 = (bf16[64,2176]{1,0:T(8,128)(2,1)S(1)}, bf16[64,2176]{1,0:T(8,128)(2,1)S(1)}, u32[]{:S(2)}, u32[]{:S(2)}) collective-permute-start(bf16[64,2176]{1,0:T(8,128)(2,1)S(1)} %relay.6.refs_0_.refs_2_), channel_id=1, source_target_pairs={{0,1},{1,0},{2,3},{3,2},{4,5},{5,4},{6,7},{7,6},{8,9},{9,8},{10,11... | collective-permute-start | bytes 835592 | tf_op jit(solution)/shard_map/ppermute | solution.py:66
  49.2 5.0 %copy-start.3 = (bf16[2,384,2048]{2,1,0:T(8,128)(2,1)S(1)}, bf16[2,384,2048]{2,1,0:T(8,128)(2,1)}, u32[]{:S(2)}) copy-start(bf16[2,384,2048]{2,1,0:T(8,128)(2,1)} %refs_16_.3) | copy-start | bytes 9437188
  54.2 4.4 %copy-start = (bf16[2,384,2048]{2,1,0:T(8,128)(2,1)S(1)}, bf16[2,384,2048]{2,1,0:T(8,128)(2,1)}, u32[]{:S(2)}) copy-start(bf16[2,384,2048]{2,1,0:T(8,128)(2,1)} %w_gate.7) | copy-start | bytes 9437188
  54.2 4.4 %copy-start.1 = (bf16[2,384,2048]{2,1,0:T(8,128)(2,1)S(1)}, bf16[2,384,2048]{2,1,0:T(8,128)(2,1)}, u32[]{:S(2)}) copy-start(bf16[2,384,2048]{2,1,0:T(8,128)(2,1)} %w_up.7) | copy-start | bytes 9437188
  60.9 10.6 %collective-permute-start.17 = (bf16[4,128,1024]{2,1,0:T(8,128)(2,1)S(1)}, bf16[4,128,1024]{2,1,0:T(8,128)(2,1)S(1)}, u32[]{:S(2)}, u32[]{:S(2)}) collective-permute-start(bf16[4,128,1024]{2,1,0:T(8,128)(2,1)S(1)} %get-tuple-element.64.refs_4_), channel_id=1, source_target_pairs={{0,2},{2,0},{4,6},{6,4},{8,10},{10,8},{12,14},{14,12},{16,18},{18,... | collective-permute-start | bytes 3145736 | tf_op jit(solution)/shard_map/ppermute | solution.py:66
  61.6 8.8 %collective-permute-start.20 = (bf16[2,64,1024]{2,1,0:T(8,128)(2,1)S(1)}, bf16[2,64,1024]{2,1,0:T(8,128)(2,1)S(1)}, u32[]{:S(2)}, u32[]{:S(2)}) collective-permute-start(bf16[2,64,1024]{2,1,0:T(8,128)(2,1)S(1)} %get-tuple-element.66._), channel_id=1, source_target_pairs={{0,1},{1,0},{2,3},{3,2},{4,5},{5,4},{6,7},{7,6},{8,9},{9,8},{10,11... | collective-permute-start | bytes 786440 | tf_op jit(solution)/shard_map/ppermute | solution.py:66
  63.1 8.4 %collective-permute-start.21 = (bf16[2,64,1024]{2,1,0:T(8,128)(2,1)S(1)}, bf16[2,64,1024]{2,1,0:T(8,128)(2,1)S(1)}, u32[]{:S(2)}, u32[]{:S(2)}) collective-permute-start(bf16[2,64,1024]{2,1,0:T(8,128)(2,1)S(1)} %get-tuple-element.67), channel_id=1, source_target_pairs={{0,4},{2,6},{4,0},{6,2},{8,12},{10,14},{12,8},{14,10},{16,20},{18,... | collective-permute-start | bytes 786440 | tf_op jit(solution)/shard_map/ppermute | solution.py:66
  65.9 6.2 %collective-permute-start.23 = (bf16[4,128,1024]{2,1,0:T(8,128)(2,1)S(1)}, bf16[4,128,1024]{2,1,0:T(8,128)(2,1)S(1)}, u32[]{:S(2)}, u32[]{:S(2)}) collective-permute-start(bf16[4,128,1024]{2,1,0:T(8,128)(2,1)S(1)} %get-tuple-element.68.refs_0_), channel_id=1, source_target_pairs={{0,2},{2,0},{4,6},{6,4},{8,10},{10,8},{12,14},{14,12},{16,18},{18,... | collective-permute-start | bytes 3145736 | tf_op jit(solution)/shard_map/ppermute | solution.py:66
  66.0 6.5 %collective-permute-start.28 = (bf16[64,2176]{1,0:T(8,128)(2,1)S(1)}, bf16[64,2176]{1,0:T(8,128)(2,1)S(1)}, u32[]{:S(2)}, u32[]{:S(2)}) collective-permute-start(bf16[64,2176]{1,0:T(8,128)(2,1)S(1)} %relay.5.refs_1_.refs_0_), channel_id=1, source_target_pairs={{0,2},{2,0},{4,6},{6,4},{8,10},{10,8},{12,14},{14,12},{16,18},{18,... | collective-permute-start | bytes 835592 | tf_op jit(solution)/shard_map/ppermute | solution.py:66
  70.3 3.0 %collective-permute-start.29 = (bf16[64,2176]{1,0:T(8,128)(2,1)S(1)}, bf16[64,2176]{1,0:T(8,128)(2,1)S(1)}, u32[]{:S(2)}, u32[]{:S(2)}) collective-permute-start(bf16[64,2176]{1,0:T(8,128)(2,1)S(1)} %relay.6.refs_0_.refs_2_), channel_id=1, source_target_pairs={{0,2},{2,0},{4,6},{6,4},{8,10},{10,8},{12,14},{14,12},{16,18},{18,... | collective-permute-start | bytes 835592 | tf_op jit(solution)/shard_map/ppermute | solution.py:66
  71.5 2.3 %collective-permute-start.32 = (bf16[64,2176]{1,0:T(8,128)(2,1)S(1)}, bf16[64,2176]{1,0:T(8,128)(2,1)S(1)}, u32[]{:S(2)}, u32[]{:S(2)}) collective-permute-start(bf16[64,2176]{1,0:T(8,128)(2,1)S(1)} %get-tuple-element.61.refs_19_.refs_0_.refs_4_.refs_8_), channel_id=1, source_target_pairs={{0,2},{2,0},{4,6},{6,4},{8,10},{10,8},{12,14},{14,12},{16,18},{18,... | collective-permute-start | bytes 835592 | tf_op jit(solution)/shard_map/ppermute | solution.py:66
  71.5 2.3 %collective-permute-start.33 = (bf16[64,2176]{1,0:T(8,128)(2,1)S(1)}, bf16[64,2176]{1,0:T(8,128)(2,1)S(1)}, u32[]{:S(2)}, u32[]{:S(2)}) collective-permute-start(bf16[64,2176]{1,0:T(8,128)(2,1)S(1)} %collective-permute-done.18.refs_1_.refs_6_.refs_10_), channel_id=1, source_target_pairs={{0,2},{2,0},{4,6},{6,4},{8,10},{10,8},{12,14},{14,12},{16,18},{18,... | collective-permute-start | bytes 835592 | tf_op jit(solution)/shard_map/ppermute | solution.py:66
  72.1 3.7 %collective-permute-start.34 = (bf16[2,64,2048]{2,1,0:T(8,128)(2,1)S(1)}, bf16[2,64,2048]{2,1,0:T(8,128)(2,1)S(1)}, u32[]{:S(2)}, u32[]{:S(2)}) collective-permute-start(bf16[2,64,2048]{2,1,0:T(8,128)(2,1)S(1)} %join.3._.refs_12_), channel_id=1, source_target_pairs={{0,2},{2,0},{4,6},{6,4},{8,10},{10,8},{12,14},{14,12},{16,18},{18,... | collective-permute-start | bytes 1572872 | tf_op jit(solution)/shard_map/ppermute | solution.py:66
  72.4 14.4 %collective-permute-start.22 = (bf16[4,64,1024]{2,1,0:T(8,128)(2,1)S(1)}, bf16[4,64,1024]{2,1,0:T(8,128)(2,1)S(1)}, u32[]{:S(2)}, u32[]{:S(2)}) collective-permute-start(bf16[4,64,1024]{2,1,0:T(8,128)(2,1)S(1)} %get-tuple-element.70._), channel_id=1, source_target_pairs={{0,1},{1,0},{2,3},{3,2},{4,5},{5,4},{6,7},{7,6},{8,9},{9,8},{10,11... | collective-permute-start | bytes 1572872 | tf_op jit(solution)/shard_map/ppermute | solution.py:66
  73.3 13.8 %collective-permute-start.24 = (bf16[2,128,1024]{2,1,0:T(8,128)(2,1)S(1)}, bf16[2,128,1024]{2,1,0:T(8,128)(2,1)S(1)}, u32[]{:S(2)}, u32[]{:S(2)}) collective-permute-start(bf16[2,128,1024]{2,1,0:T(8,128)(2,1)S(1)} %get-tuple-element.73._.refs_19_), channel_id=1, source_target_pairs={{0,4},{2,6},{4,0},{6,2},{8,12},{10,14},{12,8},{14,10},{16,20},{18,... | collective-permute-start | bytes 1572872 | tf_op jit(solution)/shard_map/ppermute | solution.py:66
  73.8 1.6 %collective-permute-start.30 = (bf16[64,2176]{1,0:T(8,128)(2,1)S(1)}, bf16[64,2176]{1,0:T(8,128)(2,1)S(1)}, u32[]{:S(2)}, u32[]{:S(2)}) collective-permute-start(bf16[64,2176]{1,0:T(8,128)(2,1)S(1)} %get-tuple-element.65.refs_2_.refs_4_), channel_id=1, source_target_pairs={{0,2},{2,0},{4,6},{6,4},{8,10},{10,8},{12,14},{14,12},{16,18},{18,... | collective-permute-start | bytes 835592 | tf_op jit(solution)/shard_map/ppermute | solution.py:66
  73.8 1.9 %collective-permute-start.31 = (bf16[64,2176]{1,0:T(8,128)(2,1)S(1)}, bf16[64,2176]{1,0:T(8,128)(2,1)S(1)}, u32[]{:S(2)}, u32[]{:S(2)}) collective-permute-start(bf16[64,2176]{1,0:T(8,128)(2,1)S(1)} %collective-permute-done.19.refs_3_.refs_6_), channel_id=1, source_target_pairs={{0,2},{2,0},{4,6},{6,4},{8,10},{10,8},{12,14},{14,12},{16,18},{18,... | collective-permute-start | bytes 835592 | tf_op jit(solution)/shard_map/ppermute | solution.py:66
  82.1 7.2 %collective-permute-start.35 = (bf16[4,128,1024]{2,1,0:T(8,128)(2,1)S(1)}, bf16[4,128,1024]{2,1,0:T(8,128)(2,1)S(1)}, u32[]{:S(2)}, u32[]{:S(2)}) collective-permute-start(bf16[4,128,1024]{2,1,0:T(8,128)(2,1)S(1)} %get-tuple-element.84._), channel_id=1, source_target_pairs={{0,2},{2,0},{4,6},{6,4},{8,10},{10,8},{12,14},{14,12},{16,18},{18,... | collective-permute-start | bytes 3145736 | tf_op jit(solution)/shard_map/ppermute | solution.py:66
  84.6 5.4 %collective-permute-start.37 = (bf16[4,128,1024]{2,1,0:T(8,128)(2,1)S(1)}, bf16[4,128,1024]{2,1,0:T(8,128)(2,1)S(1)}, u32[]{:S(2)}, u32[]{:S(2)}) collective-permute-start(bf16[4,128,1024]{2,1,0:T(8,128)(2,1)S(1)} %get-tuple-element.88), channel_id=1, source_target_pairs={{0,2},{2,0},{4,6},{6,4},{8,10},{10,8},{12,14},{14,12},{16,18},{18,... | collective-permute-start | bytes 3145736 | tf_op jit(solution)/shard_map/ppermute | solution.py:66
  87.3 9.3 %collective-permute-start.25 = (bf16[2,64,1024]{2,1,0:T(8,128)(2,1)S(1)}, bf16[2,64,1024]{2,1,0:T(8,128)(2,1)S(1)}, u32[]{:S(2)}, u32[]{:S(2)}) collective-permute-start(bf16[2,64,1024]{2,1,0:T(8,128)(2,1)S(1)} %get-tuple-element.75._), channel_id=1, source_target_pairs={{0,4},{2,6},{4,0},{6,2},{8,12},{10,14},{12,8},{14,10},{16,20},{18,... | collective-permute-start | bytes 786440 | tf_op jit(solution)/shard_map/ppermute | solution.py:66
  87.8 9.2 %collective-permute-start.26 = (bf16[2,64,1024]{2,1,0:T(8,128)(2,1)S(1)}, bf16[2,64,1024]{2,1,0:T(8,128)(2,1)S(1)}, u32[]{:S(2)}, u32[]{:S(2)}) collective-permute-start(bf16[2,64,1024]{2,1,0:T(8,128)(2,1)S(1)} %get-tuple-element.77), channel_id=1, source_target_pairs={{0,1},{1,0},{2,3},{3,2},{4,5},{5,4},{6,7},{7,6},{8,9},{9,8},{10,11... | collective-permute-start | bytes 786440 | tf_op jit(solution)/shard_map/ppermute | solution.py:66
  89.4 17.0 %collective-permute-start.36 = (bf16[4,64,1024]{2,1,0:T(8,128)(2,1)S(1)}, bf16[4,64,1024]{2,1,0:T(8,128)(2,1)S(1)}, u32[]{:S(2)}, u32[]{:S(2)}) collective-permute-start(bf16[4,64,1024]{2,1,0:T(8,128)(2,1)S(1)} %get-tuple-element.86._), channel_id=1, source_target_pairs={{0,1},{1,0},{2,3},{3,2},{4,5},{5,4},{6,7},{7,6},{8,9},{9,8},{10,11... | collective-permute-start | bytes 1572872 | tf_op jit(solution)/shard_map/ppermute | solution.py:66
  90.1 16.3 %collective-permute-start.38 = (bf16[2,128,1024]{2,1,0:T(8,128)(2,1)S(1)}, bf16[2,128,1024]{2,1,0:T(8,128)(2,1)S(1)}, u32[]{:S(2)}, u32[]{:S(2)}) collective-permute-start(bf16[2,128,1024]{2,1,0:T(8,128)(2,1)S(1)} %get-tuple-element.90), channel_id=1, source_target_pairs={{0,4},{2,6},{4,0},{6,2},{8,12},{10,14},{12,8},{14,10},{16,20},{18,... | collective-permute-start | bytes 1572872 | tf_op jit(solution)/shard_map/ppermute | solution.py:66
  97.2 12.4 %collective-permute-start.27 = (bf16[64,2048]{1,0:T(8,128)(2,1)S(1)}, bf16[64,2048]{1,0:T(8,128)(2,1)S(1)}, u32[]{:S(2)}, u32[]{:S(2)}) collective-permute-start(bf16[64,2048]{1,0:T(8,128)(2,1)S(1)} %get-tuple-element.79), channel_id=1, source_target_pairs={{0,16},{2,18},{4,20},{6,22},{8,24},{10,26},{12,28},{14,30},{16,0},... | collective-permute-start | bytes 786440 | tf_op jit(solution)/shard_map/ppermute | solution.py:71
  106.6 6.6 %collective-permute-start.39 = (bf16[2,64,1024]{2,1,0:T(8,128)(2,1)S(1)}, bf16[2,64,1024]{2,1,0:T(8,128)(2,1)S(1)}, u32[]{:S(2)}, u32[]{:S(2)}) collective-permute-start(bf16[2,64,1024]{2,1,0:T(8,128)(2,1)S(1)} %get-tuple-element.92), channel_id=1, source_target_pairs={{0,4},{2,6},{4,0},{6,2},{8,12},{10,14},{12,8},{14,10},{16,20},{18,... | collective-permute-start | bytes 786440 | tf_op jit(solution)/shard_map/ppermute | solution.py:66
  108.1 6.4 %collective-permute-start.40 = (bf16[2,64,1024]{2,1,0:T(8,128)(2,1)S(1)}, bf16[2,64,1024]{2,1,0:T(8,128)(2,1)S(1)}, u32[]{:S(2)}, u32[]{:S(2)}) collective-permute-start(bf16[2,64,1024]{2,1,0:T(8,128)(2,1)S(1)} %get-tuple-element.94), channel_id=1, source_target_pairs={{0,1},{1,0},{2,3},{3,2},{4,5},{5,4},{6,7},{7,6},{8,9},{9,8},{10,11... | collective-permute-start | bytes 786440 | tf_op jit(solution)/shard_map/ppermute | solution.py:66
  114.6 8.8 %collective-permute-start.41 = (bf16[64,2048]{1,0:T(8,128)(2,1)S(1)}, bf16[64,2048]{1,0:T(8,128)(2,1)S(1)}, u32[]{:S(2)}, u32[]{:S(2)}) collective-permute-start(bf16[64,2048]{1,0:T(8,128)(2,1)S(1)} %get-tuple-element.95), channel_id=1, source_target_pairs={{0,24},{2,26},{4,28},{6,30},{8,0},{10,2},{12,4},{14,6},{16,8},{18,... | collective-permute-start | bytes 786440 | tf_op jit(solution)/shard_map/ppermute | solution.py:71
  117.7 9.8 %collective-permute-start.42 = (bf16[64,2048]{1,0:T(8,128)(2,1)S(1)}, bf16[64,2048]{1,0:T(8,128)(2,1)S(1)}, u32[]{:S(2)}, u32[]{:S(2)}) collective-permute-start(bf16[64,2048]{1,0:T(8,128)(2,1)S(1)} %get-tuple-element.96), channel_id=1, source_target_pairs={{0,8},{2,10},{4,12},{6,14},{8,16},{10,18},{12,20},{14,22},{16,24},... | collective-permute-start | bytes 786440 | tf_op jit(solution)/shard_map/ppermute | solution.py:71

commit v7 on v5

--- a/solution.py
+++ b/solution.py
@@ -128,7 +128,7 @@
             pltpu.VMEM(ids.shape, jnp.int32),
             pltpu.SemaphoreType.DMA((3,)),
         ],
-        limit=4,
+        limit=60,
     )
 
 
@@ -232,7 +232,7 @@
     result[:, :, middle:] = right[...]
 
 
-def join(left, right, *after):
+def join(left, right, *after, work=0):
     dims = left.shape
     return small(
         join_kernel,
@@ -240,7 +240,7 @@
         [dims[:-1] + (2 * dims[-1],)],
         "vv" + "o" * len(after),
         (left, right, *after),
-        work=1 << 36,
+        work=work,
     )[0]
 
 
@@ -438,7 +438,7 @@
             send[p, :, at] = total[tokens:]
 
 
-def sums(offset, width, grads, w_gate, w_up, pick_t, after):
+def sums(offset, width, grads, w_gate, w_up, pick_t, after, work=0):
     pairs, tokens, _ = pick_t.shape
     _, count, units = grads.shape
     return small(
@@ -449,6 +449,7 @@
         (grads, w_gate, w_up, pick_t, after),
         [pltpu.VMEM((2, count, TILE), jnp.bfloat16)],
         limit=8,
+        work=work,
     )
 
 
@@ -565,10 +566,9 @@
         )
         return grads, pick_t
 
-    def spread(grads, pick_t, after):
-        keep_l, send_l = sums(0, middle, grads, w_gate, w_up, pick_t, after)
-        keep_r, send_r = sums(middle, middle, grads, w_gate, w_up, pick_t, send_l)
-        return keep_l, swap(send_l, "expert", 1), keep_r, swap(send_r, "expert", 1), send_r
+    def sums_by_token(offset, grads, pick_t, after, work=0):
+        keep, send = sums(offset, middle, grads, w_gate, w_up, pick_t, after, work)
+        return [keep, swap(send, "expert", 1)], send
 
     for offsets in CHUNKS:
         pieces = [along_line(part, -r) for r in offsets if r != 0]
@@ -583,10 +583,12 @@
             after = (left,)
         else:
             early = compute(0, line)
-            left, right = corner(over, side, middle, early[0])
-            early = spread(*early, left)
-            after = (early[-1],)
-        diag = join(swap(left, "tp", 1), swap(right, "expert", 2), *after)
+            grads, pick_t = early
+            early_l, after = sums_by_token(0, grads, pick_t, grads)
+            left, right = corner(over, side, middle, after)
+            early_r, after = sums_by_token(middle, grads, pick_t, left, 68719476736)
+            after = (after,)
+        diag = join(swap(left, "tp", 1), swap(right, "expert", 2), *after, work=8589934592)
         moved = []
         for array in (line, side, over, diag):
             moved += [array, swap(array, "expert", 1)]
@@ -603,10 +605,12 @@
         rows = third_sum(offsets, left, came_l, right, came_r, send_l if came is None else came)
         return rows[0], [row if r == 0 else along_line(row, r) for r, row in zip(offsets, rows)], send_l
 
-    early = first_step(*early[:4], gathered[1][6])
-    late = spread(*compute(1, early[4]), early[4])
+    early = first_step(*early_l, *early_r, gathered[1][6])
+    grads, pick_t = compute(1, early[4])
+    late_l, after = sums_by_token(0, grads, pick_t, grads)
+    late_r, _ = sums_by_token(middle, grads, pick_t, after)
     done, early, after = second_step(CHUNKS[0], early[:4], early[4], None)
-    late = first_step(*late[:4], after)
+    late = first_step(*late_l, *late_r, after)
     _, late, _ = second_step(CHUNKS[1], late[:4], done, early[-1])
     terms = early + late
     return pl.pallas_call(

time: 120 us -> 117 us (0.975)
  waiting for transfers between devices: 59 us -> 54.6 us
  Pallas kernels: 23.4 us -> 25.3 us
    ppermute x31, waiting for transfers between devices: 35 us -> 31 us  [swap(): return lax.ppermute(value, axis, [(i, i ^ step) for i in range(count)])]
    pallas_call x24, Pallas kernels: 22.5 us -> 24.4 us  [small(): pl.pallas_call(kernel, out_shape=[out if hasattr(out, 'dtype') else jax.S...]
    unnamed x18 -> x20, local copies, waits for them, and re-layouts: 3.71 us -> 2.92 us
  transfers between devices with their start and end apart: 37 -> 37, of which waited for: 20 -> 19; matrix products, arithmetic and copies ran while one was open for 0% -> 0% of each run, Pallas kernels for 18% -> 19%
where the time goes in v7:
time: 117 us
  waiting for transfers between devices  54.6 us (47%)
  starting transfers between devices  33.2 us (28%)
  Pallas kernels  25.3 us (22%)
  local copies, waits for them, and re-layouts  2.92 us (2%)
    ppermute x31, waiting for transfers between devices, swap(): return lax.ppermute(value, axis, [(i, i ^ step) for i in range(count)])  31 us
    pallas_call x24, Pallas kernels, small(): pl.pallas_call(kernel, out_shape=[out if hasattr(out, 'dtype') else jax.S...  24.4 us
    ppermute x6, waiting for transfers between devices, along_line(): lax.ppermute(value, 'expert', [(i, (i + 4 * shift) % count) for i in rang...  23.6 us
    ppermute x31, starting transfers between devices, swap(): return lax.ppermute(value, axis, [(i, i ^ step) for i in range(count)])  21.5 us
    ppermute x6, starting transfers between devices, along_line(): lax.ppermute(value, 'expert', [(i, (i + 4 * shift) % count) for i in rang...  11.8 us
    unnamed x20, local copies, waits for them, and re-layouts  2.92 us
  transfers between devices with their start and end apart: 37, of which 19 were waited for; matrix products, arithmetic and copies ran while one was open for 0% of the time, Pallas kernels for 19%

profile of v7, /device:TPU:0, one launch (start us, length us, event | category | flops | bytes accessed | tf_op | source)
XLA Modules:
  0.0 117.0 jit_solution(17728222123316943683)
XLA Ops:
  0.0 0.7 pad_add_fusion.place
  0.7 2.5 %prepare.1 = (bf16[64,2176]{1,0:T(8,128)(2,1)}, bf16[64,128]{1,0:T(8,128)(2,1)}) custom-call(s32[4]{0:T(128)} %pad_add_fusion.place, bf16[128,2048]{1,0:T(8,128)(2,1)} %own.3, f32[8,128]{1,0:T(8,128)} %bitcast.6, s32[8,128]{1,0:T(8,128)} %bitcast.7), custom_call_target="tpu_custom_call" | custom-call | tf_op jit(solution)/shard_map/prepare/pallas_call | solution.py:76
  3.2 4.1 %collective-permute-start.1 = (bf16[64,2176]{1,0:T(8,128)(2,1)}, bf16[64,2176]{1,0:T(8,128)(2,1)S(1)}, u32[]{:S(2)}, u32[]{:S(2)}) collective-permute-start(bf16[64,2176]{1,0:T(8,128)(2,1)} %get-tuple-element.50.part), channel_id=1, source_target_pairs={{0,16},{2,18},{4,20},{6,22},{8,24},{10,26},{12,28},{14,30},{16,0},... | collective-permute-start | bytes 835592 | tf_op jit(solution)/shard_map/ppermute | solution.py:71
  7.3 1.5 %collective-permute-start.5 = (bf16[64,2176]{1,0:T(8,128)(2,1)}, bf16[64,2176]{1,0:T(8,128)(2,1)S(1)}, u32[]{:S(2)}, u32[]{:S(2)}) collective-permute-start(bf16[64,2176]{1,0:T(8,128)(2,1)} %get-tuple-element.50.part), channel_id=1, source_target_pairs={{0,4},{2,6},{4,0},{6,2},{8,12},{10,14},{12,8},{14,10},{16,20},{18,... | collective-permute-start | bytes 835592 | tf_op jit(solution)/shard_map/ppermute | solution.py:66
  8.8 11.3 %collective-permute-done.1.came = bf16[64,2176]{1,0:T(8,128)(2,1)S(1)} collective-permute-done((bf16[64,2176]{1,0:T(8,128)(2,1)}, bf16[64,2176]{1,0:T(8,128)(2,1)S(1)}, u32[]{:S(2)}, u32[]{:S(2)}) %collective-permute-start.1) | collective-permute-done | bytes 278560 | tf_op jit(solution)/shard_map/ppermute | solution.py:71
  20.1 1.0 copy-done.6
  21.1 1.6 %collective-permute-start.3 = (bf16[1,64,2176]{2,1,0:T(8,128)(2,1)S(1)}, bf16[1,64,2176]{2,1,0:T(8,128)(2,1)S(1)}, u32[]{:S(2)}, u32[]{:S(2)}) collective-permute-start(bf16[1,64,2176]{2,1,0:T(8,128)(2,1)S(1)} %get-tuple-element.51.lines._), channel_id=1, source_target_pairs={{0,1},{1,0},{2,3},{3,2},{4,5},{5,4},{6,7},{7,6},{8,9},{9,8},{10,11... | collective-permute-start | bytes 835592 | tf_op jit(solution)/shard_map/ppermute | solution.py:66
  22.7 1.5 %collective-permute-start.6 = (bf16[1,64,2176]{2,1,0:T(8,128)(2,1)S(1)}, bf16[1,64,2176]{2,1,0:T(8,128)(2,1)S(1)}, u32[]{:S(2)}, u32[]{:S(2)}) collective-permute-start(bf16[1,64,2176]{2,1,0:T(8,128)(2,1)S(1)} %get-tuple-element.51.lines._), channel_id=1, source_target_pairs={{0,4},{2,6},{4,0},{6,2},{8,12},{10,14},{12,8},{14,10},{16,20},{18,... | collective-permute-start | bytes 835592 | tf_op jit(solution)/shard_map/ppermute | solution.py:66
  24.2 3.5 %collective-permute-start.12 = (bf16[64,2176]{1,0:T(8,128)(2,1)S(1)}, bf16[64,2176]{1,0:T(8,128)(2,1)S(1)}, u32[]{:S(2)}, u32[]{:S(2)}) collective-permute-start(bf16[64,2176]{1,0:T(8,128)(2,1)S(1)} %get-tuple-element.60), channel_id=1, source_target_pairs={{0,24},{2,26},{4,28},{6,30},{8,0},{10,2},{12,4},{14,6},{16,8},{18,... | collective-permute-start | bytes 835592 | tf_op jit(solution)/shard_map/ppermute | solution.py:71
  27.7 1.3 %collective-permute-done.3.side = bf16[1,64,2176]{2,1,0:T(8,128)(2,1)S(1)} collective-permute-done((bf16[1,64,2176]{2,1,0:T(8,128)(2,1)S(1)}, bf16[1,64,2176]{2,1,0:T(8,128)(2,1)S(1)}, u32[]{:S(2)}, u32[]{:S(2)}) %collective-permute-start.3) | collective-permute-done | bytes 278560 | tf_op jit(solution)/shard_map/ppermute | solution.py:66
  29.0 1.0 collective-permute-done.6.over
  30.0 0.7 copy-done.8
  30.7 0.6 own_corner.1
  31.3 0.8 collective-permute-start.8
  32.2 1.3 %collective-permute-start.9 = (bf16[2,64,1024]{2,1,0:T(8,128)(2,1)S(1)}, bf16[2,64,1024]{2,1,0:T(8,128)(2,1)S(1)}, u32[]{:S(2)}, u32[]{:S(2)}) collective-permute-start(bf16[2,64,1024]{2,1,0:T(8,128)(2,1)S(1)} %get-tuple-element.54), channel_id=1, source_target_pairs={{0,4},{2,6},{4,0},{6,2},{8,12},{10,14},{12,8},{14,10},{16,20},{18,... | collective-permute-start | bytes 786440 | tf_op jit(solution)/shard_map/ppermute | solution.py:66
  33.5 1.3 %copy-done.5 = bf16[2,384,768]{2,1,0:T(8,128)(2,1)S(1)} copy-done((bf16[2,384,768]{2,1,0:T(8,128)(2,1)S(1)}, bf16[2,384,768]{2,1,0:T(8,128)(2,1)}, u32[]{:S(2)}) %copy-start.5) | copy-done | bytes 1179672
  34.7 0.7 turn.1
  35.4 0.6 collective-permute-start.2
  36.0 4.0 %collective-permute-done.13.refs_1_ = bf16[64,2176]{1,0:T(8,128)(2,1)S(1)} collective-permute-done((bf16[64,2176]{1,0:T(8,128)(2,1)S(1)}, bf16[64,2176]{1,0:T(8,128)(2,1)S(1)}, u32[]{:S(2)}, u32[]{:S(2)}) %collective-permute-start.13) | collective-permute-done | bytes 278560 | tf_op jit(solution)/shard_map/ppermute | solution.py:71
  40.0 0.6 collective-permute-start.15
  40.6 0.5 collective-permute-start.16
  41.2 0.6 collective-permute-start
  41.9 1.2 %collective-permute-done.7.over_c = bf16[2,64,2176]{2,1,0:T(8,128)(2,1)S(1)} collective-permute-done((bf16[2,64,2176]{2,1,0:T(8,128)(2,1)S(1)}, bf16[2,64,2176]{2,1,0:T(8,128)(2,1)S(1)}, u32[]{:S(2)}, u32[]{:S(2)}) %collective-permute-start.7) | collective-permute-done | bytes 557088 | tf_op jit(solution)/shard_map/ppermute | solution.py:66
  43.1 0.1 collective-permute-start.4
  43.2 1.1 route.2
  44.4 0.6 collective-permute-done.4.side_c
  45.0 4.2 %hidden.2.grads._ = bf16[2,384,768]{2,1,0:T(8,128)(2,1)S(1)} custom-call(s32[4]{0:T(128)S(1)} %copy-done.9, bf16[128,2048]{1,0:T(8,128)(2,1)S(1)} %copy-done.3, bf16[128,2048]{1,0:T(8,128)(2,1)S(1)} %collective-permute-done.own_c, bf16[1,64,2176]{2,1,0:T(8,128)(2,1)S(1)} %get-tuple-element.51.lines._, ...), custom_call_target="tpu_custom_call" | custom-call | tf_op jit(solution)/shard_map/hidden/pallas_call | solution.py:76
  49.2 2.2 %sums.4 = (bf16[4,128,1024]{2,1,0:T(8,128)(2,1)S(1)}, bf16[4,128,1024]{2,1,0:T(8,128)(2,1)S(1)}) custom-call(bf16[2,384,768]{2,1,0:T(8,128)(2,1)S(1)} %hidden.2.grads._, bf16[2,384,2048]{2,1,0:T(8,128)(2,1)S(1)} %copy-done, bf16[2,384,2048]{2,1,0:T(8,128)(2,1)S(1)} %copy-done.1, bf16[4,256,192]{2,1,0:T(8,128)(2,1)S(1)} %get-tuple-element.61.pick_t, ...), custom_call_target="tpu_custom_call" | custom-call | tf_op jit(solution)/shard_map/sums/pallas_call | solution.py:76
  51.5 0.2 collective-permute-start.14
  51.7 1.8 %collective-permute-done.15.over = bf16[2,64,2176]{2,1,0:T(8,128)(2,1)S(1)} collective-permute-done((bf16[2,64,2176]{2,1,0:T(8,128)(2,1)S(1)}, bf16[2,64,2176]{2,1,0:T(8,128)(2,1)S(1)}, u32[]{:S(2)}, u32[]{:S(2)}) %collective-permute-start.15) | collective-permute-done | bytes 557088 | tf_op jit(solution)/shard_map/ppermute | solution.py:66
  53.5 0.2 collective-permute-done.16.side
  53.7 0.6 collective-permute-start.17
  54.3 1.5 %collective-permute-start.18 = (bf16[2,64,1024]{2,1,0:T(8,128)(2,1)S(1)}, bf16[2,64,1024]{2,1,0:T(8,128)(2,1)S(1)}, u32[]{:S(2)}, u32[]{:S(2)}) collective-permute-start(bf16[2,64,1024]{2,1,0:T(8,128)(2,1)S(1)} %get-tuple-element.65), channel_id=1, source_target_pairs={{0,4},{2,6},{4,0},{6,2},{8,12},{10,14},{12,8},{14,10},{16,20},{18,... | collective-permute-start | bytes 786440 | tf_op jit(solution)/shard_map/ppermute | solution.py:66
  55.9 2.2 %sums.5 = (bf16[4,128,1024]{2,1,0:T(8,128)(2,1)S(1)}, bf16[4,128,1024]{2,1,0:T(8,128)(2,1)S(1)}) custom-call(bf16[2,384,768]{2,1,0:T(8,128)(2,1)S(1)} %hidden.2.grads._, bf16[2,384,2048]{2,1,0:T(8,128)(2,1)S(1)} %copy-done, bf16[2,384,2048]{2,1,0:T(8,128)(2,1)S(1)} %copy-done.1, bf16[4,256,192]{2,1,0:T(8,128)(2,1)S(1)} %get-tuple-element.61.pick_t, ...), custom_call_target="tpu_custom_call" | custom-call | flops 68719476736 | bytes 268435456 | tf_op jit(solution)/shard_map/sums/pallas_call | solution.py:76
  58.2 0.5 collective-permute-start.25
  58.7 1.7 %collective-permute-done.17.left = bf16[2,64,1024]{2,1,0:T(8,128)(2,1)S(1)} collective-permute-done((bf16[2,64,1024]{2,1,0:T(8,128)(2,1)S(1)}, bf16[2,64,1024]{2,1,0:T(8,128)(2,1)S(1)}, u32[]{:S(2)}, u32[]{:S(2)}) %collective-permute-start.17) | collective-permute-done | bytes 262176 | tf_op jit(solution)/shard_map/ppermute | solution.py:66
  60.4 1.2 %collective-permute-done.18.right = bf16[2,64,1024]{2,1,0:T(8,128)(2,1)S(1)} collective-permute-done((bf16[2,64,1024]{2,1,0:T(8,128)(2,1)S(1)}, bf16[2,64,1024]{2,1,0:T(8,128)(2,1)S(1)}, u32[]{:S(2)}, u32[]{:S(2)}) %collective-permute-start.18) | collective-permute-done | bytes 262176 | tf_op jit(solution)/shard_map/ppermute | solution.py:66
  61.6 0.6 collective-permute-start.28
  62.3 0.7 collective-permute-start.19
  63.1 1.6 %collective-permute-start.21 = (bf16[2,128,1024]{2,1,0:T(8,128)(2,1)S(1)}, bf16[2,128,1024]{2,1,0:T(8,128)(2,1)S(1)}, u32[]{:S(2)}, u32[]{:S(2)}) collective-permute-start(bf16[2,128,1024]{2,1,0:T(8,128)(2,1)S(1)} %get-tuple-element.71._), channel_id=1, source_target_pairs={{0,4},{2,6},{4,0},{6,2},{8,12},{10,14},{12,8},{14,10},{16,20},{18,... | collective-permute-start | bytes 1572872 | tf_op jit(solution)/shard_map/ppermute | solution.py:66
  64.7 1.1 route.3
  65.9 4.1 %hidden.3.grads._ = bf16[2,384,768]{2,1,0:T(8,128)(2,1)S(1)} custom-call(s32[4]{0:T(128)S(1)} %copy-done.9, bf16[128,2048]{1,0:T(8,128)(2,1)S(1)} %copy-done.3, bf16[128,2048]{1,0:T(8,128)(2,1)S(1)} %collective-permute-done.own_c, bf16[2,64,2176]{2,1,0:T(8,128)(2,1)S(1)} %stack.21._.lines, bf16[2,64,2176]{2,1,0:T(8,128)(2,1)S(1)} %collective-permute-done.25.lines_c, ...), custom_call_target="tpu_custom_call" | custom-call | tf_op jit(solution)/shard_map/hidden/pallas_call | solution.py:76
  70.0 2.2 %sums.6 = (bf16[4,128,1024]{2,1,0:T(8,128)(2,1)S(1)}, bf16[4,128,1024]{2,1,0:T(8,128)(2,1)S(1)}) custom-call(bf16[2,384,768]{2,1,0:T(8,128)(2,1)S(1)} %hidden.3.grads._, bf16[2,384,2048]{2,1,0:T(8,128)(2,1)S(1)} %copy-done, bf16[2,384,2048]{2,1,0:T(8,128)(2,1)S(1)} %copy-done.1, bf16[4,256,192]{2,1,0:T(8,128)(2,1)S(1)} %get-tuple-element.80.pick_t, ...), custom_call_target="tpu_custom_call" | custom-call | tf_op jit(solution)/shard_map/sums/pallas_call | solution.py:76
  72.3 2.2 %sums.7 = (bf16[4,128,1024]{2,1,0:T(8,128)(2,1)S(1)}, bf16[4,128,1024]{2,1,0:T(8,128)(2,1)S(1)}) custom-call(bf16[2,384,768]{2,1,0:T(8,128)(2,1)S(1)} %hidden.3.grads._, bf16[2,384,2048]{2,1,0:T(8,128)(2,1)S(1)} %copy-done, bf16[2,384,2048]{2,1,0:T(8,128)(2,1)S(1)} %copy-done.1, bf16[4,256,192]{2,1,0:T(8,128)(2,1)S(1)} %get-tuple-element.80.pick_t, ...), custom_call_target="tpu_custom_call" | custom-call | tf_op jit(solution)/shard_map/sums/pallas_call | solution.py:76
  74.6 0.6 collective-permute-start.31
  75.1 1.1 collective-permute-done.19.came_l
  76.2 0.7 collective-permute-done.21.came_r
  77.0 1.6 %collective-permute-start.22 = (bf16[2,64,1024]{2,1,0:T(8,128)(2,1)S(1)}, bf16[2,64,1024]{2,1,0:T(8,128)(2,1)S(1)}, u32[]{:S(2)}, u32[]{:S(2)}) collective-permute-start(bf16[2,64,1024]{2,1,0:T(8,128)(2,1)S(1)} %get-tuple-element.73._), channel_id=1, source_target_pairs={{0,4},{2,6},{4,0},{6,2},{8,12},{10,14},{12,8},{14,10},{16,20},{18,... | collective-permute-start | bytes 786440 | tf_op jit(solution)/shard_map/ppermute | solution.py:66
  78.6 1.3 %collective-permute-start.23 = (bf16[2,64,1024]{2,1,0:T(8,128)(2,1)S(1)}, bf16[2,64,1024]{2,1,0:T(8,128)(2,1)S(1)}, u32[]{:S(2)}, u32[]{:S(2)}) collective-permute-start(bf16[2,64,1024]{2,1,0:T(8,128)(2,1)S(1)} %get-tuple-element.75), channel_id=1, source_target_pairs={{0,1},{1,0},{2,3},{3,2},{4,5},{5,4},{6,7},{7,6},{8,9},{9,8},{10,11... | collective-permute-start | bytes 786440 | tf_op jit(solution)/shard_map/ppermute | solution.py:66
  80.0 0.8 collective-permute-start.30
  80.9 0.6 collective-permute-start.32
  81.5 4.8 %collective-permute-done.22.came_l = bf16[2,64,1024]{2,1,0:T(8,128)(2,1)S(1)} collective-permute-done((bf16[2,64,1024]{2,1,0:T(8,128)(2,1)S(1)}, bf16[2,64,1024]{2,1,0:T(8,128)(2,1)S(1)}, u32[]{:S(2)}, u32[]{:S(2)}) %collective-permute-start.22) | collective-permute-done | bytes 262176 | tf_op jit(solution)/shard_map/ppermute | solution.py:66
  86.3 1.5 %collective-permute-done.23.came_r = bf16[2,64,1024]{2,1,0:T(8,128)(2,1)S(1)} collective-permute-done((bf16[2,64,1024]{2,1,0:T(8,128)(2,1)S(1)}, bf16[2,64,1024]{2,1,0:T(8,128)(2,1)S(1)}, u32[]{:S(2)}, u32[]{:S(2)}) %collective-permute-start.23) | collective-permute-done | bytes 262176 | tf_op jit(solution)/shard_map/ppermute | solution.py:66
  88.0 0.3 collective-permute-start.24
  88.2 8.5 %collective-permute-done.30.came_l = bf16[4,64,1024]{2,1,0:T(8,128)(2,1)S(1)} collective-permute-done((bf16[4,64,1024]{2,1,0:T(8,128)(2,1)S(1)}, bf16[4,64,1024]{2,1,0:T(8,128)(2,1)S(1)}, u32[]{:S(2)}, u32[]{:S(2)}) %collective-permute-start.30) | collective-permute-done | bytes 524320 | tf_op jit(solution)/shard_map/ppermute | solution.py:66
  96.9 0.6 collective-permute-start.33
  97.5 1.1 collective-permute-start.34
  98.6 4.8 %collective-permute-done.33.came_l = bf16[2,64,1024]{2,1,0:T(8,128)(2,1)S(1)} collective-permute-done((bf16[2,64,1024]{2,1,0:T(8,128)(2,1)S(1)}, bf16[2,64,1024]{2,1,0:T(8,128)(2,1)S(1)}, u32[]{:S(2)}, u32[]{:S(2)}) %collective-permute-start.33) | collective-permute-done | bytes 262176 | tf_op jit(solution)/shard_map/ppermute | solution.py:66
  103.3 0.5 collective-permute-done.34.came_r
  104.0 2.0 %collective-permute-start.35 = (bf16[64,2048]{1,0:T(8,128)(2,1)S(1)}, bf16[64,2048]{1,0:T(8,128)(2,1)S(1)}, u32[]{:S(2)}, u32[]{:S(2)}) collective-permute-start(bf16[64,2048]{1,0:T(8,128)(2,1)S(1)} %get-tuple-element.93), channel_id=1, source_target_pairs={{0,8},{2,10},{4,12},{6,14},{8,16},{10,18},{12,20},{14,22},{16,24},... | collective-permute-start | bytes 786440 | tf_op jit(solution)/shard_map/ppermute | solution.py:71
  106.0 1.9 %collective-permute-start.36 = (bf16[64,2048]{1,0:T(8,128)(2,1)S(1)}, bf16[64,2048]{1,0:T(8,128)(2,1)S(1)}, u32[]{:S(2)}, u32[]{:S(2)}) collective-permute-start(bf16[64,2048]{1,0:T(8,128)(2,1)S(1)} %get-tuple-element.94), channel_id=1, source_target_pairs={{0,24},{2,26},{4,28},{6,30},{8,0},{10,2},{12,4},{14,6},{16,8},{18,... | collective-permute-start | bytes 786440 | tf_op jit(solution)/shard_map/ppermute | solution.py:71
  107.8 5.6 %collective-permute-done.35.refs_2_ = bf16[64,2048]{1,0:T(8,128)(2,1)S(1)} collective-permute-done((bf16[64,2048]{1,0:T(8,128)(2,1)S(1)}, bf16[64,2048]{1,0:T(8,128)(2,1)S(1)}, u32[]{:S(2)}, u32[]{:S(2)}) %collective-permute-start.35) | collective-permute-done | bytes 262176 | tf_op jit(solution)/shard_map/ppermute | solution.py:71
  113.5 2.6 %collective-permute-done.36.refs_3_ = bf16[64,2048]{1,0:T(8,128)(2,1)S(1)} collective-permute-done((bf16[64,2048]{1,0:T(8,128)(2,1)S(1)}, bf16[64,2048]{1,0:T(8,128)(2,1)S(1)}, u32[]{:S(2)}, u32[]{:S(2)}) %collective-permute-start.36) | collective-permute-done | bytes 262176 | tf_op jit(solution)/shard_map/ppermute | solution.py:71
  116.1 0.9 last_sum.1
  (56 shorter events, 1.4 us)
Async XLA Ops:
  0.0 30.0 %copy-start.3 = (bf16[128,2048]{1,0:T(8,128)(2,1)S(1)}, bf16[128,2048]{1,0:T(8,128)(2,1)}, u32[]{:S(2)}) copy-start(bf16[128,2048]{1,0:T(8,128)(2,1)} %own.3) | copy-start | bytes 1572868
  0.7 32.8 %copy-start.4 = (bf16[2,384,768]{2,1,0:T(8,128)(2,1)S(1)}, bf16[2,384,768]{2,1,0:T(8,128)(2,1)}, u32[]{:S(2)}) copy-start(bf16[2,384,768]{2,1,0:T(8,128)(2,1)} %gate.1) | copy-start | bytes 3538948
  3.2 16.9 %collective-permute-start.1 = (bf16[64,2176]{1,0:T(8,128)(2,1)}, bf16[64,2176]{1,0:T(8,128)(2,1)S(1)}, u32[]{:S(2)}, u32[]{:S(2)}) collective-permute-start(bf16[64,2176]{1,0:T(8,128)(2,1)} %get-tuple-element.50.part), channel_id=1, source_target_pairs={{0,16},{2,18},{4,20},{6,22},{8,24},{10,26},{12,28},{14,30},{16,0},... | collective-permute-start | bytes 835592 | tf_op jit(solution)/shard_map/ppermute | solution.py:71
  7.3 20.5 %collective-permute-start.5 = (bf16[64,2176]{1,0:T(8,128)(2,1)}, bf16[64,2176]{1,0:T(8,128)(2,1)S(1)}, u32[]{:S(2)}, u32[]{:S(2)}) collective-permute-start(bf16[64,2176]{1,0:T(8,128)(2,1)} %get-tuple-element.50.part), channel_id=1, source_target_pairs={{0,4},{2,6},{4,0},{6,2},{8,12},{10,14},{12,8},{14,10},{16,20},{18,... | collective-permute-start | bytes 835592 | tf_op jit(solution)/shard_map/ppermute | solution.py:66
  20.1 1.0 copy-start.6
  21.1 12.4 %copy-start.7 = (bf16[64,128]{1,0:T(8,128)(2,1)S(1)}, bf16[64,128]{1,0:T(8,128)(2,1)}, u32[]{:S(2)}) copy-start(bf16[64,128]{1,0:T(8,128)(2,1)} %get-tuple-element.55.own) | copy-start | bytes 49156
  21.1 7.9 %collective-permute-start.3 = (bf16[1,64,2176]{2,1,0:T(8,128)(2,1)S(1)}, bf16[1,64,2176]{2,1,0:T(8,128)(2,1)S(1)}, u32[]{:S(2)}, u32[]{:S(2)}) collective-permute-start(bf16[1,64,2176]{2,1,0:T(8,128)(2,1)S(1)} %get-tuple-element.51.lines._), channel_id=1, source_target_pairs={{0,1},{1,0},{2,3},{3,2},{4,5},{5,4},{6,7},{7,6},{8,9},{9,8},{10,11... | collective-permute-start | bytes 835592 | tf_op jit(solution)/shard_map/ppermute | solution.py:66
  22.7 7.3 %collective-permute-start.6 = (bf16[1,64,2176]{2,1,0:T(8,128)(2,1)S(1)}, bf16[1,64,2176]{2,1,0:T(8,128)(2,1)S(1)}, u32[]{:S(2)}, u32[]{:S(2)}) collective-permute-start(bf16[1,64,2176]{2,1,0:T(8,128)(2,1)S(1)} %get-tuple-element.51.lines._), channel_id=1, source_target_pairs={{0,4},{2,6},{4,0},{6,2},{8,12},{10,14},{12,8},{14,10},{16,20},{18,... | collective-permute-start | bytes 835592 | tf_op jit(solution)/shard_map/ppermute | solution.py:66
  24.2 11.2 %collective-permute-start.12 = (bf16[64,2176]{1,0:T(8,128)(2,1)S(1)}, bf16[64,2176]{1,0:T(8,128)(2,1)S(1)}, u32[]{:S(2)}, u32[]{:S(2)}) collective-permute-start(bf16[64,2176]{1,0:T(8,128)(2,1)S(1)} %get-tuple-element.60), channel_id=1, source_target_pairs={{0,24},{2,26},{4,28},{6,30},{8,0},{10,2},{12,4},{14,6},{16,8},{18,... | collective-permute-start | bytes 835592 | tf_op jit(solution)/shard_map/ppermute | solution.py:71
  27.7 12.2 %collective-permute-start.13 = (bf16[64,2176]{1,0:T(8,128)(2,1)S(1)}, bf16[64,2176]{1,0:T(8,128)(2,1)S(1)}, u32[]{:S(2)}, u32[]{:S(2)}) collective-permute-start(bf16[64,2176]{1,0:T(8,128)(2,1)S(1)} %get-tuple-element.60), channel_id=1, source_target_pairs={{0,8},{2,10},{4,12},{6,14},{8,16},{10,18},{12,20},{14,22},{16,24},... | collective-permute-start | bytes 835592 | tf_op jit(solution)/shard_map/ppermute | solution.py:71
  30.0 0.7 copy-start.8
  31.3 9.3 %collective-permute-start.8 = (bf16[2,64,1024]{2,1,0:T(8,128)(2,1)S(1)}, bf16[2,64,1024]{2,1,0:T(8,128)(2,1)S(1)}, u32[]{:S(2)}, u32[]{:S(2)}) collective-permute-start(bf16[2,64,1024]{2,1,0:T(8,128)(2,1)S(1)} %get-tuple-element.53.refs_0_), channel_id=1, source_target_pairs={{0,1},{1,0},{2,3},{3,2},{4,5},{5,4},{6,7},{7,6},{8,9},{9,8},{10,11... | collective-permute-start | bytes 786440 | tf_op jit(solution)/shard_map/ppermute | solution.py:66
  32.2 9.0 %collective-permute-start.9 = (bf16[2,64,1024]{2,1,0:T(8,128)(2,1)S(1)}, bf16[2,64,1024]{2,1,0:T(8,128)(2,1)S(1)}, u32[]{:S(2)}, u32[]{:S(2)}) collective-permute-start(bf16[2,64,1024]{2,1,0:T(8,128)(2,1)S(1)} %get-tuple-element.54), channel_id=1, source_target_pairs={{0,4},{2,6},{4,0},{6,2},{8,12},{10,14},{12,8},{14,10},{16,20},{18,... | collective-permute-start | bytes 786440 | tf_op jit(solution)/shard_map/ppermute | solution.py:66
  33.4 7.8 %collective-permute-start.11 = (bf16[64,128]{1,0:T(8,128)(2,1)S(1)}, bf16[64,128]{1,0:T(8,128)(2,1)S(1)}, u32[]{:S(2)}, u32[]{:S(2)}) collective-permute-start(bf16[64,128]{1,0:T(8,128)(2,1)S(1)} %copy-done.7), channel_id=1, source_target_pairs={{0,2},{2,0},{4,6},{6,4},{8,10},{10,8},{12,14},{14,12},{16,18},{18,... | collective-permute-start | bytes 49160 | tf_op jit(solution)/shard_map/ppermute | solution.py:66
  33.4 1.3 %copy-start.5 = (bf16[2,384,768]{2,1,0:T(8,128)(2,1)S(1)}, bf16[2,384,768]{2,1,0:T(8,128)(2,1)}, u32[]{:S(2)}) copy-start(bf16[2,384,768]{2,1,0:T(8,128)(2,1)} %up.1) | copy-start | bytes 3538948
  35.4 6.4 %collective-permute-start.2 = (bf16[1,64,2176]{2,1,0:T(8,128)(2,1)S(1)}, bf16[1,64,2176]{2,1,0:T(8,128)(2,1)S(1)}, u32[]{:S(2)}, u32[]{:S(2)}) collective-permute-start(bf16[1,64,2176]{2,1,0:T(8,128)(2,1)S(1)} %get-tuple-element.51.lines._), channel_id=1, source_target_pairs={{0,2},{2,0},{4,6},{6,4},{8,10},{10,8},{12,14},{14,12},{16,18},{18,... | collective-permute-start | bytes 835592 | tf_op jit(solution)/shard_map/ppermute | solution.py:66
  40.0 13.4 %collective-permute-start.15 = (bf16[2,64,2176]{2,1,0:T(8,128)(2,1)S(1)}, bf16[2,64,2176]{2,1,0:T(8,128)(2,1)S(1)}, u32[]{:S(2)}, u32[]{:S(2)}) collective-permute-start(bf16[2,64,2176]{2,1,0:T(8,128)(2,1)S(1)} %stack.21._.lines), channel_id=1, source_target_pairs={{0,4},{2,6},{4,0},{6,2},{8,12},{10,14},{12,8},{14,10},{16,20},{18,... | collective-permute-start | bytes 1671176 | tf_op jit(solution)/shard_map/ppermute | solution.py:66
  40.6 13.1 %collective-permute-start.16 = (bf16[2,64,2176]{2,1,0:T(8,128)(2,1)S(1)}, bf16[2,64,2176]{2,1,0:T(8,128)(2,1)S(1)}, u32[]{:S(2)}, u32[]{:S(2)}) collective-permute-start(bf16[2,64,2176]{2,1,0:T(8,128)(2,1)S(1)} %stack.21._.lines), channel_id=1, source_target_pairs={{0,1},{1,0},{2,3},{3,2},{4,5},{5,4},{6,7},{7,6},{8,9},{9,8},{10,11... | collective-permute-start | bytes 1671176 | tf_op jit(solution)/shard_map/ppermute | solution.py:66
  41.1 2.1 %copy-start.9 = (s32[4]{0:T(128)S(1)}, s32[4]{0:T(128)}, u32[]{:S(2)}) copy-start(s32[4]{0:T(128)} %pad_add_fusion.place) | copy-start | bytes 52
  41.1 2.0 %collective-permute-start.7 = (bf16[2,64,2176]{2,1,0:T(8,128)(2,1)S(1)}, bf16[2,64,2176]{2,1,0:T(8,128)(2,1)S(1)}, u32[]{:S(2)}, u32[]{:S(2)}) collective-permute-start(bf16[2,64,2176]{2,1,0:T(8,128)(2,1)S(1)} %get-tuple-element.52.over), channel_id=1, source_target_pairs={{0,2},{2,0},{4,6},{6,4},{8,10},{10,8},{12,14},{14,12},{16,18},{18,... | collective-permute-start | bytes 1671176 | tf_op jit(solution)/shard_map/ppermute | solution.py:66
  41.1 3.9 %copy-start.2 = (bf16[2,384,2048]{2,1,0:T(8,128)(2,1)S(1)}, bf16[2,384,2048]{2,1,0:T(8,128)(2,1)}, u32[]{:S(2)}) copy-start(bf16[2,384,2048]{2,1,0:T(8,128)(2,1)} %w_down.3) | copy-start | bytes 9437188
  41.2 3.1 %collective-permute-start = (bf16[128,2048]{1,0:T(8,128)(2,1)S(1)}, bf16[128,2048]{1,0:T(8,128)(2,1)S(1)}, u32[]{:S(2)}, u32[]{:S(2)}) collective-permute-start(bf16[128,2048]{1,0:T(8,128)(2,1)S(1)} %copy-done.3), channel_id=1, source_target_pairs={{0,2},{2,0},{4,6},{6,4},{8,10},{10,8},{12,14},{14,12},{16,18},{18,... | collective-permute-start | bytes 1572872 | tf_op jit(solution)/shard_map/ppermute | solution.py:66
  41.8 3.2 %collective-permute-start.10 = (bf16[2,64,2048]{2,1,0:T(8,128)(2,1)S(1)}, bf16[2,64,2048]{2,1,0:T(8,128)(2,1)S(1)}, u32[]{:S(2)}, u32[]{:S(2)}) collective-permute-start(bf16[2,64,2048]{2,1,0:T(8,128)(2,1)S(1)} %join.2.diag), channel_id=1, source_target_pairs={{0,2},{2,0},{4,6},{6,4},{8,10},{10,8},{12,14},{14,12},{16,18},{18,... | collective-permute-start | bytes 1572872 | tf_op jit(solution)/shard_map/ppermute | solution.py:66
  43.1 1.9 %collective-permute-start.4 = (bf16[1,64,2176]{2,1,0:T(8,128)(2,1)S(1)}, bf16[1,64,2176]{2,1,0:T(8,128)(2,1)S(1)}, u32[]{:S(2)}, u32[]{:S(2)}) collective-permute-start(bf16[1,64,2176]{2,1,0:T(8,128)(2,1)S(1)} %collective-permute-done.3.side), channel_id=1, source_target_pairs={{0,2},{2,0},{4,6},{6,4},{8,10},{10,8},{12,14},{14,12},{16,18},{18,... | collective-permute-start | bytes 835592 | tf_op jit(solution)/shard_map/ppermute | solution.py:66
  45.0 4.2 %copy-start = (bf16[2,384,2048]{2,1,0:T(8,128)(2,1)S(1)}, bf16[2,384,2048]{2,1,0:T(8,128)(2,1)}, u32[]{:S(2)}) copy-start(bf16[2,384,2048]{2,1,0:T(8,128)(2,1)} %w_gate.7) | copy-start | bytes 9437188
  45.0 4.2 %copy-start.1 = (bf16[2,384,2048]{2,1,0:T(8,128)(2,1)S(1)}, bf16[2,384,2048]{2,1,0:T(8,128)(2,1)}, u32[]{:S(2)}) copy-start(bf16[2,384,2048]{2,1,0:T(8,128)(2,1)} %w_up.7) | copy-start | bytes 9437188
  51.5 10.2 %collective-permute-start.14 = (bf16[4,128,1024]{2,1,0:T(8,128)(2,1)S(1)}, bf16[4,128,1024]{2,1,0:T(8,128)(2,1)S(1)}, u32[]{:S(2)}, u32[]{:S(2)}) collective-permute-start(bf16[4,128,1024]{2,1,0:T(8,128)(2,1)S(1)} %get-tuple-element.63._), channel_id=1, source_target_pairs={{0,2},{2,0},{4,6},{6,4},{8,10},{10,8},{12,14},{14,12},{16,18},{18,... | collective-permute-start | bytes 3145736 | tf_op jit(solution)/shard_map/ppermute | solution.py:66
  53.7 6.6 %collective-permute-start.17 = (bf16[2,64,1024]{2,1,0:T(8,128)(2,1)S(1)}, bf16[2,64,1024]{2,1,0:T(8,128)(2,1)S(1)}, u32[]{:S(2)}, u32[]{:S(2)}) collective-permute-start(bf16[2,64,1024]{2,1,0:T(8,128)(2,1)S(1)} %get-tuple-element.64._), channel_id=1, source_target_pairs={{0,1},{1,0},{2,3},{3,2},{4,5},{5,4},{6,7},{7,6},{8,9},{9,8},{10,11... | collective-permute-start | bytes 786440 | tf_op jit(solution)/shard_map/ppermute | solution.py:66
  54.3 7.2 %collective-permute-start.18 = (bf16[2,64,1024]{2,1,0:T(8,128)(2,1)S(1)}, bf16[2,64,1024]{2,1,0:T(8,128)(2,1)S(1)}, u32[]{:S(2)}, u32[]{:S(2)}) collective-permute-start(bf16[2,64,1024]{2,1,0:T(8,128)(2,1)S(1)} %get-tuple-element.65), channel_id=1, source_target_pairs={{0,4},{2,6},{4,0},{6,2},{8,12},{10,14},{12,8},{14,10},{16,20},{18,... | collective-permute-start | bytes 786440 | tf_op jit(solution)/shard_map/ppermute | solution.py:66
  58.1 4.2 %collective-permute-start.20 = (bf16[4,128,1024]{2,1,0:T(8,128)(2,1)S(1)}, bf16[4,128,1024]{2,1,0:T(8,128)(2,1)S(1)}, u32[]{:S(2)}, u32[]{:S(2)}) collective-permute-start(bf16[4,128,1024]{2,1,0:T(8,128)(2,1)S(1)} %get-tuple-element.66.refs_0_), channel_id=1, source_target_pairs={{0,2},{2,0},{4,6},{6,4},{8,10},{10,8},{12,14},{14,12},{16,18},{18,... | collective-permute-start | bytes 3145736 | tf_op jit(solution)/shard_map/ppermute | solution.py:66
  58.2 4.9 %collective-permute-start.25 = (bf16[2,64,2176]{2,1,0:T(8,128)(2,1)S(1)}, bf16[2,64,2176]{2,1,0:T(8,128)(2,1)S(1)}, u32[]{:S(2)}, u32[]{:S(2)}) collective-permute-start(bf16[2,64,2176]{2,1,0:T(8,128)(2,1)S(1)} %stack.21._.lines), channel_id=1, source_target_pairs={{0,2},{2,0},{4,6},{6,4},{8,10},{10,8},{12,14},{14,12},{16,18},{18,... | collective-permute-start | bytes 1671176 | tf_op jit(solution)/shard_map/ppermute | solution.py:66
  60.4 5.5 %collective-permute-start.26 = (bf16[2,64,2176]{2,1,0:T(8,128)(2,1)S(1)}, bf16[2,64,2176]{2,1,0:T(8,128)(2,1)S(1)}, u32[]{:S(2)}, u32[]{:S(2)}) collective-permute-start(bf16[2,64,2176]{2,1,0:T(8,128)(2,1)S(1)} %collective-permute-done.16.side), channel_id=1, source_target_pairs={{0,2},{2,0},{4,6},{6,4},{8,10},{10,8},{12,14},{14,12},{16,18},{18,... | collective-permute-start | bytes 1671176 | tf_op jit(solution)/shard_map/ppermute | solution.py:66
  61.6 3.1 %collective-permute-start.27 = (bf16[2,64,2176]{2,1,0:T(8,128)(2,1)S(1)}, bf16[2,64,2176]{2,1,0:T(8,128)(2,1)S(1)}, u32[]{:S(2)}, u32[]{:S(2)}) collective-permute-start(bf16[2,64,2176]{2,1,0:T(8,128)(2,1)S(1)} %collective-permute-done.15.over), channel_id=1, source_target_pairs={{0,2},{2,0},{4,6},{6,4},{8,10},{10,8},{12,14},{14,12},{16,18},{18,... | collective-permute-start | bytes 1671176 | tf_op jit(solution)/shard_map/ppermute | solution.py:66
  61.6 4.2 %collective-permute-start.28 = (bf16[2,64,2048]{2,1,0:T(8,128)(2,1)S(1)}, bf16[2,64,2048]{2,1,0:T(8,128)(2,1)S(1)}, u32[]{:S(2)}, u32[]{:S(2)}) collective-permute-start(bf16[2,64,2048]{2,1,0:T(8,128)(2,1)S(1)} %join.3._.diag), channel_id=1, source_target_pairs={{0,2},{2,0},{4,6},{6,4},{8,10},{10,8},{12,14},{14,12},{16,18},{18,... | collective-permute-start | bytes 1572872 | tf_op jit(solution)/shard_map/ppermute | solution.py:66
  62.3 13.9 %collective-permute-start.19 = (bf16[4,64,1024]{2,1,0:T(8,128)(2,1)S(1)}, bf16[4,64,1024]{2,1,0:T(8,128)(2,1)S(1)}, u32[]{:S(2)}, u32[]{:S(2)}) collective-permute-start(bf16[4,64,1024]{2,1,0:T(8,128)(2,1)S(1)} %get-tuple-element.68._), channel_id=1, source_target_pairs={{0,1},{1,0},{2,3},{3,2},{4,5},{5,4},{6,7},{7,6},{8,9},{9,8},{10,11... | collective-permute-start | bytes 1572872 | tf_op jit(solution)/shard_map/ppermute | solution.py:66
  63.1 13.8 %collective-permute-start.21 = (bf16[2,128,1024]{2,1,0:T(8,128)(2,1)S(1)}, bf16[2,128,1024]{2,1,0:T(8,128)(2,1)S(1)}, u32[]{:S(2)}, u32[]{:S(2)}) collective-permute-start(bf16[2,128,1024]{2,1,0:T(8,128)(2,1)S(1)} %get-tuple-element.71._), channel_id=1, source_target_pairs={{0,4},{2,6},{4,0},{6,2},{8,12},{10,14},{12,8},{14,10},{16,20},{18,... | collective-permute-start | bytes 1572872 | tf_op jit(solution)/shard_map/ppermute | solution.py:66
  72.2 7.6 %collective-permute-start.29 = (bf16[4,128,1024]{2,1,0:T(8,128)(2,1)S(1)}, bf16[4,128,1024]{2,1,0:T(8,128)(2,1)S(1)}, u32[]{:S(2)}, u32[]{:S(2)}) collective-permute-start(bf16[4,128,1024]{2,1,0:T(8,128)(2,1)S(1)} %get-tuple-element.82._), channel_id=1, source_target_pairs={{0,2},{2,0},{4,6},{6,4},{8,10},{10,8},{12,14},{14,12},{16,18},{18,... | collective-permute-start | bytes 3145736 | tf_op jit(solution)/shard_map/ppermute | solution.py:66
  74.6 6.2 %collective-permute-start.31 = (bf16[4,128,1024]{2,1,0:T(8,128)(2,1)S(1)}, bf16[4,128,1024]{2,1,0:T(8,128)(2,1)S(1)}, u32[]{:S(2)}, u32[]{:S(2)}) collective-permute-start(bf16[4,128,1024]{2,1,0:T(8,128)(2,1)S(1)} %get-tuple-element.86), channel_id=1, source_target_pairs={{0,2},{2,0},{4,6},{6,4},{8,10},{10,8},{12,14},{14,12},{16,18},{18,... | collective-permute-start | bytes 3145736 | tf_op jit(solution)/shard_map/ppermute | solution.py:66
  77.0 9.3 %collective-permute-start.22 = (bf16[2,64,1024]{2,1,0:T(8,128)(2,1)S(1)}, bf16[2,64,1024]{2,1,0:T(8,128)(2,1)S(1)}, u32[]{:S(2)}, u32[]{:S(2)}) collective-permute-start(bf16[2,64,1024]{2,1,0:T(8,128)(2,1)S(1)} %get-tuple-element.73._), channel_id=1, source_target_pairs={{0,4},{2,6},{4,0},{6,2},{8,12},{10,14},{12,8},{14,10},{16,20},{18,... | collective-permute-start | bytes 786440 | tf_op jit(solution)/shard_map/ppermute | solution.py:66
  78.6 9.2 %collective-permute-start.23 = (bf16[2,64,1024]{2,1,0:T(8,128)(2,1)S(1)}, bf16[2,64,1024]{2,1,0:T(8,128)(2,1)S(1)}, u32[]{:S(2)}, u32[]{:S(2)}) collective-permute-start(bf16[2,64,1024]{2,1,0:T(8,128)(2,1)S(1)} %get-tuple-element.75), channel_id=1, source_target_pairs={{0,1},{1,0},{2,3},{3,2},{4,5},{5,4},{6,7},{7,6},{8,9},{9,8},{10,11... | collective-permute-start | bytes 786440 | tf_op jit(solution)/shard_map/ppermute | solution.py:66
  80.0 16.8 %collective-permute-start.30 = (bf16[4,64,1024]{2,1,0:T(8,128)(2,1)S(1)}, bf16[4,64,1024]{2,1,0:T(8,128)(2,1)S(1)}, u32[]{:S(2)}, u32[]{:S(2)}) collective-permute-start(bf16[4,64,1024]{2,1,0:T(8,128)(2,1)S(1)} %get-tuple-element.84._), channel_id=1, source_target_pairs={{0,1},{1,0},{2,3},{3,2},{4,5},{5,4},{6,7},{7,6},{8,9},{9,8},{10,11... | collective-permute-start | bytes 1572872 | tf_op jit(solution)/shard_map/ppermute | solution.py:66
  80.9 15.9 %collective-permute-start.32 = (bf16[2,128,1024]{2,1,0:T(8,128)(2,1)S(1)}, bf16[2,128,1024]{2,1,0:T(8,128)(2,1)S(1)}, u32[]{:S(2)}, u32[]{:S(2)}) collective-permute-start(bf16[2,128,1024]{2,1,0:T(8,128)(2,1)S(1)} %get-tuple-element.88), channel_id=1, source_target_pairs={{0,4},{2,6},{4,0},{6,2},{8,12},{10,14},{12,8},{14,10},{16,20},{18,... | collective-permute-start | bytes 1572872 | tf_op jit(solution)/shard_map/ppermute | solution.py:66
  88.0 10.6 %collective-permute-start.24 = (bf16[64,2048]{1,0:T(8,128)(2,1)S(1)}, bf16[64,2048]{1,0:T(8,128)(2,1)S(1)}, u32[]{:S(2)}, u32[]{:S(2)}) collective-permute-start(bf16[64,2048]{1,0:T(8,128)(2,1)S(1)} %get-tuple-element.77), channel_id=1, source_target_pairs={{0,16},{2,18},{4,20},{6,22},{8,24},{10,26},{12,28},{14,30},{16,0},... | collective-permute-start | bytes 786440 | tf_op jit(solution)/shard_map/ppermute | solution.py:71
  96.9 6.4 %collective-permute-start.33 = (bf16[2,64,1024]{2,1,0:T(8,128)(2,1)S(1)}, bf16[2,64,1024]{2,1,0:T(8,128)(2,1)S(1)}, u32[]{:S(2)}, u32[]{:S(2)}) collective-permute-start(bf16[2,64,1024]{2,1,0:T(8,128)(2,1)S(1)} %get-tuple-element.90), channel_id=1, source_target_pairs={{0,4},{2,6},{4,0},{6,2},{8,12},{10,14},{12,8},{14,10},{16,20},{18,... | collective-permute-start | bytes 786440 | tf_op jit(solution)/shard_map/ppermute | solution.py:66
  97.5 6.4 %collective-permute-start.34 = (bf16[2,64,1024]{2,1,0:T(8,128)(2,1)S(1)}, bf16[2,64,1024]{2,1,0:T(8,128)(2,1)S(1)}, u32[]{:S(2)}, u32[]{:S(2)}) collective-permute-start(bf16[2,64,1024]{2,1,0:T(8,128)(2,1)S(1)} %get-tuple-element.92), channel_id=1, source_target_pairs={{0,1},{1,0},{2,3},{3,2},{4,5},{5,4},{6,7},{7,6},{8,9},{9,8},{10,11... | collective-permute-start | bytes 786440 | tf_op jit(solution)/shard_map/ppermute | solution.py:66
  104.0 9.5 %collective-permute-start.35 = (bf16[64,2048]{1,0:T(8,128)(2,1)S(1)}, bf16[64,2048]{1,0:T(8,128)(2,1)S(1)}, u32[]{:S(2)}, u32[]{:S(2)}) collective-permute-start(bf16[64,2048]{1,0:T(8,128)(2,1)S(1)} %get-tuple-element.93), channel_id=1, source_target_pairs={{0,8},{2,10},{4,12},{6,14},{8,16},{10,18},{12,20},{14,22},{16,24},... | collective-permute-start | bytes 786440 | tf_op jit(solution)/shard_map/ppermute | solution.py:71
  106.0 10.1 %collective-permute-start.36 = (bf16[64,2048]{1,0:T(8,128)(2,1)S(1)}, bf16[64,2048]{1,0:T(8,128)(2,1)S(1)}, u32[]{:S(2)}, u32[]{:S(2)}) collective-permute-start(bf16[64,2048]{1,0:T(8,128)(2,1)S(1)} %get-tuple-element.94), channel_id=1, source_target_pairs={{0,24},{2,26},{4,28},{6,30},{8,0},{10,2},{12,4},{14,6},{16,8},{18,... | collective-permute-start | bytes 786440 | tf_op jit(solution)/shard_map/ppermute | solution.py:71

commit v8 on v7

--- a/solution.py
+++ b/solution.py
@@ -86,50 +86,28 @@
     )(*operands)
 
 
-def prepare_kernel(place, tokens, gates_any, ids_any, first, table, gates, ids, sems):
-    piece = first.shape[0]
-    width = first.shape[1] - table.shape[1]
-    near = pl.multiple_of(place[3] * piece, piece)
-    copies = [
-        pltpu.make_async_copy(gates_any, gates, sems.at[0]),
-        pltpu.make_async_copy(ids_any, ids, sems.at[1]),
-        pltpu.make_async_copy(
-            tokens.at[pl.ds(near, piece), :], first.at[:, pl.ds(0, width)], sems.at[2]
-        ),
-    ]
-    for copy in copies:
-        copy.start()
-    copies[0].wait()
-    copies[1].wait()
+def take_kernel(place, tokens, part):
+    near = pl.multiple_of(place[3] * part.shape[0], part.shape[0])
+    part[...] = tokens[pl.ds(near, part.shape[0]), :]
+
+
+def take(place, cotangent, piece):
+    return small(take_kernel, "take", [(piece, cotangent.shape[1])], "sv", (place, cotangent), limit=2)[0]
+
+
+def table_kernel(gates, ids, table):
+    count = gates.shape[0]
     rest = gates[...]
-    terms = []
-    for _ in range(3):
+    for i in range(3):
         term = rest.astype(jnp.bfloat16).astype(jnp.float32)
-        terms.append(term)
+        table[i * count:(i + 1) * count] = term.astype(jnp.bfloat16)
         rest = rest - term
-    terms.append(ids[...].astype(jnp.float32))
-    unused = piece - 4 * gates.shape[0]
-    terms.append(jnp.zeros((unused, gates.shape[1]), jnp.float32))
-    packed = jnp.concatenate(terms, axis=0).astype(jnp.bfloat16)
-    first[:, width:] = packed
-    table[...] = packed
-    copies[2].wait()
-
-
-def prepare(place, cotangent, gates, ids, piece):
-    return small(
-        prepare_kernel,
-        "prepare",
-        [(piece, cotangent.shape[1] + 128), (piece, 128)],
-        "shhh",
-        (place, cotangent, gates, ids),
-        [
-            pltpu.VMEM(gates.shape, jnp.float32),
-            pltpu.VMEM(ids.shape, jnp.int32),
-            pltpu.SemaphoreType.DMA((3,)),
-        ],
-        limit=60,
-    )
+    table[3 * count:] = ids[...].astype(jnp.float32).astype(jnp.bfloat16)
+
+
+def routing_table(gates, ids):
+    count, tokens = gates.shape
+    return small(table_kernel, "table", [(4 * count, tokens)], "vv", (gates, ids), limit=2)[0]
 
 
 def stack_kernel(*refs):
@@ -148,18 +126,18 @@
     )[0]
 
 
-def relay_kernel(came, part, line, following):
+def relay_kernel(came, part, _, __, line, following):
     line[0] = came[...]
     following[...] = part[...]
 
 
-def relay(came, part):
-    return small(
-        relay_kernel, "relay", [(1,) + came.shape, part.shape], "vv", (came, part)
-    )
-
-
-def turn_kernel(gate, up, _, gate_t, up_t):
+def relay(came, part, *after):
+    return small(
+        relay_kernel, "relay", [(1,) + came.shape, part.shape], "vvoo", (came, part, *after)
+    )
+
+
+def turn_kernel(gate, up, _, __, gate_t, up_t):
     tile = 128
     for source, target in ((gate, gate_t), (up, up_t)):
         for e in range(source.shape[0]):
@@ -169,31 +147,27 @@
                 )
 
 
-def turn(saved_gate, saved_up, after):
+def turn(saved_gate, saved_up, *after):
     count, units, slots = saved_gate.shape
     return small(
         turn_kernel,
         "turn",
         [(count, slots, units)] * 2,
-        "vvo",
-        (saved_gate, saved_up, after),
+        "vvoo",
+        (saved_gate, saved_up, *after),
         limit=12,
     )
 
 
-def corner_kernel(place, tokens, first, over, side, whole_over, left, right, sem):
+def corner_kernel(place, tokens, first, over, side, whole_over, left, right):
     _, piece, middle = left.shape
     far = pl.multiple_of((1 - place[3]) * piece, piece)
-    copy = pltpu.make_async_copy(
-        tokens.at[pl.ds(far, piece), pl.ds(middle, middle)], right.at[0], sem.at[0]
-    )
-    copy.start()
+    right[0] = tokens[pl.ds(far, piece), middle:]
     whole_over[0] = first[...]
     whole_over[1:] = over[...]
     left[0] = first[:, :middle]
     left[1:] = over[:, :, :middle]
     right[1:] = side[:, :, middle:2 * middle]
-    copy.wait()
 
 
 def own_corner(place, cotangent, first, over, side):
@@ -203,9 +177,8 @@
         corner_kernel,
         "own_corner",
         [(count + 1, piece, width)] + [(count + 1, piece, middle)] * 2,
-        "shvvv",
+        "svvvv",
         (place, cotangent, first, over, side),
-        (pltpu.SemaphoreType.DMA((1,)),),
     )
 
 
@@ -260,23 +233,13 @@
     return pl.multiple_of((line * 2 + row) * width, width)
 
 
-def route_kernel(offsets, capacity, place, own, own_c, lines, lines_c, over, over_c, pick, pick_t, gate,
-                 hits, gates):
+def route_kernel(offsets, capacity, place, table, table_c, pick, pick_t, gate, hits, gates):
     tokens = pick.shape[2] // 2
-    width = over.shape[2] - 128
     core, row, line, half = place[0], place[1], place[2], place[3]
     first = (line * 4 + row * 2 + core) * 2
     for i, r in enumerate(offsets):
         for ry in range(2):
-            tables = []
-            for c in range(2):
-                if ry == 1:
-                    table = (over, over_c)[c][i, :32, width:]
-                elif r == 0:
-                    table = (own, own_c)[c][:32]
-                else:
-                    table = (lines, lines_c)[c][r_place(r, offsets), :32, width:]
-                tables.append(table.astype(jnp.float32))
+            tables = [table[ry, r].astype(jnp.float32), table_c[ry, r].astype(jnp.float32)]
             swapped = core > 0
             ordered = [
                 jnp.where(swapped, tables[1], tables[0]), jnp.where(swapped, tables[0], tables[1])
@@ -327,8 +290,8 @@
         pick_t[p] = square.T[:, :count].astype(jnp.bfloat16)
 
 
-def route(offsets, place, table, table_c, lines, lines_c, over, over_c, capacity):
-    tokens = 2 * over.shape[1]
+def route(offsets, place, table, table_c, capacity):
+    tokens = table.shape[3]
     pairs = 2 * len(offsets)
     rows = 4 * capacity
     return small(
@@ -339,8 +302,8 @@
             (pairs, 2 * tokens, rows),
             jax.ShapeDtypeStruct((pairs, rows, 128), jnp.float32),
         ],
-        "s" + "v" * 6,
-        (place, table, table_c, lines, lines_c, over, over_c),
+        "svv",
+        (place, table, table_c),
         [pltpu.VMEM((4 * pairs, tokens), jnp.float32)] * 2,
     )
 
@@ -529,7 +492,7 @@
         ],
         "vvvvo",
         (left, came_l, right, came_r, after),
-        work=1 << 36,
+        work=2,
     )
 
 
@@ -550,54 +513,36 @@
     me, half = lax.axis_index("expert"), lax.axis_index("tp")
     place = jnp.stack([me % 2, me // 2 % 2, me // 4, half]).astype(jnp.int32)
 
-    part, table = prepare(place, cotangent, gates.T, expert_ids.T, piece)
+    part = take(place, cotangent, piece)
     first = swap(part, "expert", 2)
-    own_c, table_c = swap(cotangent, "expert", 1), swap(table, "expert", 1)
-    gathered, saved = [], None
+    own_c = swap(cotangent, "expert", 1)
+    table = routing_table(gates.T, expert_ids.T)
+    table = stack([table] + [along_line(table, -r) for r in range(1, lines)])
+    table = stack([table, swap(table, "expert", 2)])
+    table_c = swap(table, "expert", 1)
+    routes = [route(offsets, place, table, table_c, capacity) for offsets in CHUNKS]
+    gathered = []
 
     def compute(index, after):
-        offsets, moved = CHUNKS[index], gathered[index]
-        line, line_c, _, _, over, over_c = moved[:6]
-        pick, pick_t, gate = route(
-            offsets, place, table, table_c, line, line_c, over, over_c, capacity
+        pick, pick_t, gate = routes[index]
+        return hidden(
+            CHUNKS[index], lines, place, cotangent, own_c, gathered[index], pick, gate, w_down, saved, after
         )
-        grads = hidden(
-            offsets, lines, place, cotangent, own_c, moved, pick, gate, w_down, saved, after
-        )
-        return grads, pick_t
+
+    def both_cores(arrays):
+        return [each for array in arrays for each in (array, swap(array, "expert", 1))]
 
     def sums_by_token(offset, grads, pick_t, after, work=0):
         keep, send = sums(offset, middle, grads, w_gate, w_up, pick_t, after, work)
         return [keep, swap(send, "expert", 1)], send
 
-    for offsets in CHUNKS:
-        pieces = [along_line(part, -r) for r in offsets if r != 0]
-        if saved is None:
-            line, part = relay(pieces[0], part)
-            saved = turn(saved_gate, saved_up, line)
-        else:
-            line = stack(pieces, saved[0])
-        side, over = swap(line, "tp", 1), swap(line, "expert", 2)
-        if offsets[0] == 0:
-            over, left, right = own_corner(place, cotangent, first, over, side)
-            after = (left,)
-        else:
-            early = compute(0, line)
-            grads, pick_t = early
-            early_l, after = sums_by_token(0, grads, pick_t, grads)
-            left, right = corner(over, side, middle, after)
-            early_r, after = sums_by_token(middle, grads, pick_t, left, 68719476736)
-            after = (after,)
-        diag = join(swap(left, "tp", 1), swap(right, "expert", 2), *after, work=8589934592)
-        moved = []
-        for array in (line, side, over, diag):
-            moved += [array, swap(array, "expert", 1)]
-        gathered.append(moved)
-
-    def first_step(keep_l, came_l, keep_r, came_r, after):
-        send_l, keep_l = first_left(keep_l, came_l, after)
-        send_r, keep_r = first_right(keep_r, came_r, send_l)
-        return keep_l, swap(send_l, "tp", 1), keep_r, swap(send_r, "expert", 2), send_r
+    def step_left(keep, came, after):
+        send, keep = first_left(keep, came, after)
+        return keep, swap(send, "tp", 1), send
+
+    def step_right(keep, came, after):
+        send, keep = first_right(keep, came, after)
+        return keep, swap(send, "expert", 2), send
 
     def second_step(offsets, sums_of_two, after, came):
         send_l, left, send_r, right = second_sum(*sums_of_two, after)
@@ -605,13 +550,33 @@
         rows = third_sum(offsets, left, came_l, right, came_r, send_l if came is None else came)
         return rows[0], [row if r == 0 else along_line(row, r) for r, row in zip(offsets, rows)], send_l
 
-    early = first_step(*early_l, *early_r, gathered[1][6])
-    grads, pick_t = compute(1, early[4])
-    late_l, after = sums_by_token(0, grads, pick_t, grads)
-    late_r, _ = sums_by_token(middle, grads, pick_t, after)
-    done, early, after = second_step(CHUNKS[0], early[:4], early[4], None)
-    late = first_step(*late_l, *late_r, after)
-    _, late, _ = second_step(CHUNKS[1], late[:4], done, early[-1])
+    (_, near), (third, second) = CHUNKS
+    line, part = relay(along_line(part, -near), part, table_c, first)
+    side, over = swap(line, "tp", 1), swap(line, "expert", 2)
+    came = [along_line(part, -third), along_line(part, -second)]
+    saved = turn(saved_gate, saved_up, routes[0][0], routes[1][0])
+    over, left, right = own_corner(place, cotangent, first, over, side)
+    left, right = swap(left, "tp", 1), swap(right, "expert", 2)
+    later = stack(came, saved[0])
+    gathered.append(both_cores([line, side, over, join(left, right, later)]))
+
+    line, side, over = later, swap(later, "tp", 1), swap(later, "expert", 2)
+    grads = compute(0, line)
+    early_l, after = sums_by_token(0, grads, routes[0][1], grads)
+    left, right = corner(over, side, middle, after)
+    early_r, after = sums_by_token(middle, grads, routes[0][1], left, 68719476736)
+    left, right = swap(left, "tp", 1), swap(right, "expert", 2)
+    gathered.append(both_cores([line, side, over, join(left, right, after, work=8589934592)]))
+
+    early_l = step_left(*early_l, gathered[1][6])
+    early_r = step_right(*early_r, early_l[-1])
+    grads = compute(1, early_r[-1])
+    late_l, after = sums_by_token(0, grads, routes[1][1], grads)
+    late_r, after = sums_by_token(middle, grads, routes[1][1], after)
+    done, early, after = second_step(CHUNKS[0], early_l[:2] + early_r[:2], early_r[-1], None)
+    late_l = step_left(*late_l, after)
+    late_r = step_right(*late_r, late_l[-1])
+    _, late, _ = second_step(CHUNKS[1], late_l[:2] + late_r[:2], done, early[-1])
     terms = early + late
     return pl.pallas_call(
         last_kernel,

time: 117 us -> 131 us (1.12)
  waiting for transfers between devices: 54.6 us -> 65 us
  starting transfers between devices: 33.2 us -> 40 us
  Pallas kernels: 25.3 us -> 23.5 us
    ppermute x6 -> x9, waiting for transfers between devices: 23.6 us -> 29.2 us  [along_line(): lax.ppermute(value, 'expert', [(i, (i + 4 * shift) % count) for i in rang...]
    ppermute x6 -> x9, starting transfers between devices: 11.8 us -> 17.3 us  [along_line(): lax.ppermute(value, 'expert', [(i, (i + 4 * shift) % count) for i in rang...]
    ppermute x31 -> x32, waiting for transfers between devices: 31 us -> 35.8 us  [swap(): return lax.ppermute(value, axis, [(i, i ^ step) for i in range(count)])]
    pallas_call x24 -> x27, Pallas kernels: 24.4 us -> 22.6 us  [small(): pl.pallas_call(kernel, out_shape=[out if hasattr(out, 'dtype') else jax.S...]
    ppermute x31 -> x32, starting transfers between devices: 21.5 us -> 22.7 us  [swap(): return lax.ppermute(value, axis, [(i, i ^ step) for i in range(count)])]
    unnamed x20 -> x18, local copies, waits for them, and re-layouts: 2.92 us -> 2.45 us
  transfers between devices with their start and end apart: 37 -> 41, of which waited for: 19 -> 22; matrix products, arithmetic and copies ran while one was open for 0% -> 0% of each run, Pallas kernels for 19% -> 17%
where the time goes in v8:
time: 131 us
  waiting for transfers between devices  65 us (50%)
  starting transfers between devices  40 us (31%)
  Pallas kernels  23.5 us (18%)
  local copies, waits for them, and re-layouts  2.45 us (2%)
    ppermute x32, waiting for transfers between devices, swap(): return lax.ppermute(value, axis, [(i, i ^ step) for i in range(count)])  35.8 us
    ppermute x9, waiting for transfers between devices, along_line(): lax.ppermute(value, 'expert', [(i, (i + 4 * shift) % count) for i in rang...  29.2 us
    ppermute x32, starting transfers between devices, swap(): return lax.ppermute(value, axis, [(i, i ^ step) for i in range(count)])  22.7 us
    pallas_call x27, Pallas kernels, small(): pl.pallas_call(kernel, out_shape=[out if hasattr(out, 'dtype') else jax.S...  22.6 us
    ppermute x9, starting transfers between devices, along_line(): lax.ppermute(value, 'expert', [(i, (i + 4 * shift) % count) for i in rang...  17.3 us
  transfers between devices with their start and end apart: 41, of which 22 were waited for; matrix products, arithmetic and copies ran while one was open for 0% of the time, Pallas kernels for 17%

profile of v8, /device:TPU:0, one launch (start us, length us, event | category | flops | bytes accessed | tf_op | source)
XLA Modules:
  0.0 131.3 jit_solution(12419618100433618466)
XLA Ops:
  0.1 1.0 copy-done.3
  1.1 0.6 take.1.part
  1.7 4.1 %collective-permute-start.1 = (bf16[64,2048]{1,0:T(8,128)(2,1)S(1)}, bf16[64,2048]{1,0:T(8,128)(2,1)S(1)}, u32[]{:S(2)}, u32[]{:S(2)}) collective-permute-start(bf16[64,2048]{1,0:T(8,128)(2,1)S(1)} %take.1.part), channel_id=1, source_target_pairs={{0,16},{2,18},{4,20},{6,22},{8,24},{10,26},{12,28},{14,30},{16,0},... | collective-permute-start | bytes 786440 | tf_op jit(solution)/shard_map/ppermute | solution.py:71
  5.8 1.5 %collective-permute-start.7 = (bf16[64,2048]{1,0:T(8,128)(2,1)S(1)}, bf16[64,2048]{1,0:T(8,128)(2,1)S(1)}, u32[]{:S(2)}, u32[]{:S(2)}) collective-permute-start(bf16[64,2048]{1,0:T(8,128)(2,1)S(1)} %take.1.part), channel_id=1, source_target_pairs={{0,4},{2,6},{4,0},{6,2},{8,12},{10,14},{12,8},{14,10},{16,20},{18,... | collective-permute-start | bytes 786440 | tf_op jit(solution)/shard_map/ppermute | solution.py:66
  7.3 0.7 copy-done.7
  8.0 0.7 copy-done.8
  8.7 1.3 %collective-permute-start.2 = (bf16[32,128]{1,0:T(8,128)(2,1)S(1)}, bf16[32,128]{1,0:T(8,128)(2,1)S(1)}, u32[]{:S(2)}, u32[]{:S(2)}) collective-permute-start(bf16[32,128]{1,0:T(8,128)(2,1)S(1)} %table.1.refs_0_), channel_id=1, source_target_pairs={{0,24},{2,26},{4,28},{6,30},{8,0},{10,2},{12,4},{14,6},{16,8},{18,... | collective-permute-start | bytes 24584 | tf_op jit(solution)/shard_map/ppermute | solution.py:71
  10.0 1.7 %collective-permute-start.3 = (bf16[32,128]{1,0:T(8,128)(2,1)S(1)}, bf16[32,128]{1,0:T(8,128)(2,1)S(1)}, u32[]{:S(2)}, u32[]{:S(2)}) collective-permute-start(bf16[32,128]{1,0:T(8,128)(2,1)S(1)} %table.1.refs_0_), channel_id=1, source_target_pairs={{0,16},{2,18},{4,20},{6,22},{8,24},{10,26},{12,28},{14,30},{16,0},... | collective-permute-start | bytes 24584 | tf_op jit(solution)/shard_map/ppermute | solution.py:71
  11.7 0.6 collective-permute-done.2.refs_1_
  12.4 6.1 %collective-permute-done.3.refs_2_ = bf16[32,128]{1,0:T(8,128)(2,1)S(1)} collective-permute-done((bf16[32,128]{1,0:T(8,128)(2,1)S(1)}, bf16[32,128]{1,0:T(8,128)(2,1)S(1)}, u32[]{:S(2)}, u32[]{:S(2)}) %collective-permute-start.3) | collective-permute-done | bytes 8224 | tf_op jit(solution)/shard_map/ppermute | solution.py:71
  18.4 1.6 %collective-permute-start.5 = (bf16[4,32,128]{2,1,0:T(8,128)(2,1)S(1)}, bf16[4,32,128]{2,1,0:T(8,128)(2,1)S(1)}, u32[]{:S(2)}, u32[]{:S(2)}) collective-permute-start(bf16[4,32,128]{2,1,0:T(8,128)(2,1)S(1)} %stack.23.refs_0_), channel_id=1, source_target_pairs={{0,4},{2,6},{4,0},{6,2},{8,12},{10,14},{12,8},{14,10},{16,20},{18,... | collective-permute-start | bytes 98312 | tf_op jit(solution)/shard_map/ppermute | solution.py:66
  20.0 2.3 %collective-permute-done.5.refs_1_ = bf16[4,32,128]{2,1,0:T(8,128)(2,1)S(1)} collective-permute-done((bf16[4,32,128]{2,1,0:T(8,128)(2,1)S(1)}, bf16[4,32,128]{2,1,0:T(8,128)(2,1)S(1)}, u32[]{:S(2)}, u32[]{:S(2)}) %collective-permute-start.5) | collective-permute-done | bytes 32800 | tf_op jit(solution)/shard_map/ppermute | solution.py:66
  22.4 1.2 collective-permute-done.6._.table_c
  23.7 1.6 %collective-permute-start.11 = (bf16[1,64,2048]{2,1,0:T(8,128)(2,1)S(1)}, bf16[1,64,2048]{2,1,0:T(8,128)(2,1)S(1)}, u32[]{:S(2)}, u32[]{:S(2)}) collective-permute-start(bf16[1,64,2048]{2,1,0:T(8,128)(2,1)S(1)} %get-tuple-element.48.lines), channel_id=1, source_target_pairs={{0,4},{2,6},{4,0},{6,2},{8,12},{10,14},{12,8},{14,10},{16,20},{18,... | collective-permute-start | bytes 786440 | tf_op jit(solution)/shard_map/ppermute | solution.py:66
  25.4 1.5 %collective-permute-start.9 = (bf16[1,64,2048]{2,1,0:T(8,128)(2,1)S(1)}, bf16[1,64,2048]{2,1,0:T(8,128)(2,1)S(1)}, u32[]{:S(2)}, u32[]{:S(2)}) collective-permute-start(bf16[1,64,2048]{2,1,0:T(8,128)(2,1)S(1)} %get-tuple-element.48.lines), channel_id=1, source_target_pairs={{0,1},{1,0},{2,3},{3,2},{4,5},{5,4},{6,7},{7,6},{8,9},{9,8},{10,11... | collective-permute-start | bytes 786440 | tf_op jit(solution)/shard_map/ppermute | solution.py:66
  26.9 3.4 %collective-permute-start.15 = (bf16[64,2048]{1,0:T(8,128)(2,1)S(1)}, bf16[64,2048]{1,0:T(8,128)(2,1)S(1)}, u32[]{:S(2)}, u32[]{:S(2)}) collective-permute-start(bf16[64,2048]{1,0:T(8,128)(2,1)S(1)} %get-tuple-element.52), channel_id=1, source_target_pairs={{0,24},{2,26},{4,28},{6,30},{8,0},{10,2},{12,4},{14,6},{16,8},{18,... | collective-permute-start | bytes 786440 | tf_op jit(solution)/shard_map/ppermute | solution.py:71
  30.3 1.9 %collective-permute-done.11.over = bf16[1,64,2048]{2,1,0:T(8,128)(2,1)S(1)} collective-permute-done((bf16[1,64,2048]{2,1,0:T(8,128)(2,1)S(1)}, bf16[1,64,2048]{2,1,0:T(8,128)(2,1)S(1)}, u32[]{:S(2)}, u32[]{:S(2)}) %collective-permute-start.11) | collective-permute-done | bytes 262176 | tf_op jit(solution)/shard_map/ppermute | solution.py:66
  32.2 1.3 collective-permute-done.9.side
  33.5 0.6 own_corner.1
  34.1 1.6 %collective-permute-start.13 = (bf16[2,64,1024]{2,1,0:T(8,128)(2,1)S(1)}, bf16[2,64,1024]{2,1,0:T(8,128)(2,1)S(1)}, u32[]{:S(2)}, u32[]{:S(2)}) collective-permute-start(bf16[2,64,1024]{2,1,0:T(8,128)(2,1)S(1)} %get-tuple-element.50), channel_id=1, source_target_pairs={{0,1},{1,0},{2,3},{3,2},{4,5},{5,4},{6,7},{7,6},{8,9},{9,8},{10,11... | collective-permute-start | bytes 786440 | tf_op jit(solution)/shard_map/ppermute | solution.py:66
  35.6 0.5 collective-permute-start.14
  36.1 0.9 collective-permute-done.15.refs_0_
  37.0 1.1 route.2
  38.1 1.1 route.3
  39.3 0.7 turn.1
  39.9 2.4 %collective-permute-done.16.refs_1_ = bf16[64,2048]{1,0:T(8,128)(2,1)S(1)} collective-permute-done((bf16[64,2048]{1,0:T(8,128)(2,1)S(1)}, bf16[64,2048]{1,0:T(8,128)(2,1)S(1)}, u32[]{:S(2)}, u32[]{:S(2)}) %collective-permute-start.16) | collective-permute-done | bytes 262176 | tf_op jit(solution)/shard_map/ppermute | solution.py:71
  42.6 0.4 collective-permute-start.17
  43.0 0.5 collective-permute-start.19
  43.5 0.5 collective-permute-start.20
  44.0 1.5 %collective-permute-done.10.side_c = bf16[1,64,2048]{2,1,0:T(8,128)(2,1)S(1)} collective-permute-done((bf16[1,64,2048]{2,1,0:T(8,128)(2,1)S(1)}, bf16[1,64,2048]{2,1,0:T(8,128)(2,1)S(1)}, u32[]{:S(2)}, u32[]{:S(2)}) %collective-permute-start.10) | collective-permute-done | bytes 262176 | tf_op jit(solution)/shard_map/ppermute | solution.py:66
  45.6 4.2 %hidden.2.grads._ = bf16[2,384,768]{2,1,0:T(8,128)(2,1)S(1)} custom-call(s32[4]{0:T(128)S(1)} %pad_add_fusion.place, bf16[128,2048]{1,0:T(8,128)(2,1)S(1)} %copy-done.4, bf16[128,2048]{1,0:T(8,128)(2,1)S(1)} %collective-permute-done.own_c, bf16[1,64,2048]{2,1,0:T(8,128)(2,1)S(1)} %get-tuple-element.48.lines, ...), custom_call_target="tpu_custom_call" | custom-call | tf_op jit(solution)/shard_map/hidden/pallas_call | solution.py:76
  49.9 2.2 %sums.4 = (bf16[4,128,1024]{2,1,0:T(8,128)(2,1)S(1)}, bf16[4,128,1024]{2,1,0:T(8,128)(2,1)S(1)}) custom-call(bf16[2,384,768]{2,1,0:T(8,128)(2,1)S(1)} %hidden.2.grads._, bf16[2,384,2048]{2,1,0:T(8,128)(2,1)S(1)} %copy-done, bf16[2,384,2048]{2,1,0:T(8,128)(2,1)S(1)} %copy-done.1, bf16[4,256,192]{2,1,0:T(8,128)(2,1)S(1)} %get-tuple-element.58.pick_t, ...), custom_call_target="tpu_custom_call" | custom-call | tf_op jit(solution)/shard_map/sums/pallas_call | solution.py:76
  52.3 4.7 %collective-permute-done.19.over = bf16[2,64,2048]{2,1,0:T(8,128)(2,1)S(1)} collective-permute-done((bf16[2,64,2048]{2,1,0:T(8,128)(2,1)S(1)}, bf16[2,64,2048]{2,1,0:T(8,128)(2,1)S(1)}, u32[]{:S(2)}, u32[]{:S(2)}) %collective-permute-start.19) | collective-permute-done | bytes 524320 | tf_op jit(solution)/shard_map/ppermute | solution.py:66
  57.0 0.3 collective-permute-done.20.side
  57.4 0.6 collective-permute-start.21
  58.0 1.4 %collective-permute-start.22 = (bf16[2,64,1024]{2,1,0:T(8,128)(2,1)S(1)}, bf16[2,64,1024]{2,1,0:T(8,128)(2,1)S(1)}, u32[]{:S(2)}, u32[]{:S(2)}) collective-permute-start(bf16[2,64,1024]{2,1,0:T(8,128)(2,1)S(1)} %get-tuple-element.62), channel_id=1, source_target_pairs={{0,4},{2,6},{4,0},{6,2},{8,12},{10,14},{12,8},{14,10},{16,20},{18,... | collective-permute-start | bytes 786440 | tf_op jit(solution)/shard_map/ppermute | solution.py:66
  59.4 2.2 %sums.5 = (bf16[4,128,1024]{2,1,0:T(8,128)(2,1)S(1)}, bf16[4,128,1024]{2,1,0:T(8,128)(2,1)S(1)}) custom-call(bf16[2,384,768]{2,1,0:T(8,128)(2,1)S(1)} %hidden.2.grads._, bf16[2,384,2048]{2,1,0:T(8,128)(2,1)S(1)} %copy-done, bf16[2,384,2048]{2,1,0:T(8,128)(2,1)S(1)} %copy-done.1, bf16[4,256,192]{2,1,0:T(8,128)(2,1)S(1)} %get-tuple-element.58.pick_t, ...), custom_call_target="tpu_custom_call" | custom-call | flops 68719476736 | bytes 268435456 | tf_op jit(solution)/shard_map/sums/pallas_call | solution.py:76
  61.7 0.5 collective-permute-start.29
  62.2 2.6 %collective-permute-done.21.left = bf16[2,64,1024]{2,1,0:T(8,128)(2,1)S(1)} collective-permute-done((bf16[2,64,1024]{2,1,0:T(8,128)(2,1)S(1)}, bf16[2,64,1024]{2,1,0:T(8,128)(2,1)S(1)}, u32[]{:S(2)}, u32[]{:S(2)}) %collective-permute-start.21) | collective-permute-done | bytes 262176 | tf_op jit(solution)/shard_map/ppermute | solution.py:66
  65.4 0.3 collective-permute-start.32
  66.0 1.4 %collective-permute-start.25 = (bf16[2,128,1024]{2,1,0:T(8,128)(2,1)S(1)}, bf16[2,128,1024]{2,1,0:T(8,128)(2,1)S(1)}, u32[]{:S(2)}, u32[]{:S(2)}) collective-permute-start(bf16[2,128,1024]{2,1,0:T(8,128)(2,1)S(1)} %get-tuple-element.68._), channel_id=1, source_target_pairs={{0,4},{2,6},{4,0},{6,2},{8,12},{10,14},{12,8},{14,10},{16,20},{18,... | collective-permute-start | bytes 1572872 | tf_op jit(solution)/shard_map/ppermute | solution.py:66
  67.4 1.5 %collective-permute-start.23 = (bf16[4,64,1024]{2,1,0:T(8,128)(2,1)S(1)}, bf16[4,64,1024]{2,1,0:T(8,128)(2,1)S(1)}, u32[]{:S(2)}, u32[]{:S(2)}) collective-permute-start(bf16[4,64,1024]{2,1,0:T(8,128)(2,1)S(1)} %get-tuple-element.65._), channel_id=1, source_target_pairs={{0,1},{1,0},{2,3},{3,2},{4,5},{5,4},{6,7},{7,6},{8,9},{9,8},{10,11... | collective-permute-start | bytes 1572872 | tf_op jit(solution)/shard_map/ppermute | solution.py:66
  68.9 4.2 %hidden.3.grads._ = bf16[2,384,768]{2,1,0:T(8,128)(2,1)S(1)} custom-call(s32[4]{0:T(128)S(1)} %pad_add_fusion.place, bf16[128,2048]{1,0:T(8,128)(2,1)S(1)} %copy-done.4, bf16[128,2048]{1,0:T(8,128)(2,1)S(1)} %collective-permute-done.own_c, bf16[2,64,2048]{2,1,0:T(8,128)(2,1)S(1)} %stack.25.refs_0_._.lines, ...), custom_call_target="tpu_custom_call" | custom-call | tf_op jit(solution)/shard_map/hidden/pallas_call | solution.py:76
  73.0 2.2 %sums.6 = (bf16[4,128,1024]{2,1,0:T(8,128)(2,1)S(1)}, bf16[4,128,1024]{2,1,0:T(8,128)(2,1)S(1)}) custom-call(bf16[2,384,768]{2,1,0:T(8,128)(2,1)S(1)} %hidden.3.grads._, bf16[2,384,2048]{2,1,0:T(8,128)(2,1)S(1)} %copy-done, bf16[2,384,2048]{2,1,0:T(8,128)(2,1)S(1)} %copy-done.1, bf16[4,256,192]{2,1,0:T(8,128)(2,1)S(1)} %get-tuple-element.76.pick_t, ...), custom_call_target="tpu_custom_call" | custom-call | tf_op jit(solution)/shard_map/sums/pallas_call | solution.py:76
  75.3 2.2 %sums.7 = (bf16[4,128,1024]{2,1,0:T(8,128)(2,1)S(1)}, bf16[4,128,1024]{2,1,0:T(8,128)(2,1)S(1)}) custom-call(bf16[2,384,768]{2,1,0:T(8,128)(2,1)S(1)} %hidden.3.grads._, bf16[2,384,2048]{2,1,0:T(8,128)(2,1)S(1)} %copy-done, bf16[2,384,2048]{2,1,0:T(8,128)(2,1)S(1)} %copy-done.1, bf16[4,256,192]{2,1,0:T(8,128)(2,1)S(1)} %get-tuple-element.76.pick_t, ...), custom_call_target="tpu_custom_call" | custom-call | tf_op jit(solution)/shard_map/sums/pallas_call | solution.py:76
  77.6 0.5 collective-permute-start.35
  78.1 2.0 %collective-permute-done.25.came_r = bf16[2,128,1024]{2,1,0:T(8,128)(2,1)S(1)} collective-permute-done((bf16[2,128,1024]{2,1,0:T(8,128)(2,1)S(1)}, bf16[2,128,1024]{2,1,0:T(8,128)(2,1)S(1)}, u32[]{:S(2)}, u32[]{:S(2)}) %collective-permute-start.25) | collective-permute-done | bytes 524320 | tf_op jit(solution)/shard_map/ppermute | solution.py:66
  80.1 1.0 collective-permute-done.23.came_l
  81.4 0.4 collective-permute-done.35.came
  81.9 0.8 collective-permute-start.36
  82.7 1.0 collective-permute-start.34
  83.6 1.2 collective-permute-start.26
  84.9 1.1 collective-permute-start.27
  86.0 15.5 %collective-permute-done.26.came_l = bf16[2,64,1024]{2,1,0:T(8,128)(2,1)S(1)} collective-permute-done((bf16[2,64,1024]{2,1,0:T(8,128)(2,1)S(1)}, bf16[2,64,1024]{2,1,0:T(8,128)(2,1)S(1)}, u32[]{:S(2)}, u32[]{:S(2)}) %collective-permute-start.26) | collective-permute-done | bytes 262176 | tf_op jit(solution)/shard_map/ppermute | solution.py:66
  101.5 0.4 collective-permute-done.27.came_r
  102.1 2.9 %collective-permute-start.28 = (bf16[64,2048]{1,0:T(8,128)(2,1)S(1)}, bf16[64,2048]{1,0:T(8,128)(2,1)S(1)}, u32[]{:S(2)}, u32[]{:S(2)}) collective-permute-start(bf16[64,2048]{1,0:T(8,128)(2,1)S(1)} %get-tuple-element.74), channel_id=1, source_target_pairs={{0,16},{2,18},{4,20},{6,22},{8,24},{10,26},{12,28},{14,30},{16,0},... | collective-permute-start | bytes 786440 | tf_op jit(solution)/shard_map/ppermute | solution.py:71
  105.1 1.4 %collective-permute-start.37 = (bf16[2,64,1024]{2,1,0:T(8,128)(2,1)S(1)}, bf16[2,64,1024]{2,1,0:T(8,128)(2,1)S(1)}, u32[]{:S(2)}, u32[]{:S(2)}) collective-permute-start(bf16[2,64,1024]{2,1,0:T(8,128)(2,1)S(1)} %get-tuple-element.86), channel_id=1, source_target_pairs={{0,4},{2,6},{4,0},{6,2},{8,12},{10,14},{12,8},{14,10},{16,20},{18,... | collective-permute-start | bytes 786440 | tf_op jit(solution)/shard_map/ppermute | solution.py:66
  106.5 0.5 collective-permute-start.38
  107.1 9.0 %collective-permute-done.28._.refs_1_ = bf16[64,2048]{1,0:T(8,128)(2,1)S(1)} collective-permute-done((bf16[64,2048]{1,0:T(8,128)(2,1)S(1)}, bf16[64,2048]{1,0:T(8,128)(2,1)S(1)}, u32[]{:S(2)}, u32[]{:S(2)}) %collective-permute-start.28) | collective-permute-done | bytes 262176 | tf_op jit(solution)/shard_map/ppermute | solution.py:71
  116.2 0.7 collective-permute-start.39
  116.9 3.2 %collective-permute-start.40 = (bf16[64,2048]{1,0:T(8,128)(2,1)S(1)}, bf16[64,2048]{1,0:T(8,128)(2,1)S(1)}, u32[]{:S(2)}, u32[]{:S(2)}) collective-permute-start(bf16[64,2048]{1,0:T(8,128)(2,1)S(1)} %get-tuple-element.90), channel_id=1, source_target_pairs={{0,24},{2,26},{4,28},{6,30},{8,0},{10,2},{12,4},{14,6},{16,8},{18,... | collective-permute-start | bytes 786440 | tf_op jit(solution)/shard_map/ppermute | solution.py:71
  120.1 7.2 %collective-permute-done.39.refs_2_ = bf16[64,2048]{1,0:T(8,128)(2,1)S(1)} collective-permute-done((bf16[64,2048]{1,0:T(8,128)(2,1)S(1)}, bf16[64,2048]{1,0:T(8,128)(2,1)S(1)}, u32[]{:S(2)}, u32[]{:S(2)}) %collective-permute-start.39) | collective-permute-done | bytes 262176 | tf_op jit(solution)/shard_map/ppermute | solution.py:71
  127.3 3.0 %collective-permute-done.40.refs_3_ = bf16[64,2048]{1,0:T(8,128)(2,1)S(1)} collective-permute-done((bf16[64,2048]{1,0:T(8,128)(2,1)S(1)}, bf16[64,2048]{1,0:T(8,128)(2,1)S(1)}, u32[]{:S(2)}, u32[]{:S(2)}) %collective-permute-start.40) | collective-permute-done | bytes 262176 | tf_op jit(solution)/shard_map/ppermute | solution.py:71
  130.4 0.9 last_sum.1
  (65 shorter events, 2.4 us)
Async XLA Ops:
  0.1 1.0 copy-start.3
  1.1 29.1 %copy-start.4 = (bf16[128,2048]{1,0:T(8,128)(2,1)S(1)}, bf16[128,2048]{1,0:T(8,128)(2,1)}, u32[]{:S(2)}) copy-start(bf16[128,2048]{1,0:T(8,128)(2,1)} %own.3) | copy-start | bytes 1572868
  1.7 22.0 %collective-permute-start.1 = (bf16[64,2048]{1,0:T(8,128)(2,1)S(1)}, bf16[64,2048]{1,0:T(8,128)(2,1)S(1)}, u32[]{:S(2)}, u32[]{:S(2)}) collective-permute-start(bf16[64,2048]{1,0:T(8,128)(2,1)S(1)} %take.1.part), channel_id=1, source_target_pairs={{0,16},{2,18},{4,20},{6,22},{8,24},{10,26},{12,28},{14,30},{16,0},... | collective-permute-start | bytes 786440 | tf_op jit(solution)/shard_map/ppermute | solution.py:71
  5.8 17.9 %collective-permute-start.7 = (bf16[64,2048]{1,0:T(8,128)(2,1)S(1)}, bf16[64,2048]{1,0:T(8,128)(2,1)S(1)}, u32[]{:S(2)}, u32[]{:S(2)}) collective-permute-start(bf16[64,2048]{1,0:T(8,128)(2,1)S(1)} %take.1.part), channel_id=1, source_target_pairs={{0,4},{2,6},{4,0},{6,2},{8,12},{10,14},{12,8},{14,10},{16,20},{18,... | collective-permute-start | bytes 786440 | tf_op jit(solution)/shard_map/ppermute | solution.py:66
  7.3 0.7 copy-start.7
  8.0 0.7 copy-start.8
  8.7 3.7 %collective-permute-start.2 = (bf16[32,128]{1,0:T(8,128)(2,1)S(1)}, bf16[32,128]{1,0:T(8,128)(2,1)S(1)}, u32[]{:S(2)}, u32[]{:S(2)}) collective-permute-start(bf16[32,128]{1,0:T(8,128)(2,1)S(1)} %table.1.refs_0_), channel_id=1, source_target_pairs={{0,24},{2,26},{4,28},{6,30},{8,0},{10,2},{12,4},{14,6},{16,8},{18,... | collective-permute-start | bytes 24584 | tf_op jit(solution)/shard_map/ppermute | solution.py:71
  10.0 8.4 %collective-permute-start.3 = (bf16[32,128]{1,0:T(8,128)(2,1)S(1)}, bf16[32,128]{1,0:T(8,128)(2,1)S(1)}, u32[]{:S(2)}, u32[]{:S(2)}) collective-permute-start(bf16[32,128]{1,0:T(8,128)(2,1)S(1)} %table.1.refs_0_), channel_id=1, source_target_pairs={{0,16},{2,18},{4,20},{6,22},{8,24},{10,26},{12,28},{14,30},{16,0},... | collective-permute-start | bytes 24584 | tf_op jit(solution)/shard_map/ppermute | solution.py:71
  11.7 6.7 %collective-permute-start.4 = (bf16[32,128]{1,0:T(8,128)(2,1)S(1)}, bf16[32,128]{1,0:T(8,128)(2,1)S(1)}, u32[]{:S(2)}, u32[]{:S(2)}) collective-permute-start(bf16[32,128]{1,0:T(8,128)(2,1)S(1)} %table.1.refs_0_), channel_id=1, source_target_pairs={{0,8},{2,10},{4,12},{6,14},{8,16},{10,18},{12,20},{14,22},{16,24},... | collective-permute-start | bytes 24584 | tf_op jit(solution)/shard_map/ppermute | solution.py:71
  18.4 3.9 %collective-permute-start.5 = (bf16[4,32,128]{2,1,0:T(8,128)(2,1)S(1)}, bf16[4,32,128]{2,1,0:T(8,128)(2,1)S(1)}, u32[]{:S(2)}, u32[]{:S(2)}) collective-permute-start(bf16[4,32,128]{2,1,0:T(8,128)(2,1)S(1)} %stack.23.refs_0_), channel_id=1, source_target_pairs={{0,4},{2,6},{4,0},{6,2},{8,12},{10,14},{12,8},{14,10},{16,20},{18,... | collective-permute-start | bytes 98312 | tf_op jit(solution)/shard_map/ppermute | solution.py:66
  22.4 16.9 %copy-start.5 = (bf16[2,384,768]{2,1,0:T(8,128)(2,1)S(1)}, bf16[2,384,768]{2,1,0:T(8,128)(2,1)}, u32[]{:S(2)}) copy-start(bf16[2,384,768]{2,1,0:T(8,128)(2,1)} %gate.1) | copy-start | bytes 3538948
  22.4 16.9 %copy-start.6 = (bf16[2,384,768]{2,1,0:T(8,128)(2,1)S(1)}, bf16[2,384,768]{2,1,0:T(8,128)(2,1)}, u32[]{:S(2)}) copy-start(bf16[2,384,768]{2,1,0:T(8,128)(2,1)} %up.1) | copy-start | bytes 3538948
  22.4 1.3 %collective-permute-start.6 = (bf16[2,4,32,128]{3,2,1,0:T(8,128)(2,1)S(1)}, bf16[2,4,32,128]{3,2,1,0:T(8,128)(2,1)S(1)}, u32[]{:S(2)}, u32[]{:S(2)}) collective-permute-start(bf16[2,4,32,128]{3,2,1,0:T(8,128)(2,1)S(1)} %stack.24.table), channel_id=1, source_target_pairs={{0,2},{2,0},{4,6},{6,4},{8,10},{10,8},{12,14},{14,12},{16,18},{18,... | collective-permute-start | bytes 196616 | tf_op jit(solution)/shard_map/ppermute | solution.py:66
  23.7 8.4 %collective-permute-start.11 = (bf16[1,64,2048]{2,1,0:T(8,128)(2,1)S(1)}, bf16[1,64,2048]{2,1,0:T(8,128)(2,1)S(1)}, u32[]{:S(2)}, u32[]{:S(2)}) collective-permute-start(bf16[1,64,2048]{2,1,0:T(8,128)(2,1)S(1)} %get-tuple-element.48.lines), channel_id=1, source_target_pairs={{0,4},{2,6},{4,0},{6,2},{8,12},{10,14},{12,8},{14,10},{16,20},{18,... | collective-permute-start | bytes 786440 | tf_op jit(solution)/shard_map/ppermute | solution.py:66
  25.4 8.1 %collective-permute-start.9 = (bf16[1,64,2048]{2,1,0:T(8,128)(2,1)S(1)}, bf16[1,64,2048]{2,1,0:T(8,128)(2,1)S(1)}, u32[]{:S(2)}, u32[]{:S(2)}) collective-permute-start(bf16[1,64,2048]{2,1,0:T(8,128)(2,1)S(1)} %get-tuple-element.48.lines), channel_id=1, source_target_pairs={{0,1},{1,0},{2,3},{3,2},{4,5},{5,4},{6,7},{7,6},{8,9},{9,8},{10,11... | collective-permute-start | bytes 786440 | tf_op jit(solution)/shard_map/ppermute | solution.py:66
  26.9 10.1 %collective-permute-start.15 = (bf16[64,2048]{1,0:T(8,128)(2,1)S(1)}, bf16[64,2048]{1,0:T(8,128)(2,1)S(1)}, u32[]{:S(2)}, u32[]{:S(2)}) collective-permute-start(bf16[64,2048]{1,0:T(8,128)(2,1)S(1)} %get-tuple-element.52), channel_id=1, source_target_pairs={{0,24},{2,26},{4,28},{6,30},{8,0},{10,2},{12,4},{14,6},{16,8},{18,... | collective-permute-start | bytes 786440 | tf_op jit(solution)/shard_map/ppermute | solution.py:71
  30.3 13.8 %collective-permute-start = (bf16[128,2048]{1,0:T(8,128)(2,1)S(1)}, bf16[128,2048]{1,0:T(8,128)(2,1)S(1)}, u32[]{:S(2)}, u32[]{:S(2)}) collective-permute-start(bf16[128,2048]{1,0:T(8,128)(2,1)S(1)} %copy-done.4), channel_id=1, source_target_pairs={{0,2},{2,0},{4,6},{6,4},{8,10},{10,8},{12,14},{14,12},{16,18},{18,... | collective-permute-start | bytes 1572872 | tf_op jit(solution)/shard_map/ppermute | solution.py:66
  30.3 12.0 %collective-permute-start.16 = (bf16[64,2048]{1,0:T(8,128)(2,1)S(1)}, bf16[64,2048]{1,0:T(8,128)(2,1)S(1)}, u32[]{:S(2)}, u32[]{:S(2)}) collective-permute-start(bf16[64,2048]{1,0:T(8,128)(2,1)S(1)} %get-tuple-element.52), channel_id=1, source_target_pairs={{0,8},{2,10},{4,12},{6,14},{8,16},{10,18},{12,20},{14,22},{16,24},... | collective-permute-start | bytes 786440 | tf_op jit(solution)/shard_map/ppermute | solution.py:71
  34.1 8.3 %collective-permute-start.13 = (bf16[2,64,1024]{2,1,0:T(8,128)(2,1)S(1)}, bf16[2,64,1024]{2,1,0:T(8,128)(2,1)S(1)}, u32[]{:S(2)}, u32[]{:S(2)}) collective-permute-start(bf16[2,64,1024]{2,1,0:T(8,128)(2,1)S(1)} %get-tuple-element.50), channel_id=1, source_target_pairs={{0,1},{1,0},{2,3},{3,2},{4,5},{5,4},{6,7},{7,6},{8,9},{9,8},{10,11... | collective-permute-start | bytes 786440 | tf_op jit(solution)/shard_map/ppermute | solution.py:66
  35.6 6.9 %collective-permute-start.14 = (bf16[2,64,1024]{2,1,0:T(8,128)(2,1)S(1)}, bf16[2,64,1024]{2,1,0:T(8,128)(2,1)S(1)}, u32[]{:S(2)}, u32[]{:S(2)}) collective-permute-start(bf16[2,64,1024]{2,1,0:T(8,128)(2,1)S(1)} %get-tuple-element.51), channel_id=1, source_target_pairs={{0,4},{2,6},{4,0},{6,2},{8,12},{10,14},{12,8},{14,10},{16,20},{18,... | collective-permute-start | bytes 786440 | tf_op jit(solution)/shard_map/ppermute | solution.py:66
  37.0 6.5 %collective-permute-start.8 = (bf16[1,64,2048]{2,1,0:T(8,128)(2,1)S(1)}, bf16[1,64,2048]{2,1,0:T(8,128)(2,1)S(1)}, u32[]{:S(2)}, u32[]{:S(2)}) collective-permute-start(bf16[1,64,2048]{2,1,0:T(8,128)(2,1)S(1)} %get-tuple-element.48.lines), channel_id=1, source_target_pairs={{0,2},{2,0},{4,6},{6,4},{8,10},{10,8},{12,14},{14,12},{16,18},{18,... | collective-permute-start | bytes 786440 | tf_op jit(solution)/shard_map/ppermute | solution.py:66
  42.3 3.3 %collective-permute-start.12 = (bf16[2,64,2048]{2,1,0:T(8,128)(2,1)S(1)}, bf16[2,64,2048]{2,1,0:T(8,128)(2,1)S(1)}, u32[]{:S(2)}, u32[]{:S(2)}) collective-permute-start(bf16[2,64,2048]{2,1,0:T(8,128)(2,1)S(1)} %get-tuple-element.49.over), channel_id=1, source_target_pairs={{0,2},{2,0},{4,6},{6,4},{8,10},{10,8},{12,14},{14,12},{16,18},{18,... | collective-permute-start | bytes 1572872 | tf_op jit(solution)/shard_map/ppermute | solution.py:66
  42.3 3.3 %copy-start.2 = (bf16[2,384,2048]{2,1,0:T(8,128)(2,1)S(1)}, bf16[2,384,2048]{2,1,0:T(8,128)(2,1)}, u32[]{:S(2)}) copy-start(bf16[2,384,2048]{2,1,0:T(8,128)(2,1)} %w_down.3) | copy-start | bytes 9437188
  42.6 3.0 %collective-permute-start.17 = (bf16[2,64,2048]{2,1,0:T(8,128)(2,1)S(1)}, bf16[2,64,2048]{2,1,0:T(8,128)(2,1)S(1)}, u32[]{:S(2)}, u32[]{:S(2)}) collective-permute-start(bf16[2,64,2048]{2,1,0:T(8,128)(2,1)S(1)} %join.2.diag), channel_id=1, source_target_pairs={{0,2},{2,0},{4,6},{6,4},{8,10},{10,8},{12,14},{14,12},{16,18},{18,... | collective-permute-start | bytes 1572872 | tf_op jit(solution)/shard_map/ppermute | solution.py:66
  43.0 14.0 %collective-permute-start.19 = (bf16[2,64,2048]{2,1,0:T(8,128)(2,1)S(1)}, bf16[2,64,2048]{2,1,0:T(8,128)(2,1)S(1)}, u32[]{:S(2)}, u32[]{:S(2)}) collective-permute-start(bf16[2,64,2048]{2,1,0:T(8,128)(2,1)S(1)} %stack.25.refs_0_._.lines), channel_id=1, source_target_pairs={{0,4},{2,6},{4,0},{6,2},{8,12},{10,14},{12,8},{14,10},{16,20},{18,... | collective-permute-start | bytes 1572872 | tf_op jit(solution)/shard_map/ppermute | solution.py:66
  43.5 13.8 %collective-permute-start.20 = (bf16[2,64,2048]{2,1,0:T(8,128)(2,1)S(1)}, bf16[2,64,2048]{2,1,0:T(8,128)(2,1)S(1)}, u32[]{:S(2)}, u32[]{:S(2)}) collective-permute-start(bf16[2,64,2048]{2,1,0:T(8,128)(2,1)S(1)} %stack.25.refs_0_._.lines), channel_id=1, source_target_pairs={{0,1},{1,0},{2,3},{3,2},{4,5},{5,4},{6,7},{7,6},{8,9},{9,8},{10,11... | collective-permute-start | bytes 1572872 | tf_op jit(solution)/shard_map/ppermute | solution.py:66
  44.0 1.5 %collective-permute-start.10 = (bf16[1,64,2048]{2,1,0:T(8,128)(2,1)S(1)}, bf16[1,64,2048]{2,1,0:T(8,128)(2,1)S(1)}, u32[]{:S(2)}, u32[]{:S(2)}) collective-permute-start(bf16[1,64,2048]{2,1,0:T(8,128)(2,1)S(1)} %collective-permute-done.9.side), channel_id=1, source_target_pairs={{0,2},{2,0},{4,6},{6,4},{8,10},{10,8},{12,14},{14,12},{16,18},{18,... | collective-permute-start | bytes 786440 | tf_op jit(solution)/shard_map/ppermute | solution.py:66
  45.6 4.3 %copy-start = (bf16[2,384,2048]{2,1,0:T(8,128)(2,1)S(1)}, bf16[2,384,2048]{2,1,0:T(8,128)(2,1)}, u32[]{:S(2)}) copy-start(bf16[2,384,2048]{2,1,0:T(8,128)(2,1)} %w_gate.7) | copy-start | bytes 9437188
  45.6 4.3 %copy-start.1 = (bf16[2,384,2048]{2,1,0:T(8,128)(2,1)S(1)}, bf16[2,384,2048]{2,1,0:T(8,128)(2,1)}, u32[]{:S(2)}) copy-start(bf16[2,384,2048]{2,1,0:T(8,128)(2,1)} %w_up.7) | copy-start | bytes 9437188
  52.1 13.2 %collective-permute-start.18 = (bf16[4,128,1024]{2,1,0:T(8,128)(2,1)S(1)}, bf16[4,128,1024]{2,1,0:T(8,128)(2,1)S(1)}, u32[]{:S(2)}, u32[]{:S(2)}) collective-permute-start(bf16[4,128,1024]{2,1,0:T(8,128)(2,1)S(1)} %get-tuple-element.60._), channel_id=1, source_target_pairs={{0,2},{2,0},{4,6},{6,4},{8,10},{10,8},{12,14},{14,12},{16,18},{18,... | collective-permute-start | bytes 3145736 | tf_op jit(solution)/shard_map/ppermute | solution.py:66
  57.4 7.4 %collective-permute-start.21 = (bf16[2,64,1024]{2,1,0:T(8,128)(2,1)S(1)}, bf16[2,64,1024]{2,1,0:T(8,128)(2,1)S(1)}, u32[]{:S(2)}, u32[]{:S(2)}) collective-permute-start(bf16[2,64,1024]{2,1,0:T(8,128)(2,1)S(1)} %get-tuple-element.61._), channel_id=1, source_target_pairs={{0,1},{1,0},{2,3},{3,2},{4,5},{5,4},{6,7},{7,6},{8,9},{9,8},{10,11... | collective-permute-start | bytes 786440 | tf_op jit(solution)/shard_map/ppermute | solution.py:66
  58.0 7.1 %collective-permute-start.22 = (bf16[2,64,1024]{2,1,0:T(8,128)(2,1)S(1)}, bf16[2,64,1024]{2,1,0:T(8,128)(2,1)S(1)}, u32[]{:S(2)}, u32[]{:S(2)}) collective-permute-start(bf16[2,64,1024]{2,1,0:T(8,128)(2,1)S(1)} %get-tuple-element.62), channel_id=1, source_target_pairs={{0,4},{2,6},{4,0},{6,2},{8,12},{10,14},{12,8},{14,10},{16,20},{18,... | collective-permute-start | bytes 786440 | tf_op jit(solution)/shard_map/ppermute | solution.py:66
  61.7 4.2 %collective-permute-start.24 = (bf16[4,128,1024]{2,1,0:T(8,128)(2,1)S(1)}, bf16[4,128,1024]{2,1,0:T(8,128)(2,1)S(1)}, u32[]{:S(2)}, u32[]{:S(2)}) collective-permute-start(bf16[4,128,1024]{2,1,0:T(8,128)(2,1)S(1)} %get-tuple-element.63.refs_0_), channel_id=1, source_target_pairs={{0,2},{2,0},{4,6},{6,4},{8,10},{10,8},{12,14},{14,12},{16,18},{18,... | collective-permute-start | bytes 3145736 | tf_op jit(solution)/shard_map/ppermute | solution.py:66
  61.7 5.6 %collective-permute-start.29 = (bf16[2,64,2048]{2,1,0:T(8,128)(2,1)S(1)}, bf16[2,64,2048]{2,1,0:T(8,128)(2,1)S(1)}, u32[]{:S(2)}, u32[]{:S(2)}) collective-permute-start(bf16[2,64,2048]{2,1,0:T(8,128)(2,1)S(1)} %stack.25.refs_0_._.lines), channel_id=1, source_target_pairs={{0,2},{2,0},{4,6},{6,4},{8,10},{10,8},{12,14},{14,12},{16,18},{18,... | collective-permute-start | bytes 1572872 | tf_op jit(solution)/shard_map/ppermute | solution.py:66
  64.8 4.0 %collective-permute-start.30 = (bf16[2,64,2048]{2,1,0:T(8,128)(2,1)S(1)}, bf16[2,64,2048]{2,1,0:T(8,128)(2,1)S(1)}, u32[]{:S(2)}, u32[]{:S(2)}) collective-permute-start(bf16[2,64,2048]{2,1,0:T(8,128)(2,1)S(1)} %collective-permute-done.20.side), channel_id=1, source_target_pairs={{0,2},{2,0},{4,6},{6,4},{8,10},{10,8},{12,14},{14,12},{16,18},{18,... | collective-permute-start | bytes 1572872 | tf_op jit(solution)/shard_map/ppermute | solution.py:66
  65.1 3.8 %collective-permute-start.31 = (bf16[2,64,2048]{2,1,0:T(8,128)(2,1)S(1)}, bf16[2,64,2048]{2,1,0:T(8,128)(2,1)S(1)}, u32[]{:S(2)}, u32[]{:S(2)}) collective-permute-start(bf16[2,64,2048]{2,1,0:T(8,128)(2,1)S(1)} %collective-permute-done.19.over), channel_id=1, source_target_pairs={{0,2},{2,0},{4,6},{6,4},{8,10},{10,8},{12,14},{14,12},{16,18},{18,... | collective-permute-start | bytes 1572872 | tf_op jit(solution)/shard_map/ppermute | solution.py:66
  65.4 3.5 %collective-permute-start.32 = (bf16[2,64,2048]{2,1,0:T(8,128)(2,1)S(1)}, bf16[2,64,2048]{2,1,0:T(8,128)(2,1)S(1)}, u32[]{:S(2)}, u32[]{:S(2)}) collective-permute-start(bf16[2,64,2048]{2,1,0:T(8,128)(2,1)S(1)} %join.3._.diag), channel_id=1, source_target_pairs={{0,2},{2,0},{4,6},{6,4},{8,10},{10,8},{12,14},{14,12},{16,18},{18,... | collective-permute-start | bytes 1572872 | tf_op jit(solution)/shard_map/ppermute | solution.py:66
  66.0 14.2 %collective-permute-start.25 = (bf16[2,128,1024]{2,1,0:T(8,128)(2,1)S(1)}, bf16[2,128,1024]{2,1,0:T(8,128)(2,1)S(1)}, u32[]{:S(2)}, u32[]{:S(2)}) collective-permute-start(bf16[2,128,1024]{2,1,0:T(8,128)(2,1)S(1)} %get-tuple-element.68._), channel_id=1, source_target_pairs={{0,4},{2,6},{4,0},{6,2},{8,12},{10,14},{12,8},{14,10},{16,20},{18,... | collective-permute-start | bytes 1572872 | tf_op jit(solution)/shard_map/ppermute | solution.py:66
  67.4 13.8 %collective-permute-start.23 = (bf16[4,64,1024]{2,1,0:T(8,128)(2,1)S(1)}, bf16[4,64,1024]{2,1,0:T(8,128)(2,1)S(1)}, u32[]{:S(2)}, u32[]{:S(2)}) collective-permute-start(bf16[4,64,1024]{2,1,0:T(8,128)(2,1)S(1)} %get-tuple-element.65._), channel_id=1, source_target_pairs={{0,1},{1,0},{2,3},{3,2},{4,5},{5,4},{6,7},{7,6},{8,9},{9,8},{10,11... | collective-permute-start | bytes 1572872 | tf_op jit(solution)/shard_map/ppermute | solution.py:66
  77.6 3.7 %collective-permute-start.33 = (bf16[4,128,1024]{2,1,0:T(8,128)(2,1)S(1)}, bf16[4,128,1024]{2,1,0:T(8,128)(2,1)S(1)}, u32[]{:S(2)}, u32[]{:S(2)}) collective-permute-start(bf16[4,128,1024]{2,1,0:T(8,128)(2,1)S(1)} %get-tuple-element.78._), channel_id=1, source_target_pairs={{0,2},{2,0},{4,6},{6,4},{8,10},{10,8},{12,14},{14,12},{16,18},{18,... | collective-permute-start | bytes 3145736 | tf_op jit(solution)/shard_map/ppermute | solution.py:66
  77.6 4.1 %collective-permute-start.35 = (bf16[4,128,1024]{2,1,0:T(8,128)(2,1)S(1)}, bf16[4,128,1024]{2,1,0:T(8,128)(2,1)S(1)}, u32[]{:S(2)}, u32[]{:S(2)}) collective-permute-start(bf16[4,128,1024]{2,1,0:T(8,128)(2,1)S(1)} %get-tuple-element.82), channel_id=1, source_target_pairs={{0,2},{2,0},{4,6},{6,4},{8,10},{10,8},{12,14},{14,12},{16,18},{18,... | collective-permute-start | bytes 3145736 | tf_op jit(solution)/shard_map/ppermute | solution.py:66
  81.9 23.1 %collective-permute-start.36 = (bf16[2,128,1024]{2,1,0:T(8,128)(2,1)S(1)}, bf16[2,128,1024]{2,1,0:T(8,128)(2,1)S(1)}, u32[]{:S(2)}, u32[]{:S(2)}) collective-permute-start(bf16[2,128,1024]{2,1,0:T(8,128)(2,1)S(1)} %get-tuple-element.84), channel_id=1, source_target_pairs={{0,4},{2,6},{4,0},{6,2},{8,12},{10,14},{12,8},{14,10},{16,20},{18,... | collective-permute-start | bytes 1572872 | tf_op jit(solution)/shard_map/ppermute | solution.py:66
  82.7 22.3 %collective-permute-start.34 = (bf16[4,64,1024]{2,1,0:T(8,128)(2,1)S(1)}, bf16[4,64,1024]{2,1,0:T(8,128)(2,1)S(1)}, u32[]{:S(2)}, u32[]{:S(2)}) collective-permute-start(bf16[4,64,1024]{2,1,0:T(8,128)(2,1)S(1)} %get-tuple-element.80._), channel_id=1, source_target_pairs={{0,1},{1,0},{2,3},{3,2},{4,5},{5,4},{6,7},{7,6},{8,9},{9,8},{10,11... | collective-permute-start | bytes 1572872 | tf_op jit(solution)/shard_map/ppermute | solution.py:66
  83.6 17.9 %collective-permute-start.26 = (bf16[2,64,1024]{2,1,0:T(8,128)(2,1)S(1)}, bf16[2,64,1024]{2,1,0:T(8,128)(2,1)S(1)}, u32[]{:S(2)}, u32[]{:S(2)}) collective-permute-start(bf16[2,64,1024]{2,1,0:T(8,128)(2,1)S(1)} %get-tuple-element.70._), channel_id=1, source_target_pairs={{0,4},{2,6},{4,0},{6,2},{8,12},{10,14},{12,8},{14,10},{16,20},{18,... | collective-permute-start | bytes 786440 | tf_op jit(solution)/shard_map/ppermute | solution.py:66
  84.9 17.1 %collective-permute-start.27 = (bf16[2,64,1024]{2,1,0:T(8,128)(2,1)S(1)}, bf16[2,64,1024]{2,1,0:T(8,128)(2,1)S(1)}, u32[]{:S(2)}, u32[]{:S(2)}) collective-permute-start(bf16[2,64,1024]{2,1,0:T(8,128)(2,1)S(1)} %get-tuple-element.72), channel_id=1, source_target_pairs={{0,1},{1,0},{2,3},{3,2},{4,5},{5,4},{6,7},{7,6},{8,9},{9,8},{10,11... | collective-permute-start | bytes 786440 | tf_op jit(solution)/shard_map/ppermute | solution.py:66
  102.1 14.0 %collective-permute-start.28 = (bf16[64,2048]{1,0:T(8,128)(2,1)S(1)}, bf16[64,2048]{1,0:T(8,128)(2,1)S(1)}, u32[]{:S(2)}, u32[]{:S(2)}) collective-permute-start(bf16[64,2048]{1,0:T(8,128)(2,1)S(1)} %get-tuple-element.74), channel_id=1, source_target_pairs={{0,16},{2,18},{4,20},{6,22},{8,24},{10,26},{12,28},{14,30},{16,0},... | collective-permute-start | bytes 786440 | tf_op jit(solution)/shard_map/ppermute | solution.py:71
  105.1 11.0 %collective-permute-start.37 = (bf16[2,64,1024]{2,1,0:T(8,128)(2,1)S(1)}, bf16[2,64,1024]{2,1,0:T(8,128)(2,1)S(1)}, u32[]{:S(2)}, u32[]{:S(2)}) collective-permute-start(bf16[2,64,1024]{2,1,0:T(8,128)(2,1)S(1)} %get-tuple-element.86), channel_id=1, source_target_pairs={{0,4},{2,6},{4,0},{6,2},{8,12},{10,14},{12,8},{14,10},{16,20},{18,... | collective-permute-start | bytes 786440 | tf_op jit(solution)/shard_map/ppermute | solution.py:66
  106.5 9.6 %collective-permute-start.38 = (bf16[2,64,1024]{2,1,0:T(8,128)(2,1)S(1)}, bf16[2,64,1024]{2,1,0:T(8,128)(2,1)S(1)}, u32[]{:S(2)}, u32[]{:S(2)}) collective-permute-start(bf16[2,64,1024]{2,1,0:T(8,128)(2,1)S(1)} %get-tuple-element.88), channel_id=1, source_target_pairs={{0,1},{1,0},{2,3},{3,2},{4,5},{5,4},{6,7},{7,6},{8,9},{9,8},{10,11... | collective-permute-start | bytes 786440 | tf_op jit(solution)/shard_map/ppermute | solution.py:66
  116.2 11.1 %collective-permute-start.39 = (bf16[64,2048]{1,0:T(8,128)(2,1)S(1)}, bf16[64,2048]{1,0:T(8,128)(2,1)S(1)}, u32[]{:S(2)}, u32[]{:S(2)}) collective-permute-start(bf16[64,2048]{1,0:T(8,128)(2,1)S(1)} %get-tuple-element.89), channel_id=1, source_target_pairs={{0,8},{2,10},{4,12},{6,14},{8,16},{10,18},{12,20},{14,22},{16,24},... | collective-permute-start | bytes 786440 | tf_op jit(solution)/shard_map/ppermute | solution.py:71
  116.9 13.5 %collective-permute-start.40 = (bf16[64,2048]{1,0:T(8,128)(2,1)S(1)}, bf16[64,2048]{1,0:T(8,128)(2,1)S(1)}, u32[]{:S(2)}, u32[]{:S(2)}) collective-permute-start(bf16[64,2048]{1,0:T(8,128)(2,1)S(1)} %get-tuple-element.90), channel_id=1, source_target_pairs={{0,24},{2,26},{4,28},{6,30},{8,0},{10,2},{12,4},{14,6},{16,8},{18,... | collective-permute-start | bytes 786440 | tf_op jit(solution)/shard_map/ppermute | solution.py:71

commit v9 on v7

--- a/solution.py
+++ b/solution.py
@@ -128,7 +128,7 @@
             pltpu.VMEM(ids.shape, jnp.int32),
             pltpu.SemaphoreType.DMA((3,)),
         ],
-        limit=60,
+        limit=4,
     )
 
 
@@ -138,13 +138,14 @@
         lines[r] = refs[r][...]
 
 
-def stack(pieces, *after):
+def stack(pieces, *after, work=0):
     return small(
         stack_kernel,
         "stack",
         [(len(pieces),) + pieces[0].shape],
         "v" * len(pieces) + "o" * len(after),
         (*pieces, *after),
+        work=work,
     )[0]
 
 
@@ -215,13 +216,14 @@
     right[...] = side[:, :, middle:2 * middle]
 
 
-def corner(over, side, middle, after):
+def corner(over, side, middle, after, work=0):
     return small(
         plain_corner_kernel,
         "corner",
         [over.shape[:2] + (middle,)] * 2,
         "vvo",
         (over, side, after),
+        work=work,
     )
 
 
@@ -553,7 +555,7 @@
     part, table = prepare(place, cotangent, gates.T, expert_ids.T, piece)
     first = swap(part, "expert", 2)
     own_c, table_c = swap(cotangent, "expert", 1), swap(table, "expert", 1)
-    gathered, saved = [], None
+    gathered = []
 
     def compute(index, after):
         offsets, moved = CHUNKS[index], gathered[index]
@@ -570,34 +572,42 @@
         keep, send = sums(offset, middle, grads, w_gate, w_up, pick_t, after, work)
         return [keep, swap(send, "expert", 1)], send
 
-    for offsets in CHUNKS:
-        pieces = [along_line(part, -r) for r in offsets if r != 0]
-        if saved is None:
-            line, part = relay(pieces[0], part)
-            saved = turn(saved_gate, saved_up, line)
-        else:
-            line = stack(pieces, saved[0])
-        side, over = swap(line, "tp", 1), swap(line, "expert", 2)
-        if offsets[0] == 0:
-            over, left, right = own_corner(place, cotangent, first, over, side)
-            after = (left,)
-        else:
-            early = compute(0, line)
-            grads, pick_t = early
-            early_l, after = sums_by_token(0, grads, pick_t, grads)
-            left, right = corner(over, side, middle, after)
-            early_r, after = sums_by_token(middle, grads, pick_t, left, 68719476736)
-            after = (after,)
-        diag = join(swap(left, "tp", 1), swap(right, "expert", 2), *after, work=8589934592)
-        moved = []
-        for array in (line, side, over, diag):
-            moved += [array, swap(array, "expert", 1)]
-        gathered.append(moved)
-
-    def first_step(keep_l, came_l, keep_r, came_r, after):
-        send_l, keep_l = first_left(keep_l, came_l, after)
-        send_r, keep_r = first_right(keep_r, came_r, send_l)
-        return keep_l, swap(send_l, "tp", 1), keep_r, swap(send_r, "expert", 2), send_r
+    def both_cores(arrays):
+        return [each for array in arrays for each in (array, swap(array, "expert", 1))]
+
+    def step_left(keep, came, after):
+        send, keep = first_left(keep, came, after)
+        return keep, swap(send, "tp", 1), send
+
+    def step_right(keep, came, after):
+        send, keep = first_right(keep, came, after)
+        return keep, swap(send, "expert", 2), send
+
+    (_, near), (third, second) = CHUNKS
+    line, part = relay(along_line(part, -near), part)
+    side, over = swap(line, "tp", 1), swap(line, "expert", 2)
+    came = [along_line(part, -third), along_line(part, -second)]
+    saved = turn(saved_gate, saved_up, line)
+    over, left, right = own_corner(place, cotangent, first, over, side)
+    left, right = swap(left, "tp", 1), swap(right, "expert", 2)
+    moved = both_cores([line, side, over])
+    line = stack(came, saved[0], work=68719476736)
+    line = stack([line], *moved[1::2], own_c, table_c)[0]
+    gathered.append(moved + both_cores([join(left, right, line)]))
+
+    side, over = swap(line, "tp", 1), swap(line, "expert", 2)
+    grads, pick_t = compute(0, line)
+    early_l, after = sums_by_token(0, grads, pick_t, grads)
+    early_r, after = sums_by_token(middle, grads, pick_t, after)
+    left, right = corner(over, side, middle, after, work=68719476736)
+    after = left
+    left, right = swap(left, "tp", 1), swap(right, "expert", 2)
+    early_l = step_left(*early_l, after)
+    early_r = step_right(*early_r, early_l[-1])
+    moved = both_cores([line, side, over])
+    other = [swap(left, "expert", 1), swap(right, "expert", 1)]
+    moved += [join(left, right, early_r[-1], work=0), join(*other, early_r[-1])]
+    gathered.append(moved)
 
     def second_step(offsets, sums_of_two, after, came):
         send_l, left, send_r, right = second_sum(*sums_of_two, after)
@@ -605,13 +615,13 @@
         rows = third_sum(offsets, left, came_l, right, came_r, send_l if came is None else came)
         return rows[0], [row if r == 0 else along_line(row, r) for r, row in zip(offsets, rows)], send_l
 
-    early = first_step(*early_l, *early_r, gathered[1][6])
-    grads, pick_t = compute(1, early[4])
+    grads, pick_t = compute(1, early_r[-1])
     late_l, after = sums_by_token(0, grads, pick_t, grads)
     late_r, _ = sums_by_token(middle, grads, pick_t, after)
-    done, early, after = second_step(CHUNKS[0], early[:4], early[4], None)
-    late = first_step(*late_l, *late_r, after)
-    _, late, _ = second_step(CHUNKS[1], late[:4], done, early[-1])
+    done, early, after = second_step(CHUNKS[0], early_l[:2] + early_r[:2], early_r[-1], None)
+    late_l = step_left(*late_l, after)
+    late_r = step_right(*late_r, late_l[-1])
+    _, late, _ = second_step(CHUNKS[1], late_l[:2] + late_r[:2], done, early[-1])
     terms = early + late
     return pl.pallas_call(
         last_kernel,

time: 117 us -> 121 us (1.034)
  waiting for transfers between devices: 54.6 us -> 56.3 us
  starting transfers between devices: 33.2 us -> 34.7 us
  Pallas kernels: 25.3 us -> 26.6 us
    ppermute x6, waiting for transfers between devices: 23.6 us -> 25.2 us  [along_line(): lax.ppermute(value, 'expert', [(i, (i + 4 * shift) % count) for i in rang...]
    ppermute x31 -> x32, starting transfers between devices: 21.5 us -> 22.9 us  [swap(): return lax.ppermute(value, axis, [(i, i ^ step) for i in range(count)])]
    pallas_call x24 -> x26, Pallas kernels: 24.4 us -> 25.7 us  [small(): pl.pallas_call(kernel, out_shape=[out if hasattr(out, 'dtype') else jax.S...]
    unnamed x20 -> x14, local copies, waits for them, and re-layouts: 2.92 us -> 2.74 us
    ppermute x31 -> x32, waiting for transfers between devices: 31 us -> 31.1 us  [swap(): return lax.ppermute(value, axis, [(i, i ^ step) for i in range(count)])]
  transfers between devices with their start and end apart: 37 -> 38, of which waited for: 19 -> 20; matrix products, arithmetic and copies ran while one was open for 0% -> 0% of each run, Pallas kernels for 19% -> 20%
where the time goes in v9:
time: 121 us
  waiting for transfers between devices  56.3 us (47%)
  starting transfers between devices  34.7 us (29%)
  Pallas kernels  26.6 us (22%)
  local copies, waits for them, and re-layouts  2.74 us (2%)
    ppermute x32, waiting for transfers between devices, swap(): return lax.ppermute(value, axis, [(i, i ^ step) for i in range(count)])  31.1 us
    pallas_call x26, Pallas kernels, small(): pl.pallas_call(kernel, out_shape=[out if hasattr(out, 'dtype') else jax.S...  25.7 us
    ppermute x6, waiting for transfers between devices, along_line(): lax.ppermute(value, 'expert', [(i, (i + 4 * shift) % count) for i in rang...  25.2 us
    ppermute x32, starting transfers between devices, swap(): return lax.ppermute(value, axis, [(i, i ^ step) for i in range(count)])  22.9 us
    ppermute x6, starting transfers between devices, along_line(): lax.ppermute(value, 'expert', [(i, (i + 4 * shift) % count) for i in rang...  11.8 us
    unnamed x14, local copies, waits for them, and re-layouts  2.74 us
  transfers between devices with their start and end apart: 38, of which 20 were waited for; matrix products, arithmetic and copies ran while one was open for 0% of the time, Pallas kernels for 20%

profile of v9, /device:TPU:0, one launch (start us, length us, event | category | flops | bytes accessed | tf_op | source)
XLA Modules:
  0.0 120.7 jit_solution(4544379514347996789)
XLA Ops:
  0.1 0.8 copy-done.5
  0.9 0.7 copy-done.6
  1.5 1.5 %prepare.1 = (bf16[64,2176]{1,0:T(8,128)(2,1)S(1)}, bf16[64,128]{1,0:T(8,128)(2,1)S(1)}) custom-call(s32[4]{0:T(128)S(1)} %pad_add_fusion.place, bf16[128,2048]{1,0:T(8,128)(2,1)} %own.3, f32[8,128]{1,0:T(8,128)S(1)} %bitcast.14, s32[8,128]{1,0:T(8,128)S(1)} %bitcast.15), custom_call_target="tpu_custom_call" | custom-call | tf_op jit(solution)/shard_map/prepare/pallas_call | solution.py:76
  3.1 4.1 %collective-permute-start.1 = (bf16[64,2176]{1,0:T(8,128)(2,1)S(1)}, bf16[64,2176]{1,0:T(8,128)(2,1)S(1)}, u32[]{:S(2)}, u32[]{:S(2)}) collective-permute-start(bf16[64,2176]{1,0:T(8,128)(2,1)S(1)} %get-tuple-element.50.part), channel_id=1, source_target_pairs={{0,16},{2,18},{4,20},{6,22},{8,24},{10,26},{12,28},{14,30},{16,0},... | collective-permute-start | bytes 835592 | tf_op jit(solution)/shard_map/ppermute | solution.py:71
  7.2 1.5 %collective-permute-start.5 = (bf16[64,2176]{1,0:T(8,128)(2,1)S(1)}, bf16[64,2176]{1,0:T(8,128)(2,1)S(1)}, u32[]{:S(2)}, u32[]{:S(2)}) collective-permute-start(bf16[64,2176]{1,0:T(8,128)(2,1)S(1)} %get-tuple-element.50.part), channel_id=1, source_target_pairs={{0,4},{2,6},{4,0},{6,2},{8,12},{10,14},{12,8},{14,10},{16,20},{18,... | collective-permute-start | bytes 835592 | tf_op jit(solution)/shard_map/ppermute | solution.py:66
  8.7 11.1 %collective-permute-done.1.came = bf16[64,2176]{1,0:T(8,128)(2,1)S(1)} collective-permute-done((bf16[64,2176]{1,0:T(8,128)(2,1)S(1)}, bf16[64,2176]{1,0:T(8,128)(2,1)S(1)}, u32[]{:S(2)}, u32[]{:S(2)}) %collective-permute-start.1) | collective-permute-done | bytes 278560 | tf_op jit(solution)/shard_map/ppermute | solution.py:71
  19.8 1.6 %collective-permute-start.3 = (bf16[1,64,2176]{2,1,0:T(8,128)(2,1)S(1)}, bf16[1,64,2176]{2,1,0:T(8,128)(2,1)S(1)}, u32[]{:S(2)}, u32[]{:S(2)}) collective-permute-start(bf16[1,64,2176]{2,1,0:T(8,128)(2,1)S(1)} %get-tuple-element.51._.lines), channel_id=1, source_target_pairs={{0,1},{1,0},{2,3},{3,2},{4,5},{5,4},{6,7},{7,6},{8,9},{9,8},{10,11... | collective-permute-start | bytes 835592 | tf_op jit(solution)/shard_map/ppermute | solution.py:66
  21.5 1.5 %collective-permute-start.6 = (bf16[1,64,2176]{2,1,0:T(8,128)(2,1)S(1)}, bf16[1,64,2176]{2,1,0:T(8,128)(2,1)S(1)}, u32[]{:S(2)}, u32[]{:S(2)}) collective-permute-start(bf16[1,64,2176]{2,1,0:T(8,128)(2,1)S(1)} %get-tuple-element.51._.lines), channel_id=1, source_target_pairs={{0,4},{2,6},{4,0},{6,2},{8,12},{10,14},{12,8},{14,10},{16,20},{18,... | collective-permute-start | bytes 835592 | tf_op jit(solution)/shard_map/ppermute | solution.py:66
  23.0 3.5 %collective-permute-start.10 = (bf16[64,2176]{1,0:T(8,128)(2,1)S(1)}, bf16[64,2176]{1,0:T(8,128)(2,1)S(1)}, u32[]{:S(2)}, u32[]{:S(2)}) collective-permute-start(bf16[64,2176]{1,0:T(8,128)(2,1)S(1)} %get-tuple-element.55), channel_id=1, source_target_pairs={{0,24},{2,26},{4,28},{6,30},{8,0},{10,2},{12,4},{14,6},{16,8},{18,... | collective-permute-start | bytes 835592 | tf_op jit(solution)/shard_map/ppermute | solution.py:71
  26.5 1.3 %collective-permute-done.3.side = bf16[1,64,2176]{2,1,0:T(8,128)(2,1)S(1)} collective-permute-done((bf16[1,64,2176]{2,1,0:T(8,128)(2,1)S(1)}, bf16[1,64,2176]{2,1,0:T(8,128)(2,1)S(1)}, u32[]{:S(2)}, u32[]{:S(2)}) %collective-permute-start.3) | collective-permute-done | bytes 278560 | tf_op jit(solution)/shard_map/ppermute | solution.py:66
  27.8 1.3 %copy-done.4 = bf16[2,384,768]{2,1,0:T(8,128)(2,1)S(1)} copy-done((bf16[2,384,768]{2,1,0:T(8,128)(2,1)S(1)}, bf16[2,384,768]{2,1,0:T(8,128)(2,1)}, u32[]{:S(2)}) %copy-start.4) | copy-done | bytes 1179672
  29.0 0.7 turn.1
  29.7 0.6 collective-permute-start.2
  30.3 1.5 %own_corner.1 = (bf16[2,64,2176]{2,1,0:T(8,128)(2,1)S(1)}, bf16[2,64,1024]{2,1,0:T(8,128)(2,1)S(1)}, bf16[2,64,1024]{2,1,0:T(8,128)(2,1)S(1)}) custom-call(s32[4]{0:T(128)S(1)} %pad_add_fusion.place, bf16[128,2048]{1,0:T(8,128)(2,1)} %own.3, bf16[64,2176]{1,0:T(8,128)(2,1)S(1)} %collective-permute-done.5.first, ...), custom_call_target="tpu_custom_call" | custom-call | tf_op jit(solution)/shard_map/own_corner/pallas_call | solution.py:76
  31.9 1.3 %collective-permute-start.8 = (bf16[2,64,1024]{2,1,0:T(8,128)(2,1)S(1)}, bf16[2,64,1024]{2,1,0:T(8,128)(2,1)S(1)}, u32[]{:S(2)}, u32[]{:S(2)}) collective-permute-start(bf16[2,64,1024]{2,1,0:T(8,128)(2,1)S(1)} %get-tuple-element.53), channel_id=1, source_target_pairs={{0,1},{1,0},{2,3},{3,2},{4,5},{5,4},{6,7},{7,6},{8,9},{9,8},{10,11... | collective-permute-start | bytes 786440 | tf_op jit(solution)/shard_map/ppermute | solution.py:66
  33.2 0.4 collective-permute-done.10.refs_0_
  33.6 1.1 collective-permute-start.9
  34.7 4.0 %collective-permute-done.11.refs_1_ = bf16[64,2176]{1,0:T(8,128)(2,1)S(1)} collective-permute-done((bf16[64,2176]{1,0:T(8,128)(2,1)S(1)}, bf16[64,2176]{1,0:T(8,128)(2,1)S(1)}, u32[]{:S(2)}, u32[]{:S(2)}) %collective-permute-start.11) | collective-permute-done | bytes 278560 | tf_op jit(solution)/shard_map/ppermute | solution.py:71
  38.8 1.5 %collective-permute-done.4.refs_2_.side_c = bf16[1,64,2176]{2,1,0:T(8,128)(2,1)S(1)} collective-permute-done((bf16[1,64,2176]{2,1,0:T(8,128)(2,1)S(1)}, bf16[1,64,2176]{2,1,0:T(8,128)(2,1)S(1)}, u32[]{:S(2)}, u32[]{:S(2)}) %collective-permute-start.4) | collective-permute-done | bytes 278560 | tf_op jit(solution)/shard_map/ppermute | solution.py:66
  40.3 0.6 collective-permute-start.15
  40.9 0.5 collective-permute-start.16
  41.7 0.5 collective-permute-start.23
  42.2 1.1 route.2
  43.3 0.3 collective-permute-done.13.diag_c
  43.6 5.0 %hidden.2.grads._ = bf16[2,384,768]{2,1,0:T(8,128)(2,1)S(1)} custom-call(s32[4]{0:T(128)S(1)} %pad_add_fusion.place, bf16[128,2048]{1,0:T(8,128)(2,1)} %own.3, bf16[128,2048]{1,0:T(8,128)(2,1)S(1)} %collective-permute-done.refs_4_.own_c, bf16[1,64,2176]{2,1,0:T(8,128)(2,1)S(1)} %get-tuple-element.51._.lines, ...), custom_call_target="tpu_custom_call" | custom-call | tf_op jit(solution)/shard_map/hidden/pallas_call | solution.py:76
  48.6 2.2 %sums.4 = (bf16[4,128,1024]{2,1,0:T(8,128)(2,1)S(1)}, bf16[4,128,1024]{2,1,0:T(8,128)(2,1)S(1)}) custom-call(bf16[2,384,768]{2,1,0:T(8,128)(2,1)S(1)} %hidden.2.grads._, bf16[2,384,2048]{2,1,0:T(8,128)(2,1)S(1)} %copy-done, bf16[2,384,2048]{2,1,0:T(8,128)(2,1)S(1)} %copy-done.1, bf16[4,256,192]{2,1,0:T(8,128)(2,1)S(1)} %get-tuple-element.61.pick_t, ...), custom_call_target="tpu_custom_call" | custom-call | tf_op jit(solution)/shard_map/sums/pallas_call | solution.py:76
  50.8 0.2 collective-permute-start.14
  51.0 2.2 %sums.5 = (bf16[4,128,1024]{2,1,0:T(8,128)(2,1)S(1)}, bf16[4,128,1024]{2,1,0:T(8,128)(2,1)S(1)}) custom-call(bf16[2,384,768]{2,1,0:T(8,128)(2,1)S(1)} %hidden.2.grads._, bf16[2,384,2048]{2,1,0:T(8,128)(2,1)S(1)} %copy-done, bf16[2,384,2048]{2,1,0:T(8,128)(2,1)S(1)} %copy-done.1, bf16[4,256,192]{2,1,0:T(8,128)(2,1)S(1)} %get-tuple-element.61.pick_t, ...), custom_call_target="tpu_custom_call" | custom-call | tf_op jit(solution)/shard_map/sums/pallas_call | solution.py:76
  53.3 0.4 collective-permute-start.18
  53.7 1.3 %collective-permute-done.15.over = bf16[2,64,2176]{2,1,0:T(8,128)(2,1)S(1)} collective-permute-done((bf16[2,64,2176]{2,1,0:T(8,128)(2,1)S(1)}, bf16[2,64,2176]{2,1,0:T(8,128)(2,1)S(1)}, u32[]{:S(2)}, u32[]{:S(2)}) %collective-permute-start.15) | collective-permute-done | bytes 557088 | tf_op jit(solution)/shard_map/ppermute | solution.py:66
  55.0 0.2 collective-permute-done.16.side
  55.3 0.6 collective-permute-start.26
  56.0 1.5 %collective-permute-start.27 = (bf16[2,64,1024]{2,1,0:T(8,128)(2,1)S(1)}, bf16[2,64,1024]{2,1,0:T(8,128)(2,1)S(1)}, u32[]{:S(2)}, u32[]{:S(2)}) collective-permute-start(bf16[2,64,1024]{2,1,0:T(8,128)(2,1)S(1)} %get-tuple-element.77), channel_id=1, source_target_pairs={{0,4},{2,6},{4,0},{6,2},{8,12},{10,14},{12,8},{14,10},{16,20},{18,... | collective-permute-start | bytes 786440 | tf_op jit(solution)/shard_map/ppermute | solution.py:66
  57.5 0.2 first_left.2
  57.7 0.2 first_right.2
  57.8 1.5 %collective-permute-start.17 = (bf16[4,64,1024]{2,1,0:T(8,128)(2,1)S(1)}, bf16[4,64,1024]{2,1,0:T(8,128)(2,1)S(1)}, u32[]{:S(2)}, u32[]{:S(2)}) collective-permute-start(bf16[4,64,1024]{2,1,0:T(8,128)(2,1)S(1)} %get-tuple-element.67._), channel_id=1, source_target_pairs={{0,1},{1,0},{2,3},{3,2},{4,5},{5,4},{6,7},{7,6},{8,9},{9,8},{10,11... | collective-permute-start | bytes 1572872 | tf_op jit(solution)/shard_map/ppermute | solution.py:66
  59.4 5.1 %collective-permute-done.26.left = bf16[2,64,1024]{2,1,0:T(8,128)(2,1)S(1)} collective-permute-done((bf16[2,64,1024]{2,1,0:T(8,128)(2,1)S(1)}, bf16[2,64,1024]{2,1,0:T(8,128)(2,1)S(1)}, u32[]{:S(2)}, u32[]{:S(2)}) %collective-permute-start.26) | collective-permute-done | bytes 262176 | tf_op jit(solution)/shard_map/ppermute | solution.py:66
  64.5 1.6 %collective-permute-start.19 = (bf16[2,128,1024]{2,1,0:T(8,128)(2,1)S(1)}, bf16[2,128,1024]{2,1,0:T(8,128)(2,1)S(1)}, u32[]{:S(2)}, u32[]{:S(2)}) collective-permute-start(bf16[2,128,1024]{2,1,0:T(8,128)(2,1)S(1)} %get-tuple-element.70._.refs_0_), channel_id=1, source_target_pairs={{0,4},{2,6},{4,0},{6,2},{8,12},{10,14},{12,8},{14,10},{16,20},{18,... | collective-permute-start | bytes 1572872 | tf_op jit(solution)/shard_map/ppermute | solution.py:66
  66.2 0.5 collective-permute-start.29
  66.7 1.1 route.3
  67.8 0.2 collective-permute-done.29.right
  68.1 4.6 %hidden.3.grads._ = bf16[2,384,768]{2,1,0:T(8,128)(2,1)S(1)} custom-call(s32[4]{0:T(128)S(1)} %pad_add_fusion.place, bf16[128,2048]{1,0:T(8,128)(2,1)} %own.3, bf16[128,2048]{1,0:T(8,128)(2,1)S(1)} %collective-permute-done.refs_4_.own_c, bf16[2,64,2176]{2,1,0:T(8,128)(2,1)S(1)} %bitcast.13, bf16[2,64,2176]{2,1,0:T(8,128)(2,1)S(1)} %collective-permute-done.23.lines_c, ...), custom_call_target="tpu_custom_call" | custom-call | tf_op jit(solution)/shard_map/hidden/pallas_call | solution.py:76
  72.8 2.3 %sums.6 = (bf16[4,128,1024]{2,1,0:T(8,128)(2,1)S(1)}, bf16[4,128,1024]{2,1,0:T(8,128)(2,1)S(1)}) custom-call(bf16[2,384,768]{2,1,0:T(8,128)(2,1)S(1)} %hidden.3.grads._, bf16[2,384,2048]{2,1,0:T(8,128)(2,1)S(1)} %copy-done, bf16[2,384,2048]{2,1,0:T(8,128)(2,1)S(1)} %copy-done.1, bf16[4,256,192]{2,1,0:T(8,128)(2,1)S(1)} %get-tuple-element.80.pick_t, ...), custom_call_target="tpu_custom_call" | custom-call | tf_op jit(solution)/shard_map/sums/pallas_call | solution.py:76
  75.0 0.2 collective-permute-start.30
  75.2 2.2 %sums.7 = (bf16[4,128,1024]{2,1,0:T(8,128)(2,1)S(1)}, bf16[4,128,1024]{2,1,0:T(8,128)(2,1)S(1)}) custom-call(bf16[2,384,768]{2,1,0:T(8,128)(2,1)S(1)} %hidden.3.grads._, bf16[2,384,2048]{2,1,0:T(8,128)(2,1)S(1)} %copy-done, bf16[2,384,2048]{2,1,0:T(8,128)(2,1)S(1)} %copy-done.1, bf16[4,256,192]{2,1,0:T(8,128)(2,1)S(1)} %get-tuple-element.80.pick_t, ...), custom_call_target="tpu_custom_call" | custom-call | tf_op jit(solution)/shard_map/sums/pallas_call | solution.py:76
  77.5 0.4 collective-permute-start.32
  78.0 0.5 collective-permute-start.20
  78.5 1.6 %collective-permute-start.21 = (bf16[2,64,1024]{2,1,0:T(8,128)(2,1)S(1)}, bf16[2,64,1024]{2,1,0:T(8,128)(2,1)S(1)}, u32[]{:S(2)}, u32[]{:S(2)}) collective-permute-start(bf16[2,64,1024]{2,1,0:T(8,128)(2,1)S(1)} %get-tuple-element.74), channel_id=1, source_target_pairs={{0,1},{1,0},{2,3},{3,2},{4,5},{5,4},{6,7},{7,6},{8,9},{9,8},{10,11... | collective-permute-start | bytes 786440 | tf_op jit(solution)/shard_map/ppermute | solution.py:66
  80.2 0.5 collective-permute-start.31
  80.8 1.7 %collective-permute-start.33 = (bf16[2,128,1024]{2,1,0:T(8,128)(2,1)S(1)}, bf16[2,128,1024]{2,1,0:T(8,128)(2,1)S(1)}, u32[]{:S(2)}, u32[]{:S(2)}) collective-permute-start(bf16[2,128,1024]{2,1,0:T(8,128)(2,1)S(1)} %get-tuple-element.88), channel_id=1, source_target_pairs={{0,4},{2,6},{4,0},{6,2},{8,12},{10,14},{12,8},{14,10},{16,20},{18,... | collective-permute-start | bytes 1572872 | tf_op jit(solution)/shard_map/ppermute | solution.py:66
  82.5 4.7 %collective-permute-done.20.came_l = bf16[2,64,1024]{2,1,0:T(8,128)(2,1)S(1)} collective-permute-done((bf16[2,64,1024]{2,1,0:T(8,128)(2,1)S(1)}, bf16[2,64,1024]{2,1,0:T(8,128)(2,1)S(1)}, u32[]{:S(2)}, u32[]{:S(2)}) %collective-permute-start.20) | collective-permute-done | bytes 262176 | tf_op jit(solution)/shard_map/ppermute | solution.py:66
  87.2 0.4 collective-permute-done.21.came_r
  87.8 0.2 collective-permute-start.22
  88.0 9.8 %collective-permute-done.31.came_l = bf16[4,64,1024]{2,1,0:T(8,128)(2,1)S(1)} collective-permute-done((bf16[4,64,1024]{2,1,0:T(8,128)(2,1)S(1)}, bf16[4,64,1024]{2,1,0:T(8,128)(2,1)S(1)}, u32[]{:S(2)}, u32[]{:S(2)}) %collective-permute-start.31) | collective-permute-done | bytes 524320 | tf_op jit(solution)/shard_map/ppermute | solution.py:66
  97.9 1.7 %collective-permute-start.34 = (bf16[2,64,1024]{2,1,0:T(8,128)(2,1)S(1)}, bf16[2,64,1024]{2,1,0:T(8,128)(2,1)S(1)}, u32[]{:S(2)}, u32[]{:S(2)}) collective-permute-start(bf16[2,64,1024]{2,1,0:T(8,128)(2,1)S(1)} %get-tuple-element.90), channel_id=1, source_target_pairs={{0,4},{2,6},{4,0},{6,2},{8,12},{10,14},{12,8},{14,10},{16,20},{18,... | collective-permute-start | bytes 786440 | tf_op jit(solution)/shard_map/ppermute | solution.py:66
  99.6 0.5 collective-permute-start.35
  100.1 0.6 collective-permute-done.22._.refs_1_
  100.7 4.7 %collective-permute-done.34.came_l = bf16[2,64,1024]{2,1,0:T(8,128)(2,1)S(1)} collective-permute-done((bf16[2,64,1024]{2,1,0:T(8,128)(2,1)S(1)}, bf16[2,64,1024]{2,1,0:T(8,128)(2,1)S(1)}, u32[]{:S(2)}, u32[]{:S(2)}) %collective-permute-start.34) | collective-permute-done | bytes 262176 | tf_op jit(solution)/shard_map/ppermute | solution.py:66
  105.4 1.1 collective-permute-done.35.came_r
  106.6 1.8 %collective-permute-start.36 = (bf16[64,2048]{1,0:T(8,128)(2,1)S(1)}, bf16[64,2048]{1,0:T(8,128)(2,1)S(1)}, u32[]{:S(2)}, u32[]{:S(2)}) collective-permute-start(bf16[64,2048]{1,0:T(8,128)(2,1)S(1)} %get-tuple-element.93), channel_id=1, source_target_pairs={{0,8},{2,10},{4,12},{6,14},{8,16},{10,18},{12,20},{14,22},{16,24},... | collective-permute-start | bytes 786440 | tf_op jit(solution)/shard_map/ppermute | solution.py:71
  108.5 2.2 %collective-permute-start.37 = (bf16[64,2048]{1,0:T(8,128)(2,1)S(1)}, bf16[64,2048]{1,0:T(8,128)(2,1)S(1)}, u32[]{:S(2)}, u32[]{:S(2)}) collective-permute-start(bf16[64,2048]{1,0:T(8,128)(2,1)S(1)} %get-tuple-element.94), channel_id=1, source_target_pairs={{0,24},{2,26},{4,28},{6,30},{8,0},{10,2},{12,4},{14,6},{16,8},{18,... | collective-permute-start | bytes 786440 | tf_op jit(solution)/shard_map/ppermute | solution.py:71
  110.7 7.1 %collective-permute-done.36.refs_2_ = bf16[64,2048]{1,0:T(8,128)(2,1)S(1)} collective-permute-done((bf16[64,2048]{1,0:T(8,128)(2,1)S(1)}, bf16[64,2048]{1,0:T(8,128)(2,1)S(1)}, u32[]{:S(2)}, u32[]{:S(2)}) %collective-permute-start.36) | collective-permute-done | bytes 262176 | tf_op jit(solution)/shard_map/ppermute | solution.py:71
  117.7 2.1 %collective-permute-done.37.refs_3_ = bf16[64,2048]{1,0:T(8,128)(2,1)S(1)} collective-permute-done((bf16[64,2048]{1,0:T(8,128)(2,1)S(1)}, bf16[64,2048]{1,0:T(8,128)(2,1)S(1)}, u32[]{:S(2)}, u32[]{:S(2)}) %collective-permute-start.37) | collective-permute-done | bytes 262176 | tf_op jit(solution)/shard_map/ppermute | solution.py:71
  119.8 0.9 last_sum.1
  (54 shorter events, 1.5 us)
Async XLA Ops:
  0.0 27.8 %copy-start.3 = (bf16[2,384,768]{2,1,0:T(8,128)(2,1)S(1)}, bf16[2,384,768]{2,1,0:T(8,128)(2,1)}, u32[]{:S(2)}) copy-start(bf16[2,384,768]{2,1,0:T(8,128)(2,1)} %gate.1) | copy-start | bytes 3538948
  0.1 0.8 copy-start.5
  0.8 0.7 copy-start.6
  3.1 16.7 %collective-permute-start.1 = (bf16[64,2176]{1,0:T(8,128)(2,1)S(1)}, bf16[64,2176]{1,0:T(8,128)(2,1)S(1)}, u32[]{:S(2)}, u32[]{:S(2)}) collective-permute-start(bf16[64,2176]{1,0:T(8,128)(2,1)S(1)} %get-tuple-element.50.part), channel_id=1, source_target_pairs={{0,16},{2,18},{4,20},{6,22},{8,24},{10,26},{12,28},{14,30},{16,0},... | collective-permute-start | bytes 835592 | tf_op jit(solution)/shard_map/ppermute | solution.py:71
  7.2 19.3 %collective-permute-start.5 = (bf16[64,2176]{1,0:T(8,128)(2,1)S(1)}, bf16[64,2176]{1,0:T(8,128)(2,1)S(1)}, u32[]{:S(2)}, u32[]{:S(2)}) collective-permute-start(bf16[64,2176]{1,0:T(8,128)(2,1)S(1)} %get-tuple-element.50.part), channel_id=1, source_target_pairs={{0,4},{2,6},{4,0},{6,2},{8,12},{10,14},{12,8},{14,10},{16,20},{18,... | collective-permute-start | bytes 835592 | tf_op jit(solution)/shard_map/ppermute | solution.py:66
  8.7 23.2 %collective-permute-start = (bf16[128,2048]{1,0:T(8,128)(2,1)}, bf16[128,2048]{1,0:T(8,128)(2,1)S(1)}, u32[]{:S(2)}, u32[]{:S(2)}) collective-permute-start(bf16[128,2048]{1,0:T(8,128)(2,1)} %own.3), channel_id=1, source_target_pairs={{0,2},{2,0},{4,6},{6,4},{8,10},{10,8},{12,14},{14,12},{16,18},{18,... | collective-permute-start | bytes 1572872 | tf_op jit(solution)/shard_map/ppermute | solution.py:66
  19.8 7.9 %collective-permute-start.3 = (bf16[1,64,2176]{2,1,0:T(8,128)(2,1)S(1)}, bf16[1,64,2176]{2,1,0:T(8,128)(2,1)S(1)}, u32[]{:S(2)}, u32[]{:S(2)}) collective-permute-start(bf16[1,64,2176]{2,1,0:T(8,128)(2,1)S(1)} %get-tuple-element.51._.lines), channel_id=1, source_target_pairs={{0,1},{1,0},{2,3},{3,2},{4,5},{5,4},{6,7},{7,6},{8,9},{9,8},{10,11... | collective-permute-start | bytes 835592 | tf_op jit(solution)/shard_map/ppermute | solution.py:66
  21.5 8.3 %collective-permute-start.6 = (bf16[1,64,2176]{2,1,0:T(8,128)(2,1)S(1)}, bf16[1,64,2176]{2,1,0:T(8,128)(2,1)S(1)}, u32[]{:S(2)}, u32[]{:S(2)}) collective-permute-start(bf16[1,64,2176]{2,1,0:T(8,128)(2,1)S(1)} %get-tuple-element.51._.lines), channel_id=1, source_target_pairs={{0,4},{2,6},{4,0},{6,2},{8,12},{10,14},{12,8},{14,10},{16,20},{18,... | collective-permute-start | bytes 835592 | tf_op jit(solution)/shard_map/ppermute | solution.py:66
  23.0 10.6 %collective-permute-start.10 = (bf16[64,2176]{1,0:T(8,128)(2,1)S(1)}, bf16[64,2176]{1,0:T(8,128)(2,1)S(1)}, u32[]{:S(2)}, u32[]{:S(2)}) collective-permute-start(bf16[64,2176]{1,0:T(8,128)(2,1)S(1)} %get-tuple-element.55), channel_id=1, source_target_pairs={{0,24},{2,26},{4,28},{6,30},{8,0},{10,2},{12,4},{14,6},{16,8},{18,... | collective-permute-start | bytes 835592 | tf_op jit(solution)/shard_map/ppermute | solution.py:71
  26.5 12.2 %collective-permute-start.11 = (bf16[64,2176]{1,0:T(8,128)(2,1)S(1)}, bf16[64,2176]{1,0:T(8,128)(2,1)S(1)}, u32[]{:S(2)}, u32[]{:S(2)}) collective-permute-start(bf16[64,2176]{1,0:T(8,128)(2,1)S(1)} %get-tuple-element.55), channel_id=1, source_target_pairs={{0,8},{2,10},{4,12},{6,14},{8,16},{10,18},{12,20},{14,22},{16,24},... | collective-permute-start | bytes 835592 | tf_op jit(solution)/shard_map/ppermute | solution.py:71
  27.8 4.0 %collective-permute-start.12 = (bf16[64,128]{1,0:T(8,128)(2,1)S(1)}, bf16[64,128]{1,0:T(8,128)(2,1)S(1)}, u32[]{:S(2)}, u32[]{:S(2)}) collective-permute-start(bf16[64,128]{1,0:T(8,128)(2,1)S(1)} %get-tuple-element.57.own), channel_id=1, source_target_pairs={{0,2},{2,0},{4,6},{6,4},{8,10},{10,8},{12,14},{14,12},{16,18},{18,... | collective-permute-start | bytes 49160 | tf_op jit(solution)/shard_map/ppermute | solution.py:66
  27.8 1.3 %copy-start.4 = (bf16[2,384,768]{2,1,0:T(8,128)(2,1)S(1)}, bf16[2,384,768]{2,1,0:T(8,128)(2,1)}, u32[]{:S(2)}) copy-start(bf16[2,384,768]{2,1,0:T(8,128)(2,1)} %up.1) | copy-start | bytes 3538948
  29.7 9.0 %collective-permute-start.2 = (bf16[1,64,2176]{2,1,0:T(8,128)(2,1)S(1)}, bf16[1,64,2176]{2,1,0:T(8,128)(2,1)S(1)}, u32[]{:S(2)}, u32[]{:S(2)}) collective-permute-start(bf16[1,64,2176]{2,1,0:T(8,128)(2,1)S(1)} %get-tuple-element.51._.lines), channel_id=1, source_target_pairs={{0,2},{2,0},{4,6},{6,4},{8,10},{10,8},{12,14},{14,12},{16,18},{18,... | collective-permute-start | bytes 835592 | tf_op jit(solution)/shard_map/ppermute | solution.py:66
  31.8 8.5 %collective-permute-start.7 = (bf16[2,64,2176]{2,1,0:T(8,128)(2,1)S(1)}, bf16[2,64,2176]{2,1,0:T(8,128)(2,1)S(1)}, u32[]{:S(2)}, u32[]{:S(2)}) collective-permute-start(bf16[2,64,2176]{2,1,0:T(8,128)(2,1)S(1)} %get-tuple-element.52.over), channel_id=1, source_target_pairs={{0,2},{2,0},{4,6},{6,4},{8,10},{10,8},{12,14},{14,12},{16,18},{18,... | collective-permute-start | bytes 1671176 | tf_op jit(solution)/shard_map/ppermute | solution.py:66
  31.9 9.6 %collective-permute-start.8 = (bf16[2,64,1024]{2,1,0:T(8,128)(2,1)S(1)}, bf16[2,64,1024]{2,1,0:T(8,128)(2,1)S(1)}, u32[]{:S(2)}, u32[]{:S(2)}) collective-permute-start(bf16[2,64,1024]{2,1,0:T(8,128)(2,1)S(1)} %get-tuple-element.53), channel_id=1, source_target_pairs={{0,1},{1,0},{2,3},{3,2},{4,5},{5,4},{6,7},{7,6},{8,9},{9,8},{10,11... | collective-permute-start | bytes 786440 | tf_op jit(solution)/shard_map/ppermute | solution.py:66
  33.6 8.0 %collective-permute-start.9 = (bf16[2,64,1024]{2,1,0:T(8,128)(2,1)S(1)}, bf16[2,64,1024]{2,1,0:T(8,128)(2,1)S(1)}, u32[]{:S(2)}, u32[]{:S(2)}) collective-permute-start(bf16[2,64,1024]{2,1,0:T(8,128)(2,1)S(1)} %get-tuple-element.54), channel_id=1, source_target_pairs={{0,4},{2,6},{4,0},{6,2},{8,12},{10,14},{12,8},{14,10},{16,20},{18,... | collective-permute-start | bytes 786440 | tf_op jit(solution)/shard_map/ppermute | solution.py:66
  38.7 1.6 %collective-permute-start.4 = (bf16[1,64,2176]{2,1,0:T(8,128)(2,1)S(1)}, bf16[1,64,2176]{2,1,0:T(8,128)(2,1)S(1)}, u32[]{:S(2)}, u32[]{:S(2)}) collective-permute-start(bf16[1,64,2176]{2,1,0:T(8,128)(2,1)S(1)} %collective-permute-done.3.side), channel_id=1, source_target_pairs={{0,2},{2,0},{4,6},{6,4},{8,10},{10,8},{12,14},{14,12},{16,18},{18,... | collective-permute-start | bytes 835592 | tf_op jit(solution)/shard_map/ppermute | solution.py:66
  40.3 14.7 %collective-permute-start.15 = (bf16[2,64,2176]{2,1,0:T(8,128)(2,1)S(1)}, bf16[2,64,2176]{2,1,0:T(8,128)(2,1)S(1)}, u32[]{:S(2)}, u32[]{:S(2)}) collective-permute-start(bf16[2,64,2176]{2,1,0:T(8,128)(2,1)S(1)} %bitcast.7), channel_id=1, source_target_pairs={{0,4},{2,6},{4,0},{6,2},{8,12},{10,14},{12,8},{14,10},{16,20},{18,... | collective-permute-start | bytes 1671176 | tf_op jit(solution)/shard_map/ppermute | solution.py:66
  40.9 14.4 %collective-permute-start.16 = (bf16[2,64,2176]{2,1,0:T(8,128)(2,1)S(1)}, bf16[2,64,2176]{2,1,0:T(8,128)(2,1)S(1)}, u32[]{:S(2)}, u32[]{:S(2)}) collective-permute-start(bf16[2,64,2176]{2,1,0:T(8,128)(2,1)S(1)} %bitcast.8), channel_id=1, source_target_pairs={{0,1},{1,0},{2,3},{3,2},{4,5},{5,4},{6,7},{7,6},{8,9},{9,8},{10,11... | collective-permute-start | bytes 1671176 | tf_op jit(solution)/shard_map/ppermute | solution.py:66
  41.6 2.0 %copy-start.2 = (bf16[2,384,2048]{2,1,0:T(8,128)(2,1)S(1)}, bf16[2,384,2048]{2,1,0:T(8,128)(2,1)}, u32[]{:S(2)}) copy-start(bf16[2,384,2048]{2,1,0:T(8,128)(2,1)} %w_down.3) | copy-start | bytes 9437188
  41.6 2.0 %collective-permute-start.13 = (bf16[2,64,2048]{2,1,0:T(8,128)(2,1)S(1)}, bf16[2,64,2048]{2,1,0:T(8,128)(2,1)S(1)}, u32[]{:S(2)}, u32[]{:S(2)}) collective-permute-start(bf16[2,64,2048]{2,1,0:T(8,128)(2,1)S(1)} %join.3.diag), channel_id=1, source_target_pairs={{0,2},{2,0},{4,6},{6,4},{8,10},{10,8},{12,14},{14,12},{16,18},{18,... | collective-permute-start | bytes 1572872 | tf_op jit(solution)/shard_map/ppermute | solution.py:66
  41.7 16.2 %collective-permute-start.23 = (bf16[2,64,2176]{2,1,0:T(8,128)(2,1)S(1)}, bf16[2,64,2176]{2,1,0:T(8,128)(2,1)S(1)}, u32[]{:S(2)}, u32[]{:S(2)}) collective-permute-start(bf16[2,64,2176]{2,1,0:T(8,128)(2,1)S(1)} %bitcast.10), channel_id=1, source_target_pairs={{0,2},{2,0},{4,6},{6,4},{8,10},{10,8},{12,14},{14,12},{16,18},{18,... | collective-permute-start | bytes 1671176 | tf_op jit(solution)/shard_map/ppermute | solution.py:66
  43.6 5.0 %copy-start = (bf16[2,384,2048]{2,1,0:T(8,128)(2,1)S(1)}, bf16[2,384,2048]{2,1,0:T(8,128)(2,1)}, u32[]{:S(2)}) copy-start(bf16[2,384,2048]{2,1,0:T(8,128)(2,1)} %w_gate.7) | copy-start | bytes 9437188
  43.6 5.0 %copy-start.1 = (bf16[2,384,2048]{2,1,0:T(8,128)(2,1)S(1)}, bf16[2,384,2048]{2,1,0:T(8,128)(2,1)}, u32[]{:S(2)}) copy-start(bf16[2,384,2048]{2,1,0:T(8,128)(2,1)} %w_up.7) | copy-start | bytes 9437188
  50.8 5.1 %collective-permute-start.14 = (bf16[4,128,1024]{2,1,0:T(8,128)(2,1)S(1)}, bf16[4,128,1024]{2,1,0:T(8,128)(2,1)S(1)}, u32[]{:S(2)}, u32[]{:S(2)}) collective-permute-start(bf16[4,128,1024]{2,1,0:T(8,128)(2,1)S(1)} %get-tuple-element.63._), channel_id=1, source_target_pairs={{0,2},{2,0},{4,6},{6,4},{8,10},{10,8},{12,14},{14,12},{16,18},{18,... | collective-permute-start | bytes 3145736 | tf_op jit(solution)/shard_map/ppermute | solution.py:66
  53.3 2.7 %collective-permute-start.18 = (bf16[4,128,1024]{2,1,0:T(8,128)(2,1)S(1)}, bf16[4,128,1024]{2,1,0:T(8,128)(2,1)S(1)}, u32[]{:S(2)}, u32[]{:S(2)}) collective-permute-start(bf16[4,128,1024]{2,1,0:T(8,128)(2,1)S(1)} %get-tuple-element.64._), channel_id=1, source_target_pairs={{0,2},{2,0},{4,6},{6,4},{8,10},{10,8},{12,14},{14,12},{16,18},{18,... | collective-permute-start | bytes 3145736 | tf_op jit(solution)/shard_map/ppermute | solution.py:66
  55.0 11.1 %collective-permute-start.25 = (bf16[2,64,2176]{2,1,0:T(8,128)(2,1)S(1)}, bf16[2,64,2176]{2,1,0:T(8,128)(2,1)S(1)}, u32[]{:S(2)}, u32[]{:S(2)}) collective-permute-start(bf16[2,64,2176]{2,1,0:T(8,128)(2,1)S(1)} %collective-permute-done.15.over), channel_id=1, source_target_pairs={{0,2},{2,0},{4,6},{6,4},{8,10},{10,8},{12,14},{14,12},{16,18},{18,... | collective-permute-start | bytes 1671176 | tf_op jit(solution)/shard_map/ppermute | solution.py:66
  55.3 9.2 %collective-permute-start.26 = (bf16[2,64,1024]{2,1,0:T(8,128)(2,1)S(1)}, bf16[2,64,1024]{2,1,0:T(8,128)(2,1)S(1)}, u32[]{:S(2)}, u32[]{:S(2)}) collective-permute-start(bf16[2,64,1024]{2,1,0:T(8,128)(2,1)S(1)} %get-tuple-element.65._), channel_id=1, source_target_pairs={{0,1},{1,0},{2,3},{3,2},{4,5},{5,4},{6,7},{7,6},{8,9},{9,8},{10,11... | collective-permute-start | bytes 786440 | tf_op jit(solution)/shard_map/ppermute | solution.py:66
  55.9 12.2 %collective-permute-start.24 = (bf16[2,64,2176]{2,1,0:T(8,128)(2,1)S(1)}, bf16[2,64,2176]{2,1,0:T(8,128)(2,1)S(1)}, u32[]{:S(2)}, u32[]{:S(2)}) collective-permute-start(bf16[2,64,2176]{2,1,0:T(8,128)(2,1)S(1)} %collective-permute-done.16.side), channel_id=1, source_target_pairs={{0,2},{2,0},{4,6},{6,4},{8,10},{10,8},{12,14},{14,12},{16,18},{18,... | collective-permute-start | bytes 1671176 | tf_op jit(solution)/shard_map/ppermute | solution.py:66
  56.0 10.1 %collective-permute-start.27 = (bf16[2,64,1024]{2,1,0:T(8,128)(2,1)S(1)}, bf16[2,64,1024]{2,1,0:T(8,128)(2,1)S(1)}, u32[]{:S(2)}, u32[]{:S(2)}) collective-permute-start(bf16[2,64,1024]{2,1,0:T(8,128)(2,1)S(1)} %get-tuple-element.77), channel_id=1, source_target_pairs={{0,4},{2,6},{4,0},{6,2},{8,12},{10,14},{12,8},{14,10},{16,20},{18,... | collective-permute-start | bytes 786440 | tf_op jit(solution)/shard_map/ppermute | solution.py:66
  57.8 20.1 %collective-permute-start.17 = (bf16[4,64,1024]{2,1,0:T(8,128)(2,1)S(1)}, bf16[4,64,1024]{2,1,0:T(8,128)(2,1)S(1)}, u32[]{:S(2)}, u32[]{:S(2)}) collective-permute-start(bf16[4,64,1024]{2,1,0:T(8,128)(2,1)S(1)} %get-tuple-element.67._), channel_id=1, source_target_pairs={{0,1},{1,0},{2,3},{3,2},{4,5},{5,4},{6,7},{7,6},{8,9},{9,8},{10,11... | collective-permute-start | bytes 1572872 | tf_op jit(solution)/shard_map/ppermute | solution.py:66
  64.5 13.4 %collective-permute-start.19 = (bf16[2,128,1024]{2,1,0:T(8,128)(2,1)S(1)}, bf16[2,128,1024]{2,1,0:T(8,128)(2,1)S(1)}, u32[]{:S(2)}, u32[]{:S(2)}) collective-permute-start(bf16[2,128,1024]{2,1,0:T(8,128)(2,1)S(1)} %get-tuple-element.70._.refs_0_), channel_id=1, source_target_pairs={{0,4},{2,6},{4,0},{6,2},{8,12},{10,14},{12,8},{14,10},{16,20},{18,... | collective-permute-start | bytes 1572872 | tf_op jit(solution)/shard_map/ppermute | solution.py:66
  66.1 1.7 %collective-permute-start.28 = (bf16[2,64,1024]{2,1,0:T(8,128)(2,1)S(1)}, bf16[2,64,1024]{2,1,0:T(8,128)(2,1)S(1)}, u32[]{:S(2)}, u32[]{:S(2)}) collective-permute-start(bf16[2,64,1024]{2,1,0:T(8,128)(2,1)S(1)} %collective-permute-done.26.left), channel_id=1, source_target_pairs={{0,2},{2,0},{4,6},{6,4},{8,10},{10,8},{12,14},{14,12},{16,18},{18,... | collective-permute-start | bytes 786440 | tf_op jit(solution)/shard_map/ppermute | solution.py:66
  66.2 1.9 %collective-permute-start.29 = (bf16[2,64,1024]{2,1,0:T(8,128)(2,1)S(1)}, bf16[2,64,1024]{2,1,0:T(8,128)(2,1)S(1)}, u32[]{:S(2)}, u32[]{:S(2)}) collective-permute-start(bf16[2,64,1024]{2,1,0:T(8,128)(2,1)S(1)} %collective-permute-done.27.right), channel_id=1, source_target_pairs={{0,2},{2,0},{4,6},{6,4},{8,10},{10,8},{12,14},{14,12},{16,18},{18,... | collective-permute-start | bytes 786440 | tf_op jit(solution)/shard_map/ppermute | solution.py:66
  75.0 5.0 %collective-permute-start.30 = (bf16[4,128,1024]{2,1,0:T(8,128)(2,1)S(1)}, bf16[4,128,1024]{2,1,0:T(8,128)(2,1)S(1)}, u32[]{:S(2)}, u32[]{:S(2)}) collective-permute-start(bf16[4,128,1024]{2,1,0:T(8,128)(2,1)S(1)} %get-tuple-element.82._), channel_id=1, source_target_pairs={{0,2},{2,0},{4,6},{6,4},{8,10},{10,8},{12,14},{14,12},{16,18},{18,... | collective-permute-start | bytes 3145736 | tf_op jit(solution)/shard_map/ppermute | solution.py:66
  77.5 3.2 %collective-permute-start.32 = (bf16[4,128,1024]{2,1,0:T(8,128)(2,1)S(1)}, bf16[4,128,1024]{2,1,0:T(8,128)(2,1)S(1)}, u32[]{:S(2)}, u32[]{:S(2)}) collective-permute-start(bf16[4,128,1024]{2,1,0:T(8,128)(2,1)S(1)} %get-tuple-element.86), channel_id=1, source_target_pairs={{0,2},{2,0},{4,6},{6,4},{8,10},{10,8},{12,14},{14,12},{16,18},{18,... | collective-permute-start | bytes 3145736 | tf_op jit(solution)/shard_map/ppermute | solution.py:66
  78.0 9.2 %collective-permute-start.20 = (bf16[2,64,1024]{2,1,0:T(8,128)(2,1)S(1)}, bf16[2,64,1024]{2,1,0:T(8,128)(2,1)S(1)}, u32[]{:S(2)}, u32[]{:S(2)}) collective-permute-start(bf16[2,64,1024]{2,1,0:T(8,128)(2,1)S(1)} %get-tuple-element.72._), channel_id=1, source_target_pairs={{0,4},{2,6},{4,0},{6,2},{8,12},{10,14},{12,8},{14,10},{16,20},{18,... | collective-permute-start | bytes 786440 | tf_op jit(solution)/shard_map/ppermute | solution.py:66
  78.5 9.2 %collective-permute-start.21 = (bf16[2,64,1024]{2,1,0:T(8,128)(2,1)S(1)}, bf16[2,64,1024]{2,1,0:T(8,128)(2,1)S(1)}, u32[]{:S(2)}, u32[]{:S(2)}) collective-permute-start(bf16[2,64,1024]{2,1,0:T(8,128)(2,1)S(1)} %get-tuple-element.74), channel_id=1, source_target_pairs={{0,1},{1,0},{2,3},{3,2},{4,5},{5,4},{6,7},{7,6},{8,9},{9,8},{10,11... | collective-permute-start | bytes 786440 | tf_op jit(solution)/shard_map/ppermute | solution.py:66
  80.2 17.6 %collective-permute-start.31 = (bf16[4,64,1024]{2,1,0:T(8,128)(2,1)S(1)}, bf16[4,64,1024]{2,1,0:T(8,128)(2,1)S(1)}, u32[]{:S(2)}, u32[]{:S(2)}) collective-permute-start(bf16[4,64,1024]{2,1,0:T(8,128)(2,1)S(1)} %get-tuple-element.84._), channel_id=1, source_target_pairs={{0,1},{1,0},{2,3},{3,2},{4,5},{5,4},{6,7},{7,6},{8,9},{9,8},{10,11... | collective-permute-start | bytes 1572872 | tf_op jit(solution)/shard_map/ppermute | solution.py:66
  80.8 17.0 %collective-permute-start.33 = (bf16[2,128,1024]{2,1,0:T(8,128)(2,1)S(1)}, bf16[2,128,1024]{2,1,0:T(8,128)(2,1)S(1)}, u32[]{:S(2)}, u32[]{:S(2)}) collective-permute-start(bf16[2,128,1024]{2,1,0:T(8,128)(2,1)S(1)} %get-tuple-element.88), channel_id=1, source_target_pairs={{0,4},{2,6},{4,0},{6,2},{8,12},{10,14},{12,8},{14,10},{16,20},{18,... | collective-permute-start | bytes 1572872 | tf_op jit(solution)/shard_map/ppermute | solution.py:66
  87.8 12.9 %collective-permute-start.22 = (bf16[64,2048]{1,0:T(8,128)(2,1)S(1)}, bf16[64,2048]{1,0:T(8,128)(2,1)S(1)}, u32[]{:S(2)}, u32[]{:S(2)}) collective-permute-start(bf16[64,2048]{1,0:T(8,128)(2,1)S(1)} %get-tuple-element.76), channel_id=1, source_target_pairs={{0,16},{2,18},{4,20},{6,22},{8,24},{10,26},{12,28},{14,30},{16,0},... | collective-permute-start | bytes 786440 | tf_op jit(solution)/shard_map/ppermute | solution.py:71
  97.9 7.5 %collective-permute-start.34 = (bf16[2,64,1024]{2,1,0:T(8,128)(2,1)S(1)}, bf16[2,64,1024]{2,1,0:T(8,128)(2,1)S(1)}, u32[]{:S(2)}, u32[]{:S(2)}) collective-permute-start(bf16[2,64,1024]{2,1,0:T(8,128)(2,1)S(1)} %get-tuple-element.90), channel_id=1, source_target_pairs={{0,4},{2,6},{4,0},{6,2},{8,12},{10,14},{12,8},{14,10},{16,20},{18,... | collective-permute-start | bytes 786440 | tf_op jit(solution)/shard_map/ppermute | solution.py:66
  99.6 6.9 %collective-permute-start.35 = (bf16[2,64,1024]{2,1,0:T(8,128)(2,1)S(1)}, bf16[2,64,1024]{2,1,0:T(8,128)(2,1)S(1)}, u32[]{:S(2)}, u32[]{:S(2)}) collective-permute-start(bf16[2,64,1024]{2,1,0:T(8,128)(2,1)S(1)} %get-tuple-element.92), channel_id=1, source_target_pairs={{0,1},{1,0},{2,3},{3,2},{4,5},{5,4},{6,7},{7,6},{8,9},{9,8},{10,11... | collective-permute-start | bytes 786440 | tf_op jit(solution)/shard_map/ppermute | solution.py:66
  106.6 11.1 %collective-permute-start.36 = (bf16[64,2048]{1,0:T(8,128)(2,1)S(1)}, bf16[64,2048]{1,0:T(8,128)(2,1)S(1)}, u32[]{:S(2)}, u32[]{:S(2)}) collective-permute-start(bf16[64,2048]{1,0:T(8,128)(2,1)S(1)} %get-tuple-element.93), channel_id=1, source_target_pairs={{0,8},{2,10},{4,12},{6,14},{8,16},{10,18},{12,20},{14,22},{16,24},... | collective-permute-start | bytes 786440 | tf_op jit(solution)/shard_map/ppermute | solution.py:71
  108.5 11.3 %collective-permute-start.37 = (bf16[64,2048]{1,0:T(8,128)(2,1)S(1)}, bf16[64,2048]{1,0:T(8,128)(2,1)S(1)}, u32[]{:S(2)}, u32[]{:S(2)}) collective-permute-start(bf16[64,2048]{1,0:T(8,128)(2,1)S(1)} %get-tuple-element.94), channel_id=1, source_target_pairs={{0,24},{2,26},{4,28},{6,30},{8,0},{10,2},{12,4},{14,6},{16,8},{18,... | collective-permute-start | bytes 786440 | tf_op jit(solution)/shard_map/ppermute | solution.py:71

commit v10 on v9

--- a/solution.py
+++ b/solution.py
@@ -86,21 +86,16 @@
     )(*operands)
 
 
-def prepare_kernel(place, tokens, gates_any, ids_any, first, table, gates, ids, sems):
-    piece = first.shape[0]
-    width = first.shape[1] - table.shape[1]
-    near = pl.multiple_of(place[3] * piece, piece)
+def prepare_kernel(place, tokens, gates, ids, near, far, sems):
+    piece, width = far.shape
+    at = pl.multiple_of(place[3] * piece, piece)
+    other = pl.multiple_of((1 - place[3]) * piece, piece)
     copies = [
-        pltpu.make_async_copy(gates_any, gates, sems.at[0]),
-        pltpu.make_async_copy(ids_any, ids, sems.at[1]),
-        pltpu.make_async_copy(
-            tokens.at[pl.ds(near, piece), :], first.at[:, pl.ds(0, width)], sems.at[2]
-        ),
+        pltpu.make_async_copy(tokens.at[pl.ds(at, piece), :], near.at[:, pl.ds(0, width)], sems.at[0]),
+        pltpu.make_async_copy(tokens.at[pl.ds(other, piece), :], far, sems.at[1]),
     ]
     for copy in copies:
         copy.start()
-    copies[0].wait()
-    copies[1].wait()
     rest = gates[...]
     terms = []
     for _ in range(3):
@@ -110,24 +105,20 @@
     terms.append(ids[...].astype(jnp.float32))
     unused = piece - 4 * gates.shape[0]
     terms.append(jnp.zeros((unused, gates.shape[1]), jnp.float32))
-    packed = jnp.concatenate(terms, axis=0).astype(jnp.bfloat16)
-    first[:, width:] = packed
-    table[...] = packed
-    copies[2].wait()
+    near[:, width:] = jnp.concatenate(terms, axis=0).astype(jnp.bfloat16)
+    for copy in copies:
+        copy.wait()
 
 
 def prepare(place, cotangent, gates, ids, piece):
+    width = cotangent.shape[1]
     return small(
         prepare_kernel,
         "prepare",
-        [(piece, cotangent.shape[1] + 128), (piece, 128)],
-        "shhh",
+        [(piece, width + 128), (piece, width)],
+        "shvv",
         (place, cotangent, gates, ids),
-        [
-            pltpu.VMEM(gates.shape, jnp.float32),
-            pltpu.VMEM(ids.shape, jnp.int32),
-            pltpu.SemaphoreType.DMA((3,)),
-        ],
+        [pltpu.SemaphoreType.DMA((2,))],
         limit=4,
     )
 
@@ -149,18 +140,19 @@
     )[0]
 
 
-def relay_kernel(came, part, line, following):
+def relay_kernel(came, part, _, __, ___, line, following):
     line[0] = came[...]
     following[...] = part[...]
 
 
-def relay(came, part):
-    return small(
-        relay_kernel, "relay", [(1,) + came.shape, part.shape], "vv", (came, part)
-    )
-
-
-def turn_kernel(gate, up, _, gate_t, up_t):
+def relay(came, part, *after):
+    return small(
+        relay_kernel, "relay", [(1,) + came.shape, part.shape], "vvooo", (came, part, *after)
+    )
+
+
+def turn_kernel(gate, up, *refs):
+    gate_t, up_t = refs[-2:]
     tile = 128
     for source, target in ((gate, gate_t), (up, up_t)):
         for e in range(source.shape[0]):
@@ -170,43 +162,37 @@
                 )
 
 
-def turn(saved_gate, saved_up, after):
+def turn(saved_gate, saved_up, *after):
     count, units, slots = saved_gate.shape
     return small(
         turn_kernel,
         "turn",
         [(count, slots, units)] * 2,
-        "vvo",
-        (saved_gate, saved_up, after),
+        "vv" + "o" * len(after),
+        (saved_gate, saved_up, *after),
         limit=12,
     )
 
 
-def corner_kernel(place, tokens, first, over, side, whole_over, left, right, sem):
-    _, piece, middle = left.shape
-    far = pl.multiple_of((1 - place[3]) * piece, piece)
-    copy = pltpu.make_async_copy(
-        tokens.at[pl.ds(far, piece), pl.ds(middle, middle)], right.at[0], sem.at[0]
-    )
-    copy.start()
+def corner_kernel(far, first, over, side, whole_over, left, right):
+    middle = left.shape[2]
     whole_over[0] = first[...]
     whole_over[1:] = over[...]
     left[0] = first[:, :middle]
     left[1:] = over[:, :, :middle]
+    right[0] = far[:, middle:]
     right[1:] = side[:, :, middle:2 * middle]
-    copy.wait()
-
-
-def own_corner(place, cotangent, first, over, side):
+
+
+def own_corner(far, first, over, side):
     count, piece, width = over.shape
-    middle = cotangent.shape[1] // 2
+    middle = far.shape[1] // 2
     return small(
         corner_kernel,
         "own_corner",
         [(count + 1, piece, width)] + [(count + 1, piece, middle)] * 2,
-        "shvvv",
-        (place, cotangent, first, over, side),
-        (pltpu.SemaphoreType.DMA((1,)),),
+        "vvvv",
+        (far, first, over, side),
     )
 
 
@@ -275,7 +261,7 @@
                 if ry == 1:
                     table = (over, over_c)[c][i, :32, width:]
                 elif r == 0:
-                    table = (own, own_c)[c][:32]
+                    table = (own, own_c)[c][:32, width:]
                 else:
                     table = (lines, lines_c)[c][r_place(r, offsets), :32, width:]
                 tables.append(table.astype(jnp.float32))
@@ -347,77 +333,72 @@
     )
 
 
-def hidden_kernel(offsets, line_count, place, own, own_c, lines, lines_c, side, side_c, over, over_c,
-                  diag, diag_c, pick, gate, w_down, saved_gate, saved_up, _, grads, slots):
-    piece = over.shape[1]
-    width = diag.shape[2]
+def hidden_kernel(offsets, rows_of, line_count, place, *refs):
+    *sources, pick, gate, w_down, saved_gate, saved_up, _, grads, slots = refs
+    sources = [sources[at:at + 2] for at in range(0, len(sources), 2)]
+    near, far = (sources.pop(0), sources.pop(0)) if offsets[0] == 0 and 0 in rows_of else (None, None)
+    lines, side = (sources.pop(0), sources.pop(0)) if 0 in rows_of else (None, None)
+    over, diag = (sources.pop(0), sources.pop(0)) if 1 in rows_of else (None, None)
+    width = w_down.shape[2]
     rows = pick.shape[1] // 2
     units = w_down.shape[1]
-    near = pl.multiple_of(place[3] * piece, piece)
-    far = pl.multiple_of((1 - place[3]) * piece, piece)
+    pairs = [(i, r, ry) for i, r in enumerate(offsets) for ry in rows_of]
 
     @pl.loop(0, width // TILE)
     def _(k):
         at = pl.ds(pl.multiple_of(k * TILE, TILE), TILE)
-        for i, r in enumerate(offsets):
-            for ry in range(2):
-                parts = []
-                for c in range(2):
-                    if ry == 1:
-                        parts += [(over, over_c)[c][i, :, at], (diag, diag_c)[c][i, :, at]]
-                    elif r == 0:
-                        group = (own, own_c)[c]
-                        parts += [group[pl.ds(near, piece), at], group[pl.ds(far, piece), at]]
-                    else:
-                        j = r_place(r, offsets)
-                        parts += [(lines, lines_c)[c][j, :, at], (side, side_c)[c][j, :, at]]
-                p = i * 2 + ry
-                picked = jnp.dot(
-                    pick[p], jnp.concatenate(parts, axis=0), preferred_element_type=jnp.float32
-                )
-                weight = gate[p]
-                weight = jnp.concatenate([weight] * (TILE // weight.shape[1]), axis=1)
-                scaled = (picked * weight).astype(jnp.bfloat16)
-                slots[0, p * rows:(p + 1) * rows, at] = scaled[:rows]
-                slots[1, p * rows:(p + 1) * rows, at] = scaled[rows:]
+        for q, (i, r, ry) in enumerate(pairs):
+            parts = []
+            for c in range(2):
+                if ry == 1:
+                    parts += [over[c][i, :, at], diag[c][i, :, at]]
+                elif r == 0:
+                    parts += [near[c][:, at], far[c][:, at]]
+                else:
+                    j = r_place(r, offsets)
+                    parts += [lines[c][j, :, at], side[c][j, :, at]]
+            p = i * 2 + ry
+            picked = jnp.dot(
+                pick[p], jnp.concatenate(parts, axis=0), preferred_element_type=jnp.float32
+            )
+            weight = gate[p]
+            weight = jnp.concatenate([weight] * (TILE // weight.shape[1]), axis=1)
+            scaled = (picked * weight).astype(jnp.bfloat16)
+            slots[0, q * rows:(q + 1) * rows, at] = scaled[:rows]
+            slots[1, q * rows:(q + 1) * rows, at] = scaled[rows:]
 
     for e in range(2):
         total = lax.dot_general(
             slots[e], w_down[e], (((1,), (1,)), ((), ())), preferred_element_type=jnp.float32
         )
-        for i, r in enumerate(offsets):
-            for ry in range(2):
-                p = i * 2 + ry
-                mine = slice(p * rows, (p + 1) * rows)
-                saved = pl.ds(pair_base(place, line_count, r, ry, rows), rows)
-                hidden_grad = total[mine]
-                gate_value = saved_gate[e, saved, :].astype(jnp.float32)
-                up_value = saved_up[e, saved, :].astype(jnp.float32)
-                sigmoid_gate = jax.nn.sigmoid(gate_value)
-                grads[e, mine, units:] = (hidden_grad * gate_value * sigmoid_gate).astype(
-                    jnp.bfloat16
-                )
-                grads[e, mine, :units] = (
-                    hidden_grad * up_value * sigmoid_gate * (1.0 + gate_value * (1.0 - sigmoid_gate))
-                ).astype(jnp.bfloat16)
-
-
-def hidden(offsets, line_count, place, own, own_c, moved, pick, gate, w_down, saved, after):
-    width = own.shape[1]
-    units = w_down.shape[1]
-    count = pick.shape[0] * pick.shape[1] // 2
-    return small(
-        functools.partial(hidden_kernel, offsets, line_count),
+        for q, (i, r, ry) in enumerate(pairs):
+            mine = slice(q * rows, (q + 1) * rows)
+            saved = pl.ds(pair_base(place, line_count, r, ry, rows), rows)
+            hidden_grad = total[mine]
+            gate_value = saved_gate[e, saved, :].astype(jnp.float32)
+            up_value = saved_up[e, saved, :].astype(jnp.float32)
+            sigmoid_gate = jax.nn.sigmoid(gate_value)
+            grads[e, mine, units:] = (hidden_grad * gate_value * sigmoid_gate).astype(jnp.bfloat16)
+            grads[e, mine, :units] = (
+                hidden_grad * up_value * sigmoid_gate * (1.0 + gate_value * (1.0 - sigmoid_gate))
+            ).astype(jnp.bfloat16)
+
+
+def hidden(offsets, rows_of, line_count, place, sources, pick, gate, w_down, saved, after):
+    _, units, width = w_down.shape
+    count = len(offsets) * len(rows_of) * pick.shape[1] // 2
+    return small(
+        functools.partial(hidden_kernel, offsets, rows_of, line_count),
         "hidden",
         [(2, count, 2 * units)],
-        "s" + "v" * 15 + "o",
-        (place, own, own_c, *moved, pick, gate, w_down, *saved, after),
+        "s" + "v" * (len(sources) + 5) + "o",
+        (place, *sources, pick, gate, w_down, *saved, after),
         [pltpu.VMEM((2, count, width), jnp.bfloat16)],
         limit=12,
     )[0]
 
 
-def sums_kernel(offset, grads, w_gate, w_up, pick_t, _, keep, send, slots):
+def sums_kernel(offset, pairs, grads, w_gate, w_up, pick_t, _, keep, send, slots):
     rows = pick_t.shape[2] // 2
     tokens = pick_t.shape[1] // 2
 
@@ -430,23 +411,23 @@
             slots[e] = jnp.dot(grads[e], weights, preferred_element_type=jnp.float32).astype(
                 jnp.bfloat16
             )
-        for p in range(pick_t.shape[0]):
-            mine = slice(p * rows, (p + 1) * rows)
+        for q, p in enumerate(pairs):
+            mine = slice(q * rows, (q + 1) * rows)
             both = jnp.concatenate([slots[0, mine], slots[1, mine]], axis=0)
             total = jnp.dot(pick_t[p], both, preferred_element_type=jnp.float32).astype(
                 jnp.bfloat16
             )
-            keep[p, :, at] = total[:tokens]
-            send[p, :, at] = total[tokens:]
-
-
-def sums(offset, width, grads, w_gate, w_up, pick_t, after, work=0):
-    pairs, tokens, _ = pick_t.shape
-    _, count, units = grads.shape
-    return small(
-        functools.partial(sums_kernel, offset),
+            keep[q, :, at] = total[:tokens]
+            send[q, :, at] = total[tokens:]
+
+
+def sums(offset, width, pairs, grads, w_gate, w_up, pick_t, after, work=0):
+    tokens = pick_t.shape[1]
+    count = grads.shape[1]
+    return small(
+        functools.partial(sums_kernel, offset, pairs),
         "sums",
-        [(pairs, tokens // 2, width)] * 2,
+        [(len(pairs), tokens // 2, width)] * 2,
         "vvvvo",
         (grads, w_gate, w_up, pick_t, after),
         [pltpu.VMEM((2, count, TILE), jnp.bfloat16)],
@@ -470,6 +451,25 @@
         "vvo",
         (keep, came, after),
     )
+
+
+def apart_right_kernel(keep_a, came_a, keep_b, came_b, _, send, kept):
+    middle = kept.shape[2]
+    kept[...] = keep_a[:, :, middle:] + came_a[:, :, middle:]
+    send[...] = keep_b[...] + came_b[...]
+
+
+def apart_left_kernel(keep_a, came_a, keep_b, came_b, _, send, kept):
+    _, piece, middle = kept.shape
+    for i in range(keep_a.shape[0]):
+        kept[2 * i] = keep_a[i, :piece, :middle] + came_a[i, :piece, :middle]
+        send[2 * i] = keep_a[i, piece:, :middle] + came_a[i, piece:, :middle]
+        kept[2 * i + 1] = keep_b[i, :piece] + came_b[i, :piece]
+        send[2 * i + 1] = keep_b[i, piece:] + came_b[i, piece:]
+
+
+def first_apart(kernel, dims, row_a, row_b, after):
+    return small(kernel, "first_apart", [dims] * 2, "vvvvo", (*row_a, *row_b, after))
 
 
 def first_right_kernel(keep, came, _, send, kept):
@@ -552,24 +552,17 @@
     me, half = lax.axis_index("expert"), lax.axis_index("tp")
     place = jnp.stack([me % 2, me // 2 % 2, me // 4, half]).astype(jnp.int32)
 
-    part, table = prepare(place, cotangent, gates.T, expert_ids.T, piece)
+    part, far = prepare(place, cotangent, gates.T, expert_ids.T, piece)
     first = swap(part, "expert", 2)
-    own_c, table_c = swap(cotangent, "expert", 1), swap(table, "expert", 1)
-    gathered = []
-
-    def compute(index, after):
-        offsets, moved = CHUNKS[index], gathered[index]
+    near_c, far_c = swap(part, "expert", 1), swap(far, "expert", 1)
+    own = [part, near_c, far, far_c]
+
+    def routed(offsets, moved):
         line, line_c, _, _, over, over_c = moved[:6]
-        pick, pick_t, gate = route(
-            offsets, place, table, table_c, line, line_c, over, over_c, capacity
-        )
-        grads = hidden(
-            offsets, lines, place, cotangent, own_c, moved, pick, gate, w_down, saved, after
-        )
-        return grads, pick_t
-
-    def sums_by_token(offset, grads, pick_t, after, work=0):
-        keep, send = sums(offset, middle, grads, w_gate, w_up, pick_t, after, work)
+        return route(offsets, place, own[0], near_c, line, line_c, over, over_c, capacity)
+
+    def sums_by_token(offset, width, pairs, grads, pick_t, after):
+        keep, send = sums(offset, width, pairs, grads, w_gate, w_up, pick_t, after)
         return [keep, swap(send, "expert", 1)], send
 
     def both_cores(arrays):
@@ -584,30 +577,39 @@
         return keep, swap(send, "expert", 2), send
 
     (_, near), (third, second) = CHUNKS
-    line, part = relay(along_line(part, -near), part)
+    line, part = relay(along_line(part, -near), part, first, near_c, far_c)
     side, over = swap(line, "tp", 1), swap(line, "expert", 2)
     came = [along_line(part, -third), along_line(part, -second)]
+    line_c = swap(line, "expert", 1)
     saved = turn(saved_gate, saved_up, line)
-    over, left, right = own_corner(place, cotangent, first, over, side)
+    over, left, right = own_corner(far, first, over, side)
     left, right = swap(left, "tp", 1), swap(right, "expert", 2)
-    moved = both_cores([line, side, over])
+    moved = [line, line_c] + both_cores([side, over])
     line = stack(came, saved[0], work=68719476736)
-    line = stack([line], *moved[1::2], own_c, table_c)[0]
-    gathered.append(moved + both_cores([join(left, right, line)]))
+    line = stack([line], moved[5])[0]
+    moved += both_cores([join(left, right, line)])
+    pick, pick_t, gate = routed(CHUNKS[0], moved)
 
     side, over = swap(line, "tp", 1), swap(line, "expert", 2)
-    grads, pick_t = compute(0, line)
-    early_l, after = sums_by_token(0, grads, pick_t, grads)
-    early_r, after = sums_by_token(middle, grads, pick_t, after)
+    grads = hidden(CHUNKS[0], (0, 1), lines, place, own + moved, pick, gate, w_down, saved, line)
+    early_l, after = sums_by_token(0, middle, (0, 1, 2, 3), grads, pick_t, grads)
+    early_r, after = sums_by_token(middle, middle, (0, 1, 2, 3), grads, pick_t, after)
     left, right = corner(over, side, middle, after, work=68719476736)
     after = left
     left, right = swap(left, "tp", 1), swap(right, "expert", 2)
-    early_l = step_left(*early_l, after)
+    moved = both_cores([line, side, over])
+    pick, pick_t, gate = routed(CHUNKS[1], moved)
+    grads = hidden(CHUNKS[1], (0,), lines, place, moved[:4], pick, gate, w_down, saved, after)
+    row_a, after = sums_by_token(0, 2 * middle, (0, 2), grads, pick_t, grads)
+    diag = join(left, right, after, work=0)
+    early_l = step_left(*early_l, diag)
     early_r = step_right(*early_r, early_l[-1])
-    moved = both_cores([line, side, over])
-    other = [swap(left, "expert", 1), swap(right, "expert", 1)]
-    moved += [join(left, right, early_r[-1], work=0), join(*other, early_r[-1])]
-    gathered.append(moved)
+    diags = both_cores([diag])
+    grads = hidden(
+        CHUNKS[1], (1,), lines, place, moved[4:] + diags, pick, gate, w_down, saved, early_r[-1]
+    )
+    row_br, after = sums_by_token(middle, middle, (1, 3), grads, pick_t, grads)
+    row_bl, after = sums_by_token(0, middle, (1, 3), grads, pick_t, after)
 
     def second_step(offsets, sums_of_two, after, came):
         send_l, left, send_r, right = second_sum(*sums_of_two, after)
@@ -615,13 +617,12 @@
         rows = third_sum(offsets, left, came_l, right, came_r, send_l if came is None else came)
         return rows[0], [row if r == 0 else along_line(row, r) for r, row in zip(offsets, rows)], send_l
 
-    grads, pick_t = compute(1, early_r[-1])
-    late_l, after = sums_by_token(0, grads, pick_t, grads)
-    late_r, _ = sums_by_token(middle, grads, pick_t, after)
     done, early, after = second_step(CHUNKS[0], early_l[:2] + early_r[:2], early_r[-1], None)
-    late_l = step_left(*late_l, after)
-    late_r = step_right(*late_r, late_l[-1])
-    _, late, _ = second_step(CHUNKS[1], late_l[:2] + late_r[:2], done, early[-1])
+    send, keep_r = first_apart(apart_right_kernel, (2, 2 * piece, middle), row_a, row_br, after)
+    came_r = swap(send, "expert", 2)
+    send, keep_l = first_apart(apart_left_kernel, (4, piece, middle), row_a, row_bl, send)
+    came_l = swap(send, "tp", 1)
+    _, late, _ = second_step(CHUNKS[1], (keep_l, came_l, keep_r, came_r), done, early[-1])
     terms = early + late
     return pl.pallas_call(
         last_kernel,

time: 121 us -> 124 us (1.025)
  waiting for transfers between devices: 56.3 us -> 59.2 us
    ppermute x32, waiting for transfers between devices: 31.1 us -> 33 us  [swap(): return lax.ppermute(value, axis, [(i, i ^ step) for i in range(count)])]
    unnamed x14 -> x16, local copies, waits for them, and re-layouts: 2.74 us -> 3.79 us
    pallas_call x26 -> x27, Pallas kernels: 25.7 us -> 25.2 us  [small(): pl.pallas_call(kernel, out_shape=[out if hasattr(out, 'dtype') else jax.S...]
  transfers between devices with their start and end apart: 38 -> 38, of which waited for: 20 -> 17; matrix products, arithmetic and copies ran while one was open for 0% -> 0% of each run, Pallas kernels for 20% -> 20%
where the time goes in v10:
time: 124 us; the launch traced here: 123 us
  waiting for transfers between devices  59.2 us (48%)
  starting transfers between devices  33.9 us (27%)
  Pallas kernels  26.1 us (21%)
  local copies, waits for them, and re-layouts  3.79 us (3%)
    ppermute x32, waiting for transfers between devices, swap(): return lax.ppermute(value, axis, [(i, i ^ step) for i in range(count)])  33 us
    ppermute x6, waiting for transfers between devices, along_line(): lax.ppermute(value, 'expert', [(i, (i + 4 * shift) % count) for i in rang...  26.2 us
    pallas_call x27, Pallas kernels, small(): pl.pallas_call(kernel, out_shape=[out if hasattr(out, 'dtype') else jax.S...  25.2 us
    ppermute x32, starting transfers between devices, swap(): return lax.ppermute(value, axis, [(i, i ^ step) for i in range(count)])  22.7 us
    ppermute x6, starting transfers between devices, along_line(): lax.ppermute(value, 'expert', [(i, (i + 4 * shift) % count) for i in rang...  11.2 us
    unnamed x16, local copies, waits for them, and re-layouts  3.79 us
  transfers between devices with their start and end apart: 38, of which 17 were waited for; matrix products, arithmetic and copies ran while one was open for 0% of the time, Pallas kernels for 20%

profile of v10, /device:TPU:0, one launch (start us, length us, event | category | flops | bytes accessed | tf_op | source)
XLA Modules:
  0.0 123.5 jit_solution(10969137384735939790)
XLA Ops:
  0.1 1.1 copy-done.5
  1.2 0.7 copy-done.6
  1.9 0.7 copy-done.7
  2.6 0.6 prepare.1
  3.2 0.5 collective-permute-start
  3.7 3.7 %collective-permute-start.2 = (bf16[64,2176]{1,0:T(8,128)(2,1)S(1)}, bf16[64,2176]{1,0:T(8,128)(2,1)S(1)}, u32[]{:S(2)}, u32[]{:S(2)}) collective-permute-start(bf16[64,2176]{1,0:T(8,128)(2,1)S(1)} %get-tuple-element.52.part.own.refs_0_), channel_id=1, source_target_pairs={{0,16},{2,18},{4,20},{6,22},{8,24},{10,26},{12,28},{14,30},{16,0},... | collective-permute-start | bytes 835592 | tf_op jit(solution)/shard_map/ppermute | solution.py:71
  7.4 1.5 %collective-permute-start.3 = (bf16[64,2176]{1,0:T(8,128)(2,1)S(1)}, bf16[64,2176]{1,0:T(8,128)(2,1)S(1)}, u32[]{:S(2)}, u32[]{:S(2)}) collective-permute-start(bf16[64,2176]{1,0:T(8,128)(2,1)S(1)} %get-tuple-element.52.part.own.refs_0_), channel_id=1, source_target_pairs={{0,4},{2,6},{4,0},{6,2},{8,12},{10,14},{12,8},{14,10},{16,20},{18,... | collective-permute-start | bytes 835592 | tf_op jit(solution)/shard_map/ppermute | solution.py:66
  8.9 1.5 %collective-permute-done.1.___.refs_3_ = bf16[64,2048]{1,0:T(8,128)(2,1)S(1)} collective-permute-done((bf16[64,2048]{1,0:T(8,128)(2,1)S(1)}, bf16[64,2048]{1,0:T(8,128)(2,1)S(1)}, u32[]{:S(2)}, u32[]{:S(2)}) %collective-permute-start.1) | collective-permute-done | bytes 262176 | tf_op jit(solution)/shard_map/ppermute | solution.py:66
  10.4 10.2 %collective-permute-done.2.came = bf16[64,2176]{1,0:T(8,128)(2,1)S(1)} collective-permute-done((bf16[64,2176]{1,0:T(8,128)(2,1)S(1)}, bf16[64,2176]{1,0:T(8,128)(2,1)S(1)}, u32[]{:S(2)}, u32[]{:S(2)}) %collective-permute-start.2) | collective-permute-done | bytes 278560 | tf_op jit(solution)/shard_map/ppermute | solution.py:71
  20.6 1.6 %collective-permute-start.5 = (bf16[1,64,2176]{2,1,0:T(8,128)(2,1)S(1)}, bf16[1,64,2176]{2,1,0:T(8,128)(2,1)S(1)}, u32[]{:S(2)}, u32[]{:S(2)}) collective-permute-start(bf16[1,64,2176]{2,1,0:T(8,128)(2,1)S(1)} %get-tuple-element.54.refs_0_.lines.refs_4_), channel_id=1, source_target_pairs={{0,1},{1,0},{2,3},{3,2},{4,5},{5,4},{6,7},{7,6},{8,9},{9,8},{10,11... | collective-permute-start | bytes 835592 | tf_op jit(solution)/shard_map/ppermute | solution.py:66
  22.3 1.5 %collective-permute-start.7 = (bf16[1,64,2176]{2,1,0:T(8,128)(2,1)S(1)}, bf16[1,64,2176]{2,1,0:T(8,128)(2,1)S(1)}, u32[]{:S(2)}, u32[]{:S(2)}) collective-permute-start(bf16[1,64,2176]{2,1,0:T(8,128)(2,1)S(1)} %get-tuple-element.54.refs_0_.lines.refs_4_), channel_id=1, source_target_pairs={{0,4},{2,6},{4,0},{6,2},{8,12},{10,14},{12,8},{14,10},{16,20},{18,... | collective-permute-start | bytes 835592 | tf_op jit(solution)/shard_map/ppermute | solution.py:66
  23.8 3.5 %collective-permute-start.11 = (bf16[64,2176]{1,0:T(8,128)(2,1)S(1)}, bf16[64,2176]{1,0:T(8,128)(2,1)S(1)}, u32[]{:S(2)}, u32[]{:S(2)}) collective-permute-start(bf16[64,2176]{1,0:T(8,128)(2,1)S(1)} %get-tuple-element.58), channel_id=1, source_target_pairs={{0,24},{2,26},{4,28},{6,30},{8,0},{10,2},{12,4},{14,6},{16,8},{18,... | collective-permute-start | bytes 835592 | tf_op jit(solution)/shard_map/ppermute | solution.py:71
  27.3 1.3 %copy-done.4 = bf16[2,384,768]{2,1,0:T(8,128)(2,1)S(1)} copy-done((bf16[2,384,768]{2,1,0:T(8,128)(2,1)S(1)}, bf16[2,384,768]{2,1,0:T(8,128)(2,1)}, u32[]{:S(2)}) %copy-start.4) | copy-done | bytes 1179672
  28.6 0.7 turn.1
  29.2 1.0 collective-permute-done.7.over
  30.4 0.7 collective-permute-start.9
  31.1 1.4 %collective-permute-start.10 = (bf16[2,64,1024]{2,1,0:T(8,128)(2,1)S(1)}, bf16[2,64,1024]{2,1,0:T(8,128)(2,1)S(1)}, u32[]{:S(2)}, u32[]{:S(2)}) collective-permute-start(bf16[2,64,1024]{2,1,0:T(8,128)(2,1)S(1)} %get-tuple-element.57), channel_id=1, source_target_pairs={{0,4},{2,6},{4,0},{6,2},{8,12},{10,14},{12,8},{14,10},{16,20},{18,... | collective-permute-start | bytes 786440 | tf_op jit(solution)/shard_map/ppermute | solution.py:66
  32.5 1.9 %collective-permute-done.11.refs_0_ = bf16[64,2176]{1,0:T(8,128)(2,1)S(1)} collective-permute-done((bf16[64,2176]{1,0:T(8,128)(2,1)S(1)}, bf16[64,2176]{1,0:T(8,128)(2,1)S(1)}, u32[]{:S(2)}, u32[]{:S(2)}) %collective-permute-start.11) | collective-permute-done | bytes 278560 | tf_op jit(solution)/shard_map/ppermute | solution.py:71
  34.4 5.2 %collective-permute-done.12.refs_1_ = bf16[64,2176]{1,0:T(8,128)(2,1)S(1)} collective-permute-done((bf16[64,2176]{1,0:T(8,128)(2,1)S(1)}, bf16[64,2176]{1,0:T(8,128)(2,1)S(1)}, u32[]{:S(2)}, u32[]{:S(2)}) %collective-permute-start.12) | collective-permute-done | bytes 278560 | tf_op jit(solution)/shard_map/ppermute | solution.py:71
  39.7 0.6 collective-permute-start.16
  40.3 0.5 collective-permute-start.15
  40.9 0.5 collective-permute-start.4
  41.5 1.7 %collective-permute-done.4.lines_c.refs_5_ = bf16[1,64,2176]{2,1,0:T(8,128)(2,1)S(1)} collective-permute-done((bf16[1,64,2176]{2,1,0:T(8,128)(2,1)S(1)}, bf16[1,64,2176]{2,1,0:T(8,128)(2,1)S(1)}, u32[]{:S(2)}, u32[]{:S(2)}) %collective-permute-start.4) | collective-permute-done | bytes 278560 | tf_op jit(solution)/shard_map/ppermute | solution.py:66
  43.3 1.1 route.2
  44.5 4.3 %hidden.3.grads._ = bf16[2,384,768]{2,1,0:T(8,128)(2,1)S(1)} custom-call(s32[4]{0:T(128)S(1)} %pad_add_fusion.place, bf16[64,2176]{1,0:T(8,128)(2,1)S(1)} %get-tuple-element.52.part.own.refs_0_, bf16[64,2176]{1,0:T(8,128)(2,1)S(1)} %collective-permute-done.__.own_c.refs_1_, bf16[64,2048]{1,0:T(8,128)(2,1)S(1)} %get-tuple-element.53.far.refs_2_, ...), custom_call_target="tpu_custom_call" | custom-call | tf_op jit(solution)/shard_map/hidden/pallas_call | solution.py:76
  48.8 2.2 %sums.5 = (bf16[4,128,1024]{2,1,0:T(8,128)(2,1)S(1)}, bf16[4,128,1024]{2,1,0:T(8,128)(2,1)S(1)}) custom-call(bf16[2,384,768]{2,1,0:T(8,128)(2,1)S(1)} %hidden.3.grads._, bf16[2,384,2048]{2,1,0:T(8,128)(2,1)S(1)} %copy-done, bf16[2,384,2048]{2,1,0:T(8,128)(2,1)S(1)} %copy-done.1, bf16[4,256,192]{2,1,0:T(8,128)(2,1)S(1)} %get-tuple-element.63.pick_t, ...), custom_call_target="tpu_custom_call" | custom-call | tf_op jit(solution)/shard_map/sums/pallas_call | solution.py:76
  51.1 0.4 collective-permute-start.14
  51.5 2.2 %sums.6 = (bf16[4,128,1024]{2,1,0:T(8,128)(2,1)S(1)}, bf16[4,128,1024]{2,1,0:T(8,128)(2,1)S(1)}) custom-call(bf16[2,384,768]{2,1,0:T(8,128)(2,1)S(1)} %hidden.3.grads._, bf16[2,384,2048]{2,1,0:T(8,128)(2,1)S(1)} %copy-done, bf16[2,384,2048]{2,1,0:T(8,128)(2,1)S(1)} %copy-done.1, bf16[4,256,192]{2,1,0:T(8,128)(2,1)S(1)} %get-tuple-element.63.pick_t, ...), custom_call_target="tpu_custom_call" | custom-call | tf_op jit(solution)/shard_map/sums/pallas_call | solution.py:76
  53.8 0.2 collective-permute-start.23
  54.0 0.4 collective-permute-start.20
  54.5 1.6 %collective-permute-start.17 = (bf16[2,64,1024]{2,1,0:T(8,128)(2,1)S(1)}, bf16[2,64,1024]{2,1,0:T(8,128)(2,1)S(1)}, u32[]{:S(2)}, u32[]{:S(2)}) collective-permute-start(bf16[2,64,1024]{2,1,0:T(8,128)(2,1)S(1)} %get-tuple-element.67.refs_9_), channel_id=1, source_target_pairs={{0,1},{1,0},{2,3},{3,2},{4,5},{5,4},{6,7},{7,6},{8,9},{9,8},{10,11... | collective-permute-start | bytes 786440 | tf_op jit(solution)/shard_map/ppermute | solution.py:66
  56.1 2.0 %collective-permute-done.21.over_c.refs_1_ = bf16[2,64,2176]{2,1,0:T(8,128)(2,1)S(1)} collective-permute-done((bf16[2,64,2176]{2,1,0:T(8,128)(2,1)S(1)}, bf16[2,64,2176]{2,1,0:T(8,128)(2,1)S(1)}, u32[]{:S(2)}, u32[]{:S(2)}) %collective-permute-start.21) | collective-permute-done | bytes 557088 | tf_op jit(solution)/shard_map/ppermute | solution.py:66
  58.1 1.5 %collective-permute-start.18 = (bf16[2,64,1024]{2,1,0:T(8,128)(2,1)S(1)}, bf16[2,64,1024]{2,1,0:T(8,128)(2,1)S(1)}, u32[]{:S(2)}, u32[]{:S(2)}) collective-permute-start(bf16[2,64,1024]{2,1,0:T(8,128)(2,1)S(1)} %get-tuple-element.68), channel_id=1, source_target_pairs={{0,4},{2,6},{4,0},{6,2},{8,12},{10,14},{12,8},{14,10},{16,20},{18,... | collective-permute-start | bytes 786440 | tf_op jit(solution)/shard_map/ppermute | solution.py:66
  59.6 1.1 route.3
  60.7 2.9 %hidden.4.grads._ = bf16[2,192,768]{2,1,0:T(8,128)(2,1)S(1)} custom-call(s32[4]{0:T(128)S(1)} %pad_add_fusion.place, bf16[2,64,2176]{2,1,0:T(8,128)(2,1)S(1)} %bitcast.13, bf16[2,64,2176]{2,1,0:T(8,128)(2,1)S(1)} %collective-permute-done.19.lines_c.refs_1_, bf16[2,64,2176]{2,1,0:T(8,128)(2,1)S(1)} %collective-permute-done.16.side.refs_2_, ...), custom_call_target="tpu_custom_call" | custom-call | tf_op jit(solution)/shard_map/hidden/pallas_call | solution.py:76
  63.6 3.0 %sums.7 = (bf16[2,128,2048]{2,1,0:T(8,128)(2,1)S(1)}, bf16[2,128,2048]{2,1,0:T(8,128)(2,1)S(1)}) custom-call(bf16[2,192,768]{2,1,0:T(8,128)(2,1)S(1)} %hidden.4.grads._, bf16[2,384,2048]{2,1,0:T(8,128)(2,1)S(1)} %copy-done, bf16[2,384,2048]{2,1,0:T(8,128)(2,1)S(1)} %copy-done.1, bf16[4,256,192]{2,1,0:T(8,128)(2,1)S(1)} %get-tuple-element.71.pick_t, ...), custom_call_target="tpu_custom_call" | custom-call | tf_op jit(solution)/shard_map/sums/pallas_call | solution.py:76
  66.9 1.6 %collective-permute-start.22 = (bf16[4,64,1024]{2,1,0:T(8,128)(2,1)S(1)}, bf16[4,64,1024]{2,1,0:T(8,128)(2,1)S(1)}, u32[]{:S(2)}, u32[]{:S(2)}) collective-permute-start(bf16[4,64,1024]{2,1,0:T(8,128)(2,1)S(1)} %get-tuple-element.74._), channel_id=1, source_target_pairs={{0,1},{1,0},{2,3},{3,2},{4,5},{5,4},{6,7},{7,6},{8,9},{9,8},{10,11... | collective-permute-start | bytes 1572872 | tf_op jit(solution)/shard_map/ppermute | solution.py:66
  68.4 0.2 first_right.1
  68.6 1.4 %collective-permute-start.24 = (bf16[2,128,1024]{2,1,0:T(8,128)(2,1)S(1)}, bf16[2,128,1024]{2,1,0:T(8,128)(2,1)S(1)}, u32[]{:S(2)}, u32[]{:S(2)}) collective-permute-start(bf16[2,128,1024]{2,1,0:T(8,128)(2,1)S(1)} %get-tuple-element.77._.refs_9_), channel_id=1, source_target_pairs={{0,4},{2,6},{4,0},{6,2},{8,12},{10,14},{12,8},{14,10},{16,20},{18,... | collective-permute-start | bytes 1572872 | tf_op jit(solution)/shard_map/ppermute | solution.py:66
  70.0 2.9 %hidden.5.grads._ = bf16[2,192,768]{2,1,0:T(8,128)(2,1)S(1)} custom-call(s32[4]{0:T(128)S(1)} %pad_add_fusion.place, bf16[2,64,2176]{2,1,0:T(8,128)(2,1)S(1)} %collective-permute-done.15.over.refs_0_, bf16[2,64,2176]{2,1,0:T(8,128)(2,1)S(1)} %collective-permute-done.21.over_c.refs_1_, bf16[2,64,2048]{2,1,0:T(8,128)(2,1)S(1)} %join.3._.refs_2_, ...), custom_call_target="tpu_custom_call" | custom-call | tf_op jit(solution)/shard_map/hidden/pallas_call | solution.py:76
  72.9 1.5 %sums.8 = (bf16[2,128,1024]{2,1,0:T(8,128)(2,1)S(1)}, bf16[2,128,1024]{2,1,0:T(8,128)(2,1)S(1)}) custom-call(bf16[2,192,768]{2,1,0:T(8,128)(2,1)S(1)} %hidden.5.grads._, bf16[2,384,2048]{2,1,0:T(8,128)(2,1)S(1)} %copy-done, bf16[2,384,2048]{2,1,0:T(8,128)(2,1)S(1)} %copy-done.1, bf16[4,256,192]{2,1,0:T(8,128)(2,1)S(1)} %get-tuple-element.71.pick_t, ...), custom_call_target="tpu_custom_call" | custom-call | tf_op jit(solution)/shard_map/sums/pallas_call | solution.py:76
  74.3 1.5 %sums.9 = (bf16[2,128,1024]{2,1,0:T(8,128)(2,1)S(1)}, bf16[2,128,1024]{2,1,0:T(8,128)(2,1)S(1)}) custom-call(bf16[2,192,768]{2,1,0:T(8,128)(2,1)S(1)} %hidden.5.grads._, bf16[2,384,2048]{2,1,0:T(8,128)(2,1)S(1)} %copy-done, bf16[2,384,2048]{2,1,0:T(8,128)(2,1)S(1)} %copy-done.1, bf16[4,256,192]{2,1,0:T(8,128)(2,1)S(1)} %get-tuple-element.71.pick_t, ...), custom_call_target="tpu_custom_call" | custom-call | tf_op jit(solution)/shard_map/sums/pallas_call | solution.py:76
  75.8 0.6 collective-permute-start.31
  76.5 4.8 %collective-permute-done.22.came_l = bf16[4,64,1024]{2,1,0:T(8,128)(2,1)S(1)} collective-permute-done((bf16[4,64,1024]{2,1,0:T(8,128)(2,1)S(1)}, bf16[4,64,1024]{2,1,0:T(8,128)(2,1)S(1)}, u32[]{:S(2)}, u32[]{:S(2)}) %collective-permute-start.22) | collective-permute-done | bytes 524320 | tf_op jit(solution)/shard_map/ppermute | solution.py:66
  81.2 1.4 %collective-permute-done.24.came_r = bf16[2,128,1024]{2,1,0:T(8,128)(2,1)S(1)} collective-permute-done((bf16[2,128,1024]{2,1,0:T(8,128)(2,1)S(1)}, bf16[2,128,1024]{2,1,0:T(8,128)(2,1)S(1)}, u32[]{:S(2)}, u32[]{:S(2)}) %collective-permute-start.24) | collective-permute-done | bytes 524320 | tf_op jit(solution)/shard_map/ppermute | solution.py:66
  82.8 1.4 %collective-permute-start.25 = (bf16[2,64,1024]{2,1,0:T(8,128)(2,1)S(1)}, bf16[2,64,1024]{2,1,0:T(8,128)(2,1)S(1)}, u32[]{:S(2)}, u32[]{:S(2)}) collective-permute-start(bf16[2,64,1024]{2,1,0:T(8,128)(2,1)S(1)} %get-tuple-element.79._), channel_id=1, source_target_pairs={{0,4},{2,6},{4,0},{6,2},{8,12},{10,14},{12,8},{14,10},{16,20},{18,... | collective-permute-start | bytes 786440 | tf_op jit(solution)/shard_map/ppermute | solution.py:66
  84.2 0.5 collective-permute-start.26
  84.9 0.7 collective-permute-start.33
  85.7 1.6 %collective-permute-start.32 = (bf16[4,64,1024]{2,1,0:T(8,128)(2,1)S(1)}, bf16[4,64,1024]{2,1,0:T(8,128)(2,1)S(1)}, u32[]{:S(2)}, u32[]{:S(2)}) collective-permute-start(bf16[4,64,1024]{2,1,0:T(8,128)(2,1)S(1)} %get-tuple-element.91), channel_id=1, source_target_pairs={{0,1},{1,0},{2,3},{3,2},{4,5},{5,4},{6,7},{7,6},{8,9},{9,8},{10,11... | collective-permute-start | bytes 1572872 | tf_op jit(solution)/shard_map/ppermute | solution.py:66
  87.3 4.8 %collective-permute-done.25.came_l = bf16[2,64,1024]{2,1,0:T(8,128)(2,1)S(1)} collective-permute-done((bf16[2,64,1024]{2,1,0:T(8,128)(2,1)S(1)}, bf16[2,64,1024]{2,1,0:T(8,128)(2,1)S(1)}, u32[]{:S(2)}, u32[]{:S(2)}) %collective-permute-start.25) | collective-permute-done | bytes 262176 | tf_op jit(solution)/shard_map/ppermute | solution.py:66
  92.1 1.4 %collective-permute-done.26.came_r = bf16[2,64,1024]{2,1,0:T(8,128)(2,1)S(1)} collective-permute-done((bf16[2,64,1024]{2,1,0:T(8,128)(2,1)S(1)}, bf16[2,64,1024]{2,1,0:T(8,128)(2,1)S(1)}, u32[]{:S(2)}, u32[]{:S(2)}) %collective-permute-start.26) | collective-permute-done | bytes 262176 | tf_op jit(solution)/shard_map/ppermute | solution.py:66
  93.6 0.2 collective-permute-start.27
  93.7 9.0 %collective-permute-done.32.came_l = bf16[4,64,1024]{2,1,0:T(8,128)(2,1)S(1)} collective-permute-done((bf16[4,64,1024]{2,1,0:T(8,128)(2,1)S(1)}, bf16[4,64,1024]{2,1,0:T(8,128)(2,1)S(1)}, u32[]{:S(2)}, u32[]{:S(2)}) %collective-permute-start.32) | collective-permute-done | bytes 524320 | tf_op jit(solution)/shard_map/ppermute | solution.py:66
  102.8 0.2 second_sum.3
  102.9 0.7 collective-permute-start.34
  103.6 0.5 collective-permute-start.35
  104.2 0.4 collective-permute-done.27._.refs_1_
  104.6 4.8 %collective-permute-done.34.came_l = bf16[2,64,1024]{2,1,0:T(8,128)(2,1)S(1)} collective-permute-done((bf16[2,64,1024]{2,1,0:T(8,128)(2,1)S(1)}, bf16[2,64,1024]{2,1,0:T(8,128)(2,1)S(1)}, u32[]{:S(2)}, u32[]{:S(2)}) %collective-permute-start.34) | collective-permute-done | bytes 262176 | tf_op jit(solution)/shard_map/ppermute | solution.py:66
  109.4 0.7 collective-permute-done.35.came_r
  110.1 1.8 %collective-permute-start.36 = (bf16[64,2048]{1,0:T(8,128)(2,1)S(1)}, bf16[64,2048]{1,0:T(8,128)(2,1)S(1)}, u32[]{:S(2)}, u32[]{:S(2)}) collective-permute-start(bf16[64,2048]{1,0:T(8,128)(2,1)S(1)} %get-tuple-element.97), channel_id=1, source_target_pairs={{0,8},{2,10},{4,12},{6,14},{8,16},{10,18},{12,20},{14,22},{16,24},... | collective-permute-start | bytes 786440 | tf_op jit(solution)/shard_map/ppermute | solution.py:71
  112.0 2.0 %collective-permute-start.37 = (bf16[64,2048]{1,0:T(8,128)(2,1)S(1)}, bf16[64,2048]{1,0:T(8,128)(2,1)S(1)}, u32[]{:S(2)}, u32[]{:S(2)}) collective-permute-start(bf16[64,2048]{1,0:T(8,128)(2,1)S(1)} %get-tuple-element.98), channel_id=1, source_target_pairs={{0,24},{2,26},{4,28},{6,30},{8,0},{10,2},{12,4},{14,6},{16,8},{18,... | collective-permute-start | bytes 786440 | tf_op jit(solution)/shard_map/ppermute | solution.py:71
  114.0 6.2 %collective-permute-done.36.refs_2_ = bf16[64,2048]{1,0:T(8,128)(2,1)S(1)} collective-permute-done((bf16[64,2048]{1,0:T(8,128)(2,1)S(1)}, bf16[64,2048]{1,0:T(8,128)(2,1)S(1)}, u32[]{:S(2)}, u32[]{:S(2)}) %collective-permute-start.36) | collective-permute-done | bytes 262176 | tf_op jit(solution)/shard_map/ppermute | solution.py:71
  120.3 2.3 %collective-permute-done.37.refs_3_ = bf16[64,2048]{1,0:T(8,128)(2,1)S(1)} collective-permute-done((bf16[64,2048]{1,0:T(8,128)(2,1)S(1)}, bf16[64,2048]{1,0:T(8,128)(2,1)S(1)}, u32[]{:S(2)}, u32[]{:S(2)}) %collective-permute-start.37) | collective-permute-done | bytes 262176 | tf_op jit(solution)/shard_map/ppermute | solution.py:71
  122.6 0.9 last_sum.1
  (57 shorter events, 1.8 us)
Async XLA Ops:
  0.0 27.3 %copy-start.3 = (bf16[2,384,768]{2,1,0:T(8,128)(2,1)S(1)}, bf16[2,384,768]{2,1,0:T(8,128)(2,1)}, u32[]{:S(2)}) copy-start(bf16[2,384,768]{2,1,0:T(8,128)(2,1)} %gate.1) | copy-start | bytes 3538948
  0.1 1.1 copy-start.5
  1.2 0.7 copy-start.6
  1.9 0.7 copy-start.7
  3.2 7.2 %collective-permute-start = (bf16[64,2176]{1,0:T(8,128)(2,1)S(1)}, bf16[64,2176]{1,0:T(8,128)(2,1)S(1)}, u32[]{:S(2)}, u32[]{:S(2)}) collective-permute-start(bf16[64,2176]{1,0:T(8,128)(2,1)S(1)} %get-tuple-element.52.part.own.refs_0_), channel_id=1, source_target_pairs={{0,2},{2,0},{4,6},{6,4},{8,10},{10,8},{12,14},{14,12},{16,18},{18,... | collective-permute-start | bytes 835592 | tf_op jit(solution)/shard_map/ppermute | solution.py:66
  3.7 16.9 %collective-permute-start.2 = (bf16[64,2176]{1,0:T(8,128)(2,1)S(1)}, bf16[64,2176]{1,0:T(8,128)(2,1)S(1)}, u32[]{:S(2)}, u32[]{:S(2)}) collective-permute-start(bf16[64,2176]{1,0:T(8,128)(2,1)S(1)} %get-tuple-element.52.part.own.refs_0_), channel_id=1, source_target_pairs={{0,16},{2,18},{4,20},{6,22},{8,24},{10,26},{12,28},{14,30},{16,0},... | collective-permute-start | bytes 835592 | tf_op jit(solution)/shard_map/ppermute | solution.py:71
  7.4 13.2 %collective-permute-start.3 = (bf16[64,2176]{1,0:T(8,128)(2,1)S(1)}, bf16[64,2176]{1,0:T(8,128)(2,1)S(1)}, u32[]{:S(2)}, u32[]{:S(2)}) collective-permute-start(bf16[64,2176]{1,0:T(8,128)(2,1)S(1)} %get-tuple-element.52.part.own.refs_0_), channel_id=1, source_target_pairs={{0,4},{2,6},{4,0},{6,2},{8,12},{10,14},{12,8},{14,10},{16,20},{18,... | collective-permute-start | bytes 835592 | tf_op jit(solution)/shard_map/ppermute | solution.py:66
  8.9 1.5 %collective-permute-start.1 = (bf16[64,2048]{1,0:T(8,128)(2,1)S(1)}, bf16[64,2048]{1,0:T(8,128)(2,1)S(1)}, u32[]{:S(2)}, u32[]{:S(2)}) collective-permute-start(bf16[64,2048]{1,0:T(8,128)(2,1)S(1)} %get-tuple-element.53.far.refs_2_), channel_id=1, source_target_pairs={{0,2},{2,0},{4,6},{6,4},{8,10},{10,8},{12,14},{14,12},{16,18},{18,... | collective-permute-start | bytes 786440 | tf_op jit(solution)/shard_map/ppermute | solution.py:66
  20.6 8.6 %collective-permute-start.5 = (bf16[1,64,2176]{2,1,0:T(8,128)(2,1)S(1)}, bf16[1,64,2176]{2,1,0:T(8,128)(2,1)S(1)}, u32[]{:S(2)}, u32[]{:S(2)}) collective-permute-start(bf16[1,64,2176]{2,1,0:T(8,128)(2,1)S(1)} %get-tuple-element.54.refs_0_.lines.refs_4_), channel_id=1, source_target_pairs={{0,1},{1,0},{2,3},{3,2},{4,5},{5,4},{6,7},{7,6},{8,9},{9,8},{10,11... | collective-permute-start | bytes 835592 | tf_op jit(solution)/shard_map/ppermute | solution.py:66
  22.3 7.9 %collective-permute-start.7 = (bf16[1,64,2176]{2,1,0:T(8,128)(2,1)S(1)}, bf16[1,64,2176]{2,1,0:T(8,128)(2,1)S(1)}, u32[]{:S(2)}, u32[]{:S(2)}) collective-permute-start(bf16[1,64,2176]{2,1,0:T(8,128)(2,1)S(1)} %get-tuple-element.54.refs_0_.lines.refs_4_), channel_id=1, source_target_pairs={{0,4},{2,6},{4,0},{6,2},{8,12},{10,14},{12,8},{14,10},{16,20},{18,... | collective-permute-start | bytes 835592 | tf_op jit(solution)/shard_map/ppermute | solution.py:66
  23.8 10.6 %collective-permute-start.11 = (bf16[64,2176]{1,0:T(8,128)(2,1)S(1)}, bf16[64,2176]{1,0:T(8,128)(2,1)S(1)}, u32[]{:S(2)}, u32[]{:S(2)}) collective-permute-start(bf16[64,2176]{1,0:T(8,128)(2,1)S(1)} %get-tuple-element.58), channel_id=1, source_target_pairs={{0,24},{2,26},{4,28},{6,30},{8,0},{10,2},{12,4},{14,6},{16,8},{18,... | collective-permute-start | bytes 835592 | tf_op jit(solution)/shard_map/ppermute | solution.py:71
  27.3 12.3 %collective-permute-start.12 = (bf16[64,2176]{1,0:T(8,128)(2,1)S(1)}, bf16[64,2176]{1,0:T(8,128)(2,1)S(1)}, u32[]{:S(2)}, u32[]{:S(2)}) collective-permute-start(bf16[64,2176]{1,0:T(8,128)(2,1)S(1)} %get-tuple-element.58), channel_id=1, source_target_pairs={{0,8},{2,10},{4,12},{6,14},{8,16},{10,18},{12,20},{14,22},{16,24},... | collective-permute-start | bytes 835592 | tf_op jit(solution)/shard_map/ppermute | solution.py:71
  27.3 1.3 %copy-start.4 = (bf16[2,384,768]{2,1,0:T(8,128)(2,1)S(1)}, bf16[2,384,768]{2,1,0:T(8,128)(2,1)}, u32[]{:S(2)}) copy-start(bf16[2,384,768]{2,1,0:T(8,128)(2,1)} %up.1) | copy-start | bytes 3538948
  30.3 9.3 %collective-permute-start.8 = (bf16[2,64,2176]{2,1,0:T(8,128)(2,1)S(1)}, bf16[2,64,2176]{2,1,0:T(8,128)(2,1)S(1)}, u32[]{:S(2)}, u32[]{:S(2)}) collective-permute-start(bf16[2,64,2176]{2,1,0:T(8,128)(2,1)S(1)} %get-tuple-element.55.over.refs_8_), channel_id=1, source_target_pairs={{0,2},{2,0},{4,6},{6,4},{8,10},{10,8},{12,14},{14,12},{16,18},{18,... | collective-permute-start | bytes 1671176 | tf_op jit(solution)/shard_map/ppermute | solution.py:66
  30.4 10.4 %collective-permute-start.9 = (bf16[2,64,1024]{2,1,0:T(8,128)(2,1)S(1)}, bf16[2,64,1024]{2,1,0:T(8,128)(2,1)S(1)}, u32[]{:S(2)}, u32[]{:S(2)}) collective-permute-start(bf16[2,64,1024]{2,1,0:T(8,128)(2,1)S(1)} %get-tuple-element.56), channel_id=1, source_target_pairs={{0,1},{1,0},{2,3},{3,2},{4,5},{5,4},{6,7},{7,6},{8,9},{9,8},{10,11... | collective-permute-start | bytes 786440 | tf_op jit(solution)/shard_map/ppermute | solution.py:66
  31.1 9.7 %collective-permute-start.10 = (bf16[2,64,1024]{2,1,0:T(8,128)(2,1)S(1)}, bf16[2,64,1024]{2,1,0:T(8,128)(2,1)S(1)}, u32[]{:S(2)}, u32[]{:S(2)}) collective-permute-start(bf16[2,64,1024]{2,1,0:T(8,128)(2,1)S(1)} %get-tuple-element.57), channel_id=1, source_target_pairs={{0,4},{2,6},{4,0},{6,2},{8,12},{10,14},{12,8},{14,10},{16,20},{18,... | collective-permute-start | bytes 786440 | tf_op jit(solution)/shard_map/ppermute | solution.py:66
  39.7 14.3 %collective-permute-start.16 = (bf16[2,64,2176]{2,1,0:T(8,128)(2,1)S(1)}, bf16[2,64,2176]{2,1,0:T(8,128)(2,1)S(1)}, u32[]{:S(2)}, u32[]{:S(2)}) collective-permute-start(bf16[2,64,2176]{2,1,0:T(8,128)(2,1)S(1)} %bitcast.7), channel_id=1, source_target_pairs={{0,1},{1,0},{2,3},{3,2},{4,5},{5,4},{6,7},{7,6},{8,9},{9,8},{10,11... | collective-permute-start | bytes 1671176 | tf_op jit(solution)/shard_map/ppermute | solution.py:66
  40.3 14.1 %collective-permute-start.15 = (bf16[2,64,2176]{2,1,0:T(8,128)(2,1)S(1)}, bf16[2,64,2176]{2,1,0:T(8,128)(2,1)S(1)}, u32[]{:S(2)}, u32[]{:S(2)}) collective-permute-start(bf16[2,64,2176]{2,1,0:T(8,128)(2,1)S(1)} %bitcast.8), channel_id=1, source_target_pairs={{0,4},{2,6},{4,0},{6,2},{8,12},{10,14},{12,8},{14,10},{16,20},{18,... | collective-permute-start | bytes 1671176 | tf_op jit(solution)/shard_map/ppermute | solution.py:66
  40.8 3.7 %copy-start.2 = (bf16[2,384,2048]{2,1,0:T(8,128)(2,1)S(1)}, bf16[2,384,2048]{2,1,0:T(8,128)(2,1)}, u32[]{:S(2)}) copy-start(bf16[2,384,2048]{2,1,0:T(8,128)(2,1)} %refs_6_.3) | copy-start | bytes 9437188
  40.8 3.6 %collective-permute-start.13 = (bf16[2,64,2048]{2,1,0:T(8,128)(2,1)S(1)}, bf16[2,64,2048]{2,1,0:T(8,128)(2,1)S(1)}, u32[]{:S(2)}, u32[]{:S(2)}) collective-permute-start(bf16[2,64,2048]{2,1,0:T(8,128)(2,1)S(1)} %join.2.refs_10_), channel_id=1, source_target_pairs={{0,2},{2,0},{4,6},{6,4},{8,10},{10,8},{12,14},{14,12},{16,18},{18,... | collective-permute-start | bytes 1572872 | tf_op jit(solution)/shard_map/ppermute | solution.py:66
  40.9 2.3 %collective-permute-start.4 = (bf16[1,64,2176]{2,1,0:T(8,128)(2,1)S(1)}, bf16[1,64,2176]{2,1,0:T(8,128)(2,1)S(1)}, u32[]{:S(2)}, u32[]{:S(2)}) collective-permute-start(bf16[1,64,2176]{2,1,0:T(8,128)(2,1)S(1)} %get-tuple-element.54.refs_0_.lines.refs_4_), channel_id=1, source_target_pairs={{0,2},{2,0},{4,6},{6,4},{8,10},{10,8},{12,14},{14,12},{16,18},{18,... | collective-permute-start | bytes 835592 | tf_op jit(solution)/shard_map/ppermute | solution.py:66
  41.4 3.1 %collective-permute-start.6 = (bf16[1,64,2176]{2,1,0:T(8,128)(2,1)S(1)}, bf16[1,64,2176]{2,1,0:T(8,128)(2,1)S(1)}, u32[]{:S(2)}, u32[]{:S(2)}) collective-permute-start(bf16[1,64,2176]{2,1,0:T(8,128)(2,1)S(1)} %collective-permute-done.5.side.refs_6_), channel_id=1, source_target_pairs={{0,2},{2,0},{4,6},{6,4},{8,10},{10,8},{12,14},{14,12},{16,18},{18,... | collective-permute-start | bytes 835592 | tf_op jit(solution)/shard_map/ppermute | solution.py:66
  43.2 11.3 %collective-permute-start.19 = (bf16[2,64,2176]{2,1,0:T(8,128)(2,1)S(1)}, bf16[2,64,2176]{2,1,0:T(8,128)(2,1)S(1)}, u32[]{:S(2)}, u32[]{:S(2)}) collective-permute-start(bf16[2,64,2176]{2,1,0:T(8,128)(2,1)S(1)} %bitcast.10), channel_id=1, source_target_pairs={{0,2},{2,0},{4,6},{6,4},{8,10},{10,8},{12,14},{14,12},{16,18},{18,... | collective-permute-start | bytes 1671176 | tf_op jit(solution)/shard_map/ppermute | solution.py:66
  44.5 4.3 %copy-start = (bf16[2,384,2048]{2,1,0:T(8,128)(2,1)S(1)}, bf16[2,384,2048]{2,1,0:T(8,128)(2,1)}, u32[]{:S(2)}) copy-start(bf16[2,384,2048]{2,1,0:T(8,128)(2,1)} %w_gate.9) | copy-start | bytes 9437188
  44.5 4.3 %copy-start.1 = (bf16[2,384,2048]{2,1,0:T(8,128)(2,1)S(1)}, bf16[2,384,2048]{2,1,0:T(8,128)(2,1)}, u32[]{:S(2)}) copy-start(bf16[2,384,2048]{2,1,0:T(8,128)(2,1)} %w_up.9) | copy-start | bytes 9437188
  51.1 15.6 %collective-permute-start.14 = (bf16[4,128,1024]{2,1,0:T(8,128)(2,1)S(1)}, bf16[4,128,1024]{2,1,0:T(8,128)(2,1)S(1)}, u32[]{:S(2)}, u32[]{:S(2)}) collective-permute-start(bf16[4,128,1024]{2,1,0:T(8,128)(2,1)S(1)} %get-tuple-element.65._), channel_id=1, source_target_pairs={{0,2},{2,0},{4,6},{6,4},{8,10},{10,8},{12,14},{14,12},{16,18},{18,... | collective-permute-start | bytes 3145736 | tf_op jit(solution)/shard_map/ppermute | solution.py:66
  53.8 14.6 %collective-permute-start.23 = (bf16[4,128,1024]{2,1,0:T(8,128)(2,1)S(1)}, bf16[4,128,1024]{2,1,0:T(8,128)(2,1)S(1)}, u32[]{:S(2)}, u32[]{:S(2)}) collective-permute-start(bf16[4,128,1024]{2,1,0:T(8,128)(2,1)S(1)} %get-tuple-element.66._), channel_id=1, source_target_pairs={{0,2},{2,0},{4,6},{6,4},{8,10},{10,8},{12,14},{14,12},{16,18},{18,... | collective-permute-start | bytes 3145736 | tf_op jit(solution)/shard_map/ppermute | solution.py:66
  54.0 6.8 %collective-permute-start.20 = (bf16[2,64,2176]{2,1,0:T(8,128)(2,1)S(1)}, bf16[2,64,2176]{2,1,0:T(8,128)(2,1)S(1)}, u32[]{:S(2)}, u32[]{:S(2)}) collective-permute-start(bf16[2,64,2176]{2,1,0:T(8,128)(2,1)S(1)} %collective-permute-done.16.side.refs_2_), channel_id=1, source_target_pairs={{0,2},{2,0},{4,6},{6,4},{8,10},{10,8},{12,14},{14,12},{16,18},{18,... | collective-permute-start | bytes 1671176 | tf_op jit(solution)/shard_map/ppermute | solution.py:66
  54.4 3.7 %collective-permute-start.21 = (bf16[2,64,2176]{2,1,0:T(8,128)(2,1)S(1)}, bf16[2,64,2176]{2,1,0:T(8,128)(2,1)S(1)}, u32[]{:S(2)}, u32[]{:S(2)}) collective-permute-start(bf16[2,64,2176]{2,1,0:T(8,128)(2,1)S(1)} %collective-permute-done.15.over.refs_0_), channel_id=1, source_target_pairs={{0,2},{2,0},{4,6},{6,4},{8,10},{10,8},{12,14},{14,12},{16,18},{18,... | collective-permute-start | bytes 1671176 | tf_op jit(solution)/shard_map/ppermute | solution.py:66
  54.5 12.0 %collective-permute-start.17 = (bf16[2,64,1024]{2,1,0:T(8,128)(2,1)S(1)}, bf16[2,64,1024]{2,1,0:T(8,128)(2,1)S(1)}, u32[]{:S(2)}, u32[]{:S(2)}) collective-permute-start(bf16[2,64,1024]{2,1,0:T(8,128)(2,1)S(1)} %get-tuple-element.67.refs_9_), channel_id=1, source_target_pairs={{0,1},{1,0},{2,3},{3,2},{4,5},{5,4},{6,7},{7,6},{8,9},{9,8},{10,11... | collective-permute-start | bytes 786440 | tf_op jit(solution)/shard_map/ppermute | solution.py:66
  58.1 8.5 %collective-permute-start.18 = (bf16[2,64,1024]{2,1,0:T(8,128)(2,1)S(1)}, bf16[2,64,1024]{2,1,0:T(8,128)(2,1)S(1)}, u32[]{:S(2)}, u32[]{:S(2)}) collective-permute-start(bf16[2,64,1024]{2,1,0:T(8,128)(2,1)S(1)} %get-tuple-element.68), channel_id=1, source_target_pairs={{0,4},{2,6},{4,0},{6,2},{8,12},{10,14},{12,8},{14,10},{16,20},{18,... | collective-permute-start | bytes 786440 | tf_op jit(solution)/shard_map/ppermute | solution.py:66
  66.7 3.3 %collective-permute-start.29 = (bf16[2,64,2048]{2,1,0:T(8,128)(2,1)S(1)}, bf16[2,64,2048]{2,1,0:T(8,128)(2,1)S(1)}, u32[]{:S(2)}, u32[]{:S(2)}) collective-permute-start(bf16[2,64,2048]{2,1,0:T(8,128)(2,1)S(1)} %join.3._.refs_2_), channel_id=1, source_target_pairs={{0,2},{2,0},{4,6},{6,4},{8,10},{10,8},{12,14},{14,12},{16,18},{18,... | collective-permute-start | bytes 1572872 | tf_op jit(solution)/shard_map/ppermute | solution.py:66
  66.9 14.4 %collective-permute-start.22 = (bf16[4,64,1024]{2,1,0:T(8,128)(2,1)S(1)}, bf16[4,64,1024]{2,1,0:T(8,128)(2,1)S(1)}, u32[]{:S(2)}, u32[]{:S(2)}) collective-permute-start(bf16[4,64,1024]{2,1,0:T(8,128)(2,1)S(1)} %get-tuple-element.74._), channel_id=1, source_target_pairs={{0,1},{1,0},{2,3},{3,2},{4,5},{5,4},{6,7},{7,6},{8,9},{9,8},{10,11... | collective-permute-start | bytes 1572872 | tf_op jit(solution)/shard_map/ppermute | solution.py:66
  68.6 14.1 %collective-permute-start.24 = (bf16[2,128,1024]{2,1,0:T(8,128)(2,1)S(1)}, bf16[2,128,1024]{2,1,0:T(8,128)(2,1)S(1)}, u32[]{:S(2)}, u32[]{:S(2)}) collective-permute-start(bf16[2,128,1024]{2,1,0:T(8,128)(2,1)S(1)} %get-tuple-element.77._.refs_9_), channel_id=1, source_target_pairs={{0,4},{2,6},{4,0},{6,2},{8,12},{10,14},{12,8},{14,10},{16,20},{18,... | collective-permute-start | bytes 1572872 | tf_op jit(solution)/shard_map/ppermute | solution.py:66
  70.0 14.7 %collective-permute-start.28 = (bf16[2,128,2048]{2,1,0:T(8,128)(2,1)S(1)}, bf16[2,128,2048]{2,1,0:T(8,128)(2,1)S(1)}, u32[]{:S(2)}, u32[]{:S(2)}) collective-permute-start(bf16[2,128,2048]{2,1,0:T(8,128)(2,1)S(1)} %get-tuple-element.72.refs_0_), channel_id=1, source_target_pairs={{0,2},{2,0},{4,6},{6,4},{8,10},{10,8},{12,14},{14,12},{16,18},{18,... | collective-permute-start | bytes 3145736 | tf_op jit(solution)/shard_map/ppermute | solution.py:66
  75.8 8.9 %collective-permute-start.31 = (bf16[2,128,1024]{2,1,0:T(8,128)(2,1)S(1)}, bf16[2,128,1024]{2,1,0:T(8,128)(2,1)S(1)}, u32[]{:S(2)}, u32[]{:S(2)}) collective-permute-start(bf16[2,128,1024]{2,1,0:T(8,128)(2,1)S(1)} %get-tuple-element.85._), channel_id=1, source_target_pairs={{0,2},{2,0},{4,6},{6,4},{8,10},{10,8},{12,14},{14,12},{16,18},{18,... | collective-permute-start | bytes 1572872 | tf_op jit(solution)/shard_map/ppermute | solution.py:66
  76.4 9.2 %collective-permute-start.30 = (bf16[2,128,1024]{2,1,0:T(8,128)(2,1)S(1)}, bf16[2,128,1024]{2,1,0:T(8,128)(2,1)S(1)}, u32[]{:S(2)}, u32[]{:S(2)}) collective-permute-start(bf16[2,128,1024]{2,1,0:T(8,128)(2,1)S(1)} %get-tuple-element.87), channel_id=1, source_target_pairs={{0,2},{2,0},{4,6},{6,4},{8,10},{10,8},{12,14},{14,12},{16,18},{18,... | collective-permute-start | bytes 1572872 | tf_op jit(solution)/shard_map/ppermute | solution.py:66
  82.8 9.3 %collective-permute-start.25 = (bf16[2,64,1024]{2,1,0:T(8,128)(2,1)S(1)}, bf16[2,64,1024]{2,1,0:T(8,128)(2,1)S(1)}, u32[]{:S(2)}, u32[]{:S(2)}) collective-permute-start(bf16[2,64,1024]{2,1,0:T(8,128)(2,1)S(1)} %get-tuple-element.79._), channel_id=1, source_target_pairs={{0,4},{2,6},{4,0},{6,2},{8,12},{10,14},{12,8},{14,10},{16,20},{18,... | collective-permute-start | bytes 786440 | tf_op jit(solution)/shard_map/ppermute | solution.py:66
  84.2 9.2 %collective-permute-start.26 = (bf16[2,64,1024]{2,1,0:T(8,128)(2,1)S(1)}, bf16[2,64,1024]{2,1,0:T(8,128)(2,1)S(1)}, u32[]{:S(2)}, u32[]{:S(2)}) collective-permute-start(bf16[2,64,1024]{2,1,0:T(8,128)(2,1)S(1)} %get-tuple-element.81), channel_id=1, source_target_pairs={{0,1},{1,0},{2,3},{3,2},{4,5},{5,4},{6,7},{7,6},{8,9},{9,8},{10,11... | collective-permute-start | bytes 786440 | tf_op jit(solution)/shard_map/ppermute | solution.py:66
  84.9 17.9 %collective-permute-start.33 = (bf16[2,128,1024]{2,1,0:T(8,128)(2,1)S(1)}, bf16[2,128,1024]{2,1,0:T(8,128)(2,1)S(1)}, u32[]{:S(2)}, u32[]{:S(2)}) collective-permute-start(bf16[2,128,1024]{2,1,0:T(8,128)(2,1)S(1)} %get-tuple-element.89._), channel_id=1, source_target_pairs={{0,4},{2,6},{4,0},{6,2},{8,12},{10,14},{12,8},{14,10},{16,20},{18,... | collective-permute-start | bytes 1572872 | tf_op jit(solution)/shard_map/ppermute | solution.py:66
  85.7 17.0 %collective-permute-start.32 = (bf16[4,64,1024]{2,1,0:T(8,128)(2,1)S(1)}, bf16[4,64,1024]{2,1,0:T(8,128)(2,1)S(1)}, u32[]{:S(2)}, u32[]{:S(2)}) collective-permute-start(bf16[4,64,1024]{2,1,0:T(8,128)(2,1)S(1)} %get-tuple-element.91), channel_id=1, source_target_pairs={{0,1},{1,0},{2,3},{3,2},{4,5},{5,4},{6,7},{7,6},{8,9},{9,8},{10,11... | collective-permute-start | bytes 1572872 | tf_op jit(solution)/shard_map/ppermute | solution.py:66
  93.6 11.0 %collective-permute-start.27 = (bf16[64,2048]{1,0:T(8,128)(2,1)S(1)}, bf16[64,2048]{1,0:T(8,128)(2,1)S(1)}, u32[]{:S(2)}, u32[]{:S(2)}) collective-permute-start(bf16[64,2048]{1,0:T(8,128)(2,1)S(1)} %get-tuple-element.83), channel_id=1, source_target_pairs={{0,16},{2,18},{4,20},{6,22},{8,24},{10,26},{12,28},{14,30},{16,0},... | collective-permute-start | bytes 786440 | tf_op jit(solution)/shard_map/ppermute | solution.py:71
  102.9 6.5 %collective-permute-start.34 = (bf16[2,64,1024]{2,1,0:T(8,128)(2,1)S(1)}, bf16[2,64,1024]{2,1,0:T(8,128)(2,1)S(1)}, u32[]{:S(2)}, u32[]{:S(2)}) collective-permute-start(bf16[2,64,1024]{2,1,0:T(8,128)(2,1)S(1)} %get-tuple-element.94), channel_id=1, source_target_pairs={{0,4},{2,6},{4,0},{6,2},{8,12},{10,14},{12,8},{14,10},{16,20},{18,... | collective-permute-start | bytes 786440 | tf_op jit(solution)/shard_map/ppermute | solution.py:66
  103.6 6.4 %collective-permute-start.35 = (bf16[2,64,1024]{2,1,0:T(8,128)(2,1)S(1)}, bf16[2,64,1024]{2,1,0:T(8,128)(2,1)S(1)}, u32[]{:S(2)}, u32[]{:S(2)}) collective-permute-start(bf16[2,64,1024]{2,1,0:T(8,128)(2,1)S(1)} %get-tuple-element.96), channel_id=1, source_target_pairs={{0,1},{1,0},{2,3},{3,2},{4,5},{5,4},{6,7},{7,6},{8,9},{9,8},{10,11... | collective-permute-start | bytes 786440 | tf_op jit(solution)/shard_map/ppermute | solution.py:66
  110.1 10.1 %collective-permute-start.36 = (bf16[64,2048]{1,0:T(8,128)(2,1)S(1)}, bf16[64,2048]{1,0:T(8,128)(2,1)S(1)}, u32[]{:S(2)}, u32[]{:S(2)}) collective-permute-start(bf16[64,2048]{1,0:T(8,128)(2,1)S(1)} %get-tuple-element.97), channel_id=1, source_target_pairs={{0,8},{2,10},{4,12},{6,14},{8,16},{10,18},{12,20},{14,22},{16,24},... | collective-permute-start | bytes 786440 | tf_op jit(solution)/shard_map/ppermute | solution.py:71
  112.0 10.6 %collective-permute-start.37 = (bf16[64,2048]{1,0:T(8,128)(2,1)S(1)}, bf16[64,2048]{1,0:T(8,128)(2,1)S(1)}, u32[]{:S(2)}, u32[]{:S(2)}) collective-permute-start(bf16[64,2048]{1,0:T(8,128)(2,1)S(1)} %get-tuple-element.98), channel_id=1, source_target_pairs={{0,24},{2,26},{4,28},{6,30},{8,0},{10,2},{12,4},{14,6},{16,8},{18,... | collective-permute-start | bytes 786440 | tf_op jit(solution)/shard_map/ppermute | solution.py:71

commit v11 on v10

--- a/solution.py
+++ b/solution.py
@@ -140,14 +140,17 @@
     )[0]
 
 
-def relay_kernel(came, part, _, __, ___, line, following):
+def relay_kernel(came, part, _, __, ___, line, tokens, table, following):
     line[0] = came[...]
+    tokens[0] = came[:, :tokens.shape[2]]
+    table[0] = came[:, tokens.shape[2]:]
     following[...] = part[...]
 
 
 def relay(came, part, *after):
-    return small(
-        relay_kernel, "relay", [(1,) + came.shape, part.shape], "vvooo", (came, part, *after)
+    piece, width = came.shape[0], came.shape[1] - 128
+    return small(
+        relay_kernel, "relay", [(1,) + came.shape, (1, piece, width), (1, piece, 128), part.shape], "vvooo", (came, part, *after)
     )
 
 
@@ -174,25 +177,27 @@
     )
 
 
-def corner_kernel(far, first, over, side, whole_over, left, right):
+def corner_kernel(far, first, over, table, side, whole_over, left, right):
     middle = left.shape[2]
     whole_over[0] = first[...]
-    whole_over[1:] = over[...]
+    whole_over[1:, :, :2 * middle] = over[...]
+    whole_over[1:, :, 2 * middle:] = table[...]
     left[0] = first[:, :middle]
     left[1:] = over[:, :, :middle]
     right[0] = far[:, middle:]
     right[1:] = side[:, :, middle:2 * middle]
 
 
-def own_corner(far, first, over, side):
-    count, piece, width = over.shape
+def own_corner(far, first, over, table, side):
+    count, piece, _ = over.shape
+    width = first.shape[1]
     middle = far.shape[1] // 2
     return small(
         corner_kernel,
         "own_corner",
         [(count + 1, piece, width)] + [(count + 1, piece, middle)] * 2,
-        "vvvv",
-        (far, first, over, side),
+        "vvvvv",
+        (far, first, over, table, side),
     )
 
 
@@ -453,25 +458,6 @@
     )
 
 
-def apart_right_kernel(keep_a, came_a, keep_b, came_b, _, send, kept):
-    middle = kept.shape[2]
-    kept[...] = keep_a[:, :, middle:] + came_a[:, :, middle:]
-    send[...] = keep_b[...] + came_b[...]
-
-
-def apart_left_kernel(keep_a, came_a, keep_b, came_b, _, send, kept):
-    _, piece, middle = kept.shape
-    for i in range(keep_a.shape[0]):
-        kept[2 * i] = keep_a[i, :piece, :middle] + came_a[i, :piece, :middle]
-        send[2 * i] = keep_a[i, piece:, :middle] + came_a[i, piece:, :middle]
-        kept[2 * i + 1] = keep_b[i, :piece] + came_b[i, :piece]
-        send[2 * i + 1] = keep_b[i, piece:] + came_b[i, piece:]
-
-
-def first_apart(kernel, dims, row_a, row_b, after):
-    return small(kernel, "first_apart", [dims] * 2, "vvvvo", (*row_a, *row_b, after))
-
-
 def first_right_kernel(keep, came, _, send, kept):
     for i in range(kept.shape[0]):
         kept[i] = keep[2 * i] + came[2 * i]
@@ -577,12 +563,13 @@
         return keep, swap(send, "expert", 2), send
 
     (_, near), (third, second) = CHUNKS
-    line, part = relay(along_line(part, -near), part, first, near_c, far_c)
-    side, over = swap(line, "tp", 1), swap(line, "expert", 2)
+    line, tokens, table, part = relay(along_line(part, -near), part, first, near_c, far_c)
+    side, over = swap(tokens, "tp", 1), swap(tokens, "expert", 2)
+    table = swap(table, "expert", 2)
     came = [along_line(part, -third), along_line(part, -second)]
     line_c = swap(line, "expert", 1)
     saved = turn(saved_gate, saved_up, line)
-    over, left, right = own_corner(far, first, over, side)
+    over, left, right = own_corner(far, first, over, table, side)
     left, right = swap(left, "tp", 1), swap(right, "expert", 2)
     moved = [line, line_c] + both_cores([side, over])
     line = stack(came, saved[0], work=68719476736)
@@ -598,18 +585,14 @@
     after = left
     left, right = swap(left, "tp", 1), swap(right, "expert", 2)
     moved = both_cores([line, side, over])
-    pick, pick_t, gate = routed(CHUNKS[1], moved)
-    grads = hidden(CHUNKS[1], (0,), lines, place, moved[:4], pick, gate, w_down, saved, after)
-    row_a, after = sums_by_token(0, 2 * middle, (0, 2), grads, pick_t, grads)
-    diag = join(left, right, after, work=0)
+    diag = join(left, right, after, work=8589934592)
     early_l = step_left(*early_l, diag)
     early_r = step_right(*early_r, early_l[-1])
-    diags = both_cores([diag])
-    grads = hidden(
-        CHUNKS[1], (1,), lines, place, moved[4:] + diags, pick, gate, w_down, saved, early_r[-1]
-    )
-    row_br, after = sums_by_token(middle, middle, (1, 3), grads, pick_t, grads)
-    row_bl, after = sums_by_token(0, middle, (1, 3), grads, pick_t, after)
+    moved += both_cores([diag])
+    pick, pick_t, gate = routed(CHUNKS[1], moved)
+    grads = hidden(CHUNKS[1], (0, 1), lines, place, moved, pick, gate, w_down, saved, early_r[-1])
+    late_l, after = sums_by_token(0, middle, (0, 1, 2, 3), grads, pick_t, grads)
+    late_r, _ = sums_by_token(middle, middle, (0, 1, 2, 3), grads, pick_t, after)
 
     def second_step(offsets, sums_of_two, after, came):
         send_l, left, send_r, right = second_sum(*sums_of_two, after)
@@ -618,11 +601,9 @@
         return rows[0], [row if r == 0 else along_line(row, r) for r, row in zip(offsets, rows)], send_l
 
     done, early, after = second_step(CHUNKS[0], early_l[:2] + early_r[:2], early_r[-1], None)
-    send, keep_r = first_apart(apart_right_kernel, (2, 2 * piece, middle), row_a, row_br, after)
-    came_r = swap(send, "expert", 2)
-    send, keep_l = first_apart(apart_left_kernel, (4, piece, middle), row_a, row_bl, send)
-    came_l = swap(send, "tp", 1)
-    _, late, _ = second_step(CHUNKS[1], (keep_l, came_l, keep_r, came_r), done, early[-1])
+    late_l = step_left(*late_l, after)
+    late_r = step_right(*late_r, late_l[-1])
+    _, late, _ = second_step(CHUNKS[1], late_l[:2] + late_r[:2], done, early[-1])
     terms = early + late
     return pl.pallas_call(
         last_kernel,

time: 124 us -> 120 us (0.968)
  Pallas kernels: 26.1 us -> 23 us
  waiting for transfers between devices: 59.2 us -> 56.8 us
  starting transfers between devices: 33.9 us -> 36.1 us
    ppermute x6, waiting for transfers between devices: 26.2 us -> 18.1 us  [along_line(): lax.ppermute(value, 'expert', [(i, (i + 4 * shift) % count) for i in rang...]
    ppermute x32, waiting for transfers between devices: 33 us -> 38.7 us  [swap(): return lax.ppermute(value, axis, [(i, i ^ step) for i in range(count)])]
    pallas_call x27 -> x25, Pallas kernels: 25.2 us -> 22.1 us  [small(): pl.pallas_call(kernel, out_shape=[out if hasattr(out, 'dtype') else jax.S...]
    ppermute x32, starting transfers between devices: 22.7 us -> 24.2 us  [swap(): return lax.ppermute(value, axis, [(i, i ^ step) for i in range(count)])]
  transfers between devices with their start and end apart: 38 -> 38, of which waited for: 17 -> 18; matrix products, arithmetic and copies ran while one was open for 0% -> 0% of each run, Pallas kernels for 20% -> 18%
where the time goes in v11:
time: 120 us
  waiting for transfers between devices  56.8 us (47%)
  starting transfers between devices  36.1 us (30%)
  Pallas kernels  23 us (19%)
  local copies, waits for them, and re-layouts  3.79 us (3%)
    ppermute x32, waiting for transfers between devices, swap(): return lax.ppermute(value, axis, [(i, i ^ step) for i in range(count)])  38.7 us
    ppermute x32, starting transfers between devices, swap(): return lax.ppermute(value, axis, [(i, i ^ step) for i in range(count)])  24.2 us
    pallas_call x25, Pallas kernels, small(): pl.pallas_call(kernel, out_shape=[out if hasattr(out, 'dtype') else jax.S...  22.1 us
    ppermute x6, waiting for transfers between devices, along_line(): lax.ppermute(value, 'expert', [(i, (i + 4 * shift) % count) for i in rang...  18.1 us
    ppermute x6, starting transfers between devices, along_line(): lax.ppermute(value, 'expert', [(i, (i + 4 * shift) % count) for i in rang...  11.8 us
    unnamed x16, local copies, waits for them, and re-layouts  3.79 us
  transfers between devices with their start and end apart: 38, of which 18 were waited for; matrix products, arithmetic and copies ran while one was open for 0% of the time, Pallas kernels for 18%

profile of v11, /device:TPU:0, one launch (start us, length us, event | category | flops | bytes accessed | tf_op | source)
XLA Modules:
  0.0 120.1 jit_solution(14802012415555319632)
XLA Ops:
  0.1 1.1 copy-done.5
  1.2 0.7 copy-done.6
  1.9 0.7 copy-done.7
  2.6 0.6 prepare.1
  3.2 0.5 collective-permute-start
  3.7 3.7 %collective-permute-start.2 = (bf16[64,2176]{1,0:T(8,128)(2,1)S(1)}, bf16[64,2176]{1,0:T(8,128)(2,1)S(1)}, u32[]{:S(2)}, u32[]{:S(2)}) collective-permute-start(bf16[64,2176]{1,0:T(8,128)(2,1)S(1)} %get-tuple-element.52.part.own.refs_0_), channel_id=1, source_target_pairs={{0,16},{2,18},{4,20},{6,22},{8,24},{10,26},{12,28},{14,30},{16,0},... | collective-permute-start | bytes 835592 | tf_op jit(solution)/shard_map/ppermute | solution.py:71
  7.4 1.5 %collective-permute-start.3 = (bf16[64,2176]{1,0:T(8,128)(2,1)S(1)}, bf16[64,2176]{1,0:T(8,128)(2,1)S(1)}, u32[]{:S(2)}, u32[]{:S(2)}) collective-permute-start(bf16[64,2176]{1,0:T(8,128)(2,1)S(1)} %get-tuple-element.52.part.own.refs_0_), channel_id=1, source_target_pairs={{0,4},{2,6},{4,0},{6,2},{8,12},{10,14},{12,8},{14,10},{16,20},{18,... | collective-permute-start | bytes 835592 | tf_op jit(solution)/shard_map/ppermute | solution.py:66
  8.9 1.5 %collective-permute-done.1.___.refs_3_ = bf16[64,2048]{1,0:T(8,128)(2,1)S(1)} collective-permute-done((bf16[64,2048]{1,0:T(8,128)(2,1)S(1)}, bf16[64,2048]{1,0:T(8,128)(2,1)S(1)}, u32[]{:S(2)}, u32[]{:S(2)}) %collective-permute-start.1) | collective-permute-done | bytes 262176 | tf_op jit(solution)/shard_map/ppermute | solution.py:66
  10.4 10.2 %collective-permute-done.2.came = bf16[64,2176]{1,0:T(8,128)(2,1)S(1)} collective-permute-done((bf16[64,2176]{1,0:T(8,128)(2,1)S(1)}, bf16[64,2176]{1,0:T(8,128)(2,1)S(1)}, u32[]{:S(2)}, u32[]{:S(2)}) %collective-permute-start.2) | collective-permute-done | bytes 278560 | tf_op jit(solution)/shard_map/ppermute | solution.py:71
  20.7 3.6 %collective-permute-start.12 = (bf16[64,2176]{1,0:T(8,128)(2,1)S(1)}, bf16[64,2176]{1,0:T(8,128)(2,1)S(1)}, u32[]{:S(2)}, u32[]{:S(2)}) collective-permute-start(bf16[64,2176]{1,0:T(8,128)(2,1)S(1)} %get-tuple-element.60), channel_id=1, source_target_pairs={{0,24},{2,26},{4,28},{6,30},{8,0},{10,2},{12,4},{14,6},{16,8},{18,... | collective-permute-start | bytes 835592 | tf_op jit(solution)/shard_map/ppermute | solution.py:71
  24.3 1.5 %collective-permute-start.5 = (bf16[1,64,2048]{2,1,0:T(8,128)(2,1)S(1)}, bf16[1,64,2048]{2,1,0:T(8,128)(2,1)S(1)}, u32[]{:S(2)}, u32[]{:S(2)}) collective-permute-start(bf16[1,64,2048]{2,1,0:T(8,128)(2,1)S(1)} %get-tuple-element.55), channel_id=1, source_target_pairs={{0,1},{1,0},{2,3},{3,2},{4,5},{5,4},{6,7},{7,6},{8,9},{9,8},{10,11... | collective-permute-start | bytes 786440 | tf_op jit(solution)/shard_map/ppermute | solution.py:66
  25.8 1.5 %collective-permute-start.7 = (bf16[1,64,2048]{2,1,0:T(8,128)(2,1)S(1)}, bf16[1,64,2048]{2,1,0:T(8,128)(2,1)S(1)}, u32[]{:S(2)}, u32[]{:S(2)}) collective-permute-start(bf16[1,64,2048]{2,1,0:T(8,128)(2,1)S(1)} %get-tuple-element.55), channel_id=1, source_target_pairs={{0,4},{2,6},{4,0},{6,2},{8,12},{10,14},{12,8},{14,10},{16,20},{18,... | collective-permute-start | bytes 786440 | tf_op jit(solution)/shard_map/ppermute | solution.py:66
  27.3 0.5 collective-permute-start.8
  27.8 1.3 %copy-done.4 = bf16[2,384,768]{2,1,0:T(8,128)(2,1)S(1)} copy-done((bf16[2,384,768]{2,1,0:T(8,128)(2,1)S(1)}, bf16[2,384,768]{2,1,0:T(8,128)(2,1)}, u32[]{:S(2)}) %copy-start.4) | copy-done | bytes 1179672
  29.1 0.7 turn.1
  29.8 4.1 %collective-permute-done.8.table = bf16[1,64,128]{2,1,0:T(8,128)(2,1)S(1)} collective-permute-done((bf16[1,64,128]{2,1,0:T(8,128)(2,1)S(1)}, bf16[1,64,128]{2,1,0:T(8,128)(2,1)S(1)}, u32[]{:S(2)}, u32[]{:S(2)}) %collective-permute-start.8) | collective-permute-done | bytes 16416 | tf_op jit(solution)/shard_map/ppermute | solution.py:66
  34.0 0.6 collective-permute-start.10
  34.6 1.5 %collective-permute-start.11 = (bf16[2,64,1024]{2,1,0:T(8,128)(2,1)S(1)}, bf16[2,64,1024]{2,1,0:T(8,128)(2,1)S(1)}, u32[]{:S(2)}, u32[]{:S(2)}) collective-permute-start(bf16[2,64,1024]{2,1,0:T(8,128)(2,1)S(1)} %get-tuple-element.59), channel_id=1, source_target_pairs={{0,4},{2,6},{4,0},{6,2},{8,12},{10,14},{12,8},{14,10},{16,20},{18,... | collective-permute-start | bytes 786440 | tf_op jit(solution)/shard_map/ppermute | solution.py:66
  36.1 1.0 collective-permute-done.13.refs_1_
  37.2 1.6 %collective-permute-start.16 = (bf16[2,64,2176]{2,1,0:T(8,128)(2,1)S(1)}, bf16[2,64,2176]{2,1,0:T(8,128)(2,1)S(1)}, u32[]{:S(2)}, u32[]{:S(2)}) collective-permute-start(bf16[2,64,2176]{2,1,0:T(8,128)(2,1)S(1)} %bitcast.7), channel_id=1, source_target_pairs={{0,4},{2,6},{4,0},{6,2},{8,12},{10,14},{12,8},{14,10},{16,20},{18,... | collective-permute-start | bytes 1671176 | tf_op jit(solution)/shard_map/ppermute | solution.py:66
  38.8 1.5 %collective-permute-start.17 = (bf16[2,64,2176]{2,1,0:T(8,128)(2,1)S(1)}, bf16[2,64,2176]{2,1,0:T(8,128)(2,1)S(1)}, u32[]{:S(2)}, u32[]{:S(2)}) collective-permute-start(bf16[2,64,2176]{2,1,0:T(8,128)(2,1)S(1)} %bitcast.8), channel_id=1, source_target_pairs={{0,1},{1,0},{2,3},{3,2},{4,5},{5,4},{6,7},{7,6},{8,9},{9,8},{10,11... | collective-permute-start | bytes 1671176 | tf_op jit(solution)/shard_map/ppermute | solution.py:66
  40.3 2.9 %collective-permute-done.10.left = bf16[2,64,1024]{2,1,0:T(8,128)(2,1)S(1)} collective-permute-done((bf16[2,64,1024]{2,1,0:T(8,128)(2,1)S(1)}, bf16[2,64,1024]{2,1,0:T(8,128)(2,1)S(1)}, u32[]{:S(2)}, u32[]{:S(2)}) %collective-permute-start.10) | collective-permute-done | bytes 262176 | tf_op jit(solution)/shard_map/ppermute | solution.py:66
  43.2 0.6 collective-permute-done.11.right
  43.9 0.5 collective-permute-start.4
  44.4 1.7 %collective-permute-done.4.lines_c.refs_5_ = bf16[1,64,2176]{2,1,0:T(8,128)(2,1)S(1)} collective-permute-done((bf16[1,64,2176]{2,1,0:T(8,128)(2,1)S(1)}, bf16[1,64,2176]{2,1,0:T(8,128)(2,1)S(1)}, u32[]{:S(2)}, u32[]{:S(2)}) %collective-permute-start.4) | collective-permute-done | bytes 278560 | tf_op jit(solution)/shard_map/ppermute | solution.py:66
  46.2 1.1 route.2
  47.3 4.3 %hidden.2.grads._ = bf16[2,384,768]{2,1,0:T(8,128)(2,1)S(1)} custom-call(s32[4]{0:T(128)S(1)} %pad_add_fusion.place, bf16[64,2176]{1,0:T(8,128)(2,1)S(1)} %get-tuple-element.52.part.own.refs_0_, bf16[64,2176]{1,0:T(8,128)(2,1)S(1)} %collective-permute-done.__.own_c.refs_1_, bf16[64,2048]{1,0:T(8,128)(2,1)S(1)} %get-tuple-element.53.far.refs_2_, ...), custom_call_target="tpu_custom_call" | custom-call | tf_op jit(solution)/shard_map/hidden/pallas_call | solution.py:76
  51.7 2.3 %sums.4 = (bf16[4,128,1024]{2,1,0:T(8,128)(2,1)S(1)}, bf16[4,128,1024]{2,1,0:T(8,128)(2,1)S(1)}) custom-call(bf16[2,384,768]{2,1,0:T(8,128)(2,1)S(1)} %hidden.2.grads._, bf16[2,384,2048]{2,1,0:T(8,128)(2,1)S(1)} %copy-done, bf16[2,384,2048]{2,1,0:T(8,128)(2,1)S(1)} %copy-done.1, bf16[4,256,192]{2,1,0:T(8,128)(2,1)S(1)} %get-tuple-element.65.pick_t, ...), custom_call_target="tpu_custom_call" | custom-call | tf_op jit(solution)/shard_map/sums/pallas_call | solution.py:76
  53.9 2.2 %sums.5 = (bf16[4,128,1024]{2,1,0:T(8,128)(2,1)S(1)}, bf16[4,128,1024]{2,1,0:T(8,128)(2,1)S(1)}) custom-call(bf16[2,384,768]{2,1,0:T(8,128)(2,1)S(1)} %hidden.2.grads._, bf16[2,384,2048]{2,1,0:T(8,128)(2,1)S(1)} %copy-done, bf16[2,384,2048]{2,1,0:T(8,128)(2,1)S(1)} %copy-done.1, bf16[4,256,192]{2,1,0:T(8,128)(2,1)S(1)} %get-tuple-element.65.pick_t, ...), custom_call_target="tpu_custom_call" | custom-call | tf_op jit(solution)/shard_map/sums/pallas_call | solution.py:76
  56.3 1.5 %collective-permute-start.18 = (bf16[2,64,1024]{2,1,0:T(8,128)(2,1)S(1)}, bf16[2,64,1024]{2,1,0:T(8,128)(2,1)S(1)}, u32[]{:S(2)}, u32[]{:S(2)}) collective-permute-start(bf16[2,64,1024]{2,1,0:T(8,128)(2,1)S(1)} %get-tuple-element.69.refs_0_), channel_id=1, source_target_pairs={{0,1},{1,0},{2,3},{3,2},{4,5},{5,4},{6,7},{7,6},{8,9},{9,8},{10,11... | collective-permute-start | bytes 786440 | tf_op jit(solution)/shard_map/ppermute | solution.py:66
  57.8 1.5 %collective-permute-start.19 = (bf16[2,64,1024]{2,1,0:T(8,128)(2,1)S(1)}, bf16[2,64,1024]{2,1,0:T(8,128)(2,1)S(1)}, u32[]{:S(2)}, u32[]{:S(2)}) collective-permute-start(bf16[2,64,1024]{2,1,0:T(8,128)(2,1)S(1)} %get-tuple-element.70), channel_id=1, source_target_pairs={{0,4},{2,6},{4,0},{6,2},{8,12},{10,14},{12,8},{14,10},{16,20},{18,... | collective-permute-start | bytes 786440 | tf_op jit(solution)/shard_map/ppermute | solution.py:66
  59.3 0.5 collective-permute-start.21
  59.8 4.8 %collective-permute-done.18.left = bf16[2,64,1024]{2,1,0:T(8,128)(2,1)S(1)} collective-permute-done((bf16[2,64,1024]{2,1,0:T(8,128)(2,1)S(1)}, bf16[2,64,1024]{2,1,0:T(8,128)(2,1)S(1)}, u32[]{:S(2)}, u32[]{:S(2)}) %collective-permute-start.18) | collective-permute-done | bytes 262176 | tf_op jit(solution)/shard_map/ppermute | solution.py:66
  64.7 1.2 collective-permute-done.19.right
  65.9 0.6 collective-permute-start.29
  66.6 0.6 collective-permute-start.20
  67.3 1.6 %collective-permute-start.22 = (bf16[2,128,1024]{2,1,0:T(8,128)(2,1)S(1)}, bf16[2,128,1024]{2,1,0:T(8,128)(2,1)S(1)}, u32[]{:S(2)}, u32[]{:S(2)}) collective-permute-start(bf16[2,128,1024]{2,1,0:T(8,128)(2,1)S(1)} %get-tuple-element.75._.refs_13_), channel_id=1, source_target_pairs={{0,4},{2,6},{4,0},{6,2},{8,12},{10,14},{12,8},{14,10},{16,20},{18,... | collective-permute-start | bytes 1572872 | tf_op jit(solution)/shard_map/ppermute | solution.py:66
  68.9 1.1 route.3
  70.1 4.1 %hidden.3.grads._ = bf16[2,384,768]{2,1,0:T(8,128)(2,1)S(1)} custom-call(s32[4]{0:T(128)S(1)} %pad_add_fusion.place, bf16[2,64,2176]{2,1,0:T(8,128)(2,1)S(1)} %bitcast.13, bf16[2,64,2176]{2,1,0:T(8,128)(2,1)S(1)} %collective-permute-done.26.lines_c.refs_1_, bf16[2,64,2176]{2,1,0:T(8,128)(2,1)S(1)} %collective-permute-done.17.side.refs_2_, ...), custom_call_target="tpu_custom_call" | custom-call | tf_op jit(solution)/shard_map/hidden/pallas_call | solution.py:76
  74.2 2.2 %sums.6 = (bf16[4,128,1024]{2,1,0:T(8,128)(2,1)S(1)}, bf16[4,128,1024]{2,1,0:T(8,128)(2,1)S(1)}) custom-call(bf16[2,384,768]{2,1,0:T(8,128)(2,1)S(1)} %hidden.3.grads._, bf16[2,384,2048]{2,1,0:T(8,128)(2,1)S(1)} %copy-done, bf16[2,384,2048]{2,1,0:T(8,128)(2,1)S(1)} %copy-done.1, bf16[4,256,192]{2,1,0:T(8,128)(2,1)S(1)} %get-tuple-element.84.pick_t, ...), custom_call_target="tpu_custom_call" | custom-call | tf_op jit(solution)/shard_map/sums/pallas_call | solution.py:76
  76.5 2.2 %sums.7 = (bf16[4,128,1024]{2,1,0:T(8,128)(2,1)S(1)}, bf16[4,128,1024]{2,1,0:T(8,128)(2,1)S(1)}) custom-call(bf16[2,384,768]{2,1,0:T(8,128)(2,1)S(1)} %hidden.3.grads._, bf16[2,384,2048]{2,1,0:T(8,128)(2,1)S(1)} %copy-done, bf16[2,384,2048]{2,1,0:T(8,128)(2,1)S(1)} %copy-done.1, bf16[4,256,192]{2,1,0:T(8,128)(2,1)S(1)} %get-tuple-element.84.pick_t, ...), custom_call_target="tpu_custom_call" | custom-call | tf_op jit(solution)/shard_map/sums/pallas_call | solution.py:76
  78.8 0.6 collective-permute-start.32
  79.3 1.2 collective-permute-done.20.came_l
  80.5 0.7 collective-permute-done.22.came_r
  81.2 0.1 second_sum.2
  81.3 1.6 %collective-permute-start.23 = (bf16[2,64,1024]{2,1,0:T(8,128)(2,1)S(1)}, bf16[2,64,1024]{2,1,0:T(8,128)(2,1)S(1)}, u32[]{:S(2)}, u32[]{:S(2)}) collective-permute-start(bf16[2,64,1024]{2,1,0:T(8,128)(2,1)S(1)} %get-tuple-element.77._), channel_id=1, source_target_pairs={{0,4},{2,6},{4,0},{6,2},{8,12},{10,14},{12,8},{14,10},{16,20},{18,... | collective-permute-start | bytes 786440 | tf_op jit(solution)/shard_map/ppermute | solution.py:66
  82.9 1.3 %collective-permute-start.24 = (bf16[2,64,1024]{2,1,0:T(8,128)(2,1)S(1)}, bf16[2,64,1024]{2,1,0:T(8,128)(2,1)S(1)}, u32[]{:S(2)}, u32[]{:S(2)}) collective-permute-start(bf16[2,64,1024]{2,1,0:T(8,128)(2,1)S(1)} %get-tuple-element.79), channel_id=1, source_target_pairs={{0,1},{1,0},{2,3},{3,2},{4,5},{5,4},{6,7},{7,6},{8,9},{9,8},{10,11... | collective-permute-start | bytes 786440 | tf_op jit(solution)/shard_map/ppermute | solution.py:66
  84.2 0.1 first_left.3
  84.3 0.8 collective-permute-start.31
  85.3 0.5 collective-permute-start.33
  85.8 4.8 %collective-permute-done.23.came_l = bf16[2,64,1024]{2,1,0:T(8,128)(2,1)S(1)} collective-permute-done((bf16[2,64,1024]{2,1,0:T(8,128)(2,1)S(1)}, bf16[2,64,1024]{2,1,0:T(8,128)(2,1)S(1)}, u32[]{:S(2)}, u32[]{:S(2)}) %collective-permute-start.23) | collective-permute-done | bytes 262176 | tf_op jit(solution)/shard_map/ppermute | solution.py:66
  90.6 1.5 %collective-permute-done.24.came_r = bf16[2,64,1024]{2,1,0:T(8,128)(2,1)S(1)} collective-permute-done((bf16[2,64,1024]{2,1,0:T(8,128)(2,1)S(1)}, bf16[2,64,1024]{2,1,0:T(8,128)(2,1)S(1)}, u32[]{:S(2)}, u32[]{:S(2)}) %collective-permute-start.24) | collective-permute-done | bytes 262176 | tf_op jit(solution)/shard_map/ppermute | solution.py:66
  92.2 0.1 third_sum.2
  92.3 0.7 collective-permute-start.25
  93.0 8.2 %collective-permute-done.31.came_l = bf16[4,64,1024]{2,1,0:T(8,128)(2,1)S(1)} collective-permute-done((bf16[4,64,1024]{2,1,0:T(8,128)(2,1)S(1)}, bf16[4,64,1024]{2,1,0:T(8,128)(2,1)S(1)}, u32[]{:S(2)}, u32[]{:S(2)}) %collective-permute-start.31) | collective-permute-done | bytes 524320 | tf_op jit(solution)/shard_map/ppermute | solution.py:66
  101.3 0.5 collective-permute-start.34
  101.9 1.0 collective-permute-start.35
  102.9 4.9 %collective-permute-done.34.came_l = bf16[2,64,1024]{2,1,0:T(8,128)(2,1)S(1)} collective-permute-done((bf16[2,64,1024]{2,1,0:T(8,128)(2,1)S(1)}, bf16[2,64,1024]{2,1,0:T(8,128)(2,1)S(1)}, u32[]{:S(2)}, u32[]{:S(2)}) %collective-permute-start.34) | collective-permute-done | bytes 262176 | tf_op jit(solution)/shard_map/ppermute | solution.py:66
  107.8 0.5 collective-permute-done.35.came_r
  108.2 0.1 third_sum.3
  108.4 3.8 %collective-permute-start.37 = (bf16[64,2048]{1,0:T(8,128)(2,1)S(1)}, bf16[64,2048]{1,0:T(8,128)(2,1)S(1)}, u32[]{:S(2)}, u32[]{:S(2)}) collective-permute-start(bf16[64,2048]{1,0:T(8,128)(2,1)S(1)} %get-tuple-element.98), channel_id=1, source_target_pairs={{0,24},{2,26},{4,28},{6,30},{8,0},{10,2},{12,4},{14,6},{16,8},{18,... | collective-permute-start | bytes 786440 | tf_op jit(solution)/shard_map/ppermute | solution.py:71
  112.3 6.1 %collective-permute-done.36.refs_2_ = bf16[64,2048]{1,0:T(8,128)(2,1)S(1)} collective-permute-done((bf16[64,2048]{1,0:T(8,128)(2,1)S(1)}, bf16[64,2048]{1,0:T(8,128)(2,1)S(1)}, u32[]{:S(2)}, u32[]{:S(2)}) %collective-permute-start.36) | collective-permute-done | bytes 262176 | tf_op jit(solution)/shard_map/ppermute | solution.py:71
  118.3 0.9 collective-permute-done.37.refs_3_
  119.2 0.9 last_sum.1
  (55 shorter events, 1.3 us)
Async XLA Ops:
  0.0 27.8 %copy-start.3 = (bf16[2,384,768]{2,1,0:T(8,128)(2,1)S(1)}, bf16[2,384,768]{2,1,0:T(8,128)(2,1)}, u32[]{:S(2)}) copy-start(bf16[2,384,768]{2,1,0:T(8,128)(2,1)} %gate.1) | copy-start | bytes 3538948
  0.1 1.1 copy-start.5
  1.2 0.7 copy-start.6
  1.9 0.7 copy-start.7
  3.2 7.2 %collective-permute-start = (bf16[64,2176]{1,0:T(8,128)(2,1)S(1)}, bf16[64,2176]{1,0:T(8,128)(2,1)S(1)}, u32[]{:S(2)}, u32[]{:S(2)}) collective-permute-start(bf16[64,2176]{1,0:T(8,128)(2,1)S(1)} %get-tuple-element.52.part.own.refs_0_), channel_id=1, source_target_pairs={{0,2},{2,0},{4,6},{6,4},{8,10},{10,8},{12,14},{14,12},{16,18},{18,... | collective-permute-start | bytes 835592 | tf_op jit(solution)/shard_map/ppermute | solution.py:66
  3.7 16.9 %collective-permute-start.2 = (bf16[64,2176]{1,0:T(8,128)(2,1)S(1)}, bf16[64,2176]{1,0:T(8,128)(2,1)S(1)}, u32[]{:S(2)}, u32[]{:S(2)}) collective-permute-start(bf16[64,2176]{1,0:T(8,128)(2,1)S(1)} %get-tuple-element.52.part.own.refs_0_), channel_id=1, source_target_pairs={{0,16},{2,18},{4,20},{6,22},{8,24},{10,26},{12,28},{14,30},{16,0},... | collective-permute-start | bytes 835592 | tf_op jit(solution)/shard_map/ppermute | solution.py:71
  7.4 13.2 %collective-permute-start.3 = (bf16[64,2176]{1,0:T(8,128)(2,1)S(1)}, bf16[64,2176]{1,0:T(8,128)(2,1)S(1)}, u32[]{:S(2)}, u32[]{:S(2)}) collective-permute-start(bf16[64,2176]{1,0:T(8,128)(2,1)S(1)} %get-tuple-element.52.part.own.refs_0_), channel_id=1, source_target_pairs={{0,4},{2,6},{4,0},{6,2},{8,12},{10,14},{12,8},{14,10},{16,20},{18,... | collective-permute-start | bytes 835592 | tf_op jit(solution)/shard_map/ppermute | solution.py:66
  8.9 1.5 %collective-permute-start.1 = (bf16[64,2048]{1,0:T(8,128)(2,1)S(1)}, bf16[64,2048]{1,0:T(8,128)(2,1)S(1)}, u32[]{:S(2)}, u32[]{:S(2)}) collective-permute-start(bf16[64,2048]{1,0:T(8,128)(2,1)S(1)} %get-tuple-element.53.far.refs_2_), channel_id=1, source_target_pairs={{0,2},{2,0},{4,6},{6,4},{8,10},{10,8},{12,14},{14,12},{16,18},{18,... | collective-permute-start | bytes 786440 | tf_op jit(solution)/shard_map/ppermute | solution.py:66
  20.7 15.5 %collective-permute-start.12 = (bf16[64,2176]{1,0:T(8,128)(2,1)S(1)}, bf16[64,2176]{1,0:T(8,128)(2,1)S(1)}, u32[]{:S(2)}, u32[]{:S(2)}) collective-permute-start(bf16[64,2176]{1,0:T(8,128)(2,1)S(1)} %get-tuple-element.60), channel_id=1, source_target_pairs={{0,24},{2,26},{4,28},{6,30},{8,0},{10,2},{12,4},{14,6},{16,8},{18,... | collective-permute-start | bytes 835592 | tf_op jit(solution)/shard_map/ppermute | solution.py:71
  24.3 12.9 %collective-permute-start.13 = (bf16[64,2176]{1,0:T(8,128)(2,1)S(1)}, bf16[64,2176]{1,0:T(8,128)(2,1)S(1)}, u32[]{:S(2)}, u32[]{:S(2)}) collective-permute-start(bf16[64,2176]{1,0:T(8,128)(2,1)S(1)} %get-tuple-element.60), channel_id=1, source_target_pairs={{0,8},{2,10},{4,12},{6,14},{8,16},{10,18},{12,20},{14,22},{16,24},... | collective-permute-start | bytes 835592 | tf_op jit(solution)/shard_map/ppermute | solution.py:71
  24.3 9.6 %collective-permute-start.5 = (bf16[1,64,2048]{2,1,0:T(8,128)(2,1)S(1)}, bf16[1,64,2048]{2,1,0:T(8,128)(2,1)S(1)}, u32[]{:S(2)}, u32[]{:S(2)}) collective-permute-start(bf16[1,64,2048]{2,1,0:T(8,128)(2,1)S(1)} %get-tuple-element.55), channel_id=1, source_target_pairs={{0,1},{1,0},{2,3},{3,2},{4,5},{5,4},{6,7},{7,6},{8,9},{9,8},{10,11... | collective-permute-start | bytes 786440 | tf_op jit(solution)/shard_map/ppermute | solution.py:66
  25.8 8.1 %collective-permute-start.7 = (bf16[1,64,2048]{2,1,0:T(8,128)(2,1)S(1)}, bf16[1,64,2048]{2,1,0:T(8,128)(2,1)S(1)}, u32[]{:S(2)}, u32[]{:S(2)}) collective-permute-start(bf16[1,64,2048]{2,1,0:T(8,128)(2,1)S(1)} %get-tuple-element.55), channel_id=1, source_target_pairs={{0,4},{2,6},{4,0},{6,2},{8,12},{10,14},{12,8},{14,10},{16,20},{18,... | collective-permute-start | bytes 786440 | tf_op jit(solution)/shard_map/ppermute | solution.py:66
  27.3 6.5 %collective-permute-start.8 = (bf16[1,64,128]{2,1,0:T(8,128)(2,1)S(1)}, bf16[1,64,128]{2,1,0:T(8,128)(2,1)S(1)}, u32[]{:S(2)}, u32[]{:S(2)}) collective-permute-start(bf16[1,64,128]{2,1,0:T(8,128)(2,1)S(1)} %get-tuple-element.56), channel_id=1, source_target_pairs={{0,4},{2,6},{4,0},{6,2},{8,12},{10,14},{12,8},{14,10},{16,20},{18,... | collective-permute-start | bytes 49160 | tf_op jit(solution)/shard_map/ppermute | solution.py:66
  27.8 1.3 %copy-start.4 = (bf16[2,384,768]{2,1,0:T(8,128)(2,1)S(1)}, bf16[2,384,768]{2,1,0:T(8,128)(2,1)}, u32[]{:S(2)}) copy-start(bf16[2,384,768]{2,1,0:T(8,128)(2,1)} %up.1) | copy-start | bytes 3538948
  33.9 3.3 %collective-permute-start.9 = (bf16[2,64,2176]{2,1,0:T(8,128)(2,1)S(1)}, bf16[2,64,2176]{2,1,0:T(8,128)(2,1)S(1)}, u32[]{:S(2)}, u32[]{:S(2)}) collective-permute-start(bf16[2,64,2176]{2,1,0:T(8,128)(2,1)S(1)} %get-tuple-element.57.over.refs_8_), channel_id=1, source_target_pairs={{0,2},{2,0},{4,6},{6,4},{8,10},{10,8},{12,14},{14,12},{16,18},{18,... | collective-permute-start | bytes 1671176 | tf_op jit(solution)/shard_map/ppermute | solution.py:66
  34.0 9.2 %collective-permute-start.10 = (bf16[2,64,1024]{2,1,0:T(8,128)(2,1)S(1)}, bf16[2,64,1024]{2,1,0:T(8,128)(2,1)S(1)}, u32[]{:S(2)}, u32[]{:S(2)}) collective-permute-start(bf16[2,64,1024]{2,1,0:T(8,128)(2,1)S(1)} %get-tuple-element.58), channel_id=1, source_target_pairs={{0,1},{1,0},{2,3},{3,2},{4,5},{5,4},{6,7},{7,6},{8,9},{9,8},{10,11... | collective-permute-start | bytes 786440 | tf_op jit(solution)/shard_map/ppermute | solution.py:66
  34.6 9.2 %collective-permute-start.11 = (bf16[2,64,1024]{2,1,0:T(8,128)(2,1)S(1)}, bf16[2,64,1024]{2,1,0:T(8,128)(2,1)S(1)}, u32[]{:S(2)}, u32[]{:S(2)}) collective-permute-start(bf16[2,64,1024]{2,1,0:T(8,128)(2,1)S(1)} %get-tuple-element.59), channel_id=1, source_target_pairs={{0,4},{2,6},{4,0},{6,2},{8,12},{10,14},{12,8},{14,10},{16,20},{18,... | collective-permute-start | bytes 786440 | tf_op jit(solution)/shard_map/ppermute | solution.py:66
  37.2 19.0 %collective-permute-start.16 = (bf16[2,64,2176]{2,1,0:T(8,128)(2,1)S(1)}, bf16[2,64,2176]{2,1,0:T(8,128)(2,1)S(1)}, u32[]{:S(2)}, u32[]{:S(2)}) collective-permute-start(bf16[2,64,2176]{2,1,0:T(8,128)(2,1)S(1)} %bitcast.7), channel_id=1, source_target_pairs={{0,4},{2,6},{4,0},{6,2},{8,12},{10,14},{12,8},{14,10},{16,20},{18,... | collective-permute-start | bytes 1671176 | tf_op jit(solution)/shard_map/ppermute | solution.py:66
  38.8 17.4 %collective-permute-start.17 = (bf16[2,64,2176]{2,1,0:T(8,128)(2,1)S(1)}, bf16[2,64,2176]{2,1,0:T(8,128)(2,1)S(1)}, u32[]{:S(2)}, u32[]{:S(2)}) collective-permute-start(bf16[2,64,2176]{2,1,0:T(8,128)(2,1)S(1)} %bitcast.8), channel_id=1, source_target_pairs={{0,1},{1,0},{2,3},{3,2},{4,5},{5,4},{6,7},{7,6},{8,9},{9,8},{10,11... | collective-permute-start | bytes 1671176 | tf_op jit(solution)/shard_map/ppermute | solution.py:66
  43.8 3.6 %copy-start.2 = (bf16[2,384,2048]{2,1,0:T(8,128)(2,1)S(1)}, bf16[2,384,2048]{2,1,0:T(8,128)(2,1)}, u32[]{:S(2)}) copy-start(bf16[2,384,2048]{2,1,0:T(8,128)(2,1)} %refs_10_.1) | copy-start | bytes 9437188
  43.8 3.5 %collective-permute-start.14 = (bf16[2,64,2048]{2,1,0:T(8,128)(2,1)S(1)}, bf16[2,64,2048]{2,1,0:T(8,128)(2,1)S(1)}, u32[]{:S(2)}, u32[]{:S(2)}) collective-permute-start(bf16[2,64,2048]{2,1,0:T(8,128)(2,1)S(1)} %join.2.refs_10_), channel_id=1, source_target_pairs={{0,2},{2,0},{4,6},{6,4},{8,10},{10,8},{12,14},{14,12},{16,18},{18,... | collective-permute-start | bytes 1572872 | tf_op jit(solution)/shard_map/ppermute | solution.py:66
  43.9 2.3 %collective-permute-start.4 = (bf16[1,64,2176]{2,1,0:T(8,128)(2,1)S(1)}, bf16[1,64,2176]{2,1,0:T(8,128)(2,1)S(1)}, u32[]{:S(2)}, u32[]{:S(2)}) collective-permute-start(bf16[1,64,2176]{2,1,0:T(8,128)(2,1)S(1)} %get-tuple-element.54.refs_0_.lines.refs_4_), channel_id=1, source_target_pairs={{0,2},{2,0},{4,6},{6,4},{8,10},{10,8},{12,14},{14,12},{16,18},{18,... | collective-permute-start | bytes 835592 | tf_op jit(solution)/shard_map/ppermute | solution.py:66
  44.4 2.9 %collective-permute-start.6 = (bf16[1,64,2048]{2,1,0:T(8,128)(2,1)S(1)}, bf16[1,64,2048]{2,1,0:T(8,128)(2,1)S(1)}, u32[]{:S(2)}, u32[]{:S(2)}) collective-permute-start(bf16[1,64,2048]{2,1,0:T(8,128)(2,1)S(1)} %collective-permute-done.5.side.refs_6_), channel_id=1, source_target_pairs={{0,2},{2,0},{4,6},{6,4},{8,10},{10,8},{12,14},{14,12},{16,18},{18,... | collective-permute-start | bytes 786440 | tf_op jit(solution)/shard_map/ppermute | solution.py:66
  47.3 4.4 %copy-start = (bf16[2,384,2048]{2,1,0:T(8,128)(2,1)S(1)}, bf16[2,384,2048]{2,1,0:T(8,128)(2,1)}, u32[]{:S(2)}) copy-start(bf16[2,384,2048]{2,1,0:T(8,128)(2,1)} %w_gate.7) | copy-start | bytes 9437188
  47.3 4.3 %copy-start.1 = (bf16[2,384,2048]{2,1,0:T(8,128)(2,1)S(1)}, bf16[2,384,2048]{2,1,0:T(8,128)(2,1)}, u32[]{:S(2)}) copy-start(bf16[2,384,2048]{2,1,0:T(8,128)(2,1)} %w_up.7) | copy-start | bytes 9437188
  56.3 8.4 %collective-permute-start.18 = (bf16[2,64,1024]{2,1,0:T(8,128)(2,1)S(1)}, bf16[2,64,1024]{2,1,0:T(8,128)(2,1)S(1)}, u32[]{:S(2)}, u32[]{:S(2)}) collective-permute-start(bf16[2,64,1024]{2,1,0:T(8,128)(2,1)S(1)} %get-tuple-element.69.refs_0_), channel_id=1, source_target_pairs={{0,1},{1,0},{2,3},{3,2},{4,5},{5,4},{6,7},{7,6},{8,9},{9,8},{10,11... | collective-permute-start | bytes 786440 | tf_op jit(solution)/shard_map/ppermute | solution.py:66
  57.8 8.1 %collective-permute-start.19 = (bf16[2,64,1024]{2,1,0:T(8,128)(2,1)S(1)}, bf16[2,64,1024]{2,1,0:T(8,128)(2,1)S(1)}, u32[]{:S(2)}, u32[]{:S(2)}) collective-permute-start(bf16[2,64,1024]{2,1,0:T(8,128)(2,1)S(1)} %get-tuple-element.70), channel_id=1, source_target_pairs={{0,4},{2,6},{4,0},{6,2},{8,12},{10,14},{12,8},{14,10},{16,20},{18,... | collective-permute-start | bytes 786440 | tf_op jit(solution)/shard_map/ppermute | solution.py:66
  59.3 6.6 %collective-permute-start.15 = (bf16[4,128,1024]{2,1,0:T(8,128)(2,1)S(1)}, bf16[4,128,1024]{2,1,0:T(8,128)(2,1)S(1)}, u32[]{:S(2)}, u32[]{:S(2)}) collective-permute-start(bf16[4,128,1024]{2,1,0:T(8,128)(2,1)S(1)} %get-tuple-element.67._), channel_id=1, source_target_pairs={{0,2},{2,0},{4,6},{6,4},{8,10},{10,8},{12,14},{14,12},{16,18},{18,... | collective-permute-start | bytes 3145736 | tf_op jit(solution)/shard_map/ppermute | solution.py:66
  59.3 7.3 %collective-permute-start.21 = (bf16[4,128,1024]{2,1,0:T(8,128)(2,1)S(1)}, bf16[4,128,1024]{2,1,0:T(8,128)(2,1)S(1)}, u32[]{:S(2)}, u32[]{:S(2)}) collective-permute-start(bf16[4,128,1024]{2,1,0:T(8,128)(2,1)S(1)} %get-tuple-element.68._), channel_id=1, source_target_pairs={{0,2},{2,0},{4,6},{6,4},{8,10},{10,8},{12,14},{14,12},{16,18},{18,... | collective-permute-start | bytes 3145736 | tf_op jit(solution)/shard_map/ppermute | solution.py:66
  59.8 7.5 %collective-permute-start.26 = (bf16[2,64,2176]{2,1,0:T(8,128)(2,1)S(1)}, bf16[2,64,2176]{2,1,0:T(8,128)(2,1)S(1)}, u32[]{:S(2)}, u32[]{:S(2)}) collective-permute-start(bf16[2,64,2176]{2,1,0:T(8,128)(2,1)S(1)} %bitcast.11), channel_id=1, source_target_pairs={{0,2},{2,0},{4,6},{6,4},{8,10},{10,8},{12,14},{14,12},{16,18},{18,... | collective-permute-start | bytes 1671176 | tf_op jit(solution)/shard_map/ppermute | solution.py:66
  64.7 5.4 %collective-permute-start.27 = (bf16[2,64,2176]{2,1,0:T(8,128)(2,1)S(1)}, bf16[2,64,2176]{2,1,0:T(8,128)(2,1)S(1)}, u32[]{:S(2)}, u32[]{:S(2)}) collective-permute-start(bf16[2,64,2176]{2,1,0:T(8,128)(2,1)S(1)} %collective-permute-done.17.side.refs_2_), channel_id=1, source_target_pairs={{0,2},{2,0},{4,6},{6,4},{8,10},{10,8},{12,14},{14,12},{16,18},{18,... | collective-permute-start | bytes 1671176 | tf_op jit(solution)/shard_map/ppermute | solution.py:66
  65.9 3.1 %collective-permute-start.28 = (bf16[2,64,2176]{2,1,0:T(8,128)(2,1)S(1)}, bf16[2,64,2176]{2,1,0:T(8,128)(2,1)S(1)}, u32[]{:S(2)}, u32[]{:S(2)}) collective-permute-start(bf16[2,64,2176]{2,1,0:T(8,128)(2,1)S(1)} %collective-permute-done.16.over.refs_4_), channel_id=1, source_target_pairs={{0,2},{2,0},{4,6},{6,4},{8,10},{10,8},{12,14},{14,12},{16,18},{18,... | collective-permute-start | bytes 1671176 | tf_op jit(solution)/shard_map/ppermute | solution.py:66
  65.9 4.2 %collective-permute-start.29 = (bf16[2,64,2048]{2,1,0:T(8,128)(2,1)S(1)}, bf16[2,64,2048]{2,1,0:T(8,128)(2,1)S(1)}, u32[]{:S(2)}, u32[]{:S(2)}) collective-permute-start(bf16[2,64,2048]{2,1,0:T(8,128)(2,1)S(1)} %join.3._.refs_6_), channel_id=1, source_target_pairs={{0,2},{2,0},{4,6},{6,4},{8,10},{10,8},{12,14},{14,12},{16,18},{18,... | collective-permute-start | bytes 1572872 | tf_op jit(solution)/shard_map/ppermute | solution.py:66
  66.6 13.9 %collective-permute-start.20 = (bf16[4,64,1024]{2,1,0:T(8,128)(2,1)S(1)}, bf16[4,64,1024]{2,1,0:T(8,128)(2,1)S(1)}, u32[]{:S(2)}, u32[]{:S(2)}) collective-permute-start(bf16[4,64,1024]{2,1,0:T(8,128)(2,1)S(1)} %get-tuple-element.72._), channel_id=1, source_target_pairs={{0,1},{1,0},{2,3},{3,2},{4,5},{5,4},{6,7},{7,6},{8,9},{9,8},{10,11... | collective-permute-start | bytes 1572872 | tf_op jit(solution)/shard_map/ppermute | solution.py:66
  67.3 13.9 %collective-permute-start.22 = (bf16[2,128,1024]{2,1,0:T(8,128)(2,1)S(1)}, bf16[2,128,1024]{2,1,0:T(8,128)(2,1)S(1)}, u32[]{:S(2)}, u32[]{:S(2)}) collective-permute-start(bf16[2,128,1024]{2,1,0:T(8,128)(2,1)S(1)} %get-tuple-element.75._.refs_13_), channel_id=1, source_target_pairs={{0,4},{2,6},{4,0},{6,2},{8,12},{10,14},{12,8},{14,10},{16,20},{18,... | collective-permute-start | bytes 1572872 | tf_op jit(solution)/shard_map/ppermute | solution.py:66
  76.4 7.7 %collective-permute-start.30 = (bf16[4,128,1024]{2,1,0:T(8,128)(2,1)S(1)}, bf16[4,128,1024]{2,1,0:T(8,128)(2,1)S(1)}, u32[]{:S(2)}, u32[]{:S(2)}) collective-permute-start(bf16[4,128,1024]{2,1,0:T(8,128)(2,1)S(1)} %get-tuple-element.86._), channel_id=1, source_target_pairs={{0,2},{2,0},{4,6},{6,4},{8,10},{10,8},{12,14},{14,12},{16,18},{18,... | collective-permute-start | bytes 3145736 | tf_op jit(solution)/shard_map/ppermute | solution.py:66
  78.8 6.4 %collective-permute-start.32 = (bf16[4,128,1024]{2,1,0:T(8,128)(2,1)S(1)}, bf16[4,128,1024]{2,1,0:T(8,128)(2,1)S(1)}, u32[]{:S(2)}, u32[]{:S(2)}) collective-permute-start(bf16[4,128,1024]{2,1,0:T(8,128)(2,1)S(1)} %get-tuple-element.90), channel_id=1, source_target_pairs={{0,2},{2,0},{4,6},{6,4},{8,10},{10,8},{12,14},{14,12},{16,18},{18,... | collective-permute-start | bytes 3145736 | tf_op jit(solution)/shard_map/ppermute | solution.py:66
  81.3 9.3 %collective-permute-start.23 = (bf16[2,64,1024]{2,1,0:T(8,128)(2,1)S(1)}, bf16[2,64,1024]{2,1,0:T(8,128)(2,1)S(1)}, u32[]{:S(2)}, u32[]{:S(2)}) collective-permute-start(bf16[2,64,1024]{2,1,0:T(8,128)(2,1)S(1)} %get-tuple-element.77._), channel_id=1, source_target_pairs={{0,4},{2,6},{4,0},{6,2},{8,12},{10,14},{12,8},{14,10},{16,20},{18,... | collective-permute-start | bytes 786440 | tf_op jit(solution)/shard_map/ppermute | solution.py:66
  82.9 9.2 %collective-permute-start.24 = (bf16[2,64,1024]{2,1,0:T(8,128)(2,1)S(1)}, bf16[2,64,1024]{2,1,0:T(8,128)(2,1)S(1)}, u32[]{:S(2)}, u32[]{:S(2)}) collective-permute-start(bf16[2,64,1024]{2,1,0:T(8,128)(2,1)S(1)} %get-tuple-element.79), channel_id=1, source_target_pairs={{0,1},{1,0},{2,3},{3,2},{4,5},{5,4},{6,7},{7,6},{8,9},{9,8},{10,11... | collective-permute-start | bytes 786440 | tf_op jit(solution)/shard_map/ppermute | solution.py:66
  84.3 16.9 %collective-permute-start.31 = (bf16[4,64,1024]{2,1,0:T(8,128)(2,1)S(1)}, bf16[4,64,1024]{2,1,0:T(8,128)(2,1)S(1)}, u32[]{:S(2)}, u32[]{:S(2)}) collective-permute-start(bf16[4,64,1024]{2,1,0:T(8,128)(2,1)S(1)} %get-tuple-element.88._), channel_id=1, source_target_pairs={{0,1},{1,0},{2,3},{3,2},{4,5},{5,4},{6,7},{7,6},{8,9},{9,8},{10,11... | collective-permute-start | bytes 1572872 | tf_op jit(solution)/shard_map/ppermute | solution.py:66
  85.3 16.0 %collective-permute-start.33 = (bf16[2,128,1024]{2,1,0:T(8,128)(2,1)S(1)}, bf16[2,128,1024]{2,1,0:T(8,128)(2,1)S(1)}, u32[]{:S(2)}, u32[]{:S(2)}) collective-permute-start(bf16[2,128,1024]{2,1,0:T(8,128)(2,1)S(1)} %get-tuple-element.92), channel_id=1, source_target_pairs={{0,4},{2,6},{4,0},{6,2},{8,12},{10,14},{12,8},{14,10},{16,20},{18,... | collective-permute-start | bytes 1572872 | tf_op jit(solution)/shard_map/ppermute | solution.py:66
  92.3 10.6 %collective-permute-start.25 = (bf16[64,2048]{1,0:T(8,128)(2,1)S(1)}, bf16[64,2048]{1,0:T(8,128)(2,1)S(1)}, u32[]{:S(2)}, u32[]{:S(2)}) collective-permute-start(bf16[64,2048]{1,0:T(8,128)(2,1)S(1)} %get-tuple-element.81), channel_id=1, source_target_pairs={{0,16},{2,18},{4,20},{6,22},{8,24},{10,26},{12,28},{14,30},{16,0},... | collective-permute-start | bytes 786440 | tf_op jit(solution)/shard_map/ppermute | solution.py:71
  101.3 6.4 %collective-permute-start.34 = (bf16[2,64,1024]{2,1,0:T(8,128)(2,1)S(1)}, bf16[2,64,1024]{2,1,0:T(8,128)(2,1)S(1)}, u32[]{:S(2)}, u32[]{:S(2)}) collective-permute-start(bf16[2,64,1024]{2,1,0:T(8,128)(2,1)S(1)} %get-tuple-element.94), channel_id=1, source_target_pairs={{0,4},{2,6},{4,0},{6,2},{8,12},{10,14},{12,8},{14,10},{16,20},{18,... | collective-permute-start | bytes 786440 | tf_op jit(solution)/shard_map/ppermute | solution.py:66
  101.9 6.4 %collective-permute-start.35 = (bf16[2,64,1024]{2,1,0:T(8,128)(2,1)S(1)}, bf16[2,64,1024]{2,1,0:T(8,128)(2,1)S(1)}, u32[]{:S(2)}, u32[]{:S(2)}) collective-permute-start(bf16[2,64,1024]{2,1,0:T(8,128)(2,1)S(1)} %get-tuple-element.96), channel_id=1, source_target_pairs={{0,1},{1,0},{2,3},{3,2},{4,5},{5,4},{6,7},{7,6},{8,9},{9,8},{10,11... | collective-permute-start | bytes 786440 | tf_op jit(solution)/shard_map/ppermute | solution.py:66
  108.4 9.9 %collective-permute-start.36 = (bf16[64,2048]{1,0:T(8,128)(2,1)S(1)}, bf16[64,2048]{1,0:T(8,128)(2,1)S(1)}, u32[]{:S(2)}, u32[]{:S(2)}) collective-permute-start(bf16[64,2048]{1,0:T(8,128)(2,1)S(1)} %get-tuple-element.97), channel_id=1, source_target_pairs={{0,8},{2,10},{4,12},{6,14},{8,16},{10,18},{12,20},{14,22},{16,24},... | collective-permute-start | bytes 786440 | tf_op jit(solution)/shard_map/ppermute | solution.py:71
  108.4 10.8 %collective-permute-start.37 = (bf16[64,2048]{1,0:T(8,128)(2,1)S(1)}, bf16[64,2048]{1,0:T(8,128)(2,1)S(1)}, u32[]{:S(2)}, u32[]{:S(2)}) collective-permute-start(bf16[64,2048]{1,0:T(8,128)(2,1)S(1)} %get-tuple-element.98), channel_id=1, source_target_pairs={{0,24},{2,26},{4,28},{6,30},{8,0},{10,2},{12,4},{14,6},{16,8},{18,... | collective-permute-start | bytes 786440 | tf_op jit(solution)/shard_map/ppermute | solution.py:71

commit v12 on v7

--- a/solution.py
+++ b/solution.py
@@ -128,7 +128,7 @@
             pltpu.VMEM(ids.shape, jnp.int32),
             pltpu.SemaphoreType.DMA((3,)),
         ],
-        limit=60,
+        limit=4,
     )
 
 
@@ -161,12 +161,15 @@
 
 def turn_kernel(gate, up, _, gate_t, up_t):
     tile = 128
-    for source, target in ((gate, gate_t), (up, up_t)):
-        for e in range(source.shape[0]):
-            for at in range(0, source.shape[2], tile):
-                target[e, at:at + tile] = source[e, :, at:at + tile].astype(jnp.float32).T.astype(
-                    jnp.bfloat16
-                )
+    for e in range(gate.shape[0]):
+        for at in range(0, gate.shape[2], tile):
+            gate_value = gate[e, :, at:at + tile].astype(jnp.float32)
+            up_value = up[e, :, at:at + tile].astype(jnp.float32)
+            sigmoid_gate = jax.nn.sigmoid(gate_value)
+            up_t[e, at:at + tile] = (gate_value * sigmoid_gate).T
+            gate_t[e, at:at + tile] = (
+                up_value * sigmoid_gate * (1.0 + gate_value * (1.0 - sigmoid_gate))
+            ).T
 
 
 def turn(saved_gate, saved_up, after):
@@ -174,10 +177,10 @@
     return small(
         turn_kernel,
         "turn",
-        [(count, slots, units)] * 2,
+        [jax.ShapeDtypeStruct((count, slots, units), jnp.float32)] * 2,
         "vvo",
         (saved_gate, saved_up, after),
-        limit=12,
+        limit=16,
     )
 
 
@@ -389,15 +392,8 @@
                 mine = slice(p * rows, (p + 1) * rows)
                 saved = pl.ds(pair_base(place, line_count, r, ry, rows), rows)
                 hidden_grad = total[mine]
-                gate_value = saved_gate[e, saved, :].astype(jnp.float32)
-                up_value = saved_up[e, saved, :].astype(jnp.float32)
-                sigmoid_gate = jax.nn.sigmoid(gate_value)
-                grads[e, mine, units:] = (hidden_grad * gate_value * sigmoid_gate).astype(
-                    jnp.bfloat16
-                )
-                grads[e, mine, :units] = (
-                    hidden_grad * up_value * sigmoid_gate * (1.0 + gate_value * (1.0 - sigmoid_gate))
-                ).astype(jnp.bfloat16)
+                grads[e, mine, units:] = (hidden_grad * saved_up[e, saved, :]).astype(jnp.bfloat16)
+                grads[e, mine, :units] = (hidden_grad * saved_gate[e, saved, :]).astype(jnp.bfloat16)
 
 
 def hidden(offsets, line_count, place, own, own_c, moved, pick, gate, w_down, saved, after):

time: 117 us -> 116 us (level)
  local copies, waits for them, and re-layouts: 2.92 us -> 6.98 us
  waiting for transfers between devices: 54.6 us -> 50.7 us
  Pallas kernels: 25.3 us -> 23.5 us
  starting transfers between devices: 33.2 us -> 34.4 us
    unnamed x20, local copies, waits for them, and re-layouts: 2.92 us -> 6.98 us
    ppermute x6, waiting for transfers between devices: 23.6 us -> 20.3 us  [along_line(): lax.ppermute(value, 'expert', [(i, (i + 4 * shift) % count) for i in rang...]
    pallas_call x24, Pallas kernels: 24.4 us -> 22.6 us  [small(): pl.pallas_call(kernel, out_shape=[out if hasattr(out, 'dtype') else jax.S...]
where the time goes in v12:
time: 116 us
  waiting for transfers between devices  50.7 us (44%)
  starting transfers between devices  34.4 us (30%)
  Pallas kernels  23.5 us (20%)
  local copies, waits for them, and re-layouts  6.98 us (6%)
    ppermute x31, waiting for transfers between devices, swap(): return lax.ppermute(value, axis, [(i, i ^ step) for i in range(count)])  30.3 us
    pallas_call x24, Pallas kernels, small(): pl.pallas_call(kernel, out_shape=[out if hasattr(out, 'dtype') else jax.S...  22.6 us
    ppermute x31, starting transfers between devices, swap(): return lax.ppermute(value, axis, [(i, i ^ step) for i in range(count)])  21.8 us
    ppermute x6, waiting for transfers between devices, along_line(): lax.ppermute(value, 'expert', [(i, (i + 4 * shift) % count) for i in rang...  20.3 us
    ppermute x6, starting transfers between devices, along_line(): lax.ppermute(value, 'expert', [(i, (i + 4 * shift) % count) for i in rang...  12.6 us
    unnamed x20, local copies, waits for them, and re-layouts  6.98 us
  transfers between devices with their start and end apart: 37, of which 19 were waited for; matrix products, arithmetic and copies ran while one was open for 0% of the time, Pallas kernels for 19%

profile of v12, /device:TPU:0, one launch (start us, length us, event | category | flops | bytes accessed | tf_op | source)
XLA Modules:
  0.0 115.9 jit_solution(560821115731265957)
XLA Ops:
  0.1 1.0 copy-done.3
  1.1 0.7 copy-done.8
  1.8 0.7 copy-done.9
  2.5 0.6 prepare.1
  3.1 4.1 %collective-permute-start.1 = (bf16[64,2176]{1,0:T(8,128)(2,1)S(1)}, bf16[64,2176]{1,0:T(8,128)(2,1)S(1)}, u32[]{:S(2)}, u32[]{:S(2)}) collective-permute-start(bf16[64,2176]{1,0:T(8,128)(2,1)S(1)} %get-tuple-element.50.part), channel_id=1, source_target_pairs={{0,16},{2,18},{4,20},{6,22},{8,24},{10,26},{12,28},{14,30},{16,0},... | collective-permute-start | bytes 835592 | tf_op jit(solution)/shard_map/ppermute | solution.py:71
  7.2 1.5 %collective-permute-start.5 = (bf16[64,2176]{1,0:T(8,128)(2,1)S(1)}, bf16[64,2176]{1,0:T(8,128)(2,1)S(1)}, u32[]{:S(2)}, u32[]{:S(2)}) collective-permute-start(bf16[64,2176]{1,0:T(8,128)(2,1)S(1)} %get-tuple-element.50.part), channel_id=1, source_target_pairs={{0,4},{2,6},{4,0},{6,2},{8,12},{10,14},{12,8},{14,10},{16,20},{18,... | collective-permute-start | bytes 835592 | tf_op jit(solution)/shard_map/ppermute | solution.py:66
  8.7 11.1 %collective-permute-done.1.came = bf16[64,2176]{1,0:T(8,128)(2,1)S(1)} collective-permute-done((bf16[64,2176]{1,0:T(8,128)(2,1)S(1)}, bf16[64,2176]{1,0:T(8,128)(2,1)S(1)}, u32[]{:S(2)}, u32[]{:S(2)}) %collective-permute-start.1) | collective-permute-done | bytes 278560 | tf_op jit(solution)/shard_map/ppermute | solution.py:71
  19.9 1.6 %collective-permute-start.3 = (bf16[1,64,2176]{2,1,0:T(8,128)(2,1)S(1)}, bf16[1,64,2176]{2,1,0:T(8,128)(2,1)S(1)}, u32[]{:S(2)}, u32[]{:S(2)}) collective-permute-start(bf16[1,64,2176]{2,1,0:T(8,128)(2,1)S(1)} %get-tuple-element.51.lines._), channel_id=1, source_target_pairs={{0,1},{1,0},{2,3},{3,2},{4,5},{5,4},{6,7},{7,6},{8,9},{9,8},{10,11... | collective-permute-start | bytes 835592 | tf_op jit(solution)/shard_map/ppermute | solution.py:66
  21.5 1.5 %collective-permute-start.6 = (bf16[1,64,2176]{2,1,0:T(8,128)(2,1)S(1)}, bf16[1,64,2176]{2,1,0:T(8,128)(2,1)S(1)}, u32[]{:S(2)}, u32[]{:S(2)}) collective-permute-start(bf16[1,64,2176]{2,1,0:T(8,128)(2,1)S(1)} %get-tuple-element.51.lines._), channel_id=1, source_target_pairs={{0,4},{2,6},{4,0},{6,2},{8,12},{10,14},{12,8},{14,10},{16,20},{18,... | collective-permute-start | bytes 835592 | tf_op jit(solution)/shard_map/ppermute | solution.py:66
  23.0 3.5 %collective-permute-start.12 = (bf16[64,2176]{1,0:T(8,128)(2,1)S(1)}, bf16[64,2176]{1,0:T(8,128)(2,1)S(1)}, u32[]{:S(2)}, u32[]{:S(2)}) collective-permute-start(bf16[64,2176]{1,0:T(8,128)(2,1)S(1)} %get-tuple-element.60), channel_id=1, source_target_pairs={{0,24},{2,26},{4,28},{6,30},{8,0},{10,2},{12,4},{14,6},{16,8},{18,... | collective-permute-start | bytes 835592 | tf_op jit(solution)/shard_map/ppermute | solution.py:71
  26.5 1.3 %collective-permute-done.3.side = bf16[1,64,2176]{2,1,0:T(8,128)(2,1)S(1)} collective-permute-done((bf16[1,64,2176]{2,1,0:T(8,128)(2,1)S(1)}, bf16[1,64,2176]{2,1,0:T(8,128)(2,1)S(1)}, u32[]{:S(2)}, u32[]{:S(2)}) %collective-permute-start.3) | collective-permute-done | bytes 278560 | tf_op jit(solution)/shard_map/ppermute | solution.py:66
  27.8 1.0 collective-permute-done.6.over
  28.8 1.0 copy-done.4
  29.8 0.6 own_corner.1
  30.5 0.8 collective-permute-start.8
  31.3 1.3 %collective-permute-start.9 = (bf16[2,64,1024]{2,1,0:T(8,128)(2,1)S(1)}, bf16[2,64,1024]{2,1,0:T(8,128)(2,1)S(1)}, u32[]{:S(2)}, u32[]{:S(2)}) collective-permute-start(bf16[2,64,1024]{2,1,0:T(8,128)(2,1)S(1)} %get-tuple-element.54), channel_id=1, source_target_pairs={{0,4},{2,6},{4,0},{6,2},{8,12},{10,14},{12,8},{14,10},{16,20},{18,... | collective-permute-start | bytes 786440 | tf_op jit(solution)/shard_map/ppermute | solution.py:66
  32.6 1.3 %copy-done.6 = bf16[2,384,768]{2,1,0:T(8,128)(2,1)S(1)} copy-done((bf16[2,384,768]{2,1,0:T(8,128)(2,1)S(1)}, bf16[2,384,768]{2,1,0:T(8,128)(2,1)}, u32[]{:S(2)}) %copy-start.6) | copy-done | bytes 1179672
  33.8 1.3 %copy-done.7 = bf16[2,384,768]{2,1,0:T(8,128)(2,1)S(1)} copy-done((bf16[2,384,768]{2,1,0:T(8,128)(2,1)S(1)}, bf16[2,384,768]{2,1,0:T(8,128)(2,1)}, u32[]{:S(2)}) %copy-start.7) | copy-done | bytes 1179672
  35.1 1.3 %turn.1 = (f32[2,768,384]{2,1,0:T(8,128)S(1)}, f32[2,768,384]{2,1,0:T(8,128)S(1)}) custom-call(bf16[2,384,768]{2,1,0:T(8,128)(2,1)S(1)} %copy-done.6, bf16[2,384,768]{2,1,0:T(8,128)(2,1)S(1)} %copy-done.7, bf16[1,64,2176]{2,1,0:T(8,128)(2,1)S(1)} %get-tuple-element.51.lines._), custom_call_target="tpu_custom_call" | custom-call | tf_op jit(solution)/shard_map/turn/pallas_call | solution.py:76
  36.4 0.6 collective-permute-start.2
  37.0 1.8 %collective-permute-done.13.refs_1_ = bf16[64,2176]{1,0:T(8,128)(2,1)S(1)} collective-permute-done((bf16[64,2176]{1,0:T(8,128)(2,1)S(1)}, bf16[64,2176]{1,0:T(8,128)(2,1)S(1)}, u32[]{:S(2)}, u32[]{:S(2)}) %collective-permute-start.13) | collective-permute-done | bytes 278560 | tf_op jit(solution)/shard_map/ppermute | solution.py:71
  38.8 0.6 collective-permute-start.15
  39.4 0.5 collective-permute-start.16
  40.0 1.0 copy-done.5
  41.0 0.5 collective-permute-start.10
  41.5 0.4 collective-permute-done.7.over_c
  42.0 1.1 route.2
  43.1 0.9 collective-permute-done.4.side_c
  44.0 3.9 %hidden.2.grads._ = bf16[2,384,768]{2,1,0:T(8,128)(2,1)S(1)} custom-call(s32[4]{0:T(128)S(1)} %pad_add_fusion.place, bf16[128,2048]{1,0:T(8,128)(2,1)S(1)} %copy-done.5, bf16[128,2048]{1,0:T(8,128)(2,1)S(1)} %collective-permute-done.own_c, bf16[1,64,2176]{2,1,0:T(8,128)(2,1)S(1)} %get-tuple-element.51.lines._, ...), custom_call_target="tpu_custom_call" | custom-call | tf_op jit(solution)/shard_map/hidden/pallas_call | solution.py:76
  47.9 2.2 %sums.4 = (bf16[4,128,1024]{2,1,0:T(8,128)(2,1)S(1)}, bf16[4,128,1024]{2,1,0:T(8,128)(2,1)S(1)}) custom-call(bf16[2,384,768]{2,1,0:T(8,128)(2,1)S(1)} %hidden.2.grads._, bf16[2,384,2048]{2,1,0:T(8,128)(2,1)S(1)} %copy-done, bf16[2,384,2048]{2,1,0:T(8,128)(2,1)S(1)} %copy-done.1, bf16[4,256,192]{2,1,0:T(8,128)(2,1)S(1)} %get-tuple-element.61.pick_t, ...), custom_call_target="tpu_custom_call" | custom-call | tf_op jit(solution)/shard_map/sums/pallas_call | solution.py:76
  50.4 1.8 %collective-permute-done.15.over = bf16[2,64,2176]{2,1,0:T(8,128)(2,1)S(1)} collective-permute-done((bf16[2,64,2176]{2,1,0:T(8,128)(2,1)S(1)}, bf16[2,64,2176]{2,1,0:T(8,128)(2,1)S(1)}, u32[]{:S(2)}, u32[]{:S(2)}) %collective-permute-start.15) | collective-permute-done | bytes 557088 | tf_op jit(solution)/shard_map/ppermute | solution.py:66
  52.2 0.2 collective-permute-done.16.side
  52.5 1.0 collective-permute-start.17
  53.5 1.5 %collective-permute-start.18 = (bf16[2,64,1024]{2,1,0:T(8,128)(2,1)S(1)}, bf16[2,64,1024]{2,1,0:T(8,128)(2,1)S(1)}, u32[]{:S(2)}, u32[]{:S(2)}) collective-permute-start(bf16[2,64,1024]{2,1,0:T(8,128)(2,1)S(1)} %get-tuple-element.65), channel_id=1, source_target_pairs={{0,4},{2,6},{4,0},{6,2},{8,12},{10,14},{12,8},{14,10},{16,20},{18,... | collective-permute-start | bytes 786440 | tf_op jit(solution)/shard_map/ppermute | solution.py:66
  55.0 2.2 %sums.5 = (bf16[4,128,1024]{2,1,0:T(8,128)(2,1)S(1)}, bf16[4,128,1024]{2,1,0:T(8,128)(2,1)S(1)}) custom-call(bf16[2,384,768]{2,1,0:T(8,128)(2,1)S(1)} %hidden.2.grads._, bf16[2,384,2048]{2,1,0:T(8,128)(2,1)S(1)} %copy-done, bf16[2,384,2048]{2,1,0:T(8,128)(2,1)S(1)} %copy-done.1, bf16[4,256,192]{2,1,0:T(8,128)(2,1)S(1)} %get-tuple-element.61.pick_t, ...), custom_call_target="tpu_custom_call" | custom-call | flops 68719476736 | bytes 268435456 | tf_op jit(solution)/shard_map/sums/pallas_call | solution.py:76
  57.3 0.5 collective-permute-start.25
  57.8 1.3 %collective-permute-done.17.left = bf16[2,64,1024]{2,1,0:T(8,128)(2,1)S(1)} collective-permute-done((bf16[2,64,1024]{2,1,0:T(8,128)(2,1)S(1)}, bf16[2,64,1024]{2,1,0:T(8,128)(2,1)S(1)}, u32[]{:S(2)}, u32[]{:S(2)}) %collective-permute-start.17) | collective-permute-done | bytes 262176 | tf_op jit(solution)/shard_map/ppermute | solution.py:66
  59.1 1.2 %collective-permute-done.18.right = bf16[2,64,1024]{2,1,0:T(8,128)(2,1)S(1)} collective-permute-done((bf16[2,64,1024]{2,1,0:T(8,128)(2,1)S(1)}, bf16[2,64,1024]{2,1,0:T(8,128)(2,1)S(1)}, u32[]{:S(2)}, u32[]{:S(2)}) %collective-permute-start.18) | collective-permute-done | bytes 262176 | tf_op jit(solution)/shard_map/ppermute | solution.py:66
  60.4 0.6 collective-permute-start.28
  61.1 0.7 collective-permute-start.19
  61.9 1.6 %collective-permute-start.21 = (bf16[2,128,1024]{2,1,0:T(8,128)(2,1)S(1)}, bf16[2,128,1024]{2,1,0:T(8,128)(2,1)S(1)}, u32[]{:S(2)}, u32[]{:S(2)}) collective-permute-start(bf16[2,128,1024]{2,1,0:T(8,128)(2,1)S(1)} %get-tuple-element.71._), channel_id=1, source_target_pairs={{0,4},{2,6},{4,0},{6,2},{8,12},{10,14},{12,8},{14,10},{16,20},{18,... | collective-permute-start | bytes 1572872 | tf_op jit(solution)/shard_map/ppermute | solution.py:66
  63.5 1.1 route.3
  64.7 3.9 %hidden.3.grads._ = bf16[2,384,768]{2,1,0:T(8,128)(2,1)S(1)} custom-call(s32[4]{0:T(128)S(1)} %pad_add_fusion.place, bf16[128,2048]{1,0:T(8,128)(2,1)S(1)} %copy-done.5, bf16[128,2048]{1,0:T(8,128)(2,1)S(1)} %collective-permute-done.own_c, bf16[2,64,2176]{2,1,0:T(8,128)(2,1)S(1)} %stack.21._.lines, bf16[2,64,2176]{2,1,0:T(8,128)(2,1)S(1)} %collective-permute-done.25.lines_c, ...), custom_call_target="tpu_custom_call" | custom-call | tf_op jit(solution)/shard_map/hidden/pallas_call | solution.py:76
  68.5 2.2 %sums.6 = (bf16[4,128,1024]{2,1,0:T(8,128)(2,1)S(1)}, bf16[4,128,1024]{2,1,0:T(8,128)(2,1)S(1)}) custom-call(bf16[2,384,768]{2,1,0:T(8,128)(2,1)S(1)} %hidden.3.grads._, bf16[2,384,2048]{2,1,0:T(8,128)(2,1)S(1)} %copy-done, bf16[2,384,2048]{2,1,0:T(8,128)(2,1)S(1)} %copy-done.1, bf16[4,256,192]{2,1,0:T(8,128)(2,1)S(1)} %get-tuple-element.80.pick_t, ...), custom_call_target="tpu_custom_call" | custom-call | tf_op jit(solution)/shard_map/sums/pallas_call | solution.py:76
  70.9 2.2 %sums.7 = (bf16[4,128,1024]{2,1,0:T(8,128)(2,1)S(1)}, bf16[4,128,1024]{2,1,0:T(8,128)(2,1)S(1)}) custom-call(bf16[2,384,768]{2,1,0:T(8,128)(2,1)S(1)} %hidden.3.grads._, bf16[2,384,2048]{2,1,0:T(8,128)(2,1)S(1)} %copy-done, bf16[2,384,2048]{2,1,0:T(8,128)(2,1)S(1)} %copy-done.1, bf16[4,256,192]{2,1,0:T(8,128)(2,1)S(1)} %get-tuple-element.80.pick_t, ...), custom_call_target="tpu_custom_call" | custom-call | tf_op jit(solution)/shard_map/sums/pallas_call | solution.py:76
  73.1 0.6 collective-permute-start.31
  73.7 1.3 %collective-permute-done.19.came_l = bf16[4,64,1024]{2,1,0:T(8,128)(2,1)S(1)} collective-permute-done((bf16[4,64,1024]{2,1,0:T(8,128)(2,1)S(1)}, bf16[4,64,1024]{2,1,0:T(8,128)(2,1)S(1)}, u32[]{:S(2)}, u32[]{:S(2)}) %collective-permute-start.19) | collective-permute-done | bytes 524320 | tf_op jit(solution)/shard_map/ppermute | solution.py:66
  75.0 0.7 collective-permute-done.21.came_r
  75.8 1.6 %collective-permute-start.22 = (bf16[2,64,1024]{2,1,0:T(8,128)(2,1)S(1)}, bf16[2,64,1024]{2,1,0:T(8,128)(2,1)S(1)}, u32[]{:S(2)}, u32[]{:S(2)}) collective-permute-start(bf16[2,64,1024]{2,1,0:T(8,128)(2,1)S(1)} %get-tuple-element.73._), channel_id=1, source_target_pairs={{0,4},{2,6},{4,0},{6,2},{8,12},{10,14},{12,8},{14,10},{16,20},{18,... | collective-permute-start | bytes 786440 | tf_op jit(solution)/shard_map/ppermute | solution.py:66
  77.4 1.3 %collective-permute-start.23 = (bf16[2,64,1024]{2,1,0:T(8,128)(2,1)S(1)}, bf16[2,64,1024]{2,1,0:T(8,128)(2,1)S(1)}, u32[]{:S(2)}, u32[]{:S(2)}) collective-permute-start(bf16[2,64,1024]{2,1,0:T(8,128)(2,1)S(1)} %get-tuple-element.75), channel_id=1, source_target_pairs={{0,1},{1,0},{2,3},{3,2},{4,5},{5,4},{6,7},{7,6},{8,9},{9,8},{10,11... | collective-permute-start | bytes 786440 | tf_op jit(solution)/shard_map/ppermute | solution.py:66
  78.8 0.8 collective-permute-start.30
  79.7 0.6 collective-permute-start.32
  80.3 4.8 %collective-permute-done.22.came_l = bf16[2,64,1024]{2,1,0:T(8,128)(2,1)S(1)} collective-permute-done((bf16[2,64,1024]{2,1,0:T(8,128)(2,1)S(1)}, bf16[2,64,1024]{2,1,0:T(8,128)(2,1)S(1)}, u32[]{:S(2)}, u32[]{:S(2)}) %collective-permute-start.22) | collective-permute-done | bytes 262176 | tf_op jit(solution)/shard_map/ppermute | solution.py:66
  85.1 1.5 %collective-permute-done.23.came_r = bf16[2,64,1024]{2,1,0:T(8,128)(2,1)S(1)} collective-permute-done((bf16[2,64,1024]{2,1,0:T(8,128)(2,1)S(1)}, bf16[2,64,1024]{2,1,0:T(8,128)(2,1)S(1)}, u32[]{:S(2)}, u32[]{:S(2)}) %collective-permute-start.23) | collective-permute-done | bytes 262176 | tf_op jit(solution)/shard_map/ppermute | solution.py:66
  86.9 8.6 %collective-permute-done.30.came_l = bf16[4,64,1024]{2,1,0:T(8,128)(2,1)S(1)} collective-permute-done((bf16[4,64,1024]{2,1,0:T(8,128)(2,1)S(1)}, bf16[4,64,1024]{2,1,0:T(8,128)(2,1)S(1)}, u32[]{:S(2)}, u32[]{:S(2)}) %collective-permute-start.30) | collective-permute-done | bytes 524320 | tf_op jit(solution)/shard_map/ppermute | solution.py:66
  95.7 0.6 collective-permute-start.33
  96.3 1.1 collective-permute-start.34
  97.4 4.7 %collective-permute-done.33.came_l = bf16[2,64,1024]{2,1,0:T(8,128)(2,1)S(1)} collective-permute-done((bf16[2,64,1024]{2,1,0:T(8,128)(2,1)S(1)}, bf16[2,64,1024]{2,1,0:T(8,128)(2,1)S(1)}, u32[]{:S(2)}, u32[]{:S(2)}) %collective-permute-start.33) | collective-permute-done | bytes 262176 | tf_op jit(solution)/shard_map/ppermute | solution.py:66
  102.1 0.5 collective-permute-done.34.came_r
  102.8 1.9 %collective-permute-start.35 = (bf16[64,2048]{1,0:T(8,128)(2,1)S(1)}, bf16[64,2048]{1,0:T(8,128)(2,1)S(1)}, u32[]{:S(2)}, u32[]{:S(2)}) collective-permute-start(bf16[64,2048]{1,0:T(8,128)(2,1)S(1)} %get-tuple-element.93), channel_id=1, source_target_pairs={{0,8},{2,10},{4,12},{6,14},{8,16},{10,18},{12,20},{14,22},{16,24},... | collective-permute-start | bytes 786440 | tf_op jit(solution)/shard_map/ppermute | solution.py:71
  104.7 2.9 %collective-permute-start.36 = (bf16[64,2048]{1,0:T(8,128)(2,1)S(1)}, bf16[64,2048]{1,0:T(8,128)(2,1)S(1)}, u32[]{:S(2)}, u32[]{:S(2)}) collective-permute-start(bf16[64,2048]{1,0:T(8,128)(2,1)S(1)} %get-tuple-element.94), channel_id=1, source_target_pairs={{0,24},{2,26},{4,28},{6,30},{8,0},{10,2},{12,4},{14,6},{16,8},{18,... | collective-permute-start | bytes 786440 | tf_op jit(solution)/shard_map/ppermute | solution.py:71
  107.6 6.2 %collective-permute-done.35.refs_2_ = bf16[64,2048]{1,0:T(8,128)(2,1)S(1)} collective-permute-done((bf16[64,2048]{1,0:T(8,128)(2,1)S(1)}, bf16[64,2048]{1,0:T(8,128)(2,1)S(1)}, u32[]{:S(2)}, u32[]{:S(2)}) %collective-permute-start.35) | collective-permute-done | bytes 262176 | tf_op jit(solution)/shard_map/ppermute | solution.py:71
  113.8 1.2 %collective-permute-done.36.refs_3_ = bf16[64,2048]{1,0:T(8,128)(2,1)S(1)} collective-permute-done((bf16[64,2048]{1,0:T(8,128)(2,1)S(1)}, bf16[64,2048]{1,0:T(8,128)(2,1)S(1)}, u32[]{:S(2)}, u32[]{:S(2)}) %collective-permute-start.36) | collective-permute-done | bytes 262176 | tf_op jit(solution)/shard_map/ppermute | solution.py:71
  115.0 0.9 last_sum.1
  (56 shorter events, 2.0 us)
Async XLA Ops:
  0.1 1.0 copy-start.3
  1.1 0.7 copy-start.8
  1.8 0.7 copy-start.9
  3.1 16.7 %collective-permute-start.1 = (bf16[64,2176]{1,0:T(8,128)(2,1)S(1)}, bf16[64,2176]{1,0:T(8,128)(2,1)S(1)}, u32[]{:S(2)}, u32[]{:S(2)}) collective-permute-start(bf16[64,2176]{1,0:T(8,128)(2,1)S(1)} %get-tuple-element.50.part), channel_id=1, source_target_pairs={{0,16},{2,18},{4,20},{6,22},{8,24},{10,26},{12,28},{14,30},{16,0},... | collective-permute-start | bytes 835592 | tf_op jit(solution)/shard_map/ppermute | solution.py:71
  7.2 19.3 %collective-permute-start.5 = (bf16[64,2176]{1,0:T(8,128)(2,1)S(1)}, bf16[64,2176]{1,0:T(8,128)(2,1)S(1)}, u32[]{:S(2)}, u32[]{:S(2)}) collective-permute-start(bf16[64,2176]{1,0:T(8,128)(2,1)S(1)} %get-tuple-element.50.part), channel_id=1, source_target_pairs={{0,4},{2,6},{4,0},{6,2},{8,12},{10,14},{12,8},{14,10},{16,20},{18,... | collective-permute-start | bytes 835592 | tf_op jit(solution)/shard_map/ppermute | solution.py:66
  19.9 7.9 %collective-permute-start.3 = (bf16[1,64,2176]{2,1,0:T(8,128)(2,1)S(1)}, bf16[1,64,2176]{2,1,0:T(8,128)(2,1)S(1)}, u32[]{:S(2)}, u32[]{:S(2)}) collective-permute-start(bf16[1,64,2176]{2,1,0:T(8,128)(2,1)S(1)} %get-tuple-element.51.lines._), channel_id=1, source_target_pairs={{0,1},{1,0},{2,3},{3,2},{4,5},{5,4},{6,7},{7,6},{8,9},{9,8},{10,11... | collective-permute-start | bytes 835592 | tf_op jit(solution)/shard_map/ppermute | solution.py:66
  21.5 7.3 %collective-permute-start.6 = (bf16[1,64,2176]{2,1,0:T(8,128)(2,1)S(1)}, bf16[1,64,2176]{2,1,0:T(8,128)(2,1)S(1)}, u32[]{:S(2)}, u32[]{:S(2)}) collective-permute-start(bf16[1,64,2176]{2,1,0:T(8,128)(2,1)S(1)} %get-tuple-element.51.lines._), channel_id=1, source_target_pairs={{0,4},{2,6},{4,0},{6,2},{8,12},{10,14},{12,8},{14,10},{16,20},{18,... | collective-permute-start | bytes 835592 | tf_op jit(solution)/shard_map/ppermute | solution.py:66
  23.0 13.4 %collective-permute-start.12 = (bf16[64,2176]{1,0:T(8,128)(2,1)S(1)}, bf16[64,2176]{1,0:T(8,128)(2,1)S(1)}, u32[]{:S(2)}, u32[]{:S(2)}) collective-permute-start(bf16[64,2176]{1,0:T(8,128)(2,1)S(1)} %get-tuple-element.60), channel_id=1, source_target_pairs={{0,24},{2,26},{4,28},{6,30},{8,0},{10,2},{12,4},{14,6},{16,8},{18,... | collective-permute-start | bytes 835592 | tf_op jit(solution)/shard_map/ppermute | solution.py:71
  26.5 12.2 %collective-permute-start.13 = (bf16[64,2176]{1,0:T(8,128)(2,1)S(1)}, bf16[64,2176]{1,0:T(8,128)(2,1)S(1)}, u32[]{:S(2)}, u32[]{:S(2)}) collective-permute-start(bf16[64,2176]{1,0:T(8,128)(2,1)S(1)} %get-tuple-element.60), channel_id=1, source_target_pairs={{0,8},{2,10},{4,12},{6,14},{8,16},{10,18},{12,20},{14,22},{16,24},... | collective-permute-start | bytes 835592 | tf_op jit(solution)/shard_map/ppermute | solution.py:71
  28.8 1.0 copy-start.4
  30.5 8.9 %collective-permute-start.8 = (bf16[2,64,1024]{2,1,0:T(8,128)(2,1)S(1)}, bf16[2,64,1024]{2,1,0:T(8,128)(2,1)S(1)}, u32[]{:S(2)}, u32[]{:S(2)}) collective-permute-start(bf16[2,64,1024]{2,1,0:T(8,128)(2,1)S(1)} %get-tuple-element.53.refs_0_), channel_id=1, source_target_pairs={{0,1},{1,0},{2,3},{3,2},{4,5},{5,4},{6,7},{7,6},{8,9},{9,8},{10,11... | collective-permute-start | bytes 786440 | tf_op jit(solution)/shard_map/ppermute | solution.py:66
  31.3 8.6 %collective-permute-start.9 = (bf16[2,64,1024]{2,1,0:T(8,128)(2,1)S(1)}, bf16[2,64,1024]{2,1,0:T(8,128)(2,1)S(1)}, u32[]{:S(2)}, u32[]{:S(2)}) collective-permute-start(bf16[2,64,1024]{2,1,0:T(8,128)(2,1)S(1)} %get-tuple-element.54), channel_id=1, source_target_pairs={{0,4},{2,6},{4,0},{6,2},{8,12},{10,14},{12,8},{14,10},{16,20},{18,... | collective-permute-start | bytes 786440 | tf_op jit(solution)/shard_map/ppermute | solution.py:66
  32.6 7.4 %collective-permute-start.11 = (bf16[64,128]{1,0:T(8,128)(2,1)S(1)}, bf16[64,128]{1,0:T(8,128)(2,1)S(1)}, u32[]{:S(2)}, u32[]{:S(2)}) collective-permute-start(bf16[64,128]{1,0:T(8,128)(2,1)S(1)} %get-tuple-element.55.own), channel_id=1, source_target_pairs={{0,2},{2,0},{4,6},{6,4},{8,10},{10,8},{12,14},{14,12},{16,18},{18,... | collective-permute-start | bytes 49160 | tf_op jit(solution)/shard_map/ppermute | solution.py:66
  32.6 1.3 %copy-start.6 = (bf16[2,384,768]{2,1,0:T(8,128)(2,1)S(1)}, bf16[2,384,768]{2,1,0:T(8,128)(2,1)}, u32[]{:S(2)}) copy-start(bf16[2,384,768]{2,1,0:T(8,128)(2,1)} %gate.1) | copy-start | bytes 3538948
  33.8 1.3 %copy-start.7 = (bf16[2,384,768]{2,1,0:T(8,128)(2,1)S(1)}, bf16[2,384,768]{2,1,0:T(8,128)(2,1)}, u32[]{:S(2)}) copy-start(bf16[2,384,768]{2,1,0:T(8,128)(2,1)} %up.1) | copy-start | bytes 3538948
  36.4 4.5 %collective-permute-start.2 = (bf16[1,64,2176]{2,1,0:T(8,128)(2,1)S(1)}, bf16[1,64,2176]{2,1,0:T(8,128)(2,1)S(1)}, u32[]{:S(2)}, u32[]{:S(2)}) collective-permute-start(bf16[1,64,2176]{2,1,0:T(8,128)(2,1)S(1)} %get-tuple-element.51.lines._), channel_id=1, source_target_pairs={{0,2},{2,0},{4,6},{6,4},{8,10},{10,8},{12,14},{14,12},{16,18},{18,... | collective-permute-start | bytes 835592 | tf_op jit(solution)/shard_map/ppermute | solution.py:66
  38.8 13.4 %collective-permute-start.15 = (bf16[2,64,2176]{2,1,0:T(8,128)(2,1)S(1)}, bf16[2,64,2176]{2,1,0:T(8,128)(2,1)S(1)}, u32[]{:S(2)}, u32[]{:S(2)}) collective-permute-start(bf16[2,64,2176]{2,1,0:T(8,128)(2,1)S(1)} %stack.21._.lines), channel_id=1, source_target_pairs={{0,4},{2,6},{4,0},{6,2},{8,12},{10,14},{12,8},{14,10},{16,20},{18,... | collective-permute-start | bytes 1671176 | tf_op jit(solution)/shard_map/ppermute | solution.py:66
  39.4 13.1 %collective-permute-start.16 = (bf16[2,64,2176]{2,1,0:T(8,128)(2,1)S(1)}, bf16[2,64,2176]{2,1,0:T(8,128)(2,1)S(1)}, u32[]{:S(2)}, u32[]{:S(2)}) collective-permute-start(bf16[2,64,2176]{2,1,0:T(8,128)(2,1)S(1)} %stack.21._.lines), channel_id=1, source_target_pairs={{0,1},{1,0},{2,3},{3,2},{4,5},{5,4},{6,7},{7,6},{8,9},{9,8},{10,11... | collective-permute-start | bytes 1671176 | tf_op jit(solution)/shard_map/ppermute | solution.py:66
  39.9 1.0 copy-start.5
  39.9 2.0 %collective-permute-start.7 = (bf16[2,64,2176]{2,1,0:T(8,128)(2,1)S(1)}, bf16[2,64,2176]{2,1,0:T(8,128)(2,1)S(1)}, u32[]{:S(2)}, u32[]{:S(2)}) collective-permute-start(bf16[2,64,2176]{2,1,0:T(8,128)(2,1)S(1)} %get-tuple-element.52.over), channel_id=1, source_target_pairs={{0,2},{2,0},{4,6},{6,4},{8,10},{10,8},{12,14},{14,12},{16,18},{18,... | collective-permute-start | bytes 1671176 | tf_op jit(solution)/shard_map/ppermute | solution.py:66
  39.9 4.1 %copy-start.2 = (bf16[2,384,2048]{2,1,0:T(8,128)(2,1)S(1)}, bf16[2,384,2048]{2,1,0:T(8,128)(2,1)}, u32[]{:S(2)}) copy-start(bf16[2,384,2048]{2,1,0:T(8,128)(2,1)} %w_down.3) | copy-start | bytes 9437188
  40.9 2.2 %collective-permute-start = (bf16[128,2048]{1,0:T(8,128)(2,1)S(1)}, bf16[128,2048]{1,0:T(8,128)(2,1)S(1)}, u32[]{:S(2)}, u32[]{:S(2)}) collective-permute-start(bf16[128,2048]{1,0:T(8,128)(2,1)S(1)} %copy-done.5), channel_id=1, source_target_pairs={{0,2},{2,0},{4,6},{6,4},{8,10},{10,8},{12,14},{14,12},{16,18},{18,... | collective-permute-start | bytes 1572872 | tf_op jit(solution)/shard_map/ppermute | solution.py:66
  41.0 3.1 %collective-permute-start.10 = (bf16[2,64,2048]{2,1,0:T(8,128)(2,1)S(1)}, bf16[2,64,2048]{2,1,0:T(8,128)(2,1)S(1)}, u32[]{:S(2)}, u32[]{:S(2)}) collective-permute-start(bf16[2,64,2048]{2,1,0:T(8,128)(2,1)S(1)} %join.2.diag), channel_id=1, source_target_pairs={{0,2},{2,0},{4,6},{6,4},{8,10},{10,8},{12,14},{14,12},{16,18},{18,... | collective-permute-start | bytes 1572872 | tf_op jit(solution)/shard_map/ppermute | solution.py:66
  41.9 2.1 %collective-permute-start.4 = (bf16[1,64,2176]{2,1,0:T(8,128)(2,1)S(1)}, bf16[1,64,2176]{2,1,0:T(8,128)(2,1)S(1)}, u32[]{:S(2)}, u32[]{:S(2)}) collective-permute-start(bf16[1,64,2176]{2,1,0:T(8,128)(2,1)S(1)} %collective-permute-done.3.side), channel_id=1, source_target_pairs={{0,2},{2,0},{4,6},{6,4},{8,10},{10,8},{12,14},{14,12},{16,18},{18,... | collective-permute-start | bytes 835592 | tf_op jit(solution)/shard_map/ppermute | solution.py:66
  44.0 3.9 %copy-start = (bf16[2,384,2048]{2,1,0:T(8,128)(2,1)S(1)}, bf16[2,384,2048]{2,1,0:T(8,128)(2,1)}, u32[]{:S(2)}) copy-start(bf16[2,384,2048]{2,1,0:T(8,128)(2,1)} %w_gate.7) | copy-start | bytes 9437188
  44.0 3.9 %copy-start.1 = (bf16[2,384,2048]{2,1,0:T(8,128)(2,1)S(1)}, bf16[2,384,2048]{2,1,0:T(8,128)(2,1)}, u32[]{:S(2)}) copy-start(bf16[2,384,2048]{2,1,0:T(8,128)(2,1)} %w_up.7) | copy-start | bytes 9437188
  50.2 10.2 %collective-permute-start.14 = (bf16[4,128,1024]{2,1,0:T(8,128)(2,1)S(1)}, bf16[4,128,1024]{2,1,0:T(8,128)(2,1)S(1)}, u32[]{:S(2)}, u32[]{:S(2)}) collective-permute-start(bf16[4,128,1024]{2,1,0:T(8,128)(2,1)S(1)} %get-tuple-element.63._), channel_id=1, source_target_pairs={{0,2},{2,0},{4,6},{6,4},{8,10},{10,8},{12,14},{14,12},{16,18},{18,... | collective-permute-start | bytes 3145736 | tf_op jit(solution)/shard_map/ppermute | solution.py:66
  52.5 6.6 %collective-permute-start.17 = (bf16[2,64,1024]{2,1,0:T(8,128)(2,1)S(1)}, bf16[2,64,1024]{2,1,0:T(8,128)(2,1)S(1)}, u32[]{:S(2)}, u32[]{:S(2)}) collective-permute-start(bf16[2,64,1024]{2,1,0:T(8,128)(2,1)S(1)} %get-tuple-element.64._), channel_id=1, source_target_pairs={{0,1},{1,0},{2,3},{3,2},{4,5},{5,4},{6,7},{7,6},{8,9},{9,8},{10,11... | collective-permute-start | bytes 786440 | tf_op jit(solution)/shard_map/ppermute | solution.py:66
  53.5 6.8 %collective-permute-start.18 = (bf16[2,64,1024]{2,1,0:T(8,128)(2,1)S(1)}, bf16[2,64,1024]{2,1,0:T(8,128)(2,1)S(1)}, u32[]{:S(2)}, u32[]{:S(2)}) collective-permute-start(bf16[2,64,1024]{2,1,0:T(8,128)(2,1)S(1)} %get-tuple-element.65), channel_id=1, source_target_pairs={{0,4},{2,6},{4,0},{6,2},{8,12},{10,14},{12,8},{14,10},{16,20},{18,... | collective-permute-start | bytes 786440 | tf_op jit(solution)/shard_map/ppermute | solution.py:66
  57.3 3.8 %collective-permute-start.20 = (bf16[4,128,1024]{2,1,0:T(8,128)(2,1)S(1)}, bf16[4,128,1024]{2,1,0:T(8,128)(2,1)S(1)}, u32[]{:S(2)}, u32[]{:S(2)}) collective-permute-start(bf16[4,128,1024]{2,1,0:T(8,128)(2,1)S(1)} %get-tuple-element.66.refs_0_), channel_id=1, source_target_pairs={{0,2},{2,0},{4,6},{6,4},{8,10},{10,8},{12,14},{14,12},{16,18},{18,... | collective-permute-start | bytes 3145736 | tf_op jit(solution)/shard_map/ppermute | solution.py:66
  57.3 4.6 %collective-permute-start.25 = (bf16[2,64,2176]{2,1,0:T(8,128)(2,1)S(1)}, bf16[2,64,2176]{2,1,0:T(8,128)(2,1)S(1)}, u32[]{:S(2)}, u32[]{:S(2)}) collective-permute-start(bf16[2,64,2176]{2,1,0:T(8,128)(2,1)S(1)} %stack.21._.lines), channel_id=1, source_target_pairs={{0,2},{2,0},{4,6},{6,4},{8,10},{10,8},{12,14},{14,12},{16,18},{18,... | collective-permute-start | bytes 1671176 | tf_op jit(solution)/shard_map/ppermute | solution.py:66
  59.1 5.6 %collective-permute-start.26 = (bf16[2,64,2176]{2,1,0:T(8,128)(2,1)S(1)}, bf16[2,64,2176]{2,1,0:T(8,128)(2,1)S(1)}, u32[]{:S(2)}, u32[]{:S(2)}) collective-permute-start(bf16[2,64,2176]{2,1,0:T(8,128)(2,1)S(1)} %collective-permute-done.16.side), channel_id=1, source_target_pairs={{0,2},{2,0},{4,6},{6,4},{8,10},{10,8},{12,14},{14,12},{16,18},{18,... | collective-permute-start | bytes 1671176 | tf_op jit(solution)/shard_map/ppermute | solution.py:66
  60.3 3.2 %collective-permute-start.27 = (bf16[2,64,2176]{2,1,0:T(8,128)(2,1)S(1)}, bf16[2,64,2176]{2,1,0:T(8,128)(2,1)S(1)}, u32[]{:S(2)}, u32[]{:S(2)}) collective-permute-start(bf16[2,64,2176]{2,1,0:T(8,128)(2,1)S(1)} %collective-permute-done.15.over), channel_id=1, source_target_pairs={{0,2},{2,0},{4,6},{6,4},{8,10},{10,8},{12,14},{14,12},{16,18},{18,... | collective-permute-start | bytes 1671176 | tf_op jit(solution)/shard_map/ppermute | solution.py:66
  60.4 4.3 %collective-permute-start.28 = (bf16[2,64,2048]{2,1,0:T(8,128)(2,1)S(1)}, bf16[2,64,2048]{2,1,0:T(8,128)(2,1)S(1)}, u32[]{:S(2)}, u32[]{:S(2)}) collective-permute-start(bf16[2,64,2048]{2,1,0:T(8,128)(2,1)S(1)} %join.3._.diag), channel_id=1, source_target_pairs={{0,2},{2,0},{4,6},{6,4},{8,10},{10,8},{12,14},{14,12},{16,18},{18,... | collective-permute-start | bytes 1572872 | tf_op jit(solution)/shard_map/ppermute | solution.py:66
  61.1 13.9 %collective-permute-start.19 = (bf16[4,64,1024]{2,1,0:T(8,128)(2,1)S(1)}, bf16[4,64,1024]{2,1,0:T(8,128)(2,1)S(1)}, u32[]{:S(2)}, u32[]{:S(2)}) collective-permute-start(bf16[4,64,1024]{2,1,0:T(8,128)(2,1)S(1)} %get-tuple-element.68._), channel_id=1, source_target_pairs={{0,1},{1,0},{2,3},{3,2},{4,5},{5,4},{6,7},{7,6},{8,9},{9,8},{10,11... | collective-permute-start | bytes 1572872 | tf_op jit(solution)/shard_map/ppermute | solution.py:66
  61.9 13.8 %collective-permute-start.21 = (bf16[2,128,1024]{2,1,0:T(8,128)(2,1)S(1)}, bf16[2,128,1024]{2,1,0:T(8,128)(2,1)S(1)}, u32[]{:S(2)}, u32[]{:S(2)}) collective-permute-start(bf16[2,128,1024]{2,1,0:T(8,128)(2,1)S(1)} %get-tuple-element.71._), channel_id=1, source_target_pairs={{0,4},{2,6},{4,0},{6,2},{8,12},{10,14},{12,8},{14,10},{16,20},{18,... | collective-permute-start | bytes 1572872 | tf_op jit(solution)/shard_map/ppermute | solution.py:66
  70.8 7.9 %collective-permute-start.29 = (bf16[4,128,1024]{2,1,0:T(8,128)(2,1)S(1)}, bf16[4,128,1024]{2,1,0:T(8,128)(2,1)S(1)}, u32[]{:S(2)}, u32[]{:S(2)}) collective-permute-start(bf16[4,128,1024]{2,1,0:T(8,128)(2,1)S(1)} %get-tuple-element.82._), channel_id=1, source_target_pairs={{0,2},{2,0},{4,6},{6,4},{8,10},{10,8},{12,14},{14,12},{16,18},{18,... | collective-permute-start | bytes 3145736 | tf_op jit(solution)/shard_map/ppermute | solution.py:66
  73.1 6.5 %collective-permute-start.31 = (bf16[4,128,1024]{2,1,0:T(8,128)(2,1)S(1)}, bf16[4,128,1024]{2,1,0:T(8,128)(2,1)S(1)}, u32[]{:S(2)}, u32[]{:S(2)}) collective-permute-start(bf16[4,128,1024]{2,1,0:T(8,128)(2,1)S(1)} %get-tuple-element.86), channel_id=1, source_target_pairs={{0,2},{2,0},{4,6},{6,4},{8,10},{10,8},{12,14},{14,12},{16,18},{18,... | collective-permute-start | bytes 3145736 | tf_op jit(solution)/shard_map/ppermute | solution.py:66
  75.8 9.3 %collective-permute-start.22 = (bf16[2,64,1024]{2,1,0:T(8,128)(2,1)S(1)}, bf16[2,64,1024]{2,1,0:T(8,128)(2,1)S(1)}, u32[]{:S(2)}, u32[]{:S(2)}) collective-permute-start(bf16[2,64,1024]{2,1,0:T(8,128)(2,1)S(1)} %get-tuple-element.73._), channel_id=1, source_target_pairs={{0,4},{2,6},{4,0},{6,2},{8,12},{10,14},{12,8},{14,10},{16,20},{18,... | collective-permute-start | bytes 786440 | tf_op jit(solution)/shard_map/ppermute | solution.py:66
  77.4 9.2 %collective-permute-start.23 = (bf16[2,64,1024]{2,1,0:T(8,128)(2,1)S(1)}, bf16[2,64,1024]{2,1,0:T(8,128)(2,1)S(1)}, u32[]{:S(2)}, u32[]{:S(2)}) collective-permute-start(bf16[2,64,1024]{2,1,0:T(8,128)(2,1)S(1)} %get-tuple-element.75), channel_id=1, source_target_pairs={{0,1},{1,0},{2,3},{3,2},{4,5},{5,4},{6,7},{7,6},{8,9},{9,8},{10,11... | collective-permute-start | bytes 786440 | tf_op jit(solution)/shard_map/ppermute | solution.py:66
  78.8 16.8 %collective-permute-start.30 = (bf16[4,64,1024]{2,1,0:T(8,128)(2,1)S(1)}, bf16[4,64,1024]{2,1,0:T(8,128)(2,1)S(1)}, u32[]{:S(2)}, u32[]{:S(2)}) collective-permute-start(bf16[4,64,1024]{2,1,0:T(8,128)(2,1)S(1)} %get-tuple-element.84._), channel_id=1, source_target_pairs={{0,1},{1,0},{2,3},{3,2},{4,5},{5,4},{6,7},{7,6},{8,9},{9,8},{10,11... | collective-permute-start | bytes 1572872 | tf_op jit(solution)/shard_map/ppermute | solution.py:66
  79.7 15.8 %collective-permute-start.32 = (bf16[2,128,1024]{2,1,0:T(8,128)(2,1)S(1)}, bf16[2,128,1024]{2,1,0:T(8,128)(2,1)S(1)}, u32[]{:S(2)}, u32[]{:S(2)}) collective-permute-start(bf16[2,128,1024]{2,1,0:T(8,128)(2,1)S(1)} %get-tuple-element.88), channel_id=1, source_target_pairs={{0,4},{2,6},{4,0},{6,2},{8,12},{10,14},{12,8},{14,10},{16,20},{18,... | collective-permute-start | bytes 1572872 | tf_op jit(solution)/shard_map/ppermute | solution.py:66
  86.8 10.6 %collective-permute-start.24 = (bf16[64,2048]{1,0:T(8,128)(2,1)S(1)}, bf16[64,2048]{1,0:T(8,128)(2,1)S(1)}, u32[]{:S(2)}, u32[]{:S(2)}) collective-permute-start(bf16[64,2048]{1,0:T(8,128)(2,1)S(1)} %get-tuple-element.77), channel_id=1, source_target_pairs={{0,16},{2,18},{4,20},{6,22},{8,24},{10,26},{12,28},{14,30},{16,0},... | collective-permute-start | bytes 786440 | tf_op jit(solution)/shard_map/ppermute | solution.py:71
  95.7 6.4 %collective-permute-start.33 = (bf16[2,64,1024]{2,1,0:T(8,128)(2,1)S(1)}, bf16[2,64,1024]{2,1,0:T(8,128)(2,1)S(1)}, u32[]{:S(2)}, u32[]{:S(2)}) collective-permute-start(bf16[2,64,1024]{2,1,0:T(8,128)(2,1)S(1)} %get-tuple-element.90), channel_id=1, source_target_pairs={{0,4},{2,6},{4,0},{6,2},{8,12},{10,14},{12,8},{14,10},{16,20},{18,... | collective-permute-start | bytes 786440 | tf_op jit(solution)/shard_map/ppermute | solution.py:66
  96.3 6.4 %collective-permute-start.34 = (bf16[2,64,1024]{2,1,0:T(8,128)(2,1)S(1)}, bf16[2,64,1024]{2,1,0:T(8,128)(2,1)S(1)}, u32[]{:S(2)}, u32[]{:S(2)}) collective-permute-start(bf16[2,64,1024]{2,1,0:T(8,128)(2,1)S(1)} %get-tuple-element.92), channel_id=1, source_target_pairs={{0,1},{1,0},{2,3},{3,2},{4,5},{5,4},{6,7},{7,6},{8,9},{9,8},{10,11... | collective-permute-start | bytes 786440 | tf_op jit(solution)/shard_map/ppermute | solution.py:66
  102.8 11.0 %collective-permute-start.35 = (bf16[64,2048]{1,0:T(8,128)(2,1)S(1)}, bf16[64,2048]{1,0:T(8,128)(2,1)S(1)}, u32[]{:S(2)}, u32[]{:S(2)}) collective-permute-start(bf16[64,2048]{1,0:T(8,128)(2,1)S(1)} %get-tuple-element.93), channel_id=1, source_target_pairs={{0,8},{2,10},{4,12},{6,14},{8,16},{10,18},{12,20},{14,22},{16,24},... | collective-permute-start | bytes 786440 | tf_op jit(solution)/shard_map/ppermute | solution.py:71
  104.7 10.3 %collective-permute-start.36 = (bf16[64,2048]{1,0:T(8,128)(2,1)S(1)}, bf16[64,2048]{1,0:T(8,128)(2,1)S(1)}, u32[]{:S(2)}, u32[]{:S(2)}) collective-permute-start(bf16[64,2048]{1,0:T(8,128)(2,1)S(1)} %get-tuple-element.94), channel_id=1, source_target_pairs={{0,24},{2,26},{4,28},{6,30},{8,0},{10,2},{12,4},{14,6},{16,8},{18,... | collective-permute-start | bytes 786440 | tf_op jit(solution)/shard_map/ppermute | solution.py:71

commit v13 on v12

--- a/solution.py
+++ b/solution.py
@@ -505,6 +505,46 @@
     )
 
 
+def second_apart_kernel(keep_l, came_l, keep_r, came_r, _, *outs):
+    piece = outs[0].shape[0]
+    for i in range(keep_r.shape[0]):
+        send_l, left, send_r, right = outs[4 * i:4 * i + 4]
+        left[...] = keep_l[2 * i] + came_l[2 * i]
+        send_l[...] = keep_l[2 * i + 1] + came_l[2 * i + 1]
+        right[...] = keep_r[i, :piece] + came_r[i, :piece]
+        send_r[...] = keep_r[i, piece:] + came_r[i, piece:]
+
+
+def second_apart(keep_l, came_l, keep_r, came_r, after):
+    lines = keep_r.shape[0]
+    _, piece, middle = keep_l.shape
+    return small(
+        second_apart_kernel,
+        "second_sum",
+        [(piece, middle)] * (4 * lines),
+        "vvvvo",
+        (keep_l, came_l, keep_r, came_r, after),
+        work=1 << 36,
+    )
+
+
+def third_apart_kernel(left, came_l, right, came_r, _, out):
+    middle = left.shape[-1]
+    out[:, :middle] = left[...] + came_l[...]
+    out[:, middle:] = right[...] + came_r[...]
+
+
+def third_apart(left, came_l, right, came_r, after):
+    piece, middle = left.shape
+    return small(
+        third_apart_kernel,
+        "third_sum",
+        [(piece, 2 * middle)],
+        "vvvvo",
+        (left, came_l, right, came_r, after),
+    )[0]
+
+
 def third_kernel(left, came_l, right, came_r, _, *outs):
     middle = left.shape[-1]
     for columns, one, other in ((slice(0, middle), left, came_l), (slice(middle, None), right, came_r)):
@@ -534,6 +574,17 @@
     for ref in refs[1:-1]:
         total = total + ref[...].astype(jnp.float32)
     refs[-1][...] = total
+
+
+def add_up(terms, name, work=0):
+    return small(
+        last_kernel,
+        name,
+        [jax.ShapeDtypeStruct(terms[0].shape, jnp.float32)],
+        "v" * len(terms),
+        terms,
+        work=work,
+    )[0]
 
 
 def tokens_body(cotangent, gates, expert_ids, saved_gate, saved_up, w_gate, w_up, w_down):
@@ -607,14 +658,16 @@
     late_r, _ = sums_by_token(middle, grads, pick_t, after)
     done, early, after = second_step(CHUNKS[0], early[:4], early[4], None)
     late = first_step(*late_l, *late_r, after)
-    _, late, _ = second_step(CHUNKS[1], late[:4], done, early[-1])
-    terms = early + late
-    return pl.pallas_call(
-        last_kernel,
-        out_shape=jax.ShapeDtypeStruct((piece, feature_dim), jnp.float32),
-        compiler_params=pltpu.CompilerParams(vmem_limit_bytes=8 << 20),
-        name="last_sum",
-    )(*terms)
+    parts = second_apart(*late[:4], done)
+    after, total = early[-1], None
+    for i, r in enumerate(CHUNKS[1]):
+        send_l, left, send_r, right = parts[4 * i:4 * i + 4]
+        came_l, came_r = swap(send_l, "expert", 2), swap(send_r, "tp", 1)
+        after = third_apart(left, came_l, right, came_r, after)
+        came = along_line(after, r)
+        if total is None:
+            total = add_up(early + [came], "middle_sum", work=0)
+    return add_up([total, came], "last_sum")
 
 
 def body(*arrays):

time: 116 us -> 115 us (level)
  waiting for transfers between devices: 50.7 us -> 45.3 us
  starting transfers between devices: 34.4 us -> 38.5 us
    ppermute x31 -> x33, waiting for transfers between devices: 30.3 us -> 27.2 us  [swap(): return lax.ppermute(value, axis, [(i, i ^ step) for i in range(count)])]
    ppermute x31 -> x33, starting transfers between devices: 21.8 us -> 24.2 us  [swap(): return lax.ppermute(value, axis, [(i, i ^ step) for i in range(count)])]
    ppermute x6, waiting for transfers between devices: 20.3 us -> 18.1 us  [along_line(): lax.ppermute(value, 'expert', [(i, (i + 4 * shift) % count) for i in rang...]
    ppermute x6, starting transfers between devices: 12.6 us -> 14.2 us  [along_line(): lax.ppermute(value, 'expert', [(i, (i + 4 * shift) % count) for i in rang...]
    pallas_call x24 -> x27, Pallas kernels: 22.6 us -> 23.5 us  [small(): pl.pallas_call(kernel, out_shape=[out if hasattr(out, 'dtype') else jax.S...]
  transfers between devices with their start and end apart: 37 -> 39, of which waited for: 19 -> 20; matrix products, arithmetic and copies ran while one was open for 0% -> 0% of each run, Pallas kernels for 19% -> 19%
where the time goes in v13:
time: 115 us
  waiting for transfers between devices  45.3 us (39%)
  starting transfers between devices  38.5 us (33%)
  Pallas kernels  23.5 us (20%)
  local copies, waits for them, and re-layouts  6.98 us (6%)
    ppermute x33, waiting for transfers between devices, swap(): return lax.ppermute(value, axis, [(i, i ^ step) for i in range(count)])  27.2 us
    ppermute x33, starting transfers between devices, swap(): return lax.ppermute(value, axis, [(i, i ^ step) for i in range(count)])  24.2 us
    pallas_call x27, Pallas kernels, small(): pl.pallas_call(kernel, out_shape=[out if hasattr(out, 'dtype') else jax.S...  23.5 us
    ppermute x6, waiting for transfers between devices, along_line(): lax.ppermute(value, 'expert', [(i, (i + 4 * shift) % count) for i in rang...  18.1 us
    ppermute x6, starting transfers between devices, along_line(): lax.ppermute(value, 'expert', [(i, (i + 4 * shift) % count) for i in rang...  14.2 us
    unnamed x20, local copies, waits for them, and re-layouts  6.98 us
  transfers between devices with their start and end apart: 39, of which 20 were waited for; matrix products, arithmetic and copies ran while one was open for 0% of the time, Pallas kernels for 19%

profile of v13, /device:TPU:0, one launch (start us, length us, event | category | flops | bytes accessed | tf_op | source)
XLA Modules:
  0.0 114.6 jit_solution(5445766613967341300)
XLA Ops:
  0.1 1.0 copy-done.3
  1.1 0.7 copy-done.8
  1.8 0.7 copy-done.9
  2.5 0.6 prepare.1
  3.1 4.1 %collective-permute-start.1 = (bf16[64,2176]{1,0:T(8,128)(2,1)S(1)}, bf16[64,2176]{1,0:T(8,128)(2,1)S(1)}, u32[]{:S(2)}, u32[]{:S(2)}) collective-permute-start(bf16[64,2176]{1,0:T(8,128)(2,1)S(1)} %get-tuple-element.52.part), channel_id=1, source_target_pairs={{0,16},{2,18},{4,20},{6,22},{8,24},{10,26},{12,28},{14,30},{16,0},... | collective-permute-start | bytes 835592 | tf_op jit(solution)/shard_map/ppermute | solution.py:71
  7.2 1.5 %collective-permute-start.5 = (bf16[64,2176]{1,0:T(8,128)(2,1)S(1)}, bf16[64,2176]{1,0:T(8,128)(2,1)S(1)}, u32[]{:S(2)}, u32[]{:S(2)}) collective-permute-start(bf16[64,2176]{1,0:T(8,128)(2,1)S(1)} %get-tuple-element.52.part), channel_id=1, source_target_pairs={{0,4},{2,6},{4,0},{6,2},{8,12},{10,14},{12,8},{14,10},{16,20},{18,... | collective-permute-start | bytes 835592 | tf_op jit(solution)/shard_map/ppermute | solution.py:66
  8.7 11.1 %collective-permute-done.1.came = bf16[64,2176]{1,0:T(8,128)(2,1)S(1)} collective-permute-done((bf16[64,2176]{1,0:T(8,128)(2,1)S(1)}, bf16[64,2176]{1,0:T(8,128)(2,1)S(1)}, u32[]{:S(2)}, u32[]{:S(2)}) %collective-permute-start.1) | collective-permute-done | bytes 278560 | tf_op jit(solution)/shard_map/ppermute | solution.py:71
  19.9 1.6 %collective-permute-start.3 = (bf16[1,64,2176]{2,1,0:T(8,128)(2,1)S(1)}, bf16[1,64,2176]{2,1,0:T(8,128)(2,1)S(1)}, u32[]{:S(2)}, u32[]{:S(2)}) collective-permute-start(bf16[1,64,2176]{2,1,0:T(8,128)(2,1)S(1)} %get-tuple-element.53.lines._), channel_id=1, source_target_pairs={{0,1},{1,0},{2,3},{3,2},{4,5},{5,4},{6,7},{7,6},{8,9},{9,8},{10,11... | collective-permute-start | bytes 835592 | tf_op jit(solution)/shard_map/ppermute | solution.py:66
  21.5 1.5 %collective-permute-start.6 = (bf16[1,64,2176]{2,1,0:T(8,128)(2,1)S(1)}, bf16[1,64,2176]{2,1,0:T(8,128)(2,1)S(1)}, u32[]{:S(2)}, u32[]{:S(2)}) collective-permute-start(bf16[1,64,2176]{2,1,0:T(8,128)(2,1)S(1)} %get-tuple-element.53.lines._), channel_id=1, source_target_pairs={{0,4},{2,6},{4,0},{6,2},{8,12},{10,14},{12,8},{14,10},{16,20},{18,... | collective-permute-start | bytes 835592 | tf_op jit(solution)/shard_map/ppermute | solution.py:66
  23.0 3.5 %collective-permute-start.12 = (bf16[64,2176]{1,0:T(8,128)(2,1)S(1)}, bf16[64,2176]{1,0:T(8,128)(2,1)S(1)}, u32[]{:S(2)}, u32[]{:S(2)}) collective-permute-start(bf16[64,2176]{1,0:T(8,128)(2,1)S(1)} %get-tuple-element.62), channel_id=1, source_target_pairs={{0,24},{2,26},{4,28},{6,30},{8,0},{10,2},{12,4},{14,6},{16,8},{18,... | collective-permute-start | bytes 835592 | tf_op jit(solution)/shard_map/ppermute | solution.py:71
  26.5 1.3 %collective-permute-done.3.side = bf16[1,64,2176]{2,1,0:T(8,128)(2,1)S(1)} collective-permute-done((bf16[1,64,2176]{2,1,0:T(8,128)(2,1)S(1)}, bf16[1,64,2176]{2,1,0:T(8,128)(2,1)S(1)}, u32[]{:S(2)}, u32[]{:S(2)}) %collective-permute-start.3) | collective-permute-done | bytes 278560 | tf_op jit(solution)/shard_map/ppermute | solution.py:66
  27.8 1.0 collective-permute-done.6.over
  28.8 1.0 copy-done.4
  29.8 0.6 own_corner.1
  30.5 0.8 collective-permute-start.8
  31.3 1.3 %collective-permute-start.9 = (bf16[2,64,1024]{2,1,0:T(8,128)(2,1)S(1)}, bf16[2,64,1024]{2,1,0:T(8,128)(2,1)S(1)}, u32[]{:S(2)}, u32[]{:S(2)}) collective-permute-start(bf16[2,64,1024]{2,1,0:T(8,128)(2,1)S(1)} %get-tuple-element.56), channel_id=1, source_target_pairs={{0,4},{2,6},{4,0},{6,2},{8,12},{10,14},{12,8},{14,10},{16,20},{18,... | collective-permute-start | bytes 786440 | tf_op jit(solution)/shard_map/ppermute | solution.py:66
  32.6 1.3 %copy-done.6 = bf16[2,384,768]{2,1,0:T(8,128)(2,1)S(1)} copy-done((bf16[2,384,768]{2,1,0:T(8,128)(2,1)S(1)}, bf16[2,384,768]{2,1,0:T(8,128)(2,1)}, u32[]{:S(2)}) %copy-start.6) | copy-done | bytes 1179672
  33.8 1.3 %copy-done.7 = bf16[2,384,768]{2,1,0:T(8,128)(2,1)S(1)} copy-done((bf16[2,384,768]{2,1,0:T(8,128)(2,1)S(1)}, bf16[2,384,768]{2,1,0:T(8,128)(2,1)}, u32[]{:S(2)}) %copy-start.7) | copy-done | bytes 1179672
  35.1 1.3 %turn.1 = (f32[2,768,384]{2,1,0:T(8,128)S(1)}, f32[2,768,384]{2,1,0:T(8,128)S(1)}) custom-call(bf16[2,384,768]{2,1,0:T(8,128)(2,1)S(1)} %copy-done.6, bf16[2,384,768]{2,1,0:T(8,128)(2,1)S(1)} %copy-done.7, bf16[1,64,2176]{2,1,0:T(8,128)(2,1)S(1)} %get-tuple-element.53.lines._), custom_call_target="tpu_custom_call" | custom-call | tf_op jit(solution)/shard_map/turn/pallas_call | solution.py:76
  36.4 0.6 collective-permute-start.2
  37.0 1.8 %collective-permute-done.13.refs_1_ = bf16[64,2176]{1,0:T(8,128)(2,1)S(1)} collective-permute-done((bf16[64,2176]{1,0:T(8,128)(2,1)S(1)}, bf16[64,2176]{1,0:T(8,128)(2,1)S(1)}, u32[]{:S(2)}, u32[]{:S(2)}) %collective-permute-start.13) | collective-permute-done | bytes 278560 | tf_op jit(solution)/shard_map/ppermute | solution.py:71
  38.8 0.6 collective-permute-start.15
  39.4 0.5 collective-permute-start.16
  40.0 1.0 copy-done.5
  41.0 0.5 collective-permute-start.10
  42.0 1.1 route.2
  43.1 0.9 collective-permute-done.4.side_c
  44.0 3.9 %hidden.2.grads._ = bf16[2,384,768]{2,1,0:T(8,128)(2,1)S(1)} custom-call(s32[4]{0:T(128)S(1)} %pad_add_fusion.place, bf16[128,2048]{1,0:T(8,128)(2,1)S(1)} %copy-done.5, bf16[128,2048]{1,0:T(8,128)(2,1)S(1)} %collective-permute-done.own_c, bf16[1,64,2176]{2,1,0:T(8,128)(2,1)S(1)} %get-tuple-element.53.lines._, ...), custom_call_target="tpu_custom_call" | custom-call | tf_op jit(solution)/shard_map/hidden/pallas_call | solution.py:76
  47.9 2.2 %sums.4 = (bf16[4,128,1024]{2,1,0:T(8,128)(2,1)S(1)}, bf16[4,128,1024]{2,1,0:T(8,128)(2,1)S(1)}) custom-call(bf16[2,384,768]{2,1,0:T(8,128)(2,1)S(1)} %hidden.2.grads._, bf16[2,384,2048]{2,1,0:T(8,128)(2,1)S(1)} %copy-done, bf16[2,384,2048]{2,1,0:T(8,128)(2,1)S(1)} %copy-done.1, bf16[4,256,192]{2,1,0:T(8,128)(2,1)S(1)} %get-tuple-element.63.pick_t, ...), custom_call_target="tpu_custom_call" | custom-call | tf_op jit(solution)/shard_map/sums/pallas_call | solution.py:76
  50.4 1.8 %collective-permute-done.15.over = bf16[2,64,2176]{2,1,0:T(8,128)(2,1)S(1)} collective-permute-done((bf16[2,64,2176]{2,1,0:T(8,128)(2,1)S(1)}, bf16[2,64,2176]{2,1,0:T(8,128)(2,1)S(1)}, u32[]{:S(2)}, u32[]{:S(2)}) %collective-permute-start.15) | collective-permute-done | bytes 557088 | tf_op jit(solution)/shard_map/ppermute | solution.py:66
  52.5 1.0 collective-permute-start.17
  53.5 1.5 %collective-permute-start.18 = (bf16[2,64,1024]{2,1,0:T(8,128)(2,1)S(1)}, bf16[2,64,1024]{2,1,0:T(8,128)(2,1)S(1)}, u32[]{:S(2)}, u32[]{:S(2)}) collective-permute-start(bf16[2,64,1024]{2,1,0:T(8,128)(2,1)S(1)} %get-tuple-element.67), channel_id=1, source_target_pairs={{0,4},{2,6},{4,0},{6,2},{8,12},{10,14},{12,8},{14,10},{16,20},{18,... | collective-permute-start | bytes 786440 | tf_op jit(solution)/shard_map/ppermute | solution.py:66
  55.0 2.2 %sums.5 = (bf16[4,128,1024]{2,1,0:T(8,128)(2,1)S(1)}, bf16[4,128,1024]{2,1,0:T(8,128)(2,1)S(1)}) custom-call(bf16[2,384,768]{2,1,0:T(8,128)(2,1)S(1)} %hidden.2.grads._, bf16[2,384,2048]{2,1,0:T(8,128)(2,1)S(1)} %copy-done, bf16[2,384,2048]{2,1,0:T(8,128)(2,1)S(1)} %copy-done.1, bf16[4,256,192]{2,1,0:T(8,128)(2,1)S(1)} %get-tuple-element.63.pick_t, ...), custom_call_target="tpu_custom_call" | custom-call | flops 68719476736 | bytes 268435456 | tf_op jit(solution)/shard_map/sums/pallas_call | solution.py:76
  57.8 1.3 %collective-permute-done.17.left = bf16[2,64,1024]{2,1,0:T(8,128)(2,1)S(1)} collective-permute-done((bf16[2,64,1024]{2,1,0:T(8,128)(2,1)S(1)}, bf16[2,64,1024]{2,1,0:T(8,128)(2,1)S(1)}, u32[]{:S(2)}, u32[]{:S(2)}) %collective-permute-start.17) | collective-permute-done | bytes 262176 | tf_op jit(solution)/shard_map/ppermute | solution.py:66
  59.1 1.2 %collective-permute-done.18.right = bf16[2,64,1024]{2,1,0:T(8,128)(2,1)S(1)} collective-permute-done((bf16[2,64,1024]{2,1,0:T(8,128)(2,1)S(1)}, bf16[2,64,1024]{2,1,0:T(8,128)(2,1)S(1)}, u32[]{:S(2)}, u32[]{:S(2)}) %collective-permute-start.18) | collective-permute-done | bytes 262176 | tf_op jit(solution)/shard_map/ppermute | solution.py:66
  60.4 0.6 collective-permute-start.28
  61.1 0.7 collective-permute-start.19
  61.9 1.6 %collective-permute-start.21 = (bf16[2,128,1024]{2,1,0:T(8,128)(2,1)S(1)}, bf16[2,128,1024]{2,1,0:T(8,128)(2,1)S(1)}, u32[]{:S(2)}, u32[]{:S(2)}) collective-permute-start(bf16[2,128,1024]{2,1,0:T(8,128)(2,1)S(1)} %get-tuple-element.73._), channel_id=1, source_target_pairs={{0,4},{2,6},{4,0},{6,2},{8,12},{10,14},{12,8},{14,10},{16,20},{18,... | collective-permute-start | bytes 1572872 | tf_op jit(solution)/shard_map/ppermute | solution.py:66
  63.5 1.1 route.3
  64.7 3.9 %hidden.3.grads._ = bf16[2,384,768]{2,1,0:T(8,128)(2,1)S(1)} custom-call(s32[4]{0:T(128)S(1)} %pad_add_fusion.place, bf16[128,2048]{1,0:T(8,128)(2,1)S(1)} %copy-done.5, bf16[128,2048]{1,0:T(8,128)(2,1)S(1)} %collective-permute-done.own_c, bf16[2,64,2176]{2,1,0:T(8,128)(2,1)S(1)} %stack.21._.lines, bf16[2,64,2176]{2,1,0:T(8,128)(2,1)S(1)} %collective-permute-done.25.lines_c, ...), custom_call_target="tpu_custom_call" | custom-call | tf_op jit(solution)/shard_map/hidden/pallas_call | solution.py:76
  68.5 2.2 %sums.6 = (bf16[4,128,1024]{2,1,0:T(8,128)(2,1)S(1)}, bf16[4,128,1024]{2,1,0:T(8,128)(2,1)S(1)}) custom-call(bf16[2,384,768]{2,1,0:T(8,128)(2,1)S(1)} %hidden.3.grads._, bf16[2,384,2048]{2,1,0:T(8,128)(2,1)S(1)} %copy-done, bf16[2,384,2048]{2,1,0:T(8,128)(2,1)S(1)} %copy-done.1, bf16[4,256,192]{2,1,0:T(8,128)(2,1)S(1)} %get-tuple-element.82.pick_t, ...), custom_call_target="tpu_custom_call" | custom-call | tf_op jit(solution)/shard_map/sums/pallas_call | solution.py:76
  70.9 2.2 %sums.7 = (bf16[4,128,1024]{2,1,0:T(8,128)(2,1)S(1)}, bf16[4,128,1024]{2,1,0:T(8,128)(2,1)S(1)}) custom-call(bf16[2,384,768]{2,1,0:T(8,128)(2,1)S(1)} %hidden.3.grads._, bf16[2,384,2048]{2,1,0:T(8,128)(2,1)S(1)} %copy-done, bf16[2,384,2048]{2,1,0:T(8,128)(2,1)S(1)} %copy-done.1, bf16[4,256,192]{2,1,0:T(8,128)(2,1)S(1)} %get-tuple-element.82.pick_t, ...), custom_call_target="tpu_custom_call" | custom-call | tf_op jit(solution)/shard_map/sums/pallas_call | solution.py:76
  73.1 0.6 collective-permute-start.31
  73.7 1.3 %collective-permute-done.19.came_l = bf16[4,64,1024]{2,1,0:T(8,128)(2,1)S(1)} collective-permute-done((bf16[4,64,1024]{2,1,0:T(8,128)(2,1)S(1)}, bf16[4,64,1024]{2,1,0:T(8,128)(2,1)S(1)}, u32[]{:S(2)}, u32[]{:S(2)}) %collective-permute-start.19) | collective-permute-done | bytes 524320 | tf_op jit(solution)/shard_map/ppermute | solution.py:66
  75.0 0.7 collective-permute-done.21.came_r
  75.8 1.6 %collective-permute-start.22 = (bf16[2,64,1024]{2,1,0:T(8,128)(2,1)S(1)}, bf16[2,64,1024]{2,1,0:T(8,128)(2,1)S(1)}, u32[]{:S(2)}, u32[]{:S(2)}) collective-permute-start(bf16[2,64,1024]{2,1,0:T(8,128)(2,1)S(1)} %get-tuple-element.75._), channel_id=1, source_target_pairs={{0,4},{2,6},{4,0},{6,2},{8,12},{10,14},{12,8},{14,10},{16,20},{18,... | collective-permute-start | bytes 786440 | tf_op jit(solution)/shard_map/ppermute | solution.py:66
  77.4 1.3 %collective-permute-start.23 = (bf16[2,64,1024]{2,1,0:T(8,128)(2,1)S(1)}, bf16[2,64,1024]{2,1,0:T(8,128)(2,1)S(1)}, u32[]{:S(2)}, u32[]{:S(2)}) collective-permute-start(bf16[2,64,1024]{2,1,0:T(8,128)(2,1)S(1)} %get-tuple-element.77), channel_id=1, source_target_pairs={{0,1},{1,0},{2,3},{3,2},{4,5},{5,4},{6,7},{7,6},{8,9},{9,8},{10,11... | collective-permute-start | bytes 786440 | tf_op jit(solution)/shard_map/ppermute | solution.py:66
  78.8 0.8 collective-permute-start.30
  79.7 0.6 collective-permute-start.32
  80.3 4.8 %collective-permute-done.22.came_l = bf16[2,64,1024]{2,1,0:T(8,128)(2,1)S(1)} collective-permute-done((bf16[2,64,1024]{2,1,0:T(8,128)(2,1)S(1)}, bf16[2,64,1024]{2,1,0:T(8,128)(2,1)S(1)}, u32[]{:S(2)}, u32[]{:S(2)}) %collective-permute-start.22) | collective-permute-done | bytes 262176 | tf_op jit(solution)/shard_map/ppermute | solution.py:66
  85.1 1.5 %collective-permute-done.23.came_r = bf16[2,64,1024]{2,1,0:T(8,128)(2,1)S(1)} collective-permute-done((bf16[2,64,1024]{2,1,0:T(8,128)(2,1)S(1)}, bf16[2,64,1024]{2,1,0:T(8,128)(2,1)S(1)}, u32[]{:S(2)}, u32[]{:S(2)}) %collective-permute-start.23) | collective-permute-done | bytes 262176 | tf_op jit(solution)/shard_map/ppermute | solution.py:66
  86.9 8.6 %collective-permute-done.30.came_l = bf16[4,64,1024]{2,1,0:T(8,128)(2,1)S(1)} collective-permute-done((bf16[4,64,1024]{2,1,0:T(8,128)(2,1)S(1)}, bf16[4,64,1024]{2,1,0:T(8,128)(2,1)S(1)}, u32[]{:S(2)}, u32[]{:S(2)}) %collective-permute-start.30) | collective-permute-done | bytes 524320 | tf_op jit(solution)/shard_map/ppermute | solution.py:66
  95.7 0.6 collective-permute-start.33
  96.3 1.1 collective-permute-start.34
  97.4 1.5 %collective-permute-start.36 = (bf16[64,1024]{1,0:T(8,128)(2,1)S(1)}, bf16[64,1024]{1,0:T(8,128)(2,1)S(1)}, u32[]{:S(2)}, u32[]{:S(2)}) collective-permute-start(bf16[64,1024]{1,0:T(8,128)(2,1)S(1)} %get-tuple-element.96), channel_id=1, source_target_pairs={{0,4},{2,6},{4,0},{6,2},{8,12},{10,14},{12,8},{14,10},{16,20},{18,... | collective-permute-start | bytes 393224 | tf_op jit(solution)/shard_map/ppermute | solution.py:66
  98.9 0.9 collective-permute-start.37
  99.8 0.9 collective-permute-done.33.came_l
  100.7 0.5 collective-permute-done.34.came_r
  101.3 1.9 %collective-permute-start.35 = (bf16[64,2048]{1,0:T(8,128)(2,1)S(1)}, bf16[64,2048]{1,0:T(8,128)(2,1)S(1)}, u32[]{:S(2)}, u32[]{:S(2)}) collective-permute-start(bf16[64,2048]{1,0:T(8,128)(2,1)S(1)} %third_sum.4._), channel_id=1, source_target_pairs={{0,8},{2,10},{4,12},{6,14},{8,16},{10,18},{12,20},{14,22},{16,24},... | collective-permute-start | bytes 786440 | tf_op jit(solution)/shard_map/ppermute | solution.py:71
  103.2 0.6 collective-permute-done.37.came_r
  103.9 4.5 %collective-permute-start.38 = (bf16[64,2048]{1,0:T(8,128)(2,1)S(1)}, bf16[64,2048]{1,0:T(8,128)(2,1)S(1)}, u32[]{:S(2)}, u32[]{:S(2)}) collective-permute-start(bf16[64,2048]{1,0:T(8,128)(2,1)S(1)} %third_sum.5), channel_id=1, source_target_pairs={{0,24},{2,26},{4,28},{6,30},{8,0},{10,2},{12,4},{14,6},{16,8},{18,... | collective-permute-start | bytes 786440 | tf_op jit(solution)/shard_map/ppermute | solution.py:71
  108.4 3.6 %collective-permute-done.35.refs_2_ = bf16[64,2048]{1,0:T(8,128)(2,1)S(1)} collective-permute-done((bf16[64,2048]{1,0:T(8,128)(2,1)S(1)}, bf16[64,2048]{1,0:T(8,128)(2,1)S(1)}, u32[]{:S(2)}, u32[]{:S(2)}) %collective-permute-start.35) | collective-permute-done | bytes 262176 | tf_op jit(solution)/shard_map/ppermute | solution.py:71
  112.1 1.7 %collective-permute-done.38.refs_1_ = bf16[64,2048]{1,0:T(8,128)(2,1)S(1)} collective-permute-done((bf16[64,2048]{1,0:T(8,128)(2,1)S(1)}, bf16[64,2048]{1,0:T(8,128)(2,1)S(1)}, u32[]{:S(2)}, u32[]{:S(2)}) %collective-permute-start.38) | collective-permute-done | bytes 262176 | tf_op jit(solution)/shard_map/ppermute | solution.py:71
  113.8 0.8 last_sum.1
  (62 shorter events, 3.1 us)
Async XLA Ops:
  0.1 1.0 copy-start.3
  1.1 0.7 copy-start.8
  1.8 0.7 copy-start.9
  3.1 16.7 %collective-permute-start.1 = (bf16[64,2176]{1,0:T(8,128)(2,1)S(1)}, bf16[64,2176]{1,0:T(8,128)(2,1)S(1)}, u32[]{:S(2)}, u32[]{:S(2)}) collective-permute-start(bf16[64,2176]{1,0:T(8,128)(2,1)S(1)} %get-tuple-element.52.part), channel_id=1, source_target_pairs={{0,16},{2,18},{4,20},{6,22},{8,24},{10,26},{12,28},{14,30},{16,0},... | collective-permute-start | bytes 835592 | tf_op jit(solution)/shard_map/ppermute | solution.py:71
  7.2 19.3 %collective-permute-start.5 = (bf16[64,2176]{1,0:T(8,128)(2,1)S(1)}, bf16[64,2176]{1,0:T(8,128)(2,1)S(1)}, u32[]{:S(2)}, u32[]{:S(2)}) collective-permute-start(bf16[64,2176]{1,0:T(8,128)(2,1)S(1)} %get-tuple-element.52.part), channel_id=1, source_target_pairs={{0,4},{2,6},{4,0},{6,2},{8,12},{10,14},{12,8},{14,10},{16,20},{18,... | collective-permute-start | bytes 835592 | tf_op jit(solution)/shard_map/ppermute | solution.py:66
  19.9 7.9 %collective-permute-start.3 = (bf16[1,64,2176]{2,1,0:T(8,128)(2,1)S(1)}, bf16[1,64,2176]{2,1,0:T(8,128)(2,1)S(1)}, u32[]{:S(2)}, u32[]{:S(2)}) collective-permute-start(bf16[1,64,2176]{2,1,0:T(8,128)(2,1)S(1)} %get-tuple-element.53.lines._), channel_id=1, source_target_pairs={{0,1},{1,0},{2,3},{3,2},{4,5},{5,4},{6,7},{7,6},{8,9},{9,8},{10,11... | collective-permute-start | bytes 835592 | tf_op jit(solution)/shard_map/ppermute | solution.py:66
  21.5 7.3 %collective-permute-start.6 = (bf16[1,64,2176]{2,1,0:T(8,128)(2,1)S(1)}, bf16[1,64,2176]{2,1,0:T(8,128)(2,1)S(1)}, u32[]{:S(2)}, u32[]{:S(2)}) collective-permute-start(bf16[1,64,2176]{2,1,0:T(8,128)(2,1)S(1)} %get-tuple-element.53.lines._), channel_id=1, source_target_pairs={{0,4},{2,6},{4,0},{6,2},{8,12},{10,14},{12,8},{14,10},{16,20},{18,... | collective-permute-start | bytes 835592 | tf_op jit(solution)/shard_map/ppermute | solution.py:66
  23.0 13.4 %collective-permute-start.12 = (bf16[64,2176]{1,0:T(8,128)(2,1)S(1)}, bf16[64,2176]{1,0:T(8,128)(2,1)S(1)}, u32[]{:S(2)}, u32[]{:S(2)}) collective-permute-start(bf16[64,2176]{1,0:T(8,128)(2,1)S(1)} %get-tuple-element.62), channel_id=1, source_target_pairs={{0,24},{2,26},{4,28},{6,30},{8,0},{10,2},{12,4},{14,6},{16,8},{18,... | collective-permute-start | bytes 835592 | tf_op jit(solution)/shard_map/ppermute | solution.py:71
  26.5 12.2 %collective-permute-start.13 = (bf16[64,2176]{1,0:T(8,128)(2,1)S(1)}, bf16[64,2176]{1,0:T(8,128)(2,1)S(1)}, u32[]{:S(2)}, u32[]{:S(2)}) collective-permute-start(bf16[64,2176]{1,0:T(8,128)(2,1)S(1)} %get-tuple-element.62), channel_id=1, source_target_pairs={{0,8},{2,10},{4,12},{6,14},{8,16},{10,18},{12,20},{14,22},{16,24},... | collective-permute-start | bytes 835592 | tf_op jit(solution)/shard_map/ppermute | solution.py:71
  28.8 1.0 copy-start.4
  30.5 8.9 %collective-permute-start.8 = (bf16[2,64,1024]{2,1,0:T(8,128)(2,1)S(1)}, bf16[2,64,1024]{2,1,0:T(8,128)(2,1)S(1)}, u32[]{:S(2)}, u32[]{:S(2)}) collective-permute-start(bf16[2,64,1024]{2,1,0:T(8,128)(2,1)S(1)} %get-tuple-element.55.refs_0_), channel_id=1, source_target_pairs={{0,1},{1,0},{2,3},{3,2},{4,5},{5,4},{6,7},{7,6},{8,9},{9,8},{10,11... | collective-permute-start | bytes 786440 | tf_op jit(solution)/shard_map/ppermute | solution.py:66
  31.3 8.6 %collective-permute-start.9 = (bf16[2,64,1024]{2,1,0:T(8,128)(2,1)S(1)}, bf16[2,64,1024]{2,1,0:T(8,128)(2,1)S(1)}, u32[]{:S(2)}, u32[]{:S(2)}) collective-permute-start(bf16[2,64,1024]{2,1,0:T(8,128)(2,1)S(1)} %get-tuple-element.56), channel_id=1, source_target_pairs={{0,4},{2,6},{4,0},{6,2},{8,12},{10,14},{12,8},{14,10},{16,20},{18,... | collective-permute-start | bytes 786440 | tf_op jit(solution)/shard_map/ppermute | solution.py:66
  32.6 7.4 %collective-permute-start.11 = (bf16[64,128]{1,0:T(8,128)(2,1)S(1)}, bf16[64,128]{1,0:T(8,128)(2,1)S(1)}, u32[]{:S(2)}, u32[]{:S(2)}) collective-permute-start(bf16[64,128]{1,0:T(8,128)(2,1)S(1)} %get-tuple-element.57.own), channel_id=1, source_target_pairs={{0,2},{2,0},{4,6},{6,4},{8,10},{10,8},{12,14},{14,12},{16,18},{18,... | collective-permute-start | bytes 49160 | tf_op jit(solution)/shard_map/ppermute | solution.py:66
  32.6 1.3 %copy-start.6 = (bf16[2,384,768]{2,1,0:T(8,128)(2,1)S(1)}, bf16[2,384,768]{2,1,0:T(8,128)(2,1)}, u32[]{:S(2)}) copy-start(bf16[2,384,768]{2,1,0:T(8,128)(2,1)} %gate.1) | copy-start | bytes 3538948
  33.8 1.3 %copy-start.7 = (bf16[2,384,768]{2,1,0:T(8,128)(2,1)S(1)}, bf16[2,384,768]{2,1,0:T(8,128)(2,1)}, u32[]{:S(2)}) copy-start(bf16[2,384,768]{2,1,0:T(8,128)(2,1)} %up.1) | copy-start | bytes 3538948
  36.4 4.5 %collective-permute-start.2 = (bf16[1,64,2176]{2,1,0:T(8,128)(2,1)S(1)}, bf16[1,64,2176]{2,1,0:T(8,128)(2,1)S(1)}, u32[]{:S(2)}, u32[]{:S(2)}) collective-permute-start(bf16[1,64,2176]{2,1,0:T(8,128)(2,1)S(1)} %get-tuple-element.53.lines._), channel_id=1, source_target_pairs={{0,2},{2,0},{4,6},{6,4},{8,10},{10,8},{12,14},{14,12},{16,18},{18,... | collective-permute-start | bytes 835592 | tf_op jit(solution)/shard_map/ppermute | solution.py:66
  38.8 13.4 %collective-permute-start.15 = (bf16[2,64,2176]{2,1,0:T(8,128)(2,1)S(1)}, bf16[2,64,2176]{2,1,0:T(8,128)(2,1)S(1)}, u32[]{:S(2)}, u32[]{:S(2)}) collective-permute-start(bf16[2,64,2176]{2,1,0:T(8,128)(2,1)S(1)} %stack.21._.lines), channel_id=1, source_target_pairs={{0,4},{2,6},{4,0},{6,2},{8,12},{10,14},{12,8},{14,10},{16,20},{18,... | collective-permute-start | bytes 1671176 | tf_op jit(solution)/shard_map/ppermute | solution.py:66
  39.4 13.1 %collective-permute-start.16 = (bf16[2,64,2176]{2,1,0:T(8,128)(2,1)S(1)}, bf16[2,64,2176]{2,1,0:T(8,128)(2,1)S(1)}, u32[]{:S(2)}, u32[]{:S(2)}) collective-permute-start(bf16[2,64,2176]{2,1,0:T(8,128)(2,1)S(1)} %stack.21._.lines), channel_id=1, source_target_pairs={{0,1},{1,0},{2,3},{3,2},{4,5},{5,4},{6,7},{7,6},{8,9},{9,8},{10,11... | collective-permute-start | bytes 1671176 | tf_op jit(solution)/shard_map/ppermute | solution.py:66
  39.9 1.0 copy-start.5
  39.9 2.0 %collective-permute-start.7 = (bf16[2,64,2176]{2,1,0:T(8,128)(2,1)S(1)}, bf16[2,64,2176]{2,1,0:T(8,128)(2,1)S(1)}, u32[]{:S(2)}, u32[]{:S(2)}) collective-permute-start(bf16[2,64,2176]{2,1,0:T(8,128)(2,1)S(1)} %get-tuple-element.54.over), channel_id=1, source_target_pairs={{0,2},{2,0},{4,6},{6,4},{8,10},{10,8},{12,14},{14,12},{16,18},{18,... | collective-permute-start | bytes 1671176 | tf_op jit(solution)/shard_map/ppermute | solution.py:66
  39.9 4.1 %copy-start.2 = (bf16[2,384,2048]{2,1,0:T(8,128)(2,1)S(1)}, bf16[2,384,2048]{2,1,0:T(8,128)(2,1)}, u32[]{:S(2)}) copy-start(bf16[2,384,2048]{2,1,0:T(8,128)(2,1)} %w_down.3) | copy-start | bytes 9437188
  40.9 2.2 %collective-permute-start = (bf16[128,2048]{1,0:T(8,128)(2,1)S(1)}, bf16[128,2048]{1,0:T(8,128)(2,1)S(1)}, u32[]{:S(2)}, u32[]{:S(2)}) collective-permute-start(bf16[128,2048]{1,0:T(8,128)(2,1)S(1)} %copy-done.5), channel_id=1, source_target_pairs={{0,2},{2,0},{4,6},{6,4},{8,10},{10,8},{12,14},{14,12},{16,18},{18,... | collective-permute-start | bytes 1572872 | tf_op jit(solution)/shard_map/ppermute | solution.py:66
  41.0 3.1 %collective-permute-start.10 = (bf16[2,64,2048]{2,1,0:T(8,128)(2,1)S(1)}, bf16[2,64,2048]{2,1,0:T(8,128)(2,1)S(1)}, u32[]{:S(2)}, u32[]{:S(2)}) collective-permute-start(bf16[2,64,2048]{2,1,0:T(8,128)(2,1)S(1)} %join.2.diag), channel_id=1, source_target_pairs={{0,2},{2,0},{4,6},{6,4},{8,10},{10,8},{12,14},{14,12},{16,18},{18,... | collective-permute-start | bytes 1572872 | tf_op jit(solution)/shard_map/ppermute | solution.py:66
  41.9 2.1 %collective-permute-start.4 = (bf16[1,64,2176]{2,1,0:T(8,128)(2,1)S(1)}, bf16[1,64,2176]{2,1,0:T(8,128)(2,1)S(1)}, u32[]{:S(2)}, u32[]{:S(2)}) collective-permute-start(bf16[1,64,2176]{2,1,0:T(8,128)(2,1)S(1)} %collective-permute-done.3.side), channel_id=1, source_target_pairs={{0,2},{2,0},{4,6},{6,4},{8,10},{10,8},{12,14},{14,12},{16,18},{18,... | collective-permute-start | bytes 835592 | tf_op jit(solution)/shard_map/ppermute | solution.py:66
  44.0 3.9 %copy-start = (bf16[2,384,2048]{2,1,0:T(8,128)(2,1)S(1)}, bf16[2,384,2048]{2,1,0:T(8,128)(2,1)}, u32[]{:S(2)}) copy-start(bf16[2,384,2048]{2,1,0:T(8,128)(2,1)} %w_gate.7) | copy-start | bytes 9437188
  44.0 3.9 %copy-start.1 = (bf16[2,384,2048]{2,1,0:T(8,128)(2,1)S(1)}, bf16[2,384,2048]{2,1,0:T(8,128)(2,1)}, u32[]{:S(2)}) copy-start(bf16[2,384,2048]{2,1,0:T(8,128)(2,1)} %w_up.7) | copy-start | bytes 9437188
  50.2 10.2 %collective-permute-start.14 = (bf16[4,128,1024]{2,1,0:T(8,128)(2,1)S(1)}, bf16[4,128,1024]{2,1,0:T(8,128)(2,1)S(1)}, u32[]{:S(2)}, u32[]{:S(2)}) collective-permute-start(bf16[4,128,1024]{2,1,0:T(8,128)(2,1)S(1)} %get-tuple-element.65._), channel_id=1, source_target_pairs={{0,2},{2,0},{4,6},{6,4},{8,10},{10,8},{12,14},{14,12},{16,18},{18,... | collective-permute-start | bytes 3145736 | tf_op jit(solution)/shard_map/ppermute | solution.py:66
  52.5 6.6 %collective-permute-start.17 = (bf16[2,64,1024]{2,1,0:T(8,128)(2,1)S(1)}, bf16[2,64,1024]{2,1,0:T(8,128)(2,1)S(1)}, u32[]{:S(2)}, u32[]{:S(2)}) collective-permute-start(bf16[2,64,1024]{2,1,0:T(8,128)(2,1)S(1)} %get-tuple-element.66._), channel_id=1, source_target_pairs={{0,1},{1,0},{2,3},{3,2},{4,5},{5,4},{6,7},{7,6},{8,9},{9,8},{10,11... | collective-permute-start | bytes 786440 | tf_op jit(solution)/shard_map/ppermute | solution.py:66
  53.5 6.8 %collective-permute-start.18 = (bf16[2,64,1024]{2,1,0:T(8,128)(2,1)S(1)}, bf16[2,64,1024]{2,1,0:T(8,128)(2,1)S(1)}, u32[]{:S(2)}, u32[]{:S(2)}) collective-permute-start(bf16[2,64,1024]{2,1,0:T(8,128)(2,1)S(1)} %get-tuple-element.67), channel_id=1, source_target_pairs={{0,4},{2,6},{4,0},{6,2},{8,12},{10,14},{12,8},{14,10},{16,20},{18,... | collective-permute-start | bytes 786440 | tf_op jit(solution)/shard_map/ppermute | solution.py:66
  57.3 3.8 %collective-permute-start.20 = (bf16[4,128,1024]{2,1,0:T(8,128)(2,1)S(1)}, bf16[4,128,1024]{2,1,0:T(8,128)(2,1)S(1)}, u32[]{:S(2)}, u32[]{:S(2)}) collective-permute-start(bf16[4,128,1024]{2,1,0:T(8,128)(2,1)S(1)} %get-tuple-element.68.refs_0_), channel_id=1, source_target_pairs={{0,2},{2,0},{4,6},{6,4},{8,10},{10,8},{12,14},{14,12},{16,18},{18,... | collective-permute-start | bytes 3145736 | tf_op jit(solution)/shard_map/ppermute | solution.py:66
  57.3 4.6 %collective-permute-start.25 = (bf16[2,64,2176]{2,1,0:T(8,128)(2,1)S(1)}, bf16[2,64,2176]{2,1,0:T(8,128)(2,1)S(1)}, u32[]{:S(2)}, u32[]{:S(2)}) collective-permute-start(bf16[2,64,2176]{2,1,0:T(8,128)(2,1)S(1)} %stack.21._.lines), channel_id=1, source_target_pairs={{0,2},{2,0},{4,6},{6,4},{8,10},{10,8},{12,14},{14,12},{16,18},{18,... | collective-permute-start | bytes 1671176 | tf_op jit(solution)/shard_map/ppermute | solution.py:66
  59.1 5.6 %collective-permute-start.26 = (bf16[2,64,2176]{2,1,0:T(8,128)(2,1)S(1)}, bf16[2,64,2176]{2,1,0:T(8,128)(2,1)S(1)}, u32[]{:S(2)}, u32[]{:S(2)}) collective-permute-start(bf16[2,64,2176]{2,1,0:T(8,128)(2,1)S(1)} %collective-permute-done.16.side), channel_id=1, source_target_pairs={{0,2},{2,0},{4,6},{6,4},{8,10},{10,8},{12,14},{14,12},{16,18},{18,... | collective-permute-start | bytes 1671176 | tf_op jit(solution)/shard_map/ppermute | solution.py:66
  60.3 3.2 %collective-permute-start.27 = (bf16[2,64,2176]{2,1,0:T(8,128)(2,1)S(1)}, bf16[2,64,2176]{2,1,0:T(8,128)(2,1)S(1)}, u32[]{:S(2)}, u32[]{:S(2)}) collective-permute-start(bf16[2,64,2176]{2,1,0:T(8,128)(2,1)S(1)} %collective-permute-done.15.over), channel_id=1, source_target_pairs={{0,2},{2,0},{4,6},{6,4},{8,10},{10,8},{12,14},{14,12},{16,18},{18,... | collective-permute-start | bytes 1671176 | tf_op jit(solution)/shard_map/ppermute | solution.py:66
  60.4 4.3 %collective-permute-start.28 = (bf16[2,64,2048]{2,1,0:T(8,128)(2,1)S(1)}, bf16[2,64,2048]{2,1,0:T(8,128)(2,1)S(1)}, u32[]{:S(2)}, u32[]{:S(2)}) collective-permute-start(bf16[2,64,2048]{2,1,0:T(8,128)(2,1)S(1)} %join.3._.diag), channel_id=1, source_target_pairs={{0,2},{2,0},{4,6},{6,4},{8,10},{10,8},{12,14},{14,12},{16,18},{18,... | collective-permute-start | bytes 1572872 | tf_op jit(solution)/shard_map/ppermute | solution.py:66
  61.1 13.9 %collective-permute-start.19 = (bf16[4,64,1024]{2,1,0:T(8,128)(2,1)S(1)}, bf16[4,64,1024]{2,1,0:T(8,128)(2,1)S(1)}, u32[]{:S(2)}, u32[]{:S(2)}) collective-permute-start(bf16[4,64,1024]{2,1,0:T(8,128)(2,1)S(1)} %get-tuple-element.70._), channel_id=1, source_target_pairs={{0,1},{1,0},{2,3},{3,2},{4,5},{5,4},{6,7},{7,6},{8,9},{9,8},{10,11... | collective-permute-start | bytes 1572872 | tf_op jit(solution)/shard_map/ppermute | solution.py:66
  61.9 13.8 %collective-permute-start.21 = (bf16[2,128,1024]{2,1,0:T(8,128)(2,1)S(1)}, bf16[2,128,1024]{2,1,0:T(8,128)(2,1)S(1)}, u32[]{:S(2)}, u32[]{:S(2)}) collective-permute-start(bf16[2,128,1024]{2,1,0:T(8,128)(2,1)S(1)} %get-tuple-element.73._), channel_id=1, source_target_pairs={{0,4},{2,6},{4,0},{6,2},{8,12},{10,14},{12,8},{14,10},{16,20},{18,... | collective-permute-start | bytes 1572872 | tf_op jit(solution)/shard_map/ppermute | solution.py:66
  70.8 7.9 %collective-permute-start.29 = (bf16[4,128,1024]{2,1,0:T(8,128)(2,1)S(1)}, bf16[4,128,1024]{2,1,0:T(8,128)(2,1)S(1)}, u32[]{:S(2)}, u32[]{:S(2)}) collective-permute-start(bf16[4,128,1024]{2,1,0:T(8,128)(2,1)S(1)} %get-tuple-element.84._), channel_id=1, source_target_pairs={{0,2},{2,0},{4,6},{6,4},{8,10},{10,8},{12,14},{14,12},{16,18},{18,... | collective-permute-start | bytes 3145736 | tf_op jit(solution)/shard_map/ppermute | solution.py:66
  73.1 6.5 %collective-permute-start.31 = (bf16[4,128,1024]{2,1,0:T(8,128)(2,1)S(1)}, bf16[4,128,1024]{2,1,0:T(8,128)(2,1)S(1)}, u32[]{:S(2)}, u32[]{:S(2)}) collective-permute-start(bf16[4,128,1024]{2,1,0:T(8,128)(2,1)S(1)} %get-tuple-element.88), channel_id=1, source_target_pairs={{0,2},{2,0},{4,6},{6,4},{8,10},{10,8},{12,14},{14,12},{16,18},{18,... | collective-permute-start | bytes 3145736 | tf_op jit(solution)/shard_map/ppermute | solution.py:66
  75.8 9.3 %collective-permute-start.22 = (bf16[2,64,1024]{2,1,0:T(8,128)(2,1)S(1)}, bf16[2,64,1024]{2,1,0:T(8,128)(2,1)S(1)}, u32[]{:S(2)}, u32[]{:S(2)}) collective-permute-start(bf16[2,64,1024]{2,1,0:T(8,128)(2,1)S(1)} %get-tuple-element.75._), channel_id=1, source_target_pairs={{0,4},{2,6},{4,0},{6,2},{8,12},{10,14},{12,8},{14,10},{16,20},{18,... | collective-permute-start | bytes 786440 | tf_op jit(solution)/shard_map/ppermute | solution.py:66
  77.4 9.2 %collective-permute-start.23 = (bf16[2,64,1024]{2,1,0:T(8,128)(2,1)S(1)}, bf16[2,64,1024]{2,1,0:T(8,128)(2,1)S(1)}, u32[]{:S(2)}, u32[]{:S(2)}) collective-permute-start(bf16[2,64,1024]{2,1,0:T(8,128)(2,1)S(1)} %get-tuple-element.77), channel_id=1, source_target_pairs={{0,1},{1,0},{2,3},{3,2},{4,5},{5,4},{6,7},{7,6},{8,9},{9,8},{10,11... | collective-permute-start | bytes 786440 | tf_op jit(solution)/shard_map/ppermute | solution.py:66
  78.8 16.8 %collective-permute-start.30 = (bf16[4,64,1024]{2,1,0:T(8,128)(2,1)S(1)}, bf16[4,64,1024]{2,1,0:T(8,128)(2,1)S(1)}, u32[]{:S(2)}, u32[]{:S(2)}) collective-permute-start(bf16[4,64,1024]{2,1,0:T(8,128)(2,1)S(1)} %get-tuple-element.86._), channel_id=1, source_target_pairs={{0,1},{1,0},{2,3},{3,2},{4,5},{5,4},{6,7},{7,6},{8,9},{9,8},{10,11... | collective-permute-start | bytes 1572872 | tf_op jit(solution)/shard_map/ppermute | solution.py:66
  79.7 15.8 %collective-permute-start.32 = (bf16[2,128,1024]{2,1,0:T(8,128)(2,1)S(1)}, bf16[2,128,1024]{2,1,0:T(8,128)(2,1)S(1)}, u32[]{:S(2)}, u32[]{:S(2)}) collective-permute-start(bf16[2,128,1024]{2,1,0:T(8,128)(2,1)S(1)} %get-tuple-element.90), channel_id=1, source_target_pairs={{0,4},{2,6},{4,0},{6,2},{8,12},{10,14},{12,8},{14,10},{16,20},{18,... | collective-permute-start | bytes 1572872 | tf_op jit(solution)/shard_map/ppermute | solution.py:66
  86.8 13.0 %collective-permute-start.24 = (bf16[64,2048]{1,0:T(8,128)(2,1)S(1)}, bf16[64,2048]{1,0:T(8,128)(2,1)S(1)}, u32[]{:S(2)}, u32[]{:S(2)}) collective-permute-start(bf16[64,2048]{1,0:T(8,128)(2,1)S(1)} %get-tuple-element.79), channel_id=1, source_target_pairs={{0,16},{2,18},{4,20},{6,22},{8,24},{10,26},{12,28},{14,30},{16,0},... | collective-permute-start | bytes 786440 | tf_op jit(solution)/shard_map/ppermute | solution.py:71
  95.7 5.0 %collective-permute-start.33 = (bf16[64,1024]{1,0:T(8,128)(2,1)S(1)}, bf16[64,1024]{1,0:T(8,128)(2,1)S(1)}, u32[]{:S(2)}, u32[]{:S(2)}) collective-permute-start(bf16[64,1024]{1,0:T(8,128)(2,1)S(1)} %get-tuple-element.92), channel_id=1, source_target_pairs={{0,4},{2,6},{4,0},{6,2},{8,12},{10,14},{12,8},{14,10},{16,20},{18,... | collective-permute-start | bytes 393224 | tf_op jit(solution)/shard_map/ppermute | solution.py:66
  96.3 5.0 %collective-permute-start.34 = (bf16[64,1024]{1,0:T(8,128)(2,1)S(1)}, bf16[64,1024]{1,0:T(8,128)(2,1)S(1)}, u32[]{:S(2)}, u32[]{:S(2)}) collective-permute-start(bf16[64,1024]{1,0:T(8,128)(2,1)S(1)} %get-tuple-element.94), channel_id=1, source_target_pairs={{0,1},{1,0},{2,3},{3,2},{4,5},{5,4},{6,7},{7,6},{8,9},{9,8},{10,11... | collective-permute-start | bytes 393224 | tf_op jit(solution)/shard_map/ppermute | solution.py:66
  97.4 5.8 %collective-permute-start.36 = (bf16[64,1024]{1,0:T(8,128)(2,1)S(1)}, bf16[64,1024]{1,0:T(8,128)(2,1)S(1)}, u32[]{:S(2)}, u32[]{:S(2)}) collective-permute-start(bf16[64,1024]{1,0:T(8,128)(2,1)S(1)} %get-tuple-element.96), channel_id=1, source_target_pairs={{0,4},{2,6},{4,0},{6,2},{8,12},{10,14},{12,8},{14,10},{16,20},{18,... | collective-permute-start | bytes 393224 | tf_op jit(solution)/shard_map/ppermute | solution.py:66
  98.9 5.0 %collective-permute-start.37 = (bf16[64,1024]{1,0:T(8,128)(2,1)S(1)}, bf16[64,1024]{1,0:T(8,128)(2,1)S(1)}, u32[]{:S(2)}, u32[]{:S(2)}) collective-permute-start(bf16[64,1024]{1,0:T(8,128)(2,1)S(1)} %get-tuple-element.98), channel_id=1, source_target_pairs={{0,1},{1,0},{2,3},{3,2},{4,5},{5,4},{6,7},{7,6},{8,9},{9,8},{10,11... | collective-permute-start | bytes 393224 | tf_op jit(solution)/shard_map/ppermute | solution.py:66
  101.3 10.7 %collective-permute-start.35 = (bf16[64,2048]{1,0:T(8,128)(2,1)S(1)}, bf16[64,2048]{1,0:T(8,128)(2,1)S(1)}, u32[]{:S(2)}, u32[]{:S(2)}) collective-permute-start(bf16[64,2048]{1,0:T(8,128)(2,1)S(1)} %third_sum.4._), channel_id=1, source_target_pairs={{0,8},{2,10},{4,12},{6,14},{8,16},{10,18},{12,20},{14,22},{16,24},... | collective-permute-start | bytes 786440 | tf_op jit(solution)/shard_map/ppermute | solution.py:71
  103.9 9.9 %collective-permute-start.38 = (bf16[64,2048]{1,0:T(8,128)(2,1)S(1)}, bf16[64,2048]{1,0:T(8,128)(2,1)S(1)}, u32[]{:S(2)}, u32[]{:S(2)}) collective-permute-start(bf16[64,2048]{1,0:T(8,128)(2,1)S(1)} %third_sum.5), channel_id=1, source_target_pairs={{0,24},{2,26},{4,28},{6,30},{8,0},{10,2},{12,4},{14,6},{16,8},{18,... | collective-permute-start | bytes 786440 | tf_op jit(solution)/shard_map/ppermute | solution.py:71

commit v14 on v13

--- a/solution.py
+++ b/solution.py
@@ -156,6 +156,18 @@
 def relay(came, part):
     return small(
         relay_kernel, "relay", [(1,) + came.shape, part.shape], "vv", (came, part)
+    )
+
+
+def hold_kernel(*refs):
+    count = (len(refs) - 1) // 2
+    for source, target in zip(refs[:count], refs[count + 1:]):
+        target[...] = source[...]
+
+
+def hold(arrays, after):
+    return small(
+        hold_kernel, "hold", [array.shape for array in arrays], "v" * len(arrays) + "o", (*arrays, after)
     )
 
 
@@ -505,6 +517,25 @@
     )
 
 
+def first_lines_left_kernel(keep, came, _, *outs):
+    piece = outs[0].shape[1]
+    for i in range(len(outs) // 2):
+        for ry in range(2):
+            outs[2 * i][ry] = keep[2 * i + ry, piece:] + came[2 * i + ry, piece:]
+            outs[2 * i + 1][ry] = keep[2 * i + ry, :piece] + came[2 * i + ry, :piece]
+
+
+def first_lines_right_kernel(keep, came, _, *outs):
+    for i in range(len(outs) // 2):
+        outs[2 * i][0] = keep[2 * i + 1] + came[2 * i + 1]
+        outs[2 * i + 1][0] = keep[2 * i] + came[2 * i]
+
+
+def first_lines(kernel, dims, keep, came, after):
+    lines = keep.shape[0] // 2
+    return small(kernel, "first_lines", [dims] * (2 * lines), "vvo", (keep, came, after))
+
+
 def second_apart_kernel(keep_l, came_l, keep_r, came_r, _, *outs):
     piece = outs[0].shape[0]
     for i in range(keep_r.shape[0]):
@@ -515,7 +546,7 @@
         send_r[...] = keep_r[i, piece:] + came_r[i, piece:]
 
 
-def second_apart(keep_l, came_l, keep_r, came_r, after):
+def second_apart(keep_l, came_l, keep_r, came_r, after, work=1 << 36):
     lines = keep_r.shape[0]
     _, piece, middle = keep_l.shape
     return small(
@@ -524,24 +555,25 @@
         [(piece, middle)] * (4 * lines),
         "vvvvo",
         (keep_l, came_l, keep_r, came_r, after),
-        work=1 << 36,
+        work=work,
     )
 
 
 def third_apart_kernel(left, came_l, right, came_r, _, out):
     middle = left.shape[-1]
-    out[:, :middle] = left[...] + came_l[...]
-    out[:, middle:] = right[...] + came_r[...]
-
-
-def third_apart(left, came_l, right, came_r, after):
+    for at, one, other in ((slice(0, middle), left, came_l), (slice(middle, None), right, came_r)):
+        out[:, at] = (one[...].astype(jnp.float32) + other[...].astype(jnp.float32)).astype(out.dtype)
+
+
+def third_apart(left, came_l, right, came_r, after, kind=jnp.bfloat16, work=0):
     piece, middle = left.shape
     return small(
         third_apart_kernel,
         "third_sum",
-        [(piece, 2 * middle)],
+        [jax.ShapeDtypeStruct((piece, 2 * middle), kind)],
         "vvvvo",
         (left, came_l, right, came_r, after),
+        work=work,
     )[0]
 
 
@@ -617,6 +649,7 @@
         keep, send = sums(offset, middle, grads, w_gate, w_up, pick_t, after, work)
         return [keep, swap(send, "expert", 1)], send
 
+    near = CHUNKS[0][1]
     for offsets in CHUNKS:
         pieces = [along_line(part, -r) for r in offsets if r != 0]
         if saved is None:
@@ -635,7 +668,7 @@
             left, right = corner(over, side, middle, after)
             early_r, after = sums_by_token(middle, grads, pick_t, left, 68719476736)
             after = (after,)
-        diag = join(swap(left, "tp", 1), swap(right, "expert", 2), *after, work=8589934592)
+        diag = join(swap(left, "tp", 1), swap(right, "expert", 2), *after, work=6074000999)
         moved = []
         for array in (line, side, over, diag):
             moved += [array, swap(array, "expert", 1)]
@@ -646,27 +679,35 @@
         send_r, keep_r = first_right(keep_r, came_r, send_l)
         return keep_l, swap(send_l, "tp", 1), keep_r, swap(send_r, "expert", 2), send_r
 
-    def second_step(offsets, sums_of_two, after, came):
-        send_l, left, send_r, right = second_sum(*sums_of_two, after)
+    def second_step(keep_l, send_l, keep_r, send_r, after, works, kind=jnp.bfloat16):
+        came_l, came_r = swap(send_l, "tp", 1), swap(send_r, "expert", 2)
+        send_l, left, send_r, right = second_apart(keep_l, came_l, keep_r, came_r, after, works[0])
         came_l, came_r = swap(send_l, "expert", 2), swap(send_r, "tp", 1)
-        rows = third_sum(offsets, left, came_l, right, came_r, send_l if came is None else came)
-        return rows[0], [row if r == 0 else along_line(row, r) for r, row in zip(offsets, rows)], send_l
-
-    early = first_step(*early_l, *early_r, gathered[1][6])
-    grads, pick_t = compute(1, early[4])
+        return third_apart(left, came_l, right, came_r, send_l, kind, works[1]), send_l
+
+    send_l0, keep_l0, send_l2, keep_l2 = first_lines(
+        first_lines_left_kernel, (2, piece, middle), *early_l, gathered[1][6]
+    )
+    send_r0, keep_r0, send_r2, keep_r2 = first_lines(
+        first_lines_right_kernel, (1, 2 * piece, middle), *early_r, send_l2
+    )
+    grads, pick_t = compute(1, send_r2)
     late_l, after = sums_by_token(0, grads, pick_t, grads)
     late_r, _ = sums_by_token(middle, grads, pick_t, after)
-    done, early, after = second_step(CHUNKS[0], early[:4], early[4], None)
+    done, after = second_step(keep_l2, send_l2, keep_r2, send_r2, send_r2, (1 << 36, 1 << 36))
+    early = along_line(done, near)
     late = first_step(*late_l, *late_r, after)
     parts = second_apart(*late[:4], done)
-    after, total = early[-1], None
+    after, total = early, None
     for i, r in enumerate(CHUNKS[1]):
         send_l, left, send_r, right = parts[4 * i:4 * i + 4]
         came_l, came_r = swap(send_l, "expert", 2), swap(send_r, "tp", 1)
         after = third_apart(left, came_l, right, came_r, after)
         came = along_line(after, r)
         if total is None:
-            total = add_up(early + [came], "middle_sum", work=0)
+            send_l0, send_r0 = hold([send_l0, send_r0], parts[0])
+            own, _ = second_step(keep_l0, send_l0, keep_r0, send_r0, send_r0, (0, 0), jnp.float32)
+            total = add_up([own, early, came], "middle_sum")
     return add_up([total, came], "last_sum")
 
 

time: 115 us -> 118 us (1.026)
  starting transfers between devices: 38.5 us -> 42.8 us
  waiting for transfers between devices: 45.3 us -> 43.5 us
    ppermute x33 -> x37, starting transfers between devices: 24.2 us -> 29.4 us  [swap(): return lax.ppermute(value, axis, [(i, i ^ step) for i in range(count)])]
    ppermute x6, waiting for transfers between devices: 18.1 us -> 13.2 us  [along_line(): lax.ppermute(value, 'expert', [(i, (i + 4 * shift) % count) for i in rang...]
    ppermute x33 -> x37, waiting for transfers between devices: 27.2 us -> 30.3 us  [swap(): return lax.ppermute(value, axis, [(i, i ^ step) for i in range(count)])]
    pallas_call x27 -> x30, Pallas kernels: 23.5 us -> 23.6 us  [small(): pl.pallas_call(kernel, out_shape=[out if hasattr(out, 'dtype') else jax.S...]
  transfers between devices with their start and end apart: 39 -> 43, of which waited for: 20 -> 19; matrix products, arithmetic and copies ran while one was open for 0% -> 0% of each run, Pallas kernels for 19% -> 19%
where the time goes in v14:
time: 118 us; the launch traced here: 117 us
  waiting for transfers between devices  43.5 us (37%)
  starting transfers between devices  42.8 us (36%)
  Pallas kernels  23.6 us (20%)
  local copies, waits for them, and re-layouts  6.98 us (6%)
    ppermute x37, waiting for transfers between devices, swap(): return lax.ppermute(value, axis, [(i, i ^ step) for i in range(count)])  30.3 us
    ppermute x37, starting transfers between devices, swap(): return lax.ppermute(value, axis, [(i, i ^ step) for i in range(count)])  29.4 us
    pallas_call x30, Pallas kernels, small(): pl.pallas_call(kernel, out_shape=[out if hasattr(out, 'dtype') else jax.S...  23.6 us
    ppermute x6, starting transfers between devices, along_line(): lax.ppermute(value, 'expert', [(i, (i + 4 * shift) % count) for i in rang...  13.4 us
    ppermute x6, waiting for transfers between devices, along_line(): lax.ppermute(value, 'expert', [(i, (i + 4 * shift) % count) for i in rang...  13.2 us
    unnamed x20, local copies, waits for them, and re-layouts  6.98 us
  transfers between devices with their start and end apart: 43, of which 19 were waited for; matrix products, arithmetic and copies ran while one was open for 0% of the time, Pallas kernels for 19%

profile of v14, /device:TPU:0, one launch (start us, length us, event | category | flops | bytes accessed | tf_op | source)
XLA Modules:
  0.0 117.2 jit_solution(14611262813856242392)
XLA Ops:
  0.1 1.0 copy-done.3
  1.1 0.7 copy-done.8
  1.8 0.7 copy-done.9
  2.5 0.6 prepare.1
  3.1 4.1 %collective-permute-start.1 = (bf16[64,2176]{1,0:T(8,128)(2,1)S(1)}, bf16[64,2176]{1,0:T(8,128)(2,1)S(1)}, u32[]{:S(2)}, u32[]{:S(2)}) collective-permute-start(bf16[64,2176]{1,0:T(8,128)(2,1)S(1)} %get-tuple-element.60.part), channel_id=1, source_target_pairs={{0,16},{2,18},{4,20},{6,22},{8,24},{10,26},{12,28},{14,30},{16,0},... | collective-permute-start | bytes 835592 | tf_op jit(solution)/shard_map/ppermute | solution.py:71
  7.2 1.5 %collective-permute-start.5 = (bf16[64,2176]{1,0:T(8,128)(2,1)S(1)}, bf16[64,2176]{1,0:T(8,128)(2,1)S(1)}, u32[]{:S(2)}, u32[]{:S(2)}) collective-permute-start(bf16[64,2176]{1,0:T(8,128)(2,1)S(1)} %get-tuple-element.60.part), channel_id=1, source_target_pairs={{0,4},{2,6},{4,0},{6,2},{8,12},{10,14},{12,8},{14,10},{16,20},{18,... | collective-permute-start | bytes 835592 | tf_op jit(solution)/shard_map/ppermute | solution.py:66
  8.7 11.1 %collective-permute-done.1.came = bf16[64,2176]{1,0:T(8,128)(2,1)S(1)} collective-permute-done((bf16[64,2176]{1,0:T(8,128)(2,1)S(1)}, bf16[64,2176]{1,0:T(8,128)(2,1)S(1)}, u32[]{:S(2)}, u32[]{:S(2)}) %collective-permute-start.1) | collective-permute-done | bytes 278560 | tf_op jit(solution)/shard_map/ppermute | solution.py:71
  19.9 1.6 %collective-permute-start.3 = (bf16[1,64,2176]{2,1,0:T(8,128)(2,1)S(1)}, bf16[1,64,2176]{2,1,0:T(8,128)(2,1)S(1)}, u32[]{:S(2)}, u32[]{:S(2)}) collective-permute-start(bf16[1,64,2176]{2,1,0:T(8,128)(2,1)S(1)} %get-tuple-element.61.lines._), channel_id=1, source_target_pairs={{0,1},{1,0},{2,3},{3,2},{4,5},{5,4},{6,7},{7,6},{8,9},{9,8},{10,11... | collective-permute-start | bytes 835592 | tf_op jit(solution)/shard_map/ppermute | solution.py:66
  21.5 1.5 %collective-permute-start.6 = (bf16[1,64,2176]{2,1,0:T(8,128)(2,1)S(1)}, bf16[1,64,2176]{2,1,0:T(8,128)(2,1)S(1)}, u32[]{:S(2)}, u32[]{:S(2)}) collective-permute-start(bf16[1,64,2176]{2,1,0:T(8,128)(2,1)S(1)} %get-tuple-element.61.lines._), channel_id=1, source_target_pairs={{0,4},{2,6},{4,0},{6,2},{8,12},{10,14},{12,8},{14,10},{16,20},{18,... | collective-permute-start | bytes 835592 | tf_op jit(solution)/shard_map/ppermute | solution.py:66
  23.0 3.5 %collective-permute-start.12 = (bf16[64,2176]{1,0:T(8,128)(2,1)S(1)}, bf16[64,2176]{1,0:T(8,128)(2,1)S(1)}, u32[]{:S(2)}, u32[]{:S(2)}) collective-permute-start(bf16[64,2176]{1,0:T(8,128)(2,1)S(1)} %get-tuple-element.70), channel_id=1, source_target_pairs={{0,24},{2,26},{4,28},{6,30},{8,0},{10,2},{12,4},{14,6},{16,8},{18,... | collective-permute-start | bytes 835592 | tf_op jit(solution)/shard_map/ppermute | solution.py:71
  26.5 1.3 %collective-permute-done.3.side = bf16[1,64,2176]{2,1,0:T(8,128)(2,1)S(1)} collective-permute-done((bf16[1,64,2176]{2,1,0:T(8,128)(2,1)S(1)}, bf16[1,64,2176]{2,1,0:T(8,128)(2,1)S(1)}, u32[]{:S(2)}, u32[]{:S(2)}) %collective-permute-start.3) | collective-permute-done | bytes 278560 | tf_op jit(solution)/shard_map/ppermute | solution.py:66
  27.8 1.0 collective-permute-done.6.over
  28.8 1.0 copy-done.4
  29.8 0.6 own_corner.1
  30.5 0.8 collective-permute-start.8
  31.3 1.3 %collective-permute-start.9 = (bf16[2,64,1024]{2,1,0:T(8,128)(2,1)S(1)}, bf16[2,64,1024]{2,1,0:T(8,128)(2,1)S(1)}, u32[]{:S(2)}, u32[]{:S(2)}) collective-permute-start(bf16[2,64,1024]{2,1,0:T(8,128)(2,1)S(1)} %get-tuple-element.64), channel_id=1, source_target_pairs={{0,4},{2,6},{4,0},{6,2},{8,12},{10,14},{12,8},{14,10},{16,20},{18,... | collective-permute-start | bytes 786440 | tf_op jit(solution)/shard_map/ppermute | solution.py:66
  32.6 1.3 %copy-done.6 = bf16[2,384,768]{2,1,0:T(8,128)(2,1)S(1)} copy-done((bf16[2,384,768]{2,1,0:T(8,128)(2,1)S(1)}, bf16[2,384,768]{2,1,0:T(8,128)(2,1)}, u32[]{:S(2)}) %copy-start.6) | copy-done | bytes 1179672
  33.8 1.3 %copy-done.7 = bf16[2,384,768]{2,1,0:T(8,128)(2,1)S(1)} copy-done((bf16[2,384,768]{2,1,0:T(8,128)(2,1)S(1)}, bf16[2,384,768]{2,1,0:T(8,128)(2,1)}, u32[]{:S(2)}) %copy-start.7) | copy-done | bytes 1179672
  35.1 1.3 %turn.1 = (f32[2,768,384]{2,1,0:T(8,128)S(1)}, f32[2,768,384]{2,1,0:T(8,128)S(1)}) custom-call(bf16[2,384,768]{2,1,0:T(8,128)(2,1)S(1)} %copy-done.6, bf16[2,384,768]{2,1,0:T(8,128)(2,1)S(1)} %copy-done.7, bf16[1,64,2176]{2,1,0:T(8,128)(2,1)S(1)} %get-tuple-element.61.lines._), custom_call_target="tpu_custom_call" | custom-call | tf_op jit(solution)/shard_map/turn/pallas_call | solution.py:76
  36.4 0.6 collective-permute-start.2
  37.0 1.8 %collective-permute-done.13.refs_1_ = bf16[64,2176]{1,0:T(8,128)(2,1)S(1)} collective-permute-done((bf16[64,2176]{1,0:T(8,128)(2,1)S(1)}, bf16[64,2176]{1,0:T(8,128)(2,1)S(1)}, u32[]{:S(2)}, u32[]{:S(2)}) %collective-permute-start.13) | collective-permute-done | bytes 278560 | tf_op jit(solution)/shard_map/ppermute | solution.py:71
  38.8 0.6 collective-permute-start.15
  39.4 0.5 collective-permute-start.16
  40.0 1.0 copy-done.5
  41.0 0.5 collective-permute-start.10
  42.0 1.1 route.2
  43.1 0.9 collective-permute-done.4.side_c
  44.0 3.9 %hidden.2.grads._ = bf16[2,384,768]{2,1,0:T(8,128)(2,1)S(1)} custom-call(s32[4]{0:T(128)S(1)} %pad_add_fusion.place, bf16[128,2048]{1,0:T(8,128)(2,1)S(1)} %copy-done.5, bf16[128,2048]{1,0:T(8,128)(2,1)S(1)} %collective-permute-done.own_c, bf16[1,64,2176]{2,1,0:T(8,128)(2,1)S(1)} %get-tuple-element.61.lines._, ...), custom_call_target="tpu_custom_call" | custom-call | tf_op jit(solution)/shard_map/hidden/pallas_call | solution.py:76
  47.9 2.2 %sums.4 = (bf16[4,128,1024]{2,1,0:T(8,128)(2,1)S(1)}, bf16[4,128,1024]{2,1,0:T(8,128)(2,1)S(1)}) custom-call(bf16[2,384,768]{2,1,0:T(8,128)(2,1)S(1)} %hidden.2.grads._, bf16[2,384,2048]{2,1,0:T(8,128)(2,1)S(1)} %copy-done, bf16[2,384,2048]{2,1,0:T(8,128)(2,1)S(1)} %copy-done.1, bf16[4,256,192]{2,1,0:T(8,128)(2,1)S(1)} %get-tuple-element.71.pick_t, ...), custom_call_target="tpu_custom_call" | custom-call | tf_op jit(solution)/shard_map/sums/pallas_call | solution.py:76
  50.4 1.8 %collective-permute-done.15.over = bf16[2,64,2176]{2,1,0:T(8,128)(2,1)S(1)} collective-permute-done((bf16[2,64,2176]{2,1,0:T(8,128)(2,1)S(1)}, bf16[2,64,2176]{2,1,0:T(8,128)(2,1)S(1)}, u32[]{:S(2)}, u32[]{:S(2)}) %collective-permute-start.15) | collective-permute-done | bytes 557088 | tf_op jit(solution)/shard_map/ppermute | solution.py:66
  52.5 1.0 collective-permute-start.17
  53.5 1.5 %collective-permute-start.18 = (bf16[2,64,1024]{2,1,0:T(8,128)(2,1)S(1)}, bf16[2,64,1024]{2,1,0:T(8,128)(2,1)S(1)}, u32[]{:S(2)}, u32[]{:S(2)}) collective-permute-start(bf16[2,64,1024]{2,1,0:T(8,128)(2,1)S(1)} %get-tuple-element.75), channel_id=1, source_target_pairs={{0,4},{2,6},{4,0},{6,2},{8,12},{10,14},{12,8},{14,10},{16,20},{18,... | collective-permute-start | bytes 786440 | tf_op jit(solution)/shard_map/ppermute | solution.py:66
  55.0 2.2 %sums.5 = (bf16[4,128,1024]{2,1,0:T(8,128)(2,1)S(1)}, bf16[4,128,1024]{2,1,0:T(8,128)(2,1)S(1)}) custom-call(bf16[2,384,768]{2,1,0:T(8,128)(2,1)S(1)} %hidden.2.grads._, bf16[2,384,2048]{2,1,0:T(8,128)(2,1)S(1)} %copy-done, bf16[2,384,2048]{2,1,0:T(8,128)(2,1)S(1)} %copy-done.1, bf16[4,256,192]{2,1,0:T(8,128)(2,1)S(1)} %get-tuple-element.71.pick_t, ...), custom_call_target="tpu_custom_call" | custom-call | flops 68719476736 | bytes 268435456 | tf_op jit(solution)/shard_map/sums/pallas_call | solution.py:76
  57.8 1.3 %collective-permute-done.17.left = bf16[2,64,1024]{2,1,0:T(8,128)(2,1)S(1)} collective-permute-done((bf16[2,64,1024]{2,1,0:T(8,128)(2,1)S(1)}, bf16[2,64,1024]{2,1,0:T(8,128)(2,1)S(1)}, u32[]{:S(2)}, u32[]{:S(2)}) %collective-permute-start.17) | collective-permute-done | bytes 262176 | tf_op jit(solution)/shard_map/ppermute | solution.py:66
  59.1 1.2 %collective-permute-done.18.right = bf16[2,64,1024]{2,1,0:T(8,128)(2,1)S(1)} collective-permute-done((bf16[2,64,1024]{2,1,0:T(8,128)(2,1)S(1)}, bf16[2,64,1024]{2,1,0:T(8,128)(2,1)S(1)}, u32[]{:S(2)}, u32[]{:S(2)}) %collective-permute-start.18) | collective-permute-done | bytes 262176 | tf_op jit(solution)/shard_map/ppermute | solution.py:66
  60.4 0.6 collective-permute-start.23
  61.2 1.6 %collective-permute-start.26 = (bf16[1,128,1024]{2,1,0:T(8,128)(2,1)S(1)}, bf16[1,128,1024]{2,1,0:T(8,128)(2,1)S(1)}, u32[]{:S(2)}, u32[]{:S(2)}) collective-permute-start(bf16[1,128,1024]{2,1,0:T(8,128)(2,1)S(1)} %get-tuple-element.84._), channel_id=1, source_target_pairs={{0,4},{2,6},{4,0},{6,2},{8,12},{10,14},{12,8},{14,10},{16,20},{18,... | collective-permute-start | bytes 786440 | tf_op jit(solution)/shard_map/ppermute | solution.py:66
  62.8 0.7 collective-permute-start.25
  63.5 1.1 route.3
  64.6 3.9 %hidden.3.grads._ = bf16[2,384,768]{2,1,0:T(8,128)(2,1)S(1)} custom-call(s32[4]{0:T(128)S(1)} %pad_add_fusion.place, bf16[128,2048]{1,0:T(8,128)(2,1)S(1)} %copy-done.5, bf16[128,2048]{1,0:T(8,128)(2,1)S(1)} %collective-permute-done.own_c, bf16[2,64,2176]{2,1,0:T(8,128)(2,1)S(1)} %stack.21._.lines, bf16[2,64,2176]{2,1,0:T(8,128)(2,1)S(1)} %collective-permute-done.20.lines_c, ...), custom_call_target="tpu_custom_call" | custom-call | tf_op jit(solution)/shard_map/hidden/pallas_call | solution.py:76
  68.5 2.2 %sums.6 = (bf16[4,128,1024]{2,1,0:T(8,128)(2,1)S(1)}, bf16[4,128,1024]{2,1,0:T(8,128)(2,1)S(1)}) custom-call(bf16[2,384,768]{2,1,0:T(8,128)(2,1)S(1)} %hidden.3.grads._, bf16[2,384,2048]{2,1,0:T(8,128)(2,1)S(1)} %copy-done, bf16[2,384,2048]{2,1,0:T(8,128)(2,1)S(1)} %copy-done.1, bf16[4,256,192]{2,1,0:T(8,128)(2,1)S(1)} %get-tuple-element.85.pick_t, ...), custom_call_target="tpu_custom_call" | custom-call | tf_op jit(solution)/shard_map/sums/pallas_call | solution.py:76
  70.7 2.2 %sums.7 = (bf16[4,128,1024]{2,1,0:T(8,128)(2,1)S(1)}, bf16[4,128,1024]{2,1,0:T(8,128)(2,1)S(1)}) custom-call(bf16[2,384,768]{2,1,0:T(8,128)(2,1)S(1)} %hidden.3.grads._, bf16[2,384,2048]{2,1,0:T(8,128)(2,1)S(1)} %copy-done, bf16[2,384,2048]{2,1,0:T(8,128)(2,1)S(1)} %copy-done.1, bf16[4,256,192]{2,1,0:T(8,128)(2,1)S(1)} %get-tuple-element.85.pick_t, ...), custom_call_target="tpu_custom_call" | custom-call | tf_op jit(solution)/shard_map/sums/pallas_call | solution.py:76
  73.6 0.6 collective-permute-start.30
  74.2 1.4 %collective-permute-start.31 = (bf16[64,1024]{1,0:T(8,128)(2,1)S(1)}, bf16[64,1024]{1,0:T(8,128)(2,1)S(1)}, u32[]{:S(2)}, u32[]{:S(2)}) collective-permute-start(bf16[64,1024]{1,0:T(8,128)(2,1)S(1)} %get-tuple-element.99), channel_id=1, source_target_pairs={{0,1},{1,0},{2,3},{3,2},{4,5},{5,4},{6,7},{7,6},{8,9},{9,8},{10,11... | collective-permute-start | bytes 393224 | tf_op jit(solution)/shard_map/ppermute | solution.py:66
  75.8 1.4 %collective-permute-start.27 = (bf16[4,64,1024]{2,1,0:T(8,128)(2,1)S(1)}, bf16[4,64,1024]{2,1,0:T(8,128)(2,1)S(1)}, u32[]{:S(2)}, u32[]{:S(2)}) collective-permute-start(bf16[4,64,1024]{2,1,0:T(8,128)(2,1)S(1)} %get-tuple-element.92._), channel_id=1, source_target_pairs={{0,1},{1,0},{2,3},{3,2},{4,5},{5,4},{6,7},{7,6},{8,9},{9,8},{10,11... | collective-permute-start | bytes 1572872 | tf_op jit(solution)/shard_map/ppermute | solution.py:66
  77.4 0.7 collective-permute-start.29
  78.1 1.1 collective-permute-done.30.came_l
  79.2 1.1 collective-permute-done.31.came_r
  80.4 11.0 %collective-permute-done.29.came_r = bf16[2,128,1024]{2,1,0:T(8,128)(2,1)S(1)} collective-permute-done((bf16[2,128,1024]{2,1,0:T(8,128)(2,1)S(1)}, bf16[2,128,1024]{2,1,0:T(8,128)(2,1)S(1)}, u32[]{:S(2)}, u32[]{:S(2)}) %collective-permute-start.29) | collective-permute-done | bytes 524320 | tf_op jit(solution)/shard_map/ppermute | solution.py:66
  91.4 0.9 collective-permute-start.37
  92.4 1.4 %collective-permute-start.32 = (bf16[2,64,1024]{2,1,0:T(8,128)(2,1)S(1)}, bf16[2,64,1024]{2,1,0:T(8,128)(2,1)S(1)}, u32[]{:S(2)}, u32[]{:S(2)}) collective-permute-start(bf16[2,64,1024]{2,1,0:T(8,128)(2,1)S(1)} %get-tuple-element.101), channel_id=1, source_target_pairs={{0,1},{1,0},{2,3},{3,2},{4,5},{5,4},{6,7},{7,6},{8,9},{9,8},{10,11... | collective-permute-start | bytes 786440 | tf_op jit(solution)/shard_map/ppermute | solution.py:66
  93.8 1.2 %collective-permute-start.33 = (bf16[1,128,1024]{2,1,0:T(8,128)(2,1)S(1)}, bf16[1,128,1024]{2,1,0:T(8,128)(2,1)S(1)}, u32[]{:S(2)}, u32[]{:S(2)}) collective-permute-start(bf16[1,128,1024]{2,1,0:T(8,128)(2,1)S(1)} %get-tuple-element.103._), channel_id=1, source_target_pairs={{0,4},{2,6},{4,0},{6,2},{8,12},{10,14},{12,8},{14,10},{16,20},{18,... | collective-permute-start | bytes 786440 | tf_op jit(solution)/shard_map/ppermute | solution.py:66
  95.0 0.7 collective-permute-start.38
  95.7 0.8 collective-permute-start.40
  96.5 1.5 %collective-permute-done.37.came_l = bf16[64,1024]{1,0:T(8,128)(2,1)S(1)} collective-permute-done((bf16[64,1024]{1,0:T(8,128)(2,1)S(1)}, bf16[64,1024]{1,0:T(8,128)(2,1)S(1)}, u32[]{:S(2)}, u32[]{:S(2)}) %collective-permute-start.37) | collective-permute-done | bytes 131104 | tf_op jit(solution)/shard_map/ppermute | solution.py:66
  97.9 1.4 %collective-permute-start.41 = (bf16[64,1024]{1,0:T(8,128)(2,1)S(1)}, bf16[64,1024]{1,0:T(8,128)(2,1)S(1)}, u32[]{:S(2)}, u32[]{:S(2)}) collective-permute-start(bf16[64,1024]{1,0:T(8,128)(2,1)S(1)} %get-tuple-element.114), channel_id=1, source_target_pairs={{0,1},{1,0},{2,3},{3,2},{4,5},{5,4},{6,7},{7,6},{8,9},{9,8},{10,11... | collective-permute-start | bytes 393224 | tf_op jit(solution)/shard_map/ppermute | solution.py:66
  99.3 4.2 %collective-permute-done.38.came_r = bf16[64,1024]{1,0:T(8,128)(2,1)S(1)} collective-permute-done((bf16[64,1024]{1,0:T(8,128)(2,1)S(1)}, bf16[64,1024]{1,0:T(8,128)(2,1)S(1)}, u32[]{:S(2)}, u32[]{:S(2)}) %collective-permute-start.38) | collective-permute-done | bytes 131104 | tf_op jit(solution)/shard_map/ppermute | solution.py:66
  103.6 1.7 %collective-permute-start.39 = (bf16[64,2048]{1,0:T(8,128)(2,1)S(1)}, bf16[64,2048]{1,0:T(8,128)(2,1)S(1)}, u32[]{:S(2)}, u32[]{:S(2)}) collective-permute-start(bf16[64,2048]{1,0:T(8,128)(2,1)S(1)} %third_sum.6._), channel_id=1, source_target_pairs={{0,8},{2,10},{4,12},{6,14},{8,16},{10,18},{12,20},{14,22},{16,24},... | collective-permute-start | bytes 786440 | tf_op jit(solution)/shard_map/ppermute | solution.py:71
  105.4 4.0 %collective-permute-start.42 = (bf16[64,2048]{1,0:T(8,128)(2,1)S(1)}, bf16[64,2048]{1,0:T(8,128)(2,1)S(1)}, u32[]{:S(2)}, u32[]{:S(2)}) collective-permute-start(bf16[64,2048]{1,0:T(8,128)(2,1)S(1)} %third_sum.7), channel_id=1, source_target_pairs={{0,24},{2,26},{4,28},{6,30},{8,0},{10,2},{12,4},{14,6},{16,8},{18,... | collective-permute-start | bytes 786440 | tf_op jit(solution)/shard_map/ppermute | solution.py:71
  109.5 1.5 %collective-permute-start.34 = (bf16[64,1024]{1,0:T(8,128)(2,1)S(1)}, bf16[64,1024]{1,0:T(8,128)(2,1)S(1)}, u32[]{:S(2)}, u32[]{:S(2)}) collective-permute-start(bf16[64,1024]{1,0:T(8,128)(2,1)S(1)} %get-tuple-element.105._), channel_id=1, source_target_pairs={{0,4},{2,6},{4,0},{6,2},{8,12},{10,14},{12,8},{14,10},{16,20},{18,... | collective-permute-start | bytes 393224 | tf_op jit(solution)/shard_map/ppermute | solution.py:66
  110.9 1.7 %collective-permute-start.35 = (bf16[64,1024]{1,0:T(8,128)(2,1)S(1)}, bf16[64,1024]{1,0:T(8,128)(2,1)S(1)}, u32[]{:S(2)}, u32[]{:S(2)}) collective-permute-start(bf16[64,1024]{1,0:T(8,128)(2,1)S(1)} %get-tuple-element.107), channel_id=1, source_target_pairs={{0,1},{1,0},{2,3},{3,2},{4,5},{5,4},{6,7},{7,6},{8,9},{9,8},{10,11... | collective-permute-start | bytes 393224 | tf_op jit(solution)/shard_map/ppermute | solution.py:66
  112.6 1.9 %collective-permute-done.34.came_l = bf16[64,1024]{1,0:T(8,128)(2,1)S(1)} collective-permute-done((bf16[64,1024]{1,0:T(8,128)(2,1)S(1)}, bf16[64,1024]{1,0:T(8,128)(2,1)S(1)}, u32[]{:S(2)}, u32[]{:S(2)}) %collective-permute-start.34) | collective-permute-done | bytes 131104 | tf_op jit(solution)/shard_map/ppermute | solution.py:66
  114.5 1.4 %collective-permute-done.35.came_r = bf16[64,1024]{1,0:T(8,128)(2,1)S(1)} collective-permute-done((bf16[64,1024]{1,0:T(8,128)(2,1)S(1)}, bf16[64,1024]{1,0:T(8,128)(2,1)S(1)}, u32[]{:S(2)}, u32[]{:S(2)}) %collective-permute-start.35) | collective-permute-done | bytes 131104 | tf_op jit(solution)/shard_map/ppermute | solution.py:66
  116.4 0.8 last_sum.1
  (73 shorter events, 4.0 us)
Async XLA Ops:
  0.1 1.0 copy-start.3
  1.1 0.7 copy-start.8
  1.8 0.7 copy-start.9
  3.1 16.7 %collective-permute-start.1 = (bf16[64,2176]{1,0:T(8,128)(2,1)S(1)}, bf16[64,2176]{1,0:T(8,128)(2,1)S(1)}, u32[]{:S(2)}, u32[]{:S(2)}) collective-permute-start(bf16[64,2176]{1,0:T(8,128)(2,1)S(1)} %get-tuple-element.60.part), channel_id=1, source_target_pairs={{0,16},{2,18},{4,20},{6,22},{8,24},{10,26},{12,28},{14,30},{16,0},... | collective-permute-start | bytes 835592 | tf_op jit(solution)/shard_map/ppermute | solution.py:71
  7.2 19.3 %collective-permute-start.5 = (bf16[64,2176]{1,0:T(8,128)(2,1)S(1)}, bf16[64,2176]{1,0:T(8,128)(2,1)S(1)}, u32[]{:S(2)}, u32[]{:S(2)}) collective-permute-start(bf16[64,2176]{1,0:T(8,128)(2,1)S(1)} %get-tuple-element.60.part), channel_id=1, source_target_pairs={{0,4},{2,6},{4,0},{6,2},{8,12},{10,14},{12,8},{14,10},{16,20},{18,... | collective-permute-start | bytes 835592 | tf_op jit(solution)/shard_map/ppermute | solution.py:66
  19.9 7.9 %collective-permute-start.3 = (bf16[1,64,2176]{2,1,0:T(8,128)(2,1)S(1)}, bf16[1,64,2176]{2,1,0:T(8,128)(2,1)S(1)}, u32[]{:S(2)}, u32[]{:S(2)}) collective-permute-start(bf16[1,64,2176]{2,1,0:T(8,128)(2,1)S(1)} %get-tuple-element.61.lines._), channel_id=1, source_target_pairs={{0,1},{1,0},{2,3},{3,2},{4,5},{5,4},{6,7},{7,6},{8,9},{9,8},{10,11... | collective-permute-start | bytes 835592 | tf_op jit(solution)/shard_map/ppermute | solution.py:66
  21.5 7.3 %collective-permute-start.6 = (bf16[1,64,2176]{2,1,0:T(8,128)(2,1)S(1)}, bf16[1,64,2176]{2,1,0:T(8,128)(2,1)S(1)}, u32[]{:S(2)}, u32[]{:S(2)}) collective-permute-start(bf16[1,64,2176]{2,1,0:T(8,128)(2,1)S(1)} %get-tuple-element.61.lines._), channel_id=1, source_target_pairs={{0,4},{2,6},{4,0},{6,2},{8,12},{10,14},{12,8},{14,10},{16,20},{18,... | collective-permute-start | bytes 835592 | tf_op jit(solution)/shard_map/ppermute | solution.py:66
  23.0 13.4 %collective-permute-start.12 = (bf16[64,2176]{1,0:T(8,128)(2,1)S(1)}, bf16[64,2176]{1,0:T(8,128)(2,1)S(1)}, u32[]{:S(2)}, u32[]{:S(2)}) collective-permute-start(bf16[64,2176]{1,0:T(8,128)(2,1)S(1)} %get-tuple-element.70), channel_id=1, source_target_pairs={{0,24},{2,26},{4,28},{6,30},{8,0},{10,2},{12,4},{14,6},{16,8},{18,... | collective-permute-start | bytes 835592 | tf_op jit(solution)/shard_map/ppermute | solution.py:71
  26.5 12.2 %collective-permute-start.13 = (bf16[64,2176]{1,0:T(8,128)(2,1)S(1)}, bf16[64,2176]{1,0:T(8,128)(2,1)S(1)}, u32[]{:S(2)}, u32[]{:S(2)}) collective-permute-start(bf16[64,2176]{1,0:T(8,128)(2,1)S(1)} %get-tuple-element.70), channel_id=1, source_target_pairs={{0,8},{2,10},{4,12},{6,14},{8,16},{10,18},{12,20},{14,22},{16,24},... | collective-permute-start | bytes 835592 | tf_op jit(solution)/shard_map/ppermute | solution.py:71
  28.8 1.0 copy-start.4
  30.5 8.9 %collective-permute-start.8 = (bf16[2,64,1024]{2,1,0:T(8,128)(2,1)S(1)}, bf16[2,64,1024]{2,1,0:T(8,128)(2,1)S(1)}, u32[]{:S(2)}, u32[]{:S(2)}) collective-permute-start(bf16[2,64,1024]{2,1,0:T(8,128)(2,1)S(1)} %get-tuple-element.63.refs_0_), channel_id=1, source_target_pairs={{0,1},{1,0},{2,3},{3,2},{4,5},{5,4},{6,7},{7,6},{8,9},{9,8},{10,11... | collective-permute-start | bytes 786440 | tf_op jit(solution)/shard_map/ppermute | solution.py:66
  31.3 8.6 %collective-permute-start.9 = (bf16[2,64,1024]{2,1,0:T(8,128)(2,1)S(1)}, bf16[2,64,1024]{2,1,0:T(8,128)(2,1)S(1)}, u32[]{:S(2)}, u32[]{:S(2)}) collective-permute-start(bf16[2,64,1024]{2,1,0:T(8,128)(2,1)S(1)} %get-tuple-element.64), channel_id=1, source_target_pairs={{0,4},{2,6},{4,0},{6,2},{8,12},{10,14},{12,8},{14,10},{16,20},{18,... | collective-permute-start | bytes 786440 | tf_op jit(solution)/shard_map/ppermute | solution.py:66
  32.6 7.4 %collective-permute-start.11 = (bf16[64,128]{1,0:T(8,128)(2,1)S(1)}, bf16[64,128]{1,0:T(8,128)(2,1)S(1)}, u32[]{:S(2)}, u32[]{:S(2)}) collective-permute-start(bf16[64,128]{1,0:T(8,128)(2,1)S(1)} %get-tuple-element.65.own), channel_id=1, source_target_pairs={{0,2},{2,0},{4,6},{6,4},{8,10},{10,8},{12,14},{14,12},{16,18},{18,... | collective-permute-start | bytes 49160 | tf_op jit(solution)/shard_map/ppermute | solution.py:66
  32.6 1.3 %copy-start.6 = (bf16[2,384,768]{2,1,0:T(8,128)(2,1)S(1)}, bf16[2,384,768]{2,1,0:T(8,128)(2,1)}, u32[]{:S(2)}) copy-start(bf16[2,384,768]{2,1,0:T(8,128)(2,1)} %gate.1) | copy-start | bytes 3538948
  33.8 1.3 %copy-start.7 = (bf16[2,384,768]{2,1,0:T(8,128)(2,1)S(1)}, bf16[2,384,768]{2,1,0:T(8,128)(2,1)}, u32[]{:S(2)}) copy-start(bf16[2,384,768]{2,1,0:T(8,128)(2,1)} %up.1) | copy-start | bytes 3538948
  36.4 4.5 %collective-permute-start.2 = (bf16[1,64,2176]{2,1,0:T(8,128)(2,1)S(1)}, bf16[1,64,2176]{2,1,0:T(8,128)(2,1)S(1)}, u32[]{:S(2)}, u32[]{:S(2)}) collective-permute-start(bf16[1,64,2176]{2,1,0:T(8,128)(2,1)S(1)} %get-tuple-element.61.lines._), channel_id=1, source_target_pairs={{0,2},{2,0},{4,6},{6,4},{8,10},{10,8},{12,14},{14,12},{16,18},{18,... | collective-permute-start | bytes 835592 | tf_op jit(solution)/shard_map/ppermute | solution.py:66
  38.8 13.4 %collective-permute-start.15 = (bf16[2,64,2176]{2,1,0:T(8,128)(2,1)S(1)}, bf16[2,64,2176]{2,1,0:T(8,128)(2,1)S(1)}, u32[]{:S(2)}, u32[]{:S(2)}) collective-permute-start(bf16[2,64,2176]{2,1,0:T(8,128)(2,1)S(1)} %stack.21._.lines), channel_id=1, source_target_pairs={{0,4},{2,6},{4,0},{6,2},{8,12},{10,14},{12,8},{14,10},{16,20},{18,... | collective-permute-start | bytes 1671176 | tf_op jit(solution)/shard_map/ppermute | solution.py:66
  39.4 13.1 %collective-permute-start.16 = (bf16[2,64,2176]{2,1,0:T(8,128)(2,1)S(1)}, bf16[2,64,2176]{2,1,0:T(8,128)(2,1)S(1)}, u32[]{:S(2)}, u32[]{:S(2)}) collective-permute-start(bf16[2,64,2176]{2,1,0:T(8,128)(2,1)S(1)} %stack.21._.lines), channel_id=1, source_target_pairs={{0,1},{1,0},{2,3},{3,2},{4,5},{5,4},{6,7},{7,6},{8,9},{9,8},{10,11... | collective-permute-start | bytes 1671176 | tf_op jit(solution)/shard_map/ppermute | solution.py:66
  39.9 1.0 copy-start.5
  39.9 2.0 %collective-permute-start.7 = (bf16[2,64,2176]{2,1,0:T(8,128)(2,1)S(1)}, bf16[2,64,2176]{2,1,0:T(8,128)(2,1)S(1)}, u32[]{:S(2)}, u32[]{:S(2)}) collective-permute-start(bf16[2,64,2176]{2,1,0:T(8,128)(2,1)S(1)} %get-tuple-element.62.over), channel_id=1, source_target_pairs={{0,2},{2,0},{4,6},{6,4},{8,10},{10,8},{12,14},{14,12},{16,18},{18,... | collective-permute-start | bytes 1671176 | tf_op jit(solution)/shard_map/ppermute | solution.py:66
  39.9 4.1 %copy-start.2 = (bf16[2,384,2048]{2,1,0:T(8,128)(2,1)S(1)}, bf16[2,384,2048]{2,1,0:T(8,128)(2,1)}, u32[]{:S(2)}) copy-start(bf16[2,384,2048]{2,1,0:T(8,128)(2,1)} %w_down.3) | copy-start | bytes 9437188
  40.9 2.2 %collective-permute-start = (bf16[128,2048]{1,0:T(8,128)(2,1)S(1)}, bf16[128,2048]{1,0:T(8,128)(2,1)S(1)}, u32[]{:S(2)}, u32[]{:S(2)}) collective-permute-start(bf16[128,2048]{1,0:T(8,128)(2,1)S(1)} %copy-done.5), channel_id=1, source_target_pairs={{0,2},{2,0},{4,6},{6,4},{8,10},{10,8},{12,14},{14,12},{16,18},{18,... | collective-permute-start | bytes 1572872 | tf_op jit(solution)/shard_map/ppermute | solution.py:66
  41.0 3.1 %collective-permute-start.10 = (bf16[2,64,2048]{2,1,0:T(8,128)(2,1)S(1)}, bf16[2,64,2048]{2,1,0:T(8,128)(2,1)S(1)}, u32[]{:S(2)}, u32[]{:S(2)}) collective-permute-start(bf16[2,64,2048]{2,1,0:T(8,128)(2,1)S(1)} %join.2.diag), channel_id=1, source_target_pairs={{0,2},{2,0},{4,6},{6,4},{8,10},{10,8},{12,14},{14,12},{16,18},{18,... | collective-permute-start | bytes 1572872 | tf_op jit(solution)/shard_map/ppermute | solution.py:66
  41.9 2.1 %collective-permute-start.4 = (bf16[1,64,2176]{2,1,0:T(8,128)(2,1)S(1)}, bf16[1,64,2176]{2,1,0:T(8,128)(2,1)S(1)}, u32[]{:S(2)}, u32[]{:S(2)}) collective-permute-start(bf16[1,64,2176]{2,1,0:T(8,128)(2,1)S(1)} %collective-permute-done.3.side), channel_id=1, source_target_pairs={{0,2},{2,0},{4,6},{6,4},{8,10},{10,8},{12,14},{14,12},{16,18},{18,... | collective-permute-start | bytes 835592 | tf_op jit(solution)/shard_map/ppermute | solution.py:66
  44.0 3.9 %copy-start = (bf16[2,384,2048]{2,1,0:T(8,128)(2,1)S(1)}, bf16[2,384,2048]{2,1,0:T(8,128)(2,1)}, u32[]{:S(2)}) copy-start(bf16[2,384,2048]{2,1,0:T(8,128)(2,1)} %w_gate.7) | copy-start | bytes 9437188
  44.0 3.9 %copy-start.1 = (bf16[2,384,2048]{2,1,0:T(8,128)(2,1)S(1)}, bf16[2,384,2048]{2,1,0:T(8,128)(2,1)}, u32[]{:S(2)}) copy-start(bf16[2,384,2048]{2,1,0:T(8,128)(2,1)} %w_up.7) | copy-start | bytes 9437188
  50.2 10.2 %collective-permute-start.14 = (bf16[4,128,1024]{2,1,0:T(8,128)(2,1)S(1)}, bf16[4,128,1024]{2,1,0:T(8,128)(2,1)S(1)}, u32[]{:S(2)}, u32[]{:S(2)}) collective-permute-start(bf16[4,128,1024]{2,1,0:T(8,128)(2,1)S(1)} %get-tuple-element.73._), channel_id=1, source_target_pairs={{0,2},{2,0},{4,6},{6,4},{8,10},{10,8},{12,14},{14,12},{16,18},{18,... | collective-permute-start | bytes 3145736 | tf_op jit(solution)/shard_map/ppermute | solution.py:66
  52.5 6.6 %collective-permute-start.17 = (bf16[2,64,1024]{2,1,0:T(8,128)(2,1)S(1)}, bf16[2,64,1024]{2,1,0:T(8,128)(2,1)S(1)}, u32[]{:S(2)}, u32[]{:S(2)}) collective-permute-start(bf16[2,64,1024]{2,1,0:T(8,128)(2,1)S(1)} %get-tuple-element.74._), channel_id=1, source_target_pairs={{0,1},{1,0},{2,3},{3,2},{4,5},{5,4},{6,7},{7,6},{8,9},{9,8},{10,11... | collective-permute-start | bytes 786440 | tf_op jit(solution)/shard_map/ppermute | solution.py:66
  53.5 6.8 %collective-permute-start.18 = (bf16[2,64,1024]{2,1,0:T(8,128)(2,1)S(1)}, bf16[2,64,1024]{2,1,0:T(8,128)(2,1)S(1)}, u32[]{:S(2)}, u32[]{:S(2)}) collective-permute-start(bf16[2,64,1024]{2,1,0:T(8,128)(2,1)S(1)} %get-tuple-element.75), channel_id=1, source_target_pairs={{0,4},{2,6},{4,0},{6,2},{8,12},{10,14},{12,8},{14,10},{16,20},{18,... | collective-permute-start | bytes 786440 | tf_op jit(solution)/shard_map/ppermute | solution.py:66
  57.3 3.8 %collective-permute-start.19 = (bf16[4,128,1024]{2,1,0:T(8,128)(2,1)S(1)}, bf16[4,128,1024]{2,1,0:T(8,128)(2,1)S(1)}, u32[]{:S(2)}, u32[]{:S(2)}) collective-permute-start(bf16[4,128,1024]{2,1,0:T(8,128)(2,1)S(1)} %get-tuple-element.76.refs_0_), channel_id=1, source_target_pairs={{0,2},{2,0},{4,6},{6,4},{8,10},{10,8},{12,14},{14,12},{16,18},{18,... | collective-permute-start | bytes 3145736 | tf_op jit(solution)/shard_map/ppermute | solution.py:66
  57.3 5.5 %collective-permute-start.20 = (bf16[2,64,2176]{2,1,0:T(8,128)(2,1)S(1)}, bf16[2,64,2176]{2,1,0:T(8,128)(2,1)S(1)}, u32[]{:S(2)}, u32[]{:S(2)}) collective-permute-start(bf16[2,64,2176]{2,1,0:T(8,128)(2,1)S(1)} %stack.21._.lines), channel_id=1, source_target_pairs={{0,2},{2,0},{4,6},{6,4},{8,10},{10,8},{12,14},{14,12},{16,18},{18,... | collective-permute-start | bytes 1671176 | tf_op jit(solution)/shard_map/ppermute | solution.py:66
  59.1 4.4 %collective-permute-start.22 = (bf16[2,64,2176]{2,1,0:T(8,128)(2,1)S(1)}, bf16[2,64,2176]{2,1,0:T(8,128)(2,1)S(1)}, u32[]{:S(2)}, u32[]{:S(2)}) collective-permute-start(bf16[2,64,2176]{2,1,0:T(8,128)(2,1)S(1)} %collective-permute-done.15.over), channel_id=1, source_target_pairs={{0,2},{2,0},{4,6},{6,4},{8,10},{10,8},{12,14},{14,12},{16,18},{18,... | collective-permute-start | bytes 1671176 | tf_op jit(solution)/shard_map/ppermute | solution.py:66
  60.3 4.3 %collective-permute-start.21 = (bf16[2,64,2176]{2,1,0:T(8,128)(2,1)S(1)}, bf16[2,64,2176]{2,1,0:T(8,128)(2,1)S(1)}, u32[]{:S(2)}, u32[]{:S(2)}) collective-permute-start(bf16[2,64,2176]{2,1,0:T(8,128)(2,1)S(1)} %collective-permute-done.16.side), channel_id=1, source_target_pairs={{0,2},{2,0},{4,6},{6,4},{8,10},{10,8},{12,14},{14,12},{16,18},{18,... | collective-permute-start | bytes 1671176 | tf_op jit(solution)/shard_map/ppermute | solution.py:66
  60.4 4.2 %collective-permute-start.23 = (bf16[2,64,2048]{2,1,0:T(8,128)(2,1)S(1)}, bf16[2,64,2048]{2,1,0:T(8,128)(2,1)S(1)}, u32[]{:S(2)}, u32[]{:S(2)}) collective-permute-start(bf16[2,64,2048]{2,1,0:T(8,128)(2,1)S(1)} %join.3._.diag), channel_id=1, source_target_pairs={{0,2},{2,0},{4,6},{6,4},{8,10},{10,8},{12,14},{14,12},{16,18},{18,... | collective-permute-start | bytes 1572872 | tf_op jit(solution)/shard_map/ppermute | solution.py:66
  61.2 12.3 %collective-permute-start.26 = (bf16[1,128,1024]{2,1,0:T(8,128)(2,1)S(1)}, bf16[1,128,1024]{2,1,0:T(8,128)(2,1)S(1)}, u32[]{:S(2)}, u32[]{:S(2)}) collective-permute-start(bf16[1,128,1024]{2,1,0:T(8,128)(2,1)S(1)} %get-tuple-element.84._), channel_id=1, source_target_pairs={{0,4},{2,6},{4,0},{6,2},{8,12},{10,14},{12,8},{14,10},{16,20},{18,... | collective-permute-start | bytes 786440 | tf_op jit(solution)/shard_map/ppermute | solution.py:66
  62.8 10.8 %collective-permute-start.25 = (bf16[2,64,1024]{2,1,0:T(8,128)(2,1)S(1)}, bf16[2,64,1024]{2,1,0:T(8,128)(2,1)S(1)}, u32[]{:S(2)}, u32[]{:S(2)}) collective-permute-start(bf16[2,64,1024]{2,1,0:T(8,128)(2,1)S(1)} %get-tuple-element.80._), channel_id=1, source_target_pairs={{0,1},{1,0},{2,3},{3,2},{4,5},{5,4},{6,7},{7,6},{8,9},{9,8},{10,11... | collective-permute-start | bytes 786440 | tf_op jit(solution)/shard_map/ppermute | solution.py:66
  73.0 2.7 %collective-permute-start.24 = (bf16[4,128,1024]{2,1,0:T(8,128)(2,1)S(1)}, bf16[4,128,1024]{2,1,0:T(8,128)(2,1)S(1)}, u32[]{:S(2)}, u32[]{:S(2)}) collective-permute-start(bf16[4,128,1024]{2,1,0:T(8,128)(2,1)S(1)} %get-tuple-element.87._), channel_id=1, source_target_pairs={{0,2},{2,0},{4,6},{6,4},{8,10},{10,8},{12,14},{14,12},{16,18},{18,... | collective-permute-start | bytes 3145736 | tf_op jit(solution)/shard_map/ppermute | solution.py:66
  73.0 4.2 %collective-permute-start.28 = (bf16[4,128,1024]{2,1,0:T(8,128)(2,1)S(1)}, bf16[4,128,1024]{2,1,0:T(8,128)(2,1)S(1)}, u32[]{:S(2)}, u32[]{:S(2)}) collective-permute-start(bf16[4,128,1024]{2,1,0:T(8,128)(2,1)S(1)} %get-tuple-element.94), channel_id=1, source_target_pairs={{0,2},{2,0},{4,6},{6,4},{8,10},{10,8},{12,14},{14,12},{16,18},{18,... | collective-permute-start | bytes 3145736 | tf_op jit(solution)/shard_map/ppermute | solution.py:66
  73.6 5.5 %collective-permute-start.30 = (bf16[64,1024]{1,0:T(8,128)(2,1)S(1)}, bf16[64,1024]{1,0:T(8,128)(2,1)S(1)}, u32[]{:S(2)}, u32[]{:S(2)}) collective-permute-start(bf16[64,1024]{1,0:T(8,128)(2,1)S(1)} %get-tuple-element.90._), channel_id=1, source_target_pairs={{0,4},{2,6},{4,0},{6,2},{8,12},{10,14},{12,8},{14,10},{16,20},{18,... | collective-permute-start | bytes 393224 | tf_op jit(solution)/shard_map/ppermute | solution.py:66
  74.2 6.0 %collective-permute-start.31 = (bf16[64,1024]{1,0:T(8,128)(2,1)S(1)}, bf16[64,1024]{1,0:T(8,128)(2,1)S(1)}, u32[]{:S(2)}, u32[]{:S(2)}) collective-permute-start(bf16[64,1024]{1,0:T(8,128)(2,1)S(1)} %get-tuple-element.99), channel_id=1, source_target_pairs={{0,1},{1,0},{2,3},{3,2},{4,5},{5,4},{6,7},{7,6},{8,9},{9,8},{10,11... | collective-permute-start | bytes 393224 | tf_op jit(solution)/shard_map/ppermute | solution.py:66
  75.8 15.5 %collective-permute-start.27 = (bf16[4,64,1024]{2,1,0:T(8,128)(2,1)S(1)}, bf16[4,64,1024]{2,1,0:T(8,128)(2,1)S(1)}, u32[]{:S(2)}, u32[]{:S(2)}) collective-permute-start(bf16[4,64,1024]{2,1,0:T(8,128)(2,1)S(1)} %get-tuple-element.92._), channel_id=1, source_target_pairs={{0,1},{1,0},{2,3},{3,2},{4,5},{5,4},{6,7},{7,6},{8,9},{9,8},{10,11... | collective-permute-start | bytes 1572872 | tf_op jit(solution)/shard_map/ppermute | solution.py:66
  77.4 14.0 %collective-permute-start.29 = (bf16[2,128,1024]{2,1,0:T(8,128)(2,1)S(1)}, bf16[2,128,1024]{2,1,0:T(8,128)(2,1)S(1)}, u32[]{:S(2)}, u32[]{:S(2)}) collective-permute-start(bf16[2,128,1024]{2,1,0:T(8,128)(2,1)S(1)} %get-tuple-element.96), channel_id=1, source_target_pairs={{0,4},{2,6},{4,0},{6,2},{8,12},{10,14},{12,8},{14,10},{16,20},{18,... | collective-permute-start | bytes 1572872 | tf_op jit(solution)/shard_map/ppermute | solution.py:66
  80.3 15.4 %collective-permute-start.36 = (bf16[64,2048]{1,0:T(8,128)(2,1)S(1)}, bf16[64,2048]{1,0:T(8,128)(2,1)S(1)}, u32[]{:S(2)}, u32[]{:S(2)}) collective-permute-start(bf16[64,2048]{1,0:T(8,128)(2,1)S(1)} %third_sum.4._), channel_id=1, source_target_pairs={{0,16},{2,18},{4,20},{6,22},{8,24},{10,26},{12,28},{14,30},{16,0},... | collective-permute-start | bytes 786440 | tf_op jit(solution)/shard_map/ppermute | solution.py:71
  91.4 6.5 %collective-permute-start.37 = (bf16[64,1024]{1,0:T(8,128)(2,1)S(1)}, bf16[64,1024]{1,0:T(8,128)(2,1)S(1)}, u32[]{:S(2)}, u32[]{:S(2)}) collective-permute-start(bf16[64,1024]{1,0:T(8,128)(2,1)S(1)} %get-tuple-element.100.refs_2_), channel_id=1, source_target_pairs={{0,4},{2,6},{4,0},{6,2},{8,12},{10,14},{12,8},{14,10},{16,20},{18,... | collective-permute-start | bytes 393224 | tf_op jit(solution)/shard_map/ppermute | solution.py:66
  92.4 17.0 %collective-permute-start.32 = (bf16[2,64,1024]{2,1,0:T(8,128)(2,1)S(1)}, bf16[2,64,1024]{2,1,0:T(8,128)(2,1)S(1)}, u32[]{:S(2)}, u32[]{:S(2)}) collective-permute-start(bf16[2,64,1024]{2,1,0:T(8,128)(2,1)S(1)} %get-tuple-element.101), channel_id=1, source_target_pairs={{0,1},{1,0},{2,3},{3,2},{4,5},{5,4},{6,7},{7,6},{8,9},{9,8},{10,11... | collective-permute-start | bytes 786440 | tf_op jit(solution)/shard_map/ppermute | solution.py:66
  93.8 15.6 %collective-permute-start.33 = (bf16[1,128,1024]{2,1,0:T(8,128)(2,1)S(1)}, bf16[1,128,1024]{2,1,0:T(8,128)(2,1)S(1)}, u32[]{:S(2)}, u32[]{:S(2)}) collective-permute-start(bf16[1,128,1024]{2,1,0:T(8,128)(2,1)S(1)} %get-tuple-element.103._), channel_id=1, source_target_pairs={{0,4},{2,6},{4,0},{6,2},{8,12},{10,14},{12,8},{14,10},{16,20},{18,... | collective-permute-start | bytes 786440 | tf_op jit(solution)/shard_map/ppermute | solution.py:66
  95.0 8.5 %collective-permute-start.38 = (bf16[64,1024]{1,0:T(8,128)(2,1)S(1)}, bf16[64,1024]{1,0:T(8,128)(2,1)S(1)}, u32[]{:S(2)}, u32[]{:S(2)}) collective-permute-start(bf16[64,1024]{1,0:T(8,128)(2,1)S(1)} %get-tuple-element.110), channel_id=1, source_target_pairs={{0,1},{1,0},{2,3},{3,2},{4,5},{5,4},{6,7},{7,6},{8,9},{9,8},{10,11... | collective-permute-start | bytes 393224 | tf_op jit(solution)/shard_map/ppermute | solution.py:66
  95.7 9.6 %collective-permute-start.40 = (bf16[64,1024]{1,0:T(8,128)(2,1)S(1)}, bf16[64,1024]{1,0:T(8,128)(2,1)S(1)}, u32[]{:S(2)}, u32[]{:S(2)}) collective-permute-start(bf16[64,1024]{1,0:T(8,128)(2,1)S(1)} %get-tuple-element.112), channel_id=1, source_target_pairs={{0,4},{2,6},{4,0},{6,2},{8,12},{10,14},{12,8},{14,10},{16,20},{18,... | collective-permute-start | bytes 393224 | tf_op jit(solution)/shard_map/ppermute | solution.py:66
  97.9 7.4 %collective-permute-start.41 = (bf16[64,1024]{1,0:T(8,128)(2,1)S(1)}, bf16[64,1024]{1,0:T(8,128)(2,1)S(1)}, u32[]{:S(2)}, u32[]{:S(2)}) collective-permute-start(bf16[64,1024]{1,0:T(8,128)(2,1)S(1)} %get-tuple-element.114), channel_id=1, source_target_pairs={{0,1},{1,0},{2,3},{3,2},{4,5},{5,4},{6,7},{7,6},{8,9},{9,8},{10,11... | collective-permute-start | bytes 393224 | tf_op jit(solution)/shard_map/ppermute | solution.py:66
  103.6 12.4 %collective-permute-start.39 = (bf16[64,2048]{1,0:T(8,128)(2,1)S(1)}, bf16[64,2048]{1,0:T(8,128)(2,1)S(1)}, u32[]{:S(2)}, u32[]{:S(2)}) collective-permute-start(bf16[64,2048]{1,0:T(8,128)(2,1)S(1)} %third_sum.6._), channel_id=1, source_target_pairs={{0,8},{2,10},{4,12},{6,14},{8,16},{10,18},{12,20},{14,22},{16,24},... | collective-permute-start | bytes 786440 | tf_op jit(solution)/shard_map/ppermute | solution.py:71
  105.4 11.0 %collective-permute-start.42 = (bf16[64,2048]{1,0:T(8,128)(2,1)S(1)}, bf16[64,2048]{1,0:T(8,128)(2,1)S(1)}, u32[]{:S(2)}, u32[]{:S(2)}) collective-permute-start(bf16[64,2048]{1,0:T(8,128)(2,1)S(1)} %third_sum.7), channel_id=1, source_target_pairs={{0,24},{2,26},{4,28},{6,30},{8,0},{10,2},{12,4},{14,6},{16,8},{18,... | collective-permute-start | bytes 786440 | tf_op jit(solution)/shard_map/ppermute | solution.py:71
  109.5 5.0 %collective-permute-start.34 = (bf16[64,1024]{1,0:T(8,128)(2,1)S(1)}, bf16[64,1024]{1,0:T(8,128)(2,1)S(1)}, u32[]{:S(2)}, u32[]{:S(2)}) collective-permute-start(bf16[64,1024]{1,0:T(8,128)(2,1)S(1)} %get-tuple-element.105._), channel_id=1, source_target_pairs={{0,4},{2,6},{4,0},{6,2},{8,12},{10,14},{12,8},{14,10},{16,20},{18,... | collective-permute-start | bytes 393224 | tf_op jit(solution)/shard_map/ppermute | solution.py:66
  110.9 5.0 %collective-permute-start.35 = (bf16[64,1024]{1,0:T(8,128)(2,1)S(1)}, bf16[64,1024]{1,0:T(8,128)(2,1)S(1)}, u32[]{:S(2)}, u32[]{:S(2)}) collective-permute-start(bf16[64,1024]{1,0:T(8,128)(2,1)S(1)} %get-tuple-element.107), channel_id=1, source_target_pairs={{0,1},{1,0},{2,3},{3,2},{4,5},{5,4},{6,7},{7,6},{8,9},{9,8},{10,11... | collective-permute-start | bytes 393224 | tf_op jit(solution)/shard_map/ppermute | solution.py:66

commit v15 on v13

--- a/solution.py
+++ b/solution.py
@@ -156,6 +156,18 @@
 def relay(came, part):
     return small(
         relay_kernel, "relay", [(1,) + came.shape, part.shape], "vv", (came, part)
+    )
+
+
+def hold_kernel(*refs):
+    count = (len(refs) - 1) // 2
+    for source, target in zip(refs[:count], refs[count + 1:]):
+        target[...] = source[...]
+
+
+def hold(arrays, after):
+    return small(
+        hold_kernel, "hold", [array.shape for array in arrays], "v" * len(arrays) + "o", (*arrays, after)
     )
 
 
@@ -483,28 +495,6 @@
     )
 
 
-def second_kernel(keep_l, came_l, keep_r, came_r, _, send_l, left, send_r, right):
-    piece = left.shape[1]
-    for i in range(left.shape[0]):
-        left[i] = keep_l[2 * i] + came_l[2 * i]
-        send_l[i] = keep_l[2 * i + 1] + came_l[2 * i + 1]
-        right[i] = keep_r[i, :piece] + came_r[i, :piece]
-        send_r[i] = keep_r[i, piece:] + came_r[i, piece:]
-
-
-def second_sum(keep_l, came_l, keep_r, came_r, after):
-    lines = keep_r.shape[0]
-    _, piece, middle = keep_l.shape
-    return small(
-        second_kernel,
-        "second_sum",
-        [(lines, piece, middle)] * 4,
-        "vvvvo",
-        (keep_l, came_l, keep_r, came_r, after),
-        work=1 << 36,
-    )
-
-
 def second_apart_kernel(keep_l, came_l, keep_r, came_r, _, *outs):
     piece = outs[0].shape[0]
     for i in range(keep_r.shape[0]):
@@ -530,47 +520,24 @@
 
 def third_apart_kernel(left, came_l, right, came_r, _, out):
     middle = left.shape[-1]
-    out[:, :middle] = left[...] + came_l[...]
-    out[:, middle:] = right[...] + came_r[...]
-
-
-def third_apart(left, came_l, right, came_r, after):
+    for at, one, other in ((slice(0, middle), left, came_l), (slice(middle, None), right, came_r)):
+        out[:, at] = (one[...].astype(jnp.float32) + other[...].astype(jnp.float32)).astype(out.dtype)
+
+
+def third_apart(left, came_l, right, came_r, after, kind=jnp.bfloat16, work=0):
     piece, middle = left.shape
     return small(
         third_apart_kernel,
         "third_sum",
-        [(piece, 2 * middle)],
+        [jax.ShapeDtypeStruct((piece, 2 * middle), kind)],
         "vvvvo",
         (left, came_l, right, came_r, after),
+        work=work,
     )[0]
 
 
-def third_kernel(left, came_l, right, came_r, _, *outs):
-    middle = left.shape[-1]
-    for columns, one, other in ((slice(0, middle), left, came_l), (slice(middle, None), right, came_r)):
-        for i, out in enumerate(outs):
-            out[:, columns] = (one[i].astype(jnp.float32) + other[i].astype(jnp.float32)).astype(
-                out.dtype
-            )
-
-
-def third_sum(offsets, left, came_l, right, came_r, after):
-    _, piece, middle = left.shape
-    return small(
-        third_kernel,
-        "third_sum",
-        [
-            jax.ShapeDtypeStruct((piece, 2 * middle), jnp.float32 if r == 0 else jnp.bfloat16)
-            for r in offsets
-        ],
-        "vvvvo",
-        (left, came_l, right, came_r, after),
-        work=1 << 36,
-    )
-
-
 def last_kernel(*refs):
-    total = refs[0][...]
+    total = refs[0][...].astype(jnp.float32)
     for ref in refs[1:-1]:
         total = total + ref[...].astype(jnp.float32)
     refs[-1][...] = total
@@ -646,28 +613,29 @@
         send_r, keep_r = first_right(keep_r, came_r, send_l)
         return keep_l, swap(send_l, "tp", 1), keep_r, swap(send_r, "expert", 2), send_r
 
-    def second_step(offsets, sums_of_two, after, came):
-        send_l, left, send_r, right = second_sum(*sums_of_two, after)
+    def across(send_l, left, send_r, right, after, kind=jnp.bfloat16, work=0):
         came_l, came_r = swap(send_l, "expert", 2), swap(send_r, "tp", 1)
-        rows = third_sum(offsets, left, came_l, right, came_r, send_l if came is None else came)
-        return rows[0], [row if r == 0 else along_line(row, r) for r, row in zip(offsets, rows)], send_l
+        return third_apart(left, came_l, right, came_r, after, kind, work)
 
     early = first_step(*early_l, *early_r, gathered[1][6])
     grads, pick_t = compute(1, early[4])
     late_l, after = sums_by_token(0, grads, pick_t, grads)
     late_r, _ = sums_by_token(middle, grads, pick_t, after)
-    done, early, after = second_step(CHUNKS[0], early[:4], early[4], None)
+    parts = second_apart(*early[:4], early[4])
+    (send_l, left, send_r, right), out = parts[:4], parts[4:]
+    done = across(*out, out[0], work=1 << 36)
+    early, after = along_line(done, CHUNKS[0][1]), out[0]
     late = first_step(*late_l, *late_r, after)
     parts = second_apart(*late[:4], done)
-    after, total = early[-1], None
+    after, total = early, None
     for i, r in enumerate(CHUNKS[1]):
-        send_l, left, send_r, right = parts[4 * i:4 * i + 4]
-        came_l, came_r = swap(send_l, "expert", 2), swap(send_r, "tp", 1)
-        after = third_apart(left, came_l, right, came_r, after)
+        after = across(*parts[4 * i:4 * i + 4], after)
         came = along_line(after, r)
         if total is None:
-            total = add_up(early + [came], "middle_sum", work=0)
-    return add_up([total, came], "last_sum")
+            total = add_up([early, came], "middle_sum")
+    send_l, send_r = hold([send_l, send_r], after)
+    own = across(send_l, left, send_r, right, after, jnp.float32)
+    return add_up([total, own, came], "last_sum")
 
 
 def body(*arrays):

time: 115 us -> 113 us (0.983)
  waiting for transfers between devices: 45.3 us -> 41.6 us
  starting transfers between devices: 38.5 us -> 40.2 us
    ppermute x6, waiting for transfers between devices: 18.1 us -> 12.9 us  [along_line(): lax.ppermute(value, 'expert', [(i, (i + 4 * shift) % count) for i in rang...]
    ppermute x33 -> x35, starting transfers between devices: 24.2 us -> 26.1 us  [swap(): return lax.ppermute(value, axis, [(i, i ^ step) for i in range(count)])]
    ppermute x33 -> x35, waiting for transfers between devices: 27.2 us -> 28.7 us  [swap(): return lax.ppermute(value, axis, [(i, i ^ step) for i in range(count)])]
    pallas_call x27 -> x29, Pallas kernels: 23.5 us -> 23.6 us  [small(): pl.pallas_call(kernel, out_shape=[out if hasattr(out, 'dtype') else jax.S...]
  transfers between devices with their start and end apart: 39 -> 41, of which waited for: 20 -> 20; matrix products, arithmetic and copies ran while one was open for 0% -> 0% of each run, Pallas kernels for 19% -> 20%
where the time goes in v15:
time: 113 us
  waiting for transfers between devices  41.6 us (37%)
  starting transfers between devices  40.2 us (36%)
  Pallas kernels  23.6 us (21%)
  local copies, waits for them, and re-layouts  6.98 us (6%)
    ppermute x35, waiting for transfers between devices, swap(): return lax.ppermute(value, axis, [(i, i ^ step) for i in range(count)])  28.7 us
    ppermute x35, starting transfers between devices, swap(): return lax.ppermute(value, axis, [(i, i ^ step) for i in range(count)])  26.1 us
    pallas_call x29, Pallas kernels, small(): pl.pallas_call(kernel, out_shape=[out if hasattr(out, 'dtype') else jax.S...  23.6 us
    ppermute x6, starting transfers between devices, along_line(): lax.ppermute(value, 'expert', [(i, (i + 4 * shift) % count) for i in rang...  14.1 us
    ppermute x6, waiting for transfers between devices, along_line(): lax.ppermute(value, 'expert', [(i, (i + 4 * shift) % count) for i in rang...  12.9 us
    unnamed x20, local copies, waits for them, and re-layouts  6.98 us
  transfers between devices with their start and end apart: 41, of which 20 were waited for; matrix products, arithmetic and copies ran while one was open for 0% of the time, Pallas kernels for 20%

profile of v15, /device:TPU:0, one launch (start us, length us, event | category | flops | bytes accessed | tf_op | source)
XLA Modules:
  0.0 112.7 jit_solution(4810875719616404867)
XLA Ops:
  0.1 1.0 copy-done.3
  1.1 0.7 copy-done.8
  1.8 0.7 copy-done.9
  2.5 0.6 prepare.1
  3.1 4.1 %collective-permute-start.1 = (bf16[64,2176]{1,0:T(8,128)(2,1)S(1)}, bf16[64,2176]{1,0:T(8,128)(2,1)S(1)}, u32[]{:S(2)}, u32[]{:S(2)}) collective-permute-start(bf16[64,2176]{1,0:T(8,128)(2,1)S(1)} %get-tuple-element.56.part), channel_id=1, source_target_pairs={{0,16},{2,18},{4,20},{6,22},{8,24},{10,26},{12,28},{14,30},{16,0},... | collective-permute-start | bytes 835592 | tf_op jit(solution)/shard_map/ppermute | solution.py:71
  7.2 1.5 %collective-permute-start.5 = (bf16[64,2176]{1,0:T(8,128)(2,1)S(1)}, bf16[64,2176]{1,0:T(8,128)(2,1)S(1)}, u32[]{:S(2)}, u32[]{:S(2)}) collective-permute-start(bf16[64,2176]{1,0:T(8,128)(2,1)S(1)} %get-tuple-element.56.part), channel_id=1, source_target_pairs={{0,4},{2,6},{4,0},{6,2},{8,12},{10,14},{12,8},{14,10},{16,20},{18,... | collective-permute-start | bytes 835592 | tf_op jit(solution)/shard_map/ppermute | solution.py:66
  8.7 11.1 %collective-permute-done.1.came = bf16[64,2176]{1,0:T(8,128)(2,1)S(1)} collective-permute-done((bf16[64,2176]{1,0:T(8,128)(2,1)S(1)}, bf16[64,2176]{1,0:T(8,128)(2,1)S(1)}, u32[]{:S(2)}, u32[]{:S(2)}) %collective-permute-start.1) | collective-permute-done | bytes 278560 | tf_op jit(solution)/shard_map/ppermute | solution.py:71
  19.9 1.6 %collective-permute-start.3 = (bf16[1,64,2176]{2,1,0:T(8,128)(2,1)S(1)}, bf16[1,64,2176]{2,1,0:T(8,128)(2,1)S(1)}, u32[]{:S(2)}, u32[]{:S(2)}) collective-permute-start(bf16[1,64,2176]{2,1,0:T(8,128)(2,1)S(1)} %get-tuple-element.57.lines._), channel_id=1, source_target_pairs={{0,1},{1,0},{2,3},{3,2},{4,5},{5,4},{6,7},{7,6},{8,9},{9,8},{10,11... | collective-permute-start | bytes 835592 | tf_op jit(solution)/shard_map/ppermute | solution.py:66
  21.5 1.5 %collective-permute-start.6 = (bf16[1,64,2176]{2,1,0:T(8,128)(2,1)S(1)}, bf16[1,64,2176]{2,1,0:T(8,128)(2,1)S(1)}, u32[]{:S(2)}, u32[]{:S(2)}) collective-permute-start(bf16[1,64,2176]{2,1,0:T(8,128)(2,1)S(1)} %get-tuple-element.57.lines._), channel_id=1, source_target_pairs={{0,4},{2,6},{4,0},{6,2},{8,12},{10,14},{12,8},{14,10},{16,20},{18,... | collective-permute-start | bytes 835592 | tf_op jit(solution)/shard_map/ppermute | solution.py:66
  23.0 3.5 %collective-permute-start.12 = (bf16[64,2176]{1,0:T(8,128)(2,1)S(1)}, bf16[64,2176]{1,0:T(8,128)(2,1)S(1)}, u32[]{:S(2)}, u32[]{:S(2)}) collective-permute-start(bf16[64,2176]{1,0:T(8,128)(2,1)S(1)} %get-tuple-element.66), channel_id=1, source_target_pairs={{0,24},{2,26},{4,28},{6,30},{8,0},{10,2},{12,4},{14,6},{16,8},{18,... | collective-permute-start | bytes 835592 | tf_op jit(solution)/shard_map/ppermute | solution.py:71
  26.5 1.3 %collective-permute-done.3.side = bf16[1,64,2176]{2,1,0:T(8,128)(2,1)S(1)} collective-permute-done((bf16[1,64,2176]{2,1,0:T(8,128)(2,1)S(1)}, bf16[1,64,2176]{2,1,0:T(8,128)(2,1)S(1)}, u32[]{:S(2)}, u32[]{:S(2)}) %collective-permute-start.3) | collective-permute-done | bytes 278560 | tf_op jit(solution)/shard_map/ppermute | solution.py:66
  27.8 1.0 collective-permute-done.6.over
  28.8 1.0 copy-done.4
  29.8 0.6 own_corner.1
  30.5 0.8 collective-permute-start.8
  31.3 1.3 %collective-permute-start.9 = (bf16[2,64,1024]{2,1,0:T(8,128)(2,1)S(1)}, bf16[2,64,1024]{2,1,0:T(8,128)(2,1)S(1)}, u32[]{:S(2)}, u32[]{:S(2)}) collective-permute-start(bf16[2,64,1024]{2,1,0:T(8,128)(2,1)S(1)} %get-tuple-element.60), channel_id=1, source_target_pairs={{0,4},{2,6},{4,0},{6,2},{8,12},{10,14},{12,8},{14,10},{16,20},{18,... | collective-permute-start | bytes 786440 | tf_op jit(solution)/shard_map/ppermute | solution.py:66
  32.6 1.3 %copy-done.6 = bf16[2,384,768]{2,1,0:T(8,128)(2,1)S(1)} copy-done((bf16[2,384,768]{2,1,0:T(8,128)(2,1)S(1)}, bf16[2,384,768]{2,1,0:T(8,128)(2,1)}, u32[]{:S(2)}) %copy-start.6) | copy-done | bytes 1179672
  33.8 1.3 %copy-done.7 = bf16[2,384,768]{2,1,0:T(8,128)(2,1)S(1)} copy-done((bf16[2,384,768]{2,1,0:T(8,128)(2,1)S(1)}, bf16[2,384,768]{2,1,0:T(8,128)(2,1)}, u32[]{:S(2)}) %copy-start.7) | copy-done | bytes 1179672
  35.1 1.3 %turn.1 = (f32[2,768,384]{2,1,0:T(8,128)S(1)}, f32[2,768,384]{2,1,0:T(8,128)S(1)}) custom-call(bf16[2,384,768]{2,1,0:T(8,128)(2,1)S(1)} %copy-done.6, bf16[2,384,768]{2,1,0:T(8,128)(2,1)S(1)} %copy-done.7, bf16[1,64,2176]{2,1,0:T(8,128)(2,1)S(1)} %get-tuple-element.57.lines._), custom_call_target="tpu_custom_call" | custom-call | tf_op jit(solution)/shard_map/turn/pallas_call | solution.py:76
  36.4 0.6 collective-permute-start.2
  37.0 1.8 %collective-permute-done.13.refs_1_ = bf16[64,2176]{1,0:T(8,128)(2,1)S(1)} collective-permute-done((bf16[64,2176]{1,0:T(8,128)(2,1)S(1)}, bf16[64,2176]{1,0:T(8,128)(2,1)S(1)}, u32[]{:S(2)}, u32[]{:S(2)}) %collective-permute-start.13) | collective-permute-done | bytes 278560 | tf_op jit(solution)/shard_map/ppermute | solution.py:71
  38.8 0.6 collective-permute-start.15
  39.4 0.5 collective-permute-start.16
  40.0 1.0 copy-done.5
  42.0 1.1 route.2
  43.1 0.9 collective-permute-done.4.side_c
  44.0 3.9 %hidden.2.grads._ = bf16[2,384,768]{2,1,0:T(8,128)(2,1)S(1)} custom-call(s32[4]{0:T(128)S(1)} %pad_add_fusion.place, bf16[128,2048]{1,0:T(8,128)(2,1)S(1)} %copy-done.5, bf16[128,2048]{1,0:T(8,128)(2,1)S(1)} %collective-permute-done.own_c, bf16[1,64,2176]{2,1,0:T(8,128)(2,1)S(1)} %get-tuple-element.57.lines._, ...), custom_call_target="tpu_custom_call" | custom-call | tf_op jit(solution)/shard_map/hidden/pallas_call | solution.py:76
  47.9 2.2 %sums.4 = (bf16[4,128,1024]{2,1,0:T(8,128)(2,1)S(1)}, bf16[4,128,1024]{2,1,0:T(8,128)(2,1)S(1)}) custom-call(bf16[2,384,768]{2,1,0:T(8,128)(2,1)S(1)} %hidden.2.grads._, bf16[2,384,2048]{2,1,0:T(8,128)(2,1)S(1)} %copy-done, bf16[2,384,2048]{2,1,0:T(8,128)(2,1)S(1)} %copy-done.1, bf16[4,256,192]{2,1,0:T(8,128)(2,1)S(1)} %get-tuple-element.67.pick_t, ...), custom_call_target="tpu_custom_call" | custom-call | tf_op jit(solution)/shard_map/sums/pallas_call | solution.py:76
  50.4 1.8 %collective-permute-done.15.over = bf16[2,64,2176]{2,1,0:T(8,128)(2,1)S(1)} collective-permute-done((bf16[2,64,2176]{2,1,0:T(8,128)(2,1)S(1)}, bf16[2,64,2176]{2,1,0:T(8,128)(2,1)S(1)}, u32[]{:S(2)}, u32[]{:S(2)}) %collective-permute-start.15) | collective-permute-done | bytes 557088 | tf_op jit(solution)/shard_map/ppermute | solution.py:66
  52.5 1.0 collective-permute-start.17
  53.5 1.5 %collective-permute-start.18 = (bf16[2,64,1024]{2,1,0:T(8,128)(2,1)S(1)}, bf16[2,64,1024]{2,1,0:T(8,128)(2,1)S(1)}, u32[]{:S(2)}, u32[]{:S(2)}) collective-permute-start(bf16[2,64,1024]{2,1,0:T(8,128)(2,1)S(1)} %get-tuple-element.71), channel_id=1, source_target_pairs={{0,4},{2,6},{4,0},{6,2},{8,12},{10,14},{12,8},{14,10},{16,20},{18,... | collective-permute-start | bytes 786440 | tf_op jit(solution)/shard_map/ppermute | solution.py:66
  55.0 2.2 %sums.5 = (bf16[4,128,1024]{2,1,0:T(8,128)(2,1)S(1)}, bf16[4,128,1024]{2,1,0:T(8,128)(2,1)S(1)}) custom-call(bf16[2,384,768]{2,1,0:T(8,128)(2,1)S(1)} %hidden.2.grads._, bf16[2,384,2048]{2,1,0:T(8,128)(2,1)S(1)} %copy-done, bf16[2,384,2048]{2,1,0:T(8,128)(2,1)S(1)} %copy-done.1, bf16[4,256,192]{2,1,0:T(8,128)(2,1)S(1)} %get-tuple-element.67.pick_t, ...), custom_call_target="tpu_custom_call" | custom-call | flops 68719476736 | bytes 268435456 | tf_op jit(solution)/shard_map/sums/pallas_call | solution.py:76
  57.8 1.3 %collective-permute-done.17.left = bf16[2,64,1024]{2,1,0:T(8,128)(2,1)S(1)} collective-permute-done((bf16[2,64,1024]{2,1,0:T(8,128)(2,1)S(1)}, bf16[2,64,1024]{2,1,0:T(8,128)(2,1)S(1)}, u32[]{:S(2)}, u32[]{:S(2)}) %collective-permute-start.17) | collective-permute-done | bytes 262176 | tf_op jit(solution)/shard_map/ppermute | solution.py:66
  59.1 1.2 %collective-permute-done.18.right = bf16[2,64,1024]{2,1,0:T(8,128)(2,1)S(1)} collective-permute-done((bf16[2,64,1024]{2,1,0:T(8,128)(2,1)S(1)}, bf16[2,64,1024]{2,1,0:T(8,128)(2,1)S(1)}, u32[]{:S(2)}, u32[]{:S(2)}) %collective-permute-start.18) | collective-permute-done | bytes 262176 | tf_op jit(solution)/shard_map/ppermute | solution.py:66
  60.4 0.6 collective-permute-start.28
  61.1 0.7 collective-permute-start.19
  61.9 1.6 %collective-permute-start.21 = (bf16[2,128,1024]{2,1,0:T(8,128)(2,1)S(1)}, bf16[2,128,1024]{2,1,0:T(8,128)(2,1)S(1)}, u32[]{:S(2)}, u32[]{:S(2)}) collective-permute-start(bf16[2,128,1024]{2,1,0:T(8,128)(2,1)S(1)} %get-tuple-element.77._), channel_id=1, source_target_pairs={{0,4},{2,6},{4,0},{6,2},{8,12},{10,14},{12,8},{14,10},{16,20},{18,... | collective-permute-start | bytes 1572872 | tf_op jit(solution)/shard_map/ppermute | solution.py:66
  63.5 1.1 route.3
  64.7 3.9 %hidden.3.grads._ = bf16[2,384,768]{2,1,0:T(8,128)(2,1)S(1)} custom-call(s32[4]{0:T(128)S(1)} %pad_add_fusion.place, bf16[128,2048]{1,0:T(8,128)(2,1)S(1)} %copy-done.5, bf16[128,2048]{1,0:T(8,128)(2,1)S(1)} %collective-permute-done.own_c, bf16[2,64,2176]{2,1,0:T(8,128)(2,1)S(1)} %stack.21._.lines, bf16[2,64,2176]{2,1,0:T(8,128)(2,1)S(1)} %collective-permute-done.25.lines_c, ...), custom_call_target="tpu_custom_call" | custom-call | tf_op jit(solution)/shard_map/hidden/pallas_call | solution.py:76
  68.5 2.2 %sums.6 = (bf16[4,128,1024]{2,1,0:T(8,128)(2,1)S(1)}, bf16[4,128,1024]{2,1,0:T(8,128)(2,1)S(1)}) custom-call(bf16[2,384,768]{2,1,0:T(8,128)(2,1)S(1)} %hidden.3.grads._, bf16[2,384,2048]{2,1,0:T(8,128)(2,1)S(1)} %copy-done, bf16[2,384,2048]{2,1,0:T(8,128)(2,1)S(1)} %copy-done.1, bf16[4,256,192]{2,1,0:T(8,128)(2,1)S(1)} %get-tuple-element.84.pick_t, ...), custom_call_target="tpu_custom_call" | custom-call | tf_op jit(solution)/shard_map/sums/pallas_call | solution.py:76
  70.9 2.2 %sums.7 = (bf16[4,128,1024]{2,1,0:T(8,128)(2,1)S(1)}, bf16[4,128,1024]{2,1,0:T(8,128)(2,1)S(1)}) custom-call(bf16[2,384,768]{2,1,0:T(8,128)(2,1)S(1)} %hidden.3.grads._, bf16[2,384,2048]{2,1,0:T(8,128)(2,1)S(1)} %copy-done, bf16[2,384,2048]{2,1,0:T(8,128)(2,1)S(1)} %copy-done.1, bf16[4,256,192]{2,1,0:T(8,128)(2,1)S(1)} %get-tuple-element.84.pick_t, ...), custom_call_target="tpu_custom_call" | custom-call | tf_op jit(solution)/shard_map/sums/pallas_call | solution.py:76
  73.1 0.6 collective-permute-start.31
  73.7 1.3 %collective-permute-done.19.came_l = bf16[4,64,1024]{2,1,0:T(8,128)(2,1)S(1)} collective-permute-done((bf16[4,64,1024]{2,1,0:T(8,128)(2,1)S(1)}, bf16[4,64,1024]{2,1,0:T(8,128)(2,1)S(1)}, u32[]{:S(2)}, u32[]{:S(2)}) %collective-permute-start.19) | collective-permute-done | bytes 524320 | tf_op jit(solution)/shard_map/ppermute | solution.py:66
  75.0 0.7 collective-permute-done.21.came_r
  75.8 1.6 %collective-permute-start.22 = (bf16[64,1024]{1,0:T(8,128)(2,1)S(1)}, bf16[64,1024]{1,0:T(8,128)(2,1)S(1)}, u32[]{:S(2)}, u32[]{:S(2)}) collective-permute-start(bf16[64,1024]{1,0:T(8,128)(2,1)S(1)} %get-tuple-element.79._), channel_id=1, source_target_pairs={{0,4},{2,6},{4,0},{6,2},{8,12},{10,14},{12,8},{14,10},{16,20},{18,... | collective-permute-start | bytes 393224 | tf_op jit(solution)/shard_map/ppermute | solution.py:66
  77.4 1.3 %collective-permute-start.23 = (bf16[64,1024]{1,0:T(8,128)(2,1)S(1)}, bf16[64,1024]{1,0:T(8,128)(2,1)S(1)}, u32[]{:S(2)}, u32[]{:S(2)}) collective-permute-start(bf16[64,1024]{1,0:T(8,128)(2,1)S(1)} %get-tuple-element.81), channel_id=1, source_target_pairs={{0,1},{1,0},{2,3},{3,2},{4,5},{5,4},{6,7},{7,6},{8,9},{9,8},{10,11... | collective-permute-start | bytes 393224 | tf_op jit(solution)/shard_map/ppermute | solution.py:66
  78.8 0.8 collective-permute-start.30
  79.7 0.6 collective-permute-start.32
  80.3 0.9 collective-permute-done.22.came_l
  81.2 2.6 %collective-permute-done.23.came_r = bf16[64,1024]{1,0:T(8,128)(2,1)S(1)} collective-permute-done((bf16[64,1024]{1,0:T(8,128)(2,1)S(1)}, bf16[64,1024]{1,0:T(8,128)(2,1)S(1)}, u32[]{:S(2)}, u32[]{:S(2)}) %collective-permute-start.23) | collective-permute-done | bytes 131104 | tf_op jit(solution)/shard_map/ppermute | solution.py:66
  84.1 8.7 %collective-permute-done.30.came_l = bf16[4,64,1024]{2,1,0:T(8,128)(2,1)S(1)} collective-permute-done((bf16[4,64,1024]{2,1,0:T(8,128)(2,1)S(1)}, bf16[4,64,1024]{2,1,0:T(8,128)(2,1)S(1)}, u32[]{:S(2)}, u32[]{:S(2)}) %collective-permute-start.30) | collective-permute-done | bytes 524320 | tf_op jit(solution)/shard_map/ppermute | solution.py:66
  92.9 0.9 collective-permute-start.33
  93.8 1.2 %collective-permute-start.34 = (bf16[64,1024]{1,0:T(8,128)(2,1)S(1)}, bf16[64,1024]{1,0:T(8,128)(2,1)S(1)}, u32[]{:S(2)}, u32[]{:S(2)}) collective-permute-start(bf16[64,1024]{1,0:T(8,128)(2,1)S(1)} %get-tuple-element.96), channel_id=1, source_target_pairs={{0,1},{1,0},{2,3},{3,2},{4,5},{5,4},{6,7},{7,6},{8,9},{9,8},{10,11... | collective-permute-start | bytes 393224 | tf_op jit(solution)/shard_map/ppermute | solution.py:66
  95.0 1.1 collective-permute-start.36
  96.1 0.9 collective-permute-start.37
  97.0 1.4 %collective-permute-done.33.came_l = bf16[64,1024]{1,0:T(8,128)(2,1)S(1)} collective-permute-done((bf16[64,1024]{1,0:T(8,128)(2,1)S(1)}, bf16[64,1024]{1,0:T(8,128)(2,1)S(1)}, u32[]{:S(2)}, u32[]{:S(2)}) %collective-permute-start.33) | collective-permute-done | bytes 131104 | tf_op jit(solution)/shard_map/ppermute | solution.py:66
  98.3 0.5 collective-permute-done.34.came_r
  98.9 1.8 %collective-permute-start.35 = (bf16[64,2048]{1,0:T(8,128)(2,1)S(1)}, bf16[64,2048]{1,0:T(8,128)(2,1)S(1)}, u32[]{:S(2)}, u32[]{:S(2)}) collective-permute-start(bf16[64,2048]{1,0:T(8,128)(2,1)S(1)} %third_sum.5._), channel_id=1, source_target_pairs={{0,8},{2,10},{4,12},{6,14},{8,16},{10,18},{12,20},{14,22},{16,24},... | collective-permute-start | bytes 786440 | tf_op jit(solution)/shard_map/ppermute | solution.py:71
  101.1 4.5 %collective-permute-start.40 = (bf16[64,2048]{1,0:T(8,128)(2,1)S(1)}, bf16[64,2048]{1,0:T(8,128)(2,1)S(1)}, u32[]{:S(2)}, u32[]{:S(2)}) collective-permute-start(bf16[64,2048]{1,0:T(8,128)(2,1)S(1)} %third_sum.6.refs_2_._), channel_id=1, source_target_pairs={{0,24},{2,26},{4,28},{6,30},{8,0},{10,2},{12,4},{14,6},{16,8},{18,... | collective-permute-start | bytes 786440 | tf_op jit(solution)/shard_map/ppermute | solution.py:71
  105.7 1.1 collective-permute-start.38
  106.7 0.8 collective-permute-start.39
  107.5 3.2 %collective-permute-done.38.came_l = bf16[64,1024]{1,0:T(8,128)(2,1)S(1)} collective-permute-done((bf16[64,1024]{1,0:T(8,128)(2,1)S(1)}, bf16[64,1024]{1,0:T(8,128)(2,1)S(1)}, u32[]{:S(2)}, u32[]{:S(2)}) %collective-permute-start.38) | collective-permute-done | bytes 131104 | tf_op jit(solution)/shard_map/ppermute | solution.py:66
  110.7 1.0 collective-permute-done.39.came_r
  111.8 0.9 last_sum.1
  (68 shorter events, 4.0 us)
Async XLA Ops:
  0.1 1.0 copy-start.3
  1.1 0.7 copy-start.8
  1.8 0.7 copy-start.9
  3.1 16.7 %collective-permute-start.1 = (bf16[64,2176]{1,0:T(8,128)(2,1)S(1)}, bf16[64,2176]{1,0:T(8,128)(2,1)S(1)}, u32[]{:S(2)}, u32[]{:S(2)}) collective-permute-start(bf16[64,2176]{1,0:T(8,128)(2,1)S(1)} %get-tuple-element.56.part), channel_id=1, source_target_pairs={{0,16},{2,18},{4,20},{6,22},{8,24},{10,26},{12,28},{14,30},{16,0},... | collective-permute-start | bytes 835592 | tf_op jit(solution)/shard_map/ppermute | solution.py:71
  7.2 19.3 %collective-permute-start.5 = (bf16[64,2176]{1,0:T(8,128)(2,1)S(1)}, bf16[64,2176]{1,0:T(8,128)(2,1)S(1)}, u32[]{:S(2)}, u32[]{:S(2)}) collective-permute-start(bf16[64,2176]{1,0:T(8,128)(2,1)S(1)} %get-tuple-element.56.part), channel_id=1, source_target_pairs={{0,4},{2,6},{4,0},{6,2},{8,12},{10,14},{12,8},{14,10},{16,20},{18,... | collective-permute-start | bytes 835592 | tf_op jit(solution)/shard_map/ppermute | solution.py:66
  19.9 7.9 %collective-permute-start.3 = (bf16[1,64,2176]{2,1,0:T(8,128)(2,1)S(1)}, bf16[1,64,2176]{2,1,0:T(8,128)(2,1)S(1)}, u32[]{:S(2)}, u32[]{:S(2)}) collective-permute-start(bf16[1,64,2176]{2,1,0:T(8,128)(2,1)S(1)} %get-tuple-element.57.lines._), channel_id=1, source_target_pairs={{0,1},{1,0},{2,3},{3,2},{4,5},{5,4},{6,7},{7,6},{8,9},{9,8},{10,11... | collective-permute-start | bytes 835592 | tf_op jit(solution)/shard_map/ppermute | solution.py:66
  21.5 7.3 %collective-permute-start.6 = (bf16[1,64,2176]{2,1,0:T(8,128)(2,1)S(1)}, bf16[1,64,2176]{2,1,0:T(8,128)(2,1)S(1)}, u32[]{:S(2)}, u32[]{:S(2)}) collective-permute-start(bf16[1,64,2176]{2,1,0:T(8,128)(2,1)S(1)} %get-tuple-element.57.lines._), channel_id=1, source_target_pairs={{0,4},{2,6},{4,0},{6,2},{8,12},{10,14},{12,8},{14,10},{16,20},{18,... | collective-permute-start | bytes 835592 | tf_op jit(solution)/shard_map/ppermute | solution.py:66
  23.0 13.4 %collective-permute-start.12 = (bf16[64,2176]{1,0:T(8,128)(2,1)S(1)}, bf16[64,2176]{1,0:T(8,128)(2,1)S(1)}, u32[]{:S(2)}, u32[]{:S(2)}) collective-permute-start(bf16[64,2176]{1,0:T(8,128)(2,1)S(1)} %get-tuple-element.66), channel_id=1, source_target_pairs={{0,24},{2,26},{4,28},{6,30},{8,0},{10,2},{12,4},{14,6},{16,8},{18,... | collective-permute-start | bytes 835592 | tf_op jit(solution)/shard_map/ppermute | solution.py:71
  26.5 12.2 %collective-permute-start.13 = (bf16[64,2176]{1,0:T(8,128)(2,1)S(1)}, bf16[64,2176]{1,0:T(8,128)(2,1)S(1)}, u32[]{:S(2)}, u32[]{:S(2)}) collective-permute-start(bf16[64,2176]{1,0:T(8,128)(2,1)S(1)} %get-tuple-element.66), channel_id=1, source_target_pairs={{0,8},{2,10},{4,12},{6,14},{8,16},{10,18},{12,20},{14,22},{16,24},... | collective-permute-start | bytes 835592 | tf_op jit(solution)/shard_map/ppermute | solution.py:71
  28.8 1.0 copy-start.4
  30.5 8.9 %collective-permute-start.8 = (bf16[2,64,1024]{2,1,0:T(8,128)(2,1)S(1)}, bf16[2,64,1024]{2,1,0:T(8,128)(2,1)S(1)}, u32[]{:S(2)}, u32[]{:S(2)}) collective-permute-start(bf16[2,64,1024]{2,1,0:T(8,128)(2,1)S(1)} %get-tuple-element.59.refs_0_), channel_id=1, source_target_pairs={{0,1},{1,0},{2,3},{3,2},{4,5},{5,4},{6,7},{7,6},{8,9},{9,8},{10,11... | collective-permute-start | bytes 786440 | tf_op jit(solution)/shard_map/ppermute | solution.py:66
  31.3 8.6 %collective-permute-start.9 = (bf16[2,64,1024]{2,1,0:T(8,128)(2,1)S(1)}, bf16[2,64,1024]{2,1,0:T(8,128)(2,1)S(1)}, u32[]{:S(2)}, u32[]{:S(2)}) collective-permute-start(bf16[2,64,1024]{2,1,0:T(8,128)(2,1)S(1)} %get-tuple-element.60), channel_id=1, source_target_pairs={{0,4},{2,6},{4,0},{6,2},{8,12},{10,14},{12,8},{14,10},{16,20},{18,... | collective-permute-start | bytes 786440 | tf_op jit(solution)/shard_map/ppermute | solution.py:66
  32.6 7.4 %collective-permute-start.11 = (bf16[64,128]{1,0:T(8,128)(2,1)S(1)}, bf16[64,128]{1,0:T(8,128)(2,1)S(1)}, u32[]{:S(2)}, u32[]{:S(2)}) collective-permute-start(bf16[64,128]{1,0:T(8,128)(2,1)S(1)} %get-tuple-element.61.own), channel_id=1, source_target_pairs={{0,2},{2,0},{4,6},{6,4},{8,10},{10,8},{12,14},{14,12},{16,18},{18,... | collective-permute-start | bytes 49160 | tf_op jit(solution)/shard_map/ppermute | solution.py:66
  32.6 1.3 %copy-start.6 = (bf16[2,384,768]{2,1,0:T(8,128)(2,1)S(1)}, bf16[2,384,768]{2,1,0:T(8,128)(2,1)}, u32[]{:S(2)}) copy-start(bf16[2,384,768]{2,1,0:T(8,128)(2,1)} %gate.1) | copy-start | bytes 3538948
  33.8 1.3 %copy-start.7 = (bf16[2,384,768]{2,1,0:T(8,128)(2,1)S(1)}, bf16[2,384,768]{2,1,0:T(8,128)(2,1)}, u32[]{:S(2)}) copy-start(bf16[2,384,768]{2,1,0:T(8,128)(2,1)} %up.1) | copy-start | bytes 3538948
  36.4 4.5 %collective-permute-start.2 = (bf16[1,64,2176]{2,1,0:T(8,128)(2,1)S(1)}, bf16[1,64,2176]{2,1,0:T(8,128)(2,1)S(1)}, u32[]{:S(2)}, u32[]{:S(2)}) collective-permute-start(bf16[1,64,2176]{2,1,0:T(8,128)(2,1)S(1)} %get-tuple-element.57.lines._), channel_id=1, source_target_pairs={{0,2},{2,0},{4,6},{6,4},{8,10},{10,8},{12,14},{14,12},{16,18},{18,... | collective-permute-start | bytes 835592 | tf_op jit(solution)/shard_map/ppermute | solution.py:66
  38.8 13.4 %collective-permute-start.15 = (bf16[2,64,2176]{2,1,0:T(8,128)(2,1)S(1)}, bf16[2,64,2176]{2,1,0:T(8,128)(2,1)S(1)}, u32[]{:S(2)}, u32[]{:S(2)}) collective-permute-start(bf16[2,64,2176]{2,1,0:T(8,128)(2,1)S(1)} %stack.21._.lines), channel_id=1, source_target_pairs={{0,4},{2,6},{4,0},{6,2},{8,12},{10,14},{12,8},{14,10},{16,20},{18,... | collective-permute-start | bytes 1671176 | tf_op jit(solution)/shard_map/ppermute | solution.py:66
  39.4 13.1 %collective-permute-start.16 = (bf16[2,64,2176]{2,1,0:T(8,128)(2,1)S(1)}, bf16[2,64,2176]{2,1,0:T(8,128)(2,1)S(1)}, u32[]{:S(2)}, u32[]{:S(2)}) collective-permute-start(bf16[2,64,2176]{2,1,0:T(8,128)(2,1)S(1)} %stack.21._.lines), channel_id=1, source_target_pairs={{0,1},{1,0},{2,3},{3,2},{4,5},{5,4},{6,7},{7,6},{8,9},{9,8},{10,11... | collective-permute-start | bytes 1671176 | tf_op jit(solution)/shard_map/ppermute | solution.py:66
  39.9 1.0 copy-start.5
  39.9 2.0 %collective-permute-start.7 = (bf16[2,64,2176]{2,1,0:T(8,128)(2,1)S(1)}, bf16[2,64,2176]{2,1,0:T(8,128)(2,1)S(1)}, u32[]{:S(2)}, u32[]{:S(2)}) collective-permute-start(bf16[2,64,2176]{2,1,0:T(8,128)(2,1)S(1)} %get-tuple-element.58.over), channel_id=1, source_target_pairs={{0,2},{2,0},{4,6},{6,4},{8,10},{10,8},{12,14},{14,12},{16,18},{18,... | collective-permute-start | bytes 1671176 | tf_op jit(solution)/shard_map/ppermute | solution.py:66
  39.9 4.1 %copy-start.2 = (bf16[2,384,2048]{2,1,0:T(8,128)(2,1)S(1)}, bf16[2,384,2048]{2,1,0:T(8,128)(2,1)}, u32[]{:S(2)}) copy-start(bf16[2,384,2048]{2,1,0:T(8,128)(2,1)} %w_down.3) | copy-start | bytes 9437188
  40.9 2.2 %collective-permute-start = (bf16[128,2048]{1,0:T(8,128)(2,1)S(1)}, bf16[128,2048]{1,0:T(8,128)(2,1)S(1)}, u32[]{:S(2)}, u32[]{:S(2)}) collective-permute-start(bf16[128,2048]{1,0:T(8,128)(2,1)S(1)} %copy-done.5), channel_id=1, source_target_pairs={{0,2},{2,0},{4,6},{6,4},{8,10},{10,8},{12,14},{14,12},{16,18},{18,... | collective-permute-start | bytes 1572872 | tf_op jit(solution)/shard_map/ppermute | solution.py:66
  41.0 3.1 %collective-permute-start.10 = (bf16[2,64,2048]{2,1,0:T(8,128)(2,1)S(1)}, bf16[2,64,2048]{2,1,0:T(8,128)(2,1)S(1)}, u32[]{:S(2)}, u32[]{:S(2)}) collective-permute-start(bf16[2,64,2048]{2,1,0:T(8,128)(2,1)S(1)} %join.2.diag), channel_id=1, source_target_pairs={{0,2},{2,0},{4,6},{6,4},{8,10},{10,8},{12,14},{14,12},{16,18},{18,... | collective-permute-start | bytes 1572872 | tf_op jit(solution)/shard_map/ppermute | solution.py:66
  41.9 2.1 %collective-permute-start.4 = (bf16[1,64,2176]{2,1,0:T(8,128)(2,1)S(1)}, bf16[1,64,2176]{2,1,0:T(8,128)(2,1)S(1)}, u32[]{:S(2)}, u32[]{:S(2)}) collective-permute-start(bf16[1,64,2176]{2,1,0:T(8,128)(2,1)S(1)} %collective-permute-done.3.side), channel_id=1, source_target_pairs={{0,2},{2,0},{4,6},{6,4},{8,10},{10,8},{12,14},{14,12},{16,18},{18,... | collective-permute-start | bytes 835592 | tf_op jit(solution)/shard_map/ppermute | solution.py:66
  44.0 3.9 %copy-start = (bf16[2,384,2048]{2,1,0:T(8,128)(2,1)S(1)}, bf16[2,384,2048]{2,1,0:T(8,128)(2,1)}, u32[]{:S(2)}) copy-start(bf16[2,384,2048]{2,1,0:T(8,128)(2,1)} %w_gate.7) | copy-start | bytes 9437188
  44.0 3.9 %copy-start.1 = (bf16[2,384,2048]{2,1,0:T(8,128)(2,1)S(1)}, bf16[2,384,2048]{2,1,0:T(8,128)(2,1)}, u32[]{:S(2)}) copy-start(bf16[2,384,2048]{2,1,0:T(8,128)(2,1)} %w_up.7) | copy-start | bytes 9437188
  50.2 10.2 %collective-permute-start.14 = (bf16[4,128,1024]{2,1,0:T(8,128)(2,1)S(1)}, bf16[4,128,1024]{2,1,0:T(8,128)(2,1)S(1)}, u32[]{:S(2)}, u32[]{:S(2)}) collective-permute-start(bf16[4,128,1024]{2,1,0:T(8,128)(2,1)S(1)} %get-tuple-element.69._), channel_id=1, source_target_pairs={{0,2},{2,0},{4,6},{6,4},{8,10},{10,8},{12,14},{14,12},{16,18},{18,... | collective-permute-start | bytes 3145736 | tf_op jit(solution)/shard_map/ppermute | solution.py:66
  52.5 6.6 %collective-permute-start.17 = (bf16[2,64,1024]{2,1,0:T(8,128)(2,1)S(1)}, bf16[2,64,1024]{2,1,0:T(8,128)(2,1)S(1)}, u32[]{:S(2)}, u32[]{:S(2)}) collective-permute-start(bf16[2,64,1024]{2,1,0:T(8,128)(2,1)S(1)} %get-tuple-element.70._), channel_id=1, source_target_pairs={{0,1},{1,0},{2,3},{3,2},{4,5},{5,4},{6,7},{7,6},{8,9},{9,8},{10,11... | collective-permute-start | bytes 786440 | tf_op jit(solution)/shard_map/ppermute | solution.py:66
  53.5 6.8 %collective-permute-start.18 = (bf16[2,64,1024]{2,1,0:T(8,128)(2,1)S(1)}, bf16[2,64,1024]{2,1,0:T(8,128)(2,1)S(1)}, u32[]{:S(2)}, u32[]{:S(2)}) collective-permute-start(bf16[2,64,1024]{2,1,0:T(8,128)(2,1)S(1)} %get-tuple-element.71), channel_id=1, source_target_pairs={{0,4},{2,6},{4,0},{6,2},{8,12},{10,14},{12,8},{14,10},{16,20},{18,... | collective-permute-start | bytes 786440 | tf_op jit(solution)/shard_map/ppermute | solution.py:66
  57.3 3.8 %collective-permute-start.20 = (bf16[4,128,1024]{2,1,0:T(8,128)(2,1)S(1)}, bf16[4,128,1024]{2,1,0:T(8,128)(2,1)S(1)}, u32[]{:S(2)}, u32[]{:S(2)}) collective-permute-start(bf16[4,128,1024]{2,1,0:T(8,128)(2,1)S(1)} %get-tuple-element.72.refs_0_), channel_id=1, source_target_pairs={{0,2},{2,0},{4,6},{6,4},{8,10},{10,8},{12,14},{14,12},{16,18},{18,... | collective-permute-start | bytes 3145736 | tf_op jit(solution)/shard_map/ppermute | solution.py:66
  57.3 4.6 %collective-permute-start.25 = (bf16[2,64,2176]{2,1,0:T(8,128)(2,1)S(1)}, bf16[2,64,2176]{2,1,0:T(8,128)(2,1)S(1)}, u32[]{:S(2)}, u32[]{:S(2)}) collective-permute-start(bf16[2,64,2176]{2,1,0:T(8,128)(2,1)S(1)} %stack.21._.lines), channel_id=1, source_target_pairs={{0,2},{2,0},{4,6},{6,4},{8,10},{10,8},{12,14},{14,12},{16,18},{18,... | collective-permute-start | bytes 1671176 | tf_op jit(solution)/shard_map/ppermute | solution.py:66
  59.1 5.6 %collective-permute-start.26 = (bf16[2,64,2176]{2,1,0:T(8,128)(2,1)S(1)}, bf16[2,64,2176]{2,1,0:T(8,128)(2,1)S(1)}, u32[]{:S(2)}, u32[]{:S(2)}) collective-permute-start(bf16[2,64,2176]{2,1,0:T(8,128)(2,1)S(1)} %collective-permute-done.16.side), channel_id=1, source_target_pairs={{0,2},{2,0},{4,6},{6,4},{8,10},{10,8},{12,14},{14,12},{16,18},{18,... | collective-permute-start | bytes 1671176 | tf_op jit(solution)/shard_map/ppermute | solution.py:66
  60.3 3.2 %collective-permute-start.27 = (bf16[2,64,2176]{2,1,0:T(8,128)(2,1)S(1)}, bf16[2,64,2176]{2,1,0:T(8,128)(2,1)S(1)}, u32[]{:S(2)}, u32[]{:S(2)}) collective-permute-start(bf16[2,64,2176]{2,1,0:T(8,128)(2,1)S(1)} %collective-permute-done.15.over), channel_id=1, source_target_pairs={{0,2},{2,0},{4,6},{6,4},{8,10},{10,8},{12,14},{14,12},{16,18},{18,... | collective-permute-start | bytes 1671176 | tf_op jit(solution)/shard_map/ppermute | solution.py:66
  60.4 4.3 %collective-permute-start.28 = (bf16[2,64,2048]{2,1,0:T(8,128)(2,1)S(1)}, bf16[2,64,2048]{2,1,0:T(8,128)(2,1)S(1)}, u32[]{:S(2)}, u32[]{:S(2)}) collective-permute-start(bf16[2,64,2048]{2,1,0:T(8,128)(2,1)S(1)} %join.3._.diag), channel_id=1, source_target_pairs={{0,2},{2,0},{4,6},{6,4},{8,10},{10,8},{12,14},{14,12},{16,18},{18,... | collective-permute-start | bytes 1572872 | tf_op jit(solution)/shard_map/ppermute | solution.py:66
  61.1 13.9 %collective-permute-start.19 = (bf16[4,64,1024]{2,1,0:T(8,128)(2,1)S(1)}, bf16[4,64,1024]{2,1,0:T(8,128)(2,1)S(1)}, u32[]{:S(2)}, u32[]{:S(2)}) collective-permute-start(bf16[4,64,1024]{2,1,0:T(8,128)(2,1)S(1)} %get-tuple-element.74._), channel_id=1, source_target_pairs={{0,1},{1,0},{2,3},{3,2},{4,5},{5,4},{6,7},{7,6},{8,9},{9,8},{10,11... | collective-permute-start | bytes 1572872 | tf_op jit(solution)/shard_map/ppermute | solution.py:66
  61.9 13.8 %collective-permute-start.21 = (bf16[2,128,1024]{2,1,0:T(8,128)(2,1)S(1)}, bf16[2,128,1024]{2,1,0:T(8,128)(2,1)S(1)}, u32[]{:S(2)}, u32[]{:S(2)}) collective-permute-start(bf16[2,128,1024]{2,1,0:T(8,128)(2,1)S(1)} %get-tuple-element.77._), channel_id=1, source_target_pairs={{0,4},{2,6},{4,0},{6,2},{8,12},{10,14},{12,8},{14,10},{16,20},{18,... | collective-permute-start | bytes 1572872 | tf_op jit(solution)/shard_map/ppermute | solution.py:66
  70.8 7.9 %collective-permute-start.29 = (bf16[4,128,1024]{2,1,0:T(8,128)(2,1)S(1)}, bf16[4,128,1024]{2,1,0:T(8,128)(2,1)S(1)}, u32[]{:S(2)}, u32[]{:S(2)}) collective-permute-start(bf16[4,128,1024]{2,1,0:T(8,128)(2,1)S(1)} %get-tuple-element.86._), channel_id=1, source_target_pairs={{0,2},{2,0},{4,6},{6,4},{8,10},{10,8},{12,14},{14,12},{16,18},{18,... | collective-permute-start | bytes 3145736 | tf_op jit(solution)/shard_map/ppermute | solution.py:66
  73.1 6.5 %collective-permute-start.31 = (bf16[4,128,1024]{2,1,0:T(8,128)(2,1)S(1)}, bf16[4,128,1024]{2,1,0:T(8,128)(2,1)S(1)}, u32[]{:S(2)}, u32[]{:S(2)}) collective-permute-start(bf16[4,128,1024]{2,1,0:T(8,128)(2,1)S(1)} %get-tuple-element.90), channel_id=1, source_target_pairs={{0,2},{2,0},{4,6},{6,4},{8,10},{10,8},{12,14},{14,12},{16,18},{18,... | collective-permute-start | bytes 3145736 | tf_op jit(solution)/shard_map/ppermute | solution.py:66
  75.8 5.4 %collective-permute-start.22 = (bf16[64,1024]{1,0:T(8,128)(2,1)S(1)}, bf16[64,1024]{1,0:T(8,128)(2,1)S(1)}, u32[]{:S(2)}, u32[]{:S(2)}) collective-permute-start(bf16[64,1024]{1,0:T(8,128)(2,1)S(1)} %get-tuple-element.79._), channel_id=1, source_target_pairs={{0,4},{2,6},{4,0},{6,2},{8,12},{10,14},{12,8},{14,10},{16,20},{18,... | collective-permute-start | bytes 393224 | tf_op jit(solution)/shard_map/ppermute | solution.py:66
  77.4 6.4 %collective-permute-start.23 = (bf16[64,1024]{1,0:T(8,128)(2,1)S(1)}, bf16[64,1024]{1,0:T(8,128)(2,1)S(1)}, u32[]{:S(2)}, u32[]{:S(2)}) collective-permute-start(bf16[64,1024]{1,0:T(8,128)(2,1)S(1)} %get-tuple-element.81), channel_id=1, source_target_pairs={{0,1},{1,0},{2,3},{3,2},{4,5},{5,4},{6,7},{7,6},{8,9},{9,8},{10,11... | collective-permute-start | bytes 393224 | tf_op jit(solution)/shard_map/ppermute | solution.py:66
  78.8 14.0 %collective-permute-start.30 = (bf16[4,64,1024]{2,1,0:T(8,128)(2,1)S(1)}, bf16[4,64,1024]{2,1,0:T(8,128)(2,1)S(1)}, u32[]{:S(2)}, u32[]{:S(2)}) collective-permute-start(bf16[4,64,1024]{2,1,0:T(8,128)(2,1)S(1)} %get-tuple-element.88._), channel_id=1, source_target_pairs={{0,1},{1,0},{2,3},{3,2},{4,5},{5,4},{6,7},{7,6},{8,9},{9,8},{10,11... | collective-permute-start | bytes 1572872 | tf_op jit(solution)/shard_map/ppermute | solution.py:66
  79.7 13.0 %collective-permute-start.32 = (bf16[2,128,1024]{2,1,0:T(8,128)(2,1)S(1)}, bf16[2,128,1024]{2,1,0:T(8,128)(2,1)S(1)}, u32[]{:S(2)}, u32[]{:S(2)}) collective-permute-start(bf16[2,128,1024]{2,1,0:T(8,128)(2,1)S(1)} %get-tuple-element.92), channel_id=1, source_target_pairs={{0,4},{2,6},{4,0},{6,2},{8,12},{10,14},{12,8},{14,10},{16,20},{18,... | collective-permute-start | bytes 1572872 | tf_op jit(solution)/shard_map/ppermute | solution.py:66
  83.9 13.1 %collective-permute-start.24 = (bf16[64,2048]{1,0:T(8,128)(2,1)S(1)}, bf16[64,2048]{1,0:T(8,128)(2,1)S(1)}, u32[]{:S(2)}, u32[]{:S(2)}) collective-permute-start(bf16[64,2048]{1,0:T(8,128)(2,1)S(1)} %third_sum.4._), channel_id=1, source_target_pairs={{0,16},{2,18},{4,20},{6,22},{8,24},{10,26},{12,28},{14,30},{16,0},... | collective-permute-start | bytes 786440 | tf_op jit(solution)/shard_map/ppermute | solution.py:71
  92.9 5.5 %collective-permute-start.33 = (bf16[64,1024]{1,0:T(8,128)(2,1)S(1)}, bf16[64,1024]{1,0:T(8,128)(2,1)S(1)}, u32[]{:S(2)}, u32[]{:S(2)}) collective-permute-start(bf16[64,1024]{1,0:T(8,128)(2,1)S(1)} %get-tuple-element.94), channel_id=1, source_target_pairs={{0,4},{2,6},{4,0},{6,2},{8,12},{10,14},{12,8},{14,10},{16,20},{18,... | collective-permute-start | bytes 393224 | tf_op jit(solution)/shard_map/ppermute | solution.py:66
  93.8 5.1 %collective-permute-start.34 = (bf16[64,1024]{1,0:T(8,128)(2,1)S(1)}, bf16[64,1024]{1,0:T(8,128)(2,1)S(1)}, u32[]{:S(2)}, u32[]{:S(2)}) collective-permute-start(bf16[64,1024]{1,0:T(8,128)(2,1)S(1)} %get-tuple-element.96), channel_id=1, source_target_pairs={{0,1},{1,0},{2,3},{3,2},{4,5},{5,4},{6,7},{7,6},{8,9},{9,8},{10,11... | collective-permute-start | bytes 393224 | tf_op jit(solution)/shard_map/ppermute | solution.py:66
  95.0 5.8 %collective-permute-start.36 = (bf16[64,1024]{1,0:T(8,128)(2,1)S(1)}, bf16[64,1024]{1,0:T(8,128)(2,1)S(1)}, u32[]{:S(2)}, u32[]{:S(2)}) collective-permute-start(bf16[64,1024]{1,0:T(8,128)(2,1)S(1)} %get-tuple-element.101), channel_id=1, source_target_pairs={{0,4},{2,6},{4,0},{6,2},{8,12},{10,14},{12,8},{14,10},{16,20},{18,... | collective-permute-start | bytes 393224 | tf_op jit(solution)/shard_map/ppermute | solution.py:66
  96.1 5.0 %collective-permute-start.37 = (bf16[64,1024]{1,0:T(8,128)(2,1)S(1)}, bf16[64,1024]{1,0:T(8,128)(2,1)S(1)}, u32[]{:S(2)}, u32[]{:S(2)}) collective-permute-start(bf16[64,1024]{1,0:T(8,128)(2,1)S(1)} %get-tuple-element.103), channel_id=1, source_target_pairs={{0,1},{1,0},{2,3},{3,2},{4,5},{5,4},{6,7},{7,6},{8,9},{9,8},{10,11... | collective-permute-start | bytes 393224 | tf_op jit(solution)/shard_map/ppermute | solution.py:66
  98.9 12.8 %collective-permute-start.35 = (bf16[64,2048]{1,0:T(8,128)(2,1)S(1)}, bf16[64,2048]{1,0:T(8,128)(2,1)S(1)}, u32[]{:S(2)}, u32[]{:S(2)}) collective-permute-start(bf16[64,2048]{1,0:T(8,128)(2,1)S(1)} %third_sum.5._), channel_id=1, source_target_pairs={{0,8},{2,10},{4,12},{6,14},{8,16},{10,18},{12,20},{14,22},{16,24},... | collective-permute-start | bytes 786440 | tf_op jit(solution)/shard_map/ppermute | solution.py:71
  101.1 10.7 %collective-permute-start.40 = (bf16[64,2048]{1,0:T(8,128)(2,1)S(1)}, bf16[64,2048]{1,0:T(8,128)(2,1)S(1)}, u32[]{:S(2)}, u32[]{:S(2)}) collective-permute-start(bf16[64,2048]{1,0:T(8,128)(2,1)S(1)} %third_sum.6.refs_2_._), channel_id=1, source_target_pairs={{0,24},{2,26},{4,28},{6,30},{8,0},{10,2},{12,4},{14,6},{16,8},{18,... | collective-permute-start | bytes 786440 | tf_op jit(solution)/shard_map/ppermute | solution.py:71
  105.7 5.0 %collective-permute-start.38 = (bf16[64,1024]{1,0:T(8,128)(2,1)S(1)}, bf16[64,1024]{1,0:T(8,128)(2,1)S(1)}, u32[]{:S(2)}, u32[]{:S(2)}) collective-permute-start(bf16[64,1024]{1,0:T(8,128)(2,1)S(1)} %get-tuple-element.104), channel_id=1, source_target_pairs={{0,4},{2,6},{4,0},{6,2},{8,12},{10,14},{12,8},{14,10},{16,20},{18,... | collective-permute-start | bytes 393224 | tf_op jit(solution)/shard_map/ppermute | solution.py:66
  106.7 5.0 %collective-permute-start.39 = (bf16[64,1024]{1,0:T(8,128)(2,1)S(1)}, bf16[64,1024]{1,0:T(8,128)(2,1)S(1)}, u32[]{:S(2)}, u32[]{:S(2)}) collective-permute-start(bf16[64,1024]{1,0:T(8,128)(2,1)S(1)} %get-tuple-element.106), channel_id=1, source_target_pairs={{0,1},{1,0},{2,3},{3,2},{4,5},{5,4},{6,7},{7,6},{8,9},{9,8},{10,11... | collective-permute-start | bytes 393224 | tf_op jit(solution)/shard_map/ppermute | solution.py:66

commit v16 on v15

--- a/solution.py
+++ b/solution.py
@@ -86,48 +86,43 @@
     )(*operands)
 
 
-def prepare_kernel(place, tokens, gates_any, ids_any, first, table, gates, ids, sems):
+def prepare_kernel(place, tokens, routing_any, first, table, routing, sems):
     piece = first.shape[0]
     width = first.shape[1] - table.shape[1]
     near = pl.multiple_of(place[3] * piece, piece)
     copies = [
-        pltpu.make_async_copy(gates_any, gates, sems.at[0]),
-        pltpu.make_async_copy(ids_any, ids, sems.at[1]),
+        pltpu.make_async_copy(routing_any, routing, sems.at[0]),
         pltpu.make_async_copy(
-            tokens.at[pl.ds(near, piece), :], first.at[:, pl.ds(0, width)], sems.at[2]
+            tokens.at[pl.ds(near, piece), :], first.at[:, pl.ds(0, width)], sems.at[1]
         ),
     ]
     for copy in copies:
         copy.start()
     copies[0].wait()
-    copies[1].wait()
-    rest = gates[...]
+    count = routing.shape[0] // 2
+    rest = routing[:count]
     terms = []
     for _ in range(3):
         term = rest.astype(jnp.bfloat16).astype(jnp.float32)
         terms.append(term)
         rest = rest - term
-    terms.append(ids[...].astype(jnp.float32))
-    unused = piece - 4 * gates.shape[0]
-    terms.append(jnp.zeros((unused, gates.shape[1]), jnp.float32))
+    terms.append(routing[count:])
+    unused = piece - 4 * count
+    terms.append(jnp.zeros((unused, routing.shape[1]), jnp.float32))
     packed = jnp.concatenate(terms, axis=0).astype(jnp.bfloat16)
     first[:, width:] = packed
     table[...] = packed
-    copies[2].wait()
-
-
-def prepare(place, cotangent, gates, ids, piece):
+    copies[1].wait()
+
+
+def prepare(place, cotangent, routing, piece):
     return small(
         prepare_kernel,
         "prepare",
         [(piece, cotangent.shape[1] + 128), (piece, 128)],
-        "shhh",
-        (place, cotangent, gates, ids),
-        [
-            pltpu.VMEM(gates.shape, jnp.float32),
-            pltpu.VMEM(ids.shape, jnp.int32),
-            pltpu.SemaphoreType.DMA((3,)),
-        ],
+        "shh",
+        (place, cotangent, routing),
+        [pltpu.VMEM(routing.shape, jnp.float32), pltpu.SemaphoreType.DMA((2,))],
         limit=4,
     )
 
@@ -564,7 +559,8 @@
     me, half = lax.axis_index("expert"), lax.axis_index("tp")
     place = jnp.stack([me % 2, me // 2 % 2, me // 4, half]).astype(jnp.int32)
 
-    part, table = prepare(place, cotangent, gates.T, expert_ids.T, piece)
+    routing = jnp.concatenate([gates.T, expert_ids.T.astype(jnp.float32)], axis=0)
+    part, table = prepare(place, cotangent, routing, piece)
     first = swap(part, "expert", 2)
     own_c, table_c = swap(cotangent, "expert", 1), swap(table, "expert", 1)
     gathered, saved = [], None
@@ -623,7 +619,7 @@
     late_r, _ = sums_by_token(middle, grads, pick_t, after)
     parts = second_apart(*early[:4], early[4])
     (send_l, left, send_r, right), out = parts[:4], parts[4:]
-    done = across(*out, out[0], work=1 << 36)
+    done = across(*out, out[0])
     early, after = along_line(done, CHUNKS[0][1]), out[0]
     late = first_step(*late_l, *late_r, after)
     parts = second_apart(*late[:4], done)

time: 113 us -> 120 us (1.062)
  waiting for transfers between devices: 41.6 us -> 50.8 us
  starting transfers between devices: 40.2 us -> 37.8 us
  local copies, waits for them, and re-layouts: 6.98 us -> 5.61 us
  other arithmetic: 0.08 us -> 1.45 us
    ppermute x6, waiting for transfers between devices: 12.9 us -> 24.3 us  [along_line(): lax.ppermute(value, 'expert', [(i, (i + 4 * shift) % count) for i in rang...]
    ppermute x6, starting transfers between devices: 14.1 us -> 11.6 us  [along_line(): lax.ppermute(value, 'expert', [(i, (i + 4 * shift) % count) for i in rang...]
    ppermute x35, waiting for transfers between devices: 28.7 us -> 26.5 us  [swap(): return lax.ppermute(value, axis, [(i, i ^ step) for i in range(count)])]
    unnamed x20 -> x16, local copies, waits for them, and re-layouts: 6.98 us -> 5.61 us
  transfers between devices with their start and end apart: 41 -> 41, of which waited for: 20 -> 18; matrix products, arithmetic and copies ran while one was open for 0% -> 0% of each run, Pallas kernels for 20% -> 18%
where the time goes in v16:
time: 120 us
  waiting for transfers between devices  50.8 us (42%)
  starting transfers between devices  37.8 us (31%)
  Pallas kernels  23.6 us (20%)
  local copies, waits for them, and re-layouts  5.61 us (5%)
  other arithmetic  1.45 us (1%)
    ppermute x35, waiting for transfers between devices, swap(): return lax.ppermute(value, axis, [(i, i ^ step) for i in range(count)])  26.5 us
    ppermute x35, starting transfers between devices, swap(): return lax.ppermute(value, axis, [(i, i ^ step) for i in range(count)])  26.2 us
    ppermute x6, waiting for transfers between devices, along_line(): lax.ppermute(value, 'expert', [(i, (i + 4 * shift) % count) for i in rang...  24.3 us
    pallas_call x29, Pallas kernels, small(): pl.pallas_call(kernel, out_shape=[out if hasattr(out, 'dtype') else jax.S...  23.6 us
    ppermute x6, starting transfers between devices, along_line(): lax.ppermute(value, 'expert', [(i, (i + 4 * shift) % count) for i in rang...  11.6 us
    unnamed x16, local copies, waits for them, and re-layouts  5.61 us
  transfers between devices with their start and end apart: 41, of which 18 were waited for; matrix products, arithmetic and copies ran while one was open for 0% of the time, Pallas kernels for 18%

profile of v16, /device:TPU:0, one launch (start us, length us, event | category | flops | bytes accessed | tf_op | source)
XLA Modules:
  0.0 119.6 jit_solution(15088460648699570738)
XLA Ops:
  0.0 0.7 convert_bitcast_fusion
  0.7 0.7 pad_maximum_fusion.routing_any
  1.5 1.0 copy-done.3
  2.5 0.6 prepare.1
  3.1 4.1 %collective-permute-start.1 = (bf16[64,2176]{1,0:T(8,128)(2,1)S(1)}, bf16[64,2176]{1,0:T(8,128)(2,1)S(1)}, u32[]{:S(2)}, u32[]{:S(2)}) collective-permute-start(bf16[64,2176]{1,0:T(8,128)(2,1)S(1)} %get-tuple-element.56.part), channel_id=1, source_target_pairs={{0,16},{2,18},{4,20},{6,22},{8,24},{10,26},{12,28},{14,30},{16,0},... | collective-permute-start | bytes 835592 | tf_op jit(solution)/shard_map/ppermute | solution.py:71
  7.2 1.5 %collective-permute-start.5 = (bf16[64,2176]{1,0:T(8,128)(2,1)S(1)}, bf16[64,2176]{1,0:T(8,128)(2,1)S(1)}, u32[]{:S(2)}, u32[]{:S(2)}) collective-permute-start(bf16[64,2176]{1,0:T(8,128)(2,1)S(1)} %get-tuple-element.56.part), channel_id=1, source_target_pairs={{0,4},{2,6},{4,0},{6,2},{8,12},{10,14},{12,8},{14,10},{16,20},{18,... | collective-permute-start | bytes 835592 | tf_op jit(solution)/shard_map/ppermute | solution.py:66
  8.7 11.1 %collective-permute-done.1.came = bf16[64,2176]{1,0:T(8,128)(2,1)S(1)} collective-permute-done((bf16[64,2176]{1,0:T(8,128)(2,1)S(1)}, bf16[64,2176]{1,0:T(8,128)(2,1)S(1)}, u32[]{:S(2)}, u32[]{:S(2)}) %collective-permute-start.1) | collective-permute-done | bytes 278560 | tf_op jit(solution)/shard_map/ppermute | solution.py:71
  19.9 1.6 %collective-permute-start.3 = (bf16[1,64,2176]{2,1,0:T(8,128)(2,1)S(1)}, bf16[1,64,2176]{2,1,0:T(8,128)(2,1)S(1)}, u32[]{:S(2)}, u32[]{:S(2)}) collective-permute-start(bf16[1,64,2176]{2,1,0:T(8,128)(2,1)S(1)} %get-tuple-element.57.lines._), channel_id=1, source_target_pairs={{0,1},{1,0},{2,3},{3,2},{4,5},{5,4},{6,7},{7,6},{8,9},{9,8},{10,11... | collective-permute-start | bytes 835592 | tf_op jit(solution)/shard_map/ppermute | solution.py:66
  21.5 1.5 %collective-permute-start.6 = (bf16[1,64,2176]{2,1,0:T(8,128)(2,1)S(1)}, bf16[1,64,2176]{2,1,0:T(8,128)(2,1)S(1)}, u32[]{:S(2)}, u32[]{:S(2)}) collective-permute-start(bf16[1,64,2176]{2,1,0:T(8,128)(2,1)S(1)} %get-tuple-element.57.lines._), channel_id=1, source_target_pairs={{0,4},{2,6},{4,0},{6,2},{8,12},{10,14},{12,8},{14,10},{16,20},{18,... | collective-permute-start | bytes 835592 | tf_op jit(solution)/shard_map/ppermute | solution.py:66
  23.0 3.5 %collective-permute-start.12 = (bf16[64,2176]{1,0:T(8,128)(2,1)S(1)}, bf16[64,2176]{1,0:T(8,128)(2,1)S(1)}, u32[]{:S(2)}, u32[]{:S(2)}) collective-permute-start(bf16[64,2176]{1,0:T(8,128)(2,1)S(1)} %get-tuple-element.66), channel_id=1, source_target_pairs={{0,24},{2,26},{4,28},{6,30},{8,0},{10,2},{12,4},{14,6},{16,8},{18,... | collective-permute-start | bytes 835592 | tf_op jit(solution)/shard_map/ppermute | solution.py:71
  26.5 1.3 %collective-permute-done.3.side = bf16[1,64,2176]{2,1,0:T(8,128)(2,1)S(1)} collective-permute-done((bf16[1,64,2176]{2,1,0:T(8,128)(2,1)S(1)}, bf16[1,64,2176]{2,1,0:T(8,128)(2,1)S(1)}, u32[]{:S(2)}, u32[]{:S(2)}) %collective-permute-start.3) | collective-permute-done | bytes 278560 | tf_op jit(solution)/shard_map/ppermute | solution.py:66
  27.8 1.0 collective-permute-done.6.over
  28.8 1.0 copy-done.4
  29.8 0.6 own_corner.1
  30.4 0.8 collective-permute-start.8
  31.3 1.3 %collective-permute-start.9 = (bf16[2,64,1024]{2,1,0:T(8,128)(2,1)S(1)}, bf16[2,64,1024]{2,1,0:T(8,128)(2,1)S(1)}, u32[]{:S(2)}, u32[]{:S(2)}) collective-permute-start(bf16[2,64,1024]{2,1,0:T(8,128)(2,1)S(1)} %get-tuple-element.60), channel_id=1, source_target_pairs={{0,4},{2,6},{4,0},{6,2},{8,12},{10,14},{12,8},{14,10},{16,20},{18,... | collective-permute-start | bytes 786440 | tf_op jit(solution)/shard_map/ppermute | solution.py:66
  32.6 1.3 %copy-done.6 = bf16[2,384,768]{2,1,0:T(8,128)(2,1)S(1)} copy-done((bf16[2,384,768]{2,1,0:T(8,128)(2,1)S(1)}, bf16[2,384,768]{2,1,0:T(8,128)(2,1)}, u32[]{:S(2)}) %copy-start.6) | copy-done | bytes 1179672
  33.8 1.3 %copy-done.7 = bf16[2,384,768]{2,1,0:T(8,128)(2,1)S(1)} copy-done((bf16[2,384,768]{2,1,0:T(8,128)(2,1)S(1)}, bf16[2,384,768]{2,1,0:T(8,128)(2,1)}, u32[]{:S(2)}) %copy-start.7) | copy-done | bytes 1179672
  35.1 1.3 %turn.1 = (f32[2,768,384]{2,1,0:T(8,128)S(1)}, f32[2,768,384]{2,1,0:T(8,128)S(1)}) custom-call(bf16[2,384,768]{2,1,0:T(8,128)(2,1)S(1)} %copy-done.6, bf16[2,384,768]{2,1,0:T(8,128)(2,1)S(1)} %copy-done.7, bf16[1,64,2176]{2,1,0:T(8,128)(2,1)S(1)} %get-tuple-element.57.lines._), custom_call_target="tpu_custom_call" | custom-call | tf_op jit(solution)/shard_map/turn/pallas_call | solution.py:76
  36.4 0.6 collective-permute-start.2
  37.0 1.8 %collective-permute-done.13.refs_1_ = bf16[64,2176]{1,0:T(8,128)(2,1)S(1)} collective-permute-done((bf16[64,2176]{1,0:T(8,128)(2,1)S(1)}, bf16[64,2176]{1,0:T(8,128)(2,1)S(1)}, u32[]{:S(2)}, u32[]{:S(2)}) %collective-permute-start.13) | collective-permute-done | bytes 278560 | tf_op jit(solution)/shard_map/ppermute | solution.py:71
  38.8 0.6 collective-permute-start.15
  39.4 0.5 collective-permute-start.16
  40.0 1.0 copy-done.5
  40.9 0.5 collective-permute-start.10
  42.0 1.1 route.2
  43.1 0.9 collective-permute-done.4.side_c
  44.0 3.9 %hidden.2.grads._ = bf16[2,384,768]{2,1,0:T(8,128)(2,1)S(1)} custom-call(s32[4]{0:T(128)S(1)} %pad_add_fusion.place, bf16[128,2048]{1,0:T(8,128)(2,1)S(1)} %copy-done.5, bf16[128,2048]{1,0:T(8,128)(2,1)S(1)} %collective-permute-done.own_c, bf16[1,64,2176]{2,1,0:T(8,128)(2,1)S(1)} %get-tuple-element.57.lines._, ...), custom_call_target="tpu_custom_call" | custom-call | tf_op jit(solution)/shard_map/hidden/pallas_call | solution.py:76
  47.9 2.3 %sums.4 = (bf16[4,128,1024]{2,1,0:T(8,128)(2,1)S(1)}, bf16[4,128,1024]{2,1,0:T(8,128)(2,1)S(1)}) custom-call(bf16[2,384,768]{2,1,0:T(8,128)(2,1)S(1)} %hidden.2.grads._, bf16[2,384,2048]{2,1,0:T(8,128)(2,1)S(1)} %copy-done, bf16[2,384,2048]{2,1,0:T(8,128)(2,1)S(1)} %copy-done.1, bf16[4,256,192]{2,1,0:T(8,128)(2,1)S(1)} %get-tuple-element.67.pick_t, ...), custom_call_target="tpu_custom_call" | custom-call | tf_op jit(solution)/shard_map/sums/pallas_call | solution.py:76
  50.4 1.8 %collective-permute-done.15.over = bf16[2,64,2176]{2,1,0:T(8,128)(2,1)S(1)} collective-permute-done((bf16[2,64,2176]{2,1,0:T(8,128)(2,1)S(1)}, bf16[2,64,2176]{2,1,0:T(8,128)(2,1)S(1)}, u32[]{:S(2)}, u32[]{:S(2)}) %collective-permute-start.15) | collective-permute-done | bytes 557088 | tf_op jit(solution)/shard_map/ppermute | solution.py:66
  52.5 1.0 collective-permute-start.17
  53.5 1.5 %collective-permute-start.18 = (bf16[2,64,1024]{2,1,0:T(8,128)(2,1)S(1)}, bf16[2,64,1024]{2,1,0:T(8,128)(2,1)S(1)}, u32[]{:S(2)}, u32[]{:S(2)}) collective-permute-start(bf16[2,64,1024]{2,1,0:T(8,128)(2,1)S(1)} %get-tuple-element.71), channel_id=1, source_target_pairs={{0,4},{2,6},{4,0},{6,2},{8,12},{10,14},{12,8},{14,10},{16,20},{18,... | collective-permute-start | bytes 786440 | tf_op jit(solution)/shard_map/ppermute | solution.py:66
  55.0 2.2 %sums.5 = (bf16[4,128,1024]{2,1,0:T(8,128)(2,1)S(1)}, bf16[4,128,1024]{2,1,0:T(8,128)(2,1)S(1)}) custom-call(bf16[2,384,768]{2,1,0:T(8,128)(2,1)S(1)} %hidden.2.grads._, bf16[2,384,2048]{2,1,0:T(8,128)(2,1)S(1)} %copy-done, bf16[2,384,2048]{2,1,0:T(8,128)(2,1)S(1)} %copy-done.1, bf16[4,256,192]{2,1,0:T(8,128)(2,1)S(1)} %get-tuple-element.67.pick_t, ...), custom_call_target="tpu_custom_call" | custom-call | flops 68719476736 | bytes 268435456 | tf_op jit(solution)/shard_map/sums/pallas_call | solution.py:76
  57.3 0.5 collective-permute-start.25
  57.8 1.3 %collective-permute-done.17.left = bf16[2,64,1024]{2,1,0:T(8,128)(2,1)S(1)} collective-permute-done((bf16[2,64,1024]{2,1,0:T(8,128)(2,1)S(1)}, bf16[2,64,1024]{2,1,0:T(8,128)(2,1)S(1)}, u32[]{:S(2)}, u32[]{:S(2)}) %collective-permute-start.17) | collective-permute-done | bytes 262176 | tf_op jit(solution)/shard_map/ppermute | solution.py:66
  59.1 1.2 %collective-permute-done.18.right = bf16[2,64,1024]{2,1,0:T(8,128)(2,1)S(1)} collective-permute-done((bf16[2,64,1024]{2,1,0:T(8,128)(2,1)S(1)}, bf16[2,64,1024]{2,1,0:T(8,128)(2,1)S(1)}, u32[]{:S(2)}, u32[]{:S(2)}) %collective-permute-start.18) | collective-permute-done | bytes 262176 | tf_op jit(solution)/shard_map/ppermute | solution.py:66
  60.4 0.6 collective-permute-start.28
  61.0 0.7 collective-permute-start.19
  61.9 1.6 %collective-permute-start.21 = (bf16[2,128,1024]{2,1,0:T(8,128)(2,1)S(1)}, bf16[2,128,1024]{2,1,0:T(8,128)(2,1)S(1)}, u32[]{:S(2)}, u32[]{:S(2)}) collective-permute-start(bf16[2,128,1024]{2,1,0:T(8,128)(2,1)S(1)} %get-tuple-element.77._), channel_id=1, source_target_pairs={{0,4},{2,6},{4,0},{6,2},{8,12},{10,14},{12,8},{14,10},{16,20},{18,... | collective-permute-start | bytes 1572872 | tf_op jit(solution)/shard_map/ppermute | solution.py:66
  63.5 1.1 route.3
  64.7 3.9 %hidden.3.grads._ = bf16[2,384,768]{2,1,0:T(8,128)(2,1)S(1)} custom-call(s32[4]{0:T(128)S(1)} %pad_add_fusion.place, bf16[128,2048]{1,0:T(8,128)(2,1)S(1)} %copy-done.5, bf16[128,2048]{1,0:T(8,128)(2,1)S(1)} %collective-permute-done.own_c, bf16[2,64,2176]{2,1,0:T(8,128)(2,1)S(1)} %stack.21._.lines, bf16[2,64,2176]{2,1,0:T(8,128)(2,1)S(1)} %collective-permute-done.25.lines_c, ...), custom_call_target="tpu_custom_call" | custom-call | tf_op jit(solution)/shard_map/hidden/pallas_call | solution.py:76
  68.5 2.2 %sums.6 = (bf16[4,128,1024]{2,1,0:T(8,128)(2,1)S(1)}, bf16[4,128,1024]{2,1,0:T(8,128)(2,1)S(1)}) custom-call(bf16[2,384,768]{2,1,0:T(8,128)(2,1)S(1)} %hidden.3.grads._, bf16[2,384,2048]{2,1,0:T(8,128)(2,1)S(1)} %copy-done, bf16[2,384,2048]{2,1,0:T(8,128)(2,1)S(1)} %copy-done.1, bf16[4,256,192]{2,1,0:T(8,128)(2,1)S(1)} %get-tuple-element.84.pick_t, ...), custom_call_target="tpu_custom_call" | custom-call | tf_op jit(solution)/shard_map/sums/pallas_call | solution.py:76
  70.9 2.2 %sums.7 = (bf16[4,128,1024]{2,1,0:T(8,128)(2,1)S(1)}, bf16[4,128,1024]{2,1,0:T(8,128)(2,1)S(1)}) custom-call(bf16[2,384,768]{2,1,0:T(8,128)(2,1)S(1)} %hidden.3.grads._, bf16[2,384,2048]{2,1,0:T(8,128)(2,1)S(1)} %copy-done, bf16[2,384,2048]{2,1,0:T(8,128)(2,1)S(1)} %copy-done.1, bf16[4,256,192]{2,1,0:T(8,128)(2,1)S(1)} %get-tuple-element.84.pick_t, ...), custom_call_target="tpu_custom_call" | custom-call | tf_op jit(solution)/shard_map/sums/pallas_call | solution.py:76
  73.1 0.6 collective-permute-start.31
  73.7 1.3 %collective-permute-done.19.came_l = bf16[4,64,1024]{2,1,0:T(8,128)(2,1)S(1)} collective-permute-done((bf16[4,64,1024]{2,1,0:T(8,128)(2,1)S(1)}, bf16[4,64,1024]{2,1,0:T(8,128)(2,1)S(1)}, u32[]{:S(2)}, u32[]{:S(2)}) %collective-permute-start.19) | collective-permute-done | bytes 524320 | tf_op jit(solution)/shard_map/ppermute | solution.py:66
  75.0 0.7 collective-permute-done.21.came_r
  75.9 1.3 %collective-permute-start.30 = (bf16[4,64,1024]{2,1,0:T(8,128)(2,1)S(1)}, bf16[4,64,1024]{2,1,0:T(8,128)(2,1)S(1)}, u32[]{:S(2)}, u32[]{:S(2)}) collective-permute-start(bf16[4,64,1024]{2,1,0:T(8,128)(2,1)S(1)} %get-tuple-element.88._), channel_id=1, source_target_pairs={{0,1},{1,0},{2,3},{3,2},{4,5},{5,4},{6,7},{7,6},{8,9},{9,8},{10,11... | collective-permute-start | bytes 1572872 | tf_op jit(solution)/shard_map/ppermute | solution.py:66
  77.4 1.6 %collective-permute-start.32 = (bf16[2,128,1024]{2,1,0:T(8,128)(2,1)S(1)}, bf16[2,128,1024]{2,1,0:T(8,128)(2,1)S(1)}, u32[]{:S(2)}, u32[]{:S(2)}) collective-permute-start(bf16[2,128,1024]{2,1,0:T(8,128)(2,1)S(1)} %get-tuple-element.92), channel_id=1, source_target_pairs={{0,4},{2,6},{4,0},{6,2},{8,12},{10,14},{12,8},{14,10},{16,20},{18,... | collective-permute-start | bytes 1572872 | tf_op jit(solution)/shard_map/ppermute | solution.py:66
  78.9 0.5 collective-permute-start.22
  79.5 0.8 collective-permute-start.23
  80.2 12.9 %collective-permute-done.22.came_l = bf16[64,1024]{1,0:T(8,128)(2,1)S(1)} collective-permute-done((bf16[64,1024]{1,0:T(8,128)(2,1)S(1)}, bf16[64,1024]{1,0:T(8,128)(2,1)S(1)}, u32[]{:S(2)}, u32[]{:S(2)}) %collective-permute-start.22) | collective-permute-done | bytes 131104 | tf_op jit(solution)/shard_map/ppermute | solution.py:66
  93.4 1.2 collective-permute-start.33
  94.6 1.0 collective-permute-start.34
  95.6 1.3 %collective-permute-start.36 = (bf16[64,1024]{1,0:T(8,128)(2,1)S(1)}, bf16[64,1024]{1,0:T(8,128)(2,1)S(1)}, u32[]{:S(2)}, u32[]{:S(2)}) collective-permute-start(bf16[64,1024]{1,0:T(8,128)(2,1)S(1)} %get-tuple-element.101), channel_id=1, source_target_pairs={{0,4},{2,6},{4,0},{6,2},{8,12},{10,14},{12,8},{14,10},{16,20},{18,... | collective-permute-start | bytes 393224 | tf_op jit(solution)/shard_map/ppermute | solution.py:66
  97.0 0.6 collective-permute-start.37
  97.6 8.6 %collective-permute-done.24._.refs_0_ = bf16[64,2048]{1,0:T(8,128)(2,1)S(1)} collective-permute-done((bf16[64,2048]{1,0:T(8,128)(2,1)S(1)}, bf16[64,2048]{1,0:T(8,128)(2,1)S(1)}, u32[]{:S(2)}, u32[]{:S(2)}) %collective-permute-start.24) | collective-permute-done | bytes 262176 | tf_op jit(solution)/shard_map/ppermute | solution.py:71
  106.4 3.8 %collective-permute-start.40 = (bf16[64,2048]{1,0:T(8,128)(2,1)S(1)}, bf16[64,2048]{1,0:T(8,128)(2,1)S(1)}, u32[]{:S(2)}, u32[]{:S(2)}) collective-permute-start(bf16[64,2048]{1,0:T(8,128)(2,1)S(1)} %third_sum.6.refs_2_._), channel_id=1, source_target_pairs={{0,24},{2,26},{4,28},{6,30},{8,0},{10,2},{12,4},{14,6},{16,8},{18,... | collective-permute-start | bytes 786440 | tf_op jit(solution)/shard_map/ppermute | solution.py:71
  110.2 0.6 collective-permute-start.38
  110.8 1.5 %collective-permute-start.39 = (bf16[64,1024]{1,0:T(8,128)(2,1)S(1)}, bf16[64,1024]{1,0:T(8,128)(2,1)S(1)}, u32[]{:S(2)}, u32[]{:S(2)}) collective-permute-start(bf16[64,1024]{1,0:T(8,128)(2,1)S(1)} %get-tuple-element.106), channel_id=1, source_target_pairs={{0,1},{1,0},{2,3},{3,2},{4,5},{5,4},{6,7},{7,6},{8,9},{9,8},{10,11... | collective-permute-start | bytes 393224 | tf_op jit(solution)/shard_map/ppermute | solution.py:66
  112.3 3.0 %collective-permute-done.38.came_l = bf16[64,1024]{1,0:T(8,128)(2,1)S(1)} collective-permute-done((bf16[64,1024]{1,0:T(8,128)(2,1)S(1)}, bf16[64,1024]{1,0:T(8,128)(2,1)S(1)}, u32[]{:S(2)}, u32[]{:S(2)}) %collective-permute-start.38) | collective-permute-done | bytes 131104 | tf_op jit(solution)/shard_map/ppermute | solution.py:66
  115.3 0.5 collective-permute-done.39.came_r
  115.9 1.5 %collective-permute-done.35.refs_1_ = bf16[64,2048]{1,0:T(8,128)(2,1)S(1)} collective-permute-done((bf16[64,2048]{1,0:T(8,128)(2,1)S(1)}, bf16[64,2048]{1,0:T(8,128)(2,1)S(1)}, u32[]{:S(2)}, u32[]{:S(2)}) %collective-permute-start.35) | collective-permute-done | bytes 262176 | tf_op jit(solution)/shard_map/ppermute | solution.py:71
  117.4 1.3 %collective-permute-done.40.refs_2_ = bf16[64,2048]{1,0:T(8,128)(2,1)S(1)} collective-permute-done((bf16[64,2048]{1,0:T(8,128)(2,1)S(1)}, bf16[64,2048]{1,0:T(8,128)(2,1)S(1)}, u32[]{:S(2)}, u32[]{:S(2)}) %collective-permute-start.40) | collective-permute-done | bytes 262176 | tf_op jit(solution)/shard_map/ppermute | solution.py:71
  118.7 0.9 last_sum.1
  (66 shorter events, 2.6 us)
Async XLA Ops:
  1.5 1.0 copy-start.3
  3.1 16.7 %collective-permute-start.1 = (bf16[64,2176]{1,0:T(8,128)(2,1)S(1)}, bf16[64,2176]{1,0:T(8,128)(2,1)S(1)}, u32[]{:S(2)}, u32[]{:S(2)}) collective-permute-start(bf16[64,2176]{1,0:T(8,128)(2,1)S(1)} %get-tuple-element.56.part), channel_id=1, source_target_pairs={{0,16},{2,18},{4,20},{6,22},{8,24},{10,26},{12,28},{14,30},{16,0},... | collective-permute-start | bytes 835592 | tf_op jit(solution)/shard_map/ppermute | solution.py:71
  7.2 19.3 %collective-permute-start.5 = (bf16[64,2176]{1,0:T(8,128)(2,1)S(1)}, bf16[64,2176]{1,0:T(8,128)(2,1)S(1)}, u32[]{:S(2)}, u32[]{:S(2)}) collective-permute-start(bf16[64,2176]{1,0:T(8,128)(2,1)S(1)} %get-tuple-element.56.part), channel_id=1, source_target_pairs={{0,4},{2,6},{4,0},{6,2},{8,12},{10,14},{12,8},{14,10},{16,20},{18,... | collective-permute-start | bytes 835592 | tf_op jit(solution)/shard_map/ppermute | solution.py:66
  19.9 7.9 %collective-permute-start.3 = (bf16[1,64,2176]{2,1,0:T(8,128)(2,1)S(1)}, bf16[1,64,2176]{2,1,0:T(8,128)(2,1)S(1)}, u32[]{:S(2)}, u32[]{:S(2)}) collective-permute-start(bf16[1,64,2176]{2,1,0:T(8,128)(2,1)S(1)} %get-tuple-element.57.lines._), channel_id=1, source_target_pairs={{0,1},{1,0},{2,3},{3,2},{4,5},{5,4},{6,7},{7,6},{8,9},{9,8},{10,11... | collective-permute-start | bytes 835592 | tf_op jit(solution)/shard_map/ppermute | solution.py:66
  21.5 7.3 %collective-permute-start.6 = (bf16[1,64,2176]{2,1,0:T(8,128)(2,1)S(1)}, bf16[1,64,2176]{2,1,0:T(8,128)(2,1)S(1)}, u32[]{:S(2)}, u32[]{:S(2)}) collective-permute-start(bf16[1,64,2176]{2,1,0:T(8,128)(2,1)S(1)} %get-tuple-element.57.lines._), channel_id=1, source_target_pairs={{0,4},{2,6},{4,0},{6,2},{8,12},{10,14},{12,8},{14,10},{16,20},{18,... | collective-permute-start | bytes 835592 | tf_op jit(solution)/shard_map/ppermute | solution.py:66
  23.0 13.4 %collective-permute-start.12 = (bf16[64,2176]{1,0:T(8,128)(2,1)S(1)}, bf16[64,2176]{1,0:T(8,128)(2,1)S(1)}, u32[]{:S(2)}, u32[]{:S(2)}) collective-permute-start(bf16[64,2176]{1,0:T(8,128)(2,1)S(1)} %get-tuple-element.66), channel_id=1, source_target_pairs={{0,24},{2,26},{4,28},{6,30},{8,0},{10,2},{12,4},{14,6},{16,8},{18,... | collective-permute-start | bytes 835592 | tf_op jit(solution)/shard_map/ppermute | solution.py:71
  26.5 12.2 %collective-permute-start.13 = (bf16[64,2176]{1,0:T(8,128)(2,1)S(1)}, bf16[64,2176]{1,0:T(8,128)(2,1)S(1)}, u32[]{:S(2)}, u32[]{:S(2)}) collective-permute-start(bf16[64,2176]{1,0:T(8,128)(2,1)S(1)} %get-tuple-element.66), channel_id=1, source_target_pairs={{0,8},{2,10},{4,12},{6,14},{8,16},{10,18},{12,20},{14,22},{16,24},... | collective-permute-start | bytes 835592 | tf_op jit(solution)/shard_map/ppermute | solution.py:71
  28.8 1.0 copy-start.4
  30.4 8.9 %collective-permute-start.8 = (bf16[2,64,1024]{2,1,0:T(8,128)(2,1)S(1)}, bf16[2,64,1024]{2,1,0:T(8,128)(2,1)S(1)}, u32[]{:S(2)}, u32[]{:S(2)}) collective-permute-start(bf16[2,64,1024]{2,1,0:T(8,128)(2,1)S(1)} %get-tuple-element.59.refs_0_), channel_id=1, source_target_pairs={{0,1},{1,0},{2,3},{3,2},{4,5},{5,4},{6,7},{7,6},{8,9},{9,8},{10,11... | collective-permute-start | bytes 786440 | tf_op jit(solution)/shard_map/ppermute | solution.py:66
  31.3 8.6 %collective-permute-start.9 = (bf16[2,64,1024]{2,1,0:T(8,128)(2,1)S(1)}, bf16[2,64,1024]{2,1,0:T(8,128)(2,1)S(1)}, u32[]{:S(2)}, u32[]{:S(2)}) collective-permute-start(bf16[2,64,1024]{2,1,0:T(8,128)(2,1)S(1)} %get-tuple-element.60), channel_id=1, source_target_pairs={{0,4},{2,6},{4,0},{6,2},{8,12},{10,14},{12,8},{14,10},{16,20},{18,... | collective-permute-start | bytes 786440 | tf_op jit(solution)/shard_map/ppermute | solution.py:66
  32.6 7.4 %collective-permute-start.11 = (bf16[64,128]{1,0:T(8,128)(2,1)S(1)}, bf16[64,128]{1,0:T(8,128)(2,1)S(1)}, u32[]{:S(2)}, u32[]{:S(2)}) collective-permute-start(bf16[64,128]{1,0:T(8,128)(2,1)S(1)} %get-tuple-element.61.own), channel_id=1, source_target_pairs={{0,2},{2,0},{4,6},{6,4},{8,10},{10,8},{12,14},{14,12},{16,18},{18,... | collective-permute-start | bytes 49160 | tf_op jit(solution)/shard_map/ppermute | solution.py:66
  32.6 1.3 %copy-start.6 = (bf16[2,384,768]{2,1,0:T(8,128)(2,1)S(1)}, bf16[2,384,768]{2,1,0:T(8,128)(2,1)}, u32[]{:S(2)}) copy-start(bf16[2,384,768]{2,1,0:T(8,128)(2,1)} %gate.1) | copy-start | bytes 3538948
  33.8 1.3 %copy-start.7 = (bf16[2,384,768]{2,1,0:T(8,128)(2,1)S(1)}, bf16[2,384,768]{2,1,0:T(8,128)(2,1)}, u32[]{:S(2)}) copy-start(bf16[2,384,768]{2,1,0:T(8,128)(2,1)} %up.1) | copy-start | bytes 3538948
  36.4 4.5 %collective-permute-start.2 = (bf16[1,64,2176]{2,1,0:T(8,128)(2,1)S(1)}, bf16[1,64,2176]{2,1,0:T(8,128)(2,1)S(1)}, u32[]{:S(2)}, u32[]{:S(2)}) collective-permute-start(bf16[1,64,2176]{2,1,0:T(8,128)(2,1)S(1)} %get-tuple-element.57.lines._), channel_id=1, source_target_pairs={{0,2},{2,0},{4,6},{6,4},{8,10},{10,8},{12,14},{14,12},{16,18},{18,... | collective-permute-start | bytes 835592 | tf_op jit(solution)/shard_map/ppermute | solution.py:66
  38.8 13.4 %collective-permute-start.15 = (bf16[2,64,2176]{2,1,0:T(8,128)(2,1)S(1)}, bf16[2,64,2176]{2,1,0:T(8,128)(2,1)S(1)}, u32[]{:S(2)}, u32[]{:S(2)}) collective-permute-start(bf16[2,64,2176]{2,1,0:T(8,128)(2,1)S(1)} %stack.21._.lines), channel_id=1, source_target_pairs={{0,4},{2,6},{4,0},{6,2},{8,12},{10,14},{12,8},{14,10},{16,20},{18,... | collective-permute-start | bytes 1671176 | tf_op jit(solution)/shard_map/ppermute | solution.py:66
  39.4 13.1 %collective-permute-start.16 = (bf16[2,64,2176]{2,1,0:T(8,128)(2,1)S(1)}, bf16[2,64,2176]{2,1,0:T(8,128)(2,1)S(1)}, u32[]{:S(2)}, u32[]{:S(2)}) collective-permute-start(bf16[2,64,2176]{2,1,0:T(8,128)(2,1)S(1)} %stack.21._.lines), channel_id=1, source_target_pairs={{0,1},{1,0},{2,3},{3,2},{4,5},{5,4},{6,7},{7,6},{8,9},{9,8},{10,11... | collective-permute-start | bytes 1671176 | tf_op jit(solution)/shard_map/ppermute | solution.py:66
  39.9 1.0 copy-start.5
  39.9 2.0 %collective-permute-start.7 = (bf16[2,64,2176]{2,1,0:T(8,128)(2,1)S(1)}, bf16[2,64,2176]{2,1,0:T(8,128)(2,1)S(1)}, u32[]{:S(2)}, u32[]{:S(2)}) collective-permute-start(bf16[2,64,2176]{2,1,0:T(8,128)(2,1)S(1)} %get-tuple-element.58.over), channel_id=1, source_target_pairs={{0,2},{2,0},{4,6},{6,4},{8,10},{10,8},{12,14},{14,12},{16,18},{18,... | collective-permute-start | bytes 1671176 | tf_op jit(solution)/shard_map/ppermute | solution.py:66
  39.9 4.1 %copy-start.2 = (bf16[2,384,2048]{2,1,0:T(8,128)(2,1)S(1)}, bf16[2,384,2048]{2,1,0:T(8,128)(2,1)}, u32[]{:S(2)}) copy-start(bf16[2,384,2048]{2,1,0:T(8,128)(2,1)} %w_down.3) | copy-start | bytes 9437188
  40.9 2.2 %collective-permute-start = (bf16[128,2048]{1,0:T(8,128)(2,1)S(1)}, bf16[128,2048]{1,0:T(8,128)(2,1)S(1)}, u32[]{:S(2)}, u32[]{:S(2)}) collective-permute-start(bf16[128,2048]{1,0:T(8,128)(2,1)S(1)} %copy-done.5), channel_id=1, source_target_pairs={{0,2},{2,0},{4,6},{6,4},{8,10},{10,8},{12,14},{14,12},{16,18},{18,... | collective-permute-start | bytes 1572872 | tf_op jit(solution)/shard_map/ppermute | solution.py:66
  40.9 3.1 %collective-permute-start.10 = (bf16[2,64,2048]{2,1,0:T(8,128)(2,1)S(1)}, bf16[2,64,2048]{2,1,0:T(8,128)(2,1)S(1)}, u32[]{:S(2)}, u32[]{:S(2)}) collective-permute-start(bf16[2,64,2048]{2,1,0:T(8,128)(2,1)S(1)} %join.2.diag), channel_id=1, source_target_pairs={{0,2},{2,0},{4,6},{6,4},{8,10},{10,8},{12,14},{14,12},{16,18},{18,... | collective-permute-start | bytes 1572872 | tf_op jit(solution)/shard_map/ppermute | solution.py:66
  41.9 2.1 %collective-permute-start.4 = (bf16[1,64,2176]{2,1,0:T(8,128)(2,1)S(1)}, bf16[1,64,2176]{2,1,0:T(8,128)(2,1)S(1)}, u32[]{:S(2)}, u32[]{:S(2)}) collective-permute-start(bf16[1,64,2176]{2,1,0:T(8,128)(2,1)S(1)} %collective-permute-done.3.side), channel_id=1, source_target_pairs={{0,2},{2,0},{4,6},{6,4},{8,10},{10,8},{12,14},{14,12},{16,18},{18,... | collective-permute-start | bytes 835592 | tf_op jit(solution)/shard_map/ppermute | solution.py:66
  44.0 3.9 %copy-start = (bf16[2,384,2048]{2,1,0:T(8,128)(2,1)S(1)}, bf16[2,384,2048]{2,1,0:T(8,128)(2,1)}, u32[]{:S(2)}) copy-start(bf16[2,384,2048]{2,1,0:T(8,128)(2,1)} %w_gate.7) | copy-start | bytes 9437188
  44.0 3.9 %copy-start.1 = (bf16[2,384,2048]{2,1,0:T(8,128)(2,1)S(1)}, bf16[2,384,2048]{2,1,0:T(8,128)(2,1)}, u32[]{:S(2)}) copy-start(bf16[2,384,2048]{2,1,0:T(8,128)(2,1)} %w_up.7) | copy-start | bytes 9437188
  50.2 10.1 %collective-permute-start.14 = (bf16[4,128,1024]{2,1,0:T(8,128)(2,1)S(1)}, bf16[4,128,1024]{2,1,0:T(8,128)(2,1)S(1)}, u32[]{:S(2)}, u32[]{:S(2)}) collective-permute-start(bf16[4,128,1024]{2,1,0:T(8,128)(2,1)S(1)} %get-tuple-element.69._), channel_id=1, source_target_pairs={{0,2},{2,0},{4,6},{6,4},{8,10},{10,8},{12,14},{14,12},{16,18},{18,... | collective-permute-start | bytes 3145736 | tf_op jit(solution)/shard_map/ppermute | solution.py:66
  52.5 6.6 %collective-permute-start.17 = (bf16[2,64,1024]{2,1,0:T(8,128)(2,1)S(1)}, bf16[2,64,1024]{2,1,0:T(8,128)(2,1)S(1)}, u32[]{:S(2)}, u32[]{:S(2)}) collective-permute-start(bf16[2,64,1024]{2,1,0:T(8,128)(2,1)S(1)} %get-tuple-element.70._), channel_id=1, source_target_pairs={{0,1},{1,0},{2,3},{3,2},{4,5},{5,4},{6,7},{7,6},{8,9},{9,8},{10,11... | collective-permute-start | bytes 786440 | tf_op jit(solution)/shard_map/ppermute | solution.py:66
  53.5 6.8 %collective-permute-start.18 = (bf16[2,64,1024]{2,1,0:T(8,128)(2,1)S(1)}, bf16[2,64,1024]{2,1,0:T(8,128)(2,1)S(1)}, u32[]{:S(2)}, u32[]{:S(2)}) collective-permute-start(bf16[2,64,1024]{2,1,0:T(8,128)(2,1)S(1)} %get-tuple-element.71), channel_id=1, source_target_pairs={{0,4},{2,6},{4,0},{6,2},{8,12},{10,14},{12,8},{14,10},{16,20},{18,... | collective-permute-start | bytes 786440 | tf_op jit(solution)/shard_map/ppermute | solution.py:66
  57.3 3.8 %collective-permute-start.20 = (bf16[4,128,1024]{2,1,0:T(8,128)(2,1)S(1)}, bf16[4,128,1024]{2,1,0:T(8,128)(2,1)S(1)}, u32[]{:S(2)}, u32[]{:S(2)}) collective-permute-start(bf16[4,128,1024]{2,1,0:T(8,128)(2,1)S(1)} %get-tuple-element.72.refs_0_), channel_id=1, source_target_pairs={{0,2},{2,0},{4,6},{6,4},{8,10},{10,8},{12,14},{14,12},{16,18},{18,... | collective-permute-start | bytes 3145736 | tf_op jit(solution)/shard_map/ppermute | solution.py:66
  57.3 4.6 %collective-permute-start.25 = (bf16[2,64,2176]{2,1,0:T(8,128)(2,1)S(1)}, bf16[2,64,2176]{2,1,0:T(8,128)(2,1)S(1)}, u32[]{:S(2)}, u32[]{:S(2)}) collective-permute-start(bf16[2,64,2176]{2,1,0:T(8,128)(2,1)S(1)} %stack.21._.lines), channel_id=1, source_target_pairs={{0,2},{2,0},{4,6},{6,4},{8,10},{10,8},{12,14},{14,12},{16,18},{18,... | collective-permute-start | bytes 1671176 | tf_op jit(solution)/shard_map/ppermute | solution.py:66
  59.1 5.5 %collective-permute-start.26 = (bf16[2,64,2176]{2,1,0:T(8,128)(2,1)S(1)}, bf16[2,64,2176]{2,1,0:T(8,128)(2,1)S(1)}, u32[]{:S(2)}, u32[]{:S(2)}) collective-permute-start(bf16[2,64,2176]{2,1,0:T(8,128)(2,1)S(1)} %collective-permute-done.16.side), channel_id=1, source_target_pairs={{0,2},{2,0},{4,6},{6,4},{8,10},{10,8},{12,14},{14,12},{16,18},{18,... | collective-permute-start | bytes 1671176 | tf_op jit(solution)/shard_map/ppermute | solution.py:66
  60.3 3.2 %collective-permute-start.27 = (bf16[2,64,2176]{2,1,0:T(8,128)(2,1)S(1)}, bf16[2,64,2176]{2,1,0:T(8,128)(2,1)S(1)}, u32[]{:S(2)}, u32[]{:S(2)}) collective-permute-start(bf16[2,64,2176]{2,1,0:T(8,128)(2,1)S(1)} %collective-permute-done.15.over), channel_id=1, source_target_pairs={{0,2},{2,0},{4,6},{6,4},{8,10},{10,8},{12,14},{14,12},{16,18},{18,... | collective-permute-start | bytes 1671176 | tf_op jit(solution)/shard_map/ppermute | solution.py:66
  60.4 4.3 %collective-permute-start.28 = (bf16[2,64,2048]{2,1,0:T(8,128)(2,1)S(1)}, bf16[2,64,2048]{2,1,0:T(8,128)(2,1)S(1)}, u32[]{:S(2)}, u32[]{:S(2)}) collective-permute-start(bf16[2,64,2048]{2,1,0:T(8,128)(2,1)S(1)} %join.3._.diag), channel_id=1, source_target_pairs={{0,2},{2,0},{4,6},{6,4},{8,10},{10,8},{12,14},{14,12},{16,18},{18,... | collective-permute-start | bytes 1572872 | tf_op jit(solution)/shard_map/ppermute | solution.py:66
  61.0 13.9 %collective-permute-start.19 = (bf16[4,64,1024]{2,1,0:T(8,128)(2,1)S(1)}, bf16[4,64,1024]{2,1,0:T(8,128)(2,1)S(1)}, u32[]{:S(2)}, u32[]{:S(2)}) collective-permute-start(bf16[4,64,1024]{2,1,0:T(8,128)(2,1)S(1)} %get-tuple-element.74._), channel_id=1, source_target_pairs={{0,1},{1,0},{2,3},{3,2},{4,5},{5,4},{6,7},{7,6},{8,9},{9,8},{10,11... | collective-permute-start | bytes 1572872 | tf_op jit(solution)/shard_map/ppermute | solution.py:66
  61.9 13.7 %collective-permute-start.21 = (bf16[2,128,1024]{2,1,0:T(8,128)(2,1)S(1)}, bf16[2,128,1024]{2,1,0:T(8,128)(2,1)S(1)}, u32[]{:S(2)}, u32[]{:S(2)}) collective-permute-start(bf16[2,128,1024]{2,1,0:T(8,128)(2,1)S(1)} %get-tuple-element.77._), channel_id=1, source_target_pairs={{0,4},{2,6},{4,0},{6,2},{8,12},{10,14},{12,8},{14,10},{16,20},{18,... | collective-permute-start | bytes 1572872 | tf_op jit(solution)/shard_map/ppermute | solution.py:66
  70.8 5.0 %collective-permute-start.29 = (bf16[4,128,1024]{2,1,0:T(8,128)(2,1)S(1)}, bf16[4,128,1024]{2,1,0:T(8,128)(2,1)S(1)}, u32[]{:S(2)}, u32[]{:S(2)}) collective-permute-start(bf16[4,128,1024]{2,1,0:T(8,128)(2,1)S(1)} %get-tuple-element.86._), channel_id=1, source_target_pairs={{0,2},{2,0},{4,6},{6,4},{8,10},{10,8},{12,14},{14,12},{16,18},{18,... | collective-permute-start | bytes 3145736 | tf_op jit(solution)/shard_map/ppermute | solution.py:66
  73.1 4.1 %collective-permute-start.31 = (bf16[4,128,1024]{2,1,0:T(8,128)(2,1)S(1)}, bf16[4,128,1024]{2,1,0:T(8,128)(2,1)S(1)}, u32[]{:S(2)}, u32[]{:S(2)}) collective-permute-start(bf16[4,128,1024]{2,1,0:T(8,128)(2,1)S(1)} %get-tuple-element.90), channel_id=1, source_target_pairs={{0,2},{2,0},{4,6},{6,4},{8,10},{10,8},{12,14},{14,12},{16,18},{18,... | collective-permute-start | bytes 3145736 | tf_op jit(solution)/shard_map/ppermute | solution.py:66
  75.9 17.4 %collective-permute-start.30 = (bf16[4,64,1024]{2,1,0:T(8,128)(2,1)S(1)}, bf16[4,64,1024]{2,1,0:T(8,128)(2,1)S(1)}, u32[]{:S(2)}, u32[]{:S(2)}) collective-permute-start(bf16[4,64,1024]{2,1,0:T(8,128)(2,1)S(1)} %get-tuple-element.88._), channel_id=1, source_target_pairs={{0,1},{1,0},{2,3},{3,2},{4,5},{5,4},{6,7},{7,6},{8,9},{9,8},{10,11... | collective-permute-start | bytes 1572872 | tf_op jit(solution)/shard_map/ppermute | solution.py:66
  77.4 15.9 %collective-permute-start.32 = (bf16[2,128,1024]{2,1,0:T(8,128)(2,1)S(1)}, bf16[2,128,1024]{2,1,0:T(8,128)(2,1)S(1)}, u32[]{:S(2)}, u32[]{:S(2)}) collective-permute-start(bf16[2,128,1024]{2,1,0:T(8,128)(2,1)S(1)} %get-tuple-element.92), channel_id=1, source_target_pairs={{0,4},{2,6},{4,0},{6,2},{8,12},{10,14},{12,8},{14,10},{16,20},{18,... | collective-permute-start | bytes 1572872 | tf_op jit(solution)/shard_map/ppermute | solution.py:66
  78.9 14.2 %collective-permute-start.22 = (bf16[64,1024]{1,0:T(8,128)(2,1)S(1)}, bf16[64,1024]{1,0:T(8,128)(2,1)S(1)}, u32[]{:S(2)}, u32[]{:S(2)}) collective-permute-start(bf16[64,1024]{1,0:T(8,128)(2,1)S(1)} %get-tuple-element.79._), channel_id=1, source_target_pairs={{0,4},{2,6},{4,0},{6,2},{8,12},{10,14},{12,8},{14,10},{16,20},{18,... | collective-permute-start | bytes 393224 | tf_op jit(solution)/shard_map/ppermute | solution.py:66
  79.5 13.7 %collective-permute-start.23 = (bf16[64,1024]{1,0:T(8,128)(2,1)S(1)}, bf16[64,1024]{1,0:T(8,128)(2,1)S(1)}, u32[]{:S(2)}, u32[]{:S(2)}) collective-permute-start(bf16[64,1024]{1,0:T(8,128)(2,1)S(1)} %get-tuple-element.81), channel_id=1, source_target_pairs={{0,1},{1,0},{2,3},{3,2},{4,5},{5,4},{6,7},{7,6},{8,9},{9,8},{10,11... | collective-permute-start | bytes 393224 | tf_op jit(solution)/shard_map/ppermute | solution.py:66
  93.2 12.9 %collective-permute-start.24 = (bf16[64,2048]{1,0:T(8,128)(2,1)S(1)}, bf16[64,2048]{1,0:T(8,128)(2,1)S(1)}, u32[]{:S(2)}, u32[]{:S(2)}) collective-permute-start(bf16[64,2048]{1,0:T(8,128)(2,1)S(1)} %third_sum.4._), channel_id=1, source_target_pairs={{0,16},{2,18},{4,20},{6,22},{8,24},{10,26},{12,28},{14,30},{16,0},... | collective-permute-start | bytes 786440 | tf_op jit(solution)/shard_map/ppermute | solution.py:71
  93.4 12.7 %collective-permute-start.33 = (bf16[64,1024]{1,0:T(8,128)(2,1)S(1)}, bf16[64,1024]{1,0:T(8,128)(2,1)S(1)}, u32[]{:S(2)}, u32[]{:S(2)}) collective-permute-start(bf16[64,1024]{1,0:T(8,128)(2,1)S(1)} %get-tuple-element.94), channel_id=1, source_target_pairs={{0,4},{2,6},{4,0},{6,2},{8,12},{10,14},{12,8},{14,10},{16,20},{18,... | collective-permute-start | bytes 393224 | tf_op jit(solution)/shard_map/ppermute | solution.py:66
  94.6 11.6 %collective-permute-start.34 = (bf16[64,1024]{1,0:T(8,128)(2,1)S(1)}, bf16[64,1024]{1,0:T(8,128)(2,1)S(1)}, u32[]{:S(2)}, u32[]{:S(2)}) collective-permute-start(bf16[64,1024]{1,0:T(8,128)(2,1)S(1)} %get-tuple-element.96), channel_id=1, source_target_pairs={{0,1},{1,0},{2,3},{3,2},{4,5},{5,4},{6,7},{7,6},{8,9},{9,8},{10,11... | collective-permute-start | bytes 393224 | tf_op jit(solution)/shard_map/ppermute | solution.py:66
  95.6 10.6 %collective-permute-start.36 = (bf16[64,1024]{1,0:T(8,128)(2,1)S(1)}, bf16[64,1024]{1,0:T(8,128)(2,1)S(1)}, u32[]{:S(2)}, u32[]{:S(2)}) collective-permute-start(bf16[64,1024]{1,0:T(8,128)(2,1)S(1)} %get-tuple-element.101), channel_id=1, source_target_pairs={{0,4},{2,6},{4,0},{6,2},{8,12},{10,14},{12,8},{14,10},{16,20},{18,... | collective-permute-start | bytes 393224 | tf_op jit(solution)/shard_map/ppermute | solution.py:66
  97.0 9.3 %collective-permute-start.37 = (bf16[64,1024]{1,0:T(8,128)(2,1)S(1)}, bf16[64,1024]{1,0:T(8,128)(2,1)S(1)}, u32[]{:S(2)}, u32[]{:S(2)}) collective-permute-start(bf16[64,1024]{1,0:T(8,128)(2,1)S(1)} %get-tuple-element.103), channel_id=1, source_target_pairs={{0,1},{1,0},{2,3},{3,2},{4,5},{5,4},{6,7},{7,6},{8,9},{9,8},{10,11... | collective-permute-start | bytes 393224 | tf_op jit(solution)/shard_map/ppermute | solution.py:66
  106.2 11.1 %collective-permute-start.35 = (bf16[64,2048]{1,0:T(8,128)(2,1)S(1)}, bf16[64,2048]{1,0:T(8,128)(2,1)S(1)}, u32[]{:S(2)}, u32[]{:S(2)}) collective-permute-start(bf16[64,2048]{1,0:T(8,128)(2,1)S(1)} %third_sum.5._), channel_id=1, source_target_pairs={{0,8},{2,10},{4,12},{6,14},{8,16},{10,18},{12,20},{14,22},{16,24},... | collective-permute-start | bytes 786440 | tf_op jit(solution)/shard_map/ppermute | solution.py:71
  106.4 12.3 %collective-permute-start.40 = (bf16[64,2048]{1,0:T(8,128)(2,1)S(1)}, bf16[64,2048]{1,0:T(8,128)(2,1)S(1)}, u32[]{:S(2)}, u32[]{:S(2)}) collective-permute-start(bf16[64,2048]{1,0:T(8,128)(2,1)S(1)} %third_sum.6.refs_2_._), channel_id=1, source_target_pairs={{0,24},{2,26},{4,28},{6,30},{8,0},{10,2},{12,4},{14,6},{16,8},{18,... | collective-permute-start | bytes 786440 | tf_op jit(solution)/shard_map/ppermute | solution.py:71
  110.2 5.0 %collective-permute-start.38 = (bf16[64,1024]{1,0:T(8,128)(2,1)S(1)}, bf16[64,1024]{1,0:T(8,128)(2,1)S(1)}, u32[]{:S(2)}, u32[]{:S(2)}) collective-permute-start(bf16[64,1024]{1,0:T(8,128)(2,1)S(1)} %get-tuple-element.104), channel_id=1, source_target_pairs={{0,4},{2,6},{4,0},{6,2},{8,12},{10,14},{12,8},{14,10},{16,20},{18,... | collective-permute-start | bytes 393224 | tf_op jit(solution)/shard_map/ppermute | solution.py:66
  110.8 5.0 %collective-permute-start.39 = (bf16[64,1024]{1,0:T(8,128)(2,1)S(1)}, bf16[64,1024]{1,0:T(8,128)(2,1)S(1)}, u32[]{:S(2)}, u32[]{:S(2)}) collective-permute-start(bf16[64,1024]{1,0:T(8,128)(2,1)S(1)} %get-tuple-element.106), channel_id=1, source_target_pairs={{0,1},{1,0},{2,3},{3,2},{4,5},{5,4},{6,7},{7,6},{8,9},{9,8},{10,11... | collective-permute-start | bytes 393224 | tf_op jit(solution)/shard_map/ppermute | solution.py:66
